TPU v7x, 32 devices: a whole 2x2x4 slice. The times are simulated.
32 devices in a mesh: seq: 8 (over z, x), tp: 4 (over y, core).
Axes of the slice: x: 2, y: 2, z: 4, core: 2. Of those that a mesh axis runs over, the one named last changes fastest.
Arguments:
- tokens: bfloat16 [4096, 4096], P('seq', 'tp'), may hold values from -6 to 6
- log_decay: float32 [4096, 16], P('seq', 'tp'), may hold values from -2 to 0
- w_query: bfloat16 [4096, 2048], P(None, 'tp'), may hold values from -0.09375 to 0.09375
- w_key: bfloat16 [4096, 512], P(None, 'tp'), may hold values from -0.09375 to 0.09375
- w_value: bfloat16 [4096, 512], P(None, 'tp'), may hold values from -0.09375 to 0.09375
- w_level: bfloat16 [4096, 96], P(None, 'tp'), may hold values from -0.09375 to 0.09375
- w_out: bfloat16 [2048, 4096], P('tp'), may hold values from -0.125 to 0.125
Outputs:
- mixed: bfloat16 [4096, 4096], P('seq', 'tp')
All inputs are finite; a program needn't handle non-finite values.
Results may differ from a plain program's by a relative error of at most 0.02.
Values may be sent and summed in bfloat16 or wider, within the bound.
No kernel may reach another device: no remote copies, remote signals or barrier semaphores. Data moves between devices by JAX's collectives and lax.ppermute only.
A program may use at most 128 MiB of HBM per device.

v0:
```python
import jax
import jax.numpy as jnp
from jax import lax
from jax.sharding import PartitionSpec as P

BLOCK = 128


HIGHEST = lax.Precision.HIGHEST


def prefix(part, axis, combine, identity):
    place = lax.axis_index(axis)
    gathered = lax.all_gather(part, axis)
    state = jnp.zeros_like(part) + jnp.asarray(identity, part.dtype)

    def one(step, state):
        return combine(state, lax.dynamic_index_in_dim(gathered, step, 0, False))

    return lax.fori_loop(0, place, one, state)


def top_bit(differ, bit_count):
    result = jnp.zeros_like(differ)
    for shift in range(1, bit_count):
        result = result + (jnp.right_shift(differ, shift) > 0).astype(jnp.int32)
    return result


def split_pair(wide):
    upper_part = wide.astype(jnp.bfloat16)
    lower_part = (wide - upper_part.astype(jnp.float32)).astype(jnp.bfloat16)
    return (upper_part, lower_part)


def body(tokens, log_decay, w_query, w_key, w_value, w_level, w_out):
    rows = tokens.shape[0]
    heads_local = log_decay.shape[1]
    head_size = w_out.shape[0] // heads_local
    level_count = w_level.shape[1] // heads_local
    kv_local = w_key.shape[1] // head_size
    group_size = heads_local // kv_local
    matrices = (w_query, w_key, w_value, w_level)
    piece = lax.all_gather(tokens, "tp", axis=1, tiled=True)
    sums = tuple(
        (jnp.dot(piece, matrix, preferred_element_type=jnp.float32) for matrix in matrices)
    )
    query = sums[0].astype(jnp.bfloat16).reshape(rows, kv_local, group_size, head_size)
    keys_here = sums[1].astype(jnp.bfloat16).reshape(rows, kv_local, head_size)
    values_here = sums[2].astype(jnp.bfloat16).reshape(rows, kv_local, head_size)
    level_weight = jax.nn.softplus(sums[3]).reshape(rows, heads_local, level_count)
    decay_sum = jnp.cumsum(log_decay, axis=0)
    slab_total = decay_sum[rows - 1]
    before = prefix(slab_total, "seq", jnp.add, jnp.zeros_like(slab_total))
    ends_here = before + slab_total
    positions = jnp.arange(rows, dtype=jnp.int32)
    block_of = positions // BLOCK
    local_bits = (rows // BLOCK).bit_length() - 1
    block_differ = jnp.bitwise_xor(block_of[:, None], block_of[None, :])
    level_table = jnp.where(block_differ == 0, 0, 1 + top_bit(block_differ, local_bits))
    causal = positions[:, None] >= positions[None, :]
    decay_heads = decay_sum.T
    gaps = jnp.where(causal[None], decay_heads[:, :, None] - decay_heads[:, None, :], -jnp.inf)
    picked = jnp.zeros((heads_local, rows, rows), jnp.float32)
    for level in range(local_bits + 1):
        picked = picked + jnp.where(
            level_table[None] == level, level_weight[:, :, level].T[:, :, None], 0.0
        )
    scores = jnp.einsum(
        "tgqd,sgd->gqts", query, keys_here, preferred_element_type=jnp.float32
    ).reshape(heads_local, rows, rows)
    mixing = (picked * jnp.exp(gaps) * scores).reshape(kv_local, group_size, rows, rows)
    mixing_upper, mixing_lower = split_pair(mixing)
    local_part = jnp.einsum(
        "gqts,sgd->gqtd", mixing_upper, values_here, preferred_element_type=jnp.float32
    )
    local_part = local_part + jnp.einsum(
        "gqts,sgd->gqtd", mixing_lower, values_here, preferred_element_type=jnp.float32
    )
    local_part = local_part.reshape(heads_local, rows, head_size)
    keep_factor = jnp.exp(slab_total[None, :] - decay_sum).reshape(rows, kv_local, group_size)
    weighted_keys = keep_factor[:, :, :, None] * keys_here.astype(jnp.float32)[:, :, None, :]
    keys_upper, keys_lower = split_pair(weighted_keys)
    own_state = jnp.einsum(
        "tgqd,tge->gqde", keys_upper, values_here, preferred_element_type=jnp.float32
    )
    own_state = own_state + jnp.einsum(
        "tgqd,tge->gqde", keys_lower, values_here, preferred_element_type=jnp.float32
    )
    own_state = own_state.reshape(heads_local, head_size, head_size)
    seq_bits = lax.axis_size("seq").bit_length() - 1
    device = lax.axis_index("seq")
    empty = jnp.zeros((seq_bits, heads_local, head_size, head_size), jnp.float32)
    states = lax.all_gather(own_state[None], "seq", axis=0, tiled=True)
    slab_ends = lax.all_gather(ends_here[None], "seq", axis=0, tiled=True)
    sources = jnp.arange(states.shape[0], dtype=jnp.int32)
    earlier = sources < device
    highest_bit = top_bit(jnp.bitwise_xor(sources, device), seq_bits)
    onehot = jnp.logical_and(
        highest_bit[:, None] == jnp.arange(seq_bits, dtype=jnp.int32)[None, :], earlier[:, None]
    ).astype(jnp.float32)
    fading = jnp.exp(jnp.where(earlier[:, None], before[None, :] - slab_ends, -jnp.inf))
    buckets = empty + jnp.einsum("nb,nh,nhde->bhde", onehot, fading, states, precision=HIGHEST)
    query_heads = query.reshape(rows, heads_local, head_size)
    buckets_upper, buckets_lower = split_pair(buckets)
    per_level = jnp.einsum(
        "thd,bhde->bthe", query_heads, buckets_upper, preferred_element_type=jnp.float32
    )
    per_level = per_level + jnp.einsum(
        "thd,bhde->bthe", query_heads, buckets_lower, preferred_element_type=jnp.float32
    )
    span_weight = (
        level_weight[:, :, local_bits + 1 : local_bits + 1 + seq_bits]
        * jnp.exp(decay_sum)[:, :, None]
    )
    remote_part = jnp.einsum("bthe,thb->hte", per_level, span_weight, precision=HIGHEST)
    combined = local_part + remote_part
    normed = (
        combined * lax.rsqrt(jnp.mean(combined * combined, axis=-1, keepdims=True) + 1e-05)
    ).astype(jnp.bfloat16)
    partial_out = jnp.einsum(
        "htd,hde->te",
        normed,
        w_out.reshape(heads_local, head_size, w_out.shape[1]),
        preferred_element_type=jnp.float32,
    )
    return lax.psum_scatter(partial_out.astype(jnp.bfloat16), "tp", scatter_dimension=1, tiled=True)


def solution(mesh):
    in_specs = (
        P("seq", "tp"),
        P("seq", "tp"),
        P(None, "tp"),
        P(None, "tp"),
        P(None, "tp"),
        P(None, "tp"),
        P("tp", None),
    )
    out_specs = P("seq", "tp")
    return jax.shard_map(body, mesh=mesh, in_specs=in_specs, out_specs=out_specs, check_vma=False)
```

profile of v0, /device:TPU:0, one launch (start us, length us, event | category | flops | bytes accessed | tf_op | source)
XLA Modules:
  0.0 166.3 jit_solution(17146469727610956307)
XLA Ops:
  6.5 0.7 all-gather.6.cloned.1.call-update
  7.3 0.7 reshape.284
  8.0 1.2 reduce-window.6
  9.7 1.2 dynamic-slice
  11.7 22.1 %all-gather.2 = f32[8,1,4]{2,1,0:T(1,128)S(1)} all-gather(f32[1,1,4]{2,1,0:T(1,128)S(1)} %bitcast.110), channel_id=1, replica_groups=mesh['seq'=8,'tp'=4] {'seq'}, dimensions={0}, use_global_device_ids=true | all-gather | bytes 144 | tf_op jit(solution)/shard_map/all_gather | solution.py:14
  33.9 12.2 %all-gather.6.cloned.1.call-done = bf16[512,4096]{1,0:T(8,128)(2,1)} async-done(((bf16[512,1024]{1,0:T(8,128)(2,1)}), bf16[512,4096]{1,0:T(8,128)(2,1)}) %all-gather.6.cloned.1.call-update) | async-done | bytes 4194320 | tf_op jit(solution)/shard_map/all_gather | solution.py:44
  46.1 3.4 %convolution_convert_fusion.2 = bf16[512,128]{1,0:T(8,128)(2,1)S(1)} fusion(bf16[512,4096]{1,0:T(8,128)(2,1)} %all-gather.6.cloned.1.call-done, bf16[4096,128]{1,0:T(8,128)(2,1)S(1)} %copy-done), kind=kOutput, calls=%fused_computation.21 | convolution fusion | flops 536936448 | bytes 5373952 | tf_op jit(solution)/shard_map/dot_general | solution.py:46
  49.7 3.5 %fusion.13 = bf16[512,128,1]{1,0,2:T(8,128)(2,1)S(1)} fusion(bf16[512,4096]{1,0:T(8,128)(2,1)} %all-gather.6.cloned.1.call-done, bf16[4096,128]{1,0:T(8,128)(2,1)S(1)} %copy-done.5), kind=kOutput, calls=%fused_computation.22 | convolution fusion | flops 536936448 | bytes 5373952 | tf_op jit(solution)/shard_map/dot_general | solution.py:46
  53.5 1.0 convolution_add_fusion
  54.7 21.6 %all-reduce = f32[32]{0:T(128)S(1)} all-reduce(f32[32]{0:T(128)S(1)} %add_dynamic-update-slice_fusion), channel_id=2, replica_groups=mesh['seq'=8,'tp'=4] {'seq'}, use_global_device_ids=true, to_apply=%add | all-reduce | flops 32 | bytes 256
  76.7 0.7 fusion.21
  77.4 3.4 %compare_select_fusion = f32[512,24]{0,1:T(8,128)S(1)} fusion(bf16[512,4096]{1,0:T(8,128)(2,1)} %all-gather.6.cloned.1.call-done, bf16[4096,24]{0,1:T(8,128)(2,1)S(1)} %copy-done.4), kind=kOutput, calls=%fused_computation.46 | convolution fusion | flops 100737024 | bytes 4440064 | tf_op jit(solution)/shard_map/dot_general | solution.py:46
  81.0 5.9 %convolution_convert_fusion = bf16[512,512]{0,1:T(8,128)(2,1)S(1)} fusion(bf16[512,4096]{1,0:T(8,128)(2,1)} %all-gather.6.cloned.1.call-done, bf16[4096,512]{1,0:T(8,128)(2,1)} %param.11), kind=kOutput, calls=%fused_computation.18 | convolution fusion | flops 2147745792 | bytes 8912896 | tf_op jit(solution)/shard_map/dot_general | solution.py:46
  86.9 2.7 %bitcast_multiply_fusion = f32[1,4,512,512]{2,3,1,0:T(8,128)S(1)} fusion(bf16[512,4,128]{0,2,1:T(8,128)(2,1)S(1)} %bitcast.103, f32[4,512]{1,0:T(4,128)S(1)} %bitcast.107, f32[4,512]{1,0:T(4,128)S(1)} %get-tuple-element.69, f32[4,512]{1,0:T(4,128)S(1)} %get-tuple-element.70, f32[4,512]{1,0:T(4,128)S(1)} %bitcast.112, ...), kind=kOutput, calls=%fused_computation.2 | convolution fusion | flops 277872640 | bytes 5931008 | tf_op jit(solution)/shard_map/tgqd,sgd->gqts/dot_general | solution.py:69
  89.6 1.9 %copy-done.1 = f32[1,4,512,512]{2,3,1,0:T(8,128)} copy-done((f32[1,4,512,512]{2,3,1,0:T(8,128)}, f32[1,4,512,512]{2,3,1,0:T(8,128)S(1)}, u32[]{:S(2)}) %copy-start.1) | copy-done | bytes 4194328
  91.5 0.7 fusion.2
  92.2 11.9 %all-gather.8.cloned.1.call-done = f32[32,128,128]{2,1,0:T(8,128)} async-done(((f32[4,128,128]{2,1,0:T(8,128)}), f32[32,128,128]{2,1,0:T(8,128)}) %all-gather.8.cloned.1.call-update) | async-done | bytes 2097168 | tf_op jit(solution)/shard_map/all_gather | solution.py:94
  104.1 3.8 %fusion.6 = f32[3,4,128,128]{3,0,2,1:T(4,128)S(1)} fusion(f32[8,4,128,128]{3,2,1,0:T(8,128)} %bitcast.102, f32[8,4]{0,1:T(4,128)S(1)} %copy.78, s32[8]{0:T(128)S(1)} %fusion.42, pred[8]{0:T(512)(128)(4,1)S(1)} %iota_compare_fusion.2), kind=kOutput, calls=%fused_computation.11 | convolution fusion | flops 19398704 | bytes 2883752 | tf_op jit(solution)/shard_map/nb,nh,nhde->bhde/dot_general | solution.py:103
  108.5 0.7 fusion
  109.2 0.9 copy-done.2
  110.1 0.9 multiply_reduce_fusion
  110.9 1.3 copy-done.3
  112.2 4.4 %bitcast_convert_fusion = bf16[512,4096]{1,0:T(8,128)(2,1)} fusion(bf16[4,128,4096]{2,1,0:T(8,128)(2,1)S(1)} %bitcast.101, f32[4,512,128]{1,2,0:T(8,128)S(1)} %get-tuple-element.68, f32[4,512]{1,0:T(4,128)S(1)} %add_rsqrt_fusion), kind=kOutput, calls=%fused_computation.1 | convolution fusion | flops 2150105088 | bytes 9445376 | tf_op jit(solution)/shard_map/htd,hde->te/dot_general | solution.py:121
  116.6 43.1 %reduce-scatter.2.cloned.1.call-done = bf16[512,1024]{1,0:T(8,128)(2,1)} async-done(((bf16[512,4096]{1,0:T(8,128)(2,1)}), bf16[512,1024]{1,0:T(8,128)(2,1)}) %reduce-scatter.2.cloned.1.call-update) | async-done | bytes 1048592 | tf_op jit(solution)/shard_map/reduce_scatter | solution.py:127
  (40 shorter events, 2.3 us)
Async XLA Ops:
  6.5 39.6 %copy-start = (bf16[4096,128]{1,0:T(8,128)(2,1)S(1)}, bf16[4096,128]{1,0:T(8,128)(2,1)}, u32[]{:S(2)}) copy-start(bf16[4096,128]{1,0:T(8,128)(2,1)} %param.12) | copy-start | bytes 3145732
  6.5 43.2 %copy-start.5 = (bf16[4096,128]{1,0:T(8,128)(2,1)S(1)}, bf16[4096,128]{1,0:T(8,128)(2,1)}, u32[]{:S(2)}) copy-start(bf16[4096,128]{1,0:T(8,128)(2,1)} %param.13) | copy-start | bytes 3145732
  6.5 39.6 %all-gather.6.cloned.1.call-start = ((), (), s32[]{:S(2)}) async-start(), calls=%async_computation.1 | async-start | bytes 5242880 | tf_op jit(solution)/shard_map/all_gather | solution.py:44
  7.3 96.8 %all-gather.8.cloned.1.call-start = ((), (), s32[]{:S(2)}) async-start(), calls=%async_computation.3 | async-start | bytes 2359296 | tf_op jit(solution)/shard_map/all_gather | solution.py:94
  49.7 27.7 %copy-start.4 = (bf16[4096,24]{0,1:T(8,128)(2,1)S(1)}, bf16[4096,24]{0,1:T(8,128)(2,1)}, u32[]{:S(2)}) copy-start(bf16[4096,24]{0,1:T(8,128)(2,1)} %param.14) | copy-start | bytes 589828
  54.6 105.2 %reduce-scatter.2.cloned.1.call-start = ((), (), s32[]{:S(2)}) async-start(), calls=%async_computation.2 | async-start | bytes 5242880 | tf_op jit(solution)/shard_map/reduce_scatter | solution.py:127
  89.6 1.9 %copy-start.1 = (f32[1,4,512,512]{2,3,1,0:T(8,128)}, f32[1,4,512,512]{2,3,1,0:T(8,128)S(1)}, u32[]{:S(2)}) copy-start(f32[1,4,512,512]{2,3,1,0:T(8,128)S(1)} %bitcast_multiply_fusion) | copy-start | bytes 12582916
  107.9 2.2 %copy-start.2 = (f32[1,4,512,512]{2,3,1,0:T(8,128)S(1)}, f32[1,4,512,512]{2,3,1,0:T(8,128)}, u32[]{:S(2)}) copy-start(f32[1,4,512,512]{2,3,1,0:T(8,128)} %copy-done.1) | copy-start | bytes 12582916
  110.1 2.2 %copy-start.3 = (bf16[512,4096]{1,0:T(8,128)(2,1)S(1)}, bf16[512,4096]{1,0:T(8,128)(2,1)}, u32[]{:S(2)}) copy-start(bf16[512,4096]{1,0:T(8,128)(2,1)} %param.15) | copy-start | bytes 12582916
Sparse Core Ops, SparseCore 0:
  8.9 37.1 all-gather.5
  54.7 49.3 all-gather.7
  116.8 42.9 reduce-scatter.1
where the time goes:
time: 167 us; the launch traced here: 166 us
  waiting for transfers between devices  68 us (41%)
  blocking collectives  43.8 us (26%)
  matrix products  31.2 us (19%)
  between operations  14 us (8%)
  local copies, waits for them, and re-layouts  6.75 us (4%)
  other arithmetic  2.55 us (2%)
    reduce_scatter x1, waiting for transfers between devices, body(): lax.psum_scatter(partial_out.astype(jnp.bfloat16), 'tp', scatter_dimensio...  43.1 us
    all_gather x1, blocking collectives, prefix(): gathered = lax.all_gather(part, axis)  22.1 us
    unnamed x1, blocking collectives  21.6 us
    dot_general x4, matrix products, body(): jnp.dot(piece, matrix, preferred_element_type=jnp.float32)  16.3 us
    all_gather x1, waiting for transfers between devices, body(): piece = lax.all_gather(tokens, 'tp', axis=1, tiled=True)  12.2 us
    all_gather x1, waiting for transfers between devices, body(): states = lax.all_gather(own_state[None], 'seq', axis=0, tiled=True)  11.9 us
    unnamed x16, local copies, waits for them, and re-layouts  5.38 us
    dot_general x1, matrix products, body(): jnp.einsum('htd,hde->te', normed, w_out.reshape(heads_local, head_size, w...  4.38 us
  transfers between devices with their start and end apart: 3, of which 3 were waited for; matrix products, arithmetic and copies ran while one was open for 11% of the time, Pallas kernels for 0%

commit v1 on v0

v1 whole, which is shorter than its diff:
```python
import functools

import jax
import jax.numpy as jnp
from jax import lax
from jax.experimental import pallas as pl
from jax.experimental.pallas import tpu as pltpu
from jax.sharding import PartitionSpec as P

BLOCK = 128
VMEM_LIMIT = 40 * 1024 * 1024
F32 = jnp.float32
BF16 = jnp.bfloat16


def dot(a, b):
    return jnp.dot(a, b, preferred_element_type=F32)


def dot_dims(a, b, left, right):
    return lax.dot_general(a, b, (((left,), (right,)), ((), ())), preferred_element_type=F32)


def whole(shape):
    return pl.BlockSpec(shape, lambda *_: (0,) * len(shape))


def project_kernel(n_x, first, final, widths, place, *refs):
    xs, refs = refs[:n_x], refs[n_x:]
    ws, refs = refs[: 4 * n_x], refs[4 * n_x :]
    if not first:
        total_in, refs = refs[0], refs[1:]
    if final:
        keep_ref, refs = refs[0], refs[1:]
        q_out, k_out, v_out, l_out, s_out, total = refs
    else:
        (total,) = refs
    step = pl.program_id(0)
    bounds = [0]
    for width in widths:
        bounds.append(bounds[-1] + width)

    @pl.when(step == 0)
    def _():
        if first:
            total[...] = jnp.zeros_like(total)
        else:
            total[...] = total_in[...]

    for which in range(4):
        add = dot(xs[0][...], ws[which][...])
        for other in range(1, n_x):
            add = add + dot(xs[other][...], ws[4 * other + which][...])
        total[:, bounds[which] : bounds[which + 1]] += add

    if final:

        @pl.when(step == pl.num_programs(0) - 1)
        def _():
            keys = total[:, bounds[1] : bounds[2]].astype(BF16)
            values = total[:, bounds[2] : bounds[3]].astype(BF16)
            k_out[...] = keys
            v_out[...] = values
            heads = keep_ref.shape[1]
            head_size = s_out.shape[1]
            kv_local = keys.shape[1] // head_size
            group = heads // kv_local
            for g in range(kv_local):
                kf = keys[:, g * head_size : (g + 1) * head_size].astype(F32)
                vg = values[:, g * head_size : (g + 1) * head_size]
                for h in range(g * group, (g + 1) * group):
                    weighted = (kf * keep_ref[:, h : h + 1]).astype(BF16)
                    s_out[h * head_size : (h + 1) * head_size, :] = dot_dims(
                        weighted, vg, 0, 0
                    ).astype(BF16)
            q_out[...] = total[:, : bounds[1]].astype(BF16)
            raw = total[:, bounds[3] : bounds[4]]
            l_out[...] = jnp.maximum(raw, 0.0) + jnp.log1p(jnp.exp(-jnp.abs(raw)))


def project(xs, places, ws, offset, tile, total, keep, head_size):
    rows, depth = xs[0].shape
    n_x = len(xs)
    shard = ws[0].shape[0] // 4
    widths = tuple(w.shape[1] for w in ws)
    columns = sum(widths)
    first, final = total is None, keep is not None
    per_shard, skip = shard // tile, offset // tile
    in_specs = [pl.BlockSpec((rows, tile), lambda s, p: (0, s)) for _ in xs]
    for i in range(n_x):
        for width in widths:
            in_specs.append(
                pl.BlockSpec((tile, width), lambda s, p, i=i: (p[i] * per_shard + skip + s, 0))
            )
    operands = list(xs) + list(ws) * n_x
    if not first:
        in_specs.append(whole((rows, columns)))
        operands.append(total)
    scratch = []
    if final:
        heads = keep.shape[1]
        in_specs.append(whole(keep.shape))
        operands.append(keep)
        shapes = [
            ((rows, widths[0]), BF16),
            ((rows, widths[1]), BF16),
            ((rows, widths[2]), BF16),
            ((rows, widths[3]), F32),
            ((heads * head_size, head_size), BF16),
        ]
        out_shape = [jax.ShapeDtypeStruct(s, t) for s, t in shapes]
        out_specs = [whole(s) for s, _ in shapes]
        scratch = [pltpu.VMEM((rows, columns), F32)]
    else:
        out_shape = jax.ShapeDtypeStruct((rows, columns), F32)
        out_specs = whole((rows, columns))
    return pl.pallas_call(
        functools.partial(project_kernel, n_x, first, final, widths),
        grid_spec=pltpu.PrefetchScalarGridSpec(
            num_scalar_prefetch=1,
            grid=(depth // tile,),
            in_specs=in_specs,
            out_specs=out_specs,
            scratch_shapes=scratch,
        ),
        out_shape=out_shape,
        compiler_params=pltpu.CompilerParams(vmem_limit_bytes=VMEM_LIMIT),
        cost_estimate=pl.CostEstimate(
            flops=2 * rows * depth * n_x * columns,
            bytes_accessed=depth * n_x * (rows + columns) * 2,
            transcendentals=0,
        ),
    )(places, *operands)


def level_of(differ):
    return differ.bit_length()


def local_kernel(head_size, group, level_count, q_ref, k_ref, v_ref, l_ref, dcol_ref, drow_ref, o_ref):
    rows = q_ref.shape[0]
    heads = q_ref.shape[1] // head_size
    row_id = lax.broadcasted_iota(jnp.int32, (BLOCK, BLOCK), 0)
    col_id = lax.broadcasted_iota(jnp.int32, (BLOCK, BLOCK), 1)
    causal = row_id >= col_id
    for h in range(heads):
        g = h // group
        cols = slice(h * head_size, (h + 1) * head_size)
        kv = slice(g * head_size, (g + 1) * head_size)
        for i in range(rows // BLOCK):
            here = slice(i * BLOCK, (i + 1) * BLOCK)
            width = (i + 1) * BLOCK
            scores = dot_dims(q_ref[here, cols], k_ref[:width, kv], 1, 1)
            d_here = jnp.broadcast_to(dcol_ref[here, h : h + 1], (BLOCK, BLOCK))
            weights = {}
            mixed = []
            for j in range(i + 1):
                level = level_of(i ^ j)
                if level not in weights:
                    column = h * level_count + level
                    weights[level] = jnp.broadcast_to(
                        l_ref[here, column : column + 1], (BLOCK, BLOCK)
                    )
                there = slice(j * BLOCK, (j + 1) * BLOCK)
                gap = d_here - drow_ref[h : h + 1, there]
                if i == j:
                    gap = jnp.where(causal, gap, -jnp.inf)
                mixed.append((weights[level] * jnp.exp(gap) * scores[:, there]).astype(BF16))
            mixing = mixed[0] if i == 0 else jnp.concatenate(mixed, axis=1)
            o_ref[here, cols] = dot(mixing, v_ref[:width, kv])


def local_attention(q, k, v, level, dcol, drow, head_size, group, level_count):
    rows, width = q.shape
    args = (q, k, v, level, dcol, drow)
    return pl.pallas_call(
        functools.partial(local_kernel, head_size, group, level_count),
        grid=(1,),
        in_specs=[whole(a.shape) for a in args],
        out_specs=whole((rows, width)),
        out_shape=jax.ShapeDtypeStruct((rows, width), F32),
        compiler_params=pltpu.CompilerParams(vmem_limit_bytes=VMEM_LIMIT),
        cost_estimate=pl.CostEstimate(
            flops=4 * rows * rows * width, bytes_accessed=rows * width * 8, transcendentals=rows * rows * 4
        ),
    )(*args)


def finish_kernel(head_size, bits, o_ref, q_ref, c_ref, *refs):
    states, n_ref = refs[:bits], refs[bits]
    heads = q_ref.shape[1] // head_size
    for h in range(heads):
        cols = slice(h * head_size, (h + 1) * head_size)
        total = o_ref[:, cols]
        q = q_ref[:, cols]
        for b in range(bits):
            column = h * bits + b
            total = total + c_ref[:, column : column + 1] * dot(q, states[b][cols, :])
        mean = jnp.mean(total * total, axis=-1, keepdims=True)
        n_ref[:, cols] = (total * lax.rsqrt(mean + 1e-05)).astype(BF16)


def finish(local, q, coef, states, head_size):
    rows, width = q.shape
    bits = len(states)
    args = (local, q, coef, *states)
    return pl.pallas_call(
        functools.partial(finish_kernel, head_size, bits),
        grid=(1,),
        in_specs=[whole(a.shape) for a in args],
        out_specs=whole((rows, width)),
        out_shape=jax.ShapeDtypeStruct((rows, width), BF16),
        compiler_params=pltpu.CompilerParams(vmem_limit_bytes=VMEM_LIMIT),
        cost_estimate=pl.CostEstimate(
            flops=2 * rows * width * head_size * bits, bytes_accessed=rows * width * 8, transcendentals=0
        ),
    )(*args)


def out_kernel(place, n0_ref, n1_ref, w0_ref, w1_ref, o_ref):
    o_ref[...] = (dot(n0_ref[...], w0_ref[...]) + dot(n1_ref[...], w1_ref[...])).astype(o_ref.dtype)


def out_block(n0, n1, w_out, w1, place, dtype, tile=256):
    rows, depth = n0.shape
    columns = w1.shape[1]
    steps = columns // tile
    return pl.pallas_call(
        out_kernel,
        grid_spec=pltpu.PrefetchScalarGridSpec(
            num_scalar_prefetch=1,
            grid=(steps,),
            in_specs=[
                whole((rows, depth)),
                whole((rows, depth)),
                pl.BlockSpec((depth, tile), lambda s, p: (0, p[0] * steps + s)),
                pl.BlockSpec((depth, tile), lambda s, p: (0, s)),
            ],
            out_specs=pl.BlockSpec((rows, tile), lambda s, p: (0, s)),
        ),
        out_shape=jax.ShapeDtypeStruct((rows, columns), dtype),
        compiler_params=pltpu.CompilerParams(vmem_limit_bytes=VMEM_LIMIT),
        cost_estimate=pl.CostEstimate(
            flops=4 * rows * columns * depth, bytes_accessed=(rows + depth) * columns * 4, transcendentals=0
        ),
    )(place, n0, n1, w_out, w1)


def body(tokens, log_decay, w_query, w_key, w_value, w_level, w_out):
    rows, shard = tokens.shape
    heads = log_decay.shape[1]
    head_size = w_out.shape[0] // heads
    level_count = w_level.shape[1] // heads
    group = heads // (w_key.shape[1] // head_size)
    seq_size = lax.axis_size("seq")
    seq_bits = seq_size.bit_length() - 1
    local_levels = level_count - seq_bits
    me = lax.axis_index("tp")
    slab = lax.axis_index("seq")
    ws = (w_query, w_key, w_value, w_level)

    def swap_tp(x, bit):
        return lax.ppermute(x, "tp", [(i, i ^ bit) for i in range(4)])

    def swap_seq(x, bit):
        return lax.ppermute(x, "seq", [(i, i ^ bit) for i in range(seq_size)])

    parts = 2
    depth = shard // parts
    far = [swap_tp(tokens[:, p * depth : (p + 1) * depth], 2) for p in range(parts)]
    near = swap_tp(tokens, 1)
    far_near = [swap_tp(x, 1) for x in far]

    dcol = jnp.cumsum(log_decay, axis=0)
    drow = dcol.T
    slab_total = dcol[rows - 1]
    keep = jnp.exp(slab_total[None, :] - dcol)
    group_total, before = slab_total, jnp.zeros_like(slab_total)
    fades, spans = [], []
    for b in range(seq_bits):
        upper = (jnp.right_shift(slab, b) & 1) == 1
        other_total = swap_seq(group_total, 1 << b)
        spans.append(jnp.where(upper, before, -jnp.inf))
        fades.append((upper, jnp.exp(jnp.where(upper, group_total, other_total))))
        before = before + jnp.where(upper, other_total, 0.0)
        group_total = group_total + other_total
    span = jnp.exp(dcol[:, :, None] + jnp.stack(spans, axis=-1)[None])

    mine = me.astype(jnp.int32)
    near_places = jnp.stack([mine, mine ^ 1])
    far_places = jnp.stack([mine ^ 2, mine ^ 3])
    total = project((tokens, near), near_places, ws, 0, 256, None, None, head_size)
    for p in range(parts):
        last = p == parts - 1
        total = project(
            (far[p], far_near[p]), far_places, ws, p * depth, 256, total, keep if last else None, head_size
        )
    q, k, v, level, state = total

    earlier = []
    for b in range(seq_bits):
        other = swap_seq(state, 1 << b)
        earlier.append(other)
        if b < seq_bits - 1:
            upper, fade = fades[b]
            rows_fade = jnp.repeat(fade, head_size)[:, None]
            last = jnp.where(upper, state, other).astype(F32)
            first = jnp.where(upper, other, state).astype(F32)
            state = (last + rows_fade * first).astype(BF16)

    local = local_attention(q, k, v, level, dcol, drow, head_size, group, level_count)
    remote_level = level.reshape(rows, heads, level_count)[:, :, local_levels:]
    coef = (remote_level * span).reshape(rows, heads * seq_bits)
    normed = finish(local, q, coef, earlier, head_size)

    def columns_of(place):
        return lax.dynamic_slice_in_dim(w_out, place * shard, shard, axis=1)

    w_far = swap_tp(columns_of(mine ^ 3), 1)
    w_here = swap_tp(columns_of(mine ^ 1), 1)
    normed_near = swap_tp(normed, 1)
    for_far = out_block(normed, normed_near, w_out, w_far, (mine ^ 2)[None], BF16)
    arrived = swap_tp(for_far, 2)
    here = out_block(normed, normed_near, w_out, w_here, mine[None], F32)
    return (here + arrived.astype(F32)).astype(BF16)


def solution(mesh):
    in_specs = (
        P("seq", "tp"),
        P("seq", "tp"),
        P(None, "tp"),
        P(None, "tp"),
        P(None, "tp"),
        P(None, "tp"),
        P("tp", None),
    )
    out_specs = P("seq", "tp")
    return jax.shard_map(body, mesh=mesh, in_specs=in_specs, out_specs=out_specs, check_vma=False)
```

time: 167 us -> 107 us (0.64)
  blocking collectives: 43.8 us -> 0 us
  matrix products: 31.2 us -> 0 us
  Pallas kernels: 0 us -> 23.2 us
  waiting for transfers between devices: 68 us -> 45.2 us
  starting transfers between devices: 0.08 us -> 15.7 us
  between operations: 14 us -> 0.24 us
  local copies, waits for them, and re-layouts: 6.75 us -> 18.2 us
  other arithmetic: 2.55 us -> 4.45 us
    ppermute x0 -> x14, waiting for transfers between devices: none -> 45.2 us  [the longest x9 38.1 us: swap_tp(): return lax.ppermute(x, 'tp', [(i, i ^ bit) for i in range(4)])]
    reduce_scatter x1 -> x0, waiting for transfers between devices: 43.1 us -> none  [body(): lax.psum_scatter(partial_out.astype(jnp.bfloat16), 'tp', scatter_dimensio...]
    dot_general x13 -> x0, matrix products: 31.2 us -> none  [the longest x4 16.3 us: body(): jnp.dot(piece, matrix, preferred_element_type=jnp.float32)]
    all_gather x2 -> x0, waiting for transfers between devices: 24.1 us -> none  [the longest x1 12.2 us: body(): piece = lax.all_gather(tokens, 'tp', axis=1, tiled=True)]
    pallas_call x0 -> x7, Pallas kernels: none -> 23.2 us  [the longest x3 13.8 us: project(): pl.pallas_call(functools.partial(project_kernel, n_x, first, final, width...]
    all_gather x1 -> x0, blocking collectives: 22.1 us -> none  [prefix(): gathered = lax.all_gather(part, axis)]
    unnamed x1 -> x0, blocking collectives: 21.6 us -> none
    ppermute x0 -> x14, starting transfers between devices: none -> 15.7 us  [the longest x5 10.5 us: swap_seq(): return lax.ppermute(x, 'seq', [(i, i ^ bit) for i in range(seq_size)])]
  transfers between devices with their start and end apart: 3 -> 14, of which waited for: 3 -> 7; matrix products, arithmetic and copies ran while one was open for 11% -> 11% of each run, Pallas kernels for 0% -> 22%
where the time goes in v1:
time: 107 us
  waiting for transfers between devices  45.2 us (42%)
  Pallas kernels  23.2 us (22%)
  local copies, waits for them, and re-layouts  18.2 us (17%)
  starting transfers between devices  15.7 us (15%)
  other arithmetic  4.45 us (4%)
    ppermute x9, waiting for transfers between devices, swap_tp(): return lax.ppermute(x, 'tp', [(i, i ^ bit) for i in range(4)])  38.1 us
    pallas_call x3, Pallas kernels, project(): pl.pallas_call(functools.partial(project_kernel, n_x, first, final, width...  13.8 us
    ppermute x5, starting transfers between devices, swap_seq(): return lax.ppermute(x, 'seq', [(i, i ^ bit) for i in range(seq_size)])  10.5 us
    unnamed x34, local copies, waits for them, and re-layouts  9.91 us
    ppermute x5, waiting for transfers between devices, swap_seq(): return lax.ppermute(x, 'seq', [(i, i ^ bit) for i in range(seq_size)])  7.07 us
    pallas_call x2, Pallas kernels, out_block(): pl.pallas_call(out_kernel, grid_spec=pltpu.PrefetchScalarGridSpec(num_sca...  5.66 us
    ppermute x9, starting transfers between devices, swap_tp(): return lax.ppermute(x, 'tp', [(i, i ^ bit) for i in range(4)])  5.16 us
    dynamic_slice x1, local copies, waits for them, and re-layouts, columns_of(): return lax.dynamic_slice_in_dim(w_out, place * shard, shard, axis=1)  3.21 us
  transfers between devices with their start and end apart: 14, of which 7 were waited for; matrix products, arithmetic and copies ran while one was open for 11% of the time, Pallas kernels for 22%

profile of v1, /device:TPU:0, one launch (start us, length us, event | category | flops | bytes accessed | tf_op | source)
XLA Modules:
  0.0 106.9 jit_solution(18246576672406560280)
XLA Ops:
  0.5 2.3 %fusion.6 = (bf16[512,512]{1,0:T(8,128)(2,1)}, bf16[512,512]{1,0:T(8,128)(2,1)}) fusion(bf16[512,1024]{1,0:T(8,128)(2,1)} %refs_0_.1), kind=kLoop, calls=%fused_computation.28 | loop fusion | bytes 2097152 | tf_op jit(solution)/shard_map/slice | solution.py:270
  2.7 2.5 %collective-permute-start.2 = (bf16[512,512]{1,0:T(8,128)(2,1)}, bf16[512,512]{1,0:T(8,128)(2,1)}, u32[]{:S(2)}, u32[]{:S(2)}) collective-permute-start(bf16[512,512]{1,0:T(8,128)(2,1)} %get-tuple-element.17), channel_id=1, source_target_pairs={{0,2},{1,3},{2,0},{3,1},{4,6},{5,7},{6,4},{7,5},{8,10},{9,11},{10,... | collective-permute-start | bytes 1572872 | tf_op jit(solution)/shard_map/ppermute | solution.py:263
  7.1 2.0 %collective-permute-start.5 = (f32[4]{0:T(128)S(1)}, f32[4]{0:T(128)S(1)}, u32[]{:S(2)}, u32[]{:S(2)}) collective-permute-start(f32[4]{0:T(128)S(1)} %slice_reduce_fusion.1), channel_id=1, source_target_pairs={{0,4},{4,0},{8,12},{12,8},{16,20},{20,16},{24,28},{28,24},{1,5},{5... | collective-permute-start | bytes 56 | tf_op jit(solution)/shard_map/ppermute | solution.py:266
  9.1 3.2 %constant_dynamic-slice_fusion = (bf16[512,1024]{1,0:T(8,128)(2,1)}, bf16[512,1024]{1,0:T(8,128)(2,1)}) fusion(bf16[512,4096]{1,0:T(8,128)(2,1)} %w0_ref.3, s32[]{:T(128)S(6)} %select_n.84, s32[]{:T(128)S(6)} %select_n.83), kind=kLoop, calls=%fused_computation.24 | loop fusion | bytes 4194312 | tf_op jit(solution)/shard_map/dynamic_slice | solution.py:317
  14.1 4.2 %collective-permute-done.2.refs_0_ = bf16[512,512]{1,0:T(8,128)(2,1)} collective-permute-done((bf16[512,512]{1,0:T(8,128)(2,1)}, bf16[512,512]{1,0:T(8,128)(2,1)}, u32[]{:S(2)}, u32[]{:S(2)}) %collective-permute-start.2) | collective-permute-done | bytes 524320 | tf_op jit(solution)/shard_map/ppermute | solution.py:263
  18.3 11.0 %collective-permute-done.refs_0_ = bf16[512,512]{1,0:T(8,128)(2,1)} collective-permute-done((bf16[512,512]{1,0:T(8,128)(2,1)}, bf16[512,512]{1,0:T(8,128)(2,1)}, u32[]{:S(2)}, u32[]{:S(2)}) %collective-permute-start) | collective-permute-done | bytes 524320 | tf_op jit(solution)/shard_map/ppermute | solution.py:263
  29.4 1.8 %collective-permute-start.6 = (f32[4]{0:T(128)S(1)}, f32[4]{0:T(128)S(1)}, u32[]{:S(2)}, u32[]{:S(2)}) collective-permute-start(f32[4]{0:T(128)S(1)} %get-tuple-element.22), channel_id=1, source_target_pairs={{0,8},{4,12},{8,0},{12,4},{16,24},{20,28},{24,16},{28,20},{1,9},{5... | collective-permute-start | bytes 56 | tf_op jit(solution)/shard_map/ppermute | solution.py:266
  31.2 1.7 %collective-permute-done.6 = f32[4]{0:T(128)S(1)} collective-permute-done((f32[4]{0:T(128)S(1)}, f32[4]{0:T(128)S(1)}, u32[]{:S(2)}, u32[]{:S(2)}) %collective-permute-start.6) | collective-permute-done | bytes 48 | tf_op jit(solution)/shard_map/ppermute | solution.py:266
  33.0 2.2 %copy-done = bf16[4096,512]{1,0:T(8,128)(2,1)S(1)} copy-done((bf16[4096,512]{1,0:T(8,128)(2,1)S(1)}, bf16[4096,512]{1,0:T(8,128)(2,1)}, u32[]{:S(2)}) %copy-start) | copy-done | bytes 4194328
  36.4 5.6 %shard_map.73.refs_10_ = f32[512,792]{1,0:T(8,128)S(1)} custom-call(s32[2]{0:T(128)S(1)} %pad_add_fusion.1.place, bf16[512,1024]{1,0:T(8,128)(2,1)S(1)} %copy-done.5, bf16[512,1024]{1,0:T(8,128)(2,1)} %collective-permute-done.4.refs_1_, bf16[4096,512]{1,0:T(8,128)(2,1)S(1)} %copy-done, bf16[4096,128]{1,0:T(8,128)(2,1)S(1)} %copy-done.2, ...), custom_call_target="tpu_custom_call" | custom-call | flops 1660944384 | bytes 5341184 | tf_op jit(solution)/shard_map/pallas_call | solution.py:117
  42.1 3.4 %shard_map.74.refs_10_ = f32[512,792]{1,0:T(8,128)S(1)} custom-call(s32[2]{0:T(128)S(1)} %pad_add_fusion.place, bf16[512,512]{1,0:T(8,128)(2,1)} %collective-permute-done.2.refs_0_, bf16[512,512]{1,0:T(8,128)(2,1)S(1)} %collective-permute-done.3.refs_1_, bf16[4096,512]{1,0:T(8,128)(2,1)S(1)} %copy-done.1, bf16[4096,128]{1,0:T(8,128)(2,1)S(1)} %copy-done.2, ...), custom_call_target="tpu_custom_call" | custom-call | flops 830472192 | bytes 2670592 | tf_op jit(solution)/shard_map/pallas_call | solution.py:117
  45.5 4.9 %shard_map.75 = (bf16[512,512]{1,0:T(8,128)(2,1)S(1)}, bf16[512,128]{1,0:T(8,128)(2,1)S(1)}, bf16[512,128]{1,0:T(8,128)(2,1)S(1)}, f32[512,24]{1,0:T(8,128)S(1)}, bf16[512,128]{1,0:T(8,128)(2,1)}) custom-call(s32[2]{0:T(128)S(1)} %pad_add_fusion.place, bf16[512,512]{1,0:T(8,128)(2,1)} %collective-permute-done.refs_0_, ...), custom_call_target="tpu_custom_call" | custom-call | flops 830472192 | bytes 2670592 | tf_op jit(solution)/shard_map/pallas_call | solution.py:117
  52.5 1.7 %collective-permute-start.7 = (bf16[512,128]{1,0:T(8,128)(2,1)}, bf16[512,128]{1,0:T(8,128)(2,1)S(1)}, u32[]{:S(2)}, u32[]{:S(2)}) collective-permute-start(bf16[512,128]{1,0:T(8,128)(2,1)} %get-tuple-element.14), channel_id=1, source_target_pairs={{0,4},{4,0},{8,12},{12,8},{16,20},{20,16},{24,28},{28,24},{1,5},{5... | collective-permute-start | bytes 393224 | tf_op jit(solution)/shard_map/ppermute | solution.py:266
  54.4 3.3 %collective-permute-done.7.refs_0_ = bf16[512,128]{1,0:T(8,128)(2,1)S(1)} collective-permute-done((bf16[512,128]{1,0:T(8,128)(2,1)}, bf16[512,128]{1,0:T(8,128)(2,1)S(1)}, u32[]{:S(2)}, u32[]{:S(2)}) %collective-permute-start.7) | collective-permute-done | bytes 131104 | tf_op jit(solution)/shard_map/ppermute | solution.py:266
  58.8 1.9 %collective-permute-start.8 = (bf16[512,128]{1,0:T(8,128)(2,1)S(1)}, bf16[512,128]{1,0:T(8,128)(2,1)S(1)}, u32[]{:S(2)}, u32[]{:S(2)}) collective-permute-start(bf16[512,128]{1,0:T(8,128)(2,1)S(1)} %add_convert_fusion.2), channel_id=1, source_target_pairs={{0,8},{4,12},{8,0},{12,4},{16,24},{20,28},{24,16},{28,20},{1,9},{5... | collective-permute-start | bytes 393224 | tf_op jit(solution)/shard_map/ppermute | solution.py:266
  61.8 2.0 %collective-permute-done.8.refs_1_ = bf16[512,128]{1,0:T(8,128)(2,1)S(1)} collective-permute-done((bf16[512,128]{1,0:T(8,128)(2,1)S(1)}, bf16[512,128]{1,0:T(8,128)(2,1)S(1)}, u32[]{:S(2)}, u32[]{:S(2)}) %collective-permute-start.8) | collective-permute-done | bytes 131104 | tf_op jit(solution)/shard_map/ppermute | solution.py:266
  64.0 3.1 %collective-permute-start.9 = (bf16[512,128]{1,0:T(8,128)(2,1)S(1)}, bf16[512,128]{1,0:T(8,128)(2,1)S(1)}, u32[]{:S(2)}, u32[]{:S(2)}) collective-permute-start(bf16[512,128]{1,0:T(8,128)(2,1)S(1)} %add_convert_fusion.1), channel_id=1, source_target_pairs={{0,16},{4,20},{8,24},{12,28},{16,0},{20,4},{24,8},{28,12},{1,17},{... | collective-permute-start | bytes 393224 | tf_op jit(solution)/shard_map/ppermute | solution.py:266
  71.2 2.3 %shard_map.76.o_ref = f32[512,512]{1,0:T(8,128)S(1)} custom-call(bf16[512,512]{1,0:T(8,128)(2,1)S(1)} %copy-done.7, bf16[512,128]{1,0:T(8,128)(2,1)S(1)} %get-tuple-element.11.k_ref, bf16[512,128]{1,0:T(8,128)(2,1)S(1)} %copy-done.12, f32[512,24]{1,0:T(8,128)S(1)} %copy-done.10, f32[512,4]{1,0:T(8,128)S(1)} %copy-done.8, f32[4,512]{1,0:T(4,128)S(1)} %bitcast.34), custom_call_target="tpu_custom_call" | custom-call | flops 536870912 | bytes 2097152 | tf_op jit(solution)/shard_map/pallas_call | solution.py:176
  73.5 1.4 %shard_map.77.n0_ref = bf16[512,512]{1,0:T(8,128)(2,1)S(1)} custom-call(f32[512,512]{1,0:T(8,128)S(1)} %shard_map.76.o_ref, bf16[512,512]{1,0:T(8,128)(2,1)S(1)} %copy-done.7, f32[512,12]{1,0:T(8,128)S(1)} %copy.28.c_ref, bf16[512,128]{1,0:T(8,128)(2,1)S(1)} %collective-permute-done.7.refs_0_, bf16[512,128]{1,0:T(8,128)(2,1)S(1)} %collective-permute-done.8.refs_1_, ...), custom_call_target="tpu_custom_call" | custom-call | flops 201326592 | bytes 2097152 | tf_op jit(solution)/shard_map/pallas_call | solution.py:207
  75.5 1.4 %collective-permute-done.10.n1_ref = bf16[512,512]{1,0:T(8,128)(2,1)S(1)} collective-permute-done((bf16[512,512]{1,0:T(8,128)(2,1)S(1)}, bf16[512,512]{1,0:T(8,128)(2,1)S(1)}, u32[]{:S(2)}, u32[]{:S(2)}) %collective-permute-start.10) | collective-permute-done | bytes 524320 | tf_op jit(solution)/shard_map/ppermute | solution.py:263
  76.9 3.4 %shard_map.79 = bf16[512,1024]{1,0:T(8,128)(2,1)S(1)} custom-call(s32[1]{0:T(128)} %bitcast.1.place, bf16[512,512]{1,0:T(8,128)(2,1)S(1)} %shard_map.77.n0_ref, bf16[512,512]{1,0:T(8,128)(2,1)S(1)} %collective-permute-done.10.n1_ref, bf16[512,4096]{1,0:T(8,128)(2,1)S(1)} %copy-done.4, bf16[512,1024]{1,0:T(8,128)(2,1)} %collective-permute-done.12.w1_ref), custom_call_target="tpu_custom_call" | custom-call | flops 1073741824 | bytes 4194304 | tf_op jit(solution)/shard_map/pallas_call | solution.py:228
  80.3 1.6 %collective-permute-start.13 = (bf16[512,1024]{1,0:T(8,128)(2,1)S(1)}, bf16[512,1024]{1,0:T(8,128)(2,1)S(1)}, u32[]{:S(2)}, u32[]{:S(2)}) collective-permute-start(bf16[512,1024]{1,0:T(8,128)(2,1)S(1)} %shard_map.79), channel_id=1, source_target_pairs={{0,2},{1,3},{2,0},{3,1},{4,6},{5,7},{6,4},{7,5},{8,10},{9,11},{10,... | collective-permute-start | bytes 3145736 | tf_op jit(solution)/shard_map/ppermute | solution.py:263
  81.9 2.2 %shard_map.78 = f32[512,1024]{1,0:T(8,128)S(1)} custom-call(s32[1]{0:T(128)} %bitcast.place, bf16[512,512]{1,0:T(8,128)(2,1)S(1)} %shard_map.77.n0_ref, bf16[512,512]{1,0:T(8,128)(2,1)S(1)} %collective-permute-done.10.n1_ref, bf16[512,4096]{1,0:T(8,128)(2,1)S(1)} %copy-done.4, bf16[512,1024]{1,0:T(8,128)(2,1)S(1)} %collective-permute-done.11.w1_ref), custom_call_target="tpu_custom_call" | custom-call | flops 1073741824 | bytes 4194304 | tf_op jit(solution)/shard_map/pallas_call | solution.py:228
  84.2 21.5 %collective-permute-done.13 = bf16[512,1024]{1,0:T(8,128)(2,1)S(1)} collective-permute-done((bf16[512,1024]{1,0:T(8,128)(2,1)S(1)}, bf16[512,1024]{1,0:T(8,128)(2,1)S(1)}, u32[]{:S(2)}, u32[]{:S(2)}) %collective-permute-start.13) | collective-permute-done | bytes 1048608 | tf_op jit(solution)/shard_map/ppermute | solution.py:263
  (73 shorter events, 16.1 us)
Async XLA Ops:
  0.0 5.3 %copy-start.15 = (f32[512,4]{0,1:T(4,128)S(1)}, f32[512,4]{0,1:T(4,128)}, u32[]{:S(2)}) copy-start(f32[512,4]{0,1:T(4,128)} %param.8) | copy-start | bytes 24580
  0.0 33.0 %collective-permute-start.4 = (bf16[512,1024]{1,0:T(8,128)(2,1)}, bf16[512,1024]{1,0:T(8,128)(2,1)}, u32[]{:S(2)}, u32[]{:S(2)}) collective-permute-start(bf16[512,1024]{1,0:T(8,128)(2,1)} %refs_0_.1), channel_id=1, source_target_pairs={{0,1},{1,0},{2,3},{3,2},{4,5},{5,4},{6,7},{7,6},{8,9},{9,8},{10,11... | collective-permute-start | bytes 3145736 | tf_op jit(solution)/shard_map/ppermute | solution.py:263
  2.7 15.6 %collective-permute-start.2 = (bf16[512,512]{1,0:T(8,128)(2,1)}, bf16[512,512]{1,0:T(8,128)(2,1)}, u32[]{:S(2)}, u32[]{:S(2)}) collective-permute-start(bf16[512,512]{1,0:T(8,128)(2,1)} %get-tuple-element.17), channel_id=1, source_target_pairs={{0,2},{1,3},{2,0},{3,1},{4,6},{5,7},{6,4},{7,5},{8,10},{9,11},{10,... | collective-permute-start | bytes 1572872 | tf_op jit(solution)/shard_map/ppermute | solution.py:263
  5.2 24.1 %collective-permute-start = (bf16[512,512]{1,0:T(8,128)(2,1)}, bf16[512,512]{1,0:T(8,128)(2,1)}, u32[]{:S(2)}, u32[]{:S(2)}) collective-permute-start(bf16[512,512]{1,0:T(8,128)(2,1)} %get-tuple-element.18), channel_id=1, source_target_pairs={{0,2},{1,3},{2,0},{3,1},{4,6},{5,7},{6,4},{7,5},{8,10},{9,11},{10,... | collective-permute-start | bytes 1572872 | tf_op jit(solution)/shard_map/ppermute | solution.py:263
  7.1 7.0 %collective-permute-start.5 = (f32[4]{0:T(128)S(1)}, f32[4]{0:T(128)S(1)}, u32[]{:S(2)}, u32[]{:S(2)}) collective-permute-start(f32[4]{0:T(128)S(1)} %slice_reduce_fusion.1), channel_id=1, source_target_pairs={{0,4},{4,0},{8,12},{12,8},{16,20},{20,16},{24,28},{28,24},{1,5},{5... | collective-permute-start | bytes 56 | tf_op jit(solution)/shard_map/ppermute | solution.py:266
  9.1 4.2 %copy-start.14 = (bf16[4096,24]{0,1:T(8,128)(2,1)S(1)}, bf16[4096,24]{0,1:T(8,128)(2,1)}, u32[]{:S(2)}) copy-start(bf16[4096,24]{0,1:T(8,128)(2,1)} %param.12) | copy-start | bytes 589828
  9.1 23.9 %copy-start.2 = (bf16[4096,128]{1,0:T(8,128)(2,1)S(1)}, bf16[4096,128]{1,0:T(8,128)(2,1)}, u32[]{:S(2)}) copy-start(bf16[4096,128]{1,0:T(8,128)(2,1)} %refs_7_.5) | copy-start | bytes 3145732
  9.1 23.9 %copy-start.3 = (bf16[4096,128]{1,0:T(8,128)(2,1)S(1)}, bf16[4096,128]{1,0:T(8,128)(2,1)}, u32[]{:S(2)}) copy-start(bf16[4096,128]{1,0:T(8,128)(2,1)} %refs_8_.5) | copy-start | bytes 3145732
  12.4 63.1 %collective-permute-start.12 = (bf16[512,1024]{1,0:T(8,128)(2,1)}, bf16[512,1024]{1,0:T(8,128)(2,1)}, u32[]{:S(2)}, u32[]{:S(2)}) collective-permute-start(bf16[512,1024]{1,0:T(8,128)(2,1)} %get-tuple-element.15), channel_id=1, source_target_pairs={{0,1},{1,0},{2,3},{3,2},{4,5},{5,4},{6,7},{7,6},{8,9},{9,8},{10,11... | collective-permute-start | bytes 3145736 | tf_op jit(solution)/shard_map/ppermute | solution.py:263
  18.3 23.7 %collective-permute-start.3 = (bf16[512,512]{1,0:T(8,128)(2,1)}, bf16[512,512]{1,0:T(8,128)(2,1)S(1)}, u32[]{:S(2)}, u32[]{:S(2)}) collective-permute-start(bf16[512,512]{1,0:T(8,128)(2,1)} %collective-permute-done.2.refs_0_), channel_id=1, source_target_pairs={{0,1},{1,0},{2,3},{3,2},{4,5},{5,4},{6,7},{7,6},{8,9},{9,8},{10,11... | collective-permute-start | bytes 1572872 | tf_op jit(solution)/shard_map/ppermute | solution.py:263
  29.4 16.1 %collective-permute-start.1 = (bf16[512,512]{1,0:T(8,128)(2,1)}, bf16[512,512]{1,0:T(8,128)(2,1)S(1)}, u32[]{:S(2)}, u32[]{:S(2)}) collective-permute-start(bf16[512,512]{1,0:T(8,128)(2,1)} %collective-permute-done.refs_0_), channel_id=1, source_target_pairs={{0,1},{1,0},{2,3},{3,2},{4,5},{5,4},{6,7},{7,6},{8,9},{9,8},{10,11... | collective-permute-start | bytes 1572872 | tf_op jit(solution)/shard_map/ppermute | solution.py:263
  29.4 3.5 %collective-permute-start.6 = (f32[4]{0:T(128)S(1)}, f32[4]{0:T(128)S(1)}, u32[]{:S(2)}, u32[]{:S(2)}) collective-permute-start(f32[4]{0:T(128)S(1)} %get-tuple-element.22), channel_id=1, source_target_pairs={{0,8},{4,12},{8,0},{12,4},{16,24},{20,28},{24,16},{28,20},{1,9},{5... | collective-permute-start | bytes 56 | tf_op jit(solution)/shard_map/ppermute | solution.py:266
  33.0 2.2 %copy-start = (bf16[4096,512]{1,0:T(8,128)(2,1)S(1)}, bf16[4096,512]{1,0:T(8,128)(2,1)}, u32[]{:S(2)}) copy-start(bf16[4096,512]{1,0:T(8,128)(2,1)} %refs_6_.5) | copy-start | bytes 12582916
  35.2 1.2 %copy-start.5 = (bf16[512,1024]{1,0:T(8,128)(2,1)S(1)}, bf16[512,1024]{1,0:T(8,128)(2,1)}, u32[]{:S(2)}) copy-start(bf16[512,1024]{1,0:T(8,128)(2,1)} %refs_0_.1) | copy-start | bytes 3145732
  36.4 5.6 %copy-start.1 = (bf16[4096,512]{1,0:T(8,128)(2,1)S(1)}, bf16[4096,512]{1,0:T(8,128)(2,1)}, u32[]{:S(2)}) copy-start(bf16[4096,512]{1,0:T(8,128)(2,1)} %refs_6_.5) | copy-start | bytes 12582916
  52.5 5.2 %collective-permute-start.7 = (bf16[512,128]{1,0:T(8,128)(2,1)}, bf16[512,128]{1,0:T(8,128)(2,1)S(1)}, u32[]{:S(2)}, u32[]{:S(2)}) collective-permute-start(bf16[512,128]{1,0:T(8,128)(2,1)} %get-tuple-element.14), channel_id=1, source_target_pairs={{0,4},{4,0},{8,12},{12,8},{16,20},{20,16},{24,28},{28,24},{1,5},{5... | collective-permute-start | bytes 393224 | tf_op jit(solution)/shard_map/ppermute | solution.py:266
  57.7 17.3 %copy-start.13 = (bf16[512,1024]{1,0:T(8,128)(2,1)S(1)}, bf16[512,1024]{1,0:T(8,128)(2,1)}, u32[]{:S(2)}) copy-start(bf16[512,1024]{1,0:T(8,128)(2,1)} %get-tuple-element.16) | copy-start | bytes 3145732
  58.8 5.0 %collective-permute-start.8 = (bf16[512,128]{1,0:T(8,128)(2,1)S(1)}, bf16[512,128]{1,0:T(8,128)(2,1)S(1)}, u32[]{:S(2)}, u32[]{:S(2)}) collective-permute-start(bf16[512,128]{1,0:T(8,128)(2,1)S(1)} %add_convert_fusion.2), channel_id=1, source_target_pairs={{0,8},{4,12},{8,0},{12,4},{16,24},{20,28},{24,16},{28,20},{1,9},{5... | collective-permute-start | bytes 393224 | tf_op jit(solution)/shard_map/ppermute | solution.py:266
  64.0 9.5 %collective-permute-start.9 = (bf16[512,128]{1,0:T(8,128)(2,1)S(1)}, bf16[512,128]{1,0:T(8,128)(2,1)S(1)}, u32[]{:S(2)}, u32[]{:S(2)}) collective-permute-start(bf16[512,128]{1,0:T(8,128)(2,1)S(1)} %add_convert_fusion.1), channel_id=1, source_target_pairs={{0,16},{4,20},{8,24},{12,28},{16,0},{20,4},{24,8},{28,12},{1,17},{... | collective-permute-start | bytes 393224 | tf_op jit(solution)/shard_map/ppermute | solution.py:266
  67.3 1.0 copy-start.7
  71.2 5.7 %copy-start.4 = (bf16[512,4096]{1,0:T(8,128)(2,1)S(1)}, bf16[512,4096]{1,0:T(8,128)(2,1)}, u32[]{:S(2)}) copy-start(bf16[512,4096]{1,0:T(8,128)(2,1)} %w0_ref.3) | copy-start | bytes 12582916
  74.9 2.0 %collective-permute-start.10 = (bf16[512,512]{1,0:T(8,128)(2,1)S(1)}, bf16[512,512]{1,0:T(8,128)(2,1)S(1)}, u32[]{:S(2)}, u32[]{:S(2)}) collective-permute-start(bf16[512,512]{1,0:T(8,128)(2,1)S(1)} %shard_map.77.n0_ref), channel_id=1, source_target_pairs={{0,1},{1,0},{2,3},{3,2},{4,5},{5,4},{6,7},{7,6},{8,9},{9,8},{10,11... | collective-permute-start | bytes 1572872 | tf_op jit(solution)/shard_map/ppermute | solution.py:263
  75.0 6.9 %collective-permute-start.11 = (bf16[512,1024]{1,0:T(8,128)(2,1)S(1)}, bf16[512,1024]{1,0:T(8,128)(2,1)S(1)}, u32[]{:S(2)}, u32[]{:S(2)}) collective-permute-start(bf16[512,1024]{1,0:T(8,128)(2,1)S(1)} %copy-done.13), channel_id=1, source_target_pairs={{0,1},{1,0},{2,3},{3,2},{4,5},{5,4},{6,7},{7,6},{8,9},{9,8},{10,11... | collective-permute-start | bytes 3145736 | tf_op jit(solution)/shard_map/ppermute | solution.py:263
  80.3 25.3 %collective-permute-start.13 = (bf16[512,1024]{1,0:T(8,128)(2,1)S(1)}, bf16[512,1024]{1,0:T(8,128)(2,1)S(1)}, u32[]{:S(2)}, u32[]{:S(2)}) collective-permute-start(bf16[512,1024]{1,0:T(8,128)(2,1)S(1)} %shard_map.79), channel_id=1, source_target_pairs={{0,2},{1,3},{2,0},{3,1},{4,6},{5,7},{6,4},{7,5},{8,10},{9,11},{10,... | collective-permute-start | bytes 3145736 | tf_op jit(solution)/shard_map/ppermute | solution.py:263
  (6 other events, 5.0 us)

commit v2 on v0

v2 whole, which is shorter than its diff:
```python
import functools

import jax
import jax.numpy as jnp
from jax import lax
from jax.experimental import pallas as pl
from jax.experimental.pallas import tpu as pltpu
from jax.sharding import PartitionSpec as P

BLOCK = 128
F32 = jnp.float32
BF16 = jnp.bfloat16
VMEM = pl.BlockSpec(memory_space=pltpu.VMEM)
SMEM = pl.BlockSpec(memory_space=pltpu.SMEM)
ANY = pl.BlockSpec(memory_space=pl.ANY)


def dot(a, b):
    return jnp.dot(a, b, preferred_element_type=F32)


def dot_dims(a, b, left, right):
    return lax.dot_general(a, b, (((left,), (right,)), ((), ())), preferred_element_type=F32)


def shape(dims, dtype):
    return jax.ShapeDtypeStruct(dims, dtype)


def call(kernel, ins, outs, flops, after=(), smem=0, aliases=None, megabytes=8):
    count = len(ins)

    def run(*refs):
        kernel(*refs[:count], *refs[count + len(after) :])

    nbytes = sum(x.size * x.dtype.itemsize for x in (*ins, *outs)) if flops else 0
    return pl.pallas_call(
        run,
        in_specs=[SMEM] * smem + [VMEM] * (count - smem) + [ANY] * len(after),
        out_specs=[VMEM] * len(outs),
        out_shape=list(outs),
        input_output_aliases=aliases or {},
        compiler_params=pltpu.CompilerParams(vmem_limit_bytes=megabytes * 1024 * 1024),
        cost_estimate=pl.CostEstimate(flops=flops, bytes_accessed=nbytes, transcendentals=0),
    )(*ins, *after)


def gate(x, *after):
    def run(*refs):
        pass

    return pl.pallas_call(
        run,
        in_specs=[ANY] * (1 + len(after)),
        out_specs=ANY,
        out_shape=shape(x.shape, x.dtype),
        input_output_aliases={0: 0},
        compiler_params=pltpu.CompilerParams(vmem_limit_bytes=1024 * 1024),
        cost_estimate=pl.CostEstimate(flops=0, bytes_accessed=0, transcendentals=0),
    )(x, *after)


def rows_of(w_ref, start, depth):
    return w_ref[pl.ds(pl.multiple_of(start, 128), depth), :]


def add_products(places, xs, w_ref, offset):
    shard = w_ref.shape[0] // 4
    total = None
    for i, x_ref in enumerate(xs):
        depth = x_ref.shape[1]
        add = dot(x_ref[...], rows_of(w_ref, places[i] * shard + offset, depth))
        total = add if total is None else total + add
    return total


def add_keys_values(places, xs, wk_ref, wv_ref, offset):
    shard = wk_ref.shape[0] // 4
    total = None
    for i, x_ref in enumerate(xs):
        depth = x_ref.shape[1]
        start = places[i] * shard + offset
        w = jnp.concatenate([rows_of(wk_ref, start, depth), rows_of(wv_ref, start, depth)], axis=1)
        add = dot(x_ref[...], w)
        total = add if total is None else total + add
    return total


def project(places, xs, ws, offset, totals, after=()):
    rows = xs[0].shape[0]
    n_x = len(xs)
    wq, wk, wv, wl = ws
    widths = (wq.shape[1], wk.shape[1] + wv.shape[1], wl.shape[1])

    def kernel(p, *refs):
        x, (q_ref, k_ref, v_ref, l_ref), rest = refs[:n_x], refs[n_x : n_x + 4], refs[n_x + 4 :]
        ins, outs = (rest[:3], rest[3:]) if totals is not None else (None, rest)
        kv = add_keys_values(p, x, k_ref, v_ref, offset)
        outs[1][...] = kv if ins is None else ins[1][...] + kv
        q = add_products(p, x, q_ref, offset)
        outs[0][...] = q if ins is None else ins[0][...] + q
        level = add_products(p, x, l_ref, offset)
        outs[2][...] = level if ins is None else ins[2][...] + level

    ins = [places, *xs, *ws]
    aliases = {}
    if totals is not None:
        aliases = {len(ins) + i: i for i in range(3)}
        ins += list(totals)
    outs = [shape((rows, w), F32) for w in widths]
    return call(kernel, ins, outs, 0, after, smem=1, aliases=aliases)


def project_state(places, xs, wk, wv, offset, total_kv, keep, head_size):
    rows, depth = xs[0].shape
    n_x = len(xs)
    heads = keep.shape[1]
    kv_width = wk.shape[1]
    group = heads // (kv_width // head_size)

    def kernel(p, *refs):
        x, (wk_ref, wv_ref, total_ref, keep_ref, k_out, v_out, s_out) = refs[:n_x], refs[n_x:]
        total = total_ref[...] + add_keys_values(p, x, wk_ref, wv_ref, offset)
        keys = total[:, :kv_width].astype(BF16)
        values = total[:, kv_width:].astype(BF16)
        k_out[...] = keys
        v_out[...] = values
        for g in range(kv_width // head_size):
            cols = slice(g * head_size, (g + 1) * head_size)
            kf = keys[:, cols].astype(F32)
            weighted = jnp.concatenate(
                [(kf * keep_ref[:, h : h + 1]).astype(BF16) for h in range(g * group, (g + 1) * group)],
                axis=1,
            )
            wide = slice(g * group * head_size, (g + 1) * group * head_size)
            s_out[:, wide] = dot_dims(values[:, cols], weighted, 0, 0).astype(BF16)

    outs = [
        shape((rows, kv_width), BF16),
        shape((rows, kv_width), BF16),
        shape((head_size, heads * head_size), BF16),
    ]
    flops = 4 * rows * depth * n_x * kv_width + 2 * rows * heads * head_size**2
    return call(kernel, [places, *xs, wk, wv, total_kv, keep], outs, flops, smem=1)


def attend(places, xs, wq, wl, offset, total_q, total_l, k, v, dcol, drow, head_size, level_count):
    rows, width = total_q.shape
    n_x = len(xs)
    heads = width // head_size
    group = heads // (k.shape[1] // head_size)

    def kernel(p, *refs):
        x, refs = refs[:n_x], refs[n_x:]
        wq_ref, wl_ref, tq_ref, tl_ref, k_ref, v_ref, dcol_ref, drow_ref, q_ref, l_ref, o_ref = refs
        raw = tl_ref[...] + add_products(p, x, wl_ref, offset)
        l_ref[...] = jnp.maximum(raw, 0.0) + jnp.log1p(jnp.exp(-jnp.abs(raw)))
        q_ref[...] = (tq_ref[...] + add_products(p, x, wq_ref, offset)).astype(BF16)
        row_id = lax.broadcasted_iota(jnp.int32, (BLOCK, BLOCK), 0)
        col_id = lax.broadcasted_iota(jnp.int32, (BLOCK, BLOCK), 1)
        causal = row_id >= col_id
        for h in range(heads):
            g = h // group
            cols = slice(h * head_size, (h + 1) * head_size)
            kv = slice(g * head_size, (g + 1) * head_size)
            for i in range(rows // BLOCK):
                here = slice(i * BLOCK, (i + 1) * BLOCK)
                span = (i + 1) * BLOCK
                scores = dot_dims(q_ref[here, cols], k_ref[:span, kv], 1, 1)
                d_here = jnp.broadcast_to(dcol_ref[here, h : h + 1], (BLOCK, BLOCK))
                weights = {}
                mixed = []
                for j in range(i + 1):
                    level = (i ^ j).bit_length()
                    if level not in weights:
                        column = h * level_count + level
                        weights[level] = jnp.broadcast_to(
                            l_ref[here, column : column + 1], (BLOCK, BLOCK)
                        )
                    there = slice(j * BLOCK, (j + 1) * BLOCK)
                    gap = d_here - drow_ref[h : h + 1, there]
                    if i == j:
                        gap = jnp.where(causal, gap, -jnp.inf)
                    mixed.append((weights[level] * jnp.exp(gap) * scores[:, there]).astype(BF16))
                mixing = mixed[0] if i == 0 else jnp.concatenate(mixed, axis=1)
                o_ref[here, cols] = dot(mixing, v_ref[:span, kv])

    ins = [places, *xs, wq, wl, total_q, total_l, k, v, dcol, drow]
    outs = [shape((rows, width), BF16), shape(total_l.shape, F32), shape((rows, width), F32)]
    flops = 2 * rows * xs[0].shape[1] * n_x * width + 4 * rows * rows * width
    return call(kernel, ins, outs, flops, smem=1)


def finish(local, q, level, span, states, rows, head_size, level_count, after=()):
    width = q.shape[1]
    heads = width // head_size
    bits = len(states)
    own_levels = level_count - bits

    def kernel(o_ref, q_ref, l_ref, c_ref, *refs):
        state_refs, n_ref = refs[:bits], refs[bits]
        for h in range(heads):
            cols = slice(h * head_size, (h + 1) * head_size)
            total = o_ref[rows, cols]
            query = q_ref[rows, cols]
            for b in range(bits):
                at = h * level_count + own_levels + b
                factor = l_ref[rows, at : at + 1] * c_ref[rows, h * bits + b : h * bits + b + 1]
                total = total + factor * dot_dims(query, state_refs[b][:, cols], 1, 1)
            mean = jnp.mean(total * total, axis=-1, keepdims=True)
            n_ref[:, cols] = (total * lax.rsqrt(mean + 1e-05)).astype(BF16)

    count = rows.stop - rows.start
    outs = [shape((count, width), BF16)]
    flops = 2 * count * width * head_size * bits
    return call(kernel, [local, q, level, span, *states], outs, flops, after)[0]


def out_block(n0s, n1s, w0, w1, dtype, after=()):
    columns = w0.shape[1]
    count = len(n0s)
    rows = sum(n.shape[0] for n in n0s)
    tile = min(columns, 512)

    def kernel(*refs):
        first, second = refs[:count], refs[count : 2 * count]
        w0_ref, w1_ref, o_ref = refs[2 * count :]
        at = 0
        for a_ref, b_ref in zip(first, second):
            here = slice(at, at + a_ref.shape[0])
            at += a_ref.shape[0]
            for c in range(0, columns, tile):
                cols = slice(c, c + tile)
                o_ref[here, cols] = (
                    dot(a_ref[...], w0_ref[:, cols]) + dot(b_ref[...], w1_ref[:, cols])
                ).astype(o_ref.dtype)

    flops = 4 * rows * columns * w0.shape[0]
    return call(kernel, [*n0s, *n1s, w0, w1], [shape((rows, columns), dtype)], flops, after)[0]


def add_rows(here, arrived, out, start):
    count, columns = arrived.shape
    block = start // count

    def kernel(h_ref, a_ref, *refs):
        o_ref = refs[-1]
        o_ref[...] = (h_ref[...] + a_ref[...].astype(F32)).astype(BF16)

    spec = pl.BlockSpec((count, columns), lambda s: (block, 0))
    ins, specs, aliases = [here, arrived], [spec, pl.BlockSpec((count, columns), lambda s: (0, 0))], {}
    if out is not None:
        ins, specs, aliases = ins + [out], specs + [ANY], {2: 0}
    return pl.pallas_call(
        kernel,
        grid=(1,),
        in_specs=specs,
        out_specs=spec,
        out_shape=shape(here.shape, BF16),
        input_output_aliases=aliases,
        compiler_params=pltpu.CompilerParams(vmem_limit_bytes=8 * 1024 * 1024),
        cost_estimate=pl.CostEstimate(flops=count * columns, bytes_accessed=count * columns * 8, transcendentals=0),
    )(*ins)


def body(tokens, log_decay, w_query, w_key, w_value, w_level, w_out):
    rows, shard = tokens.shape
    heads = log_decay.shape[1]
    head_size = w_out.shape[0] // heads
    level_count = w_level.shape[1] // heads
    seq_size = lax.axis_size("seq")
    seq_bits = seq_size.bit_length() - 1
    me = lax.axis_index("tp").astype(jnp.int32)
    slab = lax.axis_index("seq")
    ws = (w_query, w_key, w_value, w_level)

    def swap_tp(x, bit):
        return lax.ppermute(x, "tp", [(i, i ^ bit) for i in range(4)])

    def swap_seq(x, bit):
        return lax.ppermute(x, "seq", [(i, i ^ bit) for i in range(seq_size)])

    parts = 4
    depth = shard // parts
    piece = tokens[:, :depth]
    piece, tokens_later = lax.optimization_barrier((piece, tokens))
    pieces = [piece] + [tokens_later[:, p * depth : (p + 1) * depth] for p in range(1, parts)]
    far = [swap_tp(x, 2) for x in pieces]
    near = swap_tp(tokens, 1)

    dcol = jnp.cumsum(log_decay, axis=0)
    drow = dcol.T
    slab_total = dcol[rows - 1]
    keep = jnp.exp(slab_total[None, :] - dcol)
    group_total, before = slab_total, jnp.zeros_like(slab_total)
    fades, spans = [], []
    for b in range(seq_bits):
        upper = (jnp.right_shift(slab, b) & 1) == 1
        spans.append(jnp.where(upper, before, -jnp.inf))
        if b < seq_bits - 1:
            other_total = swap_seq(group_total, 1 << b)
            fade = jnp.exp(jnp.where(upper, group_total, other_total))
            fades.append((upper, jnp.repeat(fade, head_size)[None, :]))
            before = before + jnp.where(upper, other_total, 0.0)
            group_total = group_total + other_total
    span = jnp.exp(dcol[:, :, None] + jnp.stack(spans, axis=-1)[None]).reshape(rows, heads * seq_bits)

    near_places = jnp.stack([me, me ^ 1])
    far_places = jnp.stack([me ^ 2, me ^ 3])
    totals = project(near_places, (tokens, near), ws, 0, None)

    def columns_of(place):
        return lax.dynamic_slice_in_dim(w_out, place * shard, shard, axis=1)

    w_far = swap_tp(columns_of(me ^ 3), 1)
    w_here = swap_tp(columns_of(me ^ 1), 1)
    w_far_own, w_here_own = columns_of(me ^ 2), columns_of(me)

    for p in range(parts):
        arrived = gate(far[p], totals[0])
        pair = (arrived, swap_tp(arrived, 1))
        if p < parts - 1:
            after = {0: (span, keep, fades[-1][1]), 2: (w_far, w_here, w_far_own, w_here_own)}.get(p, ())
            totals = project(far_places, pair, ws, p * depth, totals, after)
    total_q, total_kv, total_l = totals
    last = (parts - 1) * depth
    k, v, state = project_state(far_places, pair, w_key, w_value, last, total_kv, keep, head_size)

    earlier = []
    for b in range(seq_bits):
        other = swap_seq(state, 1 << b)
        earlier.append(other)
        if b < seq_bits - 1:
            upper, fade = fades[b]
            later = jnp.where(upper, state, other).astype(F32)
            sooner = jnp.where(upper, other, state).astype(F32)
            state = (later + fade * sooner).astype(BF16)

    q, level, local = attend(
        far_places, pair, w_query, w_level, last, total_q, total_l, k, v, dcol, drow, head_size, level_count
    )

    step = rows // 4
    cuts = [slice(r, r + step) for r in range(0, rows, step)]
    own, near_normed, crossing = [], [], []
    for r, cut in enumerate(cuts):
        after = (own[-1],) if r else ()
        if r >= 2:
            after += (crossing[r - 2],)
        normed = finish(local, q, level, span, earlier, cut, head_size, level_count, after)
        own.append(normed)
        near_normed.append(swap_tp(normed, 1))
        if r:
            crossing.append(out_block(own[r - 1 : r], near_normed[r - 1 : r], w_far_own, w_far, BF16))
    crossing.append(out_block(own[-1:], near_normed[-1:], w_far_own, w_far, BF16))
    here = out_block(own, near_normed, w_here_own, w_here, F32, (crossing[-1],))
    out = None
    for cut, x in zip(cuts, crossing):
        out = add_rows(here, swap_tp(x, 2), out, cut.start)
    return out


def solution(mesh):
    in_specs = (
        P("seq", "tp"),
        P("seq", "tp"),
        P(None, "tp"),
        P(None, "tp"),
        P(None, "tp"),
        P(None, "tp"),
        P("tp", None),
    )
    out_specs = P("seq", "tp")
    return jax.shard_map(body, mesh=mesh, in_specs=in_specs, out_specs=out_specs, check_vma=False)
```

time: 167 us -> 133 us (0.80)
  blocking collectives: 43.8 us -> 0 us
  local copies, waits for them, and re-layouts: 6.75 us -> 41.3 us
  waiting for transfers between devices: 68 us -> 33.9 us
  Pallas kernels: 0 us -> 31.6 us
  matrix products: 31.2 us -> 0 us
  starting transfers between devices: 0.08 us -> 20.6 us
  between operations: 14 us -> 0.36 us
    reduce_scatter x1 -> x0, waiting for transfers between devices: 43.1 us -> none  [body(): lax.psum_scatter(partial_out.astype(jnp.bfloat16), 'tp', scatter_dimensio...]
    ppermute x0 -> x24, waiting for transfers between devices: none -> 33.9 us  [the longest x19 23.4 us: swap_tp(): return lax.ppermute(x, 'tp', [(i, i ^ bit) for i in range(4)])]
    pallas_call x0 -> x23, Pallas kernels: none -> 31.6 us  [the longest x15 28.6 us: call(): pl.pallas_call(run, in_specs=[SMEM] * smem + [VMEM] * (count - smem) + [A...]
    dot_general x13 -> x0, matrix products: 31.2 us -> none  [the longest x4 16.3 us: body(): jnp.dot(piece, matrix, preferred_element_type=jnp.float32)]
    unnamed x16 -> x78, local copies, waits for them, and re-layouts: 5.38 us -> 30.4 us
    all_gather x2 -> x0, waiting for transfers between devices: 24.1 us -> none  [the longest x1 12.2 us: body(): piece = lax.all_gather(tokens, 'tp', axis=1, tiled=True)]
    all_gather x1 -> x0, blocking collectives: 22.1 us -> none  [prefix(): gathered = lax.all_gather(part, axis)]
    unnamed x1 -> x0, blocking collectives: 21.6 us -> none
  transfers between devices with their start and end apart: 3 -> 24, of which waited for: 3 -> 10; matrix products, arithmetic and copies ran while one was open for 11% -> 12% of each run, Pallas kernels for 0% -> 21%
where the time goes in v2:
time: 133 us; the launch traced here: 132 us
  local copies, waits for them, and re-layouts  41.3 us (31%)
  waiting for transfers between devices  33.9 us (25%)
  Pallas kernels  31.6 us (24%)
  starting transfers between devices  20.6 us (15%)
  other arithmetic  4.12 us (3%)
    unnamed x78, local copies, waits for them, and re-layouts  30.4 us
    pallas_call x15, Pallas kernels, call(): pl.pallas_call(run, in_specs=[SMEM] * smem + [VMEM] * (count - smem) + [A...  28.6 us
    ppermute x19, waiting for transfers between devices, swap_tp(): return lax.ppermute(x, 'tp', [(i, i ^ bit) for i in range(4)])  23.4 us
    ppermute x19, starting transfers between devices, swap_tp(): return lax.ppermute(x, 'tp', [(i, i ^ bit) for i in range(4)])  12.5 us
    ppermute x5, waiting for transfers between devices, swap_seq(): return lax.ppermute(x, 'seq', [(i, i ^ bit) for i in range(seq_size)])  10.4 us
    ppermute x5, starting transfers between devices, swap_seq(): return lax.ppermute(x, 'seq', [(i, i ^ bit) for i in range(seq_size)])  8.14 us
    dynamic_slice x1, local copies, waits for them, and re-layouts, columns_of(): return lax.dynamic_slice_in_dim(w_out, place * shard, shard, axis=1)  3.89 us
    pallas_call x4, Pallas kernels, add_rows(): pl.pallas_call(kernel, grid=(1,), in_specs=specs, out_specs=spec, out_sha...  2.99 us
  transfers between devices with their start and end apart: 24, of which 10 were waited for; matrix products, arithmetic and copies ran while one was open for 12% of the time, Pallas kernels for 21%

profile of v2, /device:TPU:0, one launch (start us, length us, event | category | flops | bytes accessed | tf_op | source)
XLA Modules:
  0.0 131.9 jit_solution(15251111462618751012)
XLA Ops:
  1.4 2.0 %fusion.6 = (bf16[512,256]{1,0:T(8,128)(2,1)}, bf16[512,256]{1,0:T(8,128)(2,1)}, bf16[512,256]{1,0:T(8,128)(2,1)}) fusion(bf16[512,1024]{1,0:T(8,128)(2,1)} %refs_1_.1), kind=kLoop, calls=%fused_computation.29 | loop fusion | bytes 1572864 | tf_op jit(solution)/shard_map/slice | solution.py:287
  3.4 2.5 %collective-permute-start.2 = (bf16[512,256]{1,0:T(8,128)(2,1)}, bf16[512,256]{1,0:T(8,128)(2,1)}, u32[]{:S(2)}, u32[]{:S(2)}) collective-permute-start(bf16[512,256]{1,0:T(8,128)(2,1)} %get-tuple-element.49), channel_id=1, source_target_pairs={{0,2},{1,3},{2,0},{3,1},{4,6},{5,7},{6,4},{7,5},{8,10},{9,11},{10,... | collective-permute-start | bytes 786440 | tf_op jit(solution)/shard_map/ppermute | solution.py:278
  8.5 2.0 %collective-permute-start.6 = (f32[4]{0:T(128)S(1)}, f32[4]{0:T(128)S(1)}, u32[]{:S(2)}, u32[]{:S(2)}) collective-permute-start(f32[4]{0:T(128)S(1)} %slice_reduce_fusion.1), channel_id=1, source_target_pairs={{0,4},{4,0},{8,12},{12,8},{16,20},{20,16},{24,28},{28,24},{1,5},{5... | collective-permute-start | bytes 56 | tf_op jit(solution)/shard_map/ppermute | solution.py:281
  10.5 3.9 %constant_dynamic-slice_fusion = (bf16[512,1024]{1,0:T(8,128)(2,1)}, bf16[512,1024]{1,0:T(8,128)(2,1)}, bf16[512,1024]{1,0:T(8,128)(2,1)}, bf16[512,1024]{1,0:T(8,128)(2,1)S(1)}) fusion(bf16[512,4096]{1,0:T(8,128)(2,1)} %param.13, s32[]{:T(128)S(6)} %select_n.85, s32[]{:T(128)S(6)} %select_n.83, s32[]{:T(128)S(6)} %select_n.82, s32[]{:T(128)S(6)} %select_n.84), kind=kLoop, calls=%fused_computation.11 | loop fusion | bytes 8388624 | tf_op jit(solution)/shard_map/dynamic_slice | solution.py:313
  20.0 2.0 %collective-permute-done.7 = f32[4]{0:T(128)S(1)} collective-permute-done((f32[4]{0:T(128)S(1)}, f32[4]{0:T(128)S(1)}, u32[]{:S(2)}, u32[]{:S(2)}) %collective-permute-start.7) | collective-permute-done | bytes 48 | tf_op jit(solution)/shard_map/ppermute | solution.py:281
  23.0 2.2 %copy-done = bf16[4096,512]{1,0:T(8,128)(2,1)S(1)} copy-done((bf16[4096,512]{1,0:T(8,128)(2,1)S(1)}, bf16[4096,512]{1,0:T(8,128)(2,1)}, u32[]{:S(2)}) %copy-start) | copy-done | bytes 4194328
  30.1 2.9 %shard_map.73 = (f32[512,512]{1,0:T(8,128)S(1)}, f32[512,256]{1,0:T(8,128)S(1)}, f32[512,24]{1,0:T(8,128)S(1)}) custom-call(s32[2]{0:T(128)S(1)} %pad_add_fusion.1.refs_0_, bf16[512,1024]{1,0:T(8,128)(2,1)S(1)} %copy-done.19, bf16[512,1024]{1,0:T(8,128)(2,1)S(1)} %copy-done.27, bf16[4096,512]{1,0:T(8,128)(2,1)S(1)} %copy-done, ...), custom_call_target="tpu_custom_call" | custom-call | tf_op jit(solution)/shard_map/pallas_call | solution.py:37
  36.5 2.2 %copy-done.1 = bf16[4096,512]{1,0:T(8,128)(2,1)S(1)} copy-done((bf16[4096,512]{1,0:T(8,128)(2,1)S(1)}, bf16[4096,512]{1,0:T(8,128)(2,1)}, u32[]{:S(2)}) %copy-start.1) | copy-done | bytes 4194328
  44.1 1.9 %shard_map.75 = (f32[512,512]{1,0:T(8,128)S(1)}, f32[512,256]{1,0:T(8,128)S(1)}, f32[512,24]{1,0:T(8,128)S(1)}) custom-call(s32[2]{0:T(128)S(1)} %pad_add_fusion.refs_0_, bf16[512,256]{1,0:T(8,128)(2,1)} %shard_map.74.refs_1_, bf16[512,256]{1,0:T(8,128)(2,1)} %collective-permute-done.5.refs_2_, ...), custom_call_target="tpu_custom_call", output_to_operand_aliasing={{0}: (7, {}), {1}: (8, {}), {2}: (9, {})} | custom-call | tf_op jit(solution)/shard_map/pallas_call | solution.py:37
  49.0 1.8 %shard_map.77 = (f32[512,512]{1,0:T(8,128)S(1)}, f32[512,256]{1,0:T(8,128)S(1)}, f32[512,24]{1,0:T(8,128)S(1)}) custom-call(s32[2]{0:T(128)S(1)} %pad_add_fusion.refs_0_, bf16[512,256]{1,0:T(8,128)(2,1)} %shard_map.76.refs_1_, bf16[512,256]{1,0:T(8,128)(2,1)S(1)} %collective-permute-done.8.refs_2_, ...), custom_call_target="tpu_custom_call", output_to_operand_aliasing={{0}: (7, {}), {1}: (8, {}), {2}: (9, {})} | custom-call | tf_op jit(solution)/shard_map/pallas_call | solution.py:37
  50.9 3.9 %collective-permute-done.1.refs_0_ = bf16[512,256]{1,0:T(8,128)(2,1)S(1)} collective-permute-done((bf16[512,256]{1,0:T(8,128)(2,1)S(1)}, bf16[512,256]{1,0:T(8,128)(2,1)S(1)}, u32[]{:S(2)}, u32[]{:S(2)}) %collective-permute-start.1) | collective-permute-done | bytes 262176 | tf_op jit(solution)/shard_map/ppermute | solution.py:278
  58.7 4.9 %collective-permute-done.refs_0_ = bf16[512,256]{1,0:T(8,128)(2,1)S(1)} collective-permute-done((bf16[512,256]{1,0:T(8,128)(2,1)S(1)}, bf16[512,256]{1,0:T(8,128)(2,1)S(1)}, u32[]{:S(2)}, u32[]{:S(2)}) %collective-permute-start) | collective-permute-done | bytes 262176 | tf_op jit(solution)/shard_map/ppermute | solution.py:278
  68.0 5.2 %collective-permute-done.13.refs_4_ = bf16[128,512]{1,0:T(8,128)(2,1)S(1)} collective-permute-done((bf16[128,512]{1,0:T(8,128)(2,1)S(1)}, bf16[128,512]{1,0:T(8,128)(2,1)S(1)}, u32[]{:S(2)}, u32[]{:S(2)}) %collective-permute-start.13) | collective-permute-done | bytes 131104 | tf_op jit(solution)/shard_map/ppermute | solution.py:281
  74.9 3.3 %collective-permute-done.14.refs_5_ = bf16[128,512]{1,0:T(8,128)(2,1)S(1)} collective-permute-done((bf16[128,512]{1,0:T(8,128)(2,1)S(1)}, bf16[128,512]{1,0:T(8,128)(2,1)S(1)}, u32[]{:S(2)}, u32[]{:S(2)}) %collective-permute-start.14) | collective-permute-done | bytes 131104 | tf_op jit(solution)/shard_map/ppermute | solution.py:281
  79.7 2.6 %collective-permute-start.15 = (bf16[128,512]{1,0:T(8,128)(2,1)}, bf16[128,512]{1,0:T(8,128)(2,1)}, u32[]{:S(2)}, u32[]{:S(2)}) collective-permute-start(bf16[128,512]{1,0:T(8,128)(2,1)} %add_convert_fusion), channel_id=1, source_target_pairs={{0,16},{4,20},{8,24},{12,28},{16,0},{20,4},{24,8},{28,12},{1,17},{... | collective-permute-start | bytes 393224 | tf_op jit(solution)/shard_map/ppermute | solution.py:281
  83.1 2.2 %copy-done.2 = bf16[4096,512]{1,0:T(8,128)(2,1)S(1)} copy-done((bf16[4096,512]{1,0:T(8,128)(2,1)S(1)}, bf16[4096,512]{1,0:T(8,128)(2,1)}, u32[]{:S(2)}) %copy-start.2) | copy-done | bytes 4194328
  90.9 3.2 %shard_map.82 = (bf16[512,512]{1,0:T(8,128)(2,1)S(1)}, f32[512,24]{1,0:T(8,128)S(1)}, f32[512,512]{1,0:T(8,128)S(1)}) custom-call(s32[2]{0:T(128)S(1)} %pad_add_fusion.refs_0_, bf16[512,256]{1,0:T(8,128)(2,1)S(1)} %copy-done.25, bf16[512,256]{1,0:T(8,128)(2,1)S(1)} %copy-done.29, bf16[4096,512]{1,0:T(8,128)(2,1)S(1)} %copy-done.2, ...), custom_call_target="tpu_custom_call" | custom-call | flops 805306368 | bytes 7913480 | tf_op jit(solution)/shard_map/pallas_call | solution.py:37
  94.1 1.8 %shard_map.83.refs_7_.refs_0_ = bf16[128,512]{1,0:T(8,128)(2,1)S(1)} custom-call(f32[512,512]{1,0:T(8,128)S(1)} %get-tuple-element.41.refs_0_, bf16[512,512]{1,0:T(8,128)(2,1)S(1)} %get-tuple-element.42.refs_1_, f32[512,24]{1,0:T(8,128)S(1)} %get-tuple-element.43.refs_2_, f32[512,12]{1,0:T(8,128)S(1)} %add_exponential_fusion.refs_10_.refs_3_, ...), custom_call_target="tpu_custom_call" | custom-call | flops 50331648 | bytes 2170880 | tf_op jit(solution)/shard_map/pallas_call | solution.py:37
  96.0 1.8 %shard_map.84.refs_7_.refs_0_.refs_1_ = bf16[128,512]{1,0:T(8,128)(2,1)S(1)} custom-call(f32[512,512]{1,0:T(8,128)S(1)} %get-tuple-element.41.refs_0_, bf16[512,512]{1,0:T(8,128)(2,1)S(1)} %get-tuple-element.42.refs_1_, f32[512,24]{1,0:T(8,128)S(1)} %get-tuple-element.43.refs_2_, f32[512,12]{1,0:T(8,128)S(1)} %add_exponential_fusion.refs_10_.refs_3_, ...), custom_call_target="tpu_custom_call" | custom-call | flops 50331648 | bytes 2170880 | tf_op jit(solution)/shard_map/pallas_call | solution.py:37
  103.5 1.9 %shard_map.88.refs_0_.refs_3_ = bf16[128,512]{1,0:T(8,128)(2,1)S(1)} custom-call(f32[512,512]{1,0:T(8,128)S(1)} %get-tuple-element.41.refs_0_, bf16[512,512]{1,0:T(8,128)(2,1)S(1)} %get-tuple-element.42.refs_1_, f32[512,24]{1,0:T(8,128)S(1)} %get-tuple-element.43.refs_2_, f32[512,12]{1,0:T(8,128)S(1)} %add_exponential_fusion.refs_10_.refs_3_, ...), custom_call_target="tpu_custom_call" | custom-call | flops 50331648 | bytes 2170880 | tf_op jit(solution)/shard_map/pallas_call | solution.py:37
  113.5 2.5 %shard_map.90.h_ref = f32[512,1024]{1,0:T(8,128)S(1)} custom-call(bf16[128,512]{1,0:T(8,128)(2,1)S(1)} %shard_map.83.refs_7_.refs_0_, bf16[128,512]{1,0:T(8,128)(2,1)S(1)} %shard_map.84.refs_7_.refs_0_.refs_1_, bf16[128,512]{1,0:T(8,128)(2,1)S(1)} %shard_map.86.refs_7_.refs_2_.refs_0_, bf16[128,512]{1,0:T(8,128)(2,1)S(1)} %shard_map.88.refs_0_.refs_3_, ...), custom_call_target="tpu_custom_call" | custom-call | flops 1073741824 | bytes 5242880 | tf_op jit(solution)/shard_map/pallas_call | solution.py:37
  116.0 4.7 %collective-permute-done.23.a_ref = bf16[128,1024]{1,0:T(8,128)(2,1)S(1)} collective-permute-done((bf16[128,1024]{1,0:T(8,128)(2,1)S(1)}, bf16[128,1024]{1,0:T(8,128)(2,1)S(1)}, u32[]{:S(2)}, u32[]{:S(2)}) %collective-permute-start.23) | collective-permute-done | bytes 262176 | tf_op jit(solution)/shard_map/ppermute | solution.py:278
  122.2 4.1 %collective-permute-done.21.a_ref = bf16[128,1024]{1,0:T(8,128)(2,1)S(1)} collective-permute-done((bf16[128,1024]{1,0:T(8,128)(2,1)S(1)}, bf16[128,1024]{1,0:T(8,128)(2,1)S(1)}, u32[]{:S(2)}, u32[]{:S(2)}) %collective-permute-start.21) | collective-permute-done | bytes 262176 | tf_op jit(solution)/shard_map/ppermute | solution.py:278
  127.1 4.0 %collective-permute-done.20.a_ref = bf16[128,1024]{1,0:T(8,128)(2,1)S(1)} collective-permute-done((bf16[128,1024]{1,0:T(8,128)(2,1)S(1)}, bf16[128,1024]{1,0:T(8,128)(2,1)S(1)}, u32[]{:S(2)}, u32[]{:S(2)}) %collective-permute-start.20) | collective-permute-done | bytes 262176 | tf_op jit(solution)/shard_map/ppermute | solution.py:278
  (154 shorter events, 62.2 us)
Async XLA Ops:
  0.0 22.0 %collective-permute-start.4 = (bf16[512,1024]{1,0:T(8,128)(2,1)}, bf16[512,1024]{1,0:T(8,128)(2,1)S(1)}, u32[]{:S(2)}, u32[]{:S(2)}) collective-permute-start(bf16[512,1024]{1,0:T(8,128)(2,1)} %refs_1_.1), channel_id=1, source_target_pairs={{0,1},{1,0},{2,3},{3,2},{4,5},{5,4},{6,7},{7,6},{8,9},{9,8},{10,11... | collective-permute-start | bytes 3145736 | tf_op jit(solution)/shard_map/ppermute | solution.py:278
  3.4 42.6 %collective-permute-start.2 = (bf16[512,256]{1,0:T(8,128)(2,1)}, bf16[512,256]{1,0:T(8,128)(2,1)}, u32[]{:S(2)}, u32[]{:S(2)}) collective-permute-start(bf16[512,256]{1,0:T(8,128)(2,1)} %get-tuple-element.49), channel_id=1, source_target_pairs={{0,2},{1,3},{2,0},{3,1},{4,6},{5,7},{6,4},{7,5},{8,10},{9,11},{10,... | collective-permute-start | bytes 786440 | tf_op jit(solution)/shard_map/ppermute | solution.py:278
  5.9 28.5 %collective-permute-start.3 = (bf16[512,256]{1,0:T(8,128)(2,1)S(1)}, bf16[512,256]{1,0:T(8,128)(2,1)}, u32[]{:S(2)}, u32[]{:S(2)}) collective-permute-start(bf16[512,256]{1,0:T(8,128)(2,1)S(1)} %slice.21), channel_id=1, source_target_pairs={{0,2},{1,3},{2,0},{3,1},{4,6},{5,7},{6,4},{7,5},{8,10},{9,11},{10,... | collective-permute-start | bytes 786440 | tf_op jit(solution)/shard_map/ppermute | solution.py:278
  8.5 9.3 %collective-permute-start.6 = (f32[4]{0:T(128)S(1)}, f32[4]{0:T(128)S(1)}, u32[]{:S(2)}, u32[]{:S(2)}) collective-permute-start(f32[4]{0:T(128)S(1)} %slice_reduce_fusion.1), channel_id=1, source_target_pairs={{0,4},{4,0},{8,12},{12,8},{16,20},{20,16},{24,28},{28,24},{1,5},{5... | collective-permute-start | bytes 56 | tf_op jit(solution)/shard_map/ppermute | solution.py:281
  14.4 41.9 %collective-permute-start.10 = (bf16[512,1024]{1,0:T(8,128)(2,1)}, bf16[512,1024]{1,0:T(8,128)(2,1)}, u32[]{:S(2)}, u32[]{:S(2)}) collective-permute-start(bf16[512,1024]{1,0:T(8,128)(2,1)} %get-tuple-element.47), channel_id=1, source_target_pairs={{0,1},{1,0},{2,3},{3,2},{4,5},{5,4},{6,7},{7,6},{8,9},{9,8},{10,11... | collective-permute-start | bytes 3145736 | tf_op jit(solution)/shard_map/ppermute | solution.py:278
  18.4 3.5 %collective-permute-start.7 = (f32[4]{0:T(128)S(1)}, f32[4]{0:T(128)S(1)}, u32[]{:S(2)}, u32[]{:S(2)}) collective-permute-start(f32[4]{0:T(128)S(1)} %get-tuple-element.55), channel_id=1, source_target_pairs={{0,8},{4,12},{8,0},{12,4},{16,24},{20,28},{24,16},{28,20},{1,9},{5... | collective-permute-start | bytes 56 | tf_op jit(solution)/shard_map/ppermute | solution.py:281
  22.0 34.4 %collective-permute-start.11 = (bf16[512,1024]{1,0:T(8,128)(2,1)}, bf16[512,1024]{1,0:T(8,128)(2,1)}, u32[]{:S(2)}, u32[]{:S(2)}) collective-permute-start(bf16[512,1024]{1,0:T(8,128)(2,1)} %get-tuple-element.46), channel_id=1, source_target_pairs={{0,1},{1,0},{2,3},{3,2},{4,5},{5,4},{6,7},{7,6},{8,9},{9,8},{10,11... | collective-permute-start | bytes 3145736 | tf_op jit(solution)/shard_map/ppermute | solution.py:278
  34.5 2.0 %collective-permute-start.5 = (bf16[512,256]{1,0:T(8,128)(2,1)}, bf16[512,256]{1,0:T(8,128)(2,1)}, u32[]{:S(2)}, u32[]{:S(2)}) collective-permute-start(bf16[512,256]{1,0:T(8,128)(2,1)} %shard_map.74.refs_1_), channel_id=1, source_target_pairs={{0,1},{1,0},{2,3},{3,2},{4,5},{5,4},{6,7},{7,6},{8,9},{9,8},{10,11... | collective-permute-start | bytes 786440 | tf_op jit(solution)/shard_map/ppermute | solution.py:278
  46.0 2.0 %collective-permute-start.8 = (bf16[512,256]{1,0:T(8,128)(2,1)}, bf16[512,256]{1,0:T(8,128)(2,1)S(1)}, u32[]{:S(2)}, u32[]{:S(2)}) collective-permute-start(bf16[512,256]{1,0:T(8,128)(2,1)} %shard_map.76.refs_1_), channel_id=1, source_target_pairs={{0,1},{1,0},{2,3},{3,2},{4,5},{5,4},{6,7},{7,6},{8,9},{9,8},{10,11... | collective-permute-start | bytes 786440 | tf_op jit(solution)/shard_map/ppermute | solution.py:278
  46.5 8.3 %collective-permute-start.1 = (bf16[512,256]{1,0:T(8,128)(2,1)S(1)}, bf16[512,256]{1,0:T(8,128)(2,1)S(1)}, u32[]{:S(2)}, u32[]{:S(2)}) collective-permute-start(bf16[512,256]{1,0:T(8,128)(2,1)S(1)} %copy-done.36), channel_id=1, source_target_pairs={{0,2},{1,3},{2,0},{3,1},{4,6},{5,7},{6,4},{7,5},{8,10},{9,11},{10,... | collective-permute-start | bytes 786440 | tf_op jit(solution)/shard_map/ppermute | solution.py:278
  54.8 1.5 %collective-permute-start.9 = (bf16[512,256]{1,0:T(8,128)(2,1)S(1)}, bf16[512,256]{1,0:T(8,128)(2,1)S(1)}, u32[]{:S(2)}, u32[]{:S(2)}) collective-permute-start(bf16[512,256]{1,0:T(8,128)(2,1)S(1)} %shard_map.78.refs_1_), channel_id=1, source_target_pairs={{0,1},{1,0},{2,3},{3,2},{4,5},{5,4},{6,7},{7,6},{8,9},{9,8},{10,11... | collective-permute-start | bytes 786440 | tf_op jit(solution)/shard_map/ppermute | solution.py:278
  54.8 8.7 %collective-permute-start = (bf16[512,256]{1,0:T(8,128)(2,1)S(1)}, bf16[512,256]{1,0:T(8,128)(2,1)S(1)}, u32[]{:S(2)}, u32[]{:S(2)}) collective-permute-start(bf16[512,256]{1,0:T(8,128)(2,1)S(1)} %copy-done.35), channel_id=1, source_target_pairs={{0,2},{1,3},{2,0},{3,1},{4,6},{5,7},{6,4},{7,5},{8,10},{9,11},{10,... | collective-permute-start | bytes 786440 | tf_op jit(solution)/shard_map/ppermute | solution.py:278
  63.5 1.5 %collective-permute-start.12 = (bf16[512,256]{1,0:T(8,128)(2,1)S(1)}, bf16[512,256]{1,0:T(8,128)(2,1)S(1)}, u32[]{:S(2)}, u32[]{:S(2)}) collective-permute-start(bf16[512,256]{1,0:T(8,128)(2,1)S(1)} %shard_map.80.refs_1_), channel_id=1, source_target_pairs={{0,1},{1,0},{2,3},{3,2},{4,5},{5,4},{6,7},{7,6},{8,9},{9,8},{10,11... | collective-permute-start | bytes 786440 | tf_op jit(solution)/shard_map/ppermute | solution.py:278
  67.6 5.5 %collective-permute-start.13 = (bf16[128,512]{1,0:T(8,128)(2,1)S(1)}, bf16[128,512]{1,0:T(8,128)(2,1)S(1)}, u32[]{:S(2)}, u32[]{:S(2)}) collective-permute-start(bf16[128,512]{1,0:T(8,128)(2,1)S(1)} %get-tuple-element.44), channel_id=1, source_target_pairs={{0,4},{4,0},{8,12},{12,8},{16,20},{20,16},{24,28},{28,24},{1,5},{5... | collective-permute-start | bytes 393224 | tf_op jit(solution)/shard_map/ppermute | solution.py:281
  73.2 5.0 %collective-permute-start.14 = (bf16[128,512]{1,0:T(8,128)(2,1)S(1)}, bf16[128,512]{1,0:T(8,128)(2,1)S(1)}, u32[]{:S(2)}, u32[]{:S(2)}) collective-permute-start(bf16[128,512]{1,0:T(8,128)(2,1)S(1)} %add_convert_fusion.1), channel_id=1, source_target_pairs={{0,8},{4,12},{8,0},{12,4},{16,24},{20,28},{24,16},{28,20},{1,9},{5... | collective-permute-start | bytes 393224 | tf_op jit(solution)/shard_map/ppermute | solution.py:281
  79.7 14.4 %collective-permute-start.15 = (bf16[128,512]{1,0:T(8,128)(2,1)}, bf16[128,512]{1,0:T(8,128)(2,1)}, u32[]{:S(2)}, u32[]{:S(2)}) collective-permute-start(bf16[128,512]{1,0:T(8,128)(2,1)} %add_convert_fusion), channel_id=1, source_target_pairs={{0,16},{4,20},{8,24},{12,28},{16,0},{20,4},{24,8},{28,12},{1,17},{... | collective-permute-start | bytes 393224 | tf_op jit(solution)/shard_map/ppermute | solution.py:281
  95.9 2.4 %collective-permute-start.16 = (bf16[128,512]{1,0:T(8,128)(2,1)S(1)}, bf16[128,512]{1,0:T(8,128)(2,1)S(1)}, u32[]{:S(2)}, u32[]{:S(2)}) collective-permute-start(bf16[128,512]{1,0:T(8,128)(2,1)S(1)} %shard_map.83.refs_7_.refs_0_), channel_id=1, source_target_pairs={{0,1},{1,0},{2,3},{3,2},{4,5},{5,4},{6,7},{7,6},{8,9},{9,8},{10,11... | collective-permute-start | bytes 393224 | tf_op jit(solution)/shard_map/ppermute | solution.py:278
  97.7 4.1 %collective-permute-start.17 = (bf16[128,512]{1,0:T(8,128)(2,1)S(1)}, bf16[128,512]{1,0:T(8,128)(2,1)S(1)}, u32[]{:S(2)}, u32[]{:S(2)}) collective-permute-start(bf16[128,512]{1,0:T(8,128)(2,1)S(1)} %shard_map.84.refs_7_.refs_0_.refs_1_), channel_id=1, source_target_pairs={{0,1},{1,0},{2,3},{3,2},{4,5},{5,4},{6,7},{7,6},{8,9},{9,8},{10,11... | collective-permute-start | bytes 393224 | tf_op jit(solution)/shard_map/ppermute | solution.py:278
  101.8 6.2 %collective-permute-start.18 = (bf16[128,512]{1,0:T(8,128)(2,1)S(1)}, bf16[128,512]{1,0:T(8,128)(2,1)S(1)}, u32[]{:S(2)}, u32[]{:S(2)}) collective-permute-start(bf16[128,512]{1,0:T(8,128)(2,1)S(1)} %shard_map.86.refs_7_.refs_2_.refs_0_), channel_id=1, source_target_pairs={{0,1},{1,0},{2,3},{3,2},{4,5},{5,4},{6,7},{7,6},{8,9},{9,8},{10,11... | collective-permute-start | bytes 393224 | tf_op jit(solution)/shard_map/ppermute | solution.py:278
  105.4 5.9 %collective-permute-start.19 = (bf16[128,512]{1,0:T(8,128)(2,1)S(1)}, bf16[128,512]{1,0:T(8,128)(2,1)S(1)}, u32[]{:S(2)}, u32[]{:S(2)}) collective-permute-start(bf16[128,512]{1,0:T(8,128)(2,1)S(1)} %shard_map.88.refs_0_.refs_3_), channel_id=1, source_target_pairs={{0,1},{1,0},{2,3},{3,2},{4,5},{5,4},{6,7},{7,6},{8,9},{9,8},{10,11... | collective-permute-start | bytes 393224 | tf_op jit(solution)/shard_map/ppermute | solution.py:278
  106.0 15.5 %collective-permute-start.22 = (bf16[128,1024]{1,0:T(8,128)(2,1)S(1)}, bf16[128,1024]{1,0:T(8,128)(2,1)S(1)}, u32[]{:S(2)}, u32[]{:S(2)}) collective-permute-start(bf16[128,1024]{1,0:T(8,128)(2,1)S(1)} %shard_map.87.refs_8_), channel_id=1, source_target_pairs={{0,2},{1,3},{2,0},{3,1},{4,6},{5,7},{6,4},{7,5},{8,10},{9,11},{10,... | collective-permute-start | bytes 786440 | tf_op jit(solution)/shard_map/ppermute | solution.py:278
  107.5 13.3 %collective-permute-start.23 = (bf16[128,1024]{1,0:T(8,128)(2,1)S(1)}, bf16[128,1024]{1,0:T(8,128)(2,1)S(1)}, u32[]{:S(2)}, u32[]{:S(2)}) collective-permute-start(bf16[128,1024]{1,0:T(8,128)(2,1)S(1)} %shard_map.85.refs_8_), channel_id=1, source_target_pairs={{0,2},{1,3},{2,0},{3,1},{4,6},{5,7},{6,4},{7,5},{8,10},{9,11},{10,... | collective-permute-start | bytes 786440 | tf_op jit(solution)/shard_map/ppermute | solution.py:278
  109.7 16.7 %collective-permute-start.21 = (bf16[128,1024]{1,0:T(8,128)(2,1)S(1)}, bf16[128,1024]{1,0:T(8,128)(2,1)S(1)}, u32[]{:S(2)}, u32[]{:S(2)}) collective-permute-start(bf16[128,1024]{1,0:T(8,128)(2,1)S(1)} %shard_map.91), channel_id=1, source_target_pairs={{0,2},{1,3},{2,0},{3,1},{4,6},{5,7},{6,4},{7,5},{8,10},{9,11},{10,... | collective-permute-start | bytes 786440 | tf_op jit(solution)/shard_map/ppermute | solution.py:278
  113.0 18.2 %collective-permute-start.20 = (bf16[128,1024]{1,0:T(8,128)(2,1)S(1)}, bf16[128,1024]{1,0:T(8,128)(2,1)S(1)}, u32[]{:S(2)}, u32[]{:S(2)}) collective-permute-start(bf16[128,1024]{1,0:T(8,128)(2,1)S(1)} %shard_map.89.refs_10_), channel_id=1, source_target_pairs={{0,2},{1,3},{2,0},{3,1},{4,6},{5,7},{6,4},{7,5},{8,10},{9,11},{10,... | collective-permute-start | bytes 786440 | tf_op jit(solution)/shard_map/ppermute | solution.py:278
  (38 other events, 119.0 us)

commit v3 on v2

v3 whole, which is shorter than its diff:
```python
import functools

import jax
import jax.numpy as jnp
from jax import lax
from jax.experimental import pallas as pl
from jax.experimental.pallas import tpu as pltpu
from jax.sharding import PartitionSpec as P

BLOCK = 128
F32 = jnp.float32
BF16 = jnp.bfloat16
VMEM = pl.BlockSpec(memory_space=pltpu.VMEM)
SMEM = pl.BlockSpec(memory_space=pltpu.SMEM)
ANY = pl.BlockSpec(memory_space=pl.ANY)


def dot(a, b):
    return jnp.dot(a, b, preferred_element_type=F32)


def dot_dims(a, b, left, right):
    return lax.dot_general(a, b, (((left,), (right,)), ((), ())), preferred_element_type=F32)


def shape(dims, dtype):
    return jax.ShapeDtypeStruct(dims, dtype)


def call(kernel, ins, outs, flops, after=(), smem=0, aliases=None, megabytes=8):
    count = len(ins)

    def run(*refs):
        kernel(*refs[:count], *refs[count + len(after) :])

    nbytes = sum(x.size * x.dtype.itemsize for x in (*ins, *outs)) if flops else 0
    return pl.pallas_call(
        run,
        in_specs=[SMEM] * smem + [VMEM] * (count - smem) + [ANY] * len(after),
        out_specs=[VMEM] * len(outs),
        out_shape=list(outs),
        input_output_aliases=aliases or {},
        compiler_params=pltpu.CompilerParams(vmem_limit_bytes=megabytes * 1024 * 1024),
        cost_estimate=pl.CostEstimate(flops=flops, bytes_accessed=nbytes, transcendentals=0),
    )(*ins, *after)


def gate(x, *after):
    def run(*refs):
        pass

    return pl.pallas_call(
        run,
        in_specs=[ANY] * (1 + len(after)),
        out_specs=ANY,
        out_shape=shape(x.shape, x.dtype),
        input_output_aliases={0: 0},
        compiler_params=pltpu.CompilerParams(vmem_limit_bytes=1024 * 1024),
        cost_estimate=pl.CostEstimate(flops=0, bytes_accessed=0, transcendentals=0),
    )(x, *after)


def cut_columns(tokens, ways):
    rows, columns = tokens.shape
    depth = columns // ways

    def kernel(t_ref, first_ref, second_ref):
        first_ref[...] = t_ref[:, :depth]
        second_ref[0] = t_ref[:, depth : depth + depth // 2]
        second_ref[1] = t_ref[:, depth + depth // 2 :]

    outs = [shape((rows, depth), tokens.dtype), shape((2, rows, depth // 2), tokens.dtype)]
    return call(kernel, [tokens], outs, 0)


def upper_half(slab_ref, bit):
    return ((slab_ref[0] >> bit) & 1) == 1


def decays(slab, log_decay_rows, head_size):
    heads, rows = log_decay_rows.shape

    def kernel(slab_ref, x_ref, row_ref, col_ref, keep_ref, total_ref, span_ref):
        x = x_ref[...]
        x = jnp.concatenate([x, jnp.zeros((-heads % 8, rows), F32)], axis=0) if heads % 8 else x
        place = lax.broadcasted_iota(jnp.int32, x.shape, 1)
        shift = 1
        while shift < rows:
            x = x + jnp.where(place >= shift, pltpu.roll(x, shift, 1), 0.0)
            shift *= 2
        total = x[:, rows - 1 : rows]
        row_ref[...] = x[:heads]
        col_ref[...] = jnp.transpose(x)[:, :heads]
        keep_ref[...] = jnp.transpose(jnp.exp(total - x))[:, :heads]
        for h in range(heads):
            total_ref[:, h * head_size : (h + 1) * head_size] = jnp.broadcast_to(
                total[h : h + 1], (8, head_size)
            )
        span_ref[...] = jnp.full(span_ref.shape, jnp.where(upper_half(slab_ref, 0), 0.0, -jnp.inf), F32)

    wide = shape((8, heads * head_size), F32)
    outs = [shape((heads, rows), F32), shape((rows, heads), F32), shape((rows, heads), F32), wide, wide]
    return call(kernel, [slab, log_decay_rows], outs, 0, smem=1)


def link(slab, bit, total, other, before):
    def kernel(slab_ref, *refs):
        total_ref, other_ref = refs[:2]
        total_out, before_out, own_out, other_out, span_out = refs[-5:]
        upper = upper_half(slab_ref, bit)
        here, there = total_ref[...], other_ref[...]
        total_out[...] = here + there
        so_far = jnp.where(upper, there, 0.0)
        if before is not None:
            so_far = so_far + refs[2][...]
        before_out[...] = so_far
        own_out[...] = jnp.where(upper, 1.0, jnp.exp(there))
        other_out[...] = jnp.where(upper, jnp.exp(here), 1.0)
        span_out[...] = jnp.where(upper_half(slab_ref, bit + 1), so_far, -jnp.inf)

    ins = [slab, total, other] + ([] if before is None else [before])
    return call(kernel, ins, [shape(total.shape, F32)] * 5, 0, smem=1)


def combine(state, other, own_factor, other_factor):
    def kernel(s_ref, o_ref, a_ref, b_ref, out_ref):
        out_ref[...] = (
            a_ref[0:1, :] * s_ref[...].astype(F32) + b_ref[0:1, :] * o_ref[...].astype(F32)
        ).astype(BF16)

    return call(kernel, [state, other, own_factor, other_factor], [shape(state.shape, BF16)], 0)[0]


def pad_widths(width):
    return -(-width // 128) * 128


def project_first(me, tokens, near, ws, after=(), tile=256):
    rows, shard = tokens.shape
    wq, wk, wv, wl = ws
    q_width, kv_width, l_width = wq.shape[1], wk.shape[1], wl.shape[0]
    steps = shard // tile
    n_after = len(after)

    def kernel(me_ref, *refs):
        x_refs, w_refs = refs[:2], refs[2:18]
        total_q, total_kv, total_l, q_out, kv_out, l_out = refs[18 + n_after :]
        step = pl.program_id(0)

        @pl.when(step == 0)
        def _():
            total_q[...] = jnp.zeros_like(total_q)
            total_kv[...] = jnp.zeros_like(total_kv)
            total_l[...] = jnp.zeros_like(total_l)

        def joined(i):
            return jnp.concatenate([w_refs[4 * i + 1][...], w_refs[4 * i + 2][...]], axis=1)

        x0, x1 = x_refs[0][...], x_refs[1][...]
        total_q[...] += dot(x0, w_refs[0][...]) + dot(x1, w_refs[4][...])
        total_kv[...] += dot(x0, joined(0)) + dot(x1, joined(1))
        total_l[...] += dot_dims(x0, w_refs[3][...], 1, 1) + dot_dims(x1, w_refs[7][...], 1, 1)
        for i in (2, 3):
            q_out[i - 2] = w_refs[4 * i][...]
            kv_out[i - 2] = joined(i)
            l_out[i - 2] = w_refs[4 * i + 3][...]

    x_spec = pl.BlockSpec((rows, tile), lambda s, m: (0, s))
    w_specs, operands = [], []
    for i in range(4):
        for w in (wq, wk, wv):
            w_specs.append(pl.BlockSpec((tile, w.shape[1]), lambda s, m, i=i: ((m[0] ^ i) * steps + s, 0)))
        w_specs.append(pl.BlockSpec((l_width, tile), lambda s, m, i=i: (0, (m[0] ^ i) * steps + s)))
        operands += [wq, wk, wv, wl]
    out_shape = [
        shape((rows, q_width), F32),
        shape((rows, 2 * kv_width), F32),
        shape((rows, l_width), F32),
        shape((2, shard, q_width), BF16),
        shape((2, shard, 2 * kv_width), BF16),
        shape((2, l_width, shard), BF16),
    ]
    out_specs = [pl.BlockSpec(o.shape, lambda s, m: (0, 0)) for o in out_shape[:3]]
    out_specs += [
        pl.BlockSpec((2, tile, q_width), lambda s, m: (0, s, 0)),
        pl.BlockSpec((2, tile, 2 * kv_width), lambda s, m: (0, s, 0)),
        pl.BlockSpec((2, l_width, tile), lambda s, m: (0, 0, s)),
    ]
    outs = pl.pallas_call(
        kernel,
        grid_spec=pltpu.PrefetchScalarGridSpec(
            num_scalar_prefetch=1,
            grid=(steps,),
            in_specs=[x_spec, x_spec, *w_specs] + [ANY] * n_after,
            out_specs=out_specs,
        ),
        out_shape=out_shape,
        compiler_params=pltpu.CompilerParams(vmem_limit_bytes=16 * 1024 * 1024),
        cost_estimate=pl.CostEstimate(flops=0, bytes_accessed=0, transcendentals=0),
    )(me, tokens, near, *operands, *after)
    return outs[:3], outs[3:]


def add_products(xs, w_ref, offset):
    total = None
    for i, x_ref in enumerate(xs):
        add = dot(x_ref[...], w_ref[i, offset : offset + x_ref.shape[1], :])
        total = add if total is None else total + add
    return total


def add_levels(xs, wl_ref, offset):
    total = None
    for i, x_ref in enumerate(xs):
        add = dot_dims(x_ref[...], wl_ref[i, :, offset : offset + x_ref.shape[1]], 1, 1)
        total = add if total is None else total + add
    return total


def project(xs, ws, offset, totals, after=()):
    n_x = len(xs)

    def kernel(*refs):
        x, (q_ref, kv_ref, l_ref), ins, outs = refs[:n_x], refs[n_x : n_x + 3], refs[-6:-3], refs[-3:]
        outs[1][...] = ins[1][...] + add_products(x, kv_ref, offset)
        outs[0][...] = ins[0][...] + add_products(x, q_ref, offset)
        outs[2][...] = ins[2][...] + add_levels(x, l_ref, offset)

    ins = [*xs, *ws, *totals]
    aliases = {n_x + 3 + i: i for i in range(3)}
    outs = [shape(t.shape, F32) for t in totals]
    return call(kernel, ins, outs, 0, after, aliases=aliases)


def project_state(xs, wkv, offset, total_kv, keep, head_size):
    rows, depth = xs[0].shape
    n_x = len(xs)
    heads = keep.shape[1]
    kv_width = wkv.shape[2] // 2
    group = heads // (kv_width // head_size)

    def kernel(*refs):
        x, (w_ref, total_ref, keep_ref, k_out, v_out, s_out) = refs[:n_x], refs[n_x:]
        total = total_ref[...] + add_products(x, w_ref, offset)
        keys = total[:, :kv_width].astype(BF16)
        values = total[:, kv_width:].astype(BF16)
        k_out[...] = keys
        v_out[...] = values
        for g in range(kv_width // head_size):
            cols = slice(g * head_size, (g + 1) * head_size)
            kf = keys[:, cols].astype(F32)
            weighted = jnp.concatenate(
                [(kf * keep_ref[:, h : h + 1]).astype(BF16) for h in range(g * group, (g + 1) * group)],
                axis=1,
            )
            wide = slice(g * group * head_size, (g + 1) * group * head_size)
            s_out[:, wide] = dot_dims(values[:, cols], weighted, 0, 0).astype(BF16)

    outs = [
        shape((rows, kv_width), BF16),
        shape((rows, kv_width), BF16),
        shape((head_size, heads * head_size), BF16),
    ]
    return call(kernel, [*xs, wkv, total_kv, keep], outs, 0)


def attend(xs, wq, wl, offset, total_q, total_l, k, v, dcol, drow, spans, states, head_size, level_count):
    rows, width = total_q.shape
    n_x = len(xs)
    bits = len(spans)
    heads = width // head_size
    group = heads // (k.shape[1] // head_size)
    own_levels = level_count - bits

    def kernel(*refs):
        x, refs = refs[:n_x], refs[n_x:]
        wq_ref, wl_ref, tq_ref, tl_ref, k_ref, v_ref, dcol_ref, drow_ref = refs[:8]
        span_refs, state_refs = refs[8 : 8 + bits], refs[8 + bits : 7 + 2 * bits]
        o_ref, s_ref, q_ref, l_ref = refs[-4:]
        raw = tl_ref[...] + add_levels(x, wl_ref, offset)
        l_ref[...] = jnp.maximum(raw, 0.0) + jnp.log1p(jnp.exp(-jnp.abs(raw)))
        q_ref[...] = (tq_ref[...] + add_products(x, wq_ref, offset)).astype(BF16)
        row_id = lax.broadcasted_iota(jnp.int32, (BLOCK, BLOCK), 0)
        col_id = lax.broadcasted_iota(jnp.int32, (BLOCK, BLOCK), 1)
        causal = row_id >= col_id
        for h in range(heads):
            g = h // group
            cols = slice(h * head_size, (h + 1) * head_size)
            kv = slice(g * head_size, (g + 1) * head_size)
            for i in range(rows // BLOCK):
                here = slice(i * BLOCK, (i + 1) * BLOCK)
                span = (i + 1) * BLOCK
                query = q_ref[here, cols]
                scores = dot_dims(query, k_ref[:span, kv], 1, 1)
                d_here = jnp.broadcast_to(dcol_ref[here, h : h + 1], (BLOCK, BLOCK))

                def weight(level):
                    column = h * level_count + level
                    return jnp.broadcast_to(l_ref[here, column : column + 1], (BLOCK, BLOCK))

                weights = {}
                mixed = []
                for j in range(i + 1):
                    level = (i ^ j).bit_length()
                    if level not in weights:
                        weights[level] = weight(level)
                    there = slice(j * BLOCK, (j + 1) * BLOCK)
                    gap = d_here - drow_ref[h : h + 1, there]
                    if i == j:
                        gap = jnp.where(causal, gap, -jnp.inf)
                    mixed.append((weights[level] * jnp.exp(gap) * scores[:, there]).astype(BF16))
                mixing = mixed[0] if i == 0 else jnp.concatenate(mixed, axis=1)
                total = dot(mixing, v_ref[:span, kv])
                wide = query.astype(F32)
                for b in range(bits):
                    factor = weight(own_levels + b) * jnp.exp(d_here + span_refs[b][0:1, cols])
                    scaled = (wide * factor).astype(BF16)
                    if b == bits - 1:
                        s_ref[here, cols] = scaled
                    else:
                        total = total + dot_dims(scaled, state_refs[b][:, cols], 1, 1)
                o_ref[here, cols] = total

    ins = [*xs, wq, wl, total_q, total_l, k, v, dcol, drow, *spans, *states]
    wide = shape((rows, width), BF16)
    outs = [shape((rows, width), F32), wide, wide, shape(total_l.shape, F32)]
    flops = 2 * rows * xs[0].shape[1] * n_x * width + 4 * rows * rows * width
    return call(kernel, ins, outs, flops)[:2]


def finish(local, scaled, state, rows, head_size, after=()):
    width = local.shape[1]

    def kernel(o_ref, q_ref, s_ref, n_ref):
        for c in range(0, width, head_size):
            cols = slice(c, c + head_size)
            total = o_ref[rows, cols] + dot_dims(q_ref[rows, cols], s_ref[:, cols], 1, 1)
            mean = jnp.mean(total * total, axis=-1, keepdims=True)
            n_ref[:, cols] = (total * lax.rsqrt(mean + 1e-05)).astype(BF16)

    outs = [shape((rows.stop - rows.start, width), BF16)]
    return call(kernel, [local, scaled, state], outs, 0, after)[0]


def cut_blocks(me, w_out, after, tile=256):
    depth, columns = w_out.shape
    block = columns // 4
    steps = block // tile

    def kernel(me_ref, *refs):
        for w_ref, o_ref in zip(refs[:4], refs[-4:]):
            o_ref[...] = w_ref[...]

    in_specs = [
        pl.BlockSpec((depth, tile), lambda s, m, i=i: (0, (m[0] ^ i) * steps + s)) for i in range(4)
    ]
    return pl.pallas_call(
        kernel,
        grid_spec=pltpu.PrefetchScalarGridSpec(
            num_scalar_prefetch=1,
            grid=(steps,),
            in_specs=in_specs + [ANY] * len(after),
            out_specs=[pl.BlockSpec((depth, tile), lambda s, m: (0, s))] * 4,
        ),
        out_shape=[shape((depth, block), w_out.dtype)] * 4,
        compiler_params=pltpu.CompilerParams(vmem_limit_bytes=8 * 1024 * 1024),
        cost_estimate=pl.CostEstimate(flops=0, bytes_accessed=0, transcendentals=0),
    )(me, *[w_out] * 4, *after)


def out_far(n0, n1, w0, w1, rows_own, rows_near):
    rows, columns = rows_own.stop - rows_own.start, w1.shape[1]
    tile = min(columns, 512)

    def kernel(n0_ref, n1_ref, w0_ref, w1_ref, o_ref):
        for c in range(0, columns, tile):
            cols = slice(c, c + tile)
            o_ref[:, cols] = (
                dot(n0_ref[rows_own, :], w0_ref[:, cols]) + dot(n1_ref[rows_near, :], w1_ref[:, cols])
            ).astype(BF16)

    return call(kernel, [n0, n1, w0, w1], [shape((rows, columns), BF16)], 0)[0]


def out_here(n0, n1, w0, w1, rows_own, rows_near, arrived, out, total_rows, start_row):
    rows, columns = arrived.shape
    block = start_row // rows
    tile = min(columns, 512)

    def kernel(n0_ref, n1_ref, w0_ref, w1_ref, a_ref, *refs):
        o_ref = refs[-1]
        for c in range(0, columns, tile):
            cols = slice(c, c + tile)
            here = dot(n0_ref[rows_own, :], w0_ref[:, cols]) + dot(n1_ref[rows_near, :], w1_ref[:, cols])
            o_ref[:, cols] = (here + a_ref[:, cols].astype(F32)).astype(BF16)

    ins, specs, aliases = [n0, n1, w0, w1, arrived], [VMEM] * 5, {}
    if out is not None:
        ins, specs, aliases = ins + [out], specs + [ANY], {5: 0}
    return pl.pallas_call(
        kernel,
        grid=(1,),
        in_specs=specs,
        out_specs=pl.BlockSpec((rows, columns), lambda s: (block, 0)),
        out_shape=shape((total_rows, columns), BF16),
        input_output_aliases=aliases,
        compiler_params=pltpu.CompilerParams(vmem_limit_bytes=8 * 1024 * 1024),
        cost_estimate=pl.CostEstimate(
            flops=4 * rows * columns * w0.shape[0], bytes_accessed=rows * columns * 16, transcendentals=0
        ),
    )(*ins)


def body(tokens, log_decay, w_query, w_key, w_value, w_level, w_out):
    rows, shard = tokens.shape
    heads = log_decay.shape[1]
    head_size = w_out.shape[0] // heads
    level_count = w_level.shape[1] // heads
    seq_size = lax.axis_size("seq")
    seq_bits = seq_size.bit_length() - 1
    me = jnp.full((1,), lax.axis_index("tp"), jnp.int32)
    slab = jnp.full((1,), lax.axis_index("seq"), jnp.int32)

    def swap_tp(x, bit):
        return lax.ppermute(x, "tp", [(i, i ^ bit) for i in range(4)])

    def swap_seq(x, bit, both=True):
        return lax.ppermute(x, "seq", [(i, i ^ bit) for i in range(seq_size) if both or not i & bit])

    half = shard // 2
    first, second = cut_columns(tokens, 2)
    far_first, far_second = swap_tp(first, 2), swap_tp(second, 2)
    near = swap_tp(tokens, 1)

    drow, dcol, keep, total, span = decays(slab, log_decay.T, head_size)
    spans, factors, before = [span], [], None
    for b in range(seq_bits - 1):
        total, before, own, other, span = link(slab, b, total, swap_seq(total, 1 << b), before)
        spans.append(span)
        factors.append((own, other))

    totals, ws = project_first(me, tokens, near, (w_query, w_key, w_value, w_level.T))
    w_here_own, w_here_send, w_far_own, w_far_send = cut_blocks(me, w_out, (totals[0],))
    w_here, w_far = swap_tp(w_here_send, 1), swap_tp(w_far_send, 1)
    arrived = gate(far_first, total, w_here_send)
    later = gate(far_second, totals[0])
    totals = project((arrived, swap_tp(arrived, 1)), ws, 0, totals, (w_far, w_here))
    arrived = later
    pair = (arrived[0], swap_tp(arrived[0], 1))
    totals = project(pair, ws, half, totals)
    pair = (arrived[1], swap_tp(arrived[1], 1))
    last = half + half // 2
    wq, wkv, wl = ws
    total_q, total_kv, total_l = totals
    k, v, state = project_state(pair, wkv, last, total_kv, keep, head_size)

    earlier = []
    for b in range(seq_bits):
        other = swap_seq(state, 1 << b, b < seq_bits - 1)
        earlier.append(other)
        if b < seq_bits - 1:
            state = combine(state, other, *factors[b])

    local, scaled = attend(
        pair, wq, wl, last, total_q, total_l, k, v, dcol, drow, spans, earlier[:-1], head_size, level_count
    )

    step = rows // 4
    normed = []
    for cut in (slice(0, step), slice(step, rows)):
        after = (normed[0][0],) if normed else ()
        own = finish(local, scaled, earlier[-1], cut, head_size, after)
        normed.append((own, swap_tp(own, 1)))
    pieces = [(normed[0], 0, 0)] + [(normed[1], r, r + step) for r in range(0, rows - step, step)]
    crossing = []
    for pair, r, _ in pieces:
        cut = slice(r, r + step)
        crossing.append(out_far(*pair, w_far_own, w_far, cut, cut))
    out = None
    for (pair, r, start), x in zip(pieces, crossing):
        cut = slice(r, r + step)
        out = out_here(*pair, w_here_own, w_here, cut, cut, swap_tp(x, 2), out, rows, start)
    return out


def solution(mesh):
    in_specs = (
        P("seq", "tp"),
        P("seq", "tp"),
        P(None, "tp"),
        P(None, "tp"),
        P(None, "tp"),
        P(None, "tp"),
        P("tp", None),
    )
    out_specs = P("seq", "tp")
    return jax.shard_map(body, mesh=mesh, in_specs=in_specs, out_specs=out_specs, check_vma=False)
```

time: 133 us -> 90.4 us (0.68)
  local copies, waits for them, and re-layouts: 41.3 us -> 11.1 us
  Pallas kernels: 31.6 us -> 24.3 us
  other arithmetic: 4.12 us -> 0 us
    unnamed x78 -> x36, local copies, waits for them, and re-layouts: 30.4 us -> 9.99 us
    pallas_call x15 -> x16, Pallas kernels: 28.6 us -> 12.6 us  [call(): pl.pallas_call(run, in_specs=[SMEM] * smem + [VMEM] * (count - smem) + [A...]
    pallas_call x4 -> x6, Pallas kernels: 2.99 us -> 11.7 us  [the longest x4 4.64 us: out_here(): pl.pallas_call(kernel, grid=(1,), in_specs=specs, out_specs=pl.BlockSpec(...]
    dynamic_slice x1 -> x0, local copies, waits for them, and re-layouts: 3.89 us -> none  [columns_of(): return lax.dynamic_slice_in_dim(w_out, place * shard, shard, axis=1)]
    slice x4 -> x0, local copies, waits for them, and re-layouts: 3.31 us -> none  [the longest x1 2 us: body(): tokens_later[:, p * depth:(p + 1) * depth]]
    ppermute x19 -> x14, starting transfers between devices: 12.5 us -> 9.49 us  [swap_tp(): return lax.ppermute(x, 'tp', [(i, i ^ bit) for i in range(4)])]
    ppermute x5, starting transfers between devices: 8.14 us -> 10.9 us  [swap_seq(): lax.ppermute(x, 'seq', [(i, i ^ bit) for i in range(seq_size) if both or...]
    exp x4 -> x0, other arithmetic: 1.67 us -> none  [the longest x1 0.99 us: body(): jnp.exp(dcol[:, :, None] + jnp.stack(spans, axis=-1)[None])]
  transfers between devices with their start and end apart: 24 -> 19, of which waited for: 10 -> 10; matrix products, arithmetic and copies ran while one was open for 12% -> 1% of each run, Pallas kernels for 21% -> 24%
where the time goes in v3:
time: 90.4 us; the launch traced here: 90 us
  waiting for transfers between devices  34 us (38%)
  Pallas kernels  24.3 us (27%)
  starting transfers between devices  20.4 us (23%)
  local copies, waits for them, and re-layouts  11.1 us (12%)
    ppermute x14, waiting for transfers between devices, swap_tp(): return lax.ppermute(x, 'tp', [(i, i ^ bit) for i in range(4)])  22.2 us
    pallas_call x16, Pallas kernels, call(): pl.pallas_call(run, in_specs=[SMEM] * smem + [VMEM] * (count - smem) + [A...  12.6 us
    ppermute x5, waiting for transfers between devices, swap_seq(): lax.ppermute(x, 'seq', [(i, i ^ bit) for i in range(seq_size) if both or...  11.8 us
    ppermute x5, starting transfers between devices, swap_seq(): lax.ppermute(x, 'seq', [(i, i ^ bit) for i in range(seq_size) if both or...  10.9 us
    unnamed x36, local copies, waits for them, and re-layouts  9.99 us
    ppermute x14, starting transfers between devices, swap_tp(): return lax.ppermute(x, 'tp', [(i, i ^ bit) for i in range(4)])  9.49 us
    pallas_call x4, Pallas kernels, out_here(): pl.pallas_call(kernel, grid=(1,), in_specs=specs, out_specs=pl.BlockSpec(...  4.64 us
    pallas_call x1, Pallas kernels, project_first(): pl.pallas_call(kernel, grid_spec=pltpu.PrefetchScalarGridSpec(num_scalar_...  4.01 us
  transfers between devices with their start and end apart: 19, of which 10 were waited for; matrix products, arithmetic and copies ran while one was open for 1% of the time, Pallas kernels for 24%

profile of v3, /device:TPU:0, one launch (start us, length us, event | category | flops | bytes accessed | tf_op | source)
XLA Modules:
  0.0 90.0 jit_solution(2742630727123654076)
XLA Ops:
  0.5 1.2 %copy-done.14 = bf16[512,1024]{1,0:T(8,128)(2,1)S(1)} copy-done((bf16[512,1024]{1,0:T(8,128)(2,1)S(1)}, bf16[512,1024]{1,0:T(8,128)(2,1)}, u32[]{:S(2)}) %copy-start.14) | copy-done | bytes 1048600
  2.8 2.5 %collective-permute-start.4 = (bf16[512,512]{1,0:T(8,128)(2,1)}, bf16[512,512]{1,0:T(8,128)(2,1)}, u32[]{:S(2)}, u32[]{:S(2)}) collective-permute-start(bf16[512,512]{1,0:T(8,128)(2,1)} %get-tuple-element.47), channel_id=1, source_target_pairs={{0,2},{1,3},{2,0},{3,1},{4,6},{5,7},{6,4},{7,5},{8,10},{9,11},{10,... | collective-permute-start | bytes 1572872 | tf_op jit(solution)/shard_map/ppermute | solution.py:425
  5.3 2.2 %copy-done.1 = bf16[4096,512]{1,0:T(8,128)(2,1)S(1)} copy-done((bf16[4096,512]{1,0:T(8,128)(2,1)S(1)}, bf16[4096,512]{1,0:T(8,128)(2,1)}, u32[]{:S(2)}) %copy-start.1) | copy-done | bytes 4194328
  12.1 4.0 %shard_map.74 = (f32[512,512]{1,0:T(8,128)S(1)}, f32[512,256]{1,0:T(8,128)S(1)}, f32[512,24]{1,0:T(8,128)S(1)}, bf16[2,1024,512]{2,1,0:T(8,128)(2,1)S(1)}, bf16[...) custom-call(s32[1]{0:T(128)} %bitcast.me_ref, bf16[512,1024]{1,0:T(8,128)(2,1)S(1)} %copy-done.15, ...), custom_call_target="tpu_custom_call" | custom-call | tf_op jit(solution)/shard_map/pallas_call | solution.py:189
  16.1 3.1 %shard_map.79 = (bf16[512,1024]{1,0:T(8,128)(2,1)S(1)}, bf16[512,1024]{1,0:T(8,128)(2,1)}, bf16[512,1024]{1,0:T(8,128)(2,1)S(1)}, bf16[512,1024]{1,0:T(8,128)(2,1)}) custom-call(s32[1]{0:T(128)} %bitcast.me_ref, bf16[512,4096]{1,0:T(8,128)(2,1)S(1)} %copy-done, bf16[512,4096]{1,0:T(8,128)(2,1)S(1)} %copy-done, bf16[512,4096]{1,0:T(8,128)(2,1)S(1)} %copy-done, ...), custom_call_target="tpu_custom_call" | custom-call | tf_op jit(solution)/shard_map/pallas_call | solution.py:357
  23.1 1.6 %collective-permute-start.5 = (f32[8,512]{1,0:T(8,128)S(1)}, f32[8,512]{1,0:T(8,128)S(1)}, u32[]{:S(2)}, u32[]{:S(2)}) collective-permute-start(f32[8,512]{1,0:T(8,128)S(1)} %get-tuple-element.48.refs_1_), channel_id=1, source_target_pairs={{0,4},{4,0},{8,12},{12,8},{16,20},{20,16},{24,28},{28,24},{1,5},{5... | collective-permute-start | bytes 49160 | tf_op jit(solution)/shard_map/ppermute | solution.py:428
  24.7 2.2 %collective-permute-done.5.refs_2_ = f32[8,512]{1,0:T(8,128)S(1)} collective-permute-done((f32[8,512]{1,0:T(8,128)S(1)}, f32[8,512]{1,0:T(8,128)S(1)}, u32[]{:S(2)}, u32[]{:S(2)}) %collective-permute-start.5) | collective-permute-done | bytes 16416 | tf_op jit(solution)/shard_map/ppermute | solution.py:428
  27.0 1.6 %collective-permute-start.6 = (f32[8,512]{1,0:T(8,128)S(1)}, f32[8,512]{1,0:T(8,128)S(1)}, u32[]{:S(2)}, u32[]{:S(2)}) collective-permute-start(f32[8,512]{1,0:T(8,128)S(1)} %get-tuple-element.49.refs_1_), channel_id=1, source_target_pairs={{0,8},{4,12},{8,0},{12,4},{16,24},{20,28},{24,16},{28,20},{1,9},{5... | collective-permute-start | bytes 49160 | tf_op jit(solution)/shard_map/ppermute | solution.py:428
  28.6 2.2 %collective-permute-done.6.refs_2_ = f32[8,512]{1,0:T(8,128)S(1)} collective-permute-done((f32[8,512]{1,0:T(8,128)S(1)}, f32[8,512]{1,0:T(8,128)S(1)}, u32[]{:S(2)}, u32[]{:S(2)}) %collective-permute-start.6) | collective-permute-done | bytes 16416 | tf_op jit(solution)/shard_map/ppermute | solution.py:428
  31.4 4.7 %collective-permute-done.refs_0_ = bf16[2,512,256]{2,1,0:T(8,128)(2,1)} collective-permute-done((bf16[2,512,256]{2,1,0:T(8,128)(2,1)}, bf16[2,512,256]{2,1,0:T(8,128)(2,1)}, u32[]{:S(2)}, u32[]{:S(2)}) %collective-permute-start) | collective-permute-done | bytes 524320 | tf_op jit(solution)/shard_map/ppermute | solution.py:425
  37.8 2.4 %shard_map.81 = (f32[512,512]{1,0:T(8,128)S(1)}, f32[512,256]{1,0:T(8,128)S(1)}, f32[512,24]{1,0:T(8,128)S(1)}) custom-call(bf16[512,512]{1,0:T(8,128)(2,1)} %shard_map.80.refs_0_, bf16[512,512]{1,0:T(8,128)(2,1)S(1)} %collective-permute-done.7.refs_1_, ...), custom_call_target="tpu_custom_call", output_to_operand_aliasing={{0}: (5, {}), {1}: (6, {}), {2}: (7, {})} | custom-call | tf_op jit(solution)/shard_map/pallas_call | solution.py:37
  41.6 1.6 %collective-permute-start.10 = (bf16[128,512]{1,0:T(8,128)(2,1)S(1)}, bf16[128,512]{1,0:T(8,128)(2,1)S(1)}, u32[]{:S(2)}, u32[]{:S(2)}) collective-permute-start(bf16[128,512]{1,0:T(8,128)(2,1)S(1)} %get-tuple-element.70.refs_0_), channel_id=1, source_target_pairs={{0,4},{4,0},{8,12},{12,8},{16,20},{20,16},{24,28},{28,24},{1,5},{5... | collective-permute-start | bytes 393224 | tf_op jit(solution)/shard_map/ppermute | solution.py:428
  43.2 4.0 %collective-permute-done.10.refs_1_.refs_13_ = bf16[128,512]{1,0:T(8,128)(2,1)S(1)} collective-permute-done((bf16[128,512]{1,0:T(8,128)(2,1)S(1)}, bf16[128,512]{1,0:T(8,128)(2,1)S(1)}, u32[]{:S(2)}, u32[]{:S(2)}) %collective-permute-start.10) | collective-permute-done | bytes 131104 | tf_op jit(solution)/shard_map/ppermute | solution.py:428
  47.2 1.6 %collective-permute-start.11 = (bf16[128,512]{1,0:T(8,128)(2,1)S(1)}, bf16[128,512]{1,0:T(8,128)(2,1)S(1)}, u32[]{:S(2)}, u32[]{:S(2)}) collective-permute-start(bf16[128,512]{1,0:T(8,128)(2,1)S(1)} %shard_map.84.refs_0_), channel_id=1, source_target_pairs={{0,8},{4,12},{8,0},{12,4},{16,24},{20,28},{24,16},{28,20},{1,9},{5... | collective-permute-start | bytes 393224 | tf_op jit(solution)/shard_map/ppermute | solution.py:428
  48.8 3.4 %collective-permute-done.11.refs_14_.refs_1_ = bf16[128,512]{1,0:T(8,128)(2,1)S(1)} collective-permute-done((bf16[128,512]{1,0:T(8,128)(2,1)S(1)}, bf16[128,512]{1,0:T(8,128)(2,1)S(1)}, u32[]{:S(2)}, u32[]{:S(2)}) %collective-permute-start.11) | collective-permute-done | bytes 131104 | tf_op jit(solution)/shard_map/ppermute | solution.py:428
  52.3 4.5 %collective-permute-start.12 = (bf16[128,512]{1,0:T(8,128)(2,1)S(1)}, bf16[128,512]{1,0:T(8,128)(2,1)S(1)}, u32[]{:S(2)}, u32[]{:S(2)}) collective-permute-start(bf16[128,512]{1,0:T(8,128)(2,1)S(1)} %shard_map.86), channel_id=1, source_target_pairs={{0,16},{4,20},{8,24},{12,28},{1,17},{5,21},{9,25},{13,29},{2,18},{... | collective-permute-start | bytes 393224 | tf_op jit(solution)/shard_map/ppermute | solution.py:428
  56.8 3.6 %shard_map.85 = (f32[512,512]{1,0:T(8,128)S(1)}, bf16[512,512]{1,0:T(8,128)(2,1)S(1)}, bf16[512,512]{1,0:T(8,128)(2,1)}, f32[512,24]{1,0:T(8,128)}) custom-call(bf16[512,256]{1,0:T(8,128)(2,1)S(1)} %get-tuple-element.80.refs_0_, bf16[512,256]{1,0:T(8,128)(2,1)S(1)} %collective-permute-done.2.refs_1_, bf16[2,1024,512]{2,1,0:T(8,128)(2,1)S(1)} %copy-done.3, ...), custom_call_target="tpu_custom_call" | custom-call | flops 805306368 | bytes 6553600 | tf_op jit(solution)/shard_map/pallas_call | solution.py:37
  61.7 1.4 %collective-permute-done.17.refs_1_.n1_ref = bf16[128,512]{1,0:T(8,128)(2,1)S(1)} collective-permute-done((bf16[128,512]{1,0:T(8,128)(2,1)S(1)}, bf16[128,512]{1,0:T(8,128)(2,1)S(1)}, u32[]{:S(2)}, u32[]{:S(2)}) %collective-permute-start.17) | collective-permute-done | bytes 131104 | tf_op jit(solution)/shard_map/ppermute | solution.py:425
  64.6 1.6 %collective-permute-start.16 = (bf16[128,1024]{1,0:T(8,128)(2,1)S(1)}, bf16[128,1024]{1,0:T(8,128)(2,1)S(1)}, u32[]{:S(2)}, u32[]{:S(2)}) collective-permute-start(bf16[128,1024]{1,0:T(8,128)(2,1)S(1)} %shard_map.91), channel_id=1, source_target_pairs={{0,2},{1,3},{2,0},{3,1},{4,6},{5,7},{6,4},{7,5},{8,10},{9,11},{10,... | collective-permute-start | bytes 786440 | tf_op jit(solution)/shard_map/ppermute | solution.py:425
  67.7 1.6 %collective-permute-start.14 = (bf16[128,1024]{1,0:T(8,128)(2,1)S(1)}, bf16[128,1024]{1,0:T(8,128)(2,1)S(1)}, u32[]{:S(2)}, u32[]{:S(2)}) collective-permute-start(bf16[128,1024]{1,0:T(8,128)(2,1)S(1)} %shard_map.89), channel_id=1, source_target_pairs={{0,2},{1,3},{2,0},{3,1},{4,6},{5,7},{6,4},{7,5},{8,10},{9,11},{10,... | collective-permute-start | bytes 786440 | tf_op jit(solution)/shard_map/ppermute | solution.py:425
  69.3 3.5 %collective-permute-done.18.a_ref = bf16[128,1024]{1,0:T(8,128)(2,1)S(1)} collective-permute-done((bf16[128,1024]{1,0:T(8,128)(2,1)S(1)}, bf16[128,1024]{1,0:T(8,128)(2,1)S(1)}, u32[]{:S(2)}, u32[]{:S(2)}) %collective-permute-start.18) | collective-permute-done | bytes 262176 | tf_op jit(solution)/shard_map/ppermute | solution.py:425
  74.0 4.4 %collective-permute-done.16.a_ref = bf16[128,1024]{1,0:T(8,128)(2,1)S(1)} collective-permute-done((bf16[128,1024]{1,0:T(8,128)(2,1)S(1)}, bf16[128,1024]{1,0:T(8,128)(2,1)S(1)}, u32[]{:S(2)}, u32[]{:S(2)}) %collective-permute-start.16) | collective-permute-done | bytes 262176 | tf_op jit(solution)/shard_map/ppermute | solution.py:425
  79.6 4.5 %collective-permute-done.15.a_ref = bf16[128,1024]{1,0:T(8,128)(2,1)S(1)} collective-permute-done((bf16[128,1024]{1,0:T(8,128)(2,1)S(1)}, bf16[128,1024]{1,0:T(8,128)(2,1)S(1)}, u32[]{:S(2)}, u32[]{:S(2)}) %collective-permute-start.15) | collective-permute-done | bytes 262176 | tf_op jit(solution)/shard_map/ppermute | solution.py:425
  85.2 3.6 %collective-permute-done.14.a_ref = bf16[128,1024]{1,0:T(8,128)(2,1)S(1)} collective-permute-done((bf16[128,1024]{1,0:T(8,128)(2,1)S(1)}, bf16[128,1024]{1,0:T(8,128)(2,1)S(1)}, u32[]{:S(2)}, u32[]{:S(2)}) %collective-permute-start.14) | collective-permute-done | bytes 262176 | tf_op jit(solution)/shard_map/ppermute | solution.py:425
  (75 shorter events, 22.7 us)
Async XLA Ops:
  0.0 5.3 %collective-permute-start.1 = (bf16[512,1024]{1,0:T(8,128)(2,1)}, bf16[512,1024]{1,0:T(8,128)(2,1)S(1)}, u32[]{:S(2)}, u32[]{:S(2)}) collective-permute-start(bf16[512,1024]{1,0:T(8,128)(2,1)} %refs_0_.4), channel_id=1, source_target_pairs={{0,1},{1,0},{2,3},{3,2},{4,5},{5,4},{6,7},{7,6},{8,9},{9,8},{10,11... | collective-permute-start | bytes 3145736 | tf_op jit(solution)/shard_map/ppermute | solution.py:425
  2.8 28.6 %collective-permute-start.4 = (bf16[512,512]{1,0:T(8,128)(2,1)}, bf16[512,512]{1,0:T(8,128)(2,1)}, u32[]{:S(2)}, u32[]{:S(2)}) collective-permute-start(bf16[512,512]{1,0:T(8,128)(2,1)} %get-tuple-element.47), channel_id=1, source_target_pairs={{0,2},{1,3},{2,0},{3,1},{4,6},{5,7},{6,4},{7,5},{8,10},{9,11},{10,... | collective-permute-start | bytes 1572872 | tf_op jit(solution)/shard_map/ppermute | solution.py:425
  21.2 16.5 %collective-permute-start.9 = (bf16[512,1024]{1,0:T(8,128)(2,1)}, bf16[512,1024]{1,0:T(8,128)(2,1)S(1)}, u32[]{:S(2)}, u32[]{:S(2)}) collective-permute-start(bf16[512,1024]{1,0:T(8,128)(2,1)} %get-tuple-element.52.refs_2_), channel_id=1, source_target_pairs={{0,1},{1,0},{2,3},{3,2},{4,5},{5,4},{6,7},{7,6},{8,9},{9,8},{10,11... | collective-permute-start | bytes 3145736 | tf_op jit(solution)/shard_map/ppermute | solution.py:425
  21.4 16.3 %collective-permute-start.8 = (bf16[512,1024]{1,0:T(8,128)(2,1)}, bf16[512,1024]{1,0:T(8,128)(2,1)S(1)}, u32[]{:S(2)}, u32[]{:S(2)}) collective-permute-start(bf16[512,1024]{1,0:T(8,128)(2,1)} %get-tuple-element.55), channel_id=1, source_target_pairs={{0,1},{1,0},{2,3},{3,2},{4,5},{5,4},{6,7},{7,6},{8,9},{9,8},{10,11... | collective-permute-start | bytes 3145736 | tf_op jit(solution)/shard_map/ppermute | solution.py:425
  21.7 14.4 %collective-permute-start = (bf16[2,512,256]{2,1,0:T(8,128)(2,1)}, bf16[2,512,256]{2,1,0:T(8,128)(2,1)}, u32[]{:S(2)}, u32[]{:S(2)}) collective-permute-start(bf16[2,512,256]{2,1,0:T(8,128)(2,1)} %get-tuple-element.42), channel_id=1, source_target_pairs={{0,2},{1,3},{2,0},{3,1},{4,6},{5,7},{6,4},{7,5},{8,10},{9,11},{10,... | collective-permute-start | bytes 1572872 | tf_op jit(solution)/shard_map/ppermute | solution.py:425
  22.3 15.5 %copy-start.3 = (bf16[2,1024,512]{2,1,0:T(8,128)(2,1)S(1)}, bf16[2,1024,512]{2,1,0:T(8,128)(2,1)}, u32[]{:S(2)}) copy-start(bf16[2,1024,512]{2,1,0:T(8,128)(2,1)} %copy-done.2) | copy-start | bytes 6291460
  22.3 15.5 %copy-start.11 = (bf16[2,1024,256]{2,1,0:T(8,128)(2,1)S(1)}, bf16[2,1024,256]{2,1,0:T(8,128)(2,1)}, u32[]{:S(2)}) copy-start(bf16[2,1024,256]{2,1,0:T(8,128)(2,1)} %copy-done.10) | copy-start | bytes 3145732
  22.3 15.5 %copy-start.13 = (f32[512,256]{1,0:T(8,128)S(1)}, f32[512,256]{1,0:T(8,128)}, u32[]{:S(2)}) copy-start(f32[512,256]{1,0:T(8,128)} %copy-done.12) | copy-start | bytes 1572868
  23.1 3.8 %collective-permute-start.5 = (f32[8,512]{1,0:T(8,128)S(1)}, f32[8,512]{1,0:T(8,128)S(1)}, u32[]{:S(2)}, u32[]{:S(2)}) collective-permute-start(f32[8,512]{1,0:T(8,128)S(1)} %get-tuple-element.48.refs_1_), channel_id=1, source_target_pairs={{0,4},{4,0},{8,12},{12,8},{16,20},{20,16},{24,28},{28,24},{1,5},{5... | collective-permute-start | bytes 49160 | tf_op jit(solution)/shard_map/ppermute | solution.py:428
  27.0 3.8 %collective-permute-start.6 = (f32[8,512]{1,0:T(8,128)S(1)}, f32[8,512]{1,0:T(8,128)S(1)}, u32[]{:S(2)}, u32[]{:S(2)}) collective-permute-start(f32[8,512]{1,0:T(8,128)S(1)} %get-tuple-element.49.refs_1_), channel_id=1, source_target_pairs={{0,8},{4,12},{8,0},{12,4},{16,24},{20,28},{24,16},{28,20},{1,9},{5... | collective-permute-start | bytes 49160 | tf_op jit(solution)/shard_map/ppermute | solution.py:428
  31.4 6.4 %collective-permute-start.7 = (bf16[512,512]{1,0:T(8,128)(2,1)}, bf16[512,512]{1,0:T(8,128)(2,1)S(1)}, u32[]{:S(2)}, u32[]{:S(2)}) collective-permute-start(bf16[512,512]{1,0:T(8,128)(2,1)} %shard_map.80.refs_0_), channel_id=1, source_target_pairs={{0,1},{1,0},{2,3},{3,2},{4,5},{5,4},{6,7},{7,6},{8,9},{9,8},{10,11... | collective-permute-start | bytes 1572872 | tf_op jit(solution)/shard_map/ppermute | solution.py:425
  37.1 3.0 %collective-permute-start.3 = (bf16[512,256]{1,0:T(8,128)(2,1)S(1)}, bf16[512,256]{1,0:T(8,128)(2,1)S(1)}, u32[]{:S(2)}, u32[]{:S(2)}) collective-permute-start(bf16[512,256]{1,0:T(8,128)(2,1)S(1)} %get-tuple-element.79.refs_0_), channel_id=1, source_target_pairs={{0,1},{1,0},{2,3},{3,2},{4,5},{5,4},{6,7},{7,6},{8,9},{9,8},{10,11... | collective-permute-start | bytes 786440 | tf_op jit(solution)/shard_map/ppermute | solution.py:425
  37.2 3.7 %collective-permute-start.2 = (bf16[512,256]{1,0:T(8,128)(2,1)S(1)}, bf16[512,256]{1,0:T(8,128)(2,1)S(1)}, u32[]{:S(2)}, u32[]{:S(2)}) collective-permute-start(bf16[512,256]{1,0:T(8,128)(2,1)S(1)} %get-tuple-element.80.refs_0_), channel_id=1, source_target_pairs={{0,1},{1,0},{2,3},{3,2},{4,5},{5,4},{6,7},{7,6},{8,9},{9,8},{10,11... | collective-permute-start | bytes 786440 | tf_op jit(solution)/shard_map/ppermute | solution.py:425
  41.6 5.5 %collective-permute-start.10 = (bf16[128,512]{1,0:T(8,128)(2,1)S(1)}, bf16[128,512]{1,0:T(8,128)(2,1)S(1)}, u32[]{:S(2)}, u32[]{:S(2)}) collective-permute-start(bf16[128,512]{1,0:T(8,128)(2,1)S(1)} %get-tuple-element.70.refs_0_), channel_id=1, source_target_pairs={{0,4},{4,0},{8,12},{12,8},{16,20},{20,16},{24,28},{28,24},{1,5},{5... | collective-permute-start | bytes 393224 | tf_op jit(solution)/shard_map/ppermute | solution.py:428
  47.2 5.0 %collective-permute-start.11 = (bf16[128,512]{1,0:T(8,128)(2,1)S(1)}, bf16[128,512]{1,0:T(8,128)(2,1)S(1)}, u32[]{:S(2)}, u32[]{:S(2)}) collective-permute-start(bf16[128,512]{1,0:T(8,128)(2,1)S(1)} %shard_map.84.refs_0_), channel_id=1, source_target_pairs={{0,8},{4,12},{8,0},{12,4},{16,24},{20,28},{24,16},{28,20},{1,9},{5... | collective-permute-start | bytes 393224 | tf_op jit(solution)/shard_map/ppermute | solution.py:428
  52.3 8.1 %collective-permute-start.12 = (bf16[128,512]{1,0:T(8,128)(2,1)S(1)}, bf16[128,512]{1,0:T(8,128)(2,1)S(1)}, u32[]{:S(2)}, u32[]{:S(2)}) collective-permute-start(bf16[128,512]{1,0:T(8,128)(2,1)S(1)} %shard_map.86), channel_id=1, source_target_pairs={{0,16},{4,20},{8,24},{12,28},{1,17},{5,21},{9,25},{13,29},{2,18},{... | collective-permute-start | bytes 393224 | tf_op jit(solution)/shard_map/ppermute | solution.py:428
  56.8 6.4 %copy-start.9 = (bf16[512,1024]{1,0:T(8,128)(2,1)S(1)}, bf16[512,1024]{1,0:T(8,128)(2,1)}, u32[]{:S(2)}) copy-start(bf16[512,1024]{1,0:T(8,128)(2,1)} %copy-done.8) | copy-start | bytes 3145732
  61.2 3.0 %collective-permute-start.13 = (bf16[384,512]{1,0:T(8,128)(2,1)S(1)}, bf16[384,512]{1,0:T(8,128)(2,1)S(1)}, u32[]{:S(2)}, u32[]{:S(2)}) collective-permute-start(bf16[384,512]{1,0:T(8,128)(2,1)S(1)} %shard_map.88.refs_0_.n0_ref), channel_id=1, source_target_pairs={{0,1},{1,0},{2,3},{3,2},{4,5},{5,4},{6,7},{7,6},{8,9},{9,8},{10,11... | collective-permute-start | bytes 1179656 | tf_op jit(solution)/shard_map/ppermute | solution.py:425
  61.2 1.9 %collective-permute-start.17 = (bf16[128,512]{1,0:T(8,128)(2,1)S(1)}, bf16[128,512]{1,0:T(8,128)(2,1)S(1)}, u32[]{:S(2)}, u32[]{:S(2)}) collective-permute-start(bf16[128,512]{1,0:T(8,128)(2,1)S(1)} %shard_map.87.refs_3_.refs_0_.n0_ref), channel_id=1, source_target_pairs={{0,1},{1,0},{2,3},{3,2},{4,5},{5,4},{6,7},{7,6},{8,9},{9,8},{10,11... | collective-permute-start | bytes 393224 | tf_op jit(solution)/shard_map/ppermute | solution.py:425
  63.6 9.2 %copy-start.7 = (bf16[512,1024]{1,0:T(8,128)(2,1)S(1)}, bf16[512,1024]{1,0:T(8,128)(2,1)}, u32[]{:S(2)}) copy-start(bf16[512,1024]{1,0:T(8,128)(2,1)} %copy-done.6) | copy-start | bytes 3145732
  63.6 9.2 %collective-permute-start.18 = (bf16[128,1024]{1,0:T(8,128)(2,1)S(1)}, bf16[128,1024]{1,0:T(8,128)(2,1)S(1)}, u32[]{:S(2)}, u32[]{:S(2)}) collective-permute-start(bf16[128,1024]{1,0:T(8,128)(2,1)S(1)} %shard_map.92), channel_id=1, source_target_pairs={{0,2},{1,3},{2,0},{3,1},{4,6},{5,7},{6,4},{7,5},{8,10},{9,11},{10,... | collective-permute-start | bytes 786440 | tf_op jit(solution)/shard_map/ppermute | solution.py:425
  64.6 13.8 %collective-permute-start.16 = (bf16[128,1024]{1,0:T(8,128)(2,1)S(1)}, bf16[128,1024]{1,0:T(8,128)(2,1)S(1)}, u32[]{:S(2)}, u32[]{:S(2)}) collective-permute-start(bf16[128,1024]{1,0:T(8,128)(2,1)S(1)} %shard_map.91), channel_id=1, source_target_pairs={{0,2},{1,3},{2,0},{3,1},{4,6},{5,7},{6,4},{7,5},{8,10},{9,11},{10,... | collective-permute-start | bytes 786440 | tf_op jit(solution)/shard_map/ppermute | solution.py:425
  66.7 17.4 %collective-permute-start.15 = (bf16[128,1024]{1,0:T(8,128)(2,1)S(1)}, bf16[128,1024]{1,0:T(8,128)(2,1)S(1)}, u32[]{:S(2)}, u32[]{:S(2)}) collective-permute-start(bf16[128,1024]{1,0:T(8,128)(2,1)S(1)} %shard_map.90), channel_id=1, source_target_pairs={{0,2},{1,3},{2,0},{3,1},{4,6},{5,7},{6,4},{7,5},{8,10},{9,11},{10,... | collective-permute-start | bytes 786440 | tf_op jit(solution)/shard_map/ppermute | solution.py:425
  67.7 21.2 %collective-permute-start.14 = (bf16[128,1024]{1,0:T(8,128)(2,1)S(1)}, bf16[128,1024]{1,0:T(8,128)(2,1)S(1)}, u32[]{:S(2)}, u32[]{:S(2)}) collective-permute-start(bf16[128,1024]{1,0:T(8,128)(2,1)S(1)} %shard_map.89), channel_id=1, source_target_pairs={{0,2},{1,3},{2,0},{3,1},{4,6},{5,7},{6,4},{7,5},{8,10},{9,11},{10,... | collective-permute-start | bytes 786440 | tf_op jit(solution)/shard_map/ppermute | solution.py:425
  (13 other events, 29.6 us)

commit v4 on v3

--- a/solution.py
+++ b/solution.py
@@ -13,6 +13,7 @@
 VMEM = pl.BlockSpec(memory_space=pltpu.VMEM)
 SMEM = pl.BlockSpec(memory_space=pltpu.SMEM)
 ANY = pl.BlockSpec(memory_space=pl.ANY)
+HBM = pl.BlockSpec(memory_space=pltpu.HBM)
 
 
 def dot(a, b):
@@ -27,8 +28,11 @@
     return jax.ShapeDtypeStruct(dims, dtype)
 
 
-def call(kernel, ins, outs, flops, after=(), smem=0, aliases=None, megabytes=8):
+def call(kernel, ins, outs, flops, after=(), smem=0, hbm=0, aliases=None, scratch=(), megabytes=8):
     count = len(ins)
+    ins = list(ins)
+    for i in range(smem, smem + hbm):
+        ins[i] = pltpu.with_memory_space_constraint(ins[i], pltpu.HBM)
 
     def run(*refs):
         kernel(*refs[:count], *refs[count + len(after) :])
@@ -36,10 +40,11 @@
     nbytes = sum(x.size * x.dtype.itemsize for x in (*ins, *outs)) if flops else 0
     return pl.pallas_call(
         run,
-        in_specs=[SMEM] * smem + [VMEM] * (count - smem) + [ANY] * len(after),
+        in_specs=[SMEM] * smem + [HBM] * hbm + [VMEM] * (count - smem - hbm) + [ANY] * len(after),
         out_specs=[VMEM] * len(outs),
         out_shape=list(outs),
         input_output_aliases=aliases or {},
+        scratch_shapes=list(scratch),
         compiler_params=pltpu.CompilerParams(vmem_limit_bytes=megabytes * 1024 * 1024),
         cost_estimate=pl.CostEstimate(flops=flops, bytes_accessed=nbytes, transcendentals=0),
     )(*ins, *after)
@@ -60,47 +65,55 @@
     )(x, *after)
 
 
-def cut_columns(tokens, ways):
-    rows, columns = tokens.shape
-    depth = columns // ways
-
-    def kernel(t_ref, first_ref, second_ref):
-        first_ref[...] = t_ref[:, :depth]
-        second_ref[0] = t_ref[:, depth : depth + depth // 2]
-        second_ref[1] = t_ref[:, depth + depth // 2 :]
-
-    outs = [shape((rows, depth), tokens.dtype), shape((2, rows, depth // 2), tokens.dtype)]
-    return call(kernel, [tokens], outs, 0)
+def copies(pairs, sems):
+    started = [pltpu.make_async_copy(src, dst, sems.at[i]) for i, (src, dst) in enumerate(pairs)]
+    for copy in started:
+        copy.start()
+    return started
+
+
+def cut_columns(tokens, cuts):
+    def kernel(t_ref, *refs):
+        for copy in copies([(t_ref.at[:, cut], o_ref) for cut, o_ref in zip(cuts, refs)], refs[-1]):
+            copy.wait()
+
+    outs = [shape((tokens.shape[0], cut.stop - cut.start), tokens.dtype) for cut in cuts]
+    return call(kernel, [tokens], outs, 0, hbm=1, scratch=[pltpu.SemaphoreType.DMA((len(cuts),))])
+
+
+def split(x, after):
+    rows, columns = x.shape
+
+    def kernel(x_ref, a_ref, b_ref):
+        a_ref[...] = x_ref[:, : columns // 2]
+        b_ref[...] = x_ref[:, columns // 2 :]
+
+    return call(kernel, [x], [shape((rows, columns // 2), x.dtype)] * 2, 0, after)
 
 
 def upper_half(slab_ref, bit):
     return ((slab_ref[0] >> bit) & 1) == 1
 
 
-def decays(slab, log_decay_rows, head_size):
-    heads, rows = log_decay_rows.shape
-
-    def kernel(slab_ref, x_ref, row_ref, col_ref, keep_ref, total_ref, span_ref):
-        x = x_ref[...]
-        x = jnp.concatenate([x, jnp.zeros((-heads % 8, rows), F32)], axis=0) if heads % 8 else x
-        place = lax.broadcasted_iota(jnp.int32, x.shape, 1)
-        shift = 1
-        while shift < rows:
-            x = x + jnp.where(place >= shift, pltpu.roll(x, shift, 1), 0.0)
-            shift *= 2
-        total = x[:, rows - 1 : rows]
-        row_ref[...] = x[:heads]
-        col_ref[...] = jnp.transpose(x)[:, :heads]
-        keep_ref[...] = jnp.transpose(jnp.exp(total - x))[:, :heads]
-        for h in range(heads):
-            total_ref[:, h * head_size : (h + 1) * head_size] = jnp.broadcast_to(
-                total[h : h + 1], (8, head_size)
-            )
-        span_ref[...] = jnp.full(span_ref.shape, jnp.where(upper_half(slab_ref, 0), 0.0, -jnp.inf), F32)
-
-    wide = shape((8, heads * head_size), F32)
-    outs = [shape((heads, rows), F32), shape((rows, heads), F32), shape((rows, heads), F32), wide, wide]
-    return call(kernel, [slab, log_decay_rows], outs, 0, smem=1)
+def decays(slab_ref, x_ref, row_ref, col_ref, keep_ref, total_ref, span_ref):
+    heads, rows = x_ref.shape
+    head_size = total_ref.shape[1] // heads
+    x = x_ref[...]
+    x = jnp.concatenate([x, jnp.zeros((-heads % 8, rows), F32)], axis=0) if heads % 8 else x
+    place = lax.broadcasted_iota(jnp.int32, x.shape, 1)
+    shift = 1
+    while shift < rows:
+        x = x + jnp.where(place >= shift, pltpu.roll(x, shift, 1), 0.0)
+        shift *= 2
+    total = x[:, rows - 1 : rows]
+    row_ref[...] = x[:heads]
+    col_ref[...] = jnp.transpose(x)[:, :heads]
+    keep_ref[...] = jnp.transpose(jnp.exp(total - x))[:, :heads]
+    for h in range(heads):
+        total_ref[:, h * head_size : (h + 1) * head_size] = jnp.broadcast_to(
+            total[h : h + 1], (8, head_size)
+        )
+    span_ref[...] = jnp.full(span_ref.shape, jnp.where(upper_half(slab_ref, 0), 0.0, -jnp.inf), F32)
 
 
 def link(slab, bit, total, other, before):
@@ -131,74 +144,75 @@
     return call(kernel, [state, other, own_factor, other_factor], [shape(state.shape, BF16)], 0)[0]
 
 
-def pad_widths(width):
-    return -(-width // 128) * 128
-
-
-def project_first(me, tokens, near, ws, after=(), tile=256):
-    rows, shard = tokens.shape
+def begin(me, slab, tokens, cuts, near, log_decay_rows, ws, w_out, head_size):
     wq, wk, wv, wl = ws
-    q_width, kv_width, l_width = wq.shape[1], wk.shape[1], wl.shape[0]
-    steps = shard // tile
-    n_after = len(after)
-
-    def kernel(me_ref, *refs):
-        x_refs, w_refs = refs[:2], refs[2:18]
-        total_q, total_kv, total_l, q_out, kv_out, l_out = refs[18 + n_after :]
-        step = pl.program_id(0)
-
-        @pl.when(step == 0)
-        def _():
-            total_q[...] = jnp.zeros_like(total_q)
-            total_kv[...] = jnp.zeros_like(total_kv)
-            total_l[...] = jnp.zeros_like(total_l)
-
-        def joined(i):
-            return jnp.concatenate([w_refs[4 * i + 1][...], w_refs[4 * i + 2][...]], axis=1)
-
-        x0, x1 = x_refs[0][...], x_refs[1][...]
-        total_q[...] += dot(x0, w_refs[0][...]) + dot(x1, w_refs[4][...])
-        total_kv[...] += dot(x0, joined(0)) + dot(x1, joined(1))
-        total_l[...] += dot_dims(x0, w_refs[3][...], 1, 1) + dot_dims(x1, w_refs[7][...], 1, 1)
-        for i in (2, 3):
-            q_out[i - 2] = w_refs[4 * i][...]
-            kv_out[i - 2] = joined(i)
-            l_out[i - 2] = w_refs[4 * i + 3][...]
-
-    x_spec = pl.BlockSpec((rows, tile), lambda s, m: (0, s))
-    w_specs, operands = [], []
-    for i in range(4):
-        for w in (wq, wk, wv):
-            w_specs.append(pl.BlockSpec((tile, w.shape[1]), lambda s, m, i=i: ((m[0] ^ i) * steps + s, 0)))
-        w_specs.append(pl.BlockSpec((l_width, tile), lambda s, m, i=i: (0, (m[0] ^ i) * steps + s)))
-        operands += [wq, wk, wv, wl]
-    out_shape = [
+    n_x = len(tokens)
+    shard = near.shape[1]
+    rows = near.shape[0]
+    q_width, kv_width = wq.shape[1], wk.shape[1]
+    heads = log_decay_rows.shape[0]
+    block = w_out.shape[1] // 4
+
+    def kernel(me_ref, slab_ref, wq_ref, wk_ref, wv_ref, wl_ref, wo_ref, *refs):
+        x_refs, near_ref, decay_ref, refs = refs[:n_x], refs[n_x], refs[n_x + 1], refs[n_x + 2 :]
+        total_q, total_kv, total_l, far_q, far_kv, all_l = refs[:6]
+        decay_outs, blocks, (own_q, own_kv, sems) = refs[6:11], refs[11:15], refs[15:]
+
+        def pairs(i, q_dst, kv_dst):
+            here = pl.ds(pl.multiple_of((me_ref[0] ^ i) * shard, 128), shard)
+            return [
+                (wk_ref.at[here, :], kv_dst.at[:, :kv_width]),
+                (wv_ref.at[here, :], kv_dst.at[:, kv_width:]),
+                (wq_ref.at[here, :], q_dst),
+            ]
+
+        def columns(i):
+            return wo_ref.at[:, pl.ds(pl.multiple_of((me_ref[0] ^ i) * block, 128), block)]
+
+        moves = pairs(0, own_q.at[0], own_kv.at[0]) + [(wl_ref, all_l)]
+        moves += pairs(1, own_q.at[1], own_kv.at[1])
+        moves += pairs(2, far_q.at[0], far_kv.at[0]) + pairs(3, far_q.at[1], far_kv.at[1])
+        moves += [(columns(i), blocks[i]) for i in range(4)]
+        started = copies(moves, sems)
+        decays(slab_ref, decay_ref, *decay_outs)
+        for copy in started[:4]:
+            copy.wait()
+        lanes = pl.ds(pl.multiple_of(me_ref[0] * shard, 128), shard)
+        own = jnp.concatenate([x_ref[...] for x_ref in x_refs], axis=1)
+        total_kv[...] = dot(own, own_kv[0])
+        total_q[...] = dot(own, own_q[0])
+        total_l[...] = dot_dims(own, all_l[:, lanes], 1, 1)
+        for copy in started[4:7]:
+            copy.wait()
+        lanes = pl.ds(pl.multiple_of((me_ref[0] ^ 1) * shard, 128), shard)
+        total_kv[...] += dot(near_ref[...], own_kv[1])
+        total_q[...] += dot(near_ref[...], own_q[1])
+        total_l[...] += dot_dims(near_ref[...], all_l[:, lanes], 1, 1)
+        for copy in started[7:]:
+            copy.wait()
+
+    wide = shape((8, heads * head_size), F32)
+    outs = [
         shape((rows, q_width), F32),
         shape((rows, 2 * kv_width), F32),
-        shape((rows, l_width), F32),
+        shape((rows, wl.shape[0]), F32),
         shape((2, shard, q_width), BF16),
         shape((2, shard, 2 * kv_width), BF16),
-        shape((2, l_width, shard), BF16),
+        shape(wl.shape, BF16),
+        shape((heads, rows), F32),
+        shape((rows, heads), F32),
+        shape((rows, heads), F32),
+        wide,
+        wide,
+    ] + [shape((w_out.shape[0], block), BF16)] * 4
+    scratch = [
+        pltpu.VMEM((2, shard, q_width), BF16),
+        pltpu.VMEM((2, shard, 2 * kv_width), BF16),
+        pltpu.SemaphoreType.DMA((17,)),
     ]
-    out_specs = [pl.BlockSpec(o.shape, lambda s, m: (0, 0)) for o in out_shape[:3]]
-    out_specs += [
-        pl.BlockSpec((2, tile, q_width), lambda s, m: (0, s, 0)),
-        pl.BlockSpec((2, tile, 2 * kv_width), lambda s, m: (0, s, 0)),
-        pl.BlockSpec((2, l_width, tile), lambda s, m: (0, 0, s)),
-    ]
-    outs = pl.pallas_call(
-        kernel,
-        grid_spec=pltpu.PrefetchScalarGridSpec(
-            num_scalar_prefetch=1,
-            grid=(steps,),
-            in_specs=[x_spec, x_spec, *w_specs] + [ANY] * n_after,
-            out_specs=out_specs,
-        ),
-        out_shape=out_shape,
-        compiler_params=pltpu.CompilerParams(vmem_limit_bytes=16 * 1024 * 1024),
-        cost_estimate=pl.CostEstimate(flops=0, bytes_accessed=0, transcendentals=0),
-    )(me, tokens, near, *operands, *after)
-    return outs[:3], outs[3:]
+    ins = [me, slab, wq, wk, wv, wl, w_out, *tokens, near, log_decay_rows]
+    outs = call(kernel, ins, outs, 0, smem=2, hbm=5, scratch=scratch, megabytes=14)
+    return outs[:3], outs[3:6], outs[6:11], outs[11:]
 
 
 def add_products(xs, w_ref, offset):
@@ -209,27 +223,29 @@
     return total
 
 
-def add_levels(xs, wl_ref, offset):
+def add_levels(me_ref, xs, wl_ref, offset):
+    shard = wl_ref.shape[1] // 4
     total = None
     for i, x_ref in enumerate(xs):
-        add = dot_dims(x_ref[...], wl_ref[i, :, offset : offset + x_ref.shape[1]], 1, 1)
+        start = pl.multiple_of((me_ref[0] ^ (2 + i)) * shard + offset, 128)
+        add = dot_dims(x_ref[...], wl_ref[:, pl.ds(start, x_ref.shape[1])], 1, 1)
         total = add if total is None else total + add
     return total
 
 
-def project(xs, ws, offset, totals, after=()):
+def project(me, xs, ws, offset, totals, after=()):
     n_x = len(xs)
 
-    def kernel(*refs):
+    def kernel(me_ref, *refs):
         x, (q_ref, kv_ref, l_ref), ins, outs = refs[:n_x], refs[n_x : n_x + 3], refs[-6:-3], refs[-3:]
         outs[1][...] = ins[1][...] + add_products(x, kv_ref, offset)
         outs[0][...] = ins[0][...] + add_products(x, q_ref, offset)
-        outs[2][...] = ins[2][...] + add_levels(x, l_ref, offset)
-
-    ins = [*xs, *ws, *totals]
-    aliases = {n_x + 3 + i: i for i in range(3)}
+        outs[2][...] = ins[2][...] + add_levels(me_ref, x, l_ref, offset)
+
+    ins = [me, *xs, *ws, *totals]
+    aliases = {n_x + 4 + i: i for i in range(3)}
     outs = [shape(t.shape, F32) for t in totals]
-    return call(kernel, ins, outs, 0, after, aliases=aliases)
+    return call(kernel, ins, outs, 0, after, smem=1, aliases=aliases)
 
 
 def project_state(xs, wkv, offset, total_kv, keep, head_size):
@@ -264,7 +280,7 @@
     return call(kernel, [*xs, wkv, total_kv, keep], outs, 0)
 
 
-def attend(xs, wq, wl, offset, total_q, total_l, k, v, dcol, drow, spans, states, head_size, level_count):
+def attend(me, xs, wq, wl, offset, total_q, total_l, k, v, dcol, drow, spans, states, head_size, level_count):
     rows, width = total_q.shape
     n_x = len(xs)
     bits = len(spans)
@@ -272,12 +288,12 @@
     group = heads // (k.shape[1] // head_size)
     own_levels = level_count - bits
 
-    def kernel(*refs):
+    def kernel(me_ref, *refs):
         x, refs = refs[:n_x], refs[n_x:]
         wq_ref, wl_ref, tq_ref, tl_ref, k_ref, v_ref, dcol_ref, drow_ref = refs[:8]
         span_refs, state_refs = refs[8 : 8 + bits], refs[8 + bits : 7 + 2 * bits]
         o_ref, s_ref, q_ref, l_ref = refs[-4:]
-        raw = tl_ref[...] + add_levels(x, wl_ref, offset)
+        raw = tl_ref[...] + add_levels(me_ref, x, wl_ref, offset)
         l_ref[...] = jnp.maximum(raw, 0.0) + jnp.log1p(jnp.exp(-jnp.abs(raw)))
         q_ref[...] = (tq_ref[...] + add_products(x, wq_ref, offset)).astype(BF16)
         row_id = lax.broadcasted_iota(jnp.int32, (BLOCK, BLOCK), 0)
@@ -321,11 +337,11 @@
                         total = total + dot_dims(scaled, state_refs[b][:, cols], 1, 1)
                 o_ref[here, cols] = total
 
-    ins = [*xs, wq, wl, total_q, total_l, k, v, dcol, drow, *spans, *states]
+    ins = [me, *xs, wq, wl, total_q, total_l, k, v, dcol, drow, *spans, *states]
     wide = shape((rows, width), BF16)
     outs = [shape((rows, width), F32), wide, wide, shape(total_l.shape, F32)]
     flops = 2 * rows * xs[0].shape[1] * n_x * width + 4 * rows * rows * width
-    return call(kernel, ins, outs, flops)[:2]
+    return call(kernel, ins, outs, flops, smem=1)[:2]
 
 
 def finish(local, scaled, state, rows, head_size, after=()):
@@ -340,32 +356,6 @@
 
     outs = [shape((rows.stop - rows.start, width), BF16)]
     return call(kernel, [local, scaled, state], outs, 0, after)[0]
-
-
-def cut_blocks(me, w_out, after, tile=256):
-    depth, columns = w_out.shape
-    block = columns // 4
-    steps = block // tile
-
-    def kernel(me_ref, *refs):
-        for w_ref, o_ref in zip(refs[:4], refs[-4:]):
-            o_ref[...] = w_ref[...]
-
-    in_specs = [
-        pl.BlockSpec((depth, tile), lambda s, m, i=i: (0, (m[0] ^ i) * steps + s)) for i in range(4)
-    ]
-    return pl.pallas_call(
-        kernel,
-        grid_spec=pltpu.PrefetchScalarGridSpec(
-            num_scalar_prefetch=1,
-            grid=(steps,),
-            in_specs=in_specs + [ANY] * len(after),
-            out_specs=[pl.BlockSpec((depth, tile), lambda s, m: (0, s))] * 4,
-        ),
-        out_shape=[shape((depth, block), w_out.dtype)] * 4,
-        compiler_params=pltpu.CompilerParams(vmem_limit_bytes=8 * 1024 * 1024),
-        cost_estimate=pl.CostEstimate(flops=0, bytes_accessed=0, transcendentals=0),
-    )(me, *[w_out] * 4, *after)
 
 
 def out_far(n0, n1, w0, w1, rows_own, rows_near):
@@ -424,45 +414,49 @@
     def swap_tp(x, bit):
         return lax.ppermute(x, "tp", [(i, i ^ bit) for i in range(4)])
 
-    def swap_seq(x, bit, both=True):
-        return lax.ppermute(x, "seq", [(i, i ^ bit) for i in range(seq_size) if both or not i & bit])
-
-    half = shard // 2
-    first, second = cut_columns(tokens, 2)
-    far_first, far_second = swap_tp(first, 2), swap_tp(second, 2)
+    def swap_seq(x, bit):
+        return lax.ppermute(x, "seq", [(i, i ^ bit) for i in range(seq_size)])
+
+    half, quarter = shard // 2, shard // 4
+    cuts = [slice(0, half), slice(half, shard)]
+    pieces = cut_columns(tokens, cuts)
+    far = [swap_tp(x, 2) for x in pieces]
     near = swap_tp(tokens, 1)
 
-    drow, dcol, keep, total, span = decays(slab, log_decay.T, head_size)
+    weights = (w_query, w_key, w_value, w_level.T)
+    totals, ws, (drow, dcol, keep, total, span), blocks = begin(
+        me, slab, pieces, cuts, near, log_decay.T, weights, w_out, head_size
+    )
+    w_here_own, w_here_send, w_far_own, w_far_send = blocks
+    w_here, w_far = swap_tp(w_here_send, 1), swap_tp(w_far_send, 1)
+
     spans, factors, before = [span], [], None
     for b in range(seq_bits - 1):
         total, before, own, other, span = link(slab, b, total, swap_seq(total, 1 << b), before)
         spans.append(span)
         factors.append((own, other))
 
-    totals, ws = project_first(me, tokens, near, (w_query, w_key, w_value, w_level.T))
-    w_here_own, w_here_send, w_far_own, w_far_send = cut_blocks(me, w_out, (totals[0],))
-    w_here, w_far = swap_tp(w_here_send, 1), swap_tp(w_far_send, 1)
-    arrived = gate(far_first, total, w_here_send)
-    later = gate(far_second, totals[0])
-    totals = project((arrived, swap_tp(arrived, 1)), ws, 0, totals, (w_far, w_here))
-    arrived = later
-    pair = (arrived[0], swap_tp(arrived[0], 1))
-    totals = project(pair, ws, half, totals)
-    pair = (arrived[1], swap_tp(arrived[1], 1))
-    last = half + half // 2
     wq, wkv, wl = ws
+    arrived = gate(far[0], total, totals[0])
+    pair = (arrived, swap_tp(arrived, 1))
+    later = split(far[1], (totals[0],))
+    totals = project(me, pair, ws, 0, totals, (w_far, w_here))
+    pair = (later[0], swap_tp(later[0], 1))
+    totals = project(me, pair, ws, half, totals)
+    pair = (later[1], swap_tp(later[1], 1))
     total_q, total_kv, total_l = totals
+    last = half + quarter
     k, v, state = project_state(pair, wkv, last, total_kv, keep, head_size)
 
     earlier = []
     for b in range(seq_bits):
-        other = swap_seq(state, 1 << b, b < seq_bits - 1)
+        other = swap_seq(state, 1 << b)
         earlier.append(other)
         if b < seq_bits - 1:
             state = combine(state, other, *factors[b])
 
     local, scaled = attend(
-        pair, wq, wl, last, total_q, total_l, k, v, dcol, drow, spans, earlier[:-1], head_size, level_count
+        me, pair, wq, wl, last, total_q, total_l, k, v, dcol, drow, spans, earlier[:-1], head_size, level_count
     )
 
     step = rows // 4

time: 90.4 us -> 79.5 us (0.88)
  local copies, waits for them, and re-layouts: 11.1 us -> 0.7 us
  Pallas kernels: 24.3 us -> 20.8 us
  waiting for transfers between devices: 34 us -> 37.4 us
    unnamed x36 -> x2, local copies, waits for them, and re-layouts: 9.99 us -> 0.7 us
    pallas_call x18 -> x17, Pallas kernels: 19.7 us -> 16.1 us  [call(): pl.pallas_call(run, in_specs=[SMEM] * smem + [HBM] * hbm + [VMEM] * (coun...]
    ppermute x14, waiting for transfers between devices: 22.2 us -> 25.2 us  [swap_tp(): return lax.ppermute(x, 'tp', [(i, i ^ bit) for i in range(4)])]
    ppermute x5, starting transfers between devices: 10.9 us -> 9.65 us  [swap_seq(): return lax.ppermute(x, 'seq', [(i, i ^ bit) for i in range(seq_size)])]
    ppermute x14, starting transfers between devices: 9.49 us -> 10.6 us  [swap_tp(): return lax.ppermute(x, 'tp', [(i, i ^ bit) for i in range(4)])]
    squeeze x1 -> x0, local copies, waits for them, and re-layouts: 1.06 us -> none  [body(): pair = (arrived[0], swap_tp(arrived[0], 1))]
  transfers between devices with their start and end apart: 19 -> 19, of which waited for: 10 -> 11; matrix products, arithmetic and copies ran while one was open for 1% -> 0% of each run, Pallas kernels for 24% -> 23%
where the time goes in v4:
time: 79.5 us; the launch traced here: 79.3 us
  waiting for transfers between devices  37.4 us (47%)
  Pallas kernels  20.8 us (26%)
  starting transfers between devices  20.3 us (26%)
    ppermute x14, waiting for transfers between devices, swap_tp(): return lax.ppermute(x, 'tp', [(i, i ^ bit) for i in range(4)])  25.2 us
    pallas_call x17, Pallas kernels, call(): pl.pallas_call(run, in_specs=[SMEM] * smem + [HBM] * hbm + [VMEM] * (coun...  16.1 us
    ppermute x5, waiting for transfers between devices, swap_seq(): return lax.ppermute(x, 'seq', [(i, i ^ bit) for i in range(seq_size)])  12.2 us
    ppermute x14, starting transfers between devices, swap_tp(): return lax.ppermute(x, 'tp', [(i, i ^ bit) for i in range(4)])  10.6 us
    ppermute x5, starting transfers between devices, swap_seq(): return lax.ppermute(x, 'seq', [(i, i ^ bit) for i in range(seq_size)])  9.65 us
    pallas_call x4, Pallas kernels, out_here(): pl.pallas_call(kernel, grid=(1,), in_specs=specs, out_specs=pl.BlockSpec(...  4.68 us
  transfers between devices with their start and end apart: 19, of which 11 were waited for; matrix products, arithmetic and copies ran while one was open for 0% of the time, Pallas kernels for 23%

profile of v4, /device:TPU:0, one launch (start us, length us, event | category | flops | bytes accessed | tf_op | source)
XLA Modules:
  0.0 79.3 jit_solution(12315313682931414914)
XLA Ops:
  0.5 1.2 %shard_map.73 = (bf16[512,512]{1,0:T(8,128)(2,1)S(1)}, bf16[512,512]{1,0:T(8,128)(2,1)S(1)}) custom-call(bf16[512,1024]{1,0:T(8,128)(2,1)} %refs_0_.1), custom_call_target="tpu_custom_call" | custom-call | tf_op jit(solution)/shard_map/pallas_call | solution.py:41
  1.7 2.6 %collective-permute-start.4 = (bf16[512,512]{1,0:T(8,128)(2,1)S(1)}, bf16[512,512]{1,0:T(8,128)(2,1)S(1)}, u32[]{:S(2)}, u32[]{:S(2)}) collective-permute-start(bf16[512,512]{1,0:T(8,128)(2,1)S(1)} %get-tuple-element.45.refs_7_), channel_id=1, source_target_pairs={{0,2},{1,3},{2,0},{3,1},{4,6},{5,7},{6,4},{7,5},{8,10},{9,11},{10,... | collective-permute-start | bytes 1572872 | tf_op jit(solution)/shard_map/ppermute | solution.py:415
  5.0 5.0 %shard_map.74 = (f32[512,512]{1,0:T(8,128)S(1)}, f32[512,256]{1,0:T(8,128)S(1)}, f32[512,24]{1,0:T(8,128)S(1)}, bf16[2,1024,512]{2,1,0:T(8,128)(2,1)S(1)}, bf16[...) custom-call(s32[1]{0:T(128)} %bitcast.refs_0_, ...), custom_call_target="tpu_custom_call" | custom-call | tf_op jit(solution)/shard_map/pallas_call | solution.py:41
  10.5 1.6 %collective-permute-start = (bf16[512,512]{1,0:T(8,128)(2,1)S(1)}, bf16[512,512]{1,0:T(8,128)(2,1)S(1)}, u32[]{:S(2)}, u32[]{:S(2)}) collective-permute-start(bf16[512,512]{1,0:T(8,128)(2,1)S(1)} %get-tuple-element.44.refs_8_), channel_id=1, source_target_pairs={{0,2},{1,3},{2,0},{3,1},{4,6},{5,7},{6,4},{7,5},{8,10},{9,11},{10,... | collective-permute-start | bytes 1572872 | tf_op jit(solution)/shard_map/ppermute | solution.py:415
  12.1 1.5 %collective-permute-start.5 = (f32[8,512]{1,0:T(8,128)S(1)}, f32[8,512]{1,0:T(8,128)S(1)}, u32[]{:S(2)}, u32[]{:S(2)}) collective-permute-start(f32[8,512]{1,0:T(8,128)S(1)} %get-tuple-element.52.refs_1_), channel_id=1, source_target_pairs={{0,4},{4,0},{8,12},{12,8},{16,20},{20,16},{24,28},{28,24},{1,5},{5... | collective-permute-start | bytes 49160 | tf_op jit(solution)/shard_map/ppermute | solution.py:418
  13.6 2.2 %collective-permute-done.5.refs_2_ = f32[8,512]{1,0:T(8,128)S(1)} collective-permute-done((f32[8,512]{1,0:T(8,128)S(1)}, f32[8,512]{1,0:T(8,128)S(1)}, u32[]{:S(2)}, u32[]{:S(2)}) %collective-permute-start.5) | collective-permute-done | bytes 16416 | tf_op jit(solution)/shard_map/ppermute | solution.py:418
  15.9 1.6 %collective-permute-start.6 = (f32[8,512]{1,0:T(8,128)S(1)}, f32[8,512]{1,0:T(8,128)S(1)}, u32[]{:S(2)}, u32[]{:S(2)}) collective-permute-start(f32[8,512]{1,0:T(8,128)S(1)} %get-tuple-element.53.refs_1_), channel_id=1, source_target_pairs={{0,8},{4,12},{8,0},{12,4},{16,24},{20,28},{24,16},{28,20},{1,9},{5... | collective-permute-start | bytes 49160 | tf_op jit(solution)/shard_map/ppermute | solution.py:418
  17.5 2.2 %collective-permute-done.6.refs_2_ = f32[8,512]{1,0:T(8,128)S(1)} collective-permute-done((f32[8,512]{1,0:T(8,128)S(1)}, f32[8,512]{1,0:T(8,128)S(1)}, u32[]{:S(2)}, u32[]{:S(2)}) %collective-permute-start.6) | collective-permute-done | bytes 16416 | tf_op jit(solution)/shard_map/ppermute | solution.py:418
  20.3 7.8 %collective-permute-done.refs_0_ = bf16[512,512]{1,0:T(8,128)(2,1)S(1)} collective-permute-done((bf16[512,512]{1,0:T(8,128)(2,1)S(1)}, bf16[512,512]{1,0:T(8,128)(2,1)S(1)}, u32[]{:S(2)}, u32[]{:S(2)}) %collective-permute-start) | collective-permute-done | bytes 524320 | tf_op jit(solution)/shard_map/ppermute | solution.py:415
  28.7 1.3 %shard_map.79 = (f32[512,512]{1,0:T(8,128)S(1)}, f32[512,256]{1,0:T(8,128)S(1)}, f32[512,24]{1,0:T(8,128)S(1)}) custom-call(s32[1]{0:T(128)} %bitcast.refs_0_, bf16[512,512]{1,0:T(8,128)(2,1)S(1)} %shard_map.78.refs_1_, bf16[512,512]{1,0:T(8,128)(2,1)S(1)} %collective-permute-done.7.refs_2_, ...), custom_call_target="tpu_custom_call", output_to_operand_aliasing={{0}: (6, {}), {1}: (7, {}), {2}: (8, {})} | custom-call | tf_op jit(solution)/shard_map/pallas_call | solution.py:41
  31.5 1.8 %collective-permute-start.10 = (bf16[128,512]{1,0:T(8,128)(2,1)S(1)}, bf16[128,512]{1,0:T(8,128)(2,1)S(1)}, u32[]{:S(2)}, u32[]{:S(2)}) collective-permute-start(bf16[128,512]{1,0:T(8,128)(2,1)S(1)} %get-tuple-element.74.refs_0_), channel_id=1, source_target_pairs={{0,4},{4,0},{8,12},{12,8},{16,20},{20,16},{24,28},{28,24},{1,5},{5... | collective-permute-start | bytes 393224 | tf_op jit(solution)/shard_map/ppermute | solution.py:418
  33.3 3.8 %collective-permute-done.10.refs_1_.refs_14_ = bf16[128,512]{1,0:T(8,128)(2,1)S(1)} collective-permute-done((bf16[128,512]{1,0:T(8,128)(2,1)S(1)}, bf16[128,512]{1,0:T(8,128)(2,1)S(1)}, u32[]{:S(2)}, u32[]{:S(2)}) %collective-permute-start.10) | collective-permute-done | bytes 131104 | tf_op jit(solution)/shard_map/ppermute | solution.py:418
  37.1 1.9 %collective-permute-start.11 = (bf16[128,512]{1,0:T(8,128)(2,1)S(1)}, bf16[128,512]{1,0:T(8,128)(2,1)S(1)}, u32[]{:S(2)}, u32[]{:S(2)}) collective-permute-start(bf16[128,512]{1,0:T(8,128)(2,1)S(1)} %shard_map.82.refs_0_), channel_id=1, source_target_pairs={{0,8},{4,12},{8,0},{12,4},{16,24},{20,28},{24,16},{28,20},{1,9},{5... | collective-permute-start | bytes 393224 | tf_op jit(solution)/shard_map/ppermute | solution.py:418
  39.0 3.2 %collective-permute-done.11.refs_15_.refs_1_ = bf16[128,512]{1,0:T(8,128)(2,1)S(1)} collective-permute-done((bf16[128,512]{1,0:T(8,128)(2,1)S(1)}, bf16[128,512]{1,0:T(8,128)(2,1)S(1)}, u32[]{:S(2)}, u32[]{:S(2)}) %collective-permute-start.11) | collective-permute-done | bytes 131104 | tf_op jit(solution)/shard_map/ppermute | solution.py:418
  42.2 2.9 %collective-permute-start.12 = (bf16[128,512]{1,0:T(8,128)(2,1)S(1)}, bf16[128,512]{1,0:T(8,128)(2,1)S(1)}, u32[]{:S(2)}, u32[]{:S(2)}) collective-permute-start(bf16[128,512]{1,0:T(8,128)(2,1)S(1)} %shard_map.84), channel_id=1, source_target_pairs={{0,16},{4,20},{8,24},{12,28},{16,0},{20,4},{24,8},{28,12},{1,17},{... | collective-permute-start | bytes 393224 | tf_op jit(solution)/shard_map/ppermute | solution.py:418
  45.1 3.7 %shard_map.83 = (f32[512,512]{1,0:T(8,128)S(1)}, bf16[512,512]{1,0:T(8,128)(2,1)S(1)}, bf16[512,512]{1,0:T(8,128)(2,1)}, f32[512,24]{1,0:T(8,128)}) custom-call(s32[1]{0:T(128)} %bitcast.refs_0_, bf16[512,256]{1,0:T(8,128)(2,1)S(1)} %get-tuple-element.47.refs_0_.refs_1_, bf16[512,256]{1,0:T(8,128)(2,1)S(1)} %collective-permute-done.2.refs_1_.refs_2_, ...), custom_call_target="tpu_custom_call" | custom-call | flops 805306368 | bytes 6651908 | tf_op jit(solution)/shard_map/pallas_call | solution.py:41
  51.0 1.4 %collective-permute-done.17.refs_1_.n1_ref = bf16[128,512]{1,0:T(8,128)(2,1)S(1)} collective-permute-done((bf16[128,512]{1,0:T(8,128)(2,1)S(1)}, bf16[128,512]{1,0:T(8,128)(2,1)S(1)}, u32[]{:S(2)}, u32[]{:S(2)}) %collective-permute-start.17) | collective-permute-done | bytes 131104 | tf_op jit(solution)/shard_map/ppermute | solution.py:415
  52.9 1.7 %collective-permute-start.18 = (bf16[128,1024]{1,0:T(8,128)(2,1)S(1)}, bf16[128,1024]{1,0:T(8,128)(2,1)S(1)}, u32[]{:S(2)}, u32[]{:S(2)}) collective-permute-start(bf16[128,1024]{1,0:T(8,128)(2,1)S(1)} %shard_map.90), channel_id=1, source_target_pairs={{0,2},{1,3},{2,0},{3,1},{4,6},{5,7},{6,4},{7,5},{8,10},{9,11},{10,... | collective-permute-start | bytes 786440 | tf_op jit(solution)/shard_map/ppermute | solution.py:415
  56.0 1.7 %collective-permute-start.15 = (bf16[128,1024]{1,0:T(8,128)(2,1)S(1)}, bf16[128,1024]{1,0:T(8,128)(2,1)S(1)}, u32[]{:S(2)}, u32[]{:S(2)}) collective-permute-start(bf16[128,1024]{1,0:T(8,128)(2,1)S(1)} %shard_map.88), channel_id=1, source_target_pairs={{0,2},{1,3},{2,0},{3,1},{4,6},{5,7},{6,4},{7,5},{8,10},{9,11},{10,... | collective-permute-start | bytes 786440 | tf_op jit(solution)/shard_map/ppermute | solution.py:415
  58.6 3.5 %collective-permute-done.18.a_ref = bf16[128,1024]{1,0:T(8,128)(2,1)S(1)} collective-permute-done((bf16[128,1024]{1,0:T(8,128)(2,1)S(1)}, bf16[128,1024]{1,0:T(8,128)(2,1)S(1)}, u32[]{:S(2)}, u32[]{:S(2)}) %collective-permute-start.18) | collective-permute-done | bytes 262176 | tf_op jit(solution)/shard_map/ppermute | solution.py:415
  63.3 4.4 %collective-permute-done.16.a_ref = bf16[128,1024]{1,0:T(8,128)(2,1)S(1)} collective-permute-done((bf16[128,1024]{1,0:T(8,128)(2,1)S(1)}, bf16[128,1024]{1,0:T(8,128)(2,1)S(1)}, u32[]{:S(2)}, u32[]{:S(2)}) %collective-permute-start.16) | collective-permute-done | bytes 262176 | tf_op jit(solution)/shard_map/ppermute | solution.py:415
  68.9 4.4 %collective-permute-done.15.a_ref = bf16[128,1024]{1,0:T(8,128)(2,1)S(1)} collective-permute-done((bf16[128,1024]{1,0:T(8,128)(2,1)S(1)}, bf16[128,1024]{1,0:T(8,128)(2,1)S(1)}, u32[]{:S(2)}, u32[]{:S(2)}) %collective-permute-start.15) | collective-permute-done | bytes 262176 | tf_op jit(solution)/shard_map/ppermute | solution.py:415
  73.3 1.2 %shard_map.93.refs_0_ = bf16[512,1024]{1,0:T(8,128)(2,1)} custom-call(bf16[384,512]{1,0:T(8,128)(2,1)S(1)} %shard_map.86.refs_0_.n0_ref, bf16[384,512]{1,0:T(8,128)(2,1)S(1)} %collective-permute-done.13.refs_1_.n1_ref, bf16[512,1024]{1,0:T(8,128)(2,1)S(1)} %get-tuple-element.81.w0_ref, ...), custom_call_target="tpu_custom_call", output_to_operand_aliasing={{}: (5, {})} | custom-call | flops 268435456 | bytes 2097152 | tf_op jit(solution)/shard_map/pallas_call | solution.py:390
  74.5 3.6 %collective-permute-done.14.a_ref = bf16[128,1024]{1,0:T(8,128)(2,1)S(1)} collective-permute-done((bf16[128,1024]{1,0:T(8,128)(2,1)S(1)}, bf16[128,1024]{1,0:T(8,128)(2,1)S(1)}, u32[]{:S(2)}, u32[]{:S(2)}) %collective-permute-start.14) | collective-permute-done | bytes 262176 | tf_op jit(solution)/shard_map/ppermute | solution.py:415
  (38 shorter events, 13.0 us)
Async XLA Ops:
  0.0 4.3 %collective-permute-start.1 = (bf16[512,1024]{1,0:T(8,128)(2,1)}, bf16[512,1024]{1,0:T(8,128)(2,1)S(1)}, u32[]{:S(2)}, u32[]{:S(2)}) collective-permute-start(bf16[512,1024]{1,0:T(8,128)(2,1)} %refs_0_.1), channel_id=1, source_target_pairs={{0,1},{1,0},{2,3},{3,2},{4,5},{5,4},{6,7},{7,6},{8,9},{9,8},{10,11... | collective-permute-start | bytes 3145736 | tf_op jit(solution)/shard_map/ppermute | solution.py:415
  1.7 18.6 %collective-permute-start.4 = (bf16[512,512]{1,0:T(8,128)(2,1)S(1)}, bf16[512,512]{1,0:T(8,128)(2,1)S(1)}, u32[]{:S(2)}, u32[]{:S(2)}) collective-permute-start(bf16[512,512]{1,0:T(8,128)(2,1)S(1)} %get-tuple-element.45.refs_7_), channel_id=1, source_target_pairs={{0,2},{1,3},{2,0},{3,1},{4,6},{5,7},{6,4},{7,5},{8,10},{9,11},{10,... | collective-permute-start | bytes 1572872 | tf_op jit(solution)/shard_map/ppermute | solution.py:415
  4.3 0.7 copy-start
  10.0 18.7 %collective-permute-start.8 = (bf16[512,1024]{1,0:T(8,128)(2,1)S(1)}, bf16[512,1024]{1,0:T(8,128)(2,1)S(1)}, u32[]{:S(2)}, u32[]{:S(2)}) collective-permute-start(bf16[512,1024]{1,0:T(8,128)(2,1)S(1)} %get-tuple-element.58), channel_id=1, source_target_pairs={{0,1},{1,0},{2,3},{3,2},{4,5},{5,4},{6,7},{7,6},{8,9},{9,8},{10,11... | collective-permute-start | bytes 3145736 | tf_op jit(solution)/shard_map/ppermute | solution.py:415
  10.3 18.5 %collective-permute-start.9 = (bf16[512,1024]{1,0:T(8,128)(2,1)S(1)}, bf16[512,1024]{1,0:T(8,128)(2,1)S(1)}, u32[]{:S(2)}, u32[]{:S(2)}) collective-permute-start(bf16[512,1024]{1,0:T(8,128)(2,1)S(1)} %get-tuple-element.59), channel_id=1, source_target_pairs={{0,1},{1,0},{2,3},{3,2},{4,5},{5,4},{6,7},{7,6},{8,9},{9,8},{10,11... | collective-permute-start | bytes 3145736 | tf_op jit(solution)/shard_map/ppermute | solution.py:415
  10.5 17.5 %collective-permute-start = (bf16[512,512]{1,0:T(8,128)(2,1)S(1)}, bf16[512,512]{1,0:T(8,128)(2,1)S(1)}, u32[]{:S(2)}, u32[]{:S(2)}) collective-permute-start(bf16[512,512]{1,0:T(8,128)(2,1)S(1)} %get-tuple-element.44.refs_8_), channel_id=1, source_target_pairs={{0,2},{1,3},{2,0},{3,1},{4,6},{5,7},{6,4},{7,5},{8,10},{9,11},{10,... | collective-permute-start | bytes 1572872 | tf_op jit(solution)/shard_map/ppermute | solution.py:415
  12.1 3.7 %collective-permute-start.5 = (f32[8,512]{1,0:T(8,128)S(1)}, f32[8,512]{1,0:T(8,128)S(1)}, u32[]{:S(2)}, u32[]{:S(2)}) collective-permute-start(f32[8,512]{1,0:T(8,128)S(1)} %get-tuple-element.52.refs_1_), channel_id=1, source_target_pairs={{0,4},{4,0},{8,12},{12,8},{16,20},{20,16},{24,28},{28,24},{1,5},{5... | collective-permute-start | bytes 49160 | tf_op jit(solution)/shard_map/ppermute | solution.py:418
  15.9 3.8 %collective-permute-start.6 = (f32[8,512]{1,0:T(8,128)S(1)}, f32[8,512]{1,0:T(8,128)S(1)}, u32[]{:S(2)}, u32[]{:S(2)}) collective-permute-start(f32[8,512]{1,0:T(8,128)S(1)} %get-tuple-element.53.refs_1_), channel_id=1, source_target_pairs={{0,8},{4,12},{8,0},{12,4},{16,24},{20,28},{24,16},{28,20},{1,9},{5... | collective-permute-start | bytes 49160 | tf_op jit(solution)/shard_map/ppermute | solution.py:418
  20.3 8.4 %collective-permute-start.7 = (bf16[512,512]{1,0:T(8,128)(2,1)S(1)}, bf16[512,512]{1,0:T(8,128)(2,1)S(1)}, u32[]{:S(2)}, u32[]{:S(2)}) collective-permute-start(bf16[512,512]{1,0:T(8,128)(2,1)S(1)} %shard_map.78.refs_1_), channel_id=1, source_target_pairs={{0,1},{1,0},{2,3},{3,2},{4,5},{5,4},{6,7},{7,6},{8,9},{9,8},{10,11... | collective-permute-start | bytes 1572872 | tf_op jit(solution)/shard_map/ppermute | solution.py:415
  28.1 1.9 %collective-permute-start.3 = (bf16[512,256]{1,0:T(8,128)(2,1)S(1)}, bf16[512,256]{1,0:T(8,128)(2,1)S(1)}, u32[]{:S(2)}, u32[]{:S(2)}) collective-permute-start(bf16[512,256]{1,0:T(8,128)(2,1)S(1)} %get-tuple-element.50.refs_1_), channel_id=1, source_target_pairs={{0,1},{1,0},{2,3},{3,2},{4,5},{5,4},{6,7},{7,6},{8,9},{9,8},{10,11... | collective-permute-start | bytes 786440 | tf_op jit(solution)/shard_map/ppermute | solution.py:415
  28.2 2.6 %collective-permute-start.2 = (bf16[512,256]{1,0:T(8,128)(2,1)S(1)}, bf16[512,256]{1,0:T(8,128)(2,1)S(1)}, u32[]{:S(2)}, u32[]{:S(2)}) collective-permute-start(bf16[512,256]{1,0:T(8,128)(2,1)S(1)} %get-tuple-element.47.refs_0_.refs_1_), channel_id=1, source_target_pairs={{0,1},{1,0},{2,3},{3,2},{4,5},{5,4},{6,7},{7,6},{8,9},{9,8},{10,11... | collective-permute-start | bytes 786440 | tf_op jit(solution)/shard_map/ppermute | solution.py:415
  31.5 5.5 %collective-permute-start.10 = (bf16[128,512]{1,0:T(8,128)(2,1)S(1)}, bf16[128,512]{1,0:T(8,128)(2,1)S(1)}, u32[]{:S(2)}, u32[]{:S(2)}) collective-permute-start(bf16[128,512]{1,0:T(8,128)(2,1)S(1)} %get-tuple-element.74.refs_0_), channel_id=1, source_target_pairs={{0,4},{4,0},{8,12},{12,8},{16,20},{20,16},{24,28},{28,24},{1,5},{5... | collective-permute-start | bytes 393224 | tf_op jit(solution)/shard_map/ppermute | solution.py:418
  37.1 5.0 %collective-permute-start.11 = (bf16[128,512]{1,0:T(8,128)(2,1)S(1)}, bf16[128,512]{1,0:T(8,128)(2,1)S(1)}, u32[]{:S(2)}, u32[]{:S(2)}) collective-permute-start(bf16[128,512]{1,0:T(8,128)(2,1)S(1)} %shard_map.82.refs_0_), channel_id=1, source_target_pairs={{0,8},{4,12},{8,0},{12,4},{16,24},{20,28},{24,16},{28,20},{1,9},{5... | collective-permute-start | bytes 393224 | tf_op jit(solution)/shard_map/ppermute | solution.py:418
  42.2 7.4 %collective-permute-start.12 = (bf16[128,512]{1,0:T(8,128)(2,1)S(1)}, bf16[128,512]{1,0:T(8,128)(2,1)S(1)}, u32[]{:S(2)}, u32[]{:S(2)}) collective-permute-start(bf16[128,512]{1,0:T(8,128)(2,1)S(1)} %shard_map.84), channel_id=1, source_target_pairs={{0,16},{4,20},{8,24},{12,28},{16,0},{20,4},{24,8},{28,12},{1,17},{... | collective-permute-start | bytes 393224 | tf_op jit(solution)/shard_map/ppermute | solution.py:418
  50.4 4.2 %collective-permute-start.13 = (bf16[384,512]{1,0:T(8,128)(2,1)S(1)}, bf16[384,512]{1,0:T(8,128)(2,1)S(1)}, u32[]{:S(2)}, u32[]{:S(2)}) collective-permute-start(bf16[384,512]{1,0:T(8,128)(2,1)S(1)} %shard_map.86.refs_0_.n0_ref), channel_id=1, source_target_pairs={{0,1},{1,0},{2,3},{3,2},{4,5},{5,4},{6,7},{7,6},{8,9},{9,8},{10,11... | collective-permute-start | bytes 1179656 | tf_op jit(solution)/shard_map/ppermute | solution.py:415
  50.5 1.9 %collective-permute-start.17 = (bf16[128,512]{1,0:T(8,128)(2,1)S(1)}, bf16[128,512]{1,0:T(8,128)(2,1)S(1)}, u32[]{:S(2)}, u32[]{:S(2)}) collective-permute-start(bf16[128,512]{1,0:T(8,128)(2,1)S(1)} %shard_map.85.refs_3_.refs_0_.n0_ref), channel_id=1, source_target_pairs={{0,1},{1,0},{2,3},{3,2},{4,5},{5,4},{6,7},{7,6},{8,9},{9,8},{10,11... | collective-permute-start | bytes 393224 | tf_op jit(solution)/shard_map/ppermute | solution.py:415
  52.9 9.2 %collective-permute-start.18 = (bf16[128,1024]{1,0:T(8,128)(2,1)S(1)}, bf16[128,1024]{1,0:T(8,128)(2,1)S(1)}, u32[]{:S(2)}, u32[]{:S(2)}) collective-permute-start(bf16[128,1024]{1,0:T(8,128)(2,1)S(1)} %shard_map.90), channel_id=1, source_target_pairs={{0,2},{1,3},{2,0},{3,1},{4,6},{5,7},{6,4},{7,5},{8,10},{9,11},{10,... | collective-permute-start | bytes 786440 | tf_op jit(solution)/shard_map/ppermute | solution.py:415
  55.1 12.6 %collective-permute-start.16 = (bf16[128,1024]{1,0:T(8,128)(2,1)S(1)}, bf16[128,1024]{1,0:T(8,128)(2,1)S(1)}, u32[]{:S(2)}, u32[]{:S(2)}) collective-permute-start(bf16[128,1024]{1,0:T(8,128)(2,1)S(1)} %shard_map.89), channel_id=1, source_target_pairs={{0,2},{1,3},{2,0},{3,1},{4,6},{5,7},{6,4},{7,5},{8,10},{9,11},{10,... | collective-permute-start | bytes 786440 | tf_op jit(solution)/shard_map/ppermute | solution.py:415
  56.0 17.3 %collective-permute-start.15 = (bf16[128,1024]{1,0:T(8,128)(2,1)S(1)}, bf16[128,1024]{1,0:T(8,128)(2,1)S(1)}, u32[]{:S(2)}, u32[]{:S(2)}) collective-permute-start(bf16[128,1024]{1,0:T(8,128)(2,1)S(1)} %shard_map.88), channel_id=1, source_target_pairs={{0,2},{1,3},{2,0},{3,1},{4,6},{5,7},{6,4},{7,5},{8,10},{9,11},{10,... | collective-permute-start | bytes 786440 | tf_op jit(solution)/shard_map/ppermute | solution.py:415
  58.2 20.0 %collective-permute-start.14 = (bf16[128,1024]{1,0:T(8,128)(2,1)S(1)}, bf16[128,1024]{1,0:T(8,128)(2,1)S(1)}, u32[]{:S(2)}, u32[]{:S(2)}) collective-permute-start(bf16[128,1024]{1,0:T(8,128)(2,1)S(1)} %shard_map.87), channel_id=1, source_target_pairs={{0,2},{1,3},{2,0},{3,1},{4,6},{5,7},{6,4},{7,5},{8,10},{9,11},{10,... | collective-permute-start | bytes 786440 | tf_op jit(solution)/shard_map/ppermute | solution.py:415

commit v5 on v4

--- a/solution.py
+++ b/solution.py
@@ -70,25 +70,6 @@
     for copy in started:
         copy.start()
     return started
-
-
-def cut_columns(tokens, cuts):
-    def kernel(t_ref, *refs):
-        for copy in copies([(t_ref.at[:, cut], o_ref) for cut, o_ref in zip(cuts, refs)], refs[-1]):
-            copy.wait()
-
-    outs = [shape((tokens.shape[0], cut.stop - cut.start), tokens.dtype) for cut in cuts]
-    return call(kernel, [tokens], outs, 0, hbm=1, scratch=[pltpu.SemaphoreType.DMA((len(cuts),))])
-
-
-def split(x, after):
-    rows, columns = x.shape
-
-    def kernel(x_ref, a_ref, b_ref):
-        a_ref[...] = x_ref[:, : columns // 2]
-        b_ref[...] = x_ref[:, columns // 2 :]
-
-    return call(kernel, [x], [shape((rows, columns // 2), x.dtype)] * 2, 0, after)
 
 
 def upper_half(slab_ref, bit):
@@ -135,6 +116,56 @@
     return call(kernel, ins, [shape(total.shape, F32)] * 5, 0, smem=1)
 
 
+def pair_totals(total, other):
+    def kernel(t_ref, o_ref, out_ref):
+        out_ref[0:4, :] = t_ref[0:4, :]
+        out_ref[4:8, :] = o_ref[0:4, :]
+
+    return call(kernel, [total, other], [shape(total.shape, F32)], 0)[0]
+
+
+def link_four(slab, here, there):
+    def kernel(slab_ref, h_ref, t_ref, total_out, before_out, factors_out, span1_out, span2_out):
+        upper, above = upper_half(slab_ref, 0), upper_half(slab_ref, 1)
+        mine, beside = h_ref[0:1, :], h_ref[4:5, :]
+        across, diagonal = t_ref[0:1, :], t_ref[4:5, :]
+        own_pair, other_pair = mine + beside, across + diagonal
+        first = jnp.where(upper, beside, 0.0)
+        second = first + jnp.where(above, other_pair, 0.0)
+        own_scale = jnp.where(above, 0.0, other_pair)
+        other_scale = jnp.where(above, own_pair, 0.0)
+        by_mine = jnp.where(upper, 0.0, beside)
+        by_beside = jnp.where(upper, mine, 0.0)
+        by_across = jnp.where(upper, 0.0, diagonal)
+        by_diagonal = jnp.where(upper, across, 0.0)
+        factors_out[0:1, :] = jnp.exp(by_mine + own_scale)
+        factors_out[1:2, :] = jnp.exp(by_beside + own_scale)
+        factors_out[2:3, :] = jnp.exp(by_across + other_scale)
+        factors_out[3:4, :] = jnp.exp(by_diagonal + other_scale)
+        factors_out[4:5, :] = jnp.exp(by_across)
+        factors_out[5:6, :] = jnp.exp(by_diagonal)
+        factors_out[6:8, :] = jnp.zeros((2, h_ref.shape[1]), F32)
+        wide = h_ref.shape
+        total_out[...] = jnp.broadcast_to(own_pair + other_pair, wide)
+        before_out[...] = jnp.broadcast_to(second, wide)
+        span1_out[...] = jnp.broadcast_to(jnp.where(above, first, -jnp.inf), wide)
+        span2_out[...] = jnp.broadcast_to(jnp.where(upper_half(slab_ref, 2), second, -jnp.inf), wide)
+
+    return call(kernel, [slab, here, there], [shape(here.shape, F32)] * 5, 0, smem=1)
+
+
+def join_four(mine, beside, across, diagonal, factors):
+    def kernel(m_ref, b_ref, a_ref, d_ref, f_ref, four_ref, pair_ref):
+        m, b = m_ref[...].astype(F32), b_ref[...].astype(F32)
+        a, d = a_ref[...].astype(F32), d_ref[...].astype(F32)
+        f = [f_ref[i : i + 1, :] for i in range(6)]
+        four_ref[...] = (f[0] * m + f[1] * b + f[2] * a + f[3] * d).astype(BF16)
+        pair_ref[...] = (f[4] * a + f[5] * d).astype(BF16)
+
+    outs = [shape(mine.shape, BF16)] * 2
+    return call(kernel, [mine, beside, across, diagonal, factors], outs, 0)
+
+
 def combine(state, other, own_factor, other_factor):
     def kernel(s_ref, o_ref, a_ref, b_ref, out_ref):
         out_ref[...] = (
@@ -144,19 +175,16 @@
     return call(kernel, [state, other, own_factor, other_factor], [shape(state.shape, BF16)], 0)[0]
 
 
-def begin(me, slab, tokens, cuts, near, log_decay_rows, ws, w_out, head_size):
+def begin(me, slab, tokens, near, log_decay_rows, ws, w_out, head_size):
     wq, wk, wv, wl = ws
-    n_x = len(tokens)
-    shard = near.shape[1]
-    rows = near.shape[0]
+    rows, shard = near.shape
     q_width, kv_width = wq.shape[1], wk.shape[1]
     heads = log_decay_rows.shape[0]
     block = w_out.shape[1] // 4
 
-    def kernel(me_ref, slab_ref, wq_ref, wk_ref, wv_ref, wl_ref, wo_ref, *refs):
-        x_refs, near_ref, decay_ref, refs = refs[:n_x], refs[n_x], refs[n_x + 1], refs[n_x + 2 :]
+    def kernel(me_ref, slab_ref, t_ref, wq_ref, wk_ref, wv_ref, wl_ref, wo_ref, near_ref, decay_ref, *refs):
         total_q, total_kv, total_l, far_q, far_kv, all_l = refs[:6]
-        decay_outs, blocks, (own_q, own_kv, sems) = refs[6:11], refs[11:15], refs[15:]
+        decay_outs, blocks, (own_x, own_q, own_kv, sems) = refs[6:11], refs[11:15], refs[15:]
 
         def pairs(i, q_dst, kv_dst):
             here = pl.ds(pl.multiple_of((me_ref[0] ^ i) * shard, 128), shard)
@@ -169,26 +197,26 @@
         def columns(i):
             return wo_ref.at[:, pl.ds(pl.multiple_of((me_ref[0] ^ i) * block, 128), block)]
 
-        moves = pairs(0, own_q.at[0], own_kv.at[0]) + [(wl_ref, all_l)]
+        moves = pairs(0, own_q.at[0], own_kv.at[0]) + [(wl_ref, all_l), (t_ref, own_x)]
         moves += pairs(1, own_q.at[1], own_kv.at[1])
         moves += pairs(2, far_q.at[0], far_kv.at[0]) + pairs(3, far_q.at[1], far_kv.at[1])
         moves += [(columns(i), blocks[i]) for i in range(4)]
         started = copies(moves, sems)
         decays(slab_ref, decay_ref, *decay_outs)
-        for copy in started[:4]:
+        for copy in started[:5]:
             copy.wait()
         lanes = pl.ds(pl.multiple_of(me_ref[0] * shard, 128), shard)
-        own = jnp.concatenate([x_ref[...] for x_ref in x_refs], axis=1)
+        own = own_x[...]
         total_kv[...] = dot(own, own_kv[0])
         total_q[...] = dot(own, own_q[0])
         total_l[...] = dot_dims(own, all_l[:, lanes], 1, 1)
-        for copy in started[4:7]:
+        for copy in started[5:8]:
             copy.wait()
         lanes = pl.ds(pl.multiple_of((me_ref[0] ^ 1) * shard, 128), shard)
         total_kv[...] += dot(near_ref[...], own_kv[1])
         total_q[...] += dot(near_ref[...], own_q[1])
         total_l[...] += dot_dims(near_ref[...], all_l[:, lanes], 1, 1)
-        for copy in started[7:]:
+        for copy in started[8:]:
             copy.wait()
 
     wide = shape((8, heads * head_size), F32)
@@ -206,58 +234,41 @@
         wide,
     ] + [shape((w_out.shape[0], block), BF16)] * 4
     scratch = [
+        pltpu.VMEM((rows, shard), BF16),
         pltpu.VMEM((2, shard, q_width), BF16),
         pltpu.VMEM((2, shard, 2 * kv_width), BF16),
-        pltpu.SemaphoreType.DMA((17,)),
+        pltpu.SemaphoreType.DMA((18,)),
     ]
-    ins = [me, slab, wq, wk, wv, wl, w_out, *tokens, near, log_decay_rows]
-    outs = call(kernel, ins, outs, 0, smem=2, hbm=5, scratch=scratch, megabytes=14)
+    ins = [me, slab, tokens, wq, wk, wv, wl, w_out, near, log_decay_rows]
+    outs = call(kernel, ins, outs, 0, smem=2, hbm=6, scratch=scratch, megabytes=14)
     return outs[:3], outs[3:6], outs[6:11], outs[11:]
 
 
-def add_products(xs, w_ref, offset):
-    total = None
-    for i, x_ref in enumerate(xs):
-        add = dot(x_ref[...], w_ref[i, offset : offset + x_ref.shape[1], :])
-        total = add if total is None else total + add
-    return total
-
-
-def add_levels(me_ref, xs, wl_ref, offset):
+def add_levels(me_ref, place, x_ref, wl_ref):
     shard = wl_ref.shape[1] // 4
-    total = None
-    for i, x_ref in enumerate(xs):
-        start = pl.multiple_of((me_ref[0] ^ (2 + i)) * shard + offset, 128)
-        add = dot_dims(x_ref[...], wl_ref[:, pl.ds(start, x_ref.shape[1])], 1, 1)
-        total = add if total is None else total + add
-    return total
-
-
-def project(me, xs, ws, offset, totals, after=()):
-    n_x = len(xs)
-
-    def kernel(me_ref, *refs):
-        x, (q_ref, kv_ref, l_ref), ins, outs = refs[:n_x], refs[n_x : n_x + 3], refs[-6:-3], refs[-3:]
-        outs[1][...] = ins[1][...] + add_products(x, kv_ref, offset)
-        outs[0][...] = ins[0][...] + add_products(x, q_ref, offset)
-        outs[2][...] = ins[2][...] + add_levels(me_ref, x, l_ref, offset)
-
-    ins = [me, *xs, *ws, *totals]
-    aliases = {n_x + 4 + i: i for i in range(3)}
+    start = pl.multiple_of((me_ref[0] ^ place) * shard, 128)
+    return dot_dims(x_ref[...], wl_ref[:, pl.ds(start, shard)], 1, 1)
+
+
+def project(me, place, x, ws, totals, after=()):
+    def kernel(me_ref, x_ref, q_ref, kv_ref, l_ref, *refs):
+        ins, outs = refs[:3], refs[3:]
+        outs[1][...] = ins[1][...] + dot(x_ref[...], kv_ref[place - 2])
+        outs[0][...] = ins[0][...] + dot(x_ref[...], q_ref[place - 2])
+        outs[2][...] = ins[2][...] + add_levels(me_ref, place, x_ref, l_ref)
+
     outs = [shape(t.shape, F32) for t in totals]
-    return call(kernel, ins, outs, 0, after, smem=1, aliases=aliases)
-
-
-def project_state(xs, wkv, offset, total_kv, keep, head_size):
-    rows, depth = xs[0].shape
-    n_x = len(xs)
+    return call(kernel, [me, x, *ws, *totals], outs, 0, after, smem=1, aliases={5: 0, 6: 1, 7: 2})
+
+
+def project_state(x, wkv, total_kv, keep, head_size):
+    rows = x.shape[0]
     heads = keep.shape[1]
     kv_width = wkv.shape[2] // 2
     group = heads // (kv_width // head_size)
 
-    def kernel(*refs):
-        x, (w_ref, total_ref, keep_ref, k_out, v_out, s_out) = refs[:n_x], refs[n_x:]
-        total = total_ref[...] + add_products(x, w_ref, offset)
+    def kernel(x_ref, w_ref, total_ref, keep_ref, k_out, v_out, s_out):
+        total = total_ref[...] + dot(x_ref[...], w_ref[1])
         keys = total[:, :kv_width].astype(BF16)
         values = total[:, kv_width:].astype(BF16)
         k_out[...] = keys
@@ -277,25 +288,23 @@
         shape((rows, kv_width), BF16),
         shape((head_size, heads * head_size), BF16),
     ]
-    return call(kernel, [*xs, wkv, total_kv, keep], outs, 0)
-
-
-def attend(me, xs, wq, wl, offset, total_q, total_l, k, v, dcol, drow, spans, states, head_size, level_count):
+    return call(kernel, [x, wkv, total_kv, keep], outs, 0)
+
+
+def attend(me, place, x, wq, wl, total_q, total_l, k, v, dcol, drow, spans, states, head_size, level_count):
     rows, width = total_q.shape
-    n_x = len(xs)
     bits = len(spans)
     heads = width // head_size
     group = heads // (k.shape[1] // head_size)
     own_levels = level_count - bits
 
-    def kernel(me_ref, *refs):
-        x, refs = refs[:n_x], refs[n_x:]
+    def kernel(me_ref, x_ref, *refs):
         wq_ref, wl_ref, tq_ref, tl_ref, k_ref, v_ref, dcol_ref, drow_ref = refs[:8]
         span_refs, state_refs = refs[8 : 8 + bits], refs[8 + bits : 7 + 2 * bits]
         o_ref, s_ref, q_ref, l_ref = refs[-4:]
-        raw = tl_ref[...] + add_levels(me_ref, x, wl_ref, offset)
+        raw = tl_ref[...] + add_levels(me_ref, place, x_ref, wl_ref)
         l_ref[...] = jnp.maximum(raw, 0.0) + jnp.log1p(jnp.exp(-jnp.abs(raw)))
-        q_ref[...] = (tq_ref[...] + add_products(x, wq_ref, offset)).astype(BF16)
+        q_ref[...] = (tq_ref[...] + dot(x_ref[...], wq_ref[place - 2])).astype(BF16)
         row_id = lax.broadcasted_iota(jnp.int32, (BLOCK, BLOCK), 0)
         col_id = lax.broadcasted_iota(jnp.int32, (BLOCK, BLOCK), 1)
         causal = row_id >= col_id
@@ -337,10 +346,10 @@
                         total = total + dot_dims(scaled, state_refs[b][:, cols], 1, 1)
                 o_ref[here, cols] = total
 
-    ins = [me, *xs, wq, wl, total_q, total_l, k, v, dcol, drow, *spans, *states]
+    ins = [me, x, wq, wl, total_q, total_l, k, v, dcol, drow, *spans, *states]
     wide = shape((rows, width), BF16)
     outs = [shape((rows, width), F32), wide, wide, shape(total_l.shape, F32)]
-    flops = 2 * rows * xs[0].shape[1] * n_x * width + 4 * rows * rows * width
+    flops = 2 * rows * x.shape[1] * width + 4 * rows * rows * width
     return call(kernel, ins, outs, flops, smem=1)[:2]
 
 
@@ -358,46 +367,46 @@
     return call(kernel, [local, scaled, state], outs, 0, after)[0]
 
 
-def out_far(n0, n1, w0, w1, rows_own, rows_near):
-    rows, columns = rows_own.stop - rows_own.start, w1.shape[1]
+def out_block(n0s, n1s, cuts, w0, w1, dtype, after=()):
+    columns = w1.shape[1]
+    count = len(n0s)
+    rows = sum(cut.stop - cut.start for cut in cuts)
     tile = min(columns, 512)
 
-    def kernel(n0_ref, n1_ref, w0_ref, w1_ref, o_ref):
-        for c in range(0, columns, tile):
-            cols = slice(c, c + tile)
-            o_ref[:, cols] = (
-                dot(n0_ref[rows_own, :], w0_ref[:, cols]) + dot(n1_ref[rows_near, :], w1_ref[:, cols])
-            ).astype(BF16)
-
-    return call(kernel, [n0, n1, w0, w1], [shape((rows, columns), BF16)], 0)[0]
-
-
-def out_here(n0, n1, w0, w1, rows_own, rows_near, arrived, out, total_rows, start_row):
+    def kernel(*refs):
+        w0_ref, w1_ref, o_ref = refs[2 * count :]
+        start = 0
+        for a_ref, b_ref, cut in zip(refs[:count], refs[count : 2 * count], cuts):
+            here = slice(start, start + cut.stop - cut.start)
+            start = here.stop
+            for c in range(0, columns, tile):
+                cols = slice(c, c + tile)
+                o_ref[here, cols] = (
+                    dot(a_ref[cut, :], w0_ref[:, cols]) + dot(b_ref[cut, :], w1_ref[:, cols])
+                ).astype(dtype)
+
+    return call(kernel, [*n0s, *n1s, w0, w1], [shape((rows, columns), dtype)], 0, after)[0]
+
+
+def add_rows(here, arrived, out, start):
     rows, columns = arrived.shape
-    block = start_row // rows
-    tile = min(columns, 512)
-
-    def kernel(n0_ref, n1_ref, w0_ref, w1_ref, a_ref, *refs):
-        o_ref = refs[-1]
-        for c in range(0, columns, tile):
-            cols = slice(c, c + tile)
-            here = dot(n0_ref[rows_own, :], w0_ref[:, cols]) + dot(n1_ref[rows_near, :], w1_ref[:, cols])
-            o_ref[:, cols] = (here + a_ref[:, cols].astype(F32)).astype(BF16)
-
-    ins, specs, aliases = [n0, n1, w0, w1, arrived], [VMEM] * 5, {}
+    block = start // rows
+
+    def kernel(h_ref, a_ref, *refs):
+        refs[-1][...] = (h_ref[start : start + rows, :] + a_ref[...].astype(F32)).astype(BF16)
+
+    ins, specs, aliases = [here, arrived], [VMEM] * 2, {}
     if out is not None:
-        ins, specs, aliases = ins + [out], specs + [ANY], {5: 0}
+        ins, specs, aliases = ins + [out], specs + [ANY], {2: 0}
     return pl.pallas_call(
         kernel,
         grid=(1,),
         in_specs=specs,
         out_specs=pl.BlockSpec((rows, columns), lambda s: (block, 0)),
-        out_shape=shape((total_rows, columns), BF16),
+        out_shape=shape(here.shape, BF16),
         input_output_aliases=aliases,
         compiler_params=pltpu.CompilerParams(vmem_limit_bytes=8 * 1024 * 1024),
-        cost_estimate=pl.CostEstimate(
-            flops=4 * rows * columns * w0.shape[0], bytes_accessed=rows * columns * 16, transcendentals=0
-        ),
+        cost_estimate=pl.CostEstimate(flops=0, bytes_accessed=rows * columns * 8, transcendentals=0),
     )(*ins)
 
 
@@ -417,63 +426,56 @@
     def swap_seq(x, bit):
         return lax.ppermute(x, "seq", [(i, i ^ bit) for i in range(seq_size)])
 
-    half, quarter = shard // 2, shard // 4
-    cuts = [slice(0, half), slice(half, shard)]
-    pieces = cut_columns(tokens, cuts)
-    far = [swap_tp(x, 2) for x in pieces]
+    far = swap_tp(tokens, 2)
     near = swap_tp(tokens, 1)
 
     weights = (w_query, w_key, w_value, w_level.T)
     totals, ws, (drow, dcol, keep, total, span), blocks = begin(
-        me, slab, pieces, cuts, near, log_decay.T, weights, w_out, head_size
+        me, slab, tokens, near, log_decay.T, weights, w_out, head_size
     )
     w_here_own, w_here_send, w_far_own, w_far_send = blocks
     w_here, w_far = swap_tp(w_here_send, 1), swap_tp(w_far_send, 1)
 
-    spans, factors, before = [span], [], None
-    for b in range(seq_bits - 1):
-        total, before, own, other, span = link(slab, b, total, swap_seq(total, 1 << b), before)
+    here = pair_totals(total, swap_seq(total, 1))
+    group_total, before, four_factors, *later_spans = link_four(slab, here, swap_seq(here, 2))
+    spans, factors = [span, *later_spans], []
+    for b in range(2, seq_bits - 1):
+        group_total, before, own, other, span = link(slab, b, group_total, swap_seq(group_total, 1 << b), before)
         spans.append(span)
         factors.append((own, other))
 
     wq, wkv, wl = ws
-    arrived = gate(far[0], total, totals[0])
-    pair = (arrived, swap_tp(arrived, 1))
-    later = split(far[1], (totals[0],))
-    totals = project(me, pair, ws, 0, totals, (w_far, w_here))
-    pair = (later[0], swap_tp(later[0], 1))
-    totals = project(me, pair, ws, half, totals)
-    pair = (later[1], swap_tp(later[1], 1))
-    total_q, total_kv, total_l = totals
-    last = half + quarter
-    k, v, state = project_state(pair, wkv, last, total_kv, keep, head_size)
-
-    earlier = []
-    for b in range(seq_bits):
+    arrived = gate(far, group_total, w_far, w_here)
+    arrived_near = swap_tp(arrived, 1)
+    total_q, total_kv, total_l = project(me, 2, arrived, ws, totals)
+    k, v, state = project_state(arrived_near, wkv, total_kv, keep, head_size)
+
+    beside, across, diagonal = (swap_seq(state, bits) for bits in (1, 2, 3))
+    state, other_pair = join_four(state, beside, across, diagonal, four_factors)
+    earlier = [beside, other_pair]
+    for b in range(2, seq_bits):
         other = swap_seq(state, 1 << b)
         earlier.append(other)
         if b < seq_bits - 1:
-            state = combine(state, other, *factors[b])
+            state = combine(state, other, *factors[b - 2])
 
     local, scaled = attend(
-        me, pair, wq, wl, last, total_q, total_l, k, v, dcol, drow, spans, earlier[:-1], head_size, level_count
+        me, 3, arrived_near, wq, wl, total_q, total_l, k, v, dcol, drow, spans, earlier[:-1], head_size, level_count
     )
 
     step = rows // 4
-    normed = []
-    for cut in (slice(0, step), slice(step, rows)):
-        after = (normed[0][0],) if normed else ()
-        own = finish(local, scaled, earlier[-1], cut, head_size, after)
-        normed.append((own, swap_tp(own, 1)))
-    pieces = [(normed[0], 0, 0)] + [(normed[1], r, r + step) for r in range(0, rows - step, step)]
-    crossing = []
-    for pair, r, _ in pieces:
-        cut = slice(r, r + step)
-        crossing.append(out_far(*pair, w_far_own, w_far, cut, cut))
+    own = finish(local, scaled, earlier[-1], slice(0, step), head_size)
+    near_own = swap_tp(own, 1)
+    rest = finish(local, scaled, earlier[-1], slice(step, rows), head_size, (near_own,))
+    near_rest = swap_tp(rest, 1)
+    crossing = [out_block([own], [near_own], [slice(0, step)], w_far_own, w_far, BF16)]
+    for r in range(0, rows - step, step):
+        crossing.append(out_block([rest], [near_rest], [slice(r, r + step)], w_far_own, w_far, BF16))
+    both = [slice(0, step), slice(0, rows - step)]
+    own_block = out_block([own, rest], [near_own, near_rest], both, w_here_own, w_here, F32, (crossing[-1],))
     out = None
-    for (pair, r, start), x in zip(pieces, crossing):
-        cut = slice(r, r + step)
-        out = out_here(*pair, w_here_own, w_here, cut, cut, swap_tp(x, 2), out, rows, start)
+    for r, x in enumerate(crossing):
+        out = add_rows(own_block, swap_tp(x, 2), out, r * step)
     return out
 
 

time: 79.5 us -> 78.3 us (0.985)
  Pallas kernels: 20.8 us -> 19.2 us
  waiting for transfers between devices: 37.4 us -> 38.2 us
    ppermute x14 -> x11, starting transfers between devices: 10.6 us -> 8.77 us  [swap_tp(): return lax.ppermute(x, 'tp', [(i, i ^ bit) for i in range(4)])]
    pallas_call x4, Pallas kernels: 4.68 us -> 2.99 us  [add_rows(): pl.pallas_call(kernel, grid=(1,), in_specs=specs, out_specs=pl.BlockSpec(...]
    ppermute x5 -> x6, starting transfers between devices: 9.65 us -> 11.1 us  [swap_seq(): return lax.ppermute(x, 'seq', [(i, i ^ bit) for i in range(seq_size)])]
    ppermute x14 -> x11, waiting for transfers between devices: 25.2 us -> 26.7 us  [swap_tp(): return lax.ppermute(x, 'tp', [(i, i ^ bit) for i in range(4)])]
    ppermute x5 -> x6, waiting for transfers between devices: 12.2 us -> 11.5 us  [swap_seq(): return lax.ppermute(x, 'seq', [(i, i ^ bit) for i in range(seq_size)])]
    pallas_call x17 -> x14, Pallas kernels: 16.1 us -> 16.2 us  [call(): pl.pallas_call(run, in_specs=[SMEM] * smem + [HBM] * hbm + [VMEM] * (coun...]
  transfers between devices with their start and end apart: 19 -> 17, of which waited for: 11 -> 12; matrix products, arithmetic and copies ran while one was open for 0% -> 0% of each run, Pallas kernels for 23% -> 21%
where the time goes in v5:
time: 78.3 us; the launch traced here: 78.1 us
  waiting for transfers between devices  38.2 us (49%)
  starting transfers between devices  19.9 us (25%)
  Pallas kernels  19.2 us (25%)
    ppermute x11, waiting for transfers between devices, swap_tp(): return lax.ppermute(x, 'tp', [(i, i ^ bit) for i in range(4)])  26.7 us
    pallas_call x14, Pallas kernels, call(): pl.pallas_call(run, in_specs=[SMEM] * smem + [HBM] * hbm + [VMEM] * (coun...  16.2 us
    ppermute x6, waiting for transfers between devices, swap_seq(): return lax.ppermute(x, 'seq', [(i, i ^ bit) for i in range(seq_size)])  11.5 us
    ppermute x6, starting transfers between devices, swap_seq(): return lax.ppermute(x, 'seq', [(i, i ^ bit) for i in range(seq_size)])  11.1 us
    ppermute x11, starting transfers between devices, swap_tp(): return lax.ppermute(x, 'tp', [(i, i ^ bit) for i in range(4)])  8.77 us
    pallas_call x4, Pallas kernels, add_rows(): pl.pallas_call(kernel, grid=(1,), in_specs=specs, out_specs=pl.BlockSpec(...  2.99 us
  transfers between devices with their start and end apart: 17, of which 12 were waited for; matrix products, arithmetic and copies ran while one was open for 0% of the time, Pallas kernels for 21%

profile of v5, /device:TPU:0, one launch (start us, length us, event | category | flops | bytes accessed | tf_op | source)
XLA Modules:
  0.0 78.1 jit_solution(14691607965739817778)
XLA Ops:
  0.5 2.5 %collective-permute-start = (bf16[512,1024]{1,0:T(8,128)(2,1)}, bf16[512,1024]{1,0:T(8,128)(2,1)S(1)}, u32[]{:S(2)}, u32[]{:S(2)}) collective-permute-start(bf16[512,1024]{1,0:T(8,128)(2,1)} %refs_2_.1), channel_id=1, source_target_pairs={{0,2},{1,3},{2,0},{3,1},{4,6},{5,7},{6,4},{7,5},{8,10},{9,11},{10,... | collective-permute-start | bytes 3145736 | tf_op jit(solution)/shard_map/ppermute | solution.py:424
  3.7 5.4 %shard_map.73 = (f32[512,512]{1,0:T(8,128)S(1)}, f32[512,256]{1,0:T(8,128)S(1)}, f32[512,24]{1,0:T(8,128)S(1)}, bf16[2,1024,512]{2,1,0:T(8,128)(2,1)S(1)}, bf16[...) custom-call(s32[1]{0:T(128)} %bitcast.refs_0_, ...), custom_call_target="tpu_custom_call" | custom-call | tf_op jit(solution)/shard_map/pallas_call | solution.py:41
  9.6 2.8 %collective-permute-start.2 = (f32[8,512]{1,0:T(8,128)S(1)}, f32[8,512]{1,0:T(8,128)S(1)}, u32[]{:S(2)}, u32[]{:S(2)}) collective-permute-start(f32[8,512]{1,0:T(8,128)S(1)} %get-tuple-element.34.refs_0_), channel_id=1, source_target_pairs={{0,4},{4,0},{8,12},{12,8},{16,20},{20,16},{24,28},{28,24},{1,5},{5... | collective-permute-start | bytes 49160 | tf_op jit(solution)/shard_map/ppermute | solution.py:427
  12.5 1.7 %collective-permute-done.2.refs_1_ = f32[8,512]{1,0:T(8,128)S(1)} collective-permute-done((f32[8,512]{1,0:T(8,128)S(1)}, f32[8,512]{1,0:T(8,128)S(1)}, u32[]{:S(2)}, u32[]{:S(2)}) %collective-permute-start.2) | collective-permute-done | bytes 16416 | tf_op jit(solution)/shard_map/ppermute | solution.py:427
  14.2 2.1 %collective-permute-start.3 = (f32[8,512]{1,0:T(8,128)S(1)}, f32[8,512]{1,0:T(8,128)S(1)}, u32[]{:S(2)}, u32[]{:S(2)}) collective-permute-start(f32[8,512]{1,0:T(8,128)S(1)} %shard_map.74.refs_1_), channel_id=1, source_target_pairs={{0,8},{4,12},{8,0},{12,4},{16,24},{20,28},{24,16},{28,20},{1,9},{5... | collective-permute-start | bytes 49160 | tf_op jit(solution)/shard_map/ppermute | solution.py:427
  16.3 1.7 %collective-permute-done.3.refs_2_ = f32[8,512]{1,0:T(8,128)S(1)} collective-permute-done((f32[8,512]{1,0:T(8,128)S(1)}, f32[8,512]{1,0:T(8,128)S(1)}, u32[]{:S(2)}, u32[]{:S(2)}) %collective-permute-start.3) | collective-permute-done | bytes 16416 | tf_op jit(solution)/shard_map/ppermute | solution.py:427
  18.6 8.4 %collective-permute-done.refs_0_ = bf16[512,1024]{1,0:T(8,128)(2,1)S(1)} collective-permute-done((bf16[512,1024]{1,0:T(8,128)(2,1)}, bf16[512,1024]{1,0:T(8,128)(2,1)S(1)}, u32[]{:S(2)}, u32[]{:S(2)}) %collective-permute-start) | collective-permute-done | bytes 1048608 | tf_op jit(solution)/shard_map/ppermute | solution.py:424
  27.1 1.3 %shard_map.77 = (f32[512,512]{1,0:T(8,128)S(1)}, f32[512,256]{1,0:T(8,128)S(1)}, f32[512,24]{1,0:T(8,128)S(1)}) custom-call(s32[1]{0:T(128)} %bitcast.refs_0_, bf16[512,1024]{1,0:T(8,128)(2,1)S(1)} %shard_map.76.refs_1_, bf16[2,1024,512]{2,1,0:T(8,128)(2,1)S(1)} %get-tuple-element.38.refs_2_, ...), custom_call_target="tpu_custom_call", output_to_operand_aliasing={{0}: (5, {}), {1}: (6, {}), {2}: (7, {})} | custom-call | tf_op jit(solution)/shard_map/pallas_call | solution.py:41
  28.4 1.3 %collective-permute-done.6.refs_0_.refs_1_ = bf16[512,1024]{1,0:T(8,128)(2,1)S(1)} collective-permute-done((bf16[512,1024]{1,0:T(8,128)(2,1)S(1)}, bf16[512,1024]{1,0:T(8,128)(2,1)S(1)}, u32[]{:S(2)}, u32[]{:S(2)}) %collective-permute-start.6) | collective-permute-done | bytes 1048608 | tf_op jit(solution)/shard_map/ppermute | solution.py:424
  30.5 2.8 %collective-permute-start.9 = (bf16[128,512]{1,0:T(8,128)(2,1)S(1)}, bf16[128,512]{1,0:T(8,128)(2,1)S(1)}, u32[]{:S(2)}, u32[]{:S(2)}) collective-permute-start(bf16[128,512]{1,0:T(8,128)(2,1)S(1)} %get-tuple-element.55.refs_0_), channel_id=1, source_target_pairs={{0,12},{4,8},{8,4},{12,0},{16,28},{20,24},{24,20},{28,16},{1,13},{... | collective-permute-start | bytes 393224 | tf_op jit(solution)/shard_map/ppermute | solution.py:427
  34.1 3.7 %collective-permute-done.9.refs_3_ = bf16[128,512]{1,0:T(8,128)(2,1)S(1)} collective-permute-done((bf16[128,512]{1,0:T(8,128)(2,1)S(1)}, bf16[128,512]{1,0:T(8,128)(2,1)S(1)}, u32[]{:S(2)}, u32[]{:S(2)}) %collective-permute-start.9) | collective-permute-done | bytes 131104 | tf_op jit(solution)/shard_map/ppermute | solution.py:427
  37.8 2.3 %collective-permute-done.8.refs_2_ = bf16[128,512]{1,0:T(8,128)(2,1)S(1)} collective-permute-done((bf16[128,512]{1,0:T(8,128)(2,1)S(1)}, bf16[128,512]{1,0:T(8,128)(2,1)S(1)}, u32[]{:S(2)}, u32[]{:S(2)}) %collective-permute-start.8) | collective-permute-done | bytes 131104 | tf_op jit(solution)/shard_map/ppermute | solution.py:427
  40.3 2.6 %collective-permute-start.10 = (bf16[128,512]{1,0:T(8,128)(2,1)S(1)}, bf16[128,512]{1,0:T(8,128)(2,1)S(1)}, u32[]{:S(2)}, u32[]{:S(2)}) collective-permute-start(bf16[128,512]{1,0:T(8,128)(2,1)S(1)} %get-tuple-element.60), channel_id=1, source_target_pairs={{0,16},{4,20},{8,24},{12,28},{16,0},{20,4},{24,8},{28,12},{1,17},{... | collective-permute-start | bytes 393224 | tf_op jit(solution)/shard_map/ppermute | solution.py:427
  42.9 4.0 %shard_map.80 = (f32[512,512]{1,0:T(8,128)S(1)}, bf16[512,512]{1,0:T(8,128)(2,1)S(1)}, bf16[512,512]{1,0:T(8,128)(2,1)}, f32[512,24]{1,0:T(8,128)}) custom-call(s32[1]{0:T(128)} %bitcast.refs_0_, bf16[512,1024]{1,0:T(8,128)(2,1)S(1)} %collective-permute-done.6.refs_0_.refs_1_, bf16[2,1024,512]{2,1,0:T(8,128)(2,1)S(1)} %get-tuple-element.38.refs_2_, ...), custom_call_target="tpu_custom_call" | custom-call | flops 1073741824 | bytes 7176196 | tf_op jit(solution)/shard_map/pallas_call | solution.py:41
  46.9 2.0 %collective-permute-done.10.refs_2_ = bf16[128,512]{1,0:T(8,128)(2,1)S(1)} collective-permute-done((bf16[128,512]{1,0:T(8,128)(2,1)S(1)}, bf16[128,512]{1,0:T(8,128)(2,1)S(1)}, u32[]{:S(2)}, u32[]{:S(2)}) %collective-permute-start.10) | collective-permute-done | bytes 131104 | tf_op jit(solution)/shard_map/ppermute | solution.py:427
  49.4 1.3 %collective-permute-done.11.refs_3_.refs_2_.refs_1_ = bf16[128,512]{1,0:T(8,128)(2,1)S(1)} collective-permute-done((bf16[128,512]{1,0:T(8,128)(2,1)S(1)}, bf16[128,512]{1,0:T(8,128)(2,1)S(1)}, u32[]{:S(2)}, u32[]{:S(2)}) %collective-permute-start.11) | collective-permute-done | bytes 131104 | tf_op jit(solution)/shard_map/ppermute | solution.py:424
  51.8 1.6 %collective-permute-start.16 = (bf16[128,1024]{1,0:T(8,128)(2,1)S(1)}, bf16[128,1024]{1,0:T(8,128)(2,1)S(1)}, u32[]{:S(2)}, u32[]{:S(2)}) collective-permute-start(bf16[128,1024]{1,0:T(8,128)(2,1)S(1)} %shard_map.87), channel_id=1, source_target_pairs={{0,2},{1,3},{2,0},{3,1},{4,6},{5,7},{6,4},{7,5},{8,10},{9,11},{10,... | collective-permute-start | bytes 786440 | tf_op jit(solution)/shard_map/ppermute | solution.py:424
  54.0 1.1 %collective-permute-start.15 = (bf16[128,1024]{1,0:T(8,128)(2,1)S(1)}, bf16[128,1024]{1,0:T(8,128)(2,1)S(1)}, u32[]{:S(2)}, u32[]{:S(2)}) collective-permute-start(bf16[128,1024]{1,0:T(8,128)(2,1)S(1)} %shard_map.86), channel_id=1, source_target_pairs={{0,2},{1,3},{2,0},{3,1},{4,6},{5,7},{6,4},{7,5},{8,10},{9,11},{10,... | collective-permute-start | bytes 786440 | tf_op jit(solution)/shard_map/ppermute | solution.py:424
  55.5 1.1 %collective-permute-start.14 = (bf16[128,1024]{1,0:T(8,128)(2,1)S(1)}, bf16[128,1024]{1,0:T(8,128)(2,1)S(1)}, u32[]{:S(2)}, u32[]{:S(2)}) collective-permute-start(bf16[128,1024]{1,0:T(8,128)(2,1)S(1)} %shard_map.85), channel_id=1, source_target_pairs={{0,2},{1,3},{2,0},{3,1},{4,6},{5,7},{6,4},{7,5},{8,10},{9,11},{10,... | collective-permute-start | bytes 786440 | tf_op jit(solution)/shard_map/ppermute | solution.py:424
  58.2 1.3 %shard_map.84.h_ref = f32[512,1024]{1,0:T(8,128)S(1)} custom-call(bf16[128,512]{1,0:T(8,128)(2,1)S(1)} %shard_map.81.refs_0_, bf16[384,512]{1,0:T(8,128)(2,1)S(1)} %shard_map.82.refs_0_.refs_1_, bf16[128,512]{1,0:T(8,128)(2,1)S(1)} %collective-permute-done.11.refs_3_.refs_2_.refs_1_, bf16[384,512]{1,0:T(8,128)(2,1)S(1)} %collective-permute-done.12.refs_1_.refs_3_, ...), custom_call_target="tpu_custom_call" | custom-call | tf_op jit(solution)/shard_map/pallas_call | solution.py:41
  59.4 1.6 %collective-permute-done.16.a_ref = bf16[128,1024]{1,0:T(8,128)(2,1)S(1)} collective-permute-done((bf16[128,1024]{1,0:T(8,128)(2,1)S(1)}, bf16[128,1024]{1,0:T(8,128)(2,1)S(1)}, u32[]{:S(2)}, u32[]{:S(2)}) %collective-permute-start.16) | collective-permute-done | bytes 262176 | tf_op jit(solution)/shard_map/ppermute | solution.py:424
  61.8 4.9 %collective-permute-done.15.a_ref = bf16[128,1024]{1,0:T(8,128)(2,1)S(1)} collective-permute-done((bf16[128,1024]{1,0:T(8,128)(2,1)S(1)}, bf16[128,1024]{1,0:T(8,128)(2,1)S(1)}, u32[]{:S(2)}, u32[]{:S(2)}) %collective-permute-start.15) | collective-permute-done | bytes 262176 | tf_op jit(solution)/shard_map/ppermute | solution.py:424
  67.4 4.9 %collective-permute-done.14.a_ref = bf16[128,1024]{1,0:T(8,128)(2,1)S(1)} collective-permute-done((bf16[128,1024]{1,0:T(8,128)(2,1)S(1)}, bf16[128,1024]{1,0:T(8,128)(2,1)S(1)}, u32[]{:S(2)}, u32[]{:S(2)}) %collective-permute-start.14) | collective-permute-done | bytes 262176 | tf_op jit(solution)/shard_map/ppermute | solution.py:424
  73.0 4.3 %collective-permute-done.13.a_ref = bf16[128,1024]{1,0:T(8,128)(2,1)S(1)} collective-permute-done((bf16[128,1024]{1,0:T(8,128)(2,1)S(1)}, bf16[128,1024]{1,0:T(8,128)(2,1)S(1)}, u32[]{:S(2)}, u32[]{:S(2)}) %collective-permute-start.13) | collective-permute-done | bytes 262176 | tf_op jit(solution)/shard_map/ppermute | solution.py:424
  (31 shorter events, 11.1 us)
Async XLA Ops:
  0.0 3.0 %collective-permute-start.1 = (bf16[512,1024]{1,0:T(8,128)(2,1)}, bf16[512,1024]{1,0:T(8,128)(2,1)S(1)}, u32[]{:S(2)}, u32[]{:S(2)}) collective-permute-start(bf16[512,1024]{1,0:T(8,128)(2,1)} %refs_2_.1), channel_id=1, source_target_pairs={{0,1},{1,0},{2,3},{3,2},{4,5},{5,4},{6,7},{7,6},{8,9},{9,8},{10,11... | collective-permute-start | bytes 3145736 | tf_op jit(solution)/shard_map/ppermute | solution.py:424
  0.5 26.6 %collective-permute-start = (bf16[512,1024]{1,0:T(8,128)(2,1)}, bf16[512,1024]{1,0:T(8,128)(2,1)S(1)}, u32[]{:S(2)}, u32[]{:S(2)}) collective-permute-start(bf16[512,1024]{1,0:T(8,128)(2,1)} %refs_2_.1), channel_id=1, source_target_pairs={{0,2},{1,3},{2,0},{3,1},{4,6},{5,7},{6,4},{7,5},{8,10},{9,11},{10,... | collective-permute-start | bytes 3145736 | tf_op jit(solution)/shard_map/ppermute | solution.py:424
  3.0 0.7 copy-start
  9.0 18.0 %collective-permute-start.4 = (bf16[512,1024]{1,0:T(8,128)(2,1)S(1)}, bf16[512,1024]{1,0:T(8,128)(2,1)S(1)}, u32[]{:S(2)}, u32[]{:S(2)}) collective-permute-start(bf16[512,1024]{1,0:T(8,128)(2,1)S(1)} %get-tuple-element.36), channel_id=1, source_target_pairs={{0,1},{1,0},{2,3},{3,2},{4,5},{5,4},{6,7},{7,6},{8,9},{9,8},{10,11... | collective-permute-start | bytes 3145736 | tf_op jit(solution)/shard_map/ppermute | solution.py:424
  9.5 17.6 %collective-permute-start.5 = (bf16[512,1024]{1,0:T(8,128)(2,1)S(1)}, bf16[512,1024]{1,0:T(8,128)(2,1)S(1)}, u32[]{:S(2)}, u32[]{:S(2)}) collective-permute-start(bf16[512,1024]{1,0:T(8,128)(2,1)S(1)} %get-tuple-element.37), channel_id=1, source_target_pairs={{0,1},{1,0},{2,3},{3,2},{4,5},{5,4},{6,7},{7,6},{8,9},{9,8},{10,11... | collective-permute-start | bytes 3145736 | tf_op jit(solution)/shard_map/ppermute | solution.py:424
  9.6 4.6 %collective-permute-start.2 = (f32[8,512]{1,0:T(8,128)S(1)}, f32[8,512]{1,0:T(8,128)S(1)}, u32[]{:S(2)}, u32[]{:S(2)}) collective-permute-start(f32[8,512]{1,0:T(8,128)S(1)} %get-tuple-element.34.refs_0_), channel_id=1, source_target_pairs={{0,4},{4,0},{8,12},{12,8},{16,20},{20,16},{24,28},{28,24},{1,5},{5... | collective-permute-start | bytes 49160 | tf_op jit(solution)/shard_map/ppermute | solution.py:427
  14.2 3.8 %collective-permute-start.3 = (f32[8,512]{1,0:T(8,128)S(1)}, f32[8,512]{1,0:T(8,128)S(1)}, u32[]{:S(2)}, u32[]{:S(2)}) collective-permute-start(f32[8,512]{1,0:T(8,128)S(1)} %shard_map.74.refs_1_), channel_id=1, source_target_pairs={{0,8},{4,12},{8,0},{12,4},{16,24},{20,28},{24,16},{28,20},{1,9},{5... | collective-permute-start | bytes 49160 | tf_op jit(solution)/shard_map/ppermute | solution.py:427
  27.0 2.7 %collective-permute-start.6 = (bf16[512,1024]{1,0:T(8,128)(2,1)S(1)}, bf16[512,1024]{1,0:T(8,128)(2,1)S(1)}, u32[]{:S(2)}, u32[]{:S(2)}) collective-permute-start(bf16[512,1024]{1,0:T(8,128)(2,1)S(1)} %shard_map.76.refs_1_), channel_id=1, source_target_pairs={{0,1},{1,0},{2,3},{3,2},{4,5},{5,4},{6,7},{7,6},{8,9},{9,8},{10,11... | collective-permute-start | bytes 3145736 | tf_op jit(solution)/shard_map/ppermute | solution.py:424
  30.5 7.3 %collective-permute-start.9 = (bf16[128,512]{1,0:T(8,128)(2,1)S(1)}, bf16[128,512]{1,0:T(8,128)(2,1)S(1)}, u32[]{:S(2)}, u32[]{:S(2)}) collective-permute-start(bf16[128,512]{1,0:T(8,128)(2,1)S(1)} %get-tuple-element.55.refs_0_), channel_id=1, source_target_pairs={{0,12},{4,8},{8,4},{12,0},{16,28},{20,24},{24,20},{28,16},{1,13},{... | collective-permute-start | bytes 393224 | tf_op jit(solution)/shard_map/ppermute | solution.py:427
  33.3 6.8 %collective-permute-start.8 = (bf16[128,512]{1,0:T(8,128)(2,1)S(1)}, bf16[128,512]{1,0:T(8,128)(2,1)S(1)}, u32[]{:S(2)}, u32[]{:S(2)}) collective-permute-start(bf16[128,512]{1,0:T(8,128)(2,1)S(1)} %get-tuple-element.55.refs_0_), channel_id=1, source_target_pairs={{0,8},{4,12},{8,0},{12,4},{16,24},{20,28},{24,16},{28,20},{1,9},{5... | collective-permute-start | bytes 393224 | tf_op jit(solution)/shard_map/ppermute | solution.py:427
  33.8 6.3 %collective-permute-start.7 = (bf16[128,512]{1,0:T(8,128)(2,1)S(1)}, bf16[128,512]{1,0:T(8,128)(2,1)S(1)}, u32[]{:S(2)}, u32[]{:S(2)}) collective-permute-start(bf16[128,512]{1,0:T(8,128)(2,1)S(1)} %get-tuple-element.55.refs_0_), channel_id=1, source_target_pairs={{0,4},{4,0},{8,12},{12,8},{16,20},{20,16},{24,28},{28,24},{1,5},{5... | collective-permute-start | bytes 393224 | tf_op jit(solution)/shard_map/ppermute | solution.py:427
  40.3 8.7 %collective-permute-start.10 = (bf16[128,512]{1,0:T(8,128)(2,1)S(1)}, bf16[128,512]{1,0:T(8,128)(2,1)S(1)}, u32[]{:S(2)}, u32[]{:S(2)}) collective-permute-start(bf16[128,512]{1,0:T(8,128)(2,1)S(1)} %get-tuple-element.60), channel_id=1, source_target_pairs={{0,16},{4,20},{8,24},{12,28},{16,0},{20,4},{24,8},{28,12},{1,17},{... | collective-permute-start | bytes 393224 | tf_op jit(solution)/shard_map/ppermute | solution.py:427
  49.3 1.4 %collective-permute-start.11 = (bf16[128,512]{1,0:T(8,128)(2,1)S(1)}, bf16[128,512]{1,0:T(8,128)(2,1)S(1)}, u32[]{:S(2)}, u32[]{:S(2)}) collective-permute-start(bf16[128,512]{1,0:T(8,128)(2,1)S(1)} %shard_map.81.refs_0_), channel_id=1, source_target_pairs={{0,1},{1,0},{2,3},{3,2},{4,5},{5,4},{6,7},{7,6},{8,9},{9,8},{10,11... | collective-permute-start | bytes 393224 | tf_op jit(solution)/shard_map/ppermute | solution.py:424
  51.1 2.3 %collective-permute-start.12 = (bf16[384,512]{1,0:T(8,128)(2,1)S(1)}, bf16[384,512]{1,0:T(8,128)(2,1)S(1)}, u32[]{:S(2)}, u32[]{:S(2)}) collective-permute-start(bf16[384,512]{1,0:T(8,128)(2,1)S(1)} %shard_map.82.refs_0_.refs_1_), channel_id=1, source_target_pairs={{0,1},{1,0},{2,3},{3,2},{4,5},{5,4},{6,7},{7,6},{8,9},{9,8},{10,11... | collective-permute-start | bytes 1179656 | tf_op jit(solution)/shard_map/ppermute | solution.py:424
  51.8 9.2 %collective-permute-start.16 = (bf16[128,1024]{1,0:T(8,128)(2,1)S(1)}, bf16[128,1024]{1,0:T(8,128)(2,1)S(1)}, u32[]{:S(2)}, u32[]{:S(2)}) collective-permute-start(bf16[128,1024]{1,0:T(8,128)(2,1)S(1)} %shard_map.87), channel_id=1, source_target_pairs={{0,2},{1,3},{2,0},{3,1},{4,6},{5,7},{6,4},{7,5},{8,10},{9,11},{10,... | collective-permute-start | bytes 786440 | tf_op jit(solution)/shard_map/ppermute | solution.py:424
  54.0 12.7 %collective-permute-start.15 = (bf16[128,1024]{1,0:T(8,128)(2,1)S(1)}, bf16[128,1024]{1,0:T(8,128)(2,1)S(1)}, u32[]{:S(2)}, u32[]{:S(2)}) collective-permute-start(bf16[128,1024]{1,0:T(8,128)(2,1)S(1)} %shard_map.86), channel_id=1, source_target_pairs={{0,2},{1,3},{2,0},{3,1},{4,6},{5,7},{6,4},{7,5},{8,10},{9,11},{10,... | collective-permute-start | bytes 786440 | tf_op jit(solution)/shard_map/ppermute | solution.py:424
  55.5 16.7 %collective-permute-start.14 = (bf16[128,1024]{1,0:T(8,128)(2,1)S(1)}, bf16[128,1024]{1,0:T(8,128)(2,1)S(1)}, u32[]{:S(2)}, u32[]{:S(2)}) collective-permute-start(bf16[128,1024]{1,0:T(8,128)(2,1)S(1)} %shard_map.85), channel_id=1, source_target_pairs={{0,2},{1,3},{2,0},{3,1},{4,6},{5,7},{6,4},{7,5},{8,10},{9,11},{10,... | collective-permute-start | bytes 786440 | tf_op jit(solution)/shard_map/ppermute | solution.py:424
  57.1 20.2 %collective-permute-start.13 = (bf16[128,1024]{1,0:T(8,128)(2,1)S(1)}, bf16[128,1024]{1,0:T(8,128)(2,1)S(1)}, u32[]{:S(2)}, u32[]{:S(2)}) collective-permute-start(bf16[128,1024]{1,0:T(8,128)(2,1)S(1)} %shard_map.83.refs_6_), channel_id=1, source_target_pairs={{0,2},{1,3},{2,0},{3,1},{4,6},{5,7},{6,4},{7,5},{8,10},{9,11},{10,... | collective-permute-start | bytes 786440 | tf_op jit(solution)/shard_map/ppermute | solution.py:424

commit v6 on v5

--- a/solution.py
+++ b/solution.py
@@ -116,63 +116,13 @@
     return call(kernel, ins, [shape(total.shape, F32)] * 5, 0, smem=1)
 
 
-def pair_totals(total, other):
-    def kernel(t_ref, o_ref, out_ref):
-        out_ref[0:4, :] = t_ref[0:4, :]
-        out_ref[4:8, :] = o_ref[0:4, :]
-
-    return call(kernel, [total, other], [shape(total.shape, F32)], 0)[0]
-
-
-def link_four(slab, here, there):
-    def kernel(slab_ref, h_ref, t_ref, total_out, before_out, factors_out, span1_out, span2_out):
-        upper, above = upper_half(slab_ref, 0), upper_half(slab_ref, 1)
-        mine, beside = h_ref[0:1, :], h_ref[4:5, :]
-        across, diagonal = t_ref[0:1, :], t_ref[4:5, :]
-        own_pair, other_pair = mine + beside, across + diagonal
-        first = jnp.where(upper, beside, 0.0)
-        second = first + jnp.where(above, other_pair, 0.0)
-        own_scale = jnp.where(above, 0.0, other_pair)
-        other_scale = jnp.where(above, own_pair, 0.0)
-        by_mine = jnp.where(upper, 0.0, beside)
-        by_beside = jnp.where(upper, mine, 0.0)
-        by_across = jnp.where(upper, 0.0, diagonal)
-        by_diagonal = jnp.where(upper, across, 0.0)
-        factors_out[0:1, :] = jnp.exp(by_mine + own_scale)
-        factors_out[1:2, :] = jnp.exp(by_beside + own_scale)
-        factors_out[2:3, :] = jnp.exp(by_across + other_scale)
-        factors_out[3:4, :] = jnp.exp(by_diagonal + other_scale)
-        factors_out[4:5, :] = jnp.exp(by_across)
-        factors_out[5:6, :] = jnp.exp(by_diagonal)
-        factors_out[6:8, :] = jnp.zeros((2, h_ref.shape[1]), F32)
-        wide = h_ref.shape
-        total_out[...] = jnp.broadcast_to(own_pair + other_pair, wide)
-        before_out[...] = jnp.broadcast_to(second, wide)
-        span1_out[...] = jnp.broadcast_to(jnp.where(above, first, -jnp.inf), wide)
-        span2_out[...] = jnp.broadcast_to(jnp.where(upper_half(slab_ref, 2), second, -jnp.inf), wide)
-
-    return call(kernel, [slab, here, there], [shape(here.shape, F32)] * 5, 0, smem=1)
-
-
-def join_four(mine, beside, across, diagonal, factors):
-    def kernel(m_ref, b_ref, a_ref, d_ref, f_ref, four_ref, pair_ref):
-        m, b = m_ref[...].astype(F32), b_ref[...].astype(F32)
-        a, d = a_ref[...].astype(F32), d_ref[...].astype(F32)
-        f = [f_ref[i : i + 1, :] for i in range(6)]
-        four_ref[...] = (f[0] * m + f[1] * b + f[2] * a + f[3] * d).astype(BF16)
-        pair_ref[...] = (f[4] * a + f[5] * d).astype(BF16)
-
-    outs = [shape(mine.shape, BF16)] * 2
-    return call(kernel, [mine, beside, across, diagonal, factors], outs, 0)
-
-
-def combine(state, other, own_factor, other_factor):
+def combine(state, other, own_factor, other_factor, after):
     def kernel(s_ref, o_ref, a_ref, b_ref, out_ref):
         out_ref[...] = (
             a_ref[0:1, :] * s_ref[...].astype(F32) + b_ref[0:1, :] * o_ref[...].astype(F32)
         ).astype(BF16)
 
-    return call(kernel, [state, other, own_factor, other_factor], [shape(state.shape, BF16)], 0)[0]
+    return call(kernel, [state, other, own_factor, other_factor], [shape(state.shape, BF16)], 0, after)[0]
 
 
 def begin(me, slab, tokens, near, log_decay_rows, ws, w_out, head_size):
@@ -183,8 +133,8 @@
     block = w_out.shape[1] // 4
 
     def kernel(me_ref, slab_ref, t_ref, wq_ref, wk_ref, wv_ref, wl_ref, wo_ref, near_ref, decay_ref, *refs):
-        total_q, total_kv, total_l, far_q, far_kv, all_l = refs[:6]
-        decay_outs, blocks, (own_x, own_q, own_kv, sems) = refs[6:11], refs[11:15], refs[15:]
+        total_q, total_kv, total_l, far_q, far_kv, send_kv, all_l = refs[:7]
+        decay_outs, blocks, (own_x, own_q, own_kv, sems) = refs[7:12], refs[12:16], refs[16:]
 
         def pairs(i, q_dst, kv_dst):
             here = pl.ds(pl.multiple_of((me_ref[0] ^ i) * shard, 128), shard)
@@ -199,7 +149,7 @@
 
         moves = pairs(0, own_q.at[0], own_kv.at[0]) + [(wl_ref, all_l), (t_ref, own_x)]
         moves += pairs(1, own_q.at[1], own_kv.at[1])
-        moves += pairs(2, far_q.at[0], far_kv.at[0]) + pairs(3, far_q.at[1], far_kv.at[1])
+        moves += pairs(2, far_q.at[0], far_kv) + pairs(3, far_q.at[1], send_kv)
         moves += [(columns(i), blocks[i]) for i in range(4)]
         started = copies(moves, sems)
         decays(slab_ref, decay_ref, *decay_outs)
@@ -225,7 +175,8 @@
         shape((rows, 2 * kv_width), F32),
         shape((rows, wl.shape[0]), F32),
         shape((2, shard, q_width), BF16),
-        shape((2, shard, 2 * kv_width), BF16),
+        shape((shard, 2 * kv_width), BF16),
+        shape((shard, 2 * kv_width), BF16),
         shape(wl.shape, BF16),
         shape((heads, rows), F32),
         shape((rows, heads), F32),
@@ -241,34 +192,51 @@
     ]
     ins = [me, slab, tokens, wq, wk, wv, wl, w_out, near, log_decay_rows]
     outs = call(kernel, ins, outs, 0, smem=2, hbm=6, scratch=scratch, megabytes=14)
-    return outs[:3], outs[3:6], outs[6:11], outs[11:]
-
-
-def add_levels(me_ref, place, x_ref, wl_ref):
+    return outs[:3], outs[3:7], outs[7:12], outs[12:]
+
+
+def add_levels(me_ref, place, x, wl_ref):
     shard = wl_ref.shape[1] // 4
     start = pl.multiple_of((me_ref[0] ^ place) * shard, 128)
-    return dot_dims(x_ref[...], wl_ref[:, pl.ds(start, shard)], 1, 1)
-
-
-def project(me, place, x, ws, totals, after=()):
-    def kernel(me_ref, x_ref, q_ref, kv_ref, l_ref, *refs):
-        ins, outs = refs[:3], refs[3:]
-        outs[1][...] = ins[1][...] + dot(x_ref[...], kv_ref[place - 2])
-        outs[0][...] = ins[0][...] + dot(x_ref[...], q_ref[place - 2])
-        outs[2][...] = ins[2][...] + add_levels(me_ref, place, x_ref, l_ref)
-
-    outs = [shape(t.shape, F32) for t in totals]
-    return call(kernel, [me, x, *ws, *totals], outs, 0, after, smem=1, aliases={5: 0, 6: 1, 7: 2})
-
-
-def project_state(x, wkv, total_kv, keep, head_size):
+    return dot_dims(x, wl_ref[:, pl.ds(start, shard)], 1, 1)
+
+
+def project(me, place, x, wq, wl, total_q, total_l, after):
+    def kernel(me_ref, x_ref, wq_ref, wl_ref, q_ref, l_ref, q_out, l_out):
+        q_out[...] = q_ref[...] + dot(x_ref[...], wq_ref[place - 2])
+        l_out[...] = l_ref[...] + add_levels(me_ref, place, x_ref[...], wl_ref)
+
+    outs = [shape(t.shape, F32) for t in (total_q, total_l)]
+    flops = 2 * x.size * (total_q.shape[1] + total_l.shape[1])
+    return call(kernel, [me, x, wq, wl, total_q, total_l], outs, flops, after, smem=1, aliases={4: 0, 5: 1})
+
+
+def split(x, ways, after):
+    rows, columns = x.shape
+    part = columns // ways
+
+    def kernel(x_ref, *outs):
+        for i, o_ref in enumerate(outs):
+            o_ref[...] = x_ref[:, i * part : (i + 1) * part]
+
+    return call(kernel, [x], [shape((rows, part), x.dtype)] * ways, 0, after)
+
+
+def partial(x, w):
+    def kernel(x_ref, w_ref, o_ref):
+        o_ref[...] = dot(x_ref[...], w_ref[...]).astype(BF16)
+
+    return call(kernel, [x, w], [shape((x.shape[0], w.shape[1]), BF16)], 0)[0]
+
+
+def project_state(x, wkv, total_kv, from_near, keep, head_size):
     rows = x.shape[0]
     heads = keep.shape[1]
-    kv_width = wkv.shape[2] // 2
+    kv_width = wkv.shape[1] // 2
     group = heads // (kv_width // head_size)
 
-    def kernel(x_ref, w_ref, total_ref, keep_ref, k_out, v_out, s_out):
-        total = total_ref[...] + dot(x_ref[...], w_ref[1])
+    def kernel(x_ref, w_ref, total_ref, near_ref, keep_ref, k_out, v_out, s_out):
+        total = total_ref[...] + near_ref[...].astype(F32) + dot(x_ref[...], w_ref[...])
         keys = total[:, :kv_width].astype(BF16)
         values = total[:, kv_width:].astype(BF16)
         k_out[...] = keys
@@ -288,23 +256,25 @@
         shape((rows, kv_width), BF16),
         shape((head_size, heads * head_size), BF16),
     ]
-    return call(kernel, [x, wkv, total_kv, keep], outs, 0)
-
-
-def attend(me, place, x, wq, wl, total_q, total_l, k, v, dcol, drow, spans, states, head_size, level_count):
+    return call(kernel, [x, wkv, total_kv, from_near, keep], outs, 0)
+
+
+def attend(me, place, xs, wq, wl, total_q, total_l, k, v, dcol, drow, spans, states, head_size, level_count):
     rows, width = total_q.shape
     bits = len(spans)
     heads = width // head_size
     group = heads // (k.shape[1] // head_size)
     own_levels = level_count - bits
 
-    def kernel(me_ref, x_ref, *refs):
+    def kernel(me_ref, *refs):
+        x = jnp.concatenate([x_ref[...] for x_ref in refs[: len(xs)]], axis=1)
+        refs = refs[len(xs) :]
         wq_ref, wl_ref, tq_ref, tl_ref, k_ref, v_ref, dcol_ref, drow_ref = refs[:8]
         span_refs, state_refs = refs[8 : 8 + bits], refs[8 + bits : 7 + 2 * bits]
         o_ref, s_ref, q_ref, l_ref = refs[-4:]
-        raw = tl_ref[...] + add_levels(me_ref, place, x_ref, wl_ref)
+        raw = tl_ref[...] + add_levels(me_ref, place, x, wl_ref)
         l_ref[...] = jnp.maximum(raw, 0.0) + jnp.log1p(jnp.exp(-jnp.abs(raw)))
-        q_ref[...] = (tq_ref[...] + dot(x_ref[...], wq_ref[place - 2])).astype(BF16)
+        q_ref[...] = (tq_ref[...] + dot(x, wq_ref[place - 2])).astype(BF16)
         row_id = lax.broadcasted_iota(jnp.int32, (BLOCK, BLOCK), 0)
         col_id = lax.broadcasted_iota(jnp.int32, (BLOCK, BLOCK), 1)
         causal = row_id >= col_id
@@ -346,10 +316,10 @@
                         total = total + dot_dims(scaled, state_refs[b][:, cols], 1, 1)
                 o_ref[here, cols] = total
 
-    ins = [me, x, wq, wl, total_q, total_l, k, v, dcol, drow, *spans, *states]
+    ins = [me, *xs, wq, wl, total_q, total_l, k, v, dcol, drow, *spans, *states]
     wide = shape((rows, width), BF16)
     outs = [shape((rows, width), F32), wide, wide, shape(total_l.shape, F32)]
-    flops = 2 * rows * x.shape[1] * width + 4 * rows * rows * width
+    flops = 2 * rows * wq.shape[1] * width + 4 * rows * rows * width
     return call(kernel, ins, outs, flops, smem=1)[:2]
 
 
@@ -436,28 +406,28 @@
     w_here_own, w_here_send, w_far_own, w_far_send = blocks
     w_here, w_far = swap_tp(w_here_send, 1), swap_tp(w_far_send, 1)
 
-    here = pair_totals(total, swap_seq(total, 1))
-    group_total, before, four_factors, *later_spans = link_four(slab, here, swap_seq(here, 2))
-    spans, factors = [span, *later_spans], []
-    for b in range(2, seq_bits - 1):
-        group_total, before, own, other, span = link(slab, b, group_total, swap_seq(group_total, 1 << b), before)
+    spans, factors, before = [span], [], None
+    for b in range(seq_bits - 1):
+        total, before, own, other, span = link(slab, b, total, swap_seq(total, 1 << b), before)
         spans.append(span)
         factors.append((own, other))
 
-    wq, wkv, wl = ws
-    arrived = gate(far, group_total, w_far, w_here)
-    arrived_near = swap_tp(arrived, 1)
-    total_q, total_kv, total_l = project(me, 2, arrived, ws, totals)
-    k, v, state = project_state(arrived_near, wkv, total_kv, keep, head_size)
-
-    beside, across, diagonal = (swap_seq(state, bits) for bits in (1, 2, 3))
-    state, other_pair = join_four(state, beside, across, diagonal, four_factors)
-    earlier = [beside, other_pair]
-    for b in range(2, seq_bits):
+    wq, wkv, wkv_send, wl = ws
+    wkv_near = swap_tp(wkv_send, 1)
+    arrived = gate(far, total, w_far, w_here)
+    from_near = swap_tp(partial(arrived, wkv_near), 1)
+    total_q, total_kv, total_l = totals
+    k, v, state = project_state(arrived, wkv, total_kv, from_near, keep, head_size)
+    total_q, total_l = project(me, 2, arrived, wq, wl, total_q, total_l, (k,))
+    arrived_near = [swap_tp(x, 1) for x in split(arrived, 4, (total_l,))]
+
+    earlier = []
+    for b in range(seq_bits):
         other = swap_seq(state, 1 << b)
         earlier.append(other)
         if b < seq_bits - 1:
-            state = combine(state, other, *factors[b - 2])
+            after = () if b else (total_l,)
+            state = combine(state, other, *factors[b], after)
 
     local, scaled = attend(
         me, 3, arrived_near, wq, wl, total_q, total_l, k, v, dcol, drow, spans, earlier[:-1], head_size, level_count
@@ -466,9 +436,9 @@
     step = rows // 4
     own = finish(local, scaled, earlier[-1], slice(0, step), head_size)
     near_own = swap_tp(own, 1)
-    rest = finish(local, scaled, earlier[-1], slice(step, rows), head_size, (near_own,))
+    crossing = [out_block([own], [near_own], [slice(0, step)], w_far_own, w_far, BF16)]
+    rest = finish(local, scaled, earlier[-1], slice(step, rows), head_size, (crossing[0],))
     near_rest = swap_tp(rest, 1)
-    crossing = [out_block([own], [near_own], [slice(0, step)], w_far_own, w_far, BF16)]
     for r in range(0, rows - step, step):
         crossing.append(out_block([rest], [near_rest], [slice(r, r + step)], w_far_own, w_far, BF16))
     both = [slice(0, step), slice(0, rows - step)]

time: 78.3 us -> 77.4 us (0.989)
  waiting for transfers between devices: 38.2 us -> 34.9 us
  starting transfers between devices: 19.9 us -> 22 us
    ppermute x6 -> x5, waiting for transfers between devices: 11.5 us -> 8.77 us  [swap_seq(): return lax.ppermute(x, 'seq', [(i, i ^ bit) for i in range(seq_size)])]
    ppermute x11 -> x16, starting transfers between devices: 8.77 us -> 10.7 us  [swap_tp(): return lax.ppermute(x, 'tp', [(i, i ^ bit) for i in range(4)])]
    ppermute x11 -> x16, waiting for transfers between devices: 26.7 us -> 26.1 us  [swap_tp(): return lax.ppermute(x, 'tp', [(i, i ^ bit) for i in range(4)])]
    pallas_call x14 -> x17, Pallas kernels: 16.2 us -> 16.4 us  [call(): pl.pallas_call(run, in_specs=[SMEM] * smem + [HBM] * hbm + [VMEM] * (coun...]
    ppermute x6 -> x5, starting transfers between devices: 11.1 us -> 11.3 us  [swap_seq(): return lax.ppermute(x, 'seq', [(i, i ^ bit) for i in range(seq_size)])]
  transfers between devices with their start and end apart: 17 -> 21, of which waited for: 12 -> 12; matrix products, arithmetic and copies ran while one was open for 0% -> 0% of each run, Pallas kernels for 21% -> 21%
where the time goes in v6:
time: 77.4 us; the launch traced here: 77.2 us
  waiting for transfers between devices  34.9 us (45%)
  starting transfers between devices  22 us (28%)
  Pallas kernels  19.4 us (25%)
    ppermute x16, waiting for transfers between devices, swap_tp(): return lax.ppermute(x, 'tp', [(i, i ^ bit) for i in range(4)])  26.1 us
    pallas_call x17, Pallas kernels, call(): pl.pallas_call(run, in_specs=[SMEM] * smem + [HBM] * hbm + [VMEM] * (coun...  16.4 us
    ppermute x5, starting transfers between devices, swap_seq(): return lax.ppermute(x, 'seq', [(i, i ^ bit) for i in range(seq_size)])  11.3 us
    ppermute x16, starting transfers between devices, swap_tp(): return lax.ppermute(x, 'tp', [(i, i ^ bit) for i in range(4)])  10.7 us
    ppermute x5, waiting for transfers between devices, swap_seq(): return lax.ppermute(x, 'seq', [(i, i ^ bit) for i in range(seq_size)])  8.77 us
    pallas_call x4, Pallas kernels, add_rows(): pl.pallas_call(kernel, grid=(1,), in_specs=specs, out_specs=pl.BlockSpec(...  3.03 us
  transfers between devices with their start and end apart: 21, of which 12 were waited for; matrix products, arithmetic and copies ran while one was open for 0% of the time, Pallas kernels for 21%

profile of v6, /device:TPU:0, one launch (start us, length us, event | category | flops | bytes accessed | tf_op | source)
XLA Modules:
  0.0 77.2 jit_solution(358592226091167507)
XLA Ops:
  0.5 2.5 %collective-permute-start = (bf16[512,1024]{1,0:T(8,128)(2,1)}, bf16[512,1024]{1,0:T(8,128)(2,1)S(1)}, u32[]{:S(2)}, u32[]{:S(2)}) collective-permute-start(bf16[512,1024]{1,0:T(8,128)(2,1)} %refs_2_.1), channel_id=1, source_target_pairs={{0,2},{1,3},{2,0},{3,1},{4,6},{5,7},{6,4},{7,5},{8,10},{9,11},{10,... | collective-permute-start | bytes 3145736 | tf_op jit(solution)/shard_map/ppermute | solution.py:394
  3.7 5.4 %shard_map.73 = (f32[512,512]{1,0:T(8,128)S(1)}, f32[512,256]{1,0:T(8,128)S(1)}, f32[512,24]{1,0:T(8,128)S(1)}, bf16[2,1024,512]{2,1,0:T(8,128)(2,1)S(1)}, bf16[...) custom-call(s32[1]{0:T(128)} %bitcast.refs_0_, ...), custom_call_target="tpu_custom_call" | custom-call | tf_op jit(solution)/shard_map/pallas_call | solution.py:41
  10.0 2.6 %collective-permute-start.2 = (f32[8,512]{1,0:T(8,128)S(1)}, f32[8,512]{1,0:T(8,128)S(1)}, u32[]{:S(2)}, u32[]{:S(2)}) collective-permute-start(f32[8,512]{1,0:T(8,128)S(1)} %get-tuple-element.41.refs_1_), channel_id=1, source_target_pairs={{0,4},{4,0},{8,12},{12,8},{16,20},{20,16},{24,28},{28,24},{1,5},{5... | collective-permute-start | bytes 49160 | tf_op jit(solution)/shard_map/ppermute | solution.py:397
  12.6 1.7 %collective-permute-done.2.refs_2_ = f32[8,512]{1,0:T(8,128)S(1)} collective-permute-done((f32[8,512]{1,0:T(8,128)S(1)}, f32[8,512]{1,0:T(8,128)S(1)}, u32[]{:S(2)}, u32[]{:S(2)}) %collective-permute-start.2) | collective-permute-done | bytes 16416 | tf_op jit(solution)/shard_map/ppermute | solution.py:397
  14.3 2.2 %collective-permute-start.3 = (f32[8,512]{1,0:T(8,128)S(1)}, f32[8,512]{1,0:T(8,128)S(1)}, u32[]{:S(2)}, u32[]{:S(2)}) collective-permute-start(f32[8,512]{1,0:T(8,128)S(1)} %get-tuple-element.42.refs_1_), channel_id=1, source_target_pairs={{0,8},{4,12},{8,0},{12,4},{16,24},{20,28},{24,16},{28,20},{1,9},{5... | collective-permute-start | bytes 49160 | tf_op jit(solution)/shard_map/ppermute | solution.py:397
  16.5 1.7 %collective-permute-done.3.refs_2_ = f32[8,512]{1,0:T(8,128)S(1)} collective-permute-done((f32[8,512]{1,0:T(8,128)S(1)}, f32[8,512]{1,0:T(8,128)S(1)}, u32[]{:S(2)}, u32[]{:S(2)}) %collective-permute-start.3) | collective-permute-done | bytes 16416 | tf_op jit(solution)/shard_map/ppermute | solution.py:397
  18.8 8.2 %collective-permute-done.refs_0_ = bf16[512,1024]{1,0:T(8,128)(2,1)S(1)} collective-permute-done((bf16[512,1024]{1,0:T(8,128)(2,1)}, bf16[512,1024]{1,0:T(8,128)(2,1)S(1)}, u32[]{:S(2)}, u32[]{:S(2)}) %collective-permute-start) | collective-permute-done | bytes 1048608 | tf_op jit(solution)/shard_map/ppermute | solution.py:394
  27.5 1.5 %collective-permute-done.7.refs_3_ = bf16[512,256]{1,0:T(8,128)(2,1)S(1)} collective-permute-done((bf16[512,256]{1,0:T(8,128)(2,1)S(1)}, bf16[512,256]{1,0:T(8,128)(2,1)S(1)}, u32[]{:S(2)}, u32[]{:S(2)}) %collective-permute-start.7) | collective-permute-done | bytes 262176 | tf_op jit(solution)/shard_map/ppermute | solution.py:394
  29.9 1.8 %collective-permute-start.12 = (bf16[128,512]{1,0:T(8,128)(2,1)S(1)}, bf16[128,512]{1,0:T(8,128)(2,1)S(1)}, u32[]{:S(2)}, u32[]{:S(2)}) collective-permute-start(bf16[128,512]{1,0:T(8,128)(2,1)S(1)} %get-tuple-element.68.refs_0_), channel_id=1, source_target_pairs={{0,4},{4,0},{8,12},{12,8},{16,20},{20,16},{24,28},{28,24},{1,5},{5... | collective-permute-start | bytes 393224 | tf_op jit(solution)/shard_map/ppermute | solution.py:397
  31.6 1.1 %shard_map.79 = (f32[512,512]{1,0:T(8,128)S(1)}, f32[512,24]{1,0:T(8,128)S(1)}) custom-call(s32[1]{0:T(128)} %bitcast.refs_0_, bf16[512,1024]{1,0:T(8,128)(2,1)S(1)} %shard_map.76.refs_0_.refs_1_, bf16[2,1024,512]{2,1,0:T(8,128)(2,1)S(1)} %get-tuple-element.47.refs_2_.refs_5_, ...), custom_call_target="tpu_custom_call", output_to_operand_aliasing={{0}: (4, {}), {1}: (5, {})} | custom-call | flops 562036736 | bytes 5537796 | tf_op jit(solution)/shard_map/pallas_call | solution.py:41
  33.9 1.6 %collective-permute-done.12.refs_1_.refs_16_ = bf16[128,512]{1,0:T(8,128)(2,1)S(1)} collective-permute-done((bf16[128,512]{1,0:T(8,128)(2,1)S(1)}, bf16[128,512]{1,0:T(8,128)(2,1)S(1)}, u32[]{:S(2)}, u32[]{:S(2)}) %collective-permute-start.12) | collective-permute-done | bytes 131104 | tf_op jit(solution)/shard_map/ppermute | solution.py:397
  35.5 1.9 %collective-permute-start.13 = (bf16[128,512]{1,0:T(8,128)(2,1)S(1)}, bf16[128,512]{1,0:T(8,128)(2,1)S(1)}, u32[]{:S(2)}, u32[]{:S(2)}) collective-permute-start(bf16[128,512]{1,0:T(8,128)(2,1)S(1)} %shard_map.81.refs_0_), channel_id=1, source_target_pairs={{0,8},{4,12},{8,0},{12,4},{16,24},{20,28},{24,16},{28,20},{1,9},{5... | collective-permute-start | bytes 393224 | tf_op jit(solution)/shard_map/ppermute | solution.py:397
  37.4 3.2 %collective-permute-done.13.refs_17_.refs_1_ = bf16[128,512]{1,0:T(8,128)(2,1)S(1)} collective-permute-done((bf16[128,512]{1,0:T(8,128)(2,1)S(1)}, bf16[128,512]{1,0:T(8,128)(2,1)S(1)}, u32[]{:S(2)}, u32[]{:S(2)}) %collective-permute-start.13) | collective-permute-done | bytes 131104 | tf_op jit(solution)/shard_map/ppermute | solution.py:397
  40.6 2.9 %collective-permute-start.14 = (bf16[128,512]{1,0:T(8,128)(2,1)S(1)}, bf16[128,512]{1,0:T(8,128)(2,1)S(1)}, u32[]{:S(2)}, u32[]{:S(2)}) collective-permute-start(bf16[128,512]{1,0:T(8,128)(2,1)S(1)} %shard_map.83), channel_id=1, source_target_pairs={{0,16},{4,20},{8,24},{12,28},{16,0},{20,4},{24,8},{28,12},{1,17},{... | collective-permute-start | bytes 393224 | tf_op jit(solution)/shard_map/ppermute | solution.py:397
  43.5 4.0 %shard_map.82 = (f32[512,512]{1,0:T(8,128)S(1)}, bf16[512,512]{1,0:T(8,128)(2,1)S(1)}, bf16[512,512]{1,0:T(8,128)(2,1)}, f32[512,24]{1,0:T(8,128)}) custom-call(s32[1]{0:T(128)} %bitcast.refs_0_, bf16[512,256]{1,0:T(8,128)(2,1)S(1)} %collective-permute-done.8.refs_1_, bf16[512,256]{1,0:T(8,128)(2,1)S(1)} %collective-permute-done.9.refs_2_, ...), custom_call_target="tpu_custom_call" | custom-call | flops 1073741824 | bytes 7176196 | tf_op jit(solution)/shard_map/pallas_call | solution.py:41
  48.5 1.3 %collective-permute-done.15.refs_1_.refs_2_ = bf16[128,512]{1,0:T(8,128)(2,1)S(1)} collective-permute-done((bf16[128,512]{1,0:T(8,128)(2,1)S(1)}, bf16[128,512]{1,0:T(8,128)(2,1)S(1)}, u32[]{:S(2)}, u32[]{:S(2)}) %collective-permute-start.15) | collective-permute-done | bytes 131104 | tf_op jit(solution)/shard_map/ppermute | solution.py:394
  51.0 1.6 %collective-permute-start.20 = (bf16[128,1024]{1,0:T(8,128)(2,1)S(1)}, bf16[128,1024]{1,0:T(8,128)(2,1)S(1)}, u32[]{:S(2)}, u32[]{:S(2)}) collective-permute-start(bf16[128,1024]{1,0:T(8,128)(2,1)S(1)} %shard_map.85.refs_3_), channel_id=1, source_target_pairs={{0,2},{1,3},{2,0},{3,1},{4,6},{5,7},{6,4},{7,5},{8,10},{9,11},{10,... | collective-permute-start | bytes 786440 | tf_op jit(solution)/shard_map/ppermute | solution.py:394
  53.1 1.6 %collective-permute-start.19 = (bf16[128,1024]{1,0:T(8,128)(2,1)S(1)}, bf16[128,1024]{1,0:T(8,128)(2,1)S(1)}, u32[]{:S(2)}, u32[]{:S(2)}) collective-permute-start(bf16[128,1024]{1,0:T(8,128)(2,1)S(1)} %shard_map.90), channel_id=1, source_target_pairs={{0,2},{1,3},{2,0},{3,1},{4,6},{5,7},{6,4},{7,5},{8,10},{9,11},{10,... | collective-permute-start | bytes 786440 | tf_op jit(solution)/shard_map/ppermute | solution.py:394
  56.2 1.6 %collective-permute-start.17 = (bf16[128,1024]{1,0:T(8,128)(2,1)S(1)}, bf16[128,1024]{1,0:T(8,128)(2,1)S(1)}, u32[]{:S(2)}, u32[]{:S(2)}) collective-permute-start(bf16[128,1024]{1,0:T(8,128)(2,1)S(1)} %shard_map.87.refs_6_), channel_id=1, source_target_pairs={{0,2},{1,3},{2,0},{3,1},{4,6},{5,7},{6,4},{7,5},{8,10},{9,11},{10,... | collective-permute-start | bytes 786440 | tf_op jit(solution)/shard_map/ppermute | solution.py:394
  57.8 1.3 %shard_map.88.h_ref = f32[512,1024]{1,0:T(8,128)S(1)} custom-call(bf16[128,512]{1,0:T(8,128)(2,1)S(1)} %shard_map.84.refs_0_, bf16[384,512]{1,0:T(8,128)(2,1)S(1)} %shard_map.86.refs_0_.refs_1_, bf16[128,512]{1,0:T(8,128)(2,1)S(1)} %collective-permute-done.15.refs_1_.refs_2_, bf16[384,512]{1,0:T(8,128)(2,1)S(1)} %collective-permute-done.16.refs_1_.refs_3_, ...), custom_call_target="tpu_custom_call" | custom-call | tf_op jit(solution)/shard_map/pallas_call | solution.py:41
  59.1 1.1 %collective-permute-done.20.a_ref = bf16[128,1024]{1,0:T(8,128)(2,1)S(1)} collective-permute-done((bf16[128,1024]{1,0:T(8,128)(2,1)S(1)}, bf16[128,1024]{1,0:T(8,128)(2,1)S(1)}, u32[]{:S(2)}, u32[]{:S(2)}) %collective-permute-start.20) | collective-permute-done | bytes 262176 | tf_op jit(solution)/shard_map/ppermute | solution.py:394
  60.9 4.9 %collective-permute-done.19.a_ref = bf16[128,1024]{1,0:T(8,128)(2,1)S(1)} collective-permute-done((bf16[128,1024]{1,0:T(8,128)(2,1)S(1)}, bf16[128,1024]{1,0:T(8,128)(2,1)S(1)}, u32[]{:S(2)}, u32[]{:S(2)}) %collective-permute-start.19) | collective-permute-done | bytes 262176 | tf_op jit(solution)/shard_map/ppermute | solution.py:394
  66.5 4.9 %collective-permute-done.18.a_ref = bf16[128,1024]{1,0:T(8,128)(2,1)S(1)} collective-permute-done((bf16[128,1024]{1,0:T(8,128)(2,1)S(1)}, bf16[128,1024]{1,0:T(8,128)(2,1)S(1)}, u32[]{:S(2)}, u32[]{:S(2)}) %collective-permute-start.18) | collective-permute-done | bytes 262176 | tf_op jit(solution)/shard_map/ppermute | solution.py:394
  72.1 4.3 %collective-permute-done.17.a_ref = bf16[128,1024]{1,0:T(8,128)(2,1)S(1)} collective-permute-done((bf16[128,1024]{1,0:T(8,128)(2,1)S(1)}, bf16[128,1024]{1,0:T(8,128)(2,1)S(1)}, u32[]{:S(2)}, u32[]{:S(2)}) %collective-permute-start.17) | collective-permute-done | bytes 262176 | tf_op jit(solution)/shard_map/ppermute | solution.py:394
  (42 shorter events, 12.4 us)
Async XLA Ops:
  0.0 3.0 %collective-permute-start.1 = (bf16[512,1024]{1,0:T(8,128)(2,1)}, bf16[512,1024]{1,0:T(8,128)(2,1)S(1)}, u32[]{:S(2)}, u32[]{:S(2)}) collective-permute-start(bf16[512,1024]{1,0:T(8,128)(2,1)} %refs_2_.1), channel_id=1, source_target_pairs={{0,1},{1,0},{2,3},{3,2},{4,5},{5,4},{6,7},{7,6},{8,9},{9,8},{10,11... | collective-permute-start | bytes 3145736 | tf_op jit(solution)/shard_map/ppermute | solution.py:394
  0.5 26.6 %collective-permute-start = (bf16[512,1024]{1,0:T(8,128)(2,1)}, bf16[512,1024]{1,0:T(8,128)(2,1)S(1)}, u32[]{:S(2)}, u32[]{:S(2)}) collective-permute-start(bf16[512,1024]{1,0:T(8,128)(2,1)} %refs_2_.1), channel_id=1, source_target_pairs={{0,2},{1,3},{2,0},{3,1},{4,6},{5,7},{6,4},{7,5},{8,10},{9,11},{10,... | collective-permute-start | bytes 3145736 | tf_op jit(solution)/shard_map/ppermute | solution.py:394
  3.0 0.7 copy-start
  9.0 18.0 %collective-permute-start.4 = (bf16[512,1024]{1,0:T(8,128)(2,1)S(1)}, bf16[512,1024]{1,0:T(8,128)(2,1)S(1)}, u32[]{:S(2)}, u32[]{:S(2)}) collective-permute-start(bf16[512,1024]{1,0:T(8,128)(2,1)S(1)} %get-tuple-element.45), channel_id=1, source_target_pairs={{0,1},{1,0},{2,3},{3,2},{4,5},{5,4},{6,7},{7,6},{8,9},{9,8},{10,11... | collective-permute-start | bytes 3145736 | tf_op jit(solution)/shard_map/ppermute | solution.py:394
  9.5 17.6 %collective-permute-start.5 = (bf16[512,1024]{1,0:T(8,128)(2,1)S(1)}, bf16[512,1024]{1,0:T(8,128)(2,1)S(1)}, u32[]{:S(2)}, u32[]{:S(2)}) collective-permute-start(bf16[512,1024]{1,0:T(8,128)(2,1)S(1)} %get-tuple-element.46), channel_id=1, source_target_pairs={{0,1},{1,0},{2,3},{3,2},{4,5},{5,4},{6,7},{7,6},{8,9},{9,8},{10,11... | collective-permute-start | bytes 3145736 | tf_op jit(solution)/shard_map/ppermute | solution.py:394
  9.6 17.4 %collective-permute-start.6 = (bf16[1024,256]{1,0:T(8,128)(2,1)S(1)}, bf16[1024,256]{1,0:T(8,128)(2,1)S(1)}, u32[]{:S(2)}, u32[]{:S(2)}) collective-permute-start(bf16[1024,256]{1,0:T(8,128)(2,1)S(1)} %get-tuple-element.53), channel_id=1, source_target_pairs={{0,1},{1,0},{2,3},{3,2},{4,5},{5,4},{6,7},{7,6},{8,9},{9,8},{10,11... | collective-permute-start | bytes 1572872 | tf_op jit(solution)/shard_map/ppermute | solution.py:394
  10.0 4.3 %collective-permute-start.2 = (f32[8,512]{1,0:T(8,128)S(1)}, f32[8,512]{1,0:T(8,128)S(1)}, u32[]{:S(2)}, u32[]{:S(2)}) collective-permute-start(f32[8,512]{1,0:T(8,128)S(1)} %get-tuple-element.41.refs_1_), channel_id=1, source_target_pairs={{0,4},{4,0},{8,12},{12,8},{16,20},{20,16},{24,28},{28,24},{1,5},{5... | collective-permute-start | bytes 49160 | tf_op jit(solution)/shard_map/ppermute | solution.py:397
  14.3 3.9 %collective-permute-start.3 = (f32[8,512]{1,0:T(8,128)S(1)}, f32[8,512]{1,0:T(8,128)S(1)}, u32[]{:S(2)}, u32[]{:S(2)}) collective-permute-start(f32[8,512]{1,0:T(8,128)S(1)} %get-tuple-element.42.refs_1_), channel_id=1, source_target_pairs={{0,8},{4,12},{8,0},{12,4},{16,24},{20,28},{24,16},{28,20},{1,9},{5... | collective-permute-start | bytes 49160 | tf_op jit(solution)/shard_map/ppermute | solution.py:397
  27.5 1.6 %collective-permute-start.7 = (bf16[512,256]{1,0:T(8,128)(2,1)S(1)}, bf16[512,256]{1,0:T(8,128)(2,1)S(1)}, u32[]{:S(2)}, u32[]{:S(2)}) collective-permute-start(bf16[512,256]{1,0:T(8,128)(2,1)S(1)} %shard_map.77), channel_id=1, source_target_pairs={{0,1},{1,0},{2,3},{3,2},{4,5},{5,4},{6,7},{7,6},{8,9},{9,8},{10,11... | collective-permute-start | bytes 786440 | tf_op jit(solution)/shard_map/ppermute | solution.py:394
  29.9 5.6 %collective-permute-start.12 = (bf16[128,512]{1,0:T(8,128)(2,1)S(1)}, bf16[128,512]{1,0:T(8,128)(2,1)S(1)}, u32[]{:S(2)}, u32[]{:S(2)}) collective-permute-start(bf16[128,512]{1,0:T(8,128)(2,1)S(1)} %get-tuple-element.68.refs_0_), channel_id=1, source_target_pairs={{0,4},{4,0},{8,12},{12,8},{16,20},{20,16},{24,28},{28,24},{1,5},{5... | collective-permute-start | bytes 393224 | tf_op jit(solution)/shard_map/ppermute | solution.py:397
  32.8 10.7 %collective-permute-start.8 = (bf16[512,256]{1,0:T(8,128)(2,1)S(1)}, bf16[512,256]{1,0:T(8,128)(2,1)S(1)}, u32[]{:S(2)}, u32[]{:S(2)}) collective-permute-start(bf16[512,256]{1,0:T(8,128)(2,1)S(1)} %get-tuple-element.57), channel_id=1, source_target_pairs={{0,1},{1,0},{2,3},{3,2},{4,5},{5,4},{6,7},{7,6},{8,9},{9,8},{10,11... | collective-permute-start | bytes 786440 | tf_op jit(solution)/shard_map/ppermute | solution.py:394
  32.9 10.6 %collective-permute-start.9 = (bf16[512,256]{1,0:T(8,128)(2,1)S(1)}, bf16[512,256]{1,0:T(8,128)(2,1)S(1)}, u32[]{:S(2)}, u32[]{:S(2)}) collective-permute-start(bf16[512,256]{1,0:T(8,128)(2,1)S(1)} %get-tuple-element.58), channel_id=1, source_target_pairs={{0,1},{1,0},{2,3},{3,2},{4,5},{5,4},{6,7},{7,6},{8,9},{9,8},{10,11... | collective-permute-start | bytes 786440 | tf_op jit(solution)/shard_map/ppermute | solution.py:394
  33.4 10.1 %collective-permute-start.10 = (bf16[512,256]{1,0:T(8,128)(2,1)S(1)}, bf16[512,256]{1,0:T(8,128)(2,1)S(1)}, u32[]{:S(2)}, u32[]{:S(2)}) collective-permute-start(bf16[512,256]{1,0:T(8,128)(2,1)S(1)} %get-tuple-element.59), channel_id=1, source_target_pairs={{0,1},{1,0},{2,3},{3,2},{4,5},{5,4},{6,7},{7,6},{8,9},{9,8},{10,11... | collective-permute-start | bytes 786440 | tf_op jit(solution)/shard_map/ppermute | solution.py:394
  33.5 10.0 %collective-permute-start.11 = (bf16[512,256]{1,0:T(8,128)(2,1)S(1)}, bf16[512,256]{1,0:T(8,128)(2,1)S(1)}, u32[]{:S(2)}, u32[]{:S(2)}) collective-permute-start(bf16[512,256]{1,0:T(8,128)(2,1)S(1)} %get-tuple-element.60), channel_id=1, source_target_pairs={{0,1},{1,0},{2,3},{3,2},{4,5},{5,4},{6,7},{7,6},{8,9},{9,8},{10,11... | collective-permute-start | bytes 786440 | tf_op jit(solution)/shard_map/ppermute | solution.py:394
  35.5 5.0 %collective-permute-start.13 = (bf16[128,512]{1,0:T(8,128)(2,1)S(1)}, bf16[128,512]{1,0:T(8,128)(2,1)S(1)}, u32[]{:S(2)}, u32[]{:S(2)}) collective-permute-start(bf16[128,512]{1,0:T(8,128)(2,1)S(1)} %shard_map.81.refs_0_), channel_id=1, source_target_pairs={{0,8},{4,12},{8,0},{12,4},{16,24},{20,28},{24,16},{28,20},{1,9},{5... | collective-permute-start | bytes 393224 | tf_op jit(solution)/shard_map/ppermute | solution.py:397
  40.6 7.5 %collective-permute-start.14 = (bf16[128,512]{1,0:T(8,128)(2,1)S(1)}, bf16[128,512]{1,0:T(8,128)(2,1)S(1)}, u32[]{:S(2)}, u32[]{:S(2)}) collective-permute-start(bf16[128,512]{1,0:T(8,128)(2,1)S(1)} %shard_map.83), channel_id=1, source_target_pairs={{0,16},{4,20},{8,24},{12,28},{16,0},{20,4},{24,8},{28,12},{1,17},{... | collective-permute-start | bytes 393224 | tf_op jit(solution)/shard_map/ppermute | solution.py:397
  48.4 1.4 %collective-permute-start.15 = (bf16[128,512]{1,0:T(8,128)(2,1)S(1)}, bf16[128,512]{1,0:T(8,128)(2,1)S(1)}, u32[]{:S(2)}, u32[]{:S(2)}) collective-permute-start(bf16[128,512]{1,0:T(8,128)(2,1)S(1)} %shard_map.84.refs_0_), channel_id=1, source_target_pairs={{0,1},{1,0},{2,3},{3,2},{4,5},{5,4},{6,7},{7,6},{8,9},{9,8},{10,11... | collective-permute-start | bytes 393224 | tf_op jit(solution)/shard_map/ppermute | solution.py:394
  50.8 1.8 %collective-permute-start.16 = (bf16[384,512]{1,0:T(8,128)(2,1)S(1)}, bf16[384,512]{1,0:T(8,128)(2,1)S(1)}, u32[]{:S(2)}, u32[]{:S(2)}) collective-permute-start(bf16[384,512]{1,0:T(8,128)(2,1)S(1)} %shard_map.86.refs_0_.refs_1_), channel_id=1, source_target_pairs={{0,1},{1,0},{2,3},{3,2},{4,5},{5,4},{6,7},{7,6},{8,9},{9,8},{10,11... | collective-permute-start | bytes 1179656 | tf_op jit(solution)/shard_map/ppermute | solution.py:394
  51.0 9.1 %collective-permute-start.20 = (bf16[128,1024]{1,0:T(8,128)(2,1)S(1)}, bf16[128,1024]{1,0:T(8,128)(2,1)S(1)}, u32[]{:S(2)}, u32[]{:S(2)}) collective-permute-start(bf16[128,1024]{1,0:T(8,128)(2,1)S(1)} %shard_map.85.refs_3_), channel_id=1, source_target_pairs={{0,2},{1,3},{2,0},{3,1},{4,6},{5,7},{6,4},{7,5},{8,10},{9,11},{10,... | collective-permute-start | bytes 786440 | tf_op jit(solution)/shard_map/ppermute | solution.py:394
  53.1 12.7 %collective-permute-start.19 = (bf16[128,1024]{1,0:T(8,128)(2,1)S(1)}, bf16[128,1024]{1,0:T(8,128)(2,1)S(1)}, u32[]{:S(2)}, u32[]{:S(2)}) collective-permute-start(bf16[128,1024]{1,0:T(8,128)(2,1)S(1)} %shard_map.90), channel_id=1, source_target_pairs={{0,2},{1,3},{2,0},{3,1},{4,6},{5,7},{6,4},{7,5},{8,10},{9,11},{10,... | collective-permute-start | bytes 786440 | tf_op jit(solution)/shard_map/ppermute | solution.py:394
  55.2 16.2 %collective-permute-start.18 = (bf16[128,1024]{1,0:T(8,128)(2,1)S(1)}, bf16[128,1024]{1,0:T(8,128)(2,1)S(1)}, u32[]{:S(2)}, u32[]{:S(2)}) collective-permute-start(bf16[128,1024]{1,0:T(8,128)(2,1)S(1)} %shard_map.89), channel_id=1, source_target_pairs={{0,2},{1,3},{2,0},{3,1},{4,6},{5,7},{6,4},{7,5},{8,10},{9,11},{10,... | collective-permute-start | bytes 786440 | tf_op jit(solution)/shard_map/ppermute | solution.py:394
  56.2 20.2 %collective-permute-start.17 = (bf16[128,1024]{1,0:T(8,128)(2,1)S(1)}, bf16[128,1024]{1,0:T(8,128)(2,1)S(1)}, u32[]{:S(2)}, u32[]{:S(2)}) collective-permute-start(bf16[128,1024]{1,0:T(8,128)(2,1)S(1)} %shard_map.87.refs_6_), channel_id=1, source_target_pairs={{0,2},{1,3},{2,0},{3,1},{4,6},{5,7},{6,4},{7,5},{8,10},{9,11},{10,... | collective-permute-start | bytes 786440 | tf_op jit(solution)/shard_map/ppermute | solution.py:394

commit v7 on v6

--- a/solution.py
+++ b/solution.py
@@ -323,56 +323,60 @@
     return call(kernel, ins, outs, flops, smem=1)[:2]
 
 
-def finish(local, scaled, state, rows, head_size, after=()):
+def finish(local, scaled, state, cuts, head_size, after=()):
     width = local.shape[1]
 
-    def kernel(o_ref, q_ref, s_ref, n_ref):
-        for c in range(0, width, head_size):
-            cols = slice(c, c + head_size)
-            total = o_ref[rows, cols] + dot_dims(q_ref[rows, cols], s_ref[:, cols], 1, 1)
-            mean = jnp.mean(total * total, axis=-1, keepdims=True)
-            n_ref[:, cols] = (total * lax.rsqrt(mean + 1e-05)).astype(BF16)
-
-    outs = [shape((rows.stop - rows.start, width), BF16)]
-    return call(kernel, [local, scaled, state], outs, 0, after)[0]
-
-
-def out_block(n0s, n1s, cuts, w0, w1, dtype, after=()):
+    def kernel(o_ref, q_ref, s_ref, *outs):
+        for rows, n_ref in zip(cuts, outs):
+            for c in range(0, width, head_size):
+                cols = slice(c, c + head_size)
+                total = o_ref[rows, cols] + dot_dims(q_ref[rows, cols], s_ref[:, cols], 1, 1)
+                mean = jnp.mean(total * total, axis=-1, keepdims=True)
+                n_ref[:, cols] = (total * lax.rsqrt(mean + 1e-05)).astype(BF16)
+
+    outs = [shape((cut.stop - cut.start, width), BF16) for cut in cuts]
+    return call(kernel, [local, scaled, state], outs, 0, after)
+
+
+def out_block(pairs, w0, w1, dtype, after=()):
     columns = w1.shape[1]
-    count = len(n0s)
-    rows = sum(cut.stop - cut.start for cut in cuts)
+    count = len(pairs)
+    rows = sum(own.shape[0] for own, _ in pairs)
     tile = min(columns, 512)
 
     def kernel(*refs):
         w0_ref, w1_ref, o_ref = refs[2 * count :]
         start = 0
-        for a_ref, b_ref, cut in zip(refs[:count], refs[count : 2 * count], cuts):
-            here = slice(start, start + cut.stop - cut.start)
+        for i in range(count):
+            a_ref, b_ref = refs[2 * i], refs[2 * i + 1]
+            here = slice(start, start + a_ref.shape[0])
             start = here.stop
             for c in range(0, columns, tile):
                 cols = slice(c, c + tile)
                 o_ref[here, cols] = (
-                    dot(a_ref[cut, :], w0_ref[:, cols]) + dot(b_ref[cut, :], w1_ref[:, cols])
+                    dot(a_ref[...], w0_ref[:, cols]) + dot(b_ref[...], w1_ref[:, cols])
                 ).astype(dtype)
 
-    return call(kernel, [*n0s, *n1s, w0, w1], [shape((rows, columns), dtype)], 0, after)[0]
-
-
-def add_rows(here, arrived, out, start):
+    ins = [x for pair in pairs for x in pair] + [w0, w1]
+    return call(kernel, ins, [shape((rows, columns), dtype)], 0, after)[0]
+
+
+def add_rows(here, arrived, out, start, unit):
     rows, columns = arrived.shape
-    block = start // rows
 
     def kernel(h_ref, a_ref, *refs):
-        refs[-1][...] = (h_ref[start : start + rows, :] + a_ref[...].astype(F32)).astype(BF16)
-
-    ins, specs, aliases = [here, arrived], [VMEM] * 2, {}
+        place = pl.ds(pl.multiple_of(start + pl.program_id(0) * unit, unit), unit)
+        refs[-1][...] = (h_ref[place, :] + a_ref[...].astype(F32)).astype(BF16)
+
+    block = (unit, columns)
+    ins, specs, aliases = [here, arrived], [VMEM, pl.BlockSpec(block, lambda s: (s, 0))], {}
     if out is not None:
         ins, specs, aliases = ins + [out], specs + [ANY], {2: 0}
     return pl.pallas_call(
         kernel,
-        grid=(1,),
+        grid=(rows // unit,),
         in_specs=specs,
-        out_specs=pl.BlockSpec((rows, columns), lambda s: (block, 0)),
+        out_specs=pl.BlockSpec(block, lambda s: (start // unit + s, 0)),
         out_shape=shape(here.shape, BF16),
         input_output_aliases=aliases,
         compiler_params=pltpu.CompilerParams(vmem_limit_bytes=8 * 1024 * 1024),
@@ -433,19 +437,17 @@
         me, 3, arrived_near, wq, wl, total_q, total_l, k, v, dcol, drow, spans, earlier[:-1], head_size, level_count
     )
 
-    step = rows // 4
-    own = finish(local, scaled, earlier[-1], slice(0, step), head_size)
-    near_own = swap_tp(own, 1)
-    crossing = [out_block([own], [near_own], [slice(0, step)], w_far_own, w_far, BF16)]
-    rest = finish(local, scaled, earlier[-1], slice(step, rows), head_size, (crossing[0],))
-    near_rest = swap_tp(rest, 1)
-    for r in range(0, rows - step, step):
-        crossing.append(out_block([rest], [near_rest], [slice(r, r + step)], w_far_own, w_far, BF16))
-    both = [slice(0, step), slice(0, rows - step)]
-    own_block = out_block([own, rest], [near_own, near_rest], both, w_here_own, w_here, F32, (crossing[-1],))
+    unit = rows // 8
+    ends = (0, 2, 4, 6, 7, 8)
+    cuts = [slice(start * unit, stop * unit) for start, stop in zip(ends, ends[1:])]
+    pieces = finish(local, scaled, earlier[-1], cuts[:1], head_size)
+    pieces += finish(local, scaled, earlier[-1], cuts[1:], head_size, pieces)
+    pairs = [(x, swap_tp(x, 1)) for x in pieces]
+    crossing = [out_block([pair], w_far_own, w_far, BF16) for pair in pairs]
+    own_block = out_block(pairs, w_here_own, w_here, F32, (crossing[-1],))
     out = None
-    for r, x in enumerate(crossing):
-        out = add_rows(own_block, swap_tp(x, 2), out, r * step)
+    for cut, x in zip(cuts, crossing):
+        out = add_rows(own_block, swap_tp(x, 2), out, cut.start, unit)
     return out
 
 

time: 77.4 us -> 76.7 us (level)
  waiting for transfers between devices: 34.9 us -> 31.1 us
  starting transfers between devices: 22 us -> 23.6 us
  Pallas kernels: 19.4 us -> 20.9 us
    ppermute x16 -> x20, waiting for transfers between devices: 26.1 us -> 22.3 us  [swap_tp(): return lax.ppermute(x, 'tp', [(i, i ^ bit) for i in range(4)])]
    ppermute x16 -> x20, starting transfers between devices: 10.7 us -> 12.2 us  [swap_tp(): return lax.ppermute(x, 'tp', [(i, i ^ bit) for i in range(4)])]
    pallas_call x17 -> x18, Pallas kernels: 16.4 us -> 17.4 us  [call(): pl.pallas_call(run, in_specs=[SMEM] * smem + [HBM] * hbm + [VMEM] * (coun...]
    pallas_call x4 -> x5, Pallas kernels: 3.03 us -> 3.56 us  [add_rows(): pl.pallas_call(kernel, grid=(rows // unit,), in_specs=specs, out_specs=pl...]
  transfers between devices with their start and end apart: 21 -> 25, of which waited for: 12 -> 13; matrix products, arithmetic and copies ran while one was open for 0% -> 0% of each run, Pallas kernels for 21% -> 24%
where the time goes in v7:
time: 76.7 us; the launch traced here: 76.5 us
  waiting for transfers between devices  31.1 us (41%)
  starting transfers between devices  23.6 us (31%)
  Pallas kernels  20.9 us (27%)
    ppermute x20, waiting for transfers between devices, swap_tp(): return lax.ppermute(x, 'tp', [(i, i ^ bit) for i in range(4)])  22.3 us
    pallas_call x18, Pallas kernels, call(): pl.pallas_call(run, in_specs=[SMEM] * smem + [HBM] * hbm + [VMEM] * (coun...  17.4 us
    ppermute x20, starting transfers between devices, swap_tp(): return lax.ppermute(x, 'tp', [(i, i ^ bit) for i in range(4)])  12.2 us
    ppermute x5, starting transfers between devices, swap_seq(): return lax.ppermute(x, 'seq', [(i, i ^ bit) for i in range(seq_size)])  11.4 us
    ppermute x5, waiting for transfers between devices, swap_seq(): return lax.ppermute(x, 'seq', [(i, i ^ bit) for i in range(seq_size)])  8.78 us
    pallas_call x5, Pallas kernels, add_rows(): pl.pallas_call(kernel, grid=(rows // unit,), in_specs=specs, out_specs=pl...  3.56 us
  transfers between devices with their start and end apart: 25, of which 13 were waited for; matrix products, arithmetic and copies ran while one was open for 0% of the time, Pallas kernels for 24%

profile of v7, /device:TPU:0, one launch (start us, length us, event | category | flops | bytes accessed | tf_op | source)
XLA Modules:
  0.0 76.5 jit_solution(6132057916947683772)
XLA Ops:
  0.5 2.5 %collective-permute-start = (bf16[512,1024]{1,0:T(8,128)(2,1)}, bf16[512,1024]{1,0:T(8,128)(2,1)S(1)}, u32[]{:S(2)}, u32[]{:S(2)}) collective-permute-start(bf16[512,1024]{1,0:T(8,128)(2,1)} %refs_2_.1), channel_id=1, source_target_pairs={{0,2},{1,3},{2,0},{3,1},{4,6},{5,7},{6,4},{7,5},{8,10},{9,11},{10,... | collective-permute-start | bytes 3145736 | tf_op jit(solution)/shard_map/ppermute | solution.py:398
  3.7 5.4 %shard_map.73 = (f32[512,512]{1,0:T(8,128)S(1)}, f32[512,256]{1,0:T(8,128)S(1)}, f32[512,24]{1,0:T(8,128)S(1)}, bf16[2,1024,512]{2,1,0:T(8,128)(2,1)S(1)}, bf16[...) custom-call(s32[1]{0:T(128)} %bitcast.refs_0_, ...), custom_call_target="tpu_custom_call" | custom-call | tf_op jit(solution)/shard_map/pallas_call | solution.py:41
  10.0 2.6 %collective-permute-start.2 = (f32[8,512]{1,0:T(8,128)S(1)}, f32[8,512]{1,0:T(8,128)S(1)}, u32[]{:S(2)}, u32[]{:S(2)}) collective-permute-start(f32[8,512]{1,0:T(8,128)S(1)} %get-tuple-element.45.refs_1_), channel_id=1, source_target_pairs={{0,4},{4,0},{8,12},{12,8},{16,20},{20,16},{24,28},{28,24},{1,5},{5... | collective-permute-start | bytes 49160 | tf_op jit(solution)/shard_map/ppermute | solution.py:401
  12.6 1.7 %collective-permute-done.2.refs_2_ = f32[8,512]{1,0:T(8,128)S(1)} collective-permute-done((f32[8,512]{1,0:T(8,128)S(1)}, f32[8,512]{1,0:T(8,128)S(1)}, u32[]{:S(2)}, u32[]{:S(2)}) %collective-permute-start.2) | collective-permute-done | bytes 16416 | tf_op jit(solution)/shard_map/ppermute | solution.py:401
  14.3 2.2 %collective-permute-start.3 = (f32[8,512]{1,0:T(8,128)S(1)}, f32[8,512]{1,0:T(8,128)S(1)}, u32[]{:S(2)}, u32[]{:S(2)}) collective-permute-start(f32[8,512]{1,0:T(8,128)S(1)} %get-tuple-element.46.refs_1_), channel_id=1, source_target_pairs={{0,8},{4,12},{8,0},{12,4},{16,24},{20,28},{24,16},{28,20},{1,9},{5... | collective-permute-start | bytes 49160 | tf_op jit(solution)/shard_map/ppermute | solution.py:401
  16.5 1.7 %collective-permute-done.3.refs_2_ = f32[8,512]{1,0:T(8,128)S(1)} collective-permute-done((f32[8,512]{1,0:T(8,128)S(1)}, f32[8,512]{1,0:T(8,128)S(1)}, u32[]{:S(2)}, u32[]{:S(2)}) %collective-permute-start.3) | collective-permute-done | bytes 16416 | tf_op jit(solution)/shard_map/ppermute | solution.py:401
  18.8 8.2 %collective-permute-done.refs_0_ = bf16[512,1024]{1,0:T(8,128)(2,1)S(1)} collective-permute-done((bf16[512,1024]{1,0:T(8,128)(2,1)}, bf16[512,1024]{1,0:T(8,128)(2,1)S(1)}, u32[]{:S(2)}, u32[]{:S(2)}) %collective-permute-start) | collective-permute-done | bytes 1048608 | tf_op jit(solution)/shard_map/ppermute | solution.py:398
  27.5 1.5 %collective-permute-done.7.refs_3_ = bf16[512,256]{1,0:T(8,128)(2,1)S(1)} collective-permute-done((bf16[512,256]{1,0:T(8,128)(2,1)S(1)}, bf16[512,256]{1,0:T(8,128)(2,1)S(1)}, u32[]{:S(2)}, u32[]{:S(2)}) %collective-permute-start.7) | collective-permute-done | bytes 262176 | tf_op jit(solution)/shard_map/ppermute | solution.py:398
  29.1 0.8 %shard_map.78 = (bf16[512,128]{1,0:T(8,128)(2,1)S(1)}, bf16[512,128]{1,0:T(8,128)(2,1)S(1)}, bf16[128,512]{1,0:T(8,128)(2,1)S(1)}) custom-call(bf16[512,1024]{1,0:T(8,128)(2,1)S(1)} %shard_map.76.refs_0_.refs_1_, bf16[1024,256]{1,0:T(8,128)(2,1)S(1)} %get-tuple-element.55.refs_1_, f32[512,256]{1,0:T(8,128)S(1)} %get-tuple-element.56.refs_2_, ...), custom_call_target="tpu_custom_call" | custom-call | tf_op jit(solution)/shard_map/pallas_call | solution.py:41
  29.9 1.8 %collective-permute-start.12 = (bf16[128,512]{1,0:T(8,128)(2,1)S(1)}, bf16[128,512]{1,0:T(8,128)(2,1)S(1)}, u32[]{:S(2)}, u32[]{:S(2)}) collective-permute-start(bf16[128,512]{1,0:T(8,128)(2,1)S(1)} %get-tuple-element.72.refs_0_), channel_id=1, source_target_pairs={{0,4},{4,0},{8,12},{12,8},{16,20},{20,16},{24,28},{28,24},{1,5},{5... | collective-permute-start | bytes 393224 | tf_op jit(solution)/shard_map/ppermute | solution.py:401
  31.6 1.1 %shard_map.79 = (f32[512,512]{1,0:T(8,128)S(1)}, f32[512,24]{1,0:T(8,128)S(1)}) custom-call(s32[1]{0:T(128)} %bitcast.refs_0_, bf16[512,1024]{1,0:T(8,128)(2,1)S(1)} %shard_map.76.refs_0_.refs_1_, bf16[2,1024,512]{2,1,0:T(8,128)(2,1)S(1)} %get-tuple-element.51.refs_2_.refs_5_, ...), custom_call_target="tpu_custom_call", output_to_operand_aliasing={{0}: (4, {}), {1}: (5, {})} | custom-call | flops 562036736 | bytes 5537796 | tf_op jit(solution)/shard_map/pallas_call | solution.py:41
  33.9 1.6 %collective-permute-done.12.refs_1_.refs_16_ = bf16[128,512]{1,0:T(8,128)(2,1)S(1)} collective-permute-done((bf16[128,512]{1,0:T(8,128)(2,1)S(1)}, bf16[128,512]{1,0:T(8,128)(2,1)S(1)}, u32[]{:S(2)}, u32[]{:S(2)}) %collective-permute-start.12) | collective-permute-done | bytes 131104 | tf_op jit(solution)/shard_map/ppermute | solution.py:401
  35.5 1.9 %collective-permute-start.13 = (bf16[128,512]{1,0:T(8,128)(2,1)S(1)}, bf16[128,512]{1,0:T(8,128)(2,1)S(1)}, u32[]{:S(2)}, u32[]{:S(2)}) collective-permute-start(bf16[128,512]{1,0:T(8,128)(2,1)S(1)} %shard_map.81.refs_0_), channel_id=1, source_target_pairs={{0,8},{4,12},{8,0},{12,4},{16,24},{20,28},{24,16},{28,20},{1,9},{5... | collective-permute-start | bytes 393224 | tf_op jit(solution)/shard_map/ppermute | solution.py:401
  37.4 3.2 %collective-permute-done.13.refs_17_.refs_1_ = bf16[128,512]{1,0:T(8,128)(2,1)S(1)} collective-permute-done((bf16[128,512]{1,0:T(8,128)(2,1)S(1)}, bf16[128,512]{1,0:T(8,128)(2,1)S(1)}, u32[]{:S(2)}, u32[]{:S(2)}) %collective-permute-start.13) | collective-permute-done | bytes 131104 | tf_op jit(solution)/shard_map/ppermute | solution.py:401
  40.6 2.9 %collective-permute-start.14 = (bf16[128,512]{1,0:T(8,128)(2,1)S(1)}, bf16[128,512]{1,0:T(8,128)(2,1)S(1)}, u32[]{:S(2)}, u32[]{:S(2)}) collective-permute-start(bf16[128,512]{1,0:T(8,128)(2,1)S(1)} %shard_map.83), channel_id=1, source_target_pairs={{0,16},{4,20},{8,24},{12,28},{16,0},{20,4},{24,8},{28,12},{1,17},{... | collective-permute-start | bytes 393224 | tf_op jit(solution)/shard_map/ppermute | solution.py:401
  43.5 4.0 %shard_map.82 = (f32[512,512]{1,0:T(8,128)S(1)}, bf16[512,512]{1,0:T(8,128)(2,1)S(1)}, bf16[512,512]{1,0:T(8,128)(2,1)}, f32[512,24]{1,0:T(8,128)}) custom-call(s32[1]{0:T(128)} %bitcast.refs_0_, bf16[512,256]{1,0:T(8,128)(2,1)S(1)} %collective-permute-done.8.refs_1_, bf16[512,256]{1,0:T(8,128)(2,1)S(1)} %collective-permute-done.9.refs_2_, ...), custom_call_target="tpu_custom_call" | custom-call | flops 1073741824 | bytes 7176196 | tf_op jit(solution)/shard_map/pallas_call | solution.py:41
  50.3 1.6 %collective-permute-start.24 = (bf16[128,1024]{1,0:T(8,128)(2,1)S(1)}, bf16[128,1024]{1,0:T(8,128)(2,1)S(1)}, u32[]{:S(2)}, u32[]{:S(2)}) collective-permute-start(bf16[128,1024]{1,0:T(8,128)(2,1)S(1)} %shard_map.91), channel_id=1, source_target_pairs={{0,2},{1,3},{2,0},{3,1},{4,6},{5,7},{6,4},{7,5},{8,10},{9,11},{10,... | collective-permute-start | bytes 786440 | tf_op jit(solution)/shard_map/ppermute | solution.py:398
  53.5 1.6 %collective-permute-start.22 = (bf16[128,1024]{1,0:T(8,128)(2,1)S(1)}, bf16[128,1024]{1,0:T(8,128)(2,1)S(1)}, u32[]{:S(2)}, u32[]{:S(2)}) collective-permute-start(bf16[128,1024]{1,0:T(8,128)(2,1)S(1)} %shard_map.89), channel_id=1, source_target_pairs={{0,2},{1,3},{2,0},{3,1},{4,6},{5,7},{6,4},{7,5},{8,10},{9,11},{10,... | collective-permute-start | bytes 786440 | tf_op jit(solution)/shard_map/ppermute | solution.py:398
  57.9 1.6 %collective-permute-start.20 = (bf16[64,1024]{1,0:T(8,128)(2,1)S(1)}, bf16[64,1024]{1,0:T(8,128)(2,1)S(1)}, u32[]{:S(2)}, u32[]{:S(2)}) collective-permute-start(bf16[64,1024]{1,0:T(8,128)(2,1)S(1)} %shard_map.86.refs_12_), channel_id=1, source_target_pairs={{0,2},{1,3},{2,0},{3,1},{4,6},{5,7},{6,4},{7,5},{8,10},{9,11},{10,... | collective-permute-start | bytes 393224 | tf_op jit(solution)/shard_map/ppermute | solution.py:398
  59.5 1.7 %shard_map.87.h_ref = f32[512,1024]{1,0:T(8,128)S(1)} custom-call(bf16[128,512]{1,0:T(8,128)(2,1)S(1)} %shard_map.84.refs_3_.refs_0_, bf16[128,512]{1,0:T(8,128)(2,1)S(1)} %collective-permute-done.15.refs_1_, bf16[128,512]{1,0:T(8,128)(2,1)S(1)} %get-tuple-element.79.refs_2_.refs_0_, bf16[128,512]{1,0:T(8,128)(2,1)S(1)} %collective-permute-done.16.refs_3_.refs_1_, ...), custom_call_target="tpu_custom_call" | custom-call | tf_op jit(solution)/shard_map/pallas_call | solution.py:41
  61.9 3.2 %collective-permute-done.23.a_ref = bf16[128,1024]{1,0:T(8,128)(2,1)S(1)} collective-permute-done((bf16[128,1024]{1,0:T(8,128)(2,1)S(1)}, bf16[128,1024]{1,0:T(8,128)(2,1)S(1)}, u32[]{:S(2)}, u32[]{:S(2)}) %collective-permute-start.23) | collective-permute-done | bytes 262176 | tf_op jit(solution)/shard_map/ppermute | solution.py:398
  65.9 4.9 %collective-permute-done.22.a_ref = bf16[128,1024]{1,0:T(8,128)(2,1)S(1)} collective-permute-done((bf16[128,1024]{1,0:T(8,128)(2,1)S(1)}, bf16[128,1024]{1,0:T(8,128)(2,1)S(1)}, u32[]{:S(2)}, u32[]{:S(2)}) %collective-permute-start.22) | collective-permute-done | bytes 262176 | tf_op jit(solution)/shard_map/ppermute | solution.py:398
  71.5 2.1 %collective-permute-done.21.a_ref = bf16[64,1024]{1,0:T(8,128)(2,1)S(1)} collective-permute-done((bf16[64,1024]{1,0:T(8,128)(2,1)S(1)}, bf16[64,1024]{1,0:T(8,128)(2,1)S(1)}, u32[]{:S(2)}, u32[]{:S(2)}) %collective-permute-start.21) | collective-permute-done | bytes 131104 | tf_op jit(solution)/shard_map/ppermute | solution.py:398
  74.3 1.5 %collective-permute-done.20.a_ref = bf16[64,1024]{1,0:T(8,128)(2,1)S(1)} collective-permute-done((bf16[64,1024]{1,0:T(8,128)(2,1)S(1)}, bf16[64,1024]{1,0:T(8,128)(2,1)S(1)}, u32[]{:S(2)}, u32[]{:S(2)}) %collective-permute-start.20) | collective-permute-done | bytes 131104 | tf_op jit(solution)/shard_map/ppermute | solution.py:398
  (52 shorter events, 15.1 us)
Async XLA Ops:
  0.0 3.0 %collective-permute-start.1 = (bf16[512,1024]{1,0:T(8,128)(2,1)}, bf16[512,1024]{1,0:T(8,128)(2,1)S(1)}, u32[]{:S(2)}, u32[]{:S(2)}) collective-permute-start(bf16[512,1024]{1,0:T(8,128)(2,1)} %refs_2_.1), channel_id=1, source_target_pairs={{0,1},{1,0},{2,3},{3,2},{4,5},{5,4},{6,7},{7,6},{8,9},{9,8},{10,11... | collective-permute-start | bytes 3145736 | tf_op jit(solution)/shard_map/ppermute | solution.py:398
  0.5 26.6 %collective-permute-start = (bf16[512,1024]{1,0:T(8,128)(2,1)}, bf16[512,1024]{1,0:T(8,128)(2,1)S(1)}, u32[]{:S(2)}, u32[]{:S(2)}) collective-permute-start(bf16[512,1024]{1,0:T(8,128)(2,1)} %refs_2_.1), channel_id=1, source_target_pairs={{0,2},{1,3},{2,0},{3,1},{4,6},{5,7},{6,4},{7,5},{8,10},{9,11},{10,... | collective-permute-start | bytes 3145736 | tf_op jit(solution)/shard_map/ppermute | solution.py:398
  9.0 18.0 %collective-permute-start.4 = (bf16[512,1024]{1,0:T(8,128)(2,1)S(1)}, bf16[512,1024]{1,0:T(8,128)(2,1)S(1)}, u32[]{:S(2)}, u32[]{:S(2)}) collective-permute-start(bf16[512,1024]{1,0:T(8,128)(2,1)S(1)} %get-tuple-element.49), channel_id=1, source_target_pairs={{0,1},{1,0},{2,3},{3,2},{4,5},{5,4},{6,7},{7,6},{8,9},{9,8},{10,11... | collective-permute-start | bytes 3145736 | tf_op jit(solution)/shard_map/ppermute | solution.py:398
  9.5 17.6 %collective-permute-start.5 = (bf16[512,1024]{1,0:T(8,128)(2,1)S(1)}, bf16[512,1024]{1,0:T(8,128)(2,1)S(1)}, u32[]{:S(2)}, u32[]{:S(2)}) collective-permute-start(bf16[512,1024]{1,0:T(8,128)(2,1)S(1)} %get-tuple-element.50), channel_id=1, source_target_pairs={{0,1},{1,0},{2,3},{3,2},{4,5},{5,4},{6,7},{7,6},{8,9},{9,8},{10,11... | collective-permute-start | bytes 3145736 | tf_op jit(solution)/shard_map/ppermute | solution.py:398
  9.6 17.4 %collective-permute-start.6 = (bf16[1024,256]{1,0:T(8,128)(2,1)S(1)}, bf16[1024,256]{1,0:T(8,128)(2,1)S(1)}, u32[]{:S(2)}, u32[]{:S(2)}) collective-permute-start(bf16[1024,256]{1,0:T(8,128)(2,1)S(1)} %get-tuple-element.57), channel_id=1, source_target_pairs={{0,1},{1,0},{2,3},{3,2},{4,5},{5,4},{6,7},{7,6},{8,9},{9,8},{10,11... | collective-permute-start | bytes 1572872 | tf_op jit(solution)/shard_map/ppermute | solution.py:398
  10.0 4.3 %collective-permute-start.2 = (f32[8,512]{1,0:T(8,128)S(1)}, f32[8,512]{1,0:T(8,128)S(1)}, u32[]{:S(2)}, u32[]{:S(2)}) collective-permute-start(f32[8,512]{1,0:T(8,128)S(1)} %get-tuple-element.45.refs_1_), channel_id=1, source_target_pairs={{0,4},{4,0},{8,12},{12,8},{16,20},{20,16},{24,28},{28,24},{1,5},{5... | collective-permute-start | bytes 49160 | tf_op jit(solution)/shard_map/ppermute | solution.py:401
  14.3 3.9 %collective-permute-start.3 = (f32[8,512]{1,0:T(8,128)S(1)}, f32[8,512]{1,0:T(8,128)S(1)}, u32[]{:S(2)}, u32[]{:S(2)}) collective-permute-start(f32[8,512]{1,0:T(8,128)S(1)} %get-tuple-element.46.refs_1_), channel_id=1, source_target_pairs={{0,8},{4,12},{8,0},{12,4},{16,24},{20,28},{24,16},{28,20},{1,9},{5... | collective-permute-start | bytes 49160 | tf_op jit(solution)/shard_map/ppermute | solution.py:401
  27.5 1.6 %collective-permute-start.7 = (bf16[512,256]{1,0:T(8,128)(2,1)S(1)}, bf16[512,256]{1,0:T(8,128)(2,1)S(1)}, u32[]{:S(2)}, u32[]{:S(2)}) collective-permute-start(bf16[512,256]{1,0:T(8,128)(2,1)S(1)} %shard_map.77), channel_id=1, source_target_pairs={{0,1},{1,0},{2,3},{3,2},{4,5},{5,4},{6,7},{7,6},{8,9},{9,8},{10,11... | collective-permute-start | bytes 786440 | tf_op jit(solution)/shard_map/ppermute | solution.py:398
  29.9 5.6 %collective-permute-start.12 = (bf16[128,512]{1,0:T(8,128)(2,1)S(1)}, bf16[128,512]{1,0:T(8,128)(2,1)S(1)}, u32[]{:S(2)}, u32[]{:S(2)}) collective-permute-start(bf16[128,512]{1,0:T(8,128)(2,1)S(1)} %get-tuple-element.72.refs_0_), channel_id=1, source_target_pairs={{0,4},{4,0},{8,12},{12,8},{16,20},{20,16},{24,28},{28,24},{1,5},{5... | collective-permute-start | bytes 393224 | tf_op jit(solution)/shard_map/ppermute | solution.py:401
  32.8 10.7 %collective-permute-start.8 = (bf16[512,256]{1,0:T(8,128)(2,1)S(1)}, bf16[512,256]{1,0:T(8,128)(2,1)S(1)}, u32[]{:S(2)}, u32[]{:S(2)}) collective-permute-start(bf16[512,256]{1,0:T(8,128)(2,1)S(1)} %get-tuple-element.61), channel_id=1, source_target_pairs={{0,1},{1,0},{2,3},{3,2},{4,5},{5,4},{6,7},{7,6},{8,9},{9,8},{10,11... | collective-permute-start | bytes 786440 | tf_op jit(solution)/shard_map/ppermute | solution.py:398
  32.9 10.6 %collective-permute-start.9 = (bf16[512,256]{1,0:T(8,128)(2,1)S(1)}, bf16[512,256]{1,0:T(8,128)(2,1)S(1)}, u32[]{:S(2)}, u32[]{:S(2)}) collective-permute-start(bf16[512,256]{1,0:T(8,128)(2,1)S(1)} %get-tuple-element.62), channel_id=1, source_target_pairs={{0,1},{1,0},{2,3},{3,2},{4,5},{5,4},{6,7},{7,6},{8,9},{9,8},{10,11... | collective-permute-start | bytes 786440 | tf_op jit(solution)/shard_map/ppermute | solution.py:398
  33.4 10.1 %collective-permute-start.10 = (bf16[512,256]{1,0:T(8,128)(2,1)S(1)}, bf16[512,256]{1,0:T(8,128)(2,1)S(1)}, u32[]{:S(2)}, u32[]{:S(2)}) collective-permute-start(bf16[512,256]{1,0:T(8,128)(2,1)S(1)} %get-tuple-element.63), channel_id=1, source_target_pairs={{0,1},{1,0},{2,3},{3,2},{4,5},{5,4},{6,7},{7,6},{8,9},{9,8},{10,11... | collective-permute-start | bytes 786440 | tf_op jit(solution)/shard_map/ppermute | solution.py:398
  33.5 10.0 %collective-permute-start.11 = (bf16[512,256]{1,0:T(8,128)(2,1)S(1)}, bf16[512,256]{1,0:T(8,128)(2,1)S(1)}, u32[]{:S(2)}, u32[]{:S(2)}) collective-permute-start(bf16[512,256]{1,0:T(8,128)(2,1)S(1)} %get-tuple-element.64), channel_id=1, source_target_pairs={{0,1},{1,0},{2,3},{3,2},{4,5},{5,4},{6,7},{7,6},{8,9},{9,8},{10,11... | collective-permute-start | bytes 786440 | tf_op jit(solution)/shard_map/ppermute | solution.py:398
  35.5 5.0 %collective-permute-start.13 = (bf16[128,512]{1,0:T(8,128)(2,1)S(1)}, bf16[128,512]{1,0:T(8,128)(2,1)S(1)}, u32[]{:S(2)}, u32[]{:S(2)}) collective-permute-start(bf16[128,512]{1,0:T(8,128)(2,1)S(1)} %shard_map.81.refs_0_), channel_id=1, source_target_pairs={{0,8},{4,12},{8,0},{12,4},{16,24},{20,28},{24,16},{28,20},{1,9},{5... | collective-permute-start | bytes 393224 | tf_op jit(solution)/shard_map/ppermute | solution.py:401
  40.6 7.5 %collective-permute-start.14 = (bf16[128,512]{1,0:T(8,128)(2,1)S(1)}, bf16[128,512]{1,0:T(8,128)(2,1)S(1)}, u32[]{:S(2)}, u32[]{:S(2)}) collective-permute-start(bf16[128,512]{1,0:T(8,128)(2,1)S(1)} %shard_map.83), channel_id=1, source_target_pairs={{0,16},{4,20},{8,24},{12,28},{16,0},{20,4},{24,8},{28,12},{1,17},{... | collective-permute-start | bytes 393224 | tf_op jit(solution)/shard_map/ppermute | solution.py:401
  48.4 1.4 %collective-permute-start.15 = (bf16[128,512]{1,0:T(8,128)(2,1)S(1)}, bf16[128,512]{1,0:T(8,128)(2,1)S(1)}, u32[]{:S(2)}, u32[]{:S(2)}) collective-permute-start(bf16[128,512]{1,0:T(8,128)(2,1)S(1)} %shard_map.84.refs_3_.refs_0_), channel_id=1, source_target_pairs={{0,1},{1,0},{2,3},{3,2},{4,5},{5,4},{6,7},{7,6},{8,9},{9,8},{10,11... | collective-permute-start | bytes 393224 | tf_op jit(solution)/shard_map/ppermute | solution.py:398
  49.1 2.9 %collective-permute-start.16 = (bf16[128,512]{1,0:T(8,128)(2,1)S(1)}, bf16[128,512]{1,0:T(8,128)(2,1)S(1)}, u32[]{:S(2)}, u32[]{:S(2)}) collective-permute-start(bf16[128,512]{1,0:T(8,128)(2,1)S(1)} %get-tuple-element.79.refs_2_.refs_0_), channel_id=1, source_target_pairs={{0,1},{1,0},{2,3},{3,2},{4,5},{5,4},{6,7},{7,6},{8,9},{9,8},{10,11... | collective-permute-start | bytes 393224 | tf_op jit(solution)/shard_map/ppermute | solution.py:398
  49.7 3.3 %collective-permute-start.17 = (bf16[128,512]{1,0:T(8,128)(2,1)S(1)}, bf16[128,512]{1,0:T(8,128)(2,1)S(1)}, u32[]{:S(2)}, u32[]{:S(2)}) collective-permute-start(bf16[128,512]{1,0:T(8,128)(2,1)S(1)} %get-tuple-element.80.refs_4_.refs_0_), channel_id=1, source_target_pairs={{0,1},{1,0},{2,3},{3,2},{4,5},{5,4},{6,7},{7,6},{8,9},{9,8},{10,11... | collective-permute-start | bytes 393224 | tf_op jit(solution)/shard_map/ppermute | solution.py:398
  50.3 10.8 %collective-permute-start.24 = (bf16[128,1024]{1,0:T(8,128)(2,1)S(1)}, bf16[128,1024]{1,0:T(8,128)(2,1)S(1)}, u32[]{:S(2)}, u32[]{:S(2)}) collective-permute-start(bf16[128,1024]{1,0:T(8,128)(2,1)S(1)} %shard_map.91), channel_id=1, source_target_pairs={{0,2},{1,3},{2,0},{3,1},{4,6},{5,7},{6,4},{7,5},{8,10},{9,11},{10,... | collective-permute-start | bytes 786440 | tf_op jit(solution)/shard_map/ppermute | solution.py:398
  52.5 12.7 %collective-permute-start.23 = (bf16[128,1024]{1,0:T(8,128)(2,1)S(1)}, bf16[128,1024]{1,0:T(8,128)(2,1)S(1)}, u32[]{:S(2)}, u32[]{:S(2)}) collective-permute-start(bf16[128,1024]{1,0:T(8,128)(2,1)S(1)} %shard_map.90), channel_id=1, source_target_pairs={{0,2},{1,3},{2,0},{3,1},{4,6},{5,7},{6,4},{7,5},{8,10},{9,11},{10,... | collective-permute-start | bytes 786440 | tf_op jit(solution)/shard_map/ppermute | solution.py:398
  53.5 17.3 %collective-permute-start.22 = (bf16[128,1024]{1,0:T(8,128)(2,1)S(1)}, bf16[128,1024]{1,0:T(8,128)(2,1)S(1)}, u32[]{:S(2)}, u32[]{:S(2)}) collective-permute-start(bf16[128,1024]{1,0:T(8,128)(2,1)S(1)} %shard_map.89), channel_id=1, source_target_pairs={{0,2},{1,3},{2,0},{3,1},{4,6},{5,7},{6,4},{7,5},{8,10},{9,11},{10,... | collective-permute-start | bytes 786440 | tf_op jit(solution)/shard_map/ppermute | solution.py:398
  55.1 2.3 %collective-permute-start.19 = (bf16[64,512]{1,0:T(8,128)(2,1)S(1)}, bf16[64,512]{1,0:T(8,128)(2,1)S(1)}, u32[]{:S(2)}, u32[]{:S(2)}) collective-permute-start(bf16[64,512]{1,0:T(8,128)(2,1)S(1)} %get-tuple-element.82.refs_0_.refs_8_), channel_id=1, source_target_pairs={{0,1},{1,0},{2,3},{3,2},{4,5},{5,4},{6,7},{7,6},{8,9},{9,8},{10,11... | collective-permute-start | bytes 196616 | tf_op jit(solution)/shard_map/ppermute | solution.py:398
  56.9 16.7 %collective-permute-start.21 = (bf16[64,1024]{1,0:T(8,128)(2,1)S(1)}, bf16[64,1024]{1,0:T(8,128)(2,1)S(1)}, u32[]{:S(2)}, u32[]{:S(2)}) collective-permute-start(bf16[64,1024]{1,0:T(8,128)(2,1)S(1)} %shard_map.88), channel_id=1, source_target_pairs={{0,2},{1,3},{2,0},{3,1},{4,6},{5,7},{6,4},{7,5},{8,10},{9,11},{10,... | collective-permute-start | bytes 393224 | tf_op jit(solution)/shard_map/ppermute | solution.py:398
  57.9 17.9 %collective-permute-start.20 = (bf16[64,1024]{1,0:T(8,128)(2,1)S(1)}, bf16[64,1024]{1,0:T(8,128)(2,1)S(1)}, u32[]{:S(2)}, u32[]{:S(2)}) collective-permute-start(bf16[64,1024]{1,0:T(8,128)(2,1)S(1)} %shard_map.86.refs_12_), channel_id=1, source_target_pairs={{0,2},{1,3},{2,0},{3,1},{4,6},{5,7},{6,4},{7,5},{8,10},{9,11},{10,... | collective-permute-start | bytes 393224 | tf_op jit(solution)/shard_map/ppermute | solution.py:398
  (2 other events, 2.0 us)

commit v8 on v7

--- a/solution.py
+++ b/solution.py
@@ -114,6 +114,61 @@
 
     ins = [slab, total, other] + ([] if before is None else [before])
     return call(kernel, ins, [shape(total.shape, F32)] * 5, 0, smem=1)
+
+
+def pair_totals(total, other):
+    def kernel(t_ref, o_ref, out_ref):
+        out_ref[0:4, :] = t_ref[0:4, :]
+        out_ref[4:8, :] = o_ref[0:4, :]
+
+    return call(kernel, [total, other], [shape(total.shape, F32)], 0)[0]
+
+
+def link_four(slab, here, there):
+    def kernel(slab_ref, h_ref, t_ref, total_out, before_out, factors_out, span1_out, span2_out):
+        upper, above = upper_half(slab_ref, 0), upper_half(slab_ref, 1)
+        mine, beside = h_ref[0:1, :], h_ref[4:5, :]
+        across, diagonal = t_ref[0:1, :], t_ref[4:5, :]
+        own_pair, other_pair = mine + beside, across + diagonal
+        first = jnp.where(upper, beside, 0.0)
+        second = first + jnp.where(above, other_pair, 0.0)
+        own_scale = jnp.where(above, 0.0, other_pair)
+        other_scale = jnp.where(above, own_pair, 0.0)
+        by_mine = jnp.where(upper, 0.0, beside)
+        by_beside = jnp.where(upper, mine, 0.0)
+        by_across = jnp.where(upper, 0.0, diagonal)
+        by_diagonal = jnp.where(upper, across, 0.0)
+        factors_out[0:1, :] = jnp.exp(by_mine + own_scale)
+        factors_out[1:2, :] = jnp.exp(by_beside + own_scale)
+        factors_out[2:3, :] = jnp.exp(by_across + other_scale)
+        factors_out[3:4, :] = jnp.exp(by_diagonal + other_scale)
+        factors_out[4:5, :] = jnp.exp(by_across)
+        factors_out[5:6, :] = jnp.exp(by_diagonal)
+        factors_out[6:8, :] = jnp.zeros((2, h_ref.shape[1]), F32)
+        wide = h_ref.shape
+        total_out[...] = jnp.broadcast_to(own_pair + other_pair, wide)
+        before_out[...] = jnp.broadcast_to(second, wide)
+        span1_out[...] = jnp.broadcast_to(jnp.where(above, first, -jnp.inf), wide)
+        span2_out[...] = jnp.broadcast_to(jnp.where(upper_half(slab_ref, 2), second, -jnp.inf), wide)
+
+    return call(kernel, [slab, here, there], [shape(here.shape, F32)] * 5, 0, smem=1)
+
+
+def join_four(me, mine, first, second, diagonal, factors, after):
+    rows = mine.shape[0]
+
+    def kernel(me_ref, m_ref, x_ref, y_ref, d_ref, f_ref, four_ref, pair_ref, beside_ref):
+        even = (me_ref[0] & 1) == 0
+        m, d = m_ref[...].astype(F32), d_ref[...].astype(F32)
+        x, y = x_ref[...].astype(F32), y_ref[0:rows, :].astype(F32)
+        b, a = jnp.where(even, x, y), jnp.where(even, y, x)
+        beside_ref[...] = b.astype(BF16)
+        f = [f_ref[i : i + 1, :] for i in range(6)]
+        four_ref[...] = (f[0] * m + f[1] * b + f[2] * a + f[3] * d).astype(BF16)
+        pair_ref[...] = (f[4] * a + f[5] * d).astype(BF16)
+
+    outs = [shape(mine.shape, BF16)] * 3
+    return call(kernel, [me, mine, first, second, diagonal, factors], outs, 0, after, smem=1)
 
 
 def combine(state, other, own_factor, other_factor, after):
@@ -211,17 +266,6 @@
     return call(kernel, [me, x, wq, wl, total_q, total_l], outs, flops, after, smem=1, aliases={4: 0, 5: 1})
 
 
-def split(x, ways, after):
-    rows, columns = x.shape
-    part = columns // ways
-
-    def kernel(x_ref, *outs):
-        for i, o_ref in enumerate(outs):
-            o_ref[...] = x_ref[:, i * part : (i + 1) * part]
-
-    return call(kernel, [x], [shape((rows, part), x.dtype)] * ways, 0, after)
-
-
 def partial(x, w):
     def kernel(x_ref, w_ref, o_ref):
         o_ref[...] = dot(x_ref[...], w_ref[...]).astype(BF16)
@@ -235,7 +279,7 @@
     kv_width = wkv.shape[1] // 2
     group = heads // (kv_width // head_size)
 
-    def kernel(x_ref, w_ref, total_ref, near_ref, keep_ref, k_out, v_out, s_out):
+    def kernel(x_ref, w_ref, total_ref, near_ref, keep_ref, k_out, v_out, s_out, wide_out):
         total = total_ref[...] + near_ref[...].astype(F32) + dot(x_ref[...], w_ref[...])
         keys = total[:, :kv_width].astype(BF16)
         values = total[:, kv_width:].astype(BF16)
@@ -249,12 +293,16 @@
                 axis=1,
             )
             wide = slice(g * group * head_size, (g + 1) * group * head_size)
-            s_out[:, wide] = dot_dims(values[:, cols], weighted, 0, 0).astype(BF16)
+            state = dot_dims(values[:, cols], weighted, 0, 0).astype(BF16)
+            s_out[:, wide] = state
+            wide_out[0:head_size, wide] = state
+        wide_out[head_size:, :] = jnp.zeros((16, wide_out.shape[1]), BF16)
 
     outs = [
         shape((rows, kv_width), BF16),
         shape((rows, kv_width), BF16),
         shape((head_size, heads * head_size), BF16),
+        shape((head_size + 16, heads * head_size), BF16),
     ]
     return call(kernel, [x, wkv, total_kv, from_near, keep], outs, 0)
 
@@ -410,8 +458,10 @@
     w_here_own, w_here_send, w_far_own, w_far_send = blocks
     w_here, w_far = swap_tp(w_here_send, 1), swap_tp(w_far_send, 1)
 
-    spans, factors, before = [span], [], None
-    for b in range(seq_bits - 1):
+    here = pair_totals(total, swap_seq(total, 1))
+    total, before, four_factors, *later_spans = link_four(slab, here, swap_seq(here, 2))
+    spans, factors = [span, *later_spans], []
+    for b in range(2, seq_bits - 1):
         total, before, own, other, span = link(slab, b, total, swap_seq(total, 1 << b), before)
         spans.append(span)
         factors.append((own, other))
@@ -420,18 +470,31 @@
     wkv_near = swap_tp(wkv_send, 1)
     arrived = gate(far, total, w_far, w_here)
     from_near = swap_tp(partial(arrived, wkv_near), 1)
+    arrived = gate(arrived, from_near)
+    arrived_near = [swap_tp(arrived, 1)]
     total_q, total_kv, total_l = totals
-    k, v, state = project_state(arrived, wkv, total_kv, from_near, keep, head_size)
-    total_q, total_l = project(me, 2, arrived, wq, wl, total_q, total_l, (k,))
-    arrived_near = [swap_tp(x, 1) for x in split(arrived, 4, (total_l,))]
-
-    earlier = []
-    for b in range(seq_bits):
+    k, v, state, state_wide = project_state(arrived, wkv, total_kv, from_near, keep, head_size)
+
+    def swap_group(x, bits):
+        tp_size = lax.axis_size("tp")
+        pairs = [
+            (i * tp_size + j, (i ^ bits[j & 1]) * tp_size + j)
+            for i in range(seq_size)
+            for j in range(tp_size)
+        ]
+        return lax.ppermute(x, ("seq", "tp"), pairs)
+
+    first = swap_group(state, (1, 2))
+    second = swap_group(state_wide, (2, 1))
+    diagonal = swap_group(first, (2, 1))
+    total_q, total_l = project(me, 2, arrived, wq, wl, total_q, total_l, (k, first))
+    state, other_pair, beside = join_four(me, state, first, second, diagonal, four_factors, (total_l,))
+    earlier = [beside, other_pair]
+    for b in range(2, seq_bits):
         other = swap_seq(state, 1 << b)
         earlier.append(other)
         if b < seq_bits - 1:
-            after = () if b else (total_l,)
-            state = combine(state, other, *factors[b], after)
+            state = combine(state, other, *factors[b - 2], ())
 
     local, scaled = attend(
         me, 3, arrived_near, wq, wl, total_q, total_l, k, v, dcol, drow, spans, earlier[:-1], head_size, level_count

time: 76.7 us -> 76.3 us (level)
  waiting for transfers between devices: 31.1 us -> 29.9 us
  starting transfers between devices: 23.6 us -> 24.5 us
    ppermute x0 -> x3, starting transfers between devices: none -> 5.73 us  [swap_group(): return lax.ppermute(x, ('seq', 'tp'), pairs)]
    ppermute x5 -> x3, waiting for transfers between devices: 8.78 us -> 3.42 us  [swap_seq(): return lax.ppermute(x, 'seq', [(i, i ^ bit) for i in range(seq_size)])]
    ppermute x0 -> x3, waiting for transfers between devices: none -> 4.02 us  [swap_group(): return lax.ppermute(x, ('seq', 'tp'), pairs)]
    ppermute x5 -> x3, starting transfers between devices: 11.4 us -> 7.54 us  [swap_seq(): return lax.ppermute(x, 'seq', [(i, i ^ bit) for i in range(seq_size)])]
    ppermute x20 -> x17, starting transfers between devices: 12.2 us -> 11.2 us  [swap_tp(): return lax.ppermute(x, 'tp', [(i, i ^ bit) for i in range(4)])]
    ppermute x20 -> x17, waiting for transfers between devices: 22.3 us -> 22.4 us  [swap_tp(): return lax.ppermute(x, 'tp', [(i, i ^ bit) for i in range(4)])]
    pallas_call x18 -> x16, Pallas kernels: 17.4 us -> 17.4 us  [call(): pl.pallas_call(run, in_specs=[SMEM] * smem + [HBM] * hbm + [VMEM] * (coun...]
  transfers between devices with their start and end apart: 25 -> 23, of which waited for: 13 -> 12; matrix products, arithmetic and copies ran while one was open for 0% -> 0% of each run, Pallas kernels for 24% -> 26%
where the time goes in v8:
time: 76.3 us; the launch traced here: 76.1 us
  waiting for transfers between devices  29.9 us (39%)
  starting transfers between devices  24.5 us (32%)
  Pallas kernels  20.9 us (27%)
    ppermute x17, waiting for transfers between devices, swap_tp(): return lax.ppermute(x, 'tp', [(i, i ^ bit) for i in range(4)])  22.4 us
    pallas_call x16, Pallas kernels, call(): pl.pallas_call(run, in_specs=[SMEM] * smem + [HBM] * hbm + [VMEM] * (coun...  17.4 us
    ppermute x17, starting transfers between devices, swap_tp(): return lax.ppermute(x, 'tp', [(i, i ^ bit) for i in range(4)])  11.2 us
    ppermute x3, starting transfers between devices, swap_seq(): return lax.ppermute(x, 'seq', [(i, i ^ bit) for i in range(seq_size)])  7.54 us
    ppermute x3, starting transfers between devices, swap_group(): return lax.ppermute(x, ('seq', 'tp'), pairs)  5.73 us
    ppermute x3, waiting for transfers between devices, swap_group(): return lax.ppermute(x, ('seq', 'tp'), pairs)  4.02 us
    pallas_call x5, Pallas kernels, add_rows(): pl.pallas_call(kernel, grid=(rows // unit,), in_specs=specs, out_specs=pl...  3.56 us
    ppermute x3, waiting for transfers between devices, swap_seq(): return lax.ppermute(x, 'seq', [(i, i ^ bit) for i in range(seq_size)])  3.42 us
  transfers between devices with their start and end apart: 23, of which 12 were waited for; matrix products, arithmetic and copies ran while one was open for 0% of the time, Pallas kernels for 26%

profile of v8, /device:TPU:0, one launch (start us, length us, event | category | flops | bytes accessed | tf_op | source)
XLA Modules:
  0.0 76.1 jit_solution(4517914848856285286)
XLA Ops:
  0.5 2.5 %collective-permute-start = (bf16[512,1024]{1,0:T(8,128)(2,1)}, bf16[512,1024]{1,0:T(8,128)(2,1)S(1)}, u32[]{:S(2)}, u32[]{:S(2)}) collective-permute-start(bf16[512,1024]{1,0:T(8,128)(2,1)} %refs_2_.1), channel_id=1, source_target_pairs={{0,2},{1,3},{2,0},{3,1},{4,6},{5,7},{6,4},{7,5},{8,10},{9,11},{10,... | collective-permute-start | bytes 3145736 | tf_op jit(solution)/shard_map/ppermute | solution.py:446
  3.7 5.4 %shard_map.73 = (f32[512,512]{1,0:T(8,128)S(1)}, f32[512,256]{1,0:T(8,128)S(1)}, f32[512,24]{1,0:T(8,128)S(1)}, bf16[2,1024,512]{2,1,0:T(8,128)(2,1)S(1)}, bf16[...) custom-call(s32[1]{0:T(128)} %bitcast.refs_0_, ...), custom_call_target="tpu_custom_call" | custom-call | tf_op jit(solution)/shard_map/pallas_call | solution.py:41
  10.0 2.6 %collective-permute-start.2 = (f32[8,512]{1,0:T(8,128)S(1)}, f32[8,512]{1,0:T(8,128)S(1)}, u32[]{:S(2)}, u32[]{:S(2)}) collective-permute-start(f32[8,512]{1,0:T(8,128)S(1)} %get-tuple-element.40.refs_0_), channel_id=1, source_target_pairs={{0,4},{4,0},{8,12},{12,8},{16,20},{20,16},{24,28},{28,24},{1,5},{5... | collective-permute-start | bytes 49160 | tf_op jit(solution)/shard_map/ppermute | solution.py:449
  12.6 1.7 %collective-permute-done.2.refs_1_ = f32[8,512]{1,0:T(8,128)S(1)} collective-permute-done((f32[8,512]{1,0:T(8,128)S(1)}, f32[8,512]{1,0:T(8,128)S(1)}, u32[]{:S(2)}, u32[]{:S(2)}) %collective-permute-start.2) | collective-permute-done | bytes 16416 | tf_op jit(solution)/shard_map/ppermute | solution.py:449
  14.3 2.1 %collective-permute-start.3 = (f32[8,512]{1,0:T(8,128)S(1)}, f32[8,512]{1,0:T(8,128)S(1)}, u32[]{:S(2)}, u32[]{:S(2)}) collective-permute-start(f32[8,512]{1,0:T(8,128)S(1)} %shard_map.74.refs_1_), channel_id=1, source_target_pairs={{0,8},{4,12},{8,0},{12,4},{16,24},{20,28},{24,16},{28,20},{1,9},{5... | collective-permute-start | bytes 49160 | tf_op jit(solution)/shard_map/ppermute | solution.py:449
  16.4 1.7 %collective-permute-done.3.refs_2_ = f32[8,512]{1,0:T(8,128)S(1)} collective-permute-done((f32[8,512]{1,0:T(8,128)S(1)}, f32[8,512]{1,0:T(8,128)S(1)}, u32[]{:S(2)}, u32[]{:S(2)}) %collective-permute-start.3) | collective-permute-done | bytes 16416 | tf_op jit(solution)/shard_map/ppermute | solution.py:449
  18.8 8.2 %collective-permute-done.refs_0_ = bf16[512,1024]{1,0:T(8,128)(2,1)S(1)} collective-permute-done((bf16[512,1024]{1,0:T(8,128)(2,1)}, bf16[512,1024]{1,0:T(8,128)(2,1)S(1)}, u32[]{:S(2)}, u32[]{:S(2)}) %collective-permute-start) | collective-permute-done | bytes 1048608 | tf_op jit(solution)/shard_map/ppermute | solution.py:446
  27.5 1.5 %collective-permute-done.7.refs_1_.refs_3_ = bf16[512,256]{1,0:T(8,128)(2,1)S(1)} collective-permute-done((bf16[512,256]{1,0:T(8,128)(2,1)S(1)}, bf16[512,256]{1,0:T(8,128)(2,1)S(1)}, u32[]{:S(2)}, u32[]{:S(2)}) %collective-permute-start.7) | collective-permute-done | bytes 262176 | tf_op jit(solution)/shard_map/ppermute | solution.py:446
  30.0 1.8 %collective-permute-start.9 = (bf16[128,512]{1,0:T(8,128)(2,1)S(1)}, bf16[128,512]{1,0:T(8,128)(2,1)S(1)}, u32[]{:S(2)}, u32[]{:S(2)}) collective-permute-start(bf16[128,512]{1,0:T(8,128)(2,1)S(1)} %get-tuple-element.53.refs_1_), channel_id=1, source_target_pairs={{0,4},{1,9},{2,6},{3,11},{4,0},{5,13},{6,2},{7,15},{8,12},{9,1},{1... | collective-permute-start | bytes 393224 | tf_op jit(solution)/shard_map/ppermute | solution.py:485
  31.8 1.6 %collective-permute-start.10 = (bf16[144,512]{1,0:T(8,128)(2,1)S(1)}, bf16[144,512]{1,0:T(8,128)(2,1)S(1)}, u32[]{:S(2)}, u32[]{:S(2)}) collective-permute-start(bf16[144,512]{1,0:T(8,128)(2,1)S(1)} %get-tuple-element.62), channel_id=1, source_target_pairs={{0,8},{1,5},{2,10},{3,7},{4,12},{5,1},{6,14},{7,3},{8,0},{9,13},{1... | collective-permute-start | bytes 442376 | tf_op jit(solution)/shard_map/ppermute | solution.py:485
  33.4 2.2 %collective-permute-done.9.refs_7_.refs_2_ = bf16[128,512]{1,0:T(8,128)(2,1)S(1)} collective-permute-done((bf16[128,512]{1,0:T(8,128)(2,1)S(1)}, bf16[128,512]{1,0:T(8,128)(2,1)S(1)}, u32[]{:S(2)}, u32[]{:S(2)}) %collective-permute-start.9) | collective-permute-done | bytes 131104 | tf_op jit(solution)/shard_map/ppermute | solution.py:485
  35.5 2.4 %collective-permute-start.11 = (bf16[128,512]{1,0:T(8,128)(2,1)S(1)}, bf16[128,512]{1,0:T(8,128)(2,1)S(1)}, u32[]{:S(2)}, u32[]{:S(2)}) collective-permute-start(bf16[128,512]{1,0:T(8,128)(2,1)S(1)} %collective-permute-done.9.refs_7_.refs_2_), channel_id=1, source_target_pairs={{0,8},{1,5},{2,10},{3,7},{4,12},{5,1},{6,14},{7,3},{8,0},{9,13},{1... | collective-permute-start | bytes 393224 | tf_op jit(solution)/shard_map/ppermute | solution.py:485
  37.9 1.1 %shard_map.80 = (f32[512,512]{1,0:T(8,128)S(1)}, f32[512,24]{1,0:T(8,128)S(1)}) custom-call(s32[1]{0:T(128)} %bitcast.refs_0_, bf16[512,1024]{1,0:T(8,128)(2,1)S(1)} %shard_map.78.refs_0_.refs_1_, bf16[2,1024,512]{2,1,0:T(8,128)(2,1)S(1)} %get-tuple-element.45.refs_2_, ...), custom_call_target="tpu_custom_call", output_to_operand_aliasing={{0}: (4, {}), {1}: (5, {})} | custom-call | flops 562036736 | bytes 5537796 | tf_op jit(solution)/shard_map/pallas_call | solution.py:41
  39.0 1.9 %collective-permute-done.11.refs_4_ = bf16[128,512]{1,0:T(8,128)(2,1)S(1)} collective-permute-done((bf16[128,512]{1,0:T(8,128)(2,1)S(1)}, bf16[128,512]{1,0:T(8,128)(2,1)S(1)}, u32[]{:S(2)}, u32[]{:S(2)}) %collective-permute-start.11) | collective-permute-done | bytes 131104 | tf_op jit(solution)/shard_map/ppermute | solution.py:485
  41.0 2.8 %collective-permute-start.12 = (bf16[128,512]{1,0:T(8,128)(2,1)S(1)}, bf16[128,512]{1,0:T(8,128)(2,1)S(1)}, u32[]{:S(2)}, u32[]{:S(2)}) collective-permute-start(bf16[128,512]{1,0:T(8,128)(2,1)S(1)} %get-tuple-element.68), channel_id=1, source_target_pairs={{0,16},{4,20},{8,24},{12,28},{16,0},{20,4},{24,8},{28,12},{1,17},{... | collective-permute-start | bytes 393224 | tf_op jit(solution)/shard_map/ppermute | solution.py:449
  43.8 4.0 %shard_map.82 = (f32[512,512]{1,0:T(8,128)S(1)}, bf16[512,512]{1,0:T(8,128)(2,1)S(1)}, bf16[512,512]{1,0:T(8,128)(2,1)}, f32[512,24]{1,0:T(8,128)}) custom-call(s32[1]{0:T(128)} %bitcast.refs_0_, bf16[512,1024]{1,0:T(8,128)(2,1)S(1)} %collective-permute-done.8.refs_1_, bf16[2,1024,512]{2,1,0:T(8,128)(2,1)S(1)} %get-tuple-element.45.refs_2_, ...), custom_call_target="tpu_custom_call" | custom-call | flops 1073741824 | bytes 7176196 | tf_op jit(solution)/shard_map/pallas_call | solution.py:41
  50.0 1.6 %collective-permute-start.22 = (bf16[128,1024]{1,0:T(8,128)(2,1)S(1)}, bf16[128,1024]{1,0:T(8,128)(2,1)S(1)}, u32[]{:S(2)}, u32[]{:S(2)}) collective-permute-start(bf16[128,1024]{1,0:T(8,128)(2,1)S(1)} %shard_map.90), channel_id=1, source_target_pairs={{0,2},{1,3},{2,0},{3,1},{4,6},{5,7},{6,4},{7,5},{8,10},{9,11},{10,... | collective-permute-start | bytes 786440 | tf_op jit(solution)/shard_map/ppermute | solution.py:446
  53.1 1.6 %collective-permute-start.20 = (bf16[128,1024]{1,0:T(8,128)(2,1)S(1)}, bf16[128,1024]{1,0:T(8,128)(2,1)S(1)}, u32[]{:S(2)}, u32[]{:S(2)}) collective-permute-start(bf16[128,1024]{1,0:T(8,128)(2,1)S(1)} %shard_map.88), channel_id=1, source_target_pairs={{0,2},{1,3},{2,0},{3,1},{4,6},{5,7},{6,4},{7,5},{8,10},{9,11},{10,... | collective-permute-start | bytes 786440 | tf_op jit(solution)/shard_map/ppermute | solution.py:446
  57.5 1.6 %collective-permute-start.18 = (bf16[64,1024]{1,0:T(8,128)(2,1)S(1)}, bf16[64,1024]{1,0:T(8,128)(2,1)S(1)}, u32[]{:S(2)}, u32[]{:S(2)}) collective-permute-start(bf16[64,1024]{1,0:T(8,128)(2,1)S(1)} %shard_map.85.refs_12_), channel_id=1, source_target_pairs={{0,2},{1,3},{2,0},{3,1},{4,6},{5,7},{6,4},{7,5},{8,10},{9,11},{10,... | collective-permute-start | bytes 393224 | tf_op jit(solution)/shard_map/ppermute | solution.py:446
  59.1 1.7 %shard_map.86.h_ref = f32[512,1024]{1,0:T(8,128)S(1)} custom-call(bf16[128,512]{1,0:T(8,128)(2,1)S(1)} %shard_map.83.refs_3_.refs_0_, bf16[128,512]{1,0:T(8,128)(2,1)S(1)} %collective-permute-done.13.refs_1_, bf16[128,512]{1,0:T(8,128)(2,1)S(1)} %get-tuple-element.69.refs_2_.refs_0_, bf16[128,512]{1,0:T(8,128)(2,1)S(1)} %collective-permute-done.14.refs_3_.refs_1_, ...), custom_call_target="tpu_custom_call" | custom-call | tf_op jit(solution)/shard_map/pallas_call | solution.py:41
  61.6 3.3 %collective-permute-done.21.a_ref = bf16[128,1024]{1,0:T(8,128)(2,1)S(1)} collective-permute-done((bf16[128,1024]{1,0:T(8,128)(2,1)S(1)}, bf16[128,1024]{1,0:T(8,128)(2,1)S(1)}, u32[]{:S(2)}, u32[]{:S(2)}) %collective-permute-start.21) | collective-permute-done | bytes 262176 | tf_op jit(solution)/shard_map/ppermute | solution.py:446
  65.6 4.9 %collective-permute-done.20.a_ref = bf16[128,1024]{1,0:T(8,128)(2,1)S(1)} collective-permute-done((bf16[128,1024]{1,0:T(8,128)(2,1)S(1)}, bf16[128,1024]{1,0:T(8,128)(2,1)S(1)}, u32[]{:S(2)}, u32[]{:S(2)}) %collective-permute-start.20) | collective-permute-done | bytes 262176 | tf_op jit(solution)/shard_map/ppermute | solution.py:446
  71.2 2.1 %collective-permute-done.19.a_ref = bf16[64,1024]{1,0:T(8,128)(2,1)S(1)} collective-permute-done((bf16[64,1024]{1,0:T(8,128)(2,1)S(1)}, bf16[64,1024]{1,0:T(8,128)(2,1)S(1)}, u32[]{:S(2)}, u32[]{:S(2)}) %collective-permute-start.19) | collective-permute-done | bytes 131104 | tf_op jit(solution)/shard_map/ppermute | solution.py:446
  73.9 1.5 %collective-permute-done.18.a_ref = bf16[64,1024]{1,0:T(8,128)(2,1)S(1)} collective-permute-done((bf16[64,1024]{1,0:T(8,128)(2,1)S(1)}, bf16[64,1024]{1,0:T(8,128)(2,1)S(1)}, u32[]{:S(2)}, u32[]{:S(2)}) %collective-permute-start.18) | collective-permute-done | bytes 131104 | tf_op jit(solution)/shard_map/ppermute | solution.py:446
  (47 shorter events, 14.4 us)
Async XLA Ops:
  0.0 3.0 %collective-permute-start.1 = (bf16[512,1024]{1,0:T(8,128)(2,1)}, bf16[512,1024]{1,0:T(8,128)(2,1)S(1)}, u32[]{:S(2)}, u32[]{:S(2)}) collective-permute-start(bf16[512,1024]{1,0:T(8,128)(2,1)} %refs_2_.1), channel_id=1, source_target_pairs={{0,1},{1,0},{2,3},{3,2},{4,5},{5,4},{6,7},{7,6},{8,9},{9,8},{10,11... | collective-permute-start | bytes 3145736 | tf_op jit(solution)/shard_map/ppermute | solution.py:446
  0.5 26.6 %collective-permute-start = (bf16[512,1024]{1,0:T(8,128)(2,1)}, bf16[512,1024]{1,0:T(8,128)(2,1)S(1)}, u32[]{:S(2)}, u32[]{:S(2)}) collective-permute-start(bf16[512,1024]{1,0:T(8,128)(2,1)} %refs_2_.1), channel_id=1, source_target_pairs={{0,2},{1,3},{2,0},{3,1},{4,6},{5,7},{6,4},{7,5},{8,10},{9,11},{10,... | collective-permute-start | bytes 3145736 | tf_op jit(solution)/shard_map/ppermute | solution.py:446
  3.0 0.7 copy-start
  9.0 18.0 %collective-permute-start.4 = (bf16[512,1024]{1,0:T(8,128)(2,1)S(1)}, bf16[512,1024]{1,0:T(8,128)(2,1)S(1)}, u32[]{:S(2)}, u32[]{:S(2)}) collective-permute-start(bf16[512,1024]{1,0:T(8,128)(2,1)S(1)} %get-tuple-element.42), channel_id=1, source_target_pairs={{0,1},{1,0},{2,3},{3,2},{4,5},{5,4},{6,7},{7,6},{8,9},{9,8},{10,11... | collective-permute-start | bytes 3145736 | tf_op jit(solution)/shard_map/ppermute | solution.py:446
  9.5 17.6 %collective-permute-start.5 = (bf16[512,1024]{1,0:T(8,128)(2,1)S(1)}, bf16[512,1024]{1,0:T(8,128)(2,1)S(1)}, u32[]{:S(2)}, u32[]{:S(2)}) collective-permute-start(bf16[512,1024]{1,0:T(8,128)(2,1)S(1)} %get-tuple-element.43), channel_id=1, source_target_pairs={{0,1},{1,0},{2,3},{3,2},{4,5},{5,4},{6,7},{7,6},{8,9},{9,8},{10,11... | collective-permute-start | bytes 3145736 | tf_op jit(solution)/shard_map/ppermute | solution.py:446
  9.6 17.4 %collective-permute-start.6 = (bf16[1024,256]{1,0:T(8,128)(2,1)S(1)}, bf16[1024,256]{1,0:T(8,128)(2,1)S(1)}, u32[]{:S(2)}, u32[]{:S(2)}) collective-permute-start(bf16[1024,256]{1,0:T(8,128)(2,1)S(1)} %get-tuple-element.44), channel_id=1, source_target_pairs={{0,1},{1,0},{2,3},{3,2},{4,5},{5,4},{6,7},{7,6},{8,9},{9,8},{10,11... | collective-permute-start | bytes 1572872 | tf_op jit(solution)/shard_map/ppermute | solution.py:446
  10.0 4.3 %collective-permute-start.2 = (f32[8,512]{1,0:T(8,128)S(1)}, f32[8,512]{1,0:T(8,128)S(1)}, u32[]{:S(2)}, u32[]{:S(2)}) collective-permute-start(f32[8,512]{1,0:T(8,128)S(1)} %get-tuple-element.40.refs_0_), channel_id=1, source_target_pairs={{0,4},{4,0},{8,12},{12,8},{16,20},{20,16},{24,28},{28,24},{1,5},{5... | collective-permute-start | bytes 49160 | tf_op jit(solution)/shard_map/ppermute | solution.py:449
  14.3 3.8 %collective-permute-start.3 = (f32[8,512]{1,0:T(8,128)S(1)}, f32[8,512]{1,0:T(8,128)S(1)}, u32[]{:S(2)}, u32[]{:S(2)}) collective-permute-start(f32[8,512]{1,0:T(8,128)S(1)} %shard_map.74.refs_1_), channel_id=1, source_target_pairs={{0,8},{4,12},{8,0},{12,4},{16,24},{20,28},{24,16},{28,20},{1,9},{5... | collective-permute-start | bytes 49160 | tf_op jit(solution)/shard_map/ppermute | solution.py:449
  27.5 1.6 %collective-permute-start.7 = (bf16[512,256]{1,0:T(8,128)(2,1)S(1)}, bf16[512,256]{1,0:T(8,128)(2,1)S(1)}, u32[]{:S(2)}, u32[]{:S(2)}) collective-permute-start(bf16[512,256]{1,0:T(8,128)(2,1)S(1)} %shard_map.77), channel_id=1, source_target_pairs={{0,1},{1,0},{2,3},{3,2},{4,5},{5,4},{6,7},{7,6},{8,9},{9,8},{10,11... | collective-permute-start | bytes 786440 | tf_op jit(solution)/shard_map/ppermute | solution.py:446
  29.1 14.8 %collective-permute-start.8 = (bf16[512,1024]{1,0:T(8,128)(2,1)S(1)}, bf16[512,1024]{1,0:T(8,128)(2,1)S(1)}, u32[]{:S(2)}, u32[]{:S(2)}) collective-permute-start(bf16[512,1024]{1,0:T(8,128)(2,1)S(1)} %shard_map.78.refs_0_.refs_1_), channel_id=1, source_target_pairs={{0,1},{1,0},{2,3},{3,2},{4,5},{5,4},{6,7},{7,6},{8,9},{9,8},{10,11... | collective-permute-start | bytes 3145736 | tf_op jit(solution)/shard_map/ppermute | solution.py:446
  30.0 5.5 %collective-permute-start.9 = (bf16[128,512]{1,0:T(8,128)(2,1)S(1)}, bf16[128,512]{1,0:T(8,128)(2,1)S(1)}, u32[]{:S(2)}, u32[]{:S(2)}) collective-permute-start(bf16[128,512]{1,0:T(8,128)(2,1)S(1)} %get-tuple-element.53.refs_1_), channel_id=1, source_target_pairs={{0,4},{1,9},{2,6},{3,11},{4,0},{5,13},{6,2},{7,15},{8,12},{9,1},{1... | collective-permute-start | bytes 393224 | tf_op jit(solution)/shard_map/ppermute | solution.py:485
  31.8 7.2 %collective-permute-start.10 = (bf16[144,512]{1,0:T(8,128)(2,1)S(1)}, bf16[144,512]{1,0:T(8,128)(2,1)S(1)}, u32[]{:S(2)}, u32[]{:S(2)}) collective-permute-start(bf16[144,512]{1,0:T(8,128)(2,1)S(1)} %get-tuple-element.62), channel_id=1, source_target_pairs={{0,8},{1,5},{2,10},{3,7},{4,12},{5,1},{6,14},{7,3},{8,0},{9,13},{1... | collective-permute-start | bytes 442376 | tf_op jit(solution)/shard_map/ppermute | solution.py:485
  35.5 5.3 %collective-permute-start.11 = (bf16[128,512]{1,0:T(8,128)(2,1)S(1)}, bf16[128,512]{1,0:T(8,128)(2,1)S(1)}, u32[]{:S(2)}, u32[]{:S(2)}) collective-permute-start(bf16[128,512]{1,0:T(8,128)(2,1)S(1)} %collective-permute-done.9.refs_7_.refs_2_), channel_id=1, source_target_pairs={{0,8},{1,5},{2,10},{3,7},{4,12},{5,1},{6,14},{7,3},{8,0},{9,13},{1... | collective-permute-start | bytes 393224 | tf_op jit(solution)/shard_map/ppermute | solution.py:485
  41.0 6.8 %collective-permute-start.12 = (bf16[128,512]{1,0:T(8,128)(2,1)S(1)}, bf16[128,512]{1,0:T(8,128)(2,1)S(1)}, u32[]{:S(2)}, u32[]{:S(2)}) collective-permute-start(bf16[128,512]{1,0:T(8,128)(2,1)S(1)} %get-tuple-element.68), channel_id=1, source_target_pairs={{0,16},{4,20},{8,24},{12,28},{16,0},{20,4},{24,8},{28,12},{1,17},{... | collective-permute-start | bytes 393224 | tf_op jit(solution)/shard_map/ppermute | solution.py:449
  48.1 1.4 %collective-permute-start.13 = (bf16[128,512]{1,0:T(8,128)(2,1)S(1)}, bf16[128,512]{1,0:T(8,128)(2,1)S(1)}, u32[]{:S(2)}, u32[]{:S(2)}) collective-permute-start(bf16[128,512]{1,0:T(8,128)(2,1)S(1)} %shard_map.83.refs_3_.refs_0_), channel_id=1, source_target_pairs={{0,1},{1,0},{2,3},{3,2},{4,5},{5,4},{6,7},{7,6},{8,9},{9,8},{10,11... | collective-permute-start | bytes 393224 | tf_op jit(solution)/shard_map/ppermute | solution.py:446
  48.8 2.8 %collective-permute-start.14 = (bf16[128,512]{1,0:T(8,128)(2,1)S(1)}, bf16[128,512]{1,0:T(8,128)(2,1)S(1)}, u32[]{:S(2)}, u32[]{:S(2)}) collective-permute-start(bf16[128,512]{1,0:T(8,128)(2,1)S(1)} %get-tuple-element.69.refs_2_.refs_0_), channel_id=1, source_target_pairs={{0,1},{1,0},{2,3},{3,2},{4,5},{5,4},{6,7},{7,6},{8,9},{9,8},{10,11... | collective-permute-start | bytes 393224 | tf_op jit(solution)/shard_map/ppermute | solution.py:446
  49.3 3.3 %collective-permute-start.15 = (bf16[128,512]{1,0:T(8,128)(2,1)S(1)}, bf16[128,512]{1,0:T(8,128)(2,1)S(1)}, u32[]{:S(2)}, u32[]{:S(2)}) collective-permute-start(bf16[128,512]{1,0:T(8,128)(2,1)S(1)} %get-tuple-element.70.refs_4_.refs_0_), channel_id=1, source_target_pairs={{0,1},{1,0},{2,3},{3,2},{4,5},{5,4},{6,7},{7,6},{8,9},{9,8},{10,11... | collective-permute-start | bytes 393224 | tf_op jit(solution)/shard_map/ppermute | solution.py:446
  50.0 10.8 %collective-permute-start.22 = (bf16[128,1024]{1,0:T(8,128)(2,1)S(1)}, bf16[128,1024]{1,0:T(8,128)(2,1)S(1)}, u32[]{:S(2)}, u32[]{:S(2)}) collective-permute-start(bf16[128,1024]{1,0:T(8,128)(2,1)S(1)} %shard_map.90), channel_id=1, source_target_pairs={{0,2},{1,3},{2,0},{3,1},{4,6},{5,7},{6,4},{7,5},{8,10},{9,11},{10,... | collective-permute-start | bytes 786440 | tf_op jit(solution)/shard_map/ppermute | solution.py:446
  52.1 12.7 %collective-permute-start.21 = (bf16[128,1024]{1,0:T(8,128)(2,1)S(1)}, bf16[128,1024]{1,0:T(8,128)(2,1)S(1)}, u32[]{:S(2)}, u32[]{:S(2)}) collective-permute-start(bf16[128,1024]{1,0:T(8,128)(2,1)S(1)} %shard_map.89), channel_id=1, source_target_pairs={{0,2},{1,3},{2,0},{3,1},{4,6},{5,7},{6,4},{7,5},{8,10},{9,11},{10,... | collective-permute-start | bytes 786440 | tf_op jit(solution)/shard_map/ppermute | solution.py:446
  53.1 17.3 %collective-permute-start.20 = (bf16[128,1024]{1,0:T(8,128)(2,1)S(1)}, bf16[128,1024]{1,0:T(8,128)(2,1)S(1)}, u32[]{:S(2)}, u32[]{:S(2)}) collective-permute-start(bf16[128,1024]{1,0:T(8,128)(2,1)S(1)} %shard_map.88), channel_id=1, source_target_pairs={{0,2},{1,3},{2,0},{3,1},{4,6},{5,7},{6,4},{7,5},{8,10},{9,11},{10,... | collective-permute-start | bytes 786440 | tf_op jit(solution)/shard_map/ppermute | solution.py:446
  54.7 1.3 %collective-permute-start.16 = (bf16[64,512]{1,0:T(8,128)(2,1)S(1)}, bf16[64,512]{1,0:T(8,128)(2,1)S(1)}, u32[]{:S(2)}, u32[]{:S(2)}) collective-permute-start(bf16[64,512]{1,0:T(8,128)(2,1)S(1)} %get-tuple-element.71.refs_6_.refs_0_), channel_id=1, source_target_pairs={{0,1},{1,0},{2,3},{3,2},{4,5},{5,4},{6,7},{7,6},{8,9},{9,8},{10,11... | collective-permute-start | bytes 196616 | tf_op jit(solution)/shard_map/ppermute | solution.py:446
  54.7 2.3 %collective-permute-start.17 = (bf16[64,512]{1,0:T(8,128)(2,1)S(1)}, bf16[64,512]{1,0:T(8,128)(2,1)S(1)}, u32[]{:S(2)}, u32[]{:S(2)}) collective-permute-start(bf16[64,512]{1,0:T(8,128)(2,1)S(1)} %get-tuple-element.72.refs_0_.refs_8_), channel_id=1, source_target_pairs={{0,1},{1,0},{2,3},{3,2},{4,5},{5,4},{6,7},{7,6},{8,9},{9,8},{10,11... | collective-permute-start | bytes 196616 | tf_op jit(solution)/shard_map/ppermute | solution.py:446
  56.5 16.8 %collective-permute-start.19 = (bf16[64,1024]{1,0:T(8,128)(2,1)S(1)}, bf16[64,1024]{1,0:T(8,128)(2,1)S(1)}, u32[]{:S(2)}, u32[]{:S(2)}) collective-permute-start(bf16[64,1024]{1,0:T(8,128)(2,1)S(1)} %shard_map.87), channel_id=1, source_target_pairs={{0,2},{1,3},{2,0},{3,1},{4,6},{5,7},{6,4},{7,5},{8,10},{9,11},{10,... | collective-permute-start | bytes 393224 | tf_op jit(solution)/shard_map/ppermute | solution.py:446
  57.5 17.9 %collective-permute-start.18 = (bf16[64,1024]{1,0:T(8,128)(2,1)S(1)}, bf16[64,1024]{1,0:T(8,128)(2,1)S(1)}, u32[]{:S(2)}, u32[]{:S(2)}) collective-permute-start(bf16[64,1024]{1,0:T(8,128)(2,1)S(1)} %shard_map.85.refs_12_), channel_id=1, source_target_pairs={{0,2},{1,3},{2,0},{3,1},{4,6},{5,7},{6,4},{7,5},{8,10},{9,11},{10,... | collective-permute-start | bytes 393224 | tf_op jit(solution)/shard_map/ppermute | solution.py:446

commit v9 on v8

--- a/solution.py
+++ b/solution.py
@@ -154,7 +154,7 @@
     return call(kernel, [slab, here, there], [shape(here.shape, F32)] * 5, 0, smem=1)
 
 
-def join_four(me, mine, first, second, diagonal, factors, after):
+def join_four(me, mine, first, second, diagonal, factors):
     rows = mine.shape[0]
 
     def kernel(me_ref, m_ref, x_ref, y_ref, d_ref, f_ref, four_ref, pair_ref, beside_ref):
@@ -168,7 +168,7 @@
         pair_ref[...] = (f[4] * a + f[5] * d).astype(BF16)
 
     outs = [shape(mine.shape, BF16)] * 3
-    return call(kernel, [me, mine, first, second, diagonal, factors], outs, 0, after, smem=1)
+    return call(kernel, [me, mine, first, second, diagonal, factors], outs, 0, smem=1)
 
 
 def combine(state, other, own_factor, other_factor, after):
@@ -256,31 +256,25 @@
     return dot_dims(x, wl_ref[:, pl.ds(start, shard)], 1, 1)
 
 
-def project(me, place, x, wq, wl, total_q, total_l, after):
-    def kernel(me_ref, x_ref, wq_ref, wl_ref, q_ref, l_ref, q_out, l_out):
-        q_out[...] = q_ref[...] + dot(x_ref[...], wq_ref[place - 2])
-        l_out[...] = l_ref[...] + add_levels(me_ref, place, x_ref[...], wl_ref)
-
-    outs = [shape(t.shape, F32) for t in (total_q, total_l)]
-    flops = 2 * x.size * (total_q.shape[1] + total_l.shape[1])
-    return call(kernel, [me, x, wq, wl, total_q, total_l], outs, flops, after, smem=1, aliases={4: 0, 5: 1})
-
-
-def partial(x, w):
-    def kernel(x_ref, w_ref, o_ref):
-        o_ref[...] = dot(x_ref[...], w_ref[...]).astype(BF16)
-
-    return call(kernel, [x, w], [shape((x.shape[0], w.shape[1]), BF16)], 0)[0]
-
-
-def project_state(x, wkv, total_kv, from_near, keep, head_size):
+def project(me, place, x, wq, wkv, wl, totals, after=()):
+    def kernel(me_ref, x_ref, q_ref, kv_ref, l_ref, *refs):
+        ins, outs = refs[:3], refs[3:]
+        outs[1][...] = ins[1][...] + dot(x_ref[...], kv_ref[...])
+        outs[0][...] = ins[0][...] + dot(x_ref[...], q_ref[place - 2])
+        outs[2][...] = ins[2][...] + add_levels(me_ref, place, x_ref[...], l_ref)
+
+    outs = [shape(t.shape, F32) for t in totals]
+    return call(kernel, [me, x, wq, wkv, wl, *totals], outs, 0, after, smem=1, aliases={5: 0, 6: 1, 7: 2})
+
+
+def project_state(x, wkv, total_kv, keep, head_size):
     rows = x.shape[0]
     heads = keep.shape[1]
     kv_width = wkv.shape[1] // 2
     group = heads // (kv_width // head_size)
 
-    def kernel(x_ref, w_ref, total_ref, near_ref, keep_ref, k_out, v_out, s_out, wide_out):
-        total = total_ref[...] + near_ref[...].astype(F32) + dot(x_ref[...], w_ref[...])
+    def kernel(x_ref, w_ref, total_ref, keep_ref, k_out, v_out, s_out, wide_out):
+        total = total_ref[...] + dot(x_ref[...], w_ref[...])
         keys = total[:, :kv_width].astype(BF16)
         values = total[:, kv_width:].astype(BF16)
         k_out[...] = keys
@@ -304,21 +298,20 @@
         shape((head_size, heads * head_size), BF16),
         shape((head_size + 16, heads * head_size), BF16),
     ]
-    return call(kernel, [x, wkv, total_kv, from_near, keep], outs, 0)
-
-
-def attend(me, place, xs, wq, wl, total_q, total_l, k, v, dcol, drow, spans, states, head_size, level_count):
+    return call(kernel, [x, wkv, total_kv, keep], outs, 0)
+
+
+def attend(me, place, x, wq, wl, total_q, total_l, k, v, dcol, drow, spans, states, head_size, level_count):
     rows, width = total_q.shape
     bits = len(spans)
     heads = width // head_size
     group = heads // (k.shape[1] // head_size)
     own_levels = level_count - bits
 
-    def kernel(me_ref, *refs):
-        x = jnp.concatenate([x_ref[...] for x_ref in refs[: len(xs)]], axis=1)
-        refs = refs[len(xs) :]
-        wq_ref, wl_ref, tq_ref, tl_ref, k_ref, v_ref, dcol_ref, drow_ref = refs[:8]
-        span_refs, state_refs = refs[8 : 8 + bits], refs[8 + bits : 7 + 2 * bits]
+    def kernel(me_ref, x_ref, wq_ref, wl_ref, *refs):
+        x = x_ref[...]
+        tq_ref, tl_ref, k_ref, v_ref, dcol_ref, drow_ref = refs[:6]
+        span_refs, state_refs = refs[6 : 6 + bits], refs[6 + bits : 5 + 2 * bits]
         o_ref, s_ref, q_ref, l_ref = refs[-4:]
         raw = tl_ref[...] + add_levels(me_ref, place, x, wl_ref)
         l_ref[...] = jnp.maximum(raw, 0.0) + jnp.log1p(jnp.exp(-jnp.abs(raw)))
@@ -364,7 +357,7 @@
                         total = total + dot_dims(scaled, state_refs[b][:, cols], 1, 1)
                 o_ref[here, cols] = total
 
-    ins = [me, *xs, wq, wl, total_q, total_l, k, v, dcol, drow, *spans, *states]
+    ins = [me, x, wq, wl, total_q, total_l, k, v, dcol, drow, *spans, *states]
     wide = shape((rows, width), BF16)
     outs = [shape((rows, width), F32), wide, wide, shape(total_l.shape, F32)]
     flops = 2 * rows * wq.shape[1] * width + 4 * rows * rows * width
@@ -466,14 +459,11 @@
         spans.append(span)
         factors.append((own, other))
 
-    wq, wkv, wkv_send, wl = ws
-    wkv_near = swap_tp(wkv_send, 1)
+    wq, wkv, wkv_near, wl = ws
     arrived = gate(far, total, w_far, w_here)
-    from_near = swap_tp(partial(arrived, wkv_near), 1)
-    arrived = gate(arrived, from_near)
-    arrived_near = [swap_tp(arrived, 1)]
-    total_q, total_kv, total_l = totals
-    k, v, state, state_wide = project_state(arrived, wkv, total_kv, from_near, keep, head_size)
+    arrived_near = swap_tp(arrived, 1)
+    total_q, total_kv, total_l = project(me, 2, arrived, wq, wkv, wl, totals)
+    k, v, state, state_wide = project_state(arrived_near, wkv_near, total_kv, keep, head_size)
 
     def swap_group(x, bits):
         tp_size = lax.axis_size("tp")
@@ -487,8 +477,7 @@
     first = swap_group(state, (1, 2))
     second = swap_group(state_wide, (2, 1))
     diagonal = swap_group(first, (2, 1))
-    total_q, total_l = project(me, 2, arrived, wq, wl, total_q, total_l, (k, first))
-    state, other_pair, beside = join_four(me, state, first, second, diagonal, four_factors, (total_l,))
+    state, other_pair, beside = join_four(me, state, first, second, diagonal, four_factors)
     earlier = [beside, other_pair]
     for b in range(2, seq_bits):
         other = swap_seq(state, 1 << b)

time: 76.3 us -> 77.6 us (1.017)
  waiting for transfers between devices: 29.9 us -> 31.4 us
    ppermute x3, waiting for transfers between devices: 4.02 us -> 5.53 us  [swap_group(): return lax.ppermute(x, ('seq', 'tp'), pairs)]
    ppermute x17 -> x15, waiting for transfers between devices: 22.4 us -> 22.1 us  [swap_tp(): return lax.ppermute(x, 'tp', [(i, i ^ bit) for i in range(4)])]
    ppermute x17 -> x15, starting transfers between devices: 11.2 us -> 11 us  [swap_tp(): return lax.ppermute(x, 'tp', [(i, i ^ bit) for i in range(4)])]
    pallas_call x16 -> x15, Pallas kernels: 17.4 us -> 17.3 us  [call(): pl.pallas_call(run, in_specs=[SMEM] * smem + [HBM] * hbm + [VMEM] * (coun...]
  transfers between devices with their start and end apart: 23 -> 21, of which waited for: 12 -> 13; matrix products, arithmetic and copies ran while one was open for 0% -> 0% of each run, Pallas kernels for 26% -> 24%
where the time goes in v9:
time: 77.6 us; the launch traced here: 77.4 us
  waiting for transfers between devices  31.4 us (40%)
  starting transfers between devices  24.4 us (31%)
  Pallas kernels  20.8 us (27%)
    ppermute x15, waiting for transfers between devices, swap_tp(): return lax.ppermute(x, 'tp', [(i, i ^ bit) for i in range(4)])  22.1 us
    pallas_call x15, Pallas kernels, call(): pl.pallas_call(run, in_specs=[SMEM] * smem + [HBM] * hbm + [VMEM] * (coun...  17.3 us
    ppermute x15, starting transfers between devices, swap_tp(): return lax.ppermute(x, 'tp', [(i, i ^ bit) for i in range(4)])  11 us
    ppermute x3, starting transfers between devices, swap_seq(): return lax.ppermute(x, 'seq', [(i, i ^ bit) for i in range(seq_size)])  8.18 us
    ppermute x3, waiting for transfers between devices, swap_group(): return lax.ppermute(x, ('seq', 'tp'), pairs)  5.53 us
    ppermute x3, starting transfers between devices, swap_group(): return lax.ppermute(x, ('seq', 'tp'), pairs)  5.23 us
    ppermute x3, waiting for transfers between devices, swap_seq(): return lax.ppermute(x, 'seq', [(i, i ^ bit) for i in range(seq_size)])  3.75 us
    pallas_call x5, Pallas kernels, add_rows(): pl.pallas_call(kernel, grid=(rows // unit,), in_specs=specs, out_specs=pl...  3.56 us
  transfers between devices with their start and end apart: 21, of which 13 were waited for; matrix products, arithmetic and copies ran while one was open for 0% of the time, Pallas kernels for 24%

profile of v9, /device:TPU:0, one launch (start us, length us, event | category | flops | bytes accessed | tf_op | source)
XLA Modules:
  0.0 77.4 jit_solution(14024891618588523418)
XLA Ops:
  0.5 2.5 %collective-permute-start = (bf16[512,1024]{1,0:T(8,128)(2,1)}, bf16[512,1024]{1,0:T(8,128)(2,1)S(1)}, u32[]{:S(2)}, u32[]{:S(2)}) collective-permute-start(bf16[512,1024]{1,0:T(8,128)(2,1)} %refs_2_.1), channel_id=1, source_target_pairs={{0,2},{1,3},{2,0},{3,1},{4,6},{5,7},{6,4},{7,5},{8,10},{9,11},{10,... | collective-permute-start | bytes 3145736 | tf_op jit(solution)/shard_map/ppermute | solution.py:439
  3.7 5.4 %shard_map.73 = (f32[512,512]{1,0:T(8,128)S(1)}, f32[512,256]{1,0:T(8,128)S(1)}, f32[512,24]{1,0:T(8,128)S(1)}, bf16[2,1024,512]{2,1,0:T(8,128)(2,1)S(1)}, bf16[...) custom-call(s32[1]{0:T(128)} %bitcast.refs_0_, ...), custom_call_target="tpu_custom_call" | custom-call | tf_op jit(solution)/shard_map/pallas_call | solution.py:41
  9.6 2.8 %collective-permute-start.2 = (f32[8,512]{1,0:T(8,128)S(1)}, f32[8,512]{1,0:T(8,128)S(1)}, u32[]{:S(2)}, u32[]{:S(2)}) collective-permute-start(f32[8,512]{1,0:T(8,128)S(1)} %get-tuple-element.41.refs_0_), channel_id=1, source_target_pairs={{0,4},{4,0},{8,12},{12,8},{16,20},{20,16},{24,28},{28,24},{1,5},{5... | collective-permute-start | bytes 49160 | tf_op jit(solution)/shard_map/ppermute | solution.py:442
  12.5 1.7 %collective-permute-done.2.refs_1_ = f32[8,512]{1,0:T(8,128)S(1)} collective-permute-done((f32[8,512]{1,0:T(8,128)S(1)}, f32[8,512]{1,0:T(8,128)S(1)}, u32[]{:S(2)}, u32[]{:S(2)}) %collective-permute-start.2) | collective-permute-done | bytes 16416 | tf_op jit(solution)/shard_map/ppermute | solution.py:442
  14.2 2.1 %collective-permute-start.3 = (f32[8,512]{1,0:T(8,128)S(1)}, f32[8,512]{1,0:T(8,128)S(1)}, u32[]{:S(2)}, u32[]{:S(2)}) collective-permute-start(f32[8,512]{1,0:T(8,128)S(1)} %shard_map.74.refs_1_), channel_id=1, source_target_pairs={{0,8},{4,12},{8,0},{12,4},{16,24},{20,28},{24,16},{28,20},{1,9},{5... | collective-permute-start | bytes 49160 | tf_op jit(solution)/shard_map/ppermute | solution.py:442
  16.3 1.7 %collective-permute-done.3.refs_2_ = f32[8,512]{1,0:T(8,128)S(1)} collective-permute-done((f32[8,512]{1,0:T(8,128)S(1)}, f32[8,512]{1,0:T(8,128)S(1)}, u32[]{:S(2)}, u32[]{:S(2)}) %collective-permute-start.3) | collective-permute-done | bytes 16416 | tf_op jit(solution)/shard_map/ppermute | solution.py:442
  18.6 8.4 %collective-permute-done.refs_0_ = bf16[512,1024]{1,0:T(8,128)(2,1)S(1)} collective-permute-done((bf16[512,1024]{1,0:T(8,128)(2,1)}, bf16[512,1024]{1,0:T(8,128)(2,1)S(1)}, u32[]{:S(2)}, u32[]{:S(2)}) %collective-permute-start) | collective-permute-done | bytes 1048608 | tf_op jit(solution)/shard_map/ppermute | solution.py:439
  27.1 1.3 %shard_map.77 = (f32[512,512]{1,0:T(8,128)S(1)}, f32[512,256]{1,0:T(8,128)S(1)}, f32[512,24]{1,0:T(8,128)S(1)}) custom-call(s32[1]{0:T(128)} %bitcast.refs_0_, bf16[512,1024]{1,0:T(8,128)(2,1)S(1)} %shard_map.76.refs_1_, bf16[2,1024,512]{2,1,0:T(8,128)(2,1)S(1)} %get-tuple-element.45.refs_2_, ...), custom_call_target="tpu_custom_call", output_to_operand_aliasing={{0}: (5, {}), {1}: (6, {}), {2}: (7, {})} | custom-call | tf_op jit(solution)/shard_map/pallas_call | solution.py:41
  28.4 1.3 %collective-permute-done.6.refs_0_.refs_1_ = bf16[512,1024]{1,0:T(8,128)(2,1)S(1)} collective-permute-done((bf16[512,1024]{1,0:T(8,128)(2,1)S(1)}, bf16[512,1024]{1,0:T(8,128)(2,1)S(1)}, u32[]{:S(2)}, u32[]{:S(2)}) %collective-permute-start.6) | collective-permute-done | bytes 1048608 | tf_op jit(solution)/shard_map/ppermute | solution.py:439
  30.5 1.8 %collective-permute-start.7 = (bf16[128,512]{1,0:T(8,128)(2,1)S(1)}, bf16[128,512]{1,0:T(8,128)(2,1)S(1)}, u32[]{:S(2)}, u32[]{:S(2)}) collective-permute-start(bf16[128,512]{1,0:T(8,128)(2,1)S(1)} %get-tuple-element.63.refs_1_), channel_id=1, source_target_pairs={{0,4},{1,9},{2,6},{3,11},{4,0},{5,13},{6,2},{7,15},{8,12},{9,1},{1... | collective-permute-start | bytes 393224 | tf_op jit(solution)/shard_map/ppermute | solution.py:475
  32.3 1.6 %collective-permute-start.8 = (bf16[144,512]{1,0:T(8,128)(2,1)S(1)}, bf16[144,512]{1,0:T(8,128)(2,1)S(1)}, u32[]{:S(2)}, u32[]{:S(2)}) collective-permute-start(bf16[144,512]{1,0:T(8,128)(2,1)S(1)} %get-tuple-element.64), channel_id=1, source_target_pairs={{0,8},{1,5},{2,10},{3,7},{4,12},{5,1},{6,14},{7,3},{8,0},{9,13},{1... | collective-permute-start | bytes 442376 | tf_op jit(solution)/shard_map/ppermute | solution.py:475
  33.9 2.4 %collective-permute-done.7.refs_2_ = bf16[128,512]{1,0:T(8,128)(2,1)S(1)} collective-permute-done((bf16[128,512]{1,0:T(8,128)(2,1)S(1)}, bf16[128,512]{1,0:T(8,128)(2,1)S(1)}, u32[]{:S(2)}, u32[]{:S(2)}) %collective-permute-start.7) | collective-permute-done | bytes 131104 | tf_op jit(solution)/shard_map/ppermute | solution.py:475
  36.3 1.9 %collective-permute-start.9 = (bf16[128,512]{1,0:T(8,128)(2,1)S(1)}, bf16[128,512]{1,0:T(8,128)(2,1)S(1)}, u32[]{:S(2)}, u32[]{:S(2)}) collective-permute-start(bf16[128,512]{1,0:T(8,128)(2,1)S(1)} %collective-permute-done.7.refs_2_), channel_id=1, source_target_pairs={{0,8},{1,5},{2,10},{3,7},{4,12},{5,1},{6,14},{7,3},{8,0},{9,13},{1... | collective-permute-start | bytes 393224 | tf_op jit(solution)/shard_map/ppermute | solution.py:475
  38.2 3.1 %collective-permute-done.9.refs_4_ = bf16[128,512]{1,0:T(8,128)(2,1)S(1)} collective-permute-done((bf16[128,512]{1,0:T(8,128)(2,1)S(1)}, bf16[128,512]{1,0:T(8,128)(2,1)S(1)}, u32[]{:S(2)}, u32[]{:S(2)}) %collective-permute-start.9) | collective-permute-done | bytes 131104 | tf_op jit(solution)/shard_map/ppermute | solution.py:475
  41.5 3.2 %collective-permute-start.10 = (bf16[128,512]{1,0:T(8,128)(2,1)S(1)}, bf16[128,512]{1,0:T(8,128)(2,1)S(1)}, u32[]{:S(2)}, u32[]{:S(2)}) collective-permute-start(bf16[128,512]{1,0:T(8,128)(2,1)S(1)} %get-tuple-element.70), channel_id=1, source_target_pairs={{0,16},{4,20},{8,24},{12,28},{16,0},{20,4},{24,8},{28,12},{1,17},{... | collective-permute-start | bytes 393224 | tf_op jit(solution)/shard_map/ppermute | solution.py:442
  44.7 4.0 %shard_map.80 = (f32[512,512]{1,0:T(8,128)S(1)}, bf16[512,512]{1,0:T(8,128)(2,1)S(1)}, bf16[512,512]{1,0:T(8,128)(2,1)}, f32[512,24]{1,0:T(8,128)}) custom-call(s32[1]{0:T(128)} %bitcast.refs_0_, bf16[512,1024]{1,0:T(8,128)(2,1)S(1)} %collective-permute-done.6.refs_0_.refs_1_, bf16[2,1024,512]{2,1,0:T(8,128)(2,1)S(1)} %get-tuple-element.45.refs_2_, ...), custom_call_target="tpu_custom_call" | custom-call | flops 1073741824 | bytes 7176196 | tf_op jit(solution)/shard_map/pallas_call | solution.py:41
  51.3 1.8 %collective-permute-start.20 = (bf16[128,1024]{1,0:T(8,128)(2,1)S(1)}, bf16[128,1024]{1,0:T(8,128)(2,1)S(1)}, u32[]{:S(2)}, u32[]{:S(2)}) collective-permute-start(bf16[128,1024]{1,0:T(8,128)(2,1)S(1)} %shard_map.88), channel_id=1, source_target_pairs={{0,2},{1,3},{2,0},{3,1},{4,6},{5,7},{6,4},{7,5},{8,10},{9,11},{10,... | collective-permute-start | bytes 786440 | tf_op jit(solution)/shard_map/ppermute | solution.py:439
  54.4 1.8 %collective-permute-start.18 = (bf16[128,1024]{1,0:T(8,128)(2,1)S(1)}, bf16[128,1024]{1,0:T(8,128)(2,1)S(1)}, u32[]{:S(2)}, u32[]{:S(2)}) collective-permute-start(bf16[128,1024]{1,0:T(8,128)(2,1)S(1)} %shard_map.86), channel_id=1, source_target_pairs={{0,2},{1,3},{2,0},{3,1},{4,6},{5,7},{6,4},{7,5},{8,10},{9,11},{10,... | collective-permute-start | bytes 786440 | tf_op jit(solution)/shard_map/ppermute | solution.py:439
  58.8 1.8 %collective-permute-start.16 = (bf16[64,1024]{1,0:T(8,128)(2,1)S(1)}, bf16[64,1024]{1,0:T(8,128)(2,1)S(1)}, u32[]{:S(2)}, u32[]{:S(2)}) collective-permute-start(bf16[64,1024]{1,0:T(8,128)(2,1)S(1)} %shard_map.83.refs_12_), channel_id=1, source_target_pairs={{0,2},{1,3},{2,0},{3,1},{4,6},{5,7},{6,4},{7,5},{8,10},{9,11},{10,... | collective-permute-start | bytes 393224 | tf_op jit(solution)/shard_map/ppermute | solution.py:439
  60.6 1.7 %shard_map.84.h_ref = f32[512,1024]{1,0:T(8,128)S(1)} custom-call(bf16[128,512]{1,0:T(8,128)(2,1)S(1)} %shard_map.81.refs_3_.refs_0_, bf16[128,512]{1,0:T(8,128)(2,1)S(1)} %collective-permute-done.11.refs_1_, bf16[128,512]{1,0:T(8,128)(2,1)S(1)} %get-tuple-element.71.refs_2_.refs_0_, bf16[128,512]{1,0:T(8,128)(2,1)S(1)} %collective-permute-done.12.refs_3_.refs_1_, ...), custom_call_target="tpu_custom_call" | custom-call | tf_op jit(solution)/shard_map/pallas_call | solution.py:41
  63.1 3.0 %collective-permute-done.19.a_ref = bf16[128,1024]{1,0:T(8,128)(2,1)S(1)} collective-permute-done((bf16[128,1024]{1,0:T(8,128)(2,1)S(1)}, bf16[128,1024]{1,0:T(8,128)(2,1)S(1)}, u32[]{:S(2)}, u32[]{:S(2)}) %collective-permute-start.19) | collective-permute-done | bytes 262176 | tf_op jit(solution)/shard_map/ppermute | solution.py:439
  66.8 4.9 %collective-permute-done.18.a_ref = bf16[128,1024]{1,0:T(8,128)(2,1)S(1)} collective-permute-done((bf16[128,1024]{1,0:T(8,128)(2,1)S(1)}, bf16[128,1024]{1,0:T(8,128)(2,1)S(1)}, u32[]{:S(2)}, u32[]{:S(2)}) %collective-permute-start.18) | collective-permute-done | bytes 262176 | tf_op jit(solution)/shard_map/ppermute | solution.py:439
  72.4 2.1 %collective-permute-done.17.a_ref = bf16[64,1024]{1,0:T(8,128)(2,1)S(1)} collective-permute-done((bf16[64,1024]{1,0:T(8,128)(2,1)S(1)}, bf16[64,1024]{1,0:T(8,128)(2,1)S(1)}, u32[]{:S(2)}, u32[]{:S(2)}) %collective-permute-start.17) | collective-permute-done | bytes 131104 | tf_op jit(solution)/shard_map/ppermute | solution.py:439
  75.2 1.6 %collective-permute-done.16.a_ref = bf16[64,1024]{1,0:T(8,128)(2,1)S(1)} collective-permute-done((bf16[64,1024]{1,0:T(8,128)(2,1)S(1)}, bf16[64,1024]{1,0:T(8,128)(2,1)S(1)}, u32[]{:S(2)}, u32[]{:S(2)}) %collective-permute-start.16) | collective-permute-done | bytes 131104 | tf_op jit(solution)/shard_map/ppermute | solution.py:439
  (41 shorter events, 13.3 us)
Async XLA Ops:
  0.0 3.0 %collective-permute-start.1 = (bf16[512,1024]{1,0:T(8,128)(2,1)}, bf16[512,1024]{1,0:T(8,128)(2,1)S(1)}, u32[]{:S(2)}, u32[]{:S(2)}) collective-permute-start(bf16[512,1024]{1,0:T(8,128)(2,1)} %refs_2_.1), channel_id=1, source_target_pairs={{0,1},{1,0},{2,3},{3,2},{4,5},{5,4},{6,7},{7,6},{8,9},{9,8},{10,11... | collective-permute-start | bytes 3145736 | tf_op jit(solution)/shard_map/ppermute | solution.py:439
  0.5 26.6 %collective-permute-start = (bf16[512,1024]{1,0:T(8,128)(2,1)}, bf16[512,1024]{1,0:T(8,128)(2,1)S(1)}, u32[]{:S(2)}, u32[]{:S(2)}) collective-permute-start(bf16[512,1024]{1,0:T(8,128)(2,1)} %refs_2_.1), channel_id=1, source_target_pairs={{0,2},{1,3},{2,0},{3,1},{4,6},{5,7},{6,4},{7,5},{8,10},{9,11},{10,... | collective-permute-start | bytes 3145736 | tf_op jit(solution)/shard_map/ppermute | solution.py:439
  3.0 0.7 copy-start
  9.0 18.0 %collective-permute-start.4 = (bf16[512,1024]{1,0:T(8,128)(2,1)S(1)}, bf16[512,1024]{1,0:T(8,128)(2,1)S(1)}, u32[]{:S(2)}, u32[]{:S(2)}) collective-permute-start(bf16[512,1024]{1,0:T(8,128)(2,1)S(1)} %get-tuple-element.43), channel_id=1, source_target_pairs={{0,1},{1,0},{2,3},{3,2},{4,5},{5,4},{6,7},{7,6},{8,9},{9,8},{10,11... | collective-permute-start | bytes 3145736 | tf_op jit(solution)/shard_map/ppermute | solution.py:439
  9.5 17.6 %collective-permute-start.5 = (bf16[512,1024]{1,0:T(8,128)(2,1)S(1)}, bf16[512,1024]{1,0:T(8,128)(2,1)S(1)}, u32[]{:S(2)}, u32[]{:S(2)}) collective-permute-start(bf16[512,1024]{1,0:T(8,128)(2,1)S(1)} %get-tuple-element.44), channel_id=1, source_target_pairs={{0,1},{1,0},{2,3},{3,2},{4,5},{5,4},{6,7},{7,6},{8,9},{9,8},{10,11... | collective-permute-start | bytes 3145736 | tf_op jit(solution)/shard_map/ppermute | solution.py:439
  9.6 4.6 %collective-permute-start.2 = (f32[8,512]{1,0:T(8,128)S(1)}, f32[8,512]{1,0:T(8,128)S(1)}, u32[]{:S(2)}, u32[]{:S(2)}) collective-permute-start(f32[8,512]{1,0:T(8,128)S(1)} %get-tuple-element.41.refs_0_), channel_id=1, source_target_pairs={{0,4},{4,0},{8,12},{12,8},{16,20},{20,16},{24,28},{28,24},{1,5},{5... | collective-permute-start | bytes 49160 | tf_op jit(solution)/shard_map/ppermute | solution.py:442
  14.2 3.8 %collective-permute-start.3 = (f32[8,512]{1,0:T(8,128)S(1)}, f32[8,512]{1,0:T(8,128)S(1)}, u32[]{:S(2)}, u32[]{:S(2)}) collective-permute-start(f32[8,512]{1,0:T(8,128)S(1)} %shard_map.74.refs_1_), channel_id=1, source_target_pairs={{0,8},{4,12},{8,0},{12,4},{16,24},{20,28},{24,16},{28,20},{1,9},{5... | collective-permute-start | bytes 49160 | tf_op jit(solution)/shard_map/ppermute | solution.py:442
  27.0 2.7 %collective-permute-start.6 = (bf16[512,1024]{1,0:T(8,128)(2,1)S(1)}, bf16[512,1024]{1,0:T(8,128)(2,1)S(1)}, u32[]{:S(2)}, u32[]{:S(2)}) collective-permute-start(bf16[512,1024]{1,0:T(8,128)(2,1)S(1)} %shard_map.76.refs_1_), channel_id=1, source_target_pairs={{0,1},{1,0},{2,3},{3,2},{4,5},{5,4},{6,7},{7,6},{8,9},{9,8},{10,11... | collective-permute-start | bytes 3145736 | tf_op jit(solution)/shard_map/ppermute | solution.py:439
  30.5 5.8 %collective-permute-start.7 = (bf16[128,512]{1,0:T(8,128)(2,1)S(1)}, bf16[128,512]{1,0:T(8,128)(2,1)S(1)}, u32[]{:S(2)}, u32[]{:S(2)}) collective-permute-start(bf16[128,512]{1,0:T(8,128)(2,1)S(1)} %get-tuple-element.63.refs_1_), channel_id=1, source_target_pairs={{0,4},{1,9},{2,6},{3,11},{4,0},{5,13},{6,2},{7,15},{8,12},{9,1},{1... | collective-permute-start | bytes 393224 | tf_op jit(solution)/shard_map/ppermute | solution.py:475
  32.3 5.9 %collective-permute-start.8 = (bf16[144,512]{1,0:T(8,128)(2,1)S(1)}, bf16[144,512]{1,0:T(8,128)(2,1)S(1)}, u32[]{:S(2)}, u32[]{:S(2)}) collective-permute-start(bf16[144,512]{1,0:T(8,128)(2,1)S(1)} %get-tuple-element.64), channel_id=1, source_target_pairs={{0,8},{1,5},{2,10},{3,7},{4,12},{5,1},{6,14},{7,3},{8,0},{9,13},{1... | collective-permute-start | bytes 442376 | tf_op jit(solution)/shard_map/ppermute | solution.py:475
  36.3 5.0 %collective-permute-start.9 = (bf16[128,512]{1,0:T(8,128)(2,1)S(1)}, bf16[128,512]{1,0:T(8,128)(2,1)S(1)}, u32[]{:S(2)}, u32[]{:S(2)}) collective-permute-start(bf16[128,512]{1,0:T(8,128)(2,1)S(1)} %collective-permute-done.7.refs_2_), channel_id=1, source_target_pairs={{0,8},{1,5},{2,10},{3,7},{4,12},{5,1},{6,14},{7,3},{8,0},{9,13},{1... | collective-permute-start | bytes 393224 | tf_op jit(solution)/shard_map/ppermute | solution.py:475
  41.5 7.6 %collective-permute-start.10 = (bf16[128,512]{1,0:T(8,128)(2,1)S(1)}, bf16[128,512]{1,0:T(8,128)(2,1)S(1)}, u32[]{:S(2)}, u32[]{:S(2)}) collective-permute-start(bf16[128,512]{1,0:T(8,128)(2,1)S(1)} %get-tuple-element.70), channel_id=1, source_target_pairs={{0,16},{4,20},{8,24},{12,28},{16,0},{20,4},{24,8},{28,12},{1,17},{... | collective-permute-start | bytes 393224 | tf_op jit(solution)/shard_map/ppermute | solution.py:442
  49.4 1.4 %collective-permute-start.11 = (bf16[128,512]{1,0:T(8,128)(2,1)S(1)}, bf16[128,512]{1,0:T(8,128)(2,1)S(1)}, u32[]{:S(2)}, u32[]{:S(2)}) collective-permute-start(bf16[128,512]{1,0:T(8,128)(2,1)S(1)} %shard_map.81.refs_3_.refs_0_), channel_id=1, source_target_pairs={{0,1},{1,0},{2,3},{3,2},{4,5},{5,4},{6,7},{7,6},{8,9},{9,8},{10,11... | collective-permute-start | bytes 393224 | tf_op jit(solution)/shard_map/ppermute | solution.py:439
  50.1 3.1 %collective-permute-start.12 = (bf16[128,512]{1,0:T(8,128)(2,1)S(1)}, bf16[128,512]{1,0:T(8,128)(2,1)S(1)}, u32[]{:S(2)}, u32[]{:S(2)}) collective-permute-start(bf16[128,512]{1,0:T(8,128)(2,1)S(1)} %get-tuple-element.71.refs_2_.refs_0_), channel_id=1, source_target_pairs={{0,1},{1,0},{2,3},{3,2},{4,5},{5,4},{6,7},{7,6},{8,9},{9,8},{10,11... | collective-permute-start | bytes 393224 | tf_op jit(solution)/shard_map/ppermute | solution.py:439
  50.6 3.3 %collective-permute-start.13 = (bf16[128,512]{1,0:T(8,128)(2,1)S(1)}, bf16[128,512]{1,0:T(8,128)(2,1)S(1)}, u32[]{:S(2)}, u32[]{:S(2)}) collective-permute-start(bf16[128,512]{1,0:T(8,128)(2,1)S(1)} %get-tuple-element.72.refs_4_.refs_0_), channel_id=1, source_target_pairs={{0,1},{1,0},{2,3},{3,2},{4,5},{5,4},{6,7},{7,6},{8,9},{9,8},{10,11... | collective-permute-start | bytes 393224 | tf_op jit(solution)/shard_map/ppermute | solution.py:439
  51.3 11.0 %collective-permute-start.20 = (bf16[128,1024]{1,0:T(8,128)(2,1)S(1)}, bf16[128,1024]{1,0:T(8,128)(2,1)S(1)}, u32[]{:S(2)}, u32[]{:S(2)}) collective-permute-start(bf16[128,1024]{1,0:T(8,128)(2,1)S(1)} %shard_map.88), channel_id=1, source_target_pairs={{0,2},{1,3},{2,0},{3,1},{4,6},{5,7},{6,4},{7,5},{8,10},{9,11},{10,... | collective-permute-start | bytes 786440 | tf_op jit(solution)/shard_map/ppermute | solution.py:439
  53.6 12.5 %collective-permute-start.19 = (bf16[128,1024]{1,0:T(8,128)(2,1)S(1)}, bf16[128,1024]{1,0:T(8,128)(2,1)S(1)}, u32[]{:S(2)}, u32[]{:S(2)}) collective-permute-start(bf16[128,1024]{1,0:T(8,128)(2,1)S(1)} %shard_map.87), channel_id=1, source_target_pairs={{0,2},{1,3},{2,0},{3,1},{4,6},{5,7},{6,4},{7,5},{8,10},{9,11},{10,... | collective-permute-start | bytes 786440 | tf_op jit(solution)/shard_map/ppermute | solution.py:439
  54.4 17.3 %collective-permute-start.18 = (bf16[128,1024]{1,0:T(8,128)(2,1)S(1)}, bf16[128,1024]{1,0:T(8,128)(2,1)S(1)}, u32[]{:S(2)}, u32[]{:S(2)}) collective-permute-start(bf16[128,1024]{1,0:T(8,128)(2,1)S(1)} %shard_map.86), channel_id=1, source_target_pairs={{0,2},{1,3},{2,0},{3,1},{4,6},{5,7},{6,4},{7,5},{8,10},{9,11},{10,... | collective-permute-start | bytes 786440 | tf_op jit(solution)/shard_map/ppermute | solution.py:439
  56.2 1.3 %collective-permute-start.14 = (bf16[64,512]{1,0:T(8,128)(2,1)S(1)}, bf16[64,512]{1,0:T(8,128)(2,1)S(1)}, u32[]{:S(2)}, u32[]{:S(2)}) collective-permute-start(bf16[64,512]{1,0:T(8,128)(2,1)S(1)} %get-tuple-element.73.refs_6_.refs_0_), channel_id=1, source_target_pairs={{0,1},{1,0},{2,3},{3,2},{4,5},{5,4},{6,7},{7,6},{8,9},{9,8},{10,11... | collective-permute-start | bytes 196616 | tf_op jit(solution)/shard_map/ppermute | solution.py:439
  56.2 2.1 %collective-permute-start.15 = (bf16[64,512]{1,0:T(8,128)(2,1)S(1)}, bf16[64,512]{1,0:T(8,128)(2,1)S(1)}, u32[]{:S(2)}, u32[]{:S(2)}) collective-permute-start(bf16[64,512]{1,0:T(8,128)(2,1)S(1)} %get-tuple-element.74.refs_0_.refs_8_), channel_id=1, source_target_pairs={{0,1},{1,0},{2,3},{3,2},{4,5},{5,4},{6,7},{7,6},{8,9},{9,8},{10,11... | collective-permute-start | bytes 196616 | tf_op jit(solution)/shard_map/ppermute | solution.py:439
  58.0 16.5 %collective-permute-start.17 = (bf16[64,1024]{1,0:T(8,128)(2,1)S(1)}, bf16[64,1024]{1,0:T(8,128)(2,1)S(1)}, u32[]{:S(2)}, u32[]{:S(2)}) collective-permute-start(bf16[64,1024]{1,0:T(8,128)(2,1)S(1)} %shard_map.85), channel_id=1, source_target_pairs={{0,2},{1,3},{2,0},{3,1},{4,6},{5,7},{6,4},{7,5},{8,10},{9,11},{10,... | collective-permute-start | bytes 393224 | tf_op jit(solution)/shard_map/ppermute | solution.py:439
  58.8 17.9 %collective-permute-start.16 = (bf16[64,1024]{1,0:T(8,128)(2,1)S(1)}, bf16[64,1024]{1,0:T(8,128)(2,1)S(1)}, u32[]{:S(2)}, u32[]{:S(2)}) collective-permute-start(bf16[64,1024]{1,0:T(8,128)(2,1)S(1)} %shard_map.83.refs_12_), channel_id=1, source_target_pairs={{0,2},{1,3},{2,0},{3,1},{4,6},{5,7},{6,4},{7,5},{8,10},{9,11},{10,... | collective-permute-start | bytes 393224 | tf_op jit(solution)/shard_map/ppermute | solution.py:439

commit v10 on v7

--- a/solution.py
+++ b/solution.py
@@ -222,21 +222,28 @@
     return call(kernel, [x], [shape((rows, part), x.dtype)] * ways, 0, after)
 
 
-def partial(x, w):
+def partial(x, w, after):
     def kernel(x_ref, w_ref, o_ref):
         o_ref[...] = dot(x_ref[...], w_ref[...]).astype(BF16)
 
-    return call(kernel, [x, w], [shape((x.shape[0], w.shape[1]), BF16)], 0)[0]
-
-
-def project_state(x, wkv, total_kv, from_near, keep, head_size):
-    rows = x.shape[0]
+    return call(kernel, [x, w], [shape((x.shape[0], w.shape[1]), BF16)], 0, after)[0]
+
+
+def add_product(x, w, total, after):
+    def kernel(x_ref, w_ref, t_ref, o_ref):
+        o_ref[...] = t_ref[...] + dot(x_ref[...], w_ref[...])
+
+    return call(kernel, [x, w, total], [shape(total.shape, F32)], 0, after, aliases={2: 0})[0]
+
+
+def project_state(total_kv, from_near, keep, head_size):
+    rows = total_kv.shape[0]
     heads = keep.shape[1]
-    kv_width = wkv.shape[1] // 2
+    kv_width = total_kv.shape[1] // 2
     group = heads // (kv_width // head_size)
 
-    def kernel(x_ref, w_ref, total_ref, near_ref, keep_ref, k_out, v_out, s_out):
-        total = total_ref[...] + near_ref[...].astype(F32) + dot(x_ref[...], w_ref[...])
+    def kernel(total_ref, near_ref, keep_ref, k_out, v_out, s_out):
+        total = total_ref[...] + near_ref[...].astype(F32)
         keys = total[:, :kv_width].astype(BF16)
         values = total[:, kv_width:].astype(BF16)
         k_out[...] = keys
@@ -256,7 +263,7 @@
         shape((rows, kv_width), BF16),
         shape((head_size, heads * head_size), BF16),
     ]
-    return call(kernel, [x, wkv, total_kv, from_near, keep], outs, 0)
+    return call(kernel, [total_kv, from_near, keep], outs, 0)
 
 
 def attend(me, place, xs, wq, wl, total_q, total_l, k, v, dcol, drow, spans, states, head_size, level_count):
@@ -418,10 +425,12 @@
 
     wq, wkv, wkv_send, wl = ws
     wkv_near = swap_tp(wkv_send, 1)
-    arrived = gate(far, total, w_far, w_here)
-    from_near = swap_tp(partial(arrived, wkv_near), 1)
+    arrived = far
+    for_near = partial(arrived, wkv_near, (total, w_far, w_here))
+    from_near = swap_tp(for_near, 1)
     total_q, total_kv, total_l = totals
-    k, v, state = project_state(arrived, wkv, total_kv, from_near, keep, head_size)
+    total_kv = add_product(arrived, wkv, total_kv, (for_near,))
+    k, v, state = project_state(total_kv, from_near, keep, head_size)
     total_q, total_l = project(me, 2, arrived, wq, wl, total_q, total_l, (k,))
     arrived_near = [swap_tp(x, 1) for x in split(arrived, 4, (total_l,))]
 
@@ -440,9 +449,7 @@
     unit = rows // 8
     ends = (0, 2, 4, 6, 7, 8)
     cuts = [slice(start * unit, stop * unit) for start, stop in zip(ends, ends[1:])]
-    pieces = finish(local, scaled, earlier[-1], cuts[:1], head_size)
-    pieces += finish(local, scaled, earlier[-1], cuts[1:], head_size, pieces)
-    pairs = [(x, swap_tp(x, 1)) for x in pieces]
+    pairs = [(x, swap_tp(x, 1)) for x in finish(local, scaled, earlier[-1], cuts, head_size)]
     crossing = [out_block([pair], w_far_own, w_far, BF16) for pair in pairs]
     own_block = out_block(pairs, w_here_own, w_here, F32, (crossing[-1],))
     out = None

time: 76.7 us -> 76.6 us (level)
  no operation moved by 1% of the time
where the time goes in v10:
time: 76.6 us; the launch traced here: 76.4 us
  waiting for transfers between devices  31 us (40%)
  starting transfers between devices  23.5 us (31%)
  Pallas kernels  21 us (27%)
    ppermute x20, waiting for transfers between devices, swap_tp(): return lax.ppermute(x, 'tp', [(i, i ^ bit) for i in range(4)])  22.3 us
    pallas_call x18, Pallas kernels, call(): pl.pallas_call(run, in_specs=[SMEM] * smem + [HBM] * hbm + [VMEM] * (coun...  17.4 us
    ppermute x20, starting transfers between devices, swap_tp(): return lax.ppermute(x, 'tp', [(i, i ^ bit) for i in range(4)])  12.2 us
    ppermute x5, starting transfers between devices, swap_seq(): return lax.ppermute(x, 'seq', [(i, i ^ bit) for i in range(seq_size)])  11.3 us
    ppermute x5, waiting for transfers between devices, swap_seq(): return lax.ppermute(x, 'seq', [(i, i ^ bit) for i in range(seq_size)])  8.75 us
    pallas_call x5, Pallas kernels, add_rows(): pl.pallas_call(kernel, grid=(rows // unit,), in_specs=specs, out_specs=pl...  3.57 us
  transfers between devices with their start and end apart: 25, of which 13 were waited for; matrix products, arithmetic and copies ran while one was open for 0% of the time, Pallas kernels for 24%

profile of v10, /device:TPU:0, one launch (start us, length us, event | category | flops | bytes accessed | tf_op | source)
XLA Modules:
  0.0 76.4 jit_solution(2761348303926356909)
XLA Ops:
  0.5 2.5 %collective-permute-start = (bf16[512,1024]{1,0:T(8,128)(2,1)}, bf16[512,1024]{1,0:T(8,128)(2,1)S(1)}, u32[]{:S(2)}, u32[]{:S(2)}) collective-permute-start(bf16[512,1024]{1,0:T(8,128)(2,1)} %refs_2_.1), channel_id=1, source_target_pairs={{0,2},{1,3},{2,0},{3,1},{4,6},{5,7},{6,4},{7,5},{8,10},{9,11},{10,... | collective-permute-start | bytes 3145736 | tf_op jit(solution)/shard_map/ppermute | solution.py:405
  3.7 5.4 %shard_map.73 = (f32[512,512]{1,0:T(8,128)S(1)}, f32[512,256]{1,0:T(8,128)S(1)}, f32[512,24]{1,0:T(8,128)S(1)}, bf16[2,1024,512]{2,1,0:T(8,128)(2,1)S(1)}, bf16[...) custom-call(s32[1]{0:T(128)} %bitcast.refs_0_, ...), custom_call_target="tpu_custom_call" | custom-call | tf_op jit(solution)/shard_map/pallas_call | solution.py:41
  10.0 2.6 %collective-permute-start.3 = (f32[8,512]{1,0:T(8,128)S(1)}, f32[8,512]{1,0:T(8,128)S(1)}, u32[]{:S(2)}, u32[]{:S(2)}) collective-permute-start(f32[8,512]{1,0:T(8,128)S(1)} %get-tuple-element.53.refs_1_), channel_id=1, source_target_pairs={{0,4},{4,0},{8,12},{12,8},{16,20},{20,16},{24,28},{28,24},{1,5},{5... | collective-permute-start | bytes 49160 | tf_op jit(solution)/shard_map/ppermute | solution.py:408
  12.6 1.7 %collective-permute-done.3.refs_2_ = f32[8,512]{1,0:T(8,128)S(1)} collective-permute-done((f32[8,512]{1,0:T(8,128)S(1)}, f32[8,512]{1,0:T(8,128)S(1)}, u32[]{:S(2)}, u32[]{:S(2)}) %collective-permute-start.3) | collective-permute-done | bytes 16416 | tf_op jit(solution)/shard_map/ppermute | solution.py:408
  14.3 2.2 %collective-permute-start.4 = (f32[8,512]{1,0:T(8,128)S(1)}, f32[8,512]{1,0:T(8,128)S(1)}, u32[]{:S(2)}, u32[]{:S(2)}) collective-permute-start(f32[8,512]{1,0:T(8,128)S(1)} %get-tuple-element.54.refs_1_), channel_id=1, source_target_pairs={{0,8},{4,12},{8,0},{12,4},{16,24},{20,28},{24,16},{28,20},{1,9},{5... | collective-permute-start | bytes 49160 | tf_op jit(solution)/shard_map/ppermute | solution.py:408
  16.5 1.7 %collective-permute-done.4.refs_2_ = f32[8,512]{1,0:T(8,128)S(1)} collective-permute-done((f32[8,512]{1,0:T(8,128)S(1)}, f32[8,512]{1,0:T(8,128)S(1)}, u32[]{:S(2)}, u32[]{:S(2)}) %collective-permute-start.4) | collective-permute-done | bytes 16416 | tf_op jit(solution)/shard_map/ppermute | solution.py:408
  18.8 8.2 %collective-permute-done.refs_0_.refs_1_ = bf16[512,1024]{1,0:T(8,128)(2,1)S(1)} collective-permute-done((bf16[512,1024]{1,0:T(8,128)(2,1)}, bf16[512,1024]{1,0:T(8,128)(2,1)S(1)}, u32[]{:S(2)}, u32[]{:S(2)}) %collective-permute-start) | collective-permute-done | bytes 1048608 | tf_op jit(solution)/shard_map/ppermute | solution.py:405
  28.0 1.1 %collective-permute-done.7.refs_1_ = bf16[512,256]{1,0:T(8,128)(2,1)S(1)} collective-permute-done((bf16[512,256]{1,0:T(8,128)(2,1)S(1)}, bf16[512,256]{1,0:T(8,128)(2,1)S(1)}, u32[]{:S(2)}, u32[]{:S(2)}) %collective-permute-start.7) | collective-permute-done | bytes 262176 | tf_op jit(solution)/shard_map/ppermute | solution.py:405
  29.7 1.8 %collective-permute-start.12 = (bf16[128,512]{1,0:T(8,128)(2,1)S(1)}, bf16[128,512]{1,0:T(8,128)(2,1)S(1)}, u32[]{:S(2)}, u32[]{:S(2)}) collective-permute-start(bf16[128,512]{1,0:T(8,128)(2,1)S(1)} %get-tuple-element.73.refs_0_), channel_id=1, source_target_pairs={{0,4},{4,0},{8,12},{12,8},{16,20},{20,16},{24,28},{28,24},{1,5},{5... | collective-permute-start | bytes 393224 | tf_op jit(solution)/shard_map/ppermute | solution.py:408
  31.4 1.1 %shard_map.79 = (f32[512,512]{1,0:T(8,128)S(1)}, f32[512,24]{1,0:T(8,128)S(1)}) custom-call(s32[1]{0:T(128)} %bitcast.refs_0_, bf16[512,1024]{1,0:T(8,128)(2,1)S(1)} %collective-permute-done.refs_0_.refs_1_, bf16[2,1024,512]{2,1,0:T(8,128)(2,1)S(1)} %get-tuple-element.46.refs_2_.refs_5_, ...), custom_call_target="tpu_custom_call", output_to_operand_aliasing={{0}: (4, {}), {1}: (5, {})} | custom-call | flops 562036736 | bytes 5537796 | tf_op jit(solution)/shard_map/pallas_call | solution.py:41
  33.7 1.6 %collective-permute-done.12.refs_1_.refs_16_ = bf16[128,512]{1,0:T(8,128)(2,1)S(1)} collective-permute-done((bf16[128,512]{1,0:T(8,128)(2,1)S(1)}, bf16[128,512]{1,0:T(8,128)(2,1)S(1)}, u32[]{:S(2)}, u32[]{:S(2)}) %collective-permute-start.12) | collective-permute-done | bytes 131104 | tf_op jit(solution)/shard_map/ppermute | solution.py:408
  35.3 1.9 %collective-permute-start.13 = (bf16[128,512]{1,0:T(8,128)(2,1)S(1)}, bf16[128,512]{1,0:T(8,128)(2,1)S(1)}, u32[]{:S(2)}, u32[]{:S(2)}) collective-permute-start(bf16[128,512]{1,0:T(8,128)(2,1)S(1)} %shard_map.81.refs_0_), channel_id=1, source_target_pairs={{0,8},{4,12},{8,0},{12,4},{16,24},{20,28},{24,16},{28,20},{1,9},{5... | collective-permute-start | bytes 393224 | tf_op jit(solution)/shard_map/ppermute | solution.py:408
  37.2 3.2 %collective-permute-done.13.refs_17_.refs_1_ = bf16[128,512]{1,0:T(8,128)(2,1)S(1)} collective-permute-done((bf16[128,512]{1,0:T(8,128)(2,1)S(1)}, bf16[128,512]{1,0:T(8,128)(2,1)S(1)}, u32[]{:S(2)}, u32[]{:S(2)}) %collective-permute-start.13) | collective-permute-done | bytes 131104 | tf_op jit(solution)/shard_map/ppermute | solution.py:408
  40.4 2.9 %collective-permute-start.14 = (bf16[128,512]{1,0:T(8,128)(2,1)S(1)}, bf16[128,512]{1,0:T(8,128)(2,1)S(1)}, u32[]{:S(2)}, u32[]{:S(2)}) collective-permute-start(bf16[128,512]{1,0:T(8,128)(2,1)S(1)} %shard_map.83), channel_id=1, source_target_pairs={{0,16},{4,20},{8,24},{12,28},{16,0},{20,4},{24,8},{28,12},{1,17},{... | collective-permute-start | bytes 393224 | tf_op jit(solution)/shard_map/ppermute | solution.py:408
  43.3 4.0 %shard_map.82 = (f32[512,512]{1,0:T(8,128)S(1)}, bf16[512,512]{1,0:T(8,128)(2,1)S(1)}, bf16[512,512]{1,0:T(8,128)(2,1)}, f32[512,24]{1,0:T(8,128)}) custom-call(s32[1]{0:T(128)} %bitcast.refs_0_, bf16[512,256]{1,0:T(8,128)(2,1)S(1)} %collective-permute-done.8.refs_1_, bf16[512,256]{1,0:T(8,128)(2,1)S(1)} %collective-permute-done.9.refs_2_, ...), custom_call_target="tpu_custom_call" | custom-call | flops 1073741824 | bytes 7176196 | tf_op jit(solution)/shard_map/pallas_call | solution.py:41
  49.2 0.8 collective-permute-done.15.refs_1_
  50.5 1.7 %collective-permute-start.24 = (bf16[128,1024]{1,0:T(8,128)(2,1)S(1)}, bf16[128,1024]{1,0:T(8,128)(2,1)S(1)}, u32[]{:S(2)}, u32[]{:S(2)}) collective-permute-start(bf16[128,1024]{1,0:T(8,128)(2,1)S(1)} %shard_map.90), channel_id=1, source_target_pairs={{0,2},{1,3},{2,0},{3,1},{4,6},{5,7},{6,4},{7,5},{8,10},{9,11},{10,... | collective-permute-start | bytes 786440 | tf_op jit(solution)/shard_map/ppermute | solution.py:405
  53.6 1.7 %collective-permute-start.22 = (bf16[128,1024]{1,0:T(8,128)(2,1)S(1)}, bf16[128,1024]{1,0:T(8,128)(2,1)S(1)}, u32[]{:S(2)}, u32[]{:S(2)}) collective-permute-start(bf16[128,1024]{1,0:T(8,128)(2,1)S(1)} %shard_map.88), channel_id=1, source_target_pairs={{0,2},{1,3},{2,0},{3,1},{4,6},{5,7},{6,4},{7,5},{8,10},{9,11},{10,... | collective-permute-start | bytes 786440 | tf_op jit(solution)/shard_map/ppermute | solution.py:405
  58.0 1.7 %collective-permute-start.20 = (bf16[64,1024]{1,0:T(8,128)(2,1)S(1)}, bf16[64,1024]{1,0:T(8,128)(2,1)S(1)}, u32[]{:S(2)}, u32[]{:S(2)}) collective-permute-start(bf16[64,1024]{1,0:T(8,128)(2,1)S(1)} %shard_map.85.refs_12_), channel_id=1, source_target_pairs={{0,2},{1,3},{2,0},{3,1},{4,6},{5,7},{6,4},{7,5},{8,10},{9,11},{10,... | collective-permute-start | bytes 393224 | tf_op jit(solution)/shard_map/ppermute | solution.py:405
  59.7 1.7 %shard_map.86.h_ref = f32[512,1024]{1,0:T(8,128)S(1)} custom-call(bf16[128,512]{1,0:T(8,128)(2,1)S(1)} %get-tuple-element.80.refs_0_, bf16[128,512]{1,0:T(8,128)(2,1)S(1)} %collective-permute-done.15.refs_1_, bf16[128,512]{1,0:T(8,128)(2,1)S(1)} %get-tuple-element.81.refs_2_.refs_0_, bf16[128,512]{1,0:T(8,128)(2,1)S(1)} %collective-permute-done.16.refs_3_.refs_1_, ...), custom_call_target="tpu_custom_call" | custom-call | tf_op jit(solution)/shard_map/pallas_call | solution.py:41
  62.1 3.2 %collective-permute-done.23.a_ref = bf16[128,1024]{1,0:T(8,128)(2,1)S(1)} collective-permute-done((bf16[128,1024]{1,0:T(8,128)(2,1)S(1)}, bf16[128,1024]{1,0:T(8,128)(2,1)S(1)}, u32[]{:S(2)}, u32[]{:S(2)}) %collective-permute-start.23) | collective-permute-done | bytes 262176 | tf_op jit(solution)/shard_map/ppermute | solution.py:405
  66.0 4.9 %collective-permute-done.22.a_ref = bf16[128,1024]{1,0:T(8,128)(2,1)S(1)} collective-permute-done((bf16[128,1024]{1,0:T(8,128)(2,1)S(1)}, bf16[128,1024]{1,0:T(8,128)(2,1)S(1)}, u32[]{:S(2)}, u32[]{:S(2)}) %collective-permute-start.22) | collective-permute-done | bytes 262176 | tf_op jit(solution)/shard_map/ppermute | solution.py:405
  71.6 2.1 %collective-permute-done.21.a_ref = bf16[64,1024]{1,0:T(8,128)(2,1)S(1)} collective-permute-done((bf16[64,1024]{1,0:T(8,128)(2,1)S(1)}, bf16[64,1024]{1,0:T(8,128)(2,1)S(1)}, u32[]{:S(2)}, u32[]{:S(2)}) %collective-permute-start.21) | collective-permute-done | bytes 131104 | tf_op jit(solution)/shard_map/ppermute | solution.py:405
  74.4 1.3 %collective-permute-done.20.a_ref = bf16[64,1024]{1,0:T(8,128)(2,1)S(1)} collective-permute-done((bf16[64,1024]{1,0:T(8,128)(2,1)S(1)}, bf16[64,1024]{1,0:T(8,128)(2,1)S(1)}, u32[]{:S(2)}, u32[]{:S(2)}) %collective-permute-start.20) | collective-permute-done | bytes 131104 | tf_op jit(solution)/shard_map/ppermute | solution.py:405
  (51 shorter events, 15.5 us)
Async XLA Ops:
  0.0 3.0 %collective-permute-start.1 = (bf16[512,1024]{1,0:T(8,128)(2,1)}, bf16[512,1024]{1,0:T(8,128)(2,1)S(1)}, u32[]{:S(2)}, u32[]{:S(2)}) collective-permute-start(bf16[512,1024]{1,0:T(8,128)(2,1)} %refs_2_.1), channel_id=1, source_target_pairs={{0,1},{1,0},{2,3},{3,2},{4,5},{5,4},{6,7},{7,6},{8,9},{9,8},{10,11... | collective-permute-start | bytes 3145736 | tf_op jit(solution)/shard_map/ppermute | solution.py:405
  0.5 26.6 %collective-permute-start = (bf16[512,1024]{1,0:T(8,128)(2,1)}, bf16[512,1024]{1,0:T(8,128)(2,1)S(1)}, u32[]{:S(2)}, u32[]{:S(2)}) collective-permute-start(bf16[512,1024]{1,0:T(8,128)(2,1)} %refs_2_.1), channel_id=1, source_target_pairs={{0,2},{1,3},{2,0},{3,1},{4,6},{5,7},{6,4},{7,5},{8,10},{9,11},{10,... | collective-permute-start | bytes 3145736 | tf_op jit(solution)/shard_map/ppermute | solution.py:405
  9.0 18.0 %collective-permute-start.5 = (bf16[512,1024]{1,0:T(8,128)(2,1)S(1)}, bf16[512,1024]{1,0:T(8,128)(2,1)S(1)}, u32[]{:S(2)}, u32[]{:S(2)}) collective-permute-start(bf16[512,1024]{1,0:T(8,128)(2,1)S(1)} %get-tuple-element.57), channel_id=1, source_target_pairs={{0,1},{1,0},{2,3},{3,2},{4,5},{5,4},{6,7},{7,6},{8,9},{9,8},{10,11... | collective-permute-start | bytes 3145736 | tf_op jit(solution)/shard_map/ppermute | solution.py:405
  9.5 17.6 %collective-permute-start.6 = (bf16[512,1024]{1,0:T(8,128)(2,1)S(1)}, bf16[512,1024]{1,0:T(8,128)(2,1)S(1)}, u32[]{:S(2)}, u32[]{:S(2)}) collective-permute-start(bf16[512,1024]{1,0:T(8,128)(2,1)S(1)} %get-tuple-element.58), channel_id=1, source_target_pairs={{0,1},{1,0},{2,3},{3,2},{4,5},{5,4},{6,7},{7,6},{8,9},{9,8},{10,11... | collective-permute-start | bytes 3145736 | tf_op jit(solution)/shard_map/ppermute | solution.py:405
  9.6 17.4 %collective-permute-start.2 = (bf16[1024,256]{1,0:T(8,128)(2,1)S(1)}, bf16[1024,256]{1,0:T(8,128)(2,1)S(1)}, u32[]{:S(2)}, u32[]{:S(2)}) collective-permute-start(bf16[1024,256]{1,0:T(8,128)(2,1)S(1)} %get-tuple-element.52), channel_id=1, source_target_pairs={{0,1},{1,0},{2,3},{3,2},{4,5},{5,4},{6,7},{7,6},{8,9},{9,8},{10,11... | collective-permute-start | bytes 1572872 | tf_op jit(solution)/shard_map/ppermute | solution.py:405
  10.0 4.3 %collective-permute-start.3 = (f32[8,512]{1,0:T(8,128)S(1)}, f32[8,512]{1,0:T(8,128)S(1)}, u32[]{:S(2)}, u32[]{:S(2)}) collective-permute-start(f32[8,512]{1,0:T(8,128)S(1)} %get-tuple-element.53.refs_1_), channel_id=1, source_target_pairs={{0,4},{4,0},{8,12},{12,8},{16,20},{20,16},{24,28},{28,24},{1,5},{5... | collective-permute-start | bytes 49160 | tf_op jit(solution)/shard_map/ppermute | solution.py:408
  14.3 3.9 %collective-permute-start.4 = (f32[8,512]{1,0:T(8,128)S(1)}, f32[8,512]{1,0:T(8,128)S(1)}, u32[]{:S(2)}, u32[]{:S(2)}) collective-permute-start(f32[8,512]{1,0:T(8,128)S(1)} %get-tuple-element.54.refs_1_), channel_id=1, source_target_pairs={{0,8},{4,12},{8,0},{12,4},{16,24},{20,28},{24,16},{28,20},{1,9},{5... | collective-permute-start | bytes 49160 | tf_op jit(solution)/shard_map/ppermute | solution.py:408
  27.5 1.6 %collective-permute-start.7 = (bf16[512,256]{1,0:T(8,128)(2,1)S(1)}, bf16[512,256]{1,0:T(8,128)(2,1)S(1)}, u32[]{:S(2)}, u32[]{:S(2)}) collective-permute-start(bf16[512,256]{1,0:T(8,128)(2,1)S(1)} %shard_map.76.refs_3_), channel_id=1, source_target_pairs={{0,1},{1,0},{2,3},{3,2},{4,5},{5,4},{6,7},{7,6},{8,9},{9,8},{10,11... | collective-permute-start | bytes 786440 | tf_op jit(solution)/shard_map/ppermute | solution.py:405
  29.7 5.6 %collective-permute-start.12 = (bf16[128,512]{1,0:T(8,128)(2,1)S(1)}, bf16[128,512]{1,0:T(8,128)(2,1)S(1)}, u32[]{:S(2)}, u32[]{:S(2)}) collective-permute-start(bf16[128,512]{1,0:T(8,128)(2,1)S(1)} %get-tuple-element.73.refs_0_), channel_id=1, source_target_pairs={{0,4},{4,0},{8,12},{12,8},{16,20},{20,16},{24,28},{28,24},{1,5},{5... | collective-permute-start | bytes 393224 | tf_op jit(solution)/shard_map/ppermute | solution.py:408
  32.6 10.7 %collective-permute-start.8 = (bf16[512,256]{1,0:T(8,128)(2,1)S(1)}, bf16[512,256]{1,0:T(8,128)(2,1)S(1)}, u32[]{:S(2)}, u32[]{:S(2)}) collective-permute-start(bf16[512,256]{1,0:T(8,128)(2,1)S(1)} %get-tuple-element.62), channel_id=1, source_target_pairs={{0,1},{1,0},{2,3},{3,2},{4,5},{5,4},{6,7},{7,6},{8,9},{9,8},{10,11... | collective-permute-start | bytes 786440 | tf_op jit(solution)/shard_map/ppermute | solution.py:405
  32.7 10.6 %collective-permute-start.9 = (bf16[512,256]{1,0:T(8,128)(2,1)S(1)}, bf16[512,256]{1,0:T(8,128)(2,1)S(1)}, u32[]{:S(2)}, u32[]{:S(2)}) collective-permute-start(bf16[512,256]{1,0:T(8,128)(2,1)S(1)} %get-tuple-element.63), channel_id=1, source_target_pairs={{0,1},{1,0},{2,3},{3,2},{4,5},{5,4},{6,7},{7,6},{8,9},{9,8},{10,11... | collective-permute-start | bytes 786440 | tf_op jit(solution)/shard_map/ppermute | solution.py:405
  33.2 10.1 %collective-permute-start.10 = (bf16[512,256]{1,0:T(8,128)(2,1)S(1)}, bf16[512,256]{1,0:T(8,128)(2,1)S(1)}, u32[]{:S(2)}, u32[]{:S(2)}) collective-permute-start(bf16[512,256]{1,0:T(8,128)(2,1)S(1)} %get-tuple-element.64), channel_id=1, source_target_pairs={{0,1},{1,0},{2,3},{3,2},{4,5},{5,4},{6,7},{7,6},{8,9},{9,8},{10,11... | collective-permute-start | bytes 786440 | tf_op jit(solution)/shard_map/ppermute | solution.py:405
  33.2 10.0 %collective-permute-start.11 = (bf16[512,256]{1,0:T(8,128)(2,1)S(1)}, bf16[512,256]{1,0:T(8,128)(2,1)S(1)}, u32[]{:S(2)}, u32[]{:S(2)}) collective-permute-start(bf16[512,256]{1,0:T(8,128)(2,1)S(1)} %get-tuple-element.65), channel_id=1, source_target_pairs={{0,1},{1,0},{2,3},{3,2},{4,5},{5,4},{6,7},{7,6},{8,9},{9,8},{10,11... | collective-permute-start | bytes 786440 | tf_op jit(solution)/shard_map/ppermute | solution.py:405
  35.3 5.0 %collective-permute-start.13 = (bf16[128,512]{1,0:T(8,128)(2,1)S(1)}, bf16[128,512]{1,0:T(8,128)(2,1)S(1)}, u32[]{:S(2)}, u32[]{:S(2)}) collective-permute-start(bf16[128,512]{1,0:T(8,128)(2,1)S(1)} %shard_map.81.refs_0_), channel_id=1, source_target_pairs={{0,8},{4,12},{8,0},{12,4},{16,24},{20,28},{24,16},{28,20},{1,9},{5... | collective-permute-start | bytes 393224 | tf_op jit(solution)/shard_map/ppermute | solution.py:408
  40.4 7.5 %collective-permute-start.14 = (bf16[128,512]{1,0:T(8,128)(2,1)S(1)}, bf16[128,512]{1,0:T(8,128)(2,1)S(1)}, u32[]{:S(2)}, u32[]{:S(2)}) collective-permute-start(bf16[128,512]{1,0:T(8,128)(2,1)S(1)} %shard_map.83), channel_id=1, source_target_pairs={{0,16},{4,20},{8,24},{12,28},{16,0},{20,4},{24,8},{28,12},{1,17},{... | collective-permute-start | bytes 393224 | tf_op jit(solution)/shard_map/ppermute | solution.py:408
  48.6 1.4 %collective-permute-start.15 = (bf16[128,512]{1,0:T(8,128)(2,1)S(1)}, bf16[128,512]{1,0:T(8,128)(2,1)S(1)}, u32[]{:S(2)}, u32[]{:S(2)}) collective-permute-start(bf16[128,512]{1,0:T(8,128)(2,1)S(1)} %get-tuple-element.80.refs_0_), channel_id=1, source_target_pairs={{0,1},{1,0},{2,3},{3,2},{4,5},{5,4},{6,7},{7,6},{8,9},{9,8},{10,11... | collective-permute-start | bytes 393224 | tf_op jit(solution)/shard_map/ppermute | solution.py:405
  48.6 3.5 %collective-permute-start.16 = (bf16[128,512]{1,0:T(8,128)(2,1)S(1)}, bf16[128,512]{1,0:T(8,128)(2,1)S(1)}, u32[]{:S(2)}, u32[]{:S(2)}) collective-permute-start(bf16[128,512]{1,0:T(8,128)(2,1)S(1)} %get-tuple-element.81.refs_2_.refs_0_), channel_id=1, source_target_pairs={{0,1},{1,0},{2,3},{3,2},{4,5},{5,4},{6,7},{7,6},{8,9},{9,8},{10,11... | collective-permute-start | bytes 393224 | tf_op jit(solution)/shard_map/ppermute | solution.py:405
  49.1 4.0 %collective-permute-start.17 = (bf16[128,512]{1,0:T(8,128)(2,1)S(1)}, bf16[128,512]{1,0:T(8,128)(2,1)S(1)}, u32[]{:S(2)}, u32[]{:S(2)}) collective-permute-start(bf16[128,512]{1,0:T(8,128)(2,1)S(1)} %get-tuple-element.82.refs_4_.refs_0_), channel_id=1, source_target_pairs={{0,1},{1,0},{2,3},{3,2},{4,5},{5,4},{6,7},{7,6},{8,9},{9,8},{10,11... | collective-permute-start | bytes 393224 | tf_op jit(solution)/shard_map/ppermute | solution.py:405
  50.5 10.9 %collective-permute-start.24 = (bf16[128,1024]{1,0:T(8,128)(2,1)S(1)}, bf16[128,1024]{1,0:T(8,128)(2,1)S(1)}, u32[]{:S(2)}, u32[]{:S(2)}) collective-permute-start(bf16[128,1024]{1,0:T(8,128)(2,1)S(1)} %shard_map.90), channel_id=1, source_target_pairs={{0,2},{1,3},{2,0},{3,1},{4,6},{5,7},{6,4},{7,5},{8,10},{9,11},{10,... | collective-permute-start | bytes 786440 | tf_op jit(solution)/shard_map/ppermute | solution.py:405
  52.6 12.7 %collective-permute-start.23 = (bf16[128,1024]{1,0:T(8,128)(2,1)S(1)}, bf16[128,1024]{1,0:T(8,128)(2,1)S(1)}, u32[]{:S(2)}, u32[]{:S(2)}) collective-permute-start(bf16[128,1024]{1,0:T(8,128)(2,1)S(1)} %shard_map.89), channel_id=1, source_target_pairs={{0,2},{1,3},{2,0},{3,1},{4,6},{5,7},{6,4},{7,5},{8,10},{9,11},{10,... | collective-permute-start | bytes 786440 | tf_op jit(solution)/shard_map/ppermute | solution.py:405
  53.6 17.3 %collective-permute-start.22 = (bf16[128,1024]{1,0:T(8,128)(2,1)S(1)}, bf16[128,1024]{1,0:T(8,128)(2,1)S(1)}, u32[]{:S(2)}, u32[]{:S(2)}) collective-permute-start(bf16[128,1024]{1,0:T(8,128)(2,1)S(1)} %shard_map.88), channel_id=1, source_target_pairs={{0,2},{1,3},{2,0},{3,1},{4,6},{5,7},{6,4},{7,5},{8,10},{9,11},{10,... | collective-permute-start | bytes 786440 | tf_op jit(solution)/shard_map/ppermute | solution.py:405
  55.3 2.2 %collective-permute-start.19 = (bf16[64,512]{1,0:T(8,128)(2,1)S(1)}, bf16[64,512]{1,0:T(8,128)(2,1)S(1)}, u32[]{:S(2)}, u32[]{:S(2)}) collective-permute-start(bf16[64,512]{1,0:T(8,128)(2,1)S(1)} %get-tuple-element.84.refs_0_.refs_8_), channel_id=1, source_target_pairs={{0,1},{1,0},{2,3},{3,2},{4,5},{5,4},{6,7},{7,6},{8,9},{9,8},{10,11... | collective-permute-start | bytes 196616 | tf_op jit(solution)/shard_map/ppermute | solution.py:405
  57.0 16.7 %collective-permute-start.21 = (bf16[64,1024]{1,0:T(8,128)(2,1)S(1)}, bf16[64,1024]{1,0:T(8,128)(2,1)S(1)}, u32[]{:S(2)}, u32[]{:S(2)}) collective-permute-start(bf16[64,1024]{1,0:T(8,128)(2,1)S(1)} %shard_map.87), channel_id=1, source_target_pairs={{0,2},{1,3},{2,0},{3,1},{4,6},{5,7},{6,4},{7,5},{8,10},{9,11},{10,... | collective-permute-start | bytes 393224 | tf_op jit(solution)/shard_map/ppermute | solution.py:405
  58.0 17.8 %collective-permute-start.20 = (bf16[64,1024]{1,0:T(8,128)(2,1)S(1)}, bf16[64,1024]{1,0:T(8,128)(2,1)S(1)}, u32[]{:S(2)}, u32[]{:S(2)}) collective-permute-start(bf16[64,1024]{1,0:T(8,128)(2,1)S(1)} %shard_map.85.refs_12_), channel_id=1, source_target_pairs={{0,2},{1,3},{2,0},{3,1},{4,6},{5,7},{6,4},{7,5},{8,10},{9,11},{10,... | collective-permute-start | bytes 393224 | tf_op jit(solution)/shard_map/ppermute | solution.py:405
  (2 other events, 2.0 us)

commit v11 on v10

--- a/solution.py
+++ b/solution.py
@@ -116,13 +116,15 @@
     return call(kernel, ins, [shape(total.shape, F32)] * 5, 0, smem=1)
 
 
-def combine(state, other, own_factor, other_factor, after):
+def combine(state, other, own_factor, other_factor, which):
+    cols = slice(which * state.shape[1], (which + 1) * state.shape[1])
+
     def kernel(s_ref, o_ref, a_ref, b_ref, out_ref):
         out_ref[...] = (
-            a_ref[0:1, :] * s_ref[...].astype(F32) + b_ref[0:1, :] * o_ref[...].astype(F32)
+            a_ref[0:1, cols] * s_ref[...].astype(F32) + b_ref[0:1, cols] * o_ref[...].astype(F32)
         ).astype(BF16)
 
-    return call(kernel, [state, other, own_factor, other_factor], [shape(state.shape, BF16)], 0, after)[0]
+    return call(kernel, [state, other, own_factor, other_factor], [shape(state.shape, BF16)], 0)[0]
 
 
 def begin(me, slab, tokens, near, log_decay_rows, ws, w_out, head_size):
@@ -201,25 +203,15 @@
     return dot_dims(x, wl_ref[:, pl.ds(start, shard)], 1, 1)
 
 
-def project(me, place, x, wq, wl, total_q, total_l, after):
-    def kernel(me_ref, x_ref, wq_ref, wl_ref, q_ref, l_ref, q_out, l_out):
-        q_out[...] = q_ref[...] + dot(x_ref[...], wq_ref[place - 2])
-        l_out[...] = l_ref[...] + add_levels(me_ref, place, x_ref[...], wl_ref)
-
-    outs = [shape(t.shape, F32) for t in (total_q, total_l)]
-    flops = 2 * x.size * (total_q.shape[1] + total_l.shape[1])
-    return call(kernel, [me, x, wq, wl, total_q, total_l], outs, flops, after, smem=1, aliases={4: 0, 5: 1})
-
-
-def split(x, ways, after):
-    rows, columns = x.shape
-    part = columns // ways
-
-    def kernel(x_ref, *outs):
-        for i, o_ref in enumerate(outs):
-            o_ref[...] = x_ref[:, i * part : (i + 1) * part]
-
-    return call(kernel, [x], [shape((rows, part), x.dtype)] * ways, 0, after)
+def project(me, place, x, wq, wkv, wl, totals, after=()):
+    def kernel(me_ref, x_ref, q_ref, kv_ref, l_ref, *refs):
+        ins, outs = refs[:3], refs[3:]
+        outs[1][...] = ins[1][...] + dot(x_ref[...], kv_ref[...])
+        outs[0][...] = ins[0][...] + dot(x_ref[...], q_ref[place - 2])
+        outs[2][...] = ins[2][...] + add_levels(me_ref, place, x_ref[...], l_ref)
+
+    outs = [shape(t.shape, F32) for t in totals]
+    return call(kernel, [me, x, wq, wkv, wl, *totals], outs, 0, after, smem=1, aliases={5: 0, 6: 1, 7: 2})
 
 
 def partial(x, w, after):
@@ -227,13 +219,6 @@
         o_ref[...] = dot(x_ref[...], w_ref[...]).astype(BF16)
 
     return call(kernel, [x, w], [shape((x.shape[0], w.shape[1]), BF16)], 0, after)[0]
-
-
-def add_product(x, w, total, after):
-    def kernel(x_ref, w_ref, t_ref, o_ref):
-        o_ref[...] = t_ref[...] + dot(x_ref[...], w_ref[...])
-
-    return call(kernel, [x, w, total], [shape(total.shape, F32)], 0, after, aliases={2: 0})[0]
 
 
 def project_state(total_kv, from_near, keep, head_size):
@@ -242,7 +227,9 @@
     kv_width = total_kv.shape[1] // 2
     group = heads // (kv_width // head_size)
 
-    def kernel(total_ref, near_ref, keep_ref, k_out, v_out, s_out):
+    half = heads // 2 * head_size
+
+    def kernel(total_ref, near_ref, keep_ref, k_out, v_out, *s_outs):
         total = total_ref[...] + near_ref[...].astype(F32)
         keys = total[:, :kv_width].astype(BF16)
         values = total[:, kv_width:].astype(BF16)
@@ -255,29 +242,35 @@
                 [(kf * keep_ref[:, h : h + 1]).astype(BF16) for h in range(g * group, (g + 1) * group)],
                 axis=1,
             )
-            wide = slice(g * group * head_size, (g + 1) * group * head_size)
-            s_out[:, wide] = dot_dims(values[:, cols], weighted, 0, 0).astype(BF16)
+            states = dot_dims(values[:, cols], weighted, 0, 0).astype(BF16)
+            for i in range(group):
+                start = (g * group + i) * head_size
+                s_outs[start // half][:, start % half : start % half + head_size] = states[
+                    :, i * head_size : (i + 1) * head_size
+                ]
 
     outs = [
         shape((rows, kv_width), BF16),
         shape((rows, kv_width), BF16),
-        shape((head_size, heads * head_size), BF16),
+        shape((head_size, half), BF16),
+        shape((head_size, half), BF16),
     ]
     return call(kernel, [total_kv, from_near, keep], outs, 0)
 
 
-def attend(me, place, xs, wq, wl, total_q, total_l, k, v, dcol, drow, spans, states, head_size, level_count):
+def attend(me, place, x, wq, wl, total_q, total_l, k, v, dcol, drow, spans, states, head_size, level_count):
     rows, width = total_q.shape
     bits = len(spans)
     heads = width // head_size
     group = heads // (k.shape[1] // head_size)
     own_levels = level_count - bits
 
-    def kernel(me_ref, *refs):
-        x = jnp.concatenate([x_ref[...] for x_ref in refs[: len(xs)]], axis=1)
-        refs = refs[len(xs) :]
-        wq_ref, wl_ref, tq_ref, tl_ref, k_ref, v_ref, dcol_ref, drow_ref = refs[:8]
-        span_refs, state_refs = refs[8 : 8 + bits], refs[8 + bits : 7 + 2 * bits]
+    half = width // 2
+
+    def kernel(me_ref, x_ref, wq_ref, wl_ref, *refs):
+        x = x_ref[...]
+        tq_ref, tl_ref, k_ref, v_ref, dcol_ref, drow_ref = refs[:6]
+        span_refs, state_refs = refs[6 : 6 + bits], refs[6 + bits : 6 + bits + len(states)]
         o_ref, s_ref, q_ref, l_ref = refs[-4:]
         raw = tl_ref[...] + add_levels(me_ref, place, x, wl_ref)
         l_ref[...] = jnp.maximum(raw, 0.0) + jnp.log1p(jnp.exp(-jnp.abs(raw)))
@@ -320,51 +313,54 @@
                     if b == bits - 1:
                         s_ref[here, cols] = scaled
                     else:
-                        total = total + dot_dims(scaled, state_refs[b][:, cols], 1, 1)
+                        state_ref = state_refs[2 * b + cols.start // half]
+                        at = cols.start % half
+                        total = total + dot_dims(scaled, state_ref[:, at : at + head_size], 1, 1)
                 o_ref[here, cols] = total
 
-    ins = [me, *xs, wq, wl, total_q, total_l, k, v, dcol, drow, *spans, *states]
+    ins = [me, x, wq, wl, total_q, total_l, k, v, dcol, drow, *spans, *states]
     wide = shape((rows, width), BF16)
     outs = [shape((rows, width), F32), wide, wide, shape(total_l.shape, F32)]
     flops = 2 * rows * wq.shape[1] * width + 4 * rows * rows * width
     return call(kernel, ins, outs, flops, smem=1)[:2]
 
 
-def finish(local, scaled, state, cuts, head_size, after=()):
-    width = local.shape[1]
+def finish(local, scaled, state, which, cuts, head_size, flops, after=()):
+    width = state.shape[1]
+    offset = which * width
 
     def kernel(o_ref, q_ref, s_ref, *outs):
         for rows, n_ref in zip(cuts, outs):
             for c in range(0, width, head_size):
-                cols = slice(c, c + head_size)
-                total = o_ref[rows, cols] + dot_dims(q_ref[rows, cols], s_ref[:, cols], 1, 1)
+                cols = slice(offset + c, offset + c + head_size)
+                here = slice(c, c + head_size)
+                total = o_ref[rows, cols] + dot_dims(q_ref[rows, cols], s_ref[:, here], 1, 1)
                 mean = jnp.mean(total * total, axis=-1, keepdims=True)
-                n_ref[:, cols] = (total * lax.rsqrt(mean + 1e-05)).astype(BF16)
+                n_ref[:, here] = (total * lax.rsqrt(mean + 1e-05)).astype(BF16)
 
     outs = [shape((cut.stop - cut.start, width), BF16) for cut in cuts]
-    return call(kernel, [local, scaled, state], outs, 0, after)
-
-
-def out_block(pairs, w0, w1, dtype, after=()):
+    return call(kernel, [local, scaled, state], outs, flops, after)
+
+
+def out_block(first, second, places, w0, w1, dtype, after=()):
     columns = w1.shape[1]
-    count = len(pairs)
-    rows = sum(own.shape[0] for own, _ in pairs)
+    rows = sum(cut.stop - cut.start for _, cut in places)
     tile = min(columns, 512)
 
     def kernel(*refs):
-        w0_ref, w1_ref, o_ref = refs[2 * count :]
+        f_refs, s_refs = refs[: 2 * len(first)], refs[2 * len(first) : -3]
+        w0_ref, w1_ref, o_ref = refs[-3:]
         start = 0
-        for i in range(count):
-            a_ref, b_ref = refs[2 * i], refs[2 * i + 1]
-            here = slice(start, start + a_ref.shape[0])
+        for i, (which, cut) in enumerate(places):
+            here = slice(start, start + cut.stop - cut.start)
             start = here.stop
+            own = jnp.concatenate([f_refs[2 * which][cut, :], s_refs[2 * i][...]], axis=1)
+            near = jnp.concatenate([f_refs[2 * which + 1][cut, :], s_refs[2 * i + 1][...]], axis=1)
             for c in range(0, columns, tile):
                 cols = slice(c, c + tile)
-                o_ref[here, cols] = (
-                    dot(a_ref[...], w0_ref[:, cols]) + dot(b_ref[...], w1_ref[:, cols])
-                ).astype(dtype)
-
-    ins = [x for pair in pairs for x in pair] + [w0, w1]
+                o_ref[here, cols] = (dot(own, w0_ref[:, cols]) + dot(near, w1_ref[:, cols])).astype(dtype)
+
+    ins = [x for pair in (*first, *second) for x in pair] + [w0, w1]
     return call(kernel, ins, [shape((rows, columns), dtype)], 0, after)[0]
 
 
@@ -425,33 +421,40 @@
 
     wq, wkv, wkv_send, wl = ws
     wkv_near = swap_tp(wkv_send, 1)
-    arrived = far
-    for_near = partial(arrived, wkv_near, (total, w_far, w_here))
+    for_near = partial(far, wkv_near, (total, w_far, w_here))
     from_near = swap_tp(for_near, 1)
+    totals = project(me, 2, far, wq, wkv, wl, totals, (for_near,))
     total_q, total_kv, total_l = totals
-    total_kv = add_product(arrived, wkv, total_kv, (for_near,))
-    k, v, state = project_state(total_kv, from_near, keep, head_size)
-    total_q, total_l = project(me, 2, arrived, wq, wl, total_q, total_l, (k,))
-    arrived_near = [swap_tp(x, 1) for x in split(arrived, 4, (total_l,))]
+    far_near = swap_tp(gate(far, total_q, from_near), 1)
+    k, v, *states = project_state(total_kv, from_near, keep, head_size)
 
     earlier = []
     for b in range(seq_bits):
-        other = swap_seq(state, 1 << b)
-        earlier.append(other)
+        others = [swap_seq(state, 1 << b) for state in states]
+        earlier.append(others)
         if b < seq_bits - 1:
-            after = () if b else (total_l,)
-            state = combine(state, other, *factors[b], after)
-
+            states = [combine(*pair, *factors[b], i) for i, pair in enumerate(zip(states, others))]
+
+    before_last = [state for others in earlier[:-1] for state in others]
     local, scaled = attend(
-        me, 3, arrived_near, wq, wl, total_q, total_l, k, v, dcol, drow, spans, earlier[:-1], head_size, level_count
+        me, 3, far_near, wq, wl, total_q, total_l, k, v, dcol, drow, spans, before_last, head_size, level_count
     )
 
     unit = rows // 8
     ends = (0, 2, 4, 6, 7, 8)
     cuts = [slice(start * unit, stop * unit) for start, stop in zip(ends, ends[1:])]
-    pairs = [(x, swap_tp(x, 1)) for x in finish(local, scaled, earlier[-1], cuts, head_size)]
-    crossing = [out_block([pair], w_far_own, w_far, BF16) for pair in pairs]
-    own_block = out_block(pairs, w_here_own, w_here, F32, (crossing[-1],))
+    middle = rows // 2
+    tops = finish(local, scaled, earlier[-1][0], 0, [slice(0, middle), slice(middle, rows)], head_size, 10**8)
+    first = [(x, swap_tp(x, 1)) for x in tops]
+    second = finish(local, scaled, earlier[-1][1], 1, cuts, head_size, 0, tops)
+    second = [(x, swap_tp(x, 1)) for x in second]
+    crossing = []
+    for pair, cut in zip(second, cuts):
+        i = cut.start // middle
+        here = slice(cut.start - i * middle, cut.stop - i * middle)
+        crossing.append(out_block([first[i]], [pair], [(0, here)], w_far_own, w_far, BF16))
+    places = [(c.start // middle, slice(c.start % middle, c.start % middle + c.stop - c.start)) for c in cuts]
+    own_block = out_block(first, second, places, w_here_own, w_here, F32, (crossing[-1],))
     out = None
     for cut, x in zip(cuts, crossing):
         out = add_rows(own_block, swap_tp(x, 2), out, cut.start, unit)

time: 76.6 us -> 77.1 us (level)
  starting transfers between devices: 23.5 us -> 26.7 us
  waiting for transfers between devices: 31 us -> 28.5 us
    ppermute x5 -> x8, starting transfers between devices: 11.3 us -> 14.7 us  [swap_seq(): return lax.ppermute(x, 'seq', [(i, i ^ bit) for i in range(seq_size)])]
    ppermute x5 -> x8, waiting for transfers between devices: 8.75 us -> 7.14 us  [swap_seq(): return lax.ppermute(x, 'seq', [(i, i ^ bit) for i in range(seq_size)])]
    ppermute x20 -> x19, waiting for transfers between devices: 22.3 us -> 21.4 us  [swap_tp(): return lax.ppermute(x, 'tp', [(i, i ^ bit) for i in range(4)])]
    ppermute x20 -> x19, starting transfers between devices: 12.2 us -> 12 us  [swap_tp(): return lax.ppermute(x, 'tp', [(i, i ^ bit) for i in range(4)])]
    pallas_call x18 -> x19, Pallas kernels: 17.4 us -> 17.4 us  [call(): pl.pallas_call(run, in_specs=[SMEM] * smem + [HBM] * hbm + [VMEM] * (coun...]
  transfers between devices with their start and end apart: 25 -> 27, of which waited for: 13 -> 12; matrix products, arithmetic and copies ran while one was open for 0% -> 0% of each run, Pallas kernels for 24% -> 26%
where the time goes in v11:
time: 77.1 us; the launch traced here: 76.9 us
  waiting for transfers between devices  28.5 us (37%)
  starting transfers between devices  26.7 us (35%)
  Pallas kernels  20.9 us (27%)
    ppermute x19, waiting for transfers between devices, swap_tp(): return lax.ppermute(x, 'tp', [(i, i ^ bit) for i in range(4)])  21.4 us
    pallas_call x19, Pallas kernels, call(): pl.pallas_call(run, in_specs=[SMEM] * smem + [HBM] * hbm + [VMEM] * (coun...  17.4 us
    ppermute x8, starting transfers between devices, swap_seq(): return lax.ppermute(x, 'seq', [(i, i ^ bit) for i in range(seq_size)])  14.7 us
    ppermute x19, starting transfers between devices, swap_tp(): return lax.ppermute(x, 'tp', [(i, i ^ bit) for i in range(4)])  12 us
    ppermute x8, waiting for transfers between devices, swap_seq(): return lax.ppermute(x, 'seq', [(i, i ^ bit) for i in range(seq_size)])  7.14 us
    pallas_call x5, Pallas kernels, add_rows(): pl.pallas_call(kernel, grid=(rows // unit,), in_specs=specs, out_specs=pl...  3.54 us
  transfers between devices with their start and end apart: 27, of which 12 were waited for; matrix products, arithmetic and copies ran while one was open for 0% of the time, Pallas kernels for 26%

profile of v11, /device:TPU:0, one launch (start us, length us, event | category | flops | bytes accessed | tf_op | source)
XLA Modules:
  0.0 76.9 jit_solution(8182988942879961501)
XLA Ops:
  0.5 2.5 %collective-permute-start = (bf16[512,1024]{1,0:T(8,128)(2,1)}, bf16[512,1024]{1,0:T(8,128)(2,1)S(1)}, u32[]{:S(2)}, u32[]{:S(2)}) collective-permute-start(bf16[512,1024]{1,0:T(8,128)(2,1)} %refs_2_.1), channel_id=1, source_target_pairs={{0,2},{1,3},{2,0},{3,1},{4,6},{5,7},{6,4},{7,5},{8,10},{9,11},{10,... | collective-permute-start | bytes 3145736 | tf_op jit(solution)/shard_map/ppermute | solution.py:401
  3.7 5.4 %shard_map.73 = (f32[512,512]{1,0:T(8,128)S(1)}, f32[512,256]{1,0:T(8,128)S(1)}, f32[512,24]{1,0:T(8,128)S(1)}, bf16[2,1024,512]{2,1,0:T(8,128)(2,1)S(1)}, bf16[...) custom-call(s32[1]{0:T(128)} %bitcast.refs_0_, ...), custom_call_target="tpu_custom_call" | custom-call | tf_op jit(solution)/shard_map/pallas_call | solution.py:41
  10.0 2.6 %collective-permute-start.3 = (f32[8,512]{1,0:T(8,128)S(1)}, f32[8,512]{1,0:T(8,128)S(1)}, u32[]{:S(2)}, u32[]{:S(2)}) collective-permute-start(f32[8,512]{1,0:T(8,128)S(1)} %get-tuple-element.53.refs_1_), channel_id=1, source_target_pairs={{0,4},{4,0},{8,12},{12,8},{16,20},{20,16},{24,28},{28,24},{1,5},{5... | collective-permute-start | bytes 49160 | tf_op jit(solution)/shard_map/ppermute | solution.py:404
  12.6 1.7 %collective-permute-done.3.refs_2_ = f32[8,512]{1,0:T(8,128)S(1)} collective-permute-done((f32[8,512]{1,0:T(8,128)S(1)}, f32[8,512]{1,0:T(8,128)S(1)}, u32[]{:S(2)}, u32[]{:S(2)}) %collective-permute-start.3) | collective-permute-done | bytes 16416 | tf_op jit(solution)/shard_map/ppermute | solution.py:404
  14.3 2.2 %collective-permute-start.4 = (f32[8,512]{1,0:T(8,128)S(1)}, f32[8,512]{1,0:T(8,128)S(1)}, u32[]{:S(2)}, u32[]{:S(2)}) collective-permute-start(f32[8,512]{1,0:T(8,128)S(1)} %get-tuple-element.54.refs_1_), channel_id=1, source_target_pairs={{0,8},{4,12},{8,0},{12,4},{16,24},{20,28},{24,16},{28,20},{1,9},{5... | collective-permute-start | bytes 49160 | tf_op jit(solution)/shard_map/ppermute | solution.py:404
  16.5 1.7 %collective-permute-done.4.refs_2_ = f32[8,512]{1,0:T(8,128)S(1)} collective-permute-done((f32[8,512]{1,0:T(8,128)S(1)}, f32[8,512]{1,0:T(8,128)S(1)}, u32[]{:S(2)}, u32[]{:S(2)}) %collective-permute-start.4) | collective-permute-done | bytes 16416 | tf_op jit(solution)/shard_map/ppermute | solution.py:404
  18.8 8.2 %collective-permute-done.refs_0_.refs_1_ = bf16[512,1024]{1,0:T(8,128)(2,1)S(1)} collective-permute-done((bf16[512,1024]{1,0:T(8,128)(2,1)}, bf16[512,1024]{1,0:T(8,128)(2,1)S(1)}, u32[]{:S(2)}, u32[]{:S(2)}) %collective-permute-start) | collective-permute-done | bytes 1048608 | tf_op jit(solution)/shard_map/ppermute | solution.py:401
  27.5 1.3 %shard_map.77 = (f32[512,512]{1,0:T(8,128)S(1)}, f32[512,256]{1,0:T(8,128)S(1)}, f32[512,24]{1,0:T(8,128)S(1)}) custom-call(s32[1]{0:T(128)} %bitcast.refs_0_, bf16[512,1024]{1,0:T(8,128)(2,1)S(1)} %collective-permute-done.refs_0_.refs_1_, ...), custom_call_target="tpu_custom_call", output_to_operand_aliasing={{0}: (5, {}), {1}: (6, {}), {2}: (7, {})} | custom-call | tf_op jit(solution)/shard_map/pallas_call | solution.py:41
  30.0 1.8 %collective-permute-start.9 = (bf16[128,256]{1,0:T(8,128)(2,1)S(1)}, bf16[128,256]{1,0:T(8,128)(2,1)S(1)}, u32[]{:S(2)}, u32[]{:S(2)}) collective-permute-start(bf16[128,256]{1,0:T(8,128)(2,1)S(1)} %get-tuple-element.70.refs_0_), channel_id=1, source_target_pairs={{0,4},{4,0},{8,12},{12,8},{16,20},{20,16},{24,28},{28,24},{1,5},{5... | collective-permute-start | bytes 196616 | tf_op jit(solution)/shard_map/ppermute | solution.py:404
  32.1 2.4 %collective-permute-done.9.refs_1_.refs_13_ = bf16[128,256]{1,0:T(8,128)(2,1)S(1)} collective-permute-done((bf16[128,256]{1,0:T(8,128)(2,1)S(1)}, bf16[128,256]{1,0:T(8,128)(2,1)S(1)}, u32[]{:S(2)}, u32[]{:S(2)}) %collective-permute-start.9) | collective-permute-done | bytes 65568 | tf_op jit(solution)/shard_map/ppermute | solution.py:404
  34.6 2.1 %collective-permute-start.11 = (bf16[128,256]{1,0:T(8,128)(2,1)S(1)}, bf16[128,256]{1,0:T(8,128)(2,1)S(1)}, u32[]{:S(2)}, u32[]{:S(2)}) collective-permute-start(bf16[128,256]{1,0:T(8,128)(2,1)S(1)} %shard_map.80.refs_0_), channel_id=1, source_target_pairs={{0,8},{4,12},{8,0},{12,4},{16,24},{20,28},{24,16},{28,20},{1,9},{5... | collective-permute-start | bytes 196616 | tf_op jit(solution)/shard_map/ppermute | solution.py:404
  36.7 1.0 %collective-permute-start.12 = (bf16[128,256]{1,0:T(8,128)(2,1)S(1)}, bf16[128,256]{1,0:T(8,128)(2,1)S(1)}, u32[]{:S(2)}, u32[]{:S(2)}) collective-permute-start(bf16[128,256]{1,0:T(8,128)(2,1)S(1)} %shard_map.81.refs_0_), channel_id=1, source_target_pairs={{0,8},{4,12},{8,0},{12,4},{16,24},{20,28},{24,16},{28,20},{1,9},{5... | collective-permute-start | bytes 196616 | tf_op jit(solution)/shard_map/ppermute | solution.py:404
  37.8 1.3 %collective-permute-done.11.refs_15_.refs_1_ = bf16[128,256]{1,0:T(8,128)(2,1)S(1)} collective-permute-done((bf16[128,256]{1,0:T(8,128)(2,1)S(1)}, bf16[128,256]{1,0:T(8,128)(2,1)S(1)}, u32[]{:S(2)}, u32[]{:S(2)}) %collective-permute-start.11) | collective-permute-done | bytes 65568 | tf_op jit(solution)/shard_map/ppermute | solution.py:404
  39.1 3.0 %collective-permute-start.13 = (bf16[128,256]{1,0:T(8,128)(2,1)S(1)}, bf16[128,256]{1,0:T(8,128)(2,1)S(1)}, u32[]{:S(2)}, u32[]{:S(2)}) collective-permute-start(bf16[128,256]{1,0:T(8,128)(2,1)S(1)} %shard_map.83), channel_id=1, source_target_pairs={{0,16},{4,20},{8,24},{12,28},{16,0},{20,4},{24,8},{28,12},{1,17},{... | collective-permute-start | bytes 196616 | tf_op jit(solution)/shard_map/ppermute | solution.py:404
  42.2 1.6 %collective-permute-start.16 = (bf16[128,256]{1,0:T(8,128)(2,1)S(1)}, bf16[128,256]{1,0:T(8,128)(2,1)S(1)}, u32[]{:S(2)}, u32[]{:S(2)}) collective-permute-start(bf16[128,256]{1,0:T(8,128)(2,1)S(1)} %shard_map.85), channel_id=1, source_target_pairs={{0,16},{4,20},{8,24},{12,28},{16,0},{20,4},{24,8},{28,12},{1,17},{... | collective-permute-start | bytes 196616 | tf_op jit(solution)/shard_map/ppermute | solution.py:404
  43.8 4.0 %shard_map.82 = (f32[512,512]{1,0:T(8,128)S(1)}, bf16[512,512]{1,0:T(8,128)(2,1)S(1)}, bf16[512,512]{1,0:T(8,128)(2,1)}, f32[512,24]{1,0:T(8,128)}) custom-call(s32[1]{0:T(128)} %bitcast.refs_0_, bf16[512,1024]{1,0:T(8,128)(2,1)S(1)} %collective-permute-done.8.refs_1_, bf16[2,1024,512]{2,1,0:T(8,128)(2,1)S(1)} %get-tuple-element.46.refs_2_, ...), custom_call_target="tpu_custom_call" | custom-call | flops 1073741824 | bytes 7176196 | tf_op jit(solution)/shard_map/pallas_call | solution.py:41
  51.0 1.6 %collective-permute-start.25 = (bf16[128,1024]{1,0:T(8,128)(2,1)S(1)}, bf16[128,1024]{1,0:T(8,128)(2,1)S(1)}, u32[]{:S(2)}, u32[]{:S(2)}) collective-permute-start(bf16[128,1024]{1,0:T(8,128)(2,1)S(1)} %shard_map.91), channel_id=1, source_target_pairs={{0,2},{1,3},{2,0},{3,1},{4,6},{5,7},{6,4},{7,5},{8,10},{9,11},{10,... | collective-permute-start | bytes 786440 | tf_op jit(solution)/shard_map/ppermute | solution.py:401
  54.1 1.6 %collective-permute-start.24 = (bf16[128,1024]{1,0:T(8,128)(2,1)S(1)}, bf16[128,1024]{1,0:T(8,128)(2,1)S(1)}, u32[]{:S(2)}, u32[]{:S(2)}) collective-permute-start(bf16[128,1024]{1,0:T(8,128)(2,1)S(1)} %shard_map.90), channel_id=1, source_target_pairs={{0,2},{1,3},{2,0},{3,1},{4,6},{5,7},{6,4},{7,5},{8,10},{9,11},{10,... | collective-permute-start | bytes 786440 | tf_op jit(solution)/shard_map/ppermute | solution.py:401
  58.4 1.6 %collective-permute-start.22 = (bf16[64,1024]{1,0:T(8,128)(2,1)S(1)}, bf16[64,1024]{1,0:T(8,128)(2,1)S(1)}, u32[]{:S(2)}, u32[]{:S(2)}) collective-permute-start(bf16[64,1024]{1,0:T(8,128)(2,1)S(1)} %shard_map.87.refs_16_), channel_id=1, source_target_pairs={{0,2},{1,3},{2,0},{3,1},{4,6},{5,7},{6,4},{7,5},{8,10},{9,11},{10,... | collective-permute-start | bytes 393224 | tf_op jit(solution)/shard_map/ppermute | solution.py:401
  60.0 1.7 %shard_map.88.h_ref = f32[512,1024]{1,0:T(8,128)S(1)} custom-call(bf16[256,256]{1,0:T(8,128)(2,1)S(1)} %get-tuple-element.78.refs_3_.refs_0_, bf16[256,256]{1,0:T(8,128)(2,1)S(1)} %collective-permute-done.14.refs_1_, bf16[256,256]{1,0:T(8,128)(2,1)S(1)} %get-tuple-element.79.refs_4_.refs_0_.refs_2_, ...), custom_call_target="tpu_custom_call" | custom-call | tf_op jit(solution)/shard_map/pallas_call | solution.py:41
  61.8 4.1 %collective-permute-done.26.a_ref = bf16[128,1024]{1,0:T(8,128)(2,1)S(1)} collective-permute-done((bf16[128,1024]{1,0:T(8,128)(2,1)S(1)}, bf16[128,1024]{1,0:T(8,128)(2,1)S(1)}, u32[]{:S(2)}, u32[]{:S(2)}) %collective-permute-start.26) | collective-permute-done | bytes 262176 | tf_op jit(solution)/shard_map/ppermute | solution.py:401
  67.3 4.2 %collective-permute-done.24.a_ref = bf16[128,1024]{1,0:T(8,128)(2,1)S(1)} collective-permute-done((bf16[128,1024]{1,0:T(8,128)(2,1)S(1)}, bf16[128,1024]{1,0:T(8,128)(2,1)S(1)}, u32[]{:S(2)}, u32[]{:S(2)}) %collective-permute-start.24) | collective-permute-done | bytes 262176 | tf_op jit(solution)/shard_map/ppermute | solution.py:401
  72.2 2.1 %collective-permute-done.23.a_ref = bf16[64,1024]{1,0:T(8,128)(2,1)S(1)} collective-permute-done((bf16[64,1024]{1,0:T(8,128)(2,1)S(1)}, bf16[64,1024]{1,0:T(8,128)(2,1)S(1)}, u32[]{:S(2)}, u32[]{:S(2)}) %collective-permute-start.23) | collective-permute-done | bytes 131104 | tf_op jit(solution)/shard_map/ppermute | solution.py:401
  74.9 1.3 %collective-permute-done.22.a_ref = bf16[64,1024]{1,0:T(8,128)(2,1)S(1)} collective-permute-done((bf16[64,1024]{1,0:T(8,128)(2,1)S(1)}, bf16[64,1024]{1,0:T(8,128)(2,1)S(1)}, u32[]{:S(2)}, u32[]{:S(2)}) %collective-permute-start.22) | collective-permute-done | bytes 131104 | tf_op jit(solution)/shard_map/ppermute | solution.py:401
  (57 shorter events, 15.8 us)
Async XLA Ops:
  0.0 3.0 %collective-permute-start.1 = (bf16[512,1024]{1,0:T(8,128)(2,1)}, bf16[512,1024]{1,0:T(8,128)(2,1)S(1)}, u32[]{:S(2)}, u32[]{:S(2)}) collective-permute-start(bf16[512,1024]{1,0:T(8,128)(2,1)} %refs_2_.1), channel_id=1, source_target_pairs={{0,1},{1,0},{2,3},{3,2},{4,5},{5,4},{6,7},{7,6},{8,9},{9,8},{10,11... | collective-permute-start | bytes 3145736 | tf_op jit(solution)/shard_map/ppermute | solution.py:401
  0.5 26.6 %collective-permute-start = (bf16[512,1024]{1,0:T(8,128)(2,1)}, bf16[512,1024]{1,0:T(8,128)(2,1)S(1)}, u32[]{:S(2)}, u32[]{:S(2)}) collective-permute-start(bf16[512,1024]{1,0:T(8,128)(2,1)} %refs_2_.1), channel_id=1, source_target_pairs={{0,2},{1,3},{2,0},{3,1},{4,6},{5,7},{6,4},{7,5},{8,10},{9,11},{10,... | collective-permute-start | bytes 3145736 | tf_op jit(solution)/shard_map/ppermute | solution.py:401
  9.0 18.0 %collective-permute-start.5 = (bf16[512,1024]{1,0:T(8,128)(2,1)S(1)}, bf16[512,1024]{1,0:T(8,128)(2,1)S(1)}, u32[]{:S(2)}, u32[]{:S(2)}) collective-permute-start(bf16[512,1024]{1,0:T(8,128)(2,1)S(1)} %get-tuple-element.57), channel_id=1, source_target_pairs={{0,1},{1,0},{2,3},{3,2},{4,5},{5,4},{6,7},{7,6},{8,9},{9,8},{10,11... | collective-permute-start | bytes 3145736 | tf_op jit(solution)/shard_map/ppermute | solution.py:401
  9.5 17.6 %collective-permute-start.6 = (bf16[512,1024]{1,0:T(8,128)(2,1)S(1)}, bf16[512,1024]{1,0:T(8,128)(2,1)S(1)}, u32[]{:S(2)}, u32[]{:S(2)}) collective-permute-start(bf16[512,1024]{1,0:T(8,128)(2,1)S(1)} %get-tuple-element.58), channel_id=1, source_target_pairs={{0,1},{1,0},{2,3},{3,2},{4,5},{5,4},{6,7},{7,6},{8,9},{9,8},{10,11... | collective-permute-start | bytes 3145736 | tf_op jit(solution)/shard_map/ppermute | solution.py:401
  9.6 17.4 %collective-permute-start.2 = (bf16[1024,256]{1,0:T(8,128)(2,1)S(1)}, bf16[1024,256]{1,0:T(8,128)(2,1)S(1)}, u32[]{:S(2)}, u32[]{:S(2)}) collective-permute-start(bf16[1024,256]{1,0:T(8,128)(2,1)S(1)} %get-tuple-element.52), channel_id=1, source_target_pairs={{0,1},{1,0},{2,3},{3,2},{4,5},{5,4},{6,7},{7,6},{8,9},{9,8},{10,11... | collective-permute-start | bytes 1572872 | tf_op jit(solution)/shard_map/ppermute | solution.py:401
  10.0 4.3 %collective-permute-start.3 = (f32[8,512]{1,0:T(8,128)S(1)}, f32[8,512]{1,0:T(8,128)S(1)}, u32[]{:S(2)}, u32[]{:S(2)}) collective-permute-start(f32[8,512]{1,0:T(8,128)S(1)} %get-tuple-element.53.refs_1_), channel_id=1, source_target_pairs={{0,4},{4,0},{8,12},{12,8},{16,20},{20,16},{24,28},{28,24},{1,5},{5... | collective-permute-start | bytes 49160 | tf_op jit(solution)/shard_map/ppermute | solution.py:404
  14.3 3.9 %collective-permute-start.4 = (f32[8,512]{1,0:T(8,128)S(1)}, f32[8,512]{1,0:T(8,128)S(1)}, u32[]{:S(2)}, u32[]{:S(2)}) collective-permute-start(f32[8,512]{1,0:T(8,128)S(1)} %get-tuple-element.54.refs_1_), channel_id=1, source_target_pairs={{0,8},{4,12},{8,0},{12,4},{16,24},{20,28},{24,16},{28,20},{1,9},{5... | collective-permute-start | bytes 49160 | tf_op jit(solution)/shard_map/ppermute | solution.py:404
  29.1 14.7 %collective-permute-start.8 = (bf16[512,1024]{1,0:T(8,128)(2,1)S(1)}, bf16[512,1024]{1,0:T(8,128)(2,1)S(1)}, u32[]{:S(2)}, u32[]{:S(2)}) collective-permute-start(bf16[512,1024]{1,0:T(8,128)(2,1)S(1)} %shard_map.78), channel_id=1, source_target_pairs={{0,1},{1,0},{2,3},{3,2},{4,5},{5,4},{6,7},{7,6},{8,9},{9,8},{10,11... | collective-permute-start | bytes 3145736 | tf_op jit(solution)/shard_map/ppermute | solution.py:401
  30.0 4.5 %collective-permute-start.9 = (bf16[128,256]{1,0:T(8,128)(2,1)S(1)}, bf16[128,256]{1,0:T(8,128)(2,1)S(1)}, u32[]{:S(2)}, u32[]{:S(2)}) collective-permute-start(bf16[128,256]{1,0:T(8,128)(2,1)S(1)} %get-tuple-element.70.refs_0_), channel_id=1, source_target_pairs={{0,4},{4,0},{8,12},{12,8},{16,20},{20,16},{24,28},{28,24},{1,5},{5... | collective-permute-start | bytes 196616 | tf_op jit(solution)/shard_map/ppermute | solution.py:404
  31.8 4.9 %collective-permute-start.10 = (bf16[128,256]{1,0:T(8,128)(2,1)S(1)}, bf16[128,256]{1,0:T(8,128)(2,1)S(1)}, u32[]{:S(2)}, u32[]{:S(2)}) collective-permute-start(bf16[128,256]{1,0:T(8,128)(2,1)S(1)} %get-tuple-element.71.refs_0_), channel_id=1, source_target_pairs={{0,4},{4,0},{8,12},{12,8},{16,20},{20,16},{24,28},{28,24},{1,5},{5... | collective-permute-start | bytes 196616 | tf_op jit(solution)/shard_map/ppermute | solution.py:404
  34.6 4.5 %collective-permute-start.11 = (bf16[128,256]{1,0:T(8,128)(2,1)S(1)}, bf16[128,256]{1,0:T(8,128)(2,1)S(1)}, u32[]{:S(2)}, u32[]{:S(2)}) collective-permute-start(bf16[128,256]{1,0:T(8,128)(2,1)S(1)} %shard_map.80.refs_0_), channel_id=1, source_target_pairs={{0,8},{4,12},{8,0},{12,4},{16,24},{20,28},{24,16},{28,20},{1,9},{5... | collective-permute-start | bytes 196616 | tf_op jit(solution)/shard_map/ppermute | solution.py:404
  36.7 5.4 %collective-permute-start.12 = (bf16[128,256]{1,0:T(8,128)(2,1)S(1)}, bf16[128,256]{1,0:T(8,128)(2,1)S(1)}, u32[]{:S(2)}, u32[]{:S(2)}) collective-permute-start(bf16[128,256]{1,0:T(8,128)(2,1)S(1)} %shard_map.81.refs_0_), channel_id=1, source_target_pairs={{0,8},{4,12},{8,0},{12,4},{16,24},{20,28},{24,16},{28,20},{1,9},{5... | collective-permute-start | bytes 196616 | tf_op jit(solution)/shard_map/ppermute | solution.py:404
  39.1 8.7 %collective-permute-start.13 = (bf16[128,256]{1,0:T(8,128)(2,1)S(1)}, bf16[128,256]{1,0:T(8,128)(2,1)S(1)}, u32[]{:S(2)}, u32[]{:S(2)}) collective-permute-start(bf16[128,256]{1,0:T(8,128)(2,1)S(1)} %shard_map.83), channel_id=1, source_target_pairs={{0,16},{4,20},{8,24},{12,28},{16,0},{20,4},{24,8},{28,12},{1,17},{... | collective-permute-start | bytes 196616 | tf_op jit(solution)/shard_map/ppermute | solution.py:404
  42.2 6.6 %collective-permute-start.16 = (bf16[128,256]{1,0:T(8,128)(2,1)S(1)}, bf16[128,256]{1,0:T(8,128)(2,1)S(1)}, u32[]{:S(2)}, u32[]{:S(2)}) collective-permute-start(bf16[128,256]{1,0:T(8,128)(2,1)S(1)} %shard_map.85), channel_id=1, source_target_pairs={{0,16},{4,20},{8,24},{12,28},{16,0},{20,4},{24,8},{28,12},{1,17},{... | collective-permute-start | bytes 196616 | tf_op jit(solution)/shard_map/ppermute | solution.py:404
  48.2 2.3 %collective-permute-start.14 = (bf16[256,256]{1,0:T(8,128)(2,1)S(1)}, bf16[256,256]{1,0:T(8,128)(2,1)S(1)}, u32[]{:S(2)}, u32[]{:S(2)}) collective-permute-start(bf16[256,256]{1,0:T(8,128)(2,1)S(1)} %get-tuple-element.78.refs_3_.refs_0_), channel_id=1, source_target_pairs={{0,1},{1,0},{2,3},{3,2},{4,5},{5,4},{6,7},{7,6},{8,9},{9,8},{10,11... | collective-permute-start | bytes 393224 | tf_op jit(solution)/shard_map/ppermute | solution.py:401
  48.2 5.4 %collective-permute-start.15 = (bf16[256,256]{1,0:T(8,128)(2,1)S(1)}, bf16[256,256]{1,0:T(8,128)(2,1)S(1)}, u32[]{:S(2)}, u32[]{:S(2)}) collective-permute-start(bf16[256,256]{1,0:T(8,128)(2,1)S(1)} %get-tuple-element.79.refs_4_.refs_0_.refs_2_), channel_id=1, source_target_pairs={{0,1},{1,0},{2,3},{3,2},{4,5},{5,4},{6,7},{7,6},{8,9},{9,8},{10,11... | collective-permute-start | bytes 393224 | tf_op jit(solution)/shard_map/ppermute | solution.py:401
  49.3 3.2 %collective-permute-start.17 = (bf16[128,256]{1,0:T(8,128)(2,1)S(1)}, bf16[128,256]{1,0:T(8,128)(2,1)S(1)}, u32[]{:S(2)}, u32[]{:S(2)}) collective-permute-start(bf16[128,256]{1,0:T(8,128)(2,1)S(1)} %get-tuple-element.80.refs_4_.refs_2_), channel_id=1, source_target_pairs={{0,1},{1,0},{2,3},{3,2},{4,5},{5,4},{6,7},{7,6},{8,9},{9,8},{10,11... | collective-permute-start | bytes 196616 | tf_op jit(solution)/shard_map/ppermute | solution.py:401
  49.8 3.9 %collective-permute-start.19 = (bf16[128,256]{1,0:T(8,128)(2,1)S(1)}, bf16[128,256]{1,0:T(8,128)(2,1)S(1)}, u32[]{:S(2)}, u32[]{:S(2)}) collective-permute-start(bf16[128,256]{1,0:T(8,128)(2,1)S(1)} %get-tuple-element.82.refs_8_.refs_2_), channel_id=1, source_target_pairs={{0,1},{1,0},{2,3},{3,2},{4,5},{5,4},{6,7},{7,6},{8,9},{9,8},{10,11... | collective-permute-start | bytes 196616 | tf_op jit(solution)/shard_map/ppermute | solution.py:401
  51.0 15.6 %collective-permute-start.25 = (bf16[128,1024]{1,0:T(8,128)(2,1)S(1)}, bf16[128,1024]{1,0:T(8,128)(2,1)S(1)}, u32[]{:S(2)}, u32[]{:S(2)}) collective-permute-start(bf16[128,1024]{1,0:T(8,128)(2,1)S(1)} %shard_map.91), channel_id=1, source_target_pairs={{0,2},{1,3},{2,0},{3,1},{4,6},{5,7},{6,4},{7,5},{8,10},{9,11},{10,... | collective-permute-start | bytes 786440 | tf_op jit(solution)/shard_map/ppermute | solution.py:401
  53.0 12.8 %collective-permute-start.26 = (bf16[128,1024]{1,0:T(8,128)(2,1)S(1)}, bf16[128,1024]{1,0:T(8,128)(2,1)S(1)}, u32[]{:S(2)}, u32[]{:S(2)}) collective-permute-start(bf16[128,1024]{1,0:T(8,128)(2,1)S(1)} %shard_map.92), channel_id=1, source_target_pairs={{0,2},{1,3},{2,0},{3,1},{4,6},{5,7},{6,4},{7,5},{8,10},{9,11},{10,... | collective-permute-start | bytes 786440 | tf_op jit(solution)/shard_map/ppermute | solution.py:401
  54.1 17.3 %collective-permute-start.24 = (bf16[128,1024]{1,0:T(8,128)(2,1)S(1)}, bf16[128,1024]{1,0:T(8,128)(2,1)S(1)}, u32[]{:S(2)}, u32[]{:S(2)}) collective-permute-start(bf16[128,1024]{1,0:T(8,128)(2,1)S(1)} %shard_map.90), channel_id=1, source_target_pairs={{0,2},{1,3},{2,0},{3,1},{4,6},{5,7},{6,4},{7,5},{8,10},{9,11},{10,... | collective-permute-start | bytes 786440 | tf_op jit(solution)/shard_map/ppermute | solution.py:401
  55.7 2.3 %collective-permute-start.21 = (bf16[64,256]{1,0:T(8,128)(2,1)S(1)}, bf16[64,256]{1,0:T(8,128)(2,1)S(1)}, u32[]{:S(2)}, u32[]{:S(2)}) collective-permute-start(bf16[64,256]{1,0:T(8,128)(2,1)S(1)} %get-tuple-element.84.refs_2_.refs_12_), channel_id=1, source_target_pairs={{0,1},{1,0},{2,3},{3,2},{4,5},{5,4},{6,7},{7,6},{8,9},{9,8},{10,11... | collective-permute-start | bytes 98312 | tf_op jit(solution)/shard_map/ppermute | solution.py:401
  57.4 16.9 %collective-permute-start.23 = (bf16[64,1024]{1,0:T(8,128)(2,1)S(1)}, bf16[64,1024]{1,0:T(8,128)(2,1)S(1)}, u32[]{:S(2)}, u32[]{:S(2)}) collective-permute-start(bf16[64,1024]{1,0:T(8,128)(2,1)S(1)} %shard_map.89), channel_id=1, source_target_pairs={{0,2},{1,3},{2,0},{3,1},{4,6},{5,7},{6,4},{7,5},{8,10},{9,11},{10,... | collective-permute-start | bytes 393224 | tf_op jit(solution)/shard_map/ppermute | solution.py:401
  58.4 17.8 %collective-permute-start.22 = (bf16[64,1024]{1,0:T(8,128)(2,1)S(1)}, bf16[64,1024]{1,0:T(8,128)(2,1)S(1)}, u32[]{:S(2)}, u32[]{:S(2)}) collective-permute-start(bf16[64,1024]{1,0:T(8,128)(2,1)S(1)} %shard_map.87.refs_16_), channel_id=1, source_target_pairs={{0,2},{1,3},{2,0},{3,1},{4,6},{5,7},{6,4},{7,5},{8,10},{9,11},{10,... | collective-permute-start | bytes 393224 | tf_op jit(solution)/shard_map/ppermute | solution.py:401
  (4 other events, 4.8 us)

commit v12 on v11

--- a/solution.py
+++ b/solution.py
@@ -116,7 +116,7 @@
     return call(kernel, ins, [shape(total.shape, F32)] * 5, 0, smem=1)
 
 
-def combine(state, other, own_factor, other_factor, which):
+def combine(state, other, own_factor, other_factor, which, after):
     cols = slice(which * state.shape[1], (which + 1) * state.shape[1])
 
     def kernel(s_ref, o_ref, a_ref, b_ref, out_ref):
@@ -124,7 +124,7 @@
             a_ref[0:1, cols] * s_ref[...].astype(F32) + b_ref[0:1, cols] * o_ref[...].astype(F32)
         ).astype(BF16)
 
-    return call(kernel, [state, other, own_factor, other_factor], [shape(state.shape, BF16)], 0)[0]
+    return call(kernel, [state, other, own_factor, other_factor], [shape(state.shape, BF16)], 0, after)[0]
 
 
 def begin(me, slab, tokens, near, log_decay_rows, ws, w_out, head_size):
@@ -258,85 +258,101 @@
     return call(kernel, [total_kv, from_near, keep], outs, 0)
 
 
-def attend(me, place, x, wq, wl, total_q, total_l, k, v, dcol, drow, spans, states, head_size, level_count):
-    rows, width = total_q.shape
-    bits = len(spans)
+def queries(me, place, x, wq, wl, total_q, total_l):
+    def kernel(me_ref, x_ref, wq_ref, wl_ref, tq_ref, tl_ref, q_ref, l_ref):
+        raw = tl_ref[...] + add_levels(me_ref, place, x_ref[...], wl_ref)
+        l_ref[...] = jnp.maximum(raw, 0.0) + jnp.log1p(jnp.exp(-jnp.abs(raw)))
+        q_ref[...] = (tq_ref[...] + dot(x_ref[...], wq_ref[place - 2])).astype(BF16)
+
+    outs = [shape(total_q.shape, BF16), shape(total_l.shape, F32)]
+    return call(kernel, [me, x, wq, wl, total_q, total_l], outs, 0, smem=1)
+
+
+def column(ref, rows, place):
+    return jnp.broadcast_to(ref[rows, place : place + 1], (BLOCK, BLOCK))
+
+
+def attend(q, level, k, v, dcol, drow, which, head_size, level_count):
+    rows, width = q.shape
     heads = width // head_size
     group = heads // (k.shape[1] // head_size)
-    own_levels = level_count - bits
-
-    half = width // 2
-
-    def kernel(me_ref, x_ref, wq_ref, wl_ref, *refs):
-        x = x_ref[...]
-        tq_ref, tl_ref, k_ref, v_ref, dcol_ref, drow_ref = refs[:6]
-        span_refs, state_refs = refs[6 : 6 + bits], refs[6 + bits : 6 + bits + len(states)]
-        o_ref, s_ref, q_ref, l_ref = refs[-4:]
-        raw = tl_ref[...] + add_levels(me_ref, place, x, wl_ref)
-        l_ref[...] = jnp.maximum(raw, 0.0) + jnp.log1p(jnp.exp(-jnp.abs(raw)))
-        q_ref[...] = (tq_ref[...] + dot(x, wq_ref[place - 2])).astype(BF16)
+    first = which * heads // 2
+
+    def kernel(q_ref, l_ref, k_ref, v_ref, dcol_ref, drow_ref, o_ref):
         row_id = lax.broadcasted_iota(jnp.int32, (BLOCK, BLOCK), 0)
         col_id = lax.broadcasted_iota(jnp.int32, (BLOCK, BLOCK), 1)
         causal = row_id >= col_id
-        for h in range(heads):
-            g = h // group
+        for h in range(first, first + heads // 2):
             cols = slice(h * head_size, (h + 1) * head_size)
-            kv = slice(g * head_size, (g + 1) * head_size)
+            kv = slice(h // group * head_size, (h // group + 1) * head_size)
             for i in range(rows // BLOCK):
                 here = slice(i * BLOCK, (i + 1) * BLOCK)
                 span = (i + 1) * BLOCK
-                query = q_ref[here, cols]
-                scores = dot_dims(query, k_ref[:span, kv], 1, 1)
-                d_here = jnp.broadcast_to(dcol_ref[here, h : h + 1], (BLOCK, BLOCK))
-
-                def weight(level):
-                    column = h * level_count + level
-                    return jnp.broadcast_to(l_ref[here, column : column + 1], (BLOCK, BLOCK))
-
+                scores = dot_dims(q_ref[here, cols], k_ref[:span, kv], 1, 1)
+                d_here = column(dcol_ref, here, h)
                 weights = {}
                 mixed = []
                 for j in range(i + 1):
-                    level = (i ^ j).bit_length()
-                    if level not in weights:
-                        weights[level] = weight(level)
+                    step = (i ^ j).bit_length()
+                    if step not in weights:
+                        weights[step] = column(l_ref, here, h * level_count + step)
                     there = slice(j * BLOCK, (j + 1) * BLOCK)
                     gap = d_here - drow_ref[h : h + 1, there]
                     if i == j:
                         gap = jnp.where(causal, gap, -jnp.inf)
-                    mixed.append((weights[level] * jnp.exp(gap) * scores[:, there]).astype(BF16))
+                    mixed.append((weights[step] * jnp.exp(gap) * scores[:, there]).astype(BF16))
                 mixing = mixed[0] if i == 0 else jnp.concatenate(mixed, axis=1)
-                total = dot(mixing, v_ref[:span, kv])
-                wide = query.astype(F32)
+                out = slice((h - first) * head_size, (h - first + 1) * head_size)
+                o_ref[here, out] = dot(mixing, v_ref[:span, kv])
+
+    ins = [q, level, k, v, dcol, drow]
+    return call(kernel, ins, [shape((rows, width // 2), F32)], 0)[0]
+
+
+def attend_earlier(locals_, q, level, dcol, spans, states, head_size, level_count):
+    rows, width = q.shape
+    bits = len(spans)
+    half = width // 2
+    own_levels = level_count - bits
+
+    def kernel(a_ref, b_ref, q_ref, l_ref, dcol_ref, *refs):
+        span_refs, state_refs = refs[:bits], refs[bits : bits + len(states)]
+        outs = refs[-4:]
+        for h in range(width // head_size):
+            cols = slice(h * head_size, (h + 1) * head_size)
+            which, at = divmod(h * head_size, half)
+            out = slice(at, at + head_size)
+            for i in range(rows // BLOCK):
+                here = slice(i * BLOCK, (i + 1) * BLOCK)
+                query = q_ref[here, cols].astype(F32)
+                d_here = column(dcol_ref, here, h)
+                total = (a_ref, b_ref)[which][here, out]
                 for b in range(bits):
-                    factor = weight(own_levels + b) * jnp.exp(d_here + span_refs[b][0:1, cols])
-                    scaled = (wide * factor).astype(BF16)
+                    factor = column(l_ref, here, h * level_count + own_levels + b)
+                    factor = factor * jnp.exp(d_here + span_refs[b][0:1, cols])
+                    scaled = (query * factor).astype(BF16)
                     if b == bits - 1:
-                        s_ref[here, cols] = scaled
+                        outs[2 + which][here, out] = scaled
                     else:
-                        state_ref = state_refs[2 * b + cols.start // half]
-                        at = cols.start % half
-                        total = total + dot_dims(scaled, state_ref[:, at : at + head_size], 1, 1)
-                o_ref[here, cols] = total
-
-    ins = [me, x, wq, wl, total_q, total_l, k, v, dcol, drow, *spans, *states]
-    wide = shape((rows, width), BF16)
-    outs = [shape((rows, width), F32), wide, wide, shape(total_l.shape, F32)]
-    flops = 2 * rows * wq.shape[1] * width + 4 * rows * rows * width
-    return call(kernel, ins, outs, flops, smem=1)[:2]
-
-
-def finish(local, scaled, state, which, cuts, head_size, flops, after=()):
+                        total = total + dot_dims(scaled, state_refs[2 * b + which][:, out], 1, 1)
+                outs[which][here, out] = total
+
+    ins = [*locals_, q, level, dcol, *spans, *states]
+    outs = [shape((rows, half), F32)] * 2 + [shape((rows, half), BF16)] * 2
+    outs = call(kernel, ins, outs, 0)
+    return list(zip(outs[:2], outs[2:]))
+
+
+def finish(local, scaled, state, cuts, head_size, flops, after=()):
     width = state.shape[1]
-    offset = which * width
 
     def kernel(o_ref, q_ref, s_ref, *outs):
         for rows, n_ref in zip(cuts, outs):
             for c in range(0, width, head_size):
-                cols = slice(offset + c, offset + c + head_size)
-                here = slice(c, c + head_size)
-                total = o_ref[rows, cols] + dot_dims(q_ref[rows, cols], s_ref[:, here], 1, 1)
+                cols = slice(c, c + head_size)
+                total = o_ref[rows, cols] + dot_dims(q_ref[rows, cols], s_ref[:, cols], 1, 1)
                 mean = jnp.mean(total * total, axis=-1, keepdims=True)
-                n_ref[:, here] = (total * lax.rsqrt(mean + 1e-05)).astype(BF16)
+                n_ref[:, cols] = (total * lax.rsqrt(mean + 1e-05)).astype(BF16)
 
     outs = [shape((cut.stop - cut.start, width), BF16) for cut in cuts]
     return call(kernel, [local, scaled, state], outs, flops, after)
@@ -428,25 +444,28 @@
     far_near = swap_tp(gate(far, total_q, from_near), 1)
     k, v, *states = project_state(total_kv, from_near, keep, head_size)
 
+    q, level = queries(me, 3, far_near, wq, wl, total_q, total_l)
+    locals_ = [attend(q, level, k, v, dcol, drow, i, head_size, level_count) for i in range(2)]
     earlier = []
     for b in range(seq_bits):
         others = [swap_seq(state, 1 << b) for state in states]
         earlier.append(others)
         if b < seq_bits - 1:
-            states = [combine(*pair, *factors[b], i) for i, pair in enumerate(zip(states, others))]
-
+            afters = (locals_[b : b + 1], ())
+            states = [
+                combine(state, other, *factors[b], i, after)
+                for i, (state, other, after) in enumerate(zip(states, others, afters))
+            ]
     before_last = [state for others in earlier[:-1] for state in others]
-    local, scaled = attend(
-        me, 3, far_near, wq, wl, total_q, total_l, k, v, dcol, drow, spans, before_last, head_size, level_count
-    )
+    halves = attend_earlier(locals_, q, level, dcol, spans, before_last, head_size, level_count)
 
     unit = rows // 8
     ends = (0, 2, 4, 6, 7, 8)
     cuts = [slice(start * unit, stop * unit) for start, stop in zip(ends, ends[1:])]
     middle = rows // 2
-    tops = finish(local, scaled, earlier[-1][0], 0, [slice(0, middle), slice(middle, rows)], head_size, 10**8)
+    tops = finish(*halves[0], earlier[-1][0], [slice(0, middle), slice(middle, rows)], head_size, 10**8)
     first = [(x, swap_tp(x, 1)) for x in tops]
-    second = finish(local, scaled, earlier[-1][1], 1, cuts, head_size, 0, tops)
+    second = finish(*halves[1], earlier[-1][1], cuts, head_size, 0, tops)
     second = [(x, swap_tp(x, 1)) for x in second]
     crossing = []
     for pair, cut in zip(second, cuts):

time: 77.1 us -> 77.1 us (level)
  waiting for transfers between devices: 28.5 us -> 27 us
  Pallas kernels: 20.9 us -> 21.9 us
    ppermute x8, waiting for transfers between devices: 7.14 us -> 5.57 us  [swap_seq(): return lax.ppermute(x, 'seq', [(i, i ^ bit) for i in range(seq_size)])]
    pallas_call x19 -> x22, Pallas kernels: 17.4 us -> 18.4 us  [call(): pl.pallas_call(run, in_specs=[SMEM] * smem + [HBM] * hbm + [VMEM] * (coun...]
  transfers between devices with their start and end apart: 27 -> 27, of which waited for: 12 -> 14; matrix products, arithmetic and copies ran while one was open for 0% -> 0% of each run, Pallas kernels for 26% -> 27%
where the time goes in v12:
time: 77.1 us; the launch traced here: 76.9 us
  starting transfers between devices  27.1 us (35%)
  waiting for transfers between devices  27 us (35%)
  Pallas kernels  21.9 us (28%)
    ppermute x19, waiting for transfers between devices, swap_tp(): return lax.ppermute(x, 'tp', [(i, i ^ bit) for i in range(4)])  21.4 us
    pallas_call x22, Pallas kernels, call(): pl.pallas_call(run, in_specs=[SMEM] * smem + [HBM] * hbm + [VMEM] * (coun...  18.4 us
    ppermute x8, starting transfers between devices, swap_seq(): return lax.ppermute(x, 'seq', [(i, i ^ bit) for i in range(seq_size)])  15.2 us
    ppermute x19, starting transfers between devices, swap_tp(): return lax.ppermute(x, 'tp', [(i, i ^ bit) for i in range(4)])  12 us
    ppermute x8, waiting for transfers between devices, swap_seq(): return lax.ppermute(x, 'seq', [(i, i ^ bit) for i in range(seq_size)])  5.57 us
    pallas_call x5, Pallas kernels, add_rows(): pl.pallas_call(kernel, grid=(rows // unit,), in_specs=specs, out_specs=pl...  3.54 us
  transfers between devices with their start and end apart: 27, of which 14 were waited for; matrix products, arithmetic and copies ran while one was open for 0% of the time, Pallas kernels for 27%

profile of v12, /device:TPU:0, one launch (start us, length us, event | category | flops | bytes accessed | tf_op | source)
XLA Modules:
  0.0 76.9 jit_solution(12099456230708971981)
XLA Ops:
  0.5 2.5 %collective-permute-start = (bf16[512,1024]{1,0:T(8,128)(2,1)}, bf16[512,1024]{1,0:T(8,128)(2,1)S(1)}, u32[]{:S(2)}, u32[]{:S(2)}) collective-permute-start(bf16[512,1024]{1,0:T(8,128)(2,1)} %refs_2_.1), channel_id=1, source_target_pairs={{0,2},{1,3},{2,0},{3,1},{4,6},{5,7},{6,4},{7,5},{8,10},{9,11},{10,... | collective-permute-start | bytes 3145736 | tf_op jit(solution)/shard_map/ppermute | solution.py:417
  3.7 5.4 %shard_map.73 = (f32[512,512]{1,0:T(8,128)S(1)}, f32[512,256]{1,0:T(8,128)S(1)}, f32[512,24]{1,0:T(8,128)S(1)}, bf16[2,1024,512]{2,1,0:T(8,128)(2,1)S(1)}, bf16[...) custom-call(s32[1]{0:T(128)} %bitcast.refs_0_, ...), custom_call_target="tpu_custom_call" | custom-call | tf_op jit(solution)/shard_map/pallas_call | solution.py:41
  10.0 2.6 %collective-permute-start.3 = (f32[8,512]{1,0:T(8,128)S(1)}, f32[8,512]{1,0:T(8,128)S(1)}, u32[]{:S(2)}, u32[]{:S(2)}) collective-permute-start(f32[8,512]{1,0:T(8,128)S(1)} %get-tuple-element.57.refs_1_), channel_id=1, source_target_pairs={{0,4},{4,0},{8,12},{12,8},{16,20},{20,16},{24,28},{28,24},{1,5},{5... | collective-permute-start | bytes 49160 | tf_op jit(solution)/shard_map/ppermute | solution.py:420
  12.6 1.7 %collective-permute-done.3.refs_2_ = f32[8,512]{1,0:T(8,128)S(1)} collective-permute-done((f32[8,512]{1,0:T(8,128)S(1)}, f32[8,512]{1,0:T(8,128)S(1)}, u32[]{:S(2)}, u32[]{:S(2)}) %collective-permute-start.3) | collective-permute-done | bytes 16416 | tf_op jit(solution)/shard_map/ppermute | solution.py:420
  14.3 2.2 %collective-permute-start.4 = (f32[8,512]{1,0:T(8,128)S(1)}, f32[8,512]{1,0:T(8,128)S(1)}, u32[]{:S(2)}, u32[]{:S(2)}) collective-permute-start(f32[8,512]{1,0:T(8,128)S(1)} %get-tuple-element.58.refs_1_), channel_id=1, source_target_pairs={{0,8},{4,12},{8,0},{12,4},{16,24},{20,28},{24,16},{28,20},{1,9},{5... | collective-permute-start | bytes 49160 | tf_op jit(solution)/shard_map/ppermute | solution.py:420
  16.5 1.7 %collective-permute-done.4.refs_2_ = f32[8,512]{1,0:T(8,128)S(1)} collective-permute-done((f32[8,512]{1,0:T(8,128)S(1)}, f32[8,512]{1,0:T(8,128)S(1)}, u32[]{:S(2)}, u32[]{:S(2)}) %collective-permute-start.4) | collective-permute-done | bytes 16416 | tf_op jit(solution)/shard_map/ppermute | solution.py:420
  18.8 8.2 %collective-permute-done.refs_0_.refs_1_ = bf16[512,1024]{1,0:T(8,128)(2,1)S(1)} collective-permute-done((bf16[512,1024]{1,0:T(8,128)(2,1)}, bf16[512,1024]{1,0:T(8,128)(2,1)S(1)}, u32[]{:S(2)}, u32[]{:S(2)}) %collective-permute-start) | collective-permute-done | bytes 1048608 | tf_op jit(solution)/shard_map/ppermute | solution.py:417
  27.6 1.3 %shard_map.77 = (f32[512,512]{1,0:T(8,128)S(1)}, f32[512,256]{1,0:T(8,128)S(1)}, f32[512,24]{1,0:T(8,128)S(1)}) custom-call(s32[1]{0:T(128)} %bitcast.refs_0_, bf16[512,1024]{1,0:T(8,128)(2,1)S(1)} %collective-permute-done.refs_0_.refs_1_, ...), custom_call_target="tpu_custom_call", output_to_operand_aliasing={{0}: (5, {}), {1}: (6, {}), {2}: (7, {})} | custom-call | tf_op jit(solution)/shard_map/pallas_call | solution.py:41
  30.1 1.8 %collective-permute-start.9 = (bf16[128,256]{1,0:T(8,128)(2,1)S(1)}, bf16[128,256]{1,0:T(8,128)(2,1)S(1)}, u32[]{:S(2)}, u32[]{:S(2)}) collective-permute-start(bf16[128,256]{1,0:T(8,128)(2,1)S(1)} %get-tuple-element.76.refs_0_), channel_id=1, source_target_pairs={{0,4},{4,0},{8,12},{12,8},{16,20},{20,16},{24,28},{28,24},{1,5},{5... | collective-permute-start | bytes 196616 | tf_op jit(solution)/shard_map/ppermute | solution.py:420
  33.2 1.3 %shard_map.81.refs_4_.refs_0_ = f32[512,256]{1,0:T(8,128)S(1)} custom-call(bf16[512,512]{1,0:T(8,128)(2,1)S(1)} %get-tuple-element.65.refs_0_.refs_2_, f32[512,24]{1,0:T(8,128)S(1)} %get-tuple-element.66.refs_1_.refs_3_, bf16[512,128]{1,0:T(8,128)(2,1)S(1)} %get-tuple-element.69.refs_2_, bf16[512,128]{1,0:T(8,128)(2,1)S(1)} %get-tuple-element.70.refs_3_, ...), custom_call_target="tpu_custom_call" | custom-call | tf_op jit(solution)/shard_map/pallas_call | solution.py:41
  34.6 2.1 %collective-permute-start.11 = (bf16[128,256]{1,0:T(8,128)(2,1)S(1)}, bf16[128,256]{1,0:T(8,128)(2,1)S(1)}, u32[]{:S(2)}, u32[]{:S(2)}) collective-permute-start(bf16[128,256]{1,0:T(8,128)(2,1)S(1)} %shard_map.83.refs_0_), channel_id=1, source_target_pairs={{0,8},{4,12},{8,0},{12,4},{16,24},{20,28},{24,16},{28,20},{1,9},{5... | collective-permute-start | bytes 196616 | tf_op jit(solution)/shard_map/ppermute | solution.py:420
  37.8 1.3 %shard_map.82.refs_1_.refs_4_ = f32[512,256]{1,0:T(8,128)S(1)} custom-call(bf16[512,512]{1,0:T(8,128)(2,1)S(1)} %get-tuple-element.65.refs_0_.refs_2_, f32[512,24]{1,0:T(8,128)S(1)} %get-tuple-element.66.refs_1_.refs_3_, bf16[512,128]{1,0:T(8,128)(2,1)S(1)} %get-tuple-element.69.refs_2_, bf16[512,128]{1,0:T(8,128)(2,1)S(1)} %get-tuple-element.70.refs_3_, ...), custom_call_target="tpu_custom_call" | custom-call | tf_op jit(solution)/shard_map/pallas_call | solution.py:41
  39.3 3.5 %collective-permute-start.13 = (bf16[128,256]{1,0:T(8,128)(2,1)S(1)}, bf16[128,256]{1,0:T(8,128)(2,1)S(1)}, u32[]{:S(2)}, u32[]{:S(2)}) collective-permute-start(bf16[128,256]{1,0:T(8,128)(2,1)S(1)} %shard_map.86), channel_id=1, source_target_pairs={{0,16},{4,20},{8,24},{12,28},{16,0},{20,4},{24,8},{28,12},{1,17},{... | collective-permute-start | bytes 196616 | tf_op jit(solution)/shard_map/ppermute | solution.py:420
  42.8 1.6 %collective-permute-start.16 = (bf16[128,256]{1,0:T(8,128)(2,1)S(1)}, bf16[128,256]{1,0:T(8,128)(2,1)S(1)}, u32[]{:S(2)}, u32[]{:S(2)}) collective-permute-start(bf16[128,256]{1,0:T(8,128)(2,1)S(1)} %shard_map.88), channel_id=1, source_target_pairs={{0,16},{4,20},{8,24},{12,28},{16,0},{20,4},{24,8},{28,12},{1,17},{... | collective-permute-start | bytes 196616 | tf_op jit(solution)/shard_map/ppermute | solution.py:420
  44.4 1.5 %shard_map.85 = (f32[512,256]{1,0:T(8,128)S(1)}, f32[512,256]{1,0:T(8,128)S(1)}, bf16[512,256]{1,0:T(8,128)(2,1)S(1)}, bf16[512,256]{1,0:T(8,128)(2,1)S(1)}) custom-call(f32[512,256]{1,0:T(8,128)S(1)} %shard_map.81.refs_4_.refs_0_, f32[512,256]{1,0:T(8,128)S(1)} %shard_map.82.refs_1_.refs_4_, bf16[512,512]{1,0:T(8,128)(2,1)S(1)} %get-tuple-element.65.refs_0_.refs_2_, ...), custom_call_target="tpu_custom_call" | custom-call | tf_op jit(solution)/shard_map/pallas_call | solution.py:41
  47.7 1.1 %collective-permute-done.16.refs_2_ = bf16[128,256]{1,0:T(8,128)(2,1)S(1)} collective-permute-done((bf16[128,256]{1,0:T(8,128)(2,1)S(1)}, bf16[128,256]{1,0:T(8,128)(2,1)S(1)}, u32[]{:S(2)}, u32[]{:S(2)}) %collective-permute-start.16) | collective-permute-done | bytes 65568 | tf_op jit(solution)/shard_map/ppermute | solution.py:420
  51.0 1.6 %collective-permute-start.25 = (bf16[128,1024]{1,0:T(8,128)(2,1)S(1)}, bf16[128,1024]{1,0:T(8,128)(2,1)S(1)}, u32[]{:S(2)}, u32[]{:S(2)}) collective-permute-start(bf16[128,1024]{1,0:T(8,128)(2,1)S(1)} %shard_map.94), channel_id=1, source_target_pairs={{0,2},{1,3},{2,0},{3,1},{4,6},{5,7},{6,4},{7,5},{8,10},{9,11},{10,... | collective-permute-start | bytes 786440 | tf_op jit(solution)/shard_map/ppermute | solution.py:417
  54.1 1.6 %collective-permute-start.24 = (bf16[128,1024]{1,0:T(8,128)(2,1)S(1)}, bf16[128,1024]{1,0:T(8,128)(2,1)S(1)}, u32[]{:S(2)}, u32[]{:S(2)}) collective-permute-start(bf16[128,1024]{1,0:T(8,128)(2,1)S(1)} %shard_map.93), channel_id=1, source_target_pairs={{0,2},{1,3},{2,0},{3,1},{4,6},{5,7},{6,4},{7,5},{8,10},{9,11},{10,... | collective-permute-start | bytes 786440 | tf_op jit(solution)/shard_map/ppermute | solution.py:417
  58.4 1.6 %collective-permute-start.22 = (bf16[64,1024]{1,0:T(8,128)(2,1)S(1)}, bf16[64,1024]{1,0:T(8,128)(2,1)S(1)}, u32[]{:S(2)}, u32[]{:S(2)}) collective-permute-start(bf16[64,1024]{1,0:T(8,128)(2,1)S(1)} %shard_map.90.refs_16_), channel_id=1, source_target_pairs={{0,2},{1,3},{2,0},{3,1},{4,6},{5,7},{6,4},{7,5},{8,10},{9,11},{10,... | collective-permute-start | bytes 393224 | tf_op jit(solution)/shard_map/ppermute | solution.py:417
  60.0 1.7 %shard_map.91.h_ref = f32[512,1024]{1,0:T(8,128)S(1)} custom-call(bf16[256,256]{1,0:T(8,128)(2,1)S(1)} %get-tuple-element.84.refs_3_.refs_0_, bf16[256,256]{1,0:T(8,128)(2,1)S(1)} %collective-permute-done.14.refs_1_, bf16[256,256]{1,0:T(8,128)(2,1)S(1)} %get-tuple-element.85.refs_4_.refs_0_.refs_2_, ...), custom_call_target="tpu_custom_call" | custom-call | tf_op jit(solution)/shard_map/pallas_call | solution.py:41
  61.7 4.1 %collective-permute-done.26.a_ref = bf16[128,1024]{1,0:T(8,128)(2,1)S(1)} collective-permute-done((bf16[128,1024]{1,0:T(8,128)(2,1)S(1)}, bf16[128,1024]{1,0:T(8,128)(2,1)S(1)}, u32[]{:S(2)}, u32[]{:S(2)}) %collective-permute-start.26) | collective-permute-done | bytes 262176 | tf_op jit(solution)/shard_map/ppermute | solution.py:417
  67.2 4.2 %collective-permute-done.24.a_ref = bf16[128,1024]{1,0:T(8,128)(2,1)S(1)} collective-permute-done((bf16[128,1024]{1,0:T(8,128)(2,1)S(1)}, bf16[128,1024]{1,0:T(8,128)(2,1)S(1)}, u32[]{:S(2)}, u32[]{:S(2)}) %collective-permute-start.24) | collective-permute-done | bytes 262176 | tf_op jit(solution)/shard_map/ppermute | solution.py:417
  72.1 2.1 %collective-permute-done.23.a_ref = bf16[64,1024]{1,0:T(8,128)(2,1)S(1)} collective-permute-done((bf16[64,1024]{1,0:T(8,128)(2,1)S(1)}, bf16[64,1024]{1,0:T(8,128)(2,1)S(1)}, u32[]{:S(2)}, u32[]{:S(2)}) %collective-permute-start.23) | collective-permute-done | bytes 131104 | tf_op jit(solution)/shard_map/ppermute | solution.py:417
  74.9 1.3 %collective-permute-done.22.a_ref = bf16[64,1024]{1,0:T(8,128)(2,1)S(1)} collective-permute-done((bf16[64,1024]{1,0:T(8,128)(2,1)S(1)}, bf16[64,1024]{1,0:T(8,128)(2,1)S(1)}, u32[]{:S(2)}, u32[]{:S(2)}) %collective-permute-start.22) | collective-permute-done | bytes 131104 | tf_op jit(solution)/shard_map/ppermute | solution.py:417
  (60 shorter events, 18.9 us)
Async XLA Ops:
  0.0 3.0 %collective-permute-start.1 = (bf16[512,1024]{1,0:T(8,128)(2,1)}, bf16[512,1024]{1,0:T(8,128)(2,1)S(1)}, u32[]{:S(2)}, u32[]{:S(2)}) collective-permute-start(bf16[512,1024]{1,0:T(8,128)(2,1)} %refs_2_.1), channel_id=1, source_target_pairs={{0,1},{1,0},{2,3},{3,2},{4,5},{5,4},{6,7},{7,6},{8,9},{9,8},{10,11... | collective-permute-start | bytes 3145736 | tf_op jit(solution)/shard_map/ppermute | solution.py:417
  0.5 26.6 %collective-permute-start = (bf16[512,1024]{1,0:T(8,128)(2,1)}, bf16[512,1024]{1,0:T(8,128)(2,1)S(1)}, u32[]{:S(2)}, u32[]{:S(2)}) collective-permute-start(bf16[512,1024]{1,0:T(8,128)(2,1)} %refs_2_.1), channel_id=1, source_target_pairs={{0,2},{1,3},{2,0},{3,1},{4,6},{5,7},{6,4},{7,5},{8,10},{9,11},{10,... | collective-permute-start | bytes 3145736 | tf_op jit(solution)/shard_map/ppermute | solution.py:417
  9.0 18.0 %collective-permute-start.5 = (bf16[512,1024]{1,0:T(8,128)(2,1)S(1)}, bf16[512,1024]{1,0:T(8,128)(2,1)S(1)}, u32[]{:S(2)}, u32[]{:S(2)}) collective-permute-start(bf16[512,1024]{1,0:T(8,128)(2,1)S(1)} %get-tuple-element.61), channel_id=1, source_target_pairs={{0,1},{1,0},{2,3},{3,2},{4,5},{5,4},{6,7},{7,6},{8,9},{9,8},{10,11... | collective-permute-start | bytes 3145736 | tf_op jit(solution)/shard_map/ppermute | solution.py:417
  9.5 17.6 %collective-permute-start.6 = (bf16[512,1024]{1,0:T(8,128)(2,1)S(1)}, bf16[512,1024]{1,0:T(8,128)(2,1)S(1)}, u32[]{:S(2)}, u32[]{:S(2)}) collective-permute-start(bf16[512,1024]{1,0:T(8,128)(2,1)S(1)} %get-tuple-element.62), channel_id=1, source_target_pairs={{0,1},{1,0},{2,3},{3,2},{4,5},{5,4},{6,7},{7,6},{8,9},{9,8},{10,11... | collective-permute-start | bytes 3145736 | tf_op jit(solution)/shard_map/ppermute | solution.py:417
  9.6 17.4 %collective-permute-start.2 = (bf16[1024,256]{1,0:T(8,128)(2,1)S(1)}, bf16[1024,256]{1,0:T(8,128)(2,1)S(1)}, u32[]{:S(2)}, u32[]{:S(2)}) collective-permute-start(bf16[1024,256]{1,0:T(8,128)(2,1)S(1)} %get-tuple-element.56), channel_id=1, source_target_pairs={{0,1},{1,0},{2,3},{3,2},{4,5},{5,4},{6,7},{7,6},{8,9},{9,8},{10,11... | collective-permute-start | bytes 1572872 | tf_op jit(solution)/shard_map/ppermute | solution.py:417
  10.0 4.3 %collective-permute-start.3 = (f32[8,512]{1,0:T(8,128)S(1)}, f32[8,512]{1,0:T(8,128)S(1)}, u32[]{:S(2)}, u32[]{:S(2)}) collective-permute-start(f32[8,512]{1,0:T(8,128)S(1)} %get-tuple-element.57.refs_1_), channel_id=1, source_target_pairs={{0,4},{4,0},{8,12},{12,8},{16,20},{20,16},{24,28},{28,24},{1,5},{5... | collective-permute-start | bytes 49160 | tf_op jit(solution)/shard_map/ppermute | solution.py:420
  14.3 3.9 %collective-permute-start.4 = (f32[8,512]{1,0:T(8,128)S(1)}, f32[8,512]{1,0:T(8,128)S(1)}, u32[]{:S(2)}, u32[]{:S(2)}) collective-permute-start(f32[8,512]{1,0:T(8,128)S(1)} %get-tuple-element.58.refs_1_), channel_id=1, source_target_pairs={{0,8},{4,12},{8,0},{12,4},{16,24},{20,28},{24,16},{28,20},{1,9},{5... | collective-permute-start | bytes 49160 | tf_op jit(solution)/shard_map/ppermute | solution.py:420
  29.1 3.1 %collective-permute-start.8 = (bf16[512,1024]{1,0:T(8,128)(2,1)S(1)}, bf16[512,1024]{1,0:T(8,128)(2,1)S(1)}, u32[]{:S(2)}, u32[]{:S(2)}) collective-permute-start(bf16[512,1024]{1,0:T(8,128)(2,1)S(1)} %shard_map.78), channel_id=1, source_target_pairs={{0,1},{1,0},{2,3},{3,2},{4,5},{5,4},{6,7},{7,6},{8,9},{9,8},{10,11... | collective-permute-start | bytes 3145736 | tf_op jit(solution)/shard_map/ppermute | solution.py:417
  30.1 4.5 %collective-permute-start.9 = (bf16[128,256]{1,0:T(8,128)(2,1)S(1)}, bf16[128,256]{1,0:T(8,128)(2,1)S(1)}, u32[]{:S(2)}, u32[]{:S(2)}) collective-permute-start(bf16[128,256]{1,0:T(8,128)(2,1)S(1)} %get-tuple-element.76.refs_0_), channel_id=1, source_target_pairs={{0,4},{4,0},{8,12},{12,8},{16,20},{20,16},{24,28},{28,24},{1,5},{5... | collective-permute-start | bytes 196616 | tf_op jit(solution)/shard_map/ppermute | solution.py:420
  31.8 4.9 %collective-permute-start.10 = (bf16[128,256]{1,0:T(8,128)(2,1)S(1)}, bf16[128,256]{1,0:T(8,128)(2,1)S(1)}, u32[]{:S(2)}, u32[]{:S(2)}) collective-permute-start(bf16[128,256]{1,0:T(8,128)(2,1)S(1)} %get-tuple-element.77.refs_0_), channel_id=1, source_target_pairs={{0,4},{4,0},{8,12},{12,8},{16,20},{20,16},{24,28},{28,24},{1,5},{5... | collective-permute-start | bytes 196616 | tf_op jit(solution)/shard_map/ppermute | solution.py:420
  34.6 4.6 %collective-permute-start.11 = (bf16[128,256]{1,0:T(8,128)(2,1)S(1)}, bf16[128,256]{1,0:T(8,128)(2,1)S(1)}, u32[]{:S(2)}, u32[]{:S(2)}) collective-permute-start(bf16[128,256]{1,0:T(8,128)(2,1)S(1)} %shard_map.83.refs_0_), channel_id=1, source_target_pairs={{0,8},{4,12},{8,0},{12,4},{16,24},{20,28},{24,16},{28,20},{1,9},{5... | collective-permute-start | bytes 196616 | tf_op jit(solution)/shard_map/ppermute | solution.py:420
  36.8 6.0 %collective-permute-start.12 = (bf16[128,256]{1,0:T(8,128)(2,1)S(1)}, bf16[128,256]{1,0:T(8,128)(2,1)S(1)}, u32[]{:S(2)}, u32[]{:S(2)}) collective-permute-start(bf16[128,256]{1,0:T(8,128)(2,1)S(1)} %shard_map.84.refs_0_), channel_id=1, source_target_pairs={{0,8},{4,12},{8,0},{12,4},{16,24},{20,28},{24,16},{28,20},{1,9},{5... | collective-permute-start | bytes 196616 | tf_op jit(solution)/shard_map/ppermute | solution.py:420
  39.3 7.4 %collective-permute-start.13 = (bf16[128,256]{1,0:T(8,128)(2,1)S(1)}, bf16[128,256]{1,0:T(8,128)(2,1)S(1)}, u32[]{:S(2)}, u32[]{:S(2)}) collective-permute-start(bf16[128,256]{1,0:T(8,128)(2,1)S(1)} %shard_map.86), channel_id=1, source_target_pairs={{0,16},{4,20},{8,24},{12,28},{16,0},{20,4},{24,8},{28,12},{1,17},{... | collective-permute-start | bytes 196616 | tf_op jit(solution)/shard_map/ppermute | solution.py:420
  42.8 5.9 %collective-permute-start.16 = (bf16[128,256]{1,0:T(8,128)(2,1)S(1)}, bf16[128,256]{1,0:T(8,128)(2,1)S(1)}, u32[]{:S(2)}, u32[]{:S(2)}) collective-permute-start(bf16[128,256]{1,0:T(8,128)(2,1)S(1)} %shard_map.88), channel_id=1, source_target_pairs={{0,16},{4,20},{8,24},{12,28},{16,0},{20,4},{24,8},{28,12},{1,17},{... | collective-permute-start | bytes 196616 | tf_op jit(solution)/shard_map/ppermute | solution.py:420
  47.1 3.4 %collective-permute-start.14 = (bf16[256,256]{1,0:T(8,128)(2,1)S(1)}, bf16[256,256]{1,0:T(8,128)(2,1)S(1)}, u32[]{:S(2)}, u32[]{:S(2)}) collective-permute-start(bf16[256,256]{1,0:T(8,128)(2,1)S(1)} %get-tuple-element.84.refs_3_.refs_0_), channel_id=1, source_target_pairs={{0,1},{1,0},{2,3},{3,2},{4,5},{5,4},{6,7},{7,6},{8,9},{9,8},{10,11... | collective-permute-start | bytes 393224 | tf_op jit(solution)/shard_map/ppermute | solution.py:417
  47.2 6.4 %collective-permute-start.15 = (bf16[256,256]{1,0:T(8,128)(2,1)S(1)}, bf16[256,256]{1,0:T(8,128)(2,1)S(1)}, u32[]{:S(2)}, u32[]{:S(2)}) collective-permute-start(bf16[256,256]{1,0:T(8,128)(2,1)S(1)} %get-tuple-element.85.refs_4_.refs_0_.refs_2_), channel_id=1, source_target_pairs={{0,1},{1,0},{2,3},{3,2},{4,5},{5,4},{6,7},{7,6},{8,9},{9,8},{10,11... | collective-permute-start | bytes 393224 | tf_op jit(solution)/shard_map/ppermute | solution.py:417
  49.2 3.3 %collective-permute-start.17 = (bf16[128,256]{1,0:T(8,128)(2,1)S(1)}, bf16[128,256]{1,0:T(8,128)(2,1)S(1)}, u32[]{:S(2)}, u32[]{:S(2)}) collective-permute-start(bf16[128,256]{1,0:T(8,128)(2,1)S(1)} %get-tuple-element.88.refs_4_.refs_2_), channel_id=1, source_target_pairs={{0,1},{1,0},{2,3},{3,2},{4,5},{5,4},{6,7},{7,6},{8,9},{9,8},{10,11... | collective-permute-start | bytes 196616 | tf_op jit(solution)/shard_map/ppermute | solution.py:417
  49.7 3.8 %collective-permute-start.19 = (bf16[128,256]{1,0:T(8,128)(2,1)S(1)}, bf16[128,256]{1,0:T(8,128)(2,1)S(1)}, u32[]{:S(2)}, u32[]{:S(2)}) collective-permute-start(bf16[128,256]{1,0:T(8,128)(2,1)S(1)} %get-tuple-element.90.refs_8_.refs_2_), channel_id=1, source_target_pairs={{0,1},{1,0},{2,3},{3,2},{4,5},{5,4},{6,7},{7,6},{8,9},{9,8},{10,11... | collective-permute-start | bytes 196616 | tf_op jit(solution)/shard_map/ppermute | solution.py:417
  51.0 15.6 %collective-permute-start.25 = (bf16[128,1024]{1,0:T(8,128)(2,1)S(1)}, bf16[128,1024]{1,0:T(8,128)(2,1)S(1)}, u32[]{:S(2)}, u32[]{:S(2)}) collective-permute-start(bf16[128,1024]{1,0:T(8,128)(2,1)S(1)} %shard_map.94), channel_id=1, source_target_pairs={{0,2},{1,3},{2,0},{3,1},{4,6},{5,7},{6,4},{7,5},{8,10},{9,11},{10,... | collective-permute-start | bytes 786440 | tf_op jit(solution)/shard_map/ppermute | solution.py:417
  53.0 12.8 %collective-permute-start.26 = (bf16[128,1024]{1,0:T(8,128)(2,1)S(1)}, bf16[128,1024]{1,0:T(8,128)(2,1)S(1)}, u32[]{:S(2)}, u32[]{:S(2)}) collective-permute-start(bf16[128,1024]{1,0:T(8,128)(2,1)S(1)} %shard_map.95), channel_id=1, source_target_pairs={{0,2},{1,3},{2,0},{3,1},{4,6},{5,7},{6,4},{7,5},{8,10},{9,11},{10,... | collective-permute-start | bytes 786440 | tf_op jit(solution)/shard_map/ppermute | solution.py:417
  54.1 17.3 %collective-permute-start.24 = (bf16[128,1024]{1,0:T(8,128)(2,1)S(1)}, bf16[128,1024]{1,0:T(8,128)(2,1)S(1)}, u32[]{:S(2)}, u32[]{:S(2)}) collective-permute-start(bf16[128,1024]{1,0:T(8,128)(2,1)S(1)} %shard_map.93), channel_id=1, source_target_pairs={{0,2},{1,3},{2,0},{3,1},{4,6},{5,7},{6,4},{7,5},{8,10},{9,11},{10,... | collective-permute-start | bytes 786440 | tf_op jit(solution)/shard_map/ppermute | solution.py:417
  55.6 2.3 %collective-permute-start.21 = (bf16[64,256]{1,0:T(8,128)(2,1)S(1)}, bf16[64,256]{1,0:T(8,128)(2,1)S(1)}, u32[]{:S(2)}, u32[]{:S(2)}) collective-permute-start(bf16[64,256]{1,0:T(8,128)(2,1)S(1)} %get-tuple-element.92.refs_2_.refs_12_), channel_id=1, source_target_pairs={{0,1},{1,0},{2,3},{3,2},{4,5},{5,4},{6,7},{7,6},{8,9},{9,8},{10,11... | collective-permute-start | bytes 98312 | tf_op jit(solution)/shard_map/ppermute | solution.py:417
  57.3 16.9 %collective-permute-start.23 = (bf16[64,1024]{1,0:T(8,128)(2,1)S(1)}, bf16[64,1024]{1,0:T(8,128)(2,1)S(1)}, u32[]{:S(2)}, u32[]{:S(2)}) collective-permute-start(bf16[64,1024]{1,0:T(8,128)(2,1)S(1)} %shard_map.92), channel_id=1, source_target_pairs={{0,2},{1,3},{2,0},{3,1},{4,6},{5,7},{6,4},{7,5},{8,10},{9,11},{10,... | collective-permute-start | bytes 393224 | tf_op jit(solution)/shard_map/ppermute | solution.py:417
  58.4 17.8 %collective-permute-start.22 = (bf16[64,1024]{1,0:T(8,128)(2,1)S(1)}, bf16[64,1024]{1,0:T(8,128)(2,1)S(1)}, u32[]{:S(2)}, u32[]{:S(2)}) collective-permute-start(bf16[64,1024]{1,0:T(8,128)(2,1)S(1)} %shard_map.90.refs_16_), channel_id=1, source_target_pairs={{0,2},{1,3},{2,0},{3,1},{4,6},{5,7},{6,4},{7,5},{8,10},{9,11},{10,... | collective-permute-start | bytes 393224 | tf_op jit(solution)/shard_map/ppermute | solution.py:417
  (4 other events, 4.8 us)

commit v13 on v12

--- a/solution.py
+++ b/solution.py
@@ -417,7 +417,8 @@
         return lax.ppermute(x, "tp", [(i, i ^ bit) for i in range(4)])
 
     def swap_seq(x, bit):
-        return lax.ppermute(x, "seq", [(i, i ^ bit) for i in range(seq_size)])
+        one_way = 2 * bit == seq_size
+        return lax.ppermute(x, "seq", [(i, i ^ bit) for i in range(seq_size) if not (one_way and i & bit)])
 
     far = swap_tp(tokens, 2)
     near = swap_tp(tokens, 1)

time: 77.1 us -> 77 us (level)
  waiting for transfers between devices: 27 us -> 25.1 us
  starting transfers between devices: 27.1 us -> 28.8 us
    ppermute x8, waiting for transfers between devices: 5.57 us -> 3.69 us  [swap_seq(): lax.ppermute(x, 'seq', [(i, i ^ bit) for i in range(seq_size) if not (one...]
    ppermute x8, starting transfers between devices: 15.2 us -> 16.8 us  [swap_seq(): lax.ppermute(x, 'seq', [(i, i ^ bit) for i in range(seq_size) if not (one...]
  transfers between devices with their start and end apart: 27 -> 27, of which waited for: 14 -> 12; matrix products, arithmetic and copies ran while one was open for 0% -> 0% of each run, Pallas kernels for 27% -> 27%
where the time goes in v13:
time: 77 us; the launch traced here: 76.8 us
  starting transfers between devices  28.8 us (37%)
  waiting for transfers between devices  25.1 us (33%)
  Pallas kernels  21.9 us (28%)
    ppermute x19, waiting for transfers between devices, swap_tp(): return lax.ppermute(x, 'tp', [(i, i ^ bit) for i in range(4)])  21.4 us
    pallas_call x22, Pallas kernels, call(): pl.pallas_call(run, in_specs=[SMEM] * smem + [HBM] * hbm + [VMEM] * (coun...  18.4 us
    ppermute x8, starting transfers between devices, swap_seq(): lax.ppermute(x, 'seq', [(i, i ^ bit) for i in range(seq_size) if not (one...  16.8 us
    ppermute x19, starting transfers between devices, swap_tp(): return lax.ppermute(x, 'tp', [(i, i ^ bit) for i in range(4)])  12 us
    ppermute x8, waiting for transfers between devices, swap_seq(): lax.ppermute(x, 'seq', [(i, i ^ bit) for i in range(seq_size) if not (one...  3.69 us
    pallas_call x5, Pallas kernels, add_rows(): pl.pallas_call(kernel, grid=(rows // unit,), in_specs=specs, out_specs=pl...  3.54 us
  transfers between devices with their start and end apart: 27, of which 12 were waited for; matrix products, arithmetic and copies ran while one was open for 0% of the time, Pallas kernels for 27%

profile of v13, /device:TPU:0, one launch (start us, length us, event | category | flops | bytes accessed | tf_op | source)
XLA Modules:
  0.0 76.8 jit_solution(8888750968627652343)
XLA Ops:
  0.5 2.5 %collective-permute-start = (bf16[512,1024]{1,0:T(8,128)(2,1)}, bf16[512,1024]{1,0:T(8,128)(2,1)S(1)}, u32[]{:S(2)}, u32[]{:S(2)}) collective-permute-start(bf16[512,1024]{1,0:T(8,128)(2,1)} %refs_2_.1), channel_id=1, source_target_pairs={{0,2},{1,3},{2,0},{3,1},{4,6},{5,7},{6,4},{7,5},{8,10},{9,11},{10,... | collective-permute-start | bytes 3145736 | tf_op jit(solution)/shard_map/ppermute | solution.py:417
  3.7 5.4 %shard_map.73 = (f32[512,512]{1,0:T(8,128)S(1)}, f32[512,256]{1,0:T(8,128)S(1)}, f32[512,24]{1,0:T(8,128)S(1)}, bf16[2,1024,512]{2,1,0:T(8,128)(2,1)S(1)}, bf16[...) custom-call(s32[1]{0:T(128)} %bitcast.refs_0_, ...), custom_call_target="tpu_custom_call" | custom-call | tf_op jit(solution)/shard_map/pallas_call | solution.py:41
  10.0 2.6 %collective-permute-start.3 = (f32[8,512]{1,0:T(8,128)S(1)}, f32[8,512]{1,0:T(8,128)S(1)}, u32[]{:S(2)}, u32[]{:S(2)}) collective-permute-start(f32[8,512]{1,0:T(8,128)S(1)} %get-tuple-element.57.refs_1_), channel_id=1, source_target_pairs={{0,4},{4,0},{8,12},{12,8},{16,20},{20,16},{24,28},{28,24},{1,5},{5... | collective-permute-start | bytes 49160 | tf_op jit(solution)/shard_map/ppermute | solution.py:421
  12.6 1.7 %collective-permute-done.3.refs_2_ = f32[8,512]{1,0:T(8,128)S(1)} collective-permute-done((f32[8,512]{1,0:T(8,128)S(1)}, f32[8,512]{1,0:T(8,128)S(1)}, u32[]{:S(2)}, u32[]{:S(2)}) %collective-permute-start.3) | collective-permute-done | bytes 16416 | tf_op jit(solution)/shard_map/ppermute | solution.py:421
  14.3 2.2 %collective-permute-start.4 = (f32[8,512]{1,0:T(8,128)S(1)}, f32[8,512]{1,0:T(8,128)S(1)}, u32[]{:S(2)}, u32[]{:S(2)}) collective-permute-start(f32[8,512]{1,0:T(8,128)S(1)} %get-tuple-element.58.refs_1_), channel_id=1, source_target_pairs={{0,8},{4,12},{8,0},{12,4},{16,24},{20,28},{24,16},{28,20},{1,9},{5... | collective-permute-start | bytes 49160 | tf_op jit(solution)/shard_map/ppermute | solution.py:421
  16.5 1.7 %collective-permute-done.4.refs_2_ = f32[8,512]{1,0:T(8,128)S(1)} collective-permute-done((f32[8,512]{1,0:T(8,128)S(1)}, f32[8,512]{1,0:T(8,128)S(1)}, u32[]{:S(2)}, u32[]{:S(2)}) %collective-permute-start.4) | collective-permute-done | bytes 16416 | tf_op jit(solution)/shard_map/ppermute | solution.py:421
  18.8 8.2 %collective-permute-done.refs_0_.refs_1_ = bf16[512,1024]{1,0:T(8,128)(2,1)S(1)} collective-permute-done((bf16[512,1024]{1,0:T(8,128)(2,1)}, bf16[512,1024]{1,0:T(8,128)(2,1)S(1)}, u32[]{:S(2)}, u32[]{:S(2)}) %collective-permute-start) | collective-permute-done | bytes 1048608 | tf_op jit(solution)/shard_map/ppermute | solution.py:417
  27.6 1.3 %shard_map.77 = (f32[512,512]{1,0:T(8,128)S(1)}, f32[512,256]{1,0:T(8,128)S(1)}, f32[512,24]{1,0:T(8,128)S(1)}) custom-call(s32[1]{0:T(128)} %bitcast.refs_0_, bf16[512,1024]{1,0:T(8,128)(2,1)S(1)} %collective-permute-done.refs_0_.refs_1_, ...), custom_call_target="tpu_custom_call", output_to_operand_aliasing={{0}: (5, {}), {1}: (6, {}), {2}: (7, {})} | custom-call | tf_op jit(solution)/shard_map/pallas_call | solution.py:41
  30.1 1.8 %collective-permute-start.9 = (bf16[128,256]{1,0:T(8,128)(2,1)S(1)}, bf16[128,256]{1,0:T(8,128)(2,1)S(1)}, u32[]{:S(2)}, u32[]{:S(2)}) collective-permute-start(bf16[128,256]{1,0:T(8,128)(2,1)S(1)} %get-tuple-element.76.refs_0_), channel_id=1, source_target_pairs={{0,4},{4,0},{8,12},{12,8},{16,20},{20,16},{24,28},{28,24},{1,5},{5... | collective-permute-start | bytes 196616 | tf_op jit(solution)/shard_map/ppermute | solution.py:421
  33.2 1.3 %shard_map.81.refs_4_.refs_0_ = f32[512,256]{1,0:T(8,128)S(1)} custom-call(bf16[512,512]{1,0:T(8,128)(2,1)S(1)} %get-tuple-element.65.refs_0_.refs_2_, f32[512,24]{1,0:T(8,128)S(1)} %get-tuple-element.66.refs_1_.refs_3_, bf16[512,128]{1,0:T(8,128)(2,1)S(1)} %get-tuple-element.69.refs_2_, bf16[512,128]{1,0:T(8,128)(2,1)S(1)} %get-tuple-element.70.refs_3_, ...), custom_call_target="tpu_custom_call" | custom-call | tf_op jit(solution)/shard_map/pallas_call | solution.py:41
  34.6 2.1 %collective-permute-start.11 = (bf16[128,256]{1,0:T(8,128)(2,1)S(1)}, bf16[128,256]{1,0:T(8,128)(2,1)S(1)}, u32[]{:S(2)}, u32[]{:S(2)}) collective-permute-start(bf16[128,256]{1,0:T(8,128)(2,1)S(1)} %shard_map.83.refs_0_), channel_id=1, source_target_pairs={{0,8},{4,12},{8,0},{12,4},{16,24},{20,28},{24,16},{28,20},{1,9},{5... | collective-permute-start | bytes 196616 | tf_op jit(solution)/shard_map/ppermute | solution.py:421
  36.8 1.0 %collective-permute-start.12 = (bf16[128,256]{1,0:T(8,128)(2,1)S(1)}, bf16[128,256]{1,0:T(8,128)(2,1)S(1)}, u32[]{:S(2)}, u32[]{:S(2)}) collective-permute-start(bf16[128,256]{1,0:T(8,128)(2,1)S(1)} %shard_map.84.refs_0_), channel_id=1, source_target_pairs={{0,8},{4,12},{8,0},{12,4},{16,24},{20,28},{24,16},{28,20},{1,9},{5... | collective-permute-start | bytes 196616 | tf_op jit(solution)/shard_map/ppermute | solution.py:421
  37.8 1.3 %shard_map.82.refs_1_.refs_4_ = f32[512,256]{1,0:T(8,128)S(1)} custom-call(bf16[512,512]{1,0:T(8,128)(2,1)S(1)} %get-tuple-element.65.refs_0_.refs_2_, f32[512,24]{1,0:T(8,128)S(1)} %get-tuple-element.66.refs_1_.refs_3_, bf16[512,128]{1,0:T(8,128)(2,1)S(1)} %get-tuple-element.69.refs_2_, bf16[512,128]{1,0:T(8,128)(2,1)S(1)} %get-tuple-element.70.refs_3_, ...), custom_call_target="tpu_custom_call" | custom-call | tf_op jit(solution)/shard_map/pallas_call | solution.py:41
  39.3 5.3 %collective-permute-start.13 = (bf16[128,256]{1,0:T(8,128)(2,1)S(1)}, bf16[128,256]{1,0:T(8,128)(2,1)S(1)}, u32[]{:S(2)}, u32[]{:S(2)}) collective-permute-start(bf16[128,256]{1,0:T(8,128)(2,1)S(1)} %shard_map.86), channel_id=1, source_target_pairs={{0,16},{4,20},{8,24},{12,28},{1,17},{5,21},{9,25},{13,29},{2,18},{... | collective-permute-start | bytes 196616 | tf_op jit(solution)/shard_map/ppermute | solution.py:421
  44.6 1.5 %collective-permute-start.16 = (bf16[128,256]{1,0:T(8,128)(2,1)S(1)}, bf16[128,256]{1,0:T(8,128)(2,1)S(1)}, u32[]{:S(2)}, u32[]{:S(2)}) collective-permute-start(bf16[128,256]{1,0:T(8,128)(2,1)S(1)} %shard_map.88), channel_id=1, source_target_pairs={{0,16},{4,20},{8,24},{12,28},{1,17},{5,21},{9,25},{13,29},{2,18},{... | collective-permute-start | bytes 196616 | tf_op jit(solution)/shard_map/ppermute | solution.py:421
  46.1 1.5 %shard_map.85 = (f32[512,256]{1,0:T(8,128)S(1)}, f32[512,256]{1,0:T(8,128)S(1)}, bf16[512,256]{1,0:T(8,128)(2,1)S(1)}, bf16[512,256]{1,0:T(8,128)(2,1)S(1)}) custom-call(f32[512,256]{1,0:T(8,128)S(1)} %shard_map.81.refs_4_.refs_0_, f32[512,256]{1,0:T(8,128)S(1)} %shard_map.82.refs_1_.refs_4_, bf16[512,512]{1,0:T(8,128)(2,1)S(1)} %get-tuple-element.65.refs_0_.refs_2_, ...), custom_call_target="tpu_custom_call" | custom-call | tf_op jit(solution)/shard_map/pallas_call | solution.py:41
  50.8 1.6 %collective-permute-start.25 = (bf16[128,1024]{1,0:T(8,128)(2,1)S(1)}, bf16[128,1024]{1,0:T(8,128)(2,1)S(1)}, u32[]{:S(2)}, u32[]{:S(2)}) collective-permute-start(bf16[128,1024]{1,0:T(8,128)(2,1)S(1)} %shard_map.94), channel_id=1, source_target_pairs={{0,2},{1,3},{2,0},{3,1},{4,6},{5,7},{6,4},{7,5},{8,10},{9,11},{10,... | collective-permute-start | bytes 786440 | tf_op jit(solution)/shard_map/ppermute | solution.py:417
  53.9 1.6 %collective-permute-start.24 = (bf16[128,1024]{1,0:T(8,128)(2,1)S(1)}, bf16[128,1024]{1,0:T(8,128)(2,1)S(1)}, u32[]{:S(2)}, u32[]{:S(2)}) collective-permute-start(bf16[128,1024]{1,0:T(8,128)(2,1)S(1)} %shard_map.93), channel_id=1, source_target_pairs={{0,2},{1,3},{2,0},{3,1},{4,6},{5,7},{6,4},{7,5},{8,10},{9,11},{10,... | collective-permute-start | bytes 786440 | tf_op jit(solution)/shard_map/ppermute | solution.py:417
  58.3 1.6 %collective-permute-start.22 = (bf16[64,1024]{1,0:T(8,128)(2,1)S(1)}, bf16[64,1024]{1,0:T(8,128)(2,1)S(1)}, u32[]{:S(2)}, u32[]{:S(2)}) collective-permute-start(bf16[64,1024]{1,0:T(8,128)(2,1)S(1)} %shard_map.90.refs_16_), channel_id=1, source_target_pairs={{0,2},{1,3},{2,0},{3,1},{4,6},{5,7},{6,4},{7,5},{8,10},{9,11},{10,... | collective-permute-start | bytes 393224 | tf_op jit(solution)/shard_map/ppermute | solution.py:417
  59.9 1.7 %shard_map.91.h_ref = f32[512,1024]{1,0:T(8,128)S(1)} custom-call(bf16[256,256]{1,0:T(8,128)(2,1)S(1)} %get-tuple-element.84.refs_3_.refs_0_, bf16[256,256]{1,0:T(8,128)(2,1)S(1)} %collective-permute-done.14.refs_1_, bf16[256,256]{1,0:T(8,128)(2,1)S(1)} %get-tuple-element.85.refs_4_.refs_0_.refs_2_, ...), custom_call_target="tpu_custom_call" | custom-call | tf_op jit(solution)/shard_map/pallas_call | solution.py:41
  61.6 4.1 %collective-permute-done.26.a_ref = bf16[128,1024]{1,0:T(8,128)(2,1)S(1)} collective-permute-done((bf16[128,1024]{1,0:T(8,128)(2,1)S(1)}, bf16[128,1024]{1,0:T(8,128)(2,1)S(1)}, u32[]{:S(2)}, u32[]{:S(2)}) %collective-permute-start.26) | collective-permute-done | bytes 262176 | tf_op jit(solution)/shard_map/ppermute | solution.py:417
  67.1 4.2 %collective-permute-done.24.a_ref = bf16[128,1024]{1,0:T(8,128)(2,1)S(1)} collective-permute-done((bf16[128,1024]{1,0:T(8,128)(2,1)S(1)}, bf16[128,1024]{1,0:T(8,128)(2,1)S(1)}, u32[]{:S(2)}, u32[]{:S(2)}) %collective-permute-start.24) | collective-permute-done | bytes 262176 | tf_op jit(solution)/shard_map/ppermute | solution.py:417
  72.0 2.1 %collective-permute-done.23.a_ref = bf16[64,1024]{1,0:T(8,128)(2,1)S(1)} collective-permute-done((bf16[64,1024]{1,0:T(8,128)(2,1)S(1)}, bf16[64,1024]{1,0:T(8,128)(2,1)S(1)}, u32[]{:S(2)}, u32[]{:S(2)}) %collective-permute-start.23) | collective-permute-done | bytes 131104 | tf_op jit(solution)/shard_map/ppermute | solution.py:417
  74.8 1.3 %collective-permute-done.22.a_ref = bf16[64,1024]{1,0:T(8,128)(2,1)S(1)} collective-permute-done((bf16[64,1024]{1,0:T(8,128)(2,1)S(1)}, bf16[64,1024]{1,0:T(8,128)(2,1)S(1)}, u32[]{:S(2)}, u32[]{:S(2)}) %collective-permute-start.22) | collective-permute-done | bytes 131104 | tf_op jit(solution)/shard_map/ppermute | solution.py:417
  (60 shorter events, 17.0 us)
Async XLA Ops:
  0.0 3.0 %collective-permute-start.1 = (bf16[512,1024]{1,0:T(8,128)(2,1)}, bf16[512,1024]{1,0:T(8,128)(2,1)S(1)}, u32[]{:S(2)}, u32[]{:S(2)}) collective-permute-start(bf16[512,1024]{1,0:T(8,128)(2,1)} %refs_2_.1), channel_id=1, source_target_pairs={{0,1},{1,0},{2,3},{3,2},{4,5},{5,4},{6,7},{7,6},{8,9},{9,8},{10,11... | collective-permute-start | bytes 3145736 | tf_op jit(solution)/shard_map/ppermute | solution.py:417
  0.5 26.6 %collective-permute-start = (bf16[512,1024]{1,0:T(8,128)(2,1)}, bf16[512,1024]{1,0:T(8,128)(2,1)S(1)}, u32[]{:S(2)}, u32[]{:S(2)}) collective-permute-start(bf16[512,1024]{1,0:T(8,128)(2,1)} %refs_2_.1), channel_id=1, source_target_pairs={{0,2},{1,3},{2,0},{3,1},{4,6},{5,7},{6,4},{7,5},{8,10},{9,11},{10,... | collective-permute-start | bytes 3145736 | tf_op jit(solution)/shard_map/ppermute | solution.py:417
  9.0 18.0 %collective-permute-start.5 = (bf16[512,1024]{1,0:T(8,128)(2,1)S(1)}, bf16[512,1024]{1,0:T(8,128)(2,1)S(1)}, u32[]{:S(2)}, u32[]{:S(2)}) collective-permute-start(bf16[512,1024]{1,0:T(8,128)(2,1)S(1)} %get-tuple-element.61), channel_id=1, source_target_pairs={{0,1},{1,0},{2,3},{3,2},{4,5},{5,4},{6,7},{7,6},{8,9},{9,8},{10,11... | collective-permute-start | bytes 3145736 | tf_op jit(solution)/shard_map/ppermute | solution.py:417
  9.5 17.6 %collective-permute-start.6 = (bf16[512,1024]{1,0:T(8,128)(2,1)S(1)}, bf16[512,1024]{1,0:T(8,128)(2,1)S(1)}, u32[]{:S(2)}, u32[]{:S(2)}) collective-permute-start(bf16[512,1024]{1,0:T(8,128)(2,1)S(1)} %get-tuple-element.62), channel_id=1, source_target_pairs={{0,1},{1,0},{2,3},{3,2},{4,5},{5,4},{6,7},{7,6},{8,9},{9,8},{10,11... | collective-permute-start | bytes 3145736 | tf_op jit(solution)/shard_map/ppermute | solution.py:417
  9.6 17.4 %collective-permute-start.2 = (bf16[1024,256]{1,0:T(8,128)(2,1)S(1)}, bf16[1024,256]{1,0:T(8,128)(2,1)S(1)}, u32[]{:S(2)}, u32[]{:S(2)}) collective-permute-start(bf16[1024,256]{1,0:T(8,128)(2,1)S(1)} %get-tuple-element.56), channel_id=1, source_target_pairs={{0,1},{1,0},{2,3},{3,2},{4,5},{5,4},{6,7},{7,6},{8,9},{9,8},{10,11... | collective-permute-start | bytes 1572872 | tf_op jit(solution)/shard_map/ppermute | solution.py:417
  10.0 4.3 %collective-permute-start.3 = (f32[8,512]{1,0:T(8,128)S(1)}, f32[8,512]{1,0:T(8,128)S(1)}, u32[]{:S(2)}, u32[]{:S(2)}) collective-permute-start(f32[8,512]{1,0:T(8,128)S(1)} %get-tuple-element.57.refs_1_), channel_id=1, source_target_pairs={{0,4},{4,0},{8,12},{12,8},{16,20},{20,16},{24,28},{28,24},{1,5},{5... | collective-permute-start | bytes 49160 | tf_op jit(solution)/shard_map/ppermute | solution.py:421
  14.3 3.9 %collective-permute-start.4 = (f32[8,512]{1,0:T(8,128)S(1)}, f32[8,512]{1,0:T(8,128)S(1)}, u32[]{:S(2)}, u32[]{:S(2)}) collective-permute-start(f32[8,512]{1,0:T(8,128)S(1)} %get-tuple-element.58.refs_1_), channel_id=1, source_target_pairs={{0,8},{4,12},{8,0},{12,4},{16,24},{20,28},{24,16},{28,20},{1,9},{5... | collective-permute-start | bytes 49160 | tf_op jit(solution)/shard_map/ppermute | solution.py:421
  29.1 3.1 %collective-permute-start.8 = (bf16[512,1024]{1,0:T(8,128)(2,1)S(1)}, bf16[512,1024]{1,0:T(8,128)(2,1)S(1)}, u32[]{:S(2)}, u32[]{:S(2)}) collective-permute-start(bf16[512,1024]{1,0:T(8,128)(2,1)S(1)} %shard_map.78), channel_id=1, source_target_pairs={{0,1},{1,0},{2,3},{3,2},{4,5},{5,4},{6,7},{7,6},{8,9},{9,8},{10,11... | collective-permute-start | bytes 3145736 | tf_op jit(solution)/shard_map/ppermute | solution.py:417
  30.1 4.5 %collective-permute-start.9 = (bf16[128,256]{1,0:T(8,128)(2,1)S(1)}, bf16[128,256]{1,0:T(8,128)(2,1)S(1)}, u32[]{:S(2)}, u32[]{:S(2)}) collective-permute-start(bf16[128,256]{1,0:T(8,128)(2,1)S(1)} %get-tuple-element.76.refs_0_), channel_id=1, source_target_pairs={{0,4},{4,0},{8,12},{12,8},{16,20},{20,16},{24,28},{28,24},{1,5},{5... | collective-permute-start | bytes 196616 | tf_op jit(solution)/shard_map/ppermute | solution.py:421
  31.8 4.9 %collective-permute-start.10 = (bf16[128,256]{1,0:T(8,128)(2,1)S(1)}, bf16[128,256]{1,0:T(8,128)(2,1)S(1)}, u32[]{:S(2)}, u32[]{:S(2)}) collective-permute-start(bf16[128,256]{1,0:T(8,128)(2,1)S(1)} %get-tuple-element.77.refs_0_), channel_id=1, source_target_pairs={{0,4},{4,0},{8,12},{12,8},{16,20},{20,16},{24,28},{28,24},{1,5},{5... | collective-permute-start | bytes 196616 | tf_op jit(solution)/shard_map/ppermute | solution.py:421
  34.6 4.6 %collective-permute-start.11 = (bf16[128,256]{1,0:T(8,128)(2,1)S(1)}, bf16[128,256]{1,0:T(8,128)(2,1)S(1)}, u32[]{:S(2)}, u32[]{:S(2)}) collective-permute-start(bf16[128,256]{1,0:T(8,128)(2,1)S(1)} %shard_map.83.refs_0_), channel_id=1, source_target_pairs={{0,8},{4,12},{8,0},{12,4},{16,24},{20,28},{24,16},{28,20},{1,9},{5... | collective-permute-start | bytes 196616 | tf_op jit(solution)/shard_map/ppermute | solution.py:421
  36.8 7.8 %collective-permute-start.12 = (bf16[128,256]{1,0:T(8,128)(2,1)S(1)}, bf16[128,256]{1,0:T(8,128)(2,1)S(1)}, u32[]{:S(2)}, u32[]{:S(2)}) collective-permute-start(bf16[128,256]{1,0:T(8,128)(2,1)S(1)} %shard_map.84.refs_0_), channel_id=1, source_target_pairs={{0,8},{4,12},{8,0},{12,4},{16,24},{20,28},{24,16},{28,20},{1,9},{5... | collective-permute-start | bytes 196616 | tf_op jit(solution)/shard_map/ppermute | solution.py:421
  39.3 8.3 %collective-permute-start.13 = (bf16[128,256]{1,0:T(8,128)(2,1)S(1)}, bf16[128,256]{1,0:T(8,128)(2,1)S(1)}, u32[]{:S(2)}, u32[]{:S(2)}) collective-permute-start(bf16[128,256]{1,0:T(8,128)(2,1)S(1)} %shard_map.86), channel_id=1, source_target_pairs={{0,16},{4,20},{8,24},{12,28},{1,17},{5,21},{9,25},{13,29},{2,18},{... | collective-permute-start | bytes 196616 | tf_op jit(solution)/shard_map/ppermute | solution.py:421
  44.6 3.9 %collective-permute-start.16 = (bf16[128,256]{1,0:T(8,128)(2,1)S(1)}, bf16[128,256]{1,0:T(8,128)(2,1)S(1)}, u32[]{:S(2)}, u32[]{:S(2)}) collective-permute-start(bf16[128,256]{1,0:T(8,128)(2,1)S(1)} %shard_map.88), channel_id=1, source_target_pairs={{0,16},{4,20},{8,24},{12,28},{1,17},{5,21},{9,25},{13,29},{2,18},{... | collective-permute-start | bytes 196616 | tf_op jit(solution)/shard_map/ppermute | solution.py:421
  48.0 2.3 %collective-permute-start.14 = (bf16[256,256]{1,0:T(8,128)(2,1)S(1)}, bf16[256,256]{1,0:T(8,128)(2,1)S(1)}, u32[]{:S(2)}, u32[]{:S(2)}) collective-permute-start(bf16[256,256]{1,0:T(8,128)(2,1)S(1)} %get-tuple-element.84.refs_3_.refs_0_), channel_id=1, source_target_pairs={{0,1},{1,0},{2,3},{3,2},{4,5},{5,4},{6,7},{7,6},{8,9},{9,8},{10,11... | collective-permute-start | bytes 393224 | tf_op jit(solution)/shard_map/ppermute | solution.py:417
  48.1 5.4 %collective-permute-start.15 = (bf16[256,256]{1,0:T(8,128)(2,1)S(1)}, bf16[256,256]{1,0:T(8,128)(2,1)S(1)}, u32[]{:S(2)}, u32[]{:S(2)}) collective-permute-start(bf16[256,256]{1,0:T(8,128)(2,1)S(1)} %get-tuple-element.85.refs_4_.refs_0_.refs_2_), channel_id=1, source_target_pairs={{0,1},{1,0},{2,3},{3,2},{4,5},{5,4},{6,7},{7,6},{8,9},{9,8},{10,11... | collective-permute-start | bytes 393224 | tf_op jit(solution)/shard_map/ppermute | solution.py:417
  49.2 3.2 %collective-permute-start.17 = (bf16[128,256]{1,0:T(8,128)(2,1)S(1)}, bf16[128,256]{1,0:T(8,128)(2,1)S(1)}, u32[]{:S(2)}, u32[]{:S(2)}) collective-permute-start(bf16[128,256]{1,0:T(8,128)(2,1)S(1)} %get-tuple-element.88.refs_4_.refs_2_), channel_id=1, source_target_pairs={{0,1},{1,0},{2,3},{3,2},{4,5},{5,4},{6,7},{7,6},{8,9},{9,8},{10,11... | collective-permute-start | bytes 196616 | tf_op jit(solution)/shard_map/ppermute | solution.py:417
  49.6 3.9 %collective-permute-start.19 = (bf16[128,256]{1,0:T(8,128)(2,1)S(1)}, bf16[128,256]{1,0:T(8,128)(2,1)S(1)}, u32[]{:S(2)}, u32[]{:S(2)}) collective-permute-start(bf16[128,256]{1,0:T(8,128)(2,1)S(1)} %get-tuple-element.90.refs_8_.refs_2_), channel_id=1, source_target_pairs={{0,1},{1,0},{2,3},{3,2},{4,5},{5,4},{6,7},{7,6},{8,9},{9,8},{10,11... | collective-permute-start | bytes 196616 | tf_op jit(solution)/shard_map/ppermute | solution.py:417
  50.8 15.6 %collective-permute-start.25 = (bf16[128,1024]{1,0:T(8,128)(2,1)S(1)}, bf16[128,1024]{1,0:T(8,128)(2,1)S(1)}, u32[]{:S(2)}, u32[]{:S(2)}) collective-permute-start(bf16[128,1024]{1,0:T(8,128)(2,1)S(1)} %shard_map.94), channel_id=1, source_target_pairs={{0,2},{1,3},{2,0},{3,1},{4,6},{5,7},{6,4},{7,5},{8,10},{9,11},{10,... | collective-permute-start | bytes 786440 | tf_op jit(solution)/shard_map/ppermute | solution.py:417
  52.9 12.8 %collective-permute-start.26 = (bf16[128,1024]{1,0:T(8,128)(2,1)S(1)}, bf16[128,1024]{1,0:T(8,128)(2,1)S(1)}, u32[]{:S(2)}, u32[]{:S(2)}) collective-permute-start(bf16[128,1024]{1,0:T(8,128)(2,1)S(1)} %shard_map.95), channel_id=1, source_target_pairs={{0,2},{1,3},{2,0},{3,1},{4,6},{5,7},{6,4},{7,5},{8,10},{9,11},{10,... | collective-permute-start | bytes 786440 | tf_op jit(solution)/shard_map/ppermute | solution.py:417
  53.9 17.3 %collective-permute-start.24 = (bf16[128,1024]{1,0:T(8,128)(2,1)S(1)}, bf16[128,1024]{1,0:T(8,128)(2,1)S(1)}, u32[]{:S(2)}, u32[]{:S(2)}) collective-permute-start(bf16[128,1024]{1,0:T(8,128)(2,1)S(1)} %shard_map.93), channel_id=1, source_target_pairs={{0,2},{1,3},{2,0},{3,1},{4,6},{5,7},{6,4},{7,5},{8,10},{9,11},{10,... | collective-permute-start | bytes 786440 | tf_op jit(solution)/shard_map/ppermute | solution.py:417
  55.5 2.3 %collective-permute-start.21 = (bf16[64,256]{1,0:T(8,128)(2,1)S(1)}, bf16[64,256]{1,0:T(8,128)(2,1)S(1)}, u32[]{:S(2)}, u32[]{:S(2)}) collective-permute-start(bf16[64,256]{1,0:T(8,128)(2,1)S(1)} %get-tuple-element.92.refs_2_.refs_12_), channel_id=1, source_target_pairs={{0,1},{1,0},{2,3},{3,2},{4,5},{5,4},{6,7},{7,6},{8,9},{9,8},{10,11... | collective-permute-start | bytes 98312 | tf_op jit(solution)/shard_map/ppermute | solution.py:417
  57.2 16.9 %collective-permute-start.23 = (bf16[64,1024]{1,0:T(8,128)(2,1)S(1)}, bf16[64,1024]{1,0:T(8,128)(2,1)S(1)}, u32[]{:S(2)}, u32[]{:S(2)}) collective-permute-start(bf16[64,1024]{1,0:T(8,128)(2,1)S(1)} %shard_map.92), channel_id=1, source_target_pairs={{0,2},{1,3},{2,0},{3,1},{4,6},{5,7},{6,4},{7,5},{8,10},{9,11},{10,... | collective-permute-start | bytes 393224 | tf_op jit(solution)/shard_map/ppermute | solution.py:417
  58.3 17.8 %collective-permute-start.22 = (bf16[64,1024]{1,0:T(8,128)(2,1)S(1)}, bf16[64,1024]{1,0:T(8,128)(2,1)S(1)}, u32[]{:S(2)}, u32[]{:S(2)}) collective-permute-start(bf16[64,1024]{1,0:T(8,128)(2,1)S(1)} %shard_map.90.refs_16_), channel_id=1, source_target_pairs={{0,2},{1,3},{2,0},{3,1},{4,6},{5,7},{6,4},{7,5},{8,10},{9,11},{10,... | collective-permute-start | bytes 393224 | tf_op jit(solution)/shard_map/ppermute | solution.py:417
  (4 other events, 4.8 us)

commit v14 on v12

--- a/solution.py
+++ b/solution.py
@@ -343,10 +343,12 @@
     return list(zip(outs[:2], outs[2:]))
 
 
-def finish(local, scaled, state, cuts, head_size, flops, after=()):
-    width = state.shape[1]
-
-    def kernel(o_ref, q_ref, s_ref, *outs):
+def finish(slab, bit, local, scaled, states, cuts, head_size, flops, after=()):
+    width = local.shape[1]
+
+    def kernel(slab_ref, o_ref, q_ref, s0_ref, s1_ref, *outs):
+        s_ref = jnp.where(upper_half(slab_ref, bit), s1_ref[...].astype(F32), s0_ref[...].astype(F32))
+        s_ref = s_ref.astype(BF16)
         for rows, n_ref in zip(cuts, outs):
             for c in range(0, width, head_size):
                 cols = slice(c, c + head_size)
@@ -355,7 +357,7 @@
                 n_ref[:, cols] = (total * lax.rsqrt(mean + 1e-05)).astype(BF16)
 
     outs = [shape((cut.stop - cut.start, width), BF16) for cut in cuts]
-    return call(kernel, [local, scaled, state], outs, flops, after)
+    return call(kernel, [slab, local, scaled, *states], outs, flops, after, smem=1)
 
 
 def out_block(first, second, places, w0, w1, dtype, after=()):
@@ -419,6 +421,13 @@
     def swap_seq(x, bit):
         return lax.ppermute(x, "seq", [(i, i ^ bit) for i in range(seq_size)])
 
+    def from_second_quarter(x, bits):
+        quarter = seq_size // 4
+        pairs = {i: i for i in range(seq_size)}
+        for i in range(quarter, 2 * quarter):
+            pairs[i], pairs[i ^ bits] = i ^ bits, i
+        return lax.ppermute(x, "seq", list(pairs.items()))
+
     far = swap_tp(tokens, 2)
     near = swap_tp(tokens, 1)
 
@@ -448,24 +457,30 @@
     locals_ = [attend(q, level, k, v, dcol, drow, i, head_size, level_count) for i in range(2)]
     earlier = []
     for b in range(seq_bits):
+        if b == seq_bits - 1:
+            last = [
+                (from_second_quarter(x, 3 << (b - 1)), from_second_quarter(x, 1 << b)) for x in states
+            ]
+            break
         others = [swap_seq(state, 1 << b) for state in states]
         earlier.append(others)
-        if b < seq_bits - 1:
-            afters = (locals_[b : b + 1], ())
-            states = [
-                combine(state, other, *factors[b], i, after)
-                for i, (state, other, after) in enumerate(zip(states, others, afters))
-            ]
-    before_last = [state for others in earlier[:-1] for state in others]
+        afters = (locals_[b : b + 1], ())
+        states = [
+            combine(state, other, *factors[b], i, after)
+            for i, (state, other, after) in enumerate(zip(states, others, afters))
+        ]
+    before_last = [state for others in earlier for state in others]
     halves = attend_earlier(locals_, q, level, dcol, spans, before_last, head_size, level_count)
 
     unit = rows // 8
     ends = (0, 2, 4, 6, 7, 8)
     cuts = [slice(start * unit, stop * unit) for start, stop in zip(ends, ends[1:])]
     middle = rows // 2
-    tops = finish(*halves[0], earlier[-1][0], [slice(0, middle), slice(middle, rows)], head_size, 10**8)
+    tops = finish(
+        slab, seq_bits - 2, *halves[0], last[0], [slice(0, middle), slice(middle, rows)], head_size, 10**8
+    )
     first = [(x, swap_tp(x, 1)) for x in tops]
-    second = finish(*halves[1], earlier[-1][1], cuts, head_size, 0, tops)
+    second = finish(slab, seq_bits - 2, *halves[1], last[1], cuts, head_size, 0, tops)
     second = [(x, swap_tp(x, 1)) for x in second]
     crossing = []
     for pair, cut in zip(second, cuts):

time: 77.1 us -> 81.1 us (1.052)
  the two profiles are of different devices: /device:TPU:0 before, /device:TPU:10 now
where the time goes in v14:
time: 81.1 us; the launch traced here: 80.9 us
  waiting for transfers between devices  31.3 us (39%)
  starting transfers between devices  26.7 us (33%)
  Pallas kernels  22 us (27%)
    ppermute x19, waiting for transfers between devices, swap_tp(): return lax.ppermute(x, 'tp', [(i, i ^ bit) for i in range(4)])  22.5 us
    pallas_call x22, Pallas kernels, call(): pl.pallas_call(run, in_specs=[SMEM] * smem + [HBM] * hbm + [VMEM] * (coun...  18.4 us
    ppermute x4, starting transfers between devices, from_second_quarter(): return lax.ppermute(x, 'seq', list(pairs.items()))  11.2 us
    ppermute x19, starting transfers between devices, swap_tp(): return lax.ppermute(x, 'tp', [(i, i ^ bit) for i in range(4)])  10.3 us
    ppermute x6, waiting for transfers between devices, swap_seq(): return lax.ppermute(x, 'seq', [(i, i ^ bit) for i in range(seq_size)])  7.95 us
    ppermute x6, starting transfers between devices, swap_seq(): return lax.ppermute(x, 'seq', [(i, i ^ bit) for i in range(seq_size)])  5.17 us
    pallas_call x5, Pallas kernels, add_rows(): pl.pallas_call(kernel, grid=(rows // unit,), in_specs=specs, out_specs=pl...  3.54 us
  transfers between devices with their start and end apart: 29, of which 15 were waited for; matrix products, arithmetic and copies ran while one was open for 0% of the time, Pallas kernels for 26%

profile of v14, /device:TPU:10, one launch (start us, length us, event | category | flops | bytes accessed | tf_op | source)
XLA Modules:
  0.0 80.9 jit_solution(2528283432799548271)
XLA Ops:
  0.0 1.5 %collective-permute-start = (bf16[512,1024]{1,0:T(8,128)(2,1)}, bf16[512,1024]{1,0:T(8,128)(2,1)S(1)}, u32[]{:S(2)}, u32[]{:S(2)}) collective-permute-start(bf16[512,1024]{1,0:T(8,128)(2,1)} %refs_2_.1), channel_id=1, source_target_pairs={{0,2},{1,3},{2,0},{3,1},{4,6},{5,7},{6,4},{7,5},{8,10},{9,11},{10,... | collective-permute-start | bytes 3145736 | tf_op jit(solution)/shard_map/ppermute | solution.py:419
  1.5 1.3 %collective-permute-done.1.refs_8_ = bf16[512,1024]{1,0:T(8,128)(2,1)S(1)} collective-permute-done((bf16[512,1024]{1,0:T(8,128)(2,1)}, bf16[512,1024]{1,0:T(8,128)(2,1)S(1)}, u32[]{:S(2)}, u32[]{:S(2)}) %collective-permute-start.1) | collective-permute-done | bytes 1048608 | tf_op jit(solution)/shard_map/ppermute | solution.py:419
  3.6 5.4 %shard_map.73 = (f32[512,512]{1,0:T(8,128)S(1)}, f32[512,256]{1,0:T(8,128)S(1)}, f32[512,24]{1,0:T(8,128)S(1)}, bf16[2,1024,512]{2,1,0:T(8,128)(2,1)S(1)}, bf16[...) custom-call(s32[1]{0:T(128)} %bitcast.1.refs_0_, ...), custom_call_target="tpu_custom_call" | custom-call | tf_op jit(solution)/shard_map/pallas_call | solution.py:41
  10.2 3.2 %collective-permute-done.3.refs_2_ = f32[8,512]{1,0:T(8,128)S(1)} collective-permute-done((f32[8,512]{1,0:T(8,128)S(1)}, f32[8,512]{1,0:T(8,128)S(1)}, u32[]{:S(2)}, u32[]{:S(2)}) %collective-permute-start.3) | collective-permute-done | bytes 16416 | tf_op jit(solution)/shard_map/ppermute | solution.py:422
  13.9 3.3 %collective-permute-done.4.refs_2_ = f32[8,512]{1,0:T(8,128)S(1)} collective-permute-done((f32[8,512]{1,0:T(8,128)S(1)}, f32[8,512]{1,0:T(8,128)S(1)}, u32[]{:S(2)}, u32[]{:S(2)}) %collective-permute-start.4) | collective-permute-done | bytes 16416 | tf_op jit(solution)/shard_map/ppermute | solution.py:422
  17.8 7.9 %collective-permute-done.refs_0_.refs_1_ = bf16[512,1024]{1,0:T(8,128)(2,1)S(1)} collective-permute-done((bf16[512,1024]{1,0:T(8,128)(2,1)}, bf16[512,1024]{1,0:T(8,128)(2,1)S(1)}, u32[]{:S(2)}, u32[]{:S(2)}) %collective-permute-start) | collective-permute-done | bytes 1048608 | tf_op jit(solution)/shard_map/ppermute | solution.py:419
  26.3 1.3 %shard_map.77 = (f32[512,512]{1,0:T(8,128)S(1)}, f32[512,256]{1,0:T(8,128)S(1)}, f32[512,24]{1,0:T(8,128)S(1)}) custom-call(s32[1]{0:T(128)} %bitcast.1.refs_0_, bf16[512,1024]{1,0:T(8,128)(2,1)S(1)} %collective-permute-done.refs_0_.refs_1_, ...), custom_call_target="tpu_custom_call", output_to_operand_aliasing={{0}: (5, {}), {1}: (6, {}), {2}: (7, {})} | custom-call | tf_op jit(solution)/shard_map/pallas_call | solution.py:41
  29.4 1.5 %collective-permute-start.10 = (bf16[128,256]{1,0:T(8,128)(2,1)S(1)}, bf16[128,256]{1,0:T(8,128)(2,1)S(1)}, u32[]{:S(2)}, u32[]{:S(2)}) collective-permute-start(bf16[128,256]{1,0:T(8,128)(2,1)S(1)} %get-tuple-element.77.refs_0_), channel_id=1, source_target_pairs={{0,4},{4,0},{8,12},{12,8},{16,20},{20,16},{24,28},{28,24},{1,5},{5... | collective-permute-start | bytes 196616 | tf_op jit(solution)/shard_map/ppermute | solution.py:422
  32.0 1.3 %shard_map.81.refs_4_.refs_0_ = f32[512,256]{1,0:T(8,128)S(1)} custom-call(bf16[512,512]{1,0:T(8,128)(2,1)S(1)} %get-tuple-element.65.refs_0_.refs_2_, f32[512,24]{1,0:T(8,128)S(1)} %get-tuple-element.66.refs_1_.refs_3_, bf16[512,128]{1,0:T(8,128)(2,1)S(1)} %get-tuple-element.69.refs_2_, bf16[512,128]{1,0:T(8,128)(2,1)S(1)} %get-tuple-element.70.refs_3_, ...), custom_call_target="tpu_custom_call" | custom-call | tf_op jit(solution)/shard_map/pallas_call | solution.py:41
  34.4 1.5 %collective-permute-start.12 = (bf16[128,256]{1,0:T(8,128)(2,1)S(1)}, bf16[128,256]{1,0:T(8,128)(2,1)S(1)}, u32[]{:S(2)}, u32[]{:S(2)}) collective-permute-start(bf16[128,256]{1,0:T(8,128)(2,1)S(1)} %shard_map.84.refs_0_), channel_id=1, source_target_pairs={{0,8},{4,12},{8,0},{12,4},{16,24},{20,28},{24,16},{28,20},{1,9},{5... | collective-permute-start | bytes 196616 | tf_op jit(solution)/shard_map/ppermute | solution.py:422
  35.9 1.3 %shard_map.82.refs_1_.refs_4_ = f32[512,256]{1,0:T(8,128)S(1)} custom-call(bf16[512,512]{1,0:T(8,128)(2,1)S(1)} %get-tuple-element.65.refs_0_.refs_2_, f32[512,24]{1,0:T(8,128)S(1)} %get-tuple-element.66.refs_1_.refs_3_, bf16[512,128]{1,0:T(8,128)(2,1)S(1)} %get-tuple-element.69.refs_2_, bf16[512,128]{1,0:T(8,128)(2,1)S(1)} %get-tuple-element.70.refs_3_, ...), custom_call_target="tpu_custom_call" | custom-call | tf_op jit(solution)/shard_map/pallas_call | solution.py:41
  38.1 4.5 %collective-permute-start.14 = (bf16[128,256]{1,0:T(8,128)(2,1)S(1)}, bf16[128,256]{1,0:T(8,128)(2,1)S(1)}, u32[]{:S(2)}, u32[]{:S(2)}) collective-permute-start(bf16[128,256]{1,0:T(8,128)(2,1)S(1)} %shard_map.86), channel_id=1, source_target_pairs={{0,0},{4,4},{8,24},{12,28},{16,16},{20,20},{24,8},{28,12},{1,1},{5... | collective-permute-start | bytes 196616 | tf_op jit(solution)/shard_map/ppermute | solution.py:429
  42.6 1.9 %collective-permute-start.13 = (bf16[128,256]{1,0:T(8,128)(2,1)S(1)}, bf16[128,256]{1,0:T(8,128)(2,1)S(1)}, u32[]{:S(2)}, u32[]{:S(2)}) collective-permute-start(bf16[128,256]{1,0:T(8,128)(2,1)S(1)} %shard_map.86), channel_id=1, source_target_pairs={{0,0},{4,4},{8,16},{12,20},{16,8},{20,12},{24,24},{28,28},{1,1},{5... | collective-permute-start | bytes 196616 | tf_op jit(solution)/shard_map/ppermute | solution.py:429
  44.6 1.9 %collective-permute-start.18 = (bf16[128,256]{1,0:T(8,128)(2,1)S(1)}, bf16[128,256]{1,0:T(8,128)(2,1)S(1)}, u32[]{:S(2)}, u32[]{:S(2)}) collective-permute-start(bf16[128,256]{1,0:T(8,128)(2,1)S(1)} %shard_map.88), channel_id=1, source_target_pairs={{0,0},{4,4},{8,24},{12,28},{16,16},{20,20},{24,8},{28,12},{1,1},{5... | collective-permute-start | bytes 196616 | tf_op jit(solution)/shard_map/ppermute | solution.py:429
  46.5 2.8 %collective-permute-start.17 = (bf16[128,256]{1,0:T(8,128)(2,1)S(1)}, bf16[128,256]{1,0:T(8,128)(2,1)S(1)}, u32[]{:S(2)}, u32[]{:S(2)}) collective-permute-start(bf16[128,256]{1,0:T(8,128)(2,1)S(1)} %shard_map.88), channel_id=1, source_target_pairs={{0,0},{4,4},{8,16},{12,20},{16,8},{20,12},{24,24},{28,28},{1,1},{5... | collective-permute-start | bytes 196616 | tf_op jit(solution)/shard_map/ppermute | solution.py:429
  49.4 1.5 %shard_map.85 = (f32[512,256]{1,0:T(8,128)S(1)}, f32[512,256]{1,0:T(8,128)S(1)}, bf16[512,256]{1,0:T(8,128)(2,1)S(1)}, bf16[512,256]{1,0:T(8,128)(2,1)S(1)}) custom-call(f32[512,256]{1,0:T(8,128)S(1)} %shard_map.81.refs_4_.refs_0_, f32[512,256]{1,0:T(8,128)S(1)} %shard_map.82.refs_1_.refs_4_, bf16[512,512]{1,0:T(8,128)(2,1)S(1)} %get-tuple-element.65.refs_0_.refs_2_, ...), custom_call_target="tpu_custom_call" | custom-call | tf_op jit(solution)/shard_map/pallas_call | solution.py:41
  54.9 1.6 %collective-permute-start.27 = (bf16[128,1024]{1,0:T(8,128)(2,1)S(1)}, bf16[128,1024]{1,0:T(8,128)(2,1)S(1)}, u32[]{:S(2)}, u32[]{:S(2)}) collective-permute-start(bf16[128,1024]{1,0:T(8,128)(2,1)S(1)} %shard_map.94), channel_id=1, source_target_pairs={{0,2},{1,3},{2,0},{3,1},{4,6},{5,7},{6,4},{7,5},{8,10},{9,11},{10,... | collective-permute-start | bytes 786440 | tf_op jit(solution)/shard_map/ppermute | solution.py:419
  58.0 1.6 %collective-permute-start.26 = (bf16[128,1024]{1,0:T(8,128)(2,1)S(1)}, bf16[128,1024]{1,0:T(8,128)(2,1)S(1)}, u32[]{:S(2)}, u32[]{:S(2)}) collective-permute-start(bf16[128,1024]{1,0:T(8,128)(2,1)S(1)} %shard_map.93), channel_id=1, source_target_pairs={{0,2},{1,3},{2,0},{3,1},{4,6},{5,7},{6,4},{7,5},{8,10},{9,11},{10,... | collective-permute-start | bytes 786440 | tf_op jit(solution)/shard_map/ppermute | solution.py:419
  62.4 1.6 %collective-permute-start.24 = (bf16[64,1024]{1,0:T(8,128)(2,1)S(1)}, bf16[64,1024]{1,0:T(8,128)(2,1)S(1)}, u32[]{:S(2)}, u32[]{:S(2)}) collective-permute-start(bf16[64,1024]{1,0:T(8,128)(2,1)S(1)} %shard_map.90.refs_16_), channel_id=1, source_target_pairs={{0,2},{1,3},{2,0},{3,1},{4,6},{5,7},{6,4},{7,5},{8,10},{9,11},{10,... | collective-permute-start | bytes 393224 | tf_op jit(solution)/shard_map/ppermute | solution.py:419
  64.0 1.7 %shard_map.91.h_ref = f32[512,1024]{1,0:T(8,128)S(1)} custom-call(bf16[256,256]{1,0:T(8,128)(2,1)S(1)} %get-tuple-element.84.refs_5_.refs_0_, bf16[256,256]{1,0:T(8,128)(2,1)S(1)} %collective-permute-done.15.refs_1_, bf16[256,256]{1,0:T(8,128)(2,1)S(1)} %get-tuple-element.85.refs_6_.refs_0_.refs_2_, ...), custom_call_target="tpu_custom_call" | custom-call | tf_op jit(solution)/shard_map/pallas_call | solution.py:41
  65.7 4.1 %collective-permute-done.28.a_ref = bf16[128,1024]{1,0:T(8,128)(2,1)S(1)} collective-permute-done((bf16[128,1024]{1,0:T(8,128)(2,1)S(1)}, bf16[128,1024]{1,0:T(8,128)(2,1)S(1)}, u32[]{:S(2)}, u32[]{:S(2)}) %collective-permute-start.28) | collective-permute-done | bytes 262176 | tf_op jit(solution)/shard_map/ppermute | solution.py:419
  71.2 4.2 %collective-permute-done.26.a_ref = bf16[128,1024]{1,0:T(8,128)(2,1)S(1)} collective-permute-done((bf16[128,1024]{1,0:T(8,128)(2,1)S(1)}, bf16[128,1024]{1,0:T(8,128)(2,1)S(1)}, u32[]{:S(2)}, u32[]{:S(2)}) %collective-permute-start.26) | collective-permute-done | bytes 262176 | tf_op jit(solution)/shard_map/ppermute | solution.py:419
  76.1 2.1 %collective-permute-done.25.a_ref = bf16[64,1024]{1,0:T(8,128)(2,1)S(1)} collective-permute-done((bf16[64,1024]{1,0:T(8,128)(2,1)S(1)}, bf16[64,1024]{1,0:T(8,128)(2,1)S(1)}, u32[]{:S(2)}, u32[]{:S(2)}) %collective-permute-start.25) | collective-permute-done | bytes 131104 | tf_op jit(solution)/shard_map/ppermute | solution.py:419
  78.9 1.3 %collective-permute-done.24.a_ref = bf16[64,1024]{1,0:T(8,128)(2,1)S(1)} collective-permute-done((bf16[64,1024]{1,0:T(8,128)(2,1)S(1)}, bf16[64,1024]{1,0:T(8,128)(2,1)S(1)}, u32[]{:S(2)}, u32[]{:S(2)}) %collective-permute-start.24) | collective-permute-done | bytes 131104 | tf_op jit(solution)/shard_map/ppermute | solution.py:419
  (64 shorter events, 20.3 us)
Async XLA Ops:
  0.0 25.8 %collective-permute-start = (bf16[512,1024]{1,0:T(8,128)(2,1)}, bf16[512,1024]{1,0:T(8,128)(2,1)S(1)}, u32[]{:S(2)}, u32[]{:S(2)}) collective-permute-start(bf16[512,1024]{1,0:T(8,128)(2,1)} %refs_2_.1), channel_id=1, source_target_pairs={{0,2},{1,3},{2,0},{3,1},{4,6},{5,7},{6,4},{7,5},{8,10},{9,11},{10,... | collective-permute-start | bytes 3145736 | tf_op jit(solution)/shard_map/ppermute | solution.py:419
  8.9 16.8 %collective-permute-start.5 = (bf16[512,1024]{1,0:T(8,128)(2,1)S(1)}, bf16[512,1024]{1,0:T(8,128)(2,1)S(1)}, u32[]{:S(2)}, u32[]{:S(2)}) collective-permute-start(bf16[512,1024]{1,0:T(8,128)(2,1)S(1)} %get-tuple-element.61), channel_id=1, source_target_pairs={{0,1},{1,0},{2,3},{3,2},{4,5},{5,4},{6,7},{7,6},{8,9},{9,8},{10,11... | collective-permute-start | bytes 3145736 | tf_op jit(solution)/shard_map/ppermute | solution.py:419
  9.1 16.6 %collective-permute-start.6 = (bf16[512,1024]{1,0:T(8,128)(2,1)S(1)}, bf16[512,1024]{1,0:T(8,128)(2,1)S(1)}, u32[]{:S(2)}, u32[]{:S(2)}) collective-permute-start(bf16[512,1024]{1,0:T(8,128)(2,1)S(1)} %get-tuple-element.62), channel_id=1, source_target_pairs={{0,1},{1,0},{2,3},{3,2},{4,5},{5,4},{6,7},{7,6},{8,9},{9,8},{10,11... | collective-permute-start | bytes 3145736 | tf_op jit(solution)/shard_map/ppermute | solution.py:419
  9.5 16.3 %collective-permute-start.2 = (bf16[1024,256]{1,0:T(8,128)(2,1)S(1)}, bf16[1024,256]{1,0:T(8,128)(2,1)S(1)}, u32[]{:S(2)}, u32[]{:S(2)}) collective-permute-start(bf16[1024,256]{1,0:T(8,128)(2,1)S(1)} %get-tuple-element.56), channel_id=1, source_target_pairs={{0,1},{1,0},{2,3},{3,2},{4,5},{5,4},{6,7},{7,6},{8,9},{9,8},{10,11... | collective-permute-start | bytes 1572872 | tf_op jit(solution)/shard_map/ppermute | solution.py:419
  9.7 3.8 %collective-permute-start.3 = (f32[8,512]{1,0:T(8,128)S(1)}, f32[8,512]{1,0:T(8,128)S(1)}, u32[]{:S(2)}, u32[]{:S(2)}) collective-permute-start(f32[8,512]{1,0:T(8,128)S(1)} %get-tuple-element.57.refs_1_), channel_id=1, source_target_pairs={{0,4},{4,0},{8,12},{12,8},{16,20},{20,16},{24,28},{28,24},{1,5},{5... | collective-permute-start | bytes 49160 | tf_op jit(solution)/shard_map/ppermute | solution.py:422
  13.4 3.8 %collective-permute-start.4 = (f32[8,512]{1,0:T(8,128)S(1)}, f32[8,512]{1,0:T(8,128)S(1)}, u32[]{:S(2)}, u32[]{:S(2)}) collective-permute-start(f32[8,512]{1,0:T(8,128)S(1)} %get-tuple-element.58.refs_1_), channel_id=1, source_target_pairs={{0,8},{4,12},{8,0},{12,4},{16,24},{20,28},{24,16},{28,20},{1,9},{5... | collective-permute-start | bytes 49160 | tf_op jit(solution)/shard_map/ppermute | solution.py:422
  27.9 3.1 %collective-permute-start.8 = (bf16[512,1024]{1,0:T(8,128)(2,1)S(1)}, bf16[512,1024]{1,0:T(8,128)(2,1)S(1)}, u32[]{:S(2)}, u32[]{:S(2)}) collective-permute-start(bf16[512,1024]{1,0:T(8,128)(2,1)S(1)} %shard_map.78), channel_id=1, source_target_pairs={{0,1},{1,0},{2,3},{3,2},{4,5},{5,4},{6,7},{7,6},{8,9},{9,8},{10,11... | collective-permute-start | bytes 3145736 | tf_op jit(solution)/shard_map/ppermute | solution.py:419
  28.8 4.9 %collective-permute-start.9 = (bf16[128,256]{1,0:T(8,128)(2,1)S(1)}, bf16[128,256]{1,0:T(8,128)(2,1)S(1)}, u32[]{:S(2)}, u32[]{:S(2)}) collective-permute-start(bf16[128,256]{1,0:T(8,128)(2,1)S(1)} %get-tuple-element.76.refs_0_), channel_id=1, source_target_pairs={{0,4},{4,0},{8,12},{12,8},{16,20},{20,16},{24,28},{28,24},{1,5},{5... | collective-permute-start | bytes 196616 | tf_op jit(solution)/shard_map/ppermute | solution.py:422
  29.4 5.0 %collective-permute-start.10 = (bf16[128,256]{1,0:T(8,128)(2,1)S(1)}, bf16[128,256]{1,0:T(8,128)(2,1)S(1)}, u32[]{:S(2)}, u32[]{:S(2)}) collective-permute-start(bf16[128,256]{1,0:T(8,128)(2,1)S(1)} %get-tuple-element.77.refs_0_), channel_id=1, source_target_pairs={{0,4},{4,0},{8,12},{12,8},{16,20},{20,16},{24,28},{28,24},{1,5},{5... | collective-permute-start | bytes 196616 | tf_op jit(solution)/shard_map/ppermute | solution.py:422
  33.7 4.3 %collective-permute-start.11 = (bf16[128,256]{1,0:T(8,128)(2,1)S(1)}, bf16[128,256]{1,0:T(8,128)(2,1)S(1)}, u32[]{:S(2)}, u32[]{:S(2)}) collective-permute-start(bf16[128,256]{1,0:T(8,128)(2,1)S(1)} %shard_map.83.refs_0_), channel_id=1, source_target_pairs={{0,8},{4,12},{8,0},{12,4},{16,24},{20,28},{24,16},{28,20},{1,9},{5... | collective-permute-start | bytes 196616 | tf_op jit(solution)/shard_map/ppermute | solution.py:422
  34.4 10.1 %collective-permute-start.12 = (bf16[128,256]{1,0:T(8,128)(2,1)S(1)}, bf16[128,256]{1,0:T(8,128)(2,1)S(1)}, u32[]{:S(2)}, u32[]{:S(2)}) collective-permute-start(bf16[128,256]{1,0:T(8,128)(2,1)S(1)} %shard_map.84.refs_0_), channel_id=1, source_target_pairs={{0,8},{4,12},{8,0},{12,4},{16,24},{20,28},{24,16},{28,20},{1,9},{5... | collective-permute-start | bytes 196616 | tf_op jit(solution)/shard_map/ppermute | solution.py:422
  38.1 12.8 %collective-permute-start.14 = (bf16[128,256]{1,0:T(8,128)(2,1)S(1)}, bf16[128,256]{1,0:T(8,128)(2,1)S(1)}, u32[]{:S(2)}, u32[]{:S(2)}) collective-permute-start(bf16[128,256]{1,0:T(8,128)(2,1)S(1)} %shard_map.86), channel_id=1, source_target_pairs={{0,0},{4,4},{8,24},{12,28},{16,16},{20,20},{24,8},{28,12},{1,1},{5... | collective-permute-start | bytes 196616 | tf_op jit(solution)/shard_map/ppermute | solution.py:429
  42.6 8.3 %collective-permute-start.13 = (bf16[128,256]{1,0:T(8,128)(2,1)S(1)}, bf16[128,256]{1,0:T(8,128)(2,1)S(1)}, u32[]{:S(2)}, u32[]{:S(2)}) collective-permute-start(bf16[128,256]{1,0:T(8,128)(2,1)S(1)} %shard_map.86), channel_id=1, source_target_pairs={{0,0},{4,4},{8,16},{12,20},{16,8},{20,12},{24,24},{28,28},{1,1},{5... | collective-permute-start | bytes 196616 | tf_op jit(solution)/shard_map/ppermute | solution.py:429
  44.6 7.3 %collective-permute-start.18 = (bf16[128,256]{1,0:T(8,128)(2,1)S(1)}, bf16[128,256]{1,0:T(8,128)(2,1)S(1)}, u32[]{:S(2)}, u32[]{:S(2)}) collective-permute-start(bf16[128,256]{1,0:T(8,128)(2,1)S(1)} %shard_map.88), channel_id=1, source_target_pairs={{0,0},{4,4},{8,24},{12,28},{16,16},{20,20},{24,8},{28,12},{1,1},{5... | collective-permute-start | bytes 196616 | tf_op jit(solution)/shard_map/ppermute | solution.py:429
  46.5 6.2 %collective-permute-start.17 = (bf16[128,256]{1,0:T(8,128)(2,1)S(1)}, bf16[128,256]{1,0:T(8,128)(2,1)S(1)}, u32[]{:S(2)}, u32[]{:S(2)}) collective-permute-start(bf16[128,256]{1,0:T(8,128)(2,1)S(1)} %shard_map.88), channel_id=1, source_target_pairs={{0,0},{4,4},{8,16},{12,20},{16,8},{20,12},{24,24},{28,28},{1,1},{5... | collective-permute-start | bytes 196616 | tf_op jit(solution)/shard_map/ppermute | solution.py:429
  51.3 3.2 %collective-permute-start.15 = (bf16[256,256]{1,0:T(8,128)(2,1)S(1)}, bf16[256,256]{1,0:T(8,128)(2,1)S(1)}, u32[]{:S(2)}, u32[]{:S(2)}) collective-permute-start(bf16[256,256]{1,0:T(8,128)(2,1)S(1)} %get-tuple-element.84.refs_5_.refs_0_), channel_id=1, source_target_pairs={{0,1},{1,0},{2,3},{3,2},{4,5},{5,4},{6,7},{7,6},{8,9},{9,8},{10,11... | collective-permute-start | bytes 393224 | tf_op jit(solution)/shard_map/ppermute | solution.py:419
  51.4 6.2 %collective-permute-start.16 = (bf16[256,256]{1,0:T(8,128)(2,1)S(1)}, bf16[256,256]{1,0:T(8,128)(2,1)S(1)}, u32[]{:S(2)}, u32[]{:S(2)}) collective-permute-start(bf16[256,256]{1,0:T(8,128)(2,1)S(1)} %get-tuple-element.85.refs_6_.refs_0_.refs_2_), channel_id=1, source_target_pairs={{0,1},{1,0},{2,3},{3,2},{4,5},{5,4},{6,7},{7,6},{8,9},{9,8},{10,11... | collective-permute-start | bytes 393224 | tf_op jit(solution)/shard_map/ppermute | solution.py:419
  53.2 3.3 %collective-permute-start.19 = (bf16[128,256]{1,0:T(8,128)(2,1)S(1)}, bf16[128,256]{1,0:T(8,128)(2,1)S(1)}, u32[]{:S(2)}, u32[]{:S(2)}) collective-permute-start(bf16[128,256]{1,0:T(8,128)(2,1)S(1)} %get-tuple-element.88.refs_4_.refs_2_), channel_id=1, source_target_pairs={{0,1},{1,0},{2,3},{3,2},{4,5},{5,4},{6,7},{7,6},{8,9},{9,8},{10,11... | collective-permute-start | bytes 196616 | tf_op jit(solution)/shard_map/ppermute | solution.py:419
  53.7 3.9 %collective-permute-start.21 = (bf16[128,256]{1,0:T(8,128)(2,1)S(1)}, bf16[128,256]{1,0:T(8,128)(2,1)S(1)}, u32[]{:S(2)}, u32[]{:S(2)}) collective-permute-start(bf16[128,256]{1,0:T(8,128)(2,1)S(1)} %get-tuple-element.90.refs_8_.refs_2_), channel_id=1, source_target_pairs={{0,1},{1,0},{2,3},{3,2},{4,5},{5,4},{6,7},{7,6},{8,9},{9,8},{10,11... | collective-permute-start | bytes 196616 | tf_op jit(solution)/shard_map/ppermute | solution.py:419
  54.9 15.6 %collective-permute-start.27 = (bf16[128,1024]{1,0:T(8,128)(2,1)S(1)}, bf16[128,1024]{1,0:T(8,128)(2,1)S(1)}, u32[]{:S(2)}, u32[]{:S(2)}) collective-permute-start(bf16[128,1024]{1,0:T(8,128)(2,1)S(1)} %shard_map.94), channel_id=1, source_target_pairs={{0,2},{1,3},{2,0},{3,1},{4,6},{5,7},{6,4},{7,5},{8,10},{9,11},{10,... | collective-permute-start | bytes 786440 | tf_op jit(solution)/shard_map/ppermute | solution.py:419
  57.0 12.8 %collective-permute-start.28 = (bf16[128,1024]{1,0:T(8,128)(2,1)S(1)}, bf16[128,1024]{1,0:T(8,128)(2,1)S(1)}, u32[]{:S(2)}, u32[]{:S(2)}) collective-permute-start(bf16[128,1024]{1,0:T(8,128)(2,1)S(1)} %shard_map.95), channel_id=1, source_target_pairs={{0,2},{1,3},{2,0},{3,1},{4,6},{5,7},{6,4},{7,5},{8,10},{9,11},{10,... | collective-permute-start | bytes 786440 | tf_op jit(solution)/shard_map/ppermute | solution.py:419
  58.0 17.3 %collective-permute-start.26 = (bf16[128,1024]{1,0:T(8,128)(2,1)S(1)}, bf16[128,1024]{1,0:T(8,128)(2,1)S(1)}, u32[]{:S(2)}, u32[]{:S(2)}) collective-permute-start(bf16[128,1024]{1,0:T(8,128)(2,1)S(1)} %shard_map.93), channel_id=1, source_target_pairs={{0,2},{1,3},{2,0},{3,1},{4,6},{5,7},{6,4},{7,5},{8,10},{9,11},{10,... | collective-permute-start | bytes 786440 | tf_op jit(solution)/shard_map/ppermute | solution.py:419
  61.3 16.9 %collective-permute-start.25 = (bf16[64,1024]{1,0:T(8,128)(2,1)S(1)}, bf16[64,1024]{1,0:T(8,128)(2,1)S(1)}, u32[]{:S(2)}, u32[]{:S(2)}) collective-permute-start(bf16[64,1024]{1,0:T(8,128)(2,1)S(1)} %shard_map.92), channel_id=1, source_target_pairs={{0,2},{1,3},{2,0},{3,1},{4,6},{5,7},{6,4},{7,5},{8,10},{9,11},{10,... | collective-permute-start | bytes 393224 | tf_op jit(solution)/shard_map/ppermute | solution.py:419
  62.4 17.8 %collective-permute-start.24 = (bf16[64,1024]{1,0:T(8,128)(2,1)S(1)}, bf16[64,1024]{1,0:T(8,128)(2,1)S(1)}, u32[]{:S(2)}, u32[]{:S(2)}) collective-permute-start(bf16[64,1024]{1,0:T(8,128)(2,1)S(1)} %shard_map.90.refs_16_), channel_id=1, source_target_pairs={{0,2},{1,3},{2,0},{3,1},{4,6},{5,7},{6,4},{7,5},{8,10},{9,11},{10,... | collective-permute-start | bytes 393224 | tf_op jit(solution)/shard_map/ppermute | solution.py:419
  (6 other events, 10.0 us)

commit v15 on v10

--- a/solution.py
+++ b/solution.py
@@ -368,25 +368,33 @@
     return call(kernel, ins, [shape((rows, columns), dtype)], 0, after)[0]
 
 
-def add_rows(here, arrived, out, start, unit):
+def add_rows(here, arrived, out, start):
     rows, columns = arrived.shape
+    half = rows // 2
 
     def kernel(h_ref, a_ref, *refs):
-        place = pl.ds(pl.multiple_of(start + pl.program_id(0) * unit, unit), unit)
-        refs[-1][...] = (h_ref[place, :] + a_ref[...].astype(F32)).astype(BF16)
-
-    block = (unit, columns)
-    ins, specs, aliases = [here, arrived], [VMEM, pl.BlockSpec(block, lambda s: (s, 0))], {}
+        o_ref, sums, sems = refs[-3:]
+        moves = []
+        for i in range(2):
+            part = slice(i * half, (i + 1) * half)
+            place = slice(start + part.start, start + part.stop)
+            sums[part, :] = (h_ref[place, :] + a_ref[part, :].astype(F32)).astype(BF16)
+            moves.append(pltpu.make_async_copy(sums.at[part, :], o_ref.at[place, :], sems.at[i]))
+            moves[-1].start()
+        for move in moves:
+            move.wait()
+
+    ins, specs, aliases = [here, arrived], [VMEM, VMEM], {}
     if out is not None:
         ins, specs, aliases = ins + [out], specs + [ANY], {2: 0}
     return pl.pallas_call(
         kernel,
-        grid=(rows // unit,),
         in_specs=specs,
-        out_specs=pl.BlockSpec(block, lambda s: (start // unit + s, 0)),
+        out_specs=ANY,
         out_shape=shape(here.shape, BF16),
         input_output_aliases=aliases,
-        compiler_params=pltpu.CompilerParams(vmem_limit_bytes=8 * 1024 * 1024),
+        scratch_shapes=[pltpu.VMEM((rows, columns), BF16), pltpu.SemaphoreType.DMA((2,))],
+        compiler_params=pltpu.CompilerParams(vmem_limit_bytes=4 * 1024 * 1024),
         cost_estimate=pl.CostEstimate(flops=0, bytes_accessed=rows * columns * 8, transcendentals=0),
     )(*ins)
 
@@ -449,12 +457,14 @@
     unit = rows // 8
     ends = (0, 2, 4, 6, 7, 8)
     cuts = [slice(start * unit, stop * unit) for start, stop in zip(ends, ends[1:])]
-    pairs = [(x, swap_tp(x, 1)) for x in finish(local, scaled, earlier[-1], cuts, head_size)]
+    pieces = finish(local, scaled, earlier[-1], cuts[:1], head_size)
+    pieces += finish(local, scaled, earlier[-1], cuts[1:], head_size, pieces)
+    pairs = [(x, swap_tp(x, 1)) for x in pieces]
     crossing = [out_block([pair], w_far_own, w_far, BF16) for pair in pairs]
     own_block = out_block(pairs, w_here_own, w_here, F32, (crossing[-1],))
     out = None
     for cut, x in zip(cuts, crossing):
-        out = add_rows(own_block, swap_tp(x, 2), out, cut.start, unit)
+        out = add_rows(own_block, swap_tp(x, 2), out, cut.start)
     return out
 
 

time: 76.6 us -> 76.4 us (level)
    pallas_call x18 -> x19, Pallas kernels: 17.4 us -> 17.6 us  [call(): pl.pallas_call(run, in_specs=[SMEM] * smem + [HBM] * hbm + [VMEM] * (coun...]
  transfers between devices with their start and end apart: 25 -> 25, of which waited for: 13 -> 13; matrix products, arithmetic and copies ran while one was open for 0% -> 0% of each run, Pallas kernels for 24% -> 25%
where the time goes in v15:
time: 76.4 us; the launch traced here: 76.2 us
  waiting for transfers between devices  30.5 us (40%)
  starting transfers between devices  23.6 us (31%)
  Pallas kernels  21.2 us (28%)
    ppermute x20, waiting for transfers between devices, swap_tp(): return lax.ppermute(x, 'tp', [(i, i ^ bit) for i in range(4)])  21.8 us
    pallas_call x19, Pallas kernels, call(): pl.pallas_call(run, in_specs=[SMEM] * smem + [HBM] * hbm + [VMEM] * (coun...  17.6 us
    ppermute x20, starting transfers between devices, swap_tp(): return lax.ppermute(x, 'tp', [(i, i ^ bit) for i in range(4)])  12.2 us
    ppermute x5, starting transfers between devices, swap_seq(): return lax.ppermute(x, 'seq', [(i, i ^ bit) for i in range(seq_size)])  11.3 us
    ppermute x5, waiting for transfers between devices, swap_seq(): return lax.ppermute(x, 'seq', [(i, i ^ bit) for i in range(seq_size)])  8.77 us
    pallas_call x5, Pallas kernels, add_rows(): pl.pallas_call(kernel, in_specs=specs, out_specs=ANY, out_shape=shape(her...  3.58 us
  transfers between devices with their start and end apart: 25, of which 13 were waited for; matrix products, arithmetic and copies ran while one was open for 0% of the time, Pallas kernels for 25%

profile of v15, /device:TPU:0, one launch (start us, length us, event | category | flops | bytes accessed | tf_op | source)
XLA Modules:
  0.0 76.2 jit_solution(12454559375139867243)
XLA Ops:
  0.5 2.5 %collective-permute-start = (bf16[512,1024]{1,0:T(8,128)(2,1)}, bf16[512,1024]{1,0:T(8,128)(2,1)S(1)}, u32[]{:S(2)}, u32[]{:S(2)}) collective-permute-start(bf16[512,1024]{1,0:T(8,128)(2,1)} %refs_2_.1), channel_id=1, source_target_pairs={{0,2},{1,3},{2,0},{3,1},{4,6},{5,7},{6,4},{7,5},{8,10},{9,11},{10,... | collective-permute-start | bytes 3145736 | tf_op jit(solution)/shard_map/ppermute | solution.py:413
  3.7 5.4 %shard_map.73 = (f32[512,512]{1,0:T(8,128)S(1)}, f32[512,256]{1,0:T(8,128)S(1)}, f32[512,24]{1,0:T(8,128)S(1)}, bf16[2,1024,512]{2,1,0:T(8,128)(2,1)S(1)}, bf16[...) custom-call(s32[1]{0:T(128)} %bitcast.refs_0_, ...), custom_call_target="tpu_custom_call" | custom-call | tf_op jit(solution)/shard_map/pallas_call | solution.py:41
  10.0 2.6 %collective-permute-start.3 = (f32[8,512]{1,0:T(8,128)S(1)}, f32[8,512]{1,0:T(8,128)S(1)}, u32[]{:S(2)}, u32[]{:S(2)}) collective-permute-start(f32[8,512]{1,0:T(8,128)S(1)} %get-tuple-element.52.refs_1_), channel_id=1, source_target_pairs={{0,4},{4,0},{8,12},{12,8},{16,20},{20,16},{24,28},{28,24},{1,5},{5... | collective-permute-start | bytes 49160 | tf_op jit(solution)/shard_map/ppermute | solution.py:416
  12.6 1.7 %collective-permute-done.3.refs_2_ = f32[8,512]{1,0:T(8,128)S(1)} collective-permute-done((f32[8,512]{1,0:T(8,128)S(1)}, f32[8,512]{1,0:T(8,128)S(1)}, u32[]{:S(2)}, u32[]{:S(2)}) %collective-permute-start.3) | collective-permute-done | bytes 16416 | tf_op jit(solution)/shard_map/ppermute | solution.py:416
  14.3 2.2 %collective-permute-start.4 = (f32[8,512]{1,0:T(8,128)S(1)}, f32[8,512]{1,0:T(8,128)S(1)}, u32[]{:S(2)}, u32[]{:S(2)}) collective-permute-start(f32[8,512]{1,0:T(8,128)S(1)} %get-tuple-element.53.refs_1_), channel_id=1, source_target_pairs={{0,8},{4,12},{8,0},{12,4},{16,24},{20,28},{24,16},{28,20},{1,9},{5... | collective-permute-start | bytes 49160 | tf_op jit(solution)/shard_map/ppermute | solution.py:416
  16.5 1.7 %collective-permute-done.4.refs_2_ = f32[8,512]{1,0:T(8,128)S(1)} collective-permute-done((f32[8,512]{1,0:T(8,128)S(1)}, f32[8,512]{1,0:T(8,128)S(1)}, u32[]{:S(2)}, u32[]{:S(2)}) %collective-permute-start.4) | collective-permute-done | bytes 16416 | tf_op jit(solution)/shard_map/ppermute | solution.py:416
  18.8 8.2 %collective-permute-done.refs_0_.refs_1_ = bf16[512,1024]{1,0:T(8,128)(2,1)S(1)} collective-permute-done((bf16[512,1024]{1,0:T(8,128)(2,1)}, bf16[512,1024]{1,0:T(8,128)(2,1)S(1)}, u32[]{:S(2)}, u32[]{:S(2)}) %collective-permute-start) | collective-permute-done | bytes 1048608 | tf_op jit(solution)/shard_map/ppermute | solution.py:413
  28.0 1.1 %collective-permute-done.7.refs_1_ = bf16[512,256]{1,0:T(8,128)(2,1)S(1)} collective-permute-done((bf16[512,256]{1,0:T(8,128)(2,1)S(1)}, bf16[512,256]{1,0:T(8,128)(2,1)S(1)}, u32[]{:S(2)}, u32[]{:S(2)}) %collective-permute-start.7) | collective-permute-done | bytes 262176 | tf_op jit(solution)/shard_map/ppermute | solution.py:413
  29.7 1.8 %collective-permute-start.12 = (bf16[128,512]{1,0:T(8,128)(2,1)S(1)}, bf16[128,512]{1,0:T(8,128)(2,1)S(1)}, u32[]{:S(2)}, u32[]{:S(2)}) collective-permute-start(bf16[128,512]{1,0:T(8,128)(2,1)S(1)} %get-tuple-element.72.refs_0_), channel_id=1, source_target_pairs={{0,4},{4,0},{8,12},{12,8},{16,20},{20,16},{24,28},{28,24},{1,5},{5... | collective-permute-start | bytes 393224 | tf_op jit(solution)/shard_map/ppermute | solution.py:416
  31.4 1.1 %shard_map.79 = (f32[512,512]{1,0:T(8,128)S(1)}, f32[512,24]{1,0:T(8,128)S(1)}) custom-call(s32[1]{0:T(128)} %bitcast.refs_0_, bf16[512,1024]{1,0:T(8,128)(2,1)S(1)} %collective-permute-done.refs_0_.refs_1_, bf16[2,1024,512]{2,1,0:T(8,128)(2,1)S(1)} %get-tuple-element.45.refs_2_.refs_5_, ...), custom_call_target="tpu_custom_call", output_to_operand_aliasing={{0}: (4, {}), {1}: (5, {})} | custom-call | flops 562036736 | bytes 5537796 | tf_op jit(solution)/shard_map/pallas_call | solution.py:41
  33.7 1.6 %collective-permute-done.12.refs_1_.refs_16_ = bf16[128,512]{1,0:T(8,128)(2,1)S(1)} collective-permute-done((bf16[128,512]{1,0:T(8,128)(2,1)S(1)}, bf16[128,512]{1,0:T(8,128)(2,1)S(1)}, u32[]{:S(2)}, u32[]{:S(2)}) %collective-permute-start.12) | collective-permute-done | bytes 131104 | tf_op jit(solution)/shard_map/ppermute | solution.py:416
  35.3 1.9 %collective-permute-start.13 = (bf16[128,512]{1,0:T(8,128)(2,1)S(1)}, bf16[128,512]{1,0:T(8,128)(2,1)S(1)}, u32[]{:S(2)}, u32[]{:S(2)}) collective-permute-start(bf16[128,512]{1,0:T(8,128)(2,1)S(1)} %shard_map.81.refs_0_), channel_id=1, source_target_pairs={{0,8},{4,12},{8,0},{12,4},{16,24},{20,28},{24,16},{28,20},{1,9},{5... | collective-permute-start | bytes 393224 | tf_op jit(solution)/shard_map/ppermute | solution.py:416
  37.2 3.2 %collective-permute-done.13.refs_17_.refs_1_ = bf16[128,512]{1,0:T(8,128)(2,1)S(1)} collective-permute-done((bf16[128,512]{1,0:T(8,128)(2,1)S(1)}, bf16[128,512]{1,0:T(8,128)(2,1)S(1)}, u32[]{:S(2)}, u32[]{:S(2)}) %collective-permute-start.13) | collective-permute-done | bytes 131104 | tf_op jit(solution)/shard_map/ppermute | solution.py:416
  40.4 2.9 %collective-permute-start.14 = (bf16[128,512]{1,0:T(8,128)(2,1)S(1)}, bf16[128,512]{1,0:T(8,128)(2,1)S(1)}, u32[]{:S(2)}, u32[]{:S(2)}) collective-permute-start(bf16[128,512]{1,0:T(8,128)(2,1)S(1)} %shard_map.83), channel_id=1, source_target_pairs={{0,16},{4,20},{8,24},{12,28},{16,0},{20,4},{24,8},{28,12},{1,17},{... | collective-permute-start | bytes 393224 | tf_op jit(solution)/shard_map/ppermute | solution.py:416
  43.3 4.0 %shard_map.82 = (f32[512,512]{1,0:T(8,128)S(1)}, bf16[512,512]{1,0:T(8,128)(2,1)S(1)}, bf16[512,512]{1,0:T(8,128)(2,1)}, f32[512,24]{1,0:T(8,128)}) custom-call(s32[1]{0:T(128)} %bitcast.refs_0_, bf16[512,256]{1,0:T(8,128)(2,1)S(1)} %collective-permute-done.8.refs_1_, bf16[512,256]{1,0:T(8,128)(2,1)S(1)} %collective-permute-done.9.refs_2_, ...), custom_call_target="tpu_custom_call" | custom-call | flops 1073741824 | bytes 7176196 | tf_op jit(solution)/shard_map/pallas_call | solution.py:41
  50.1 1.7 %collective-permute-start.24 = (bf16[128,1024]{1,0:T(8,128)(2,1)S(1)}, bf16[128,1024]{1,0:T(8,128)(2,1)S(1)}, u32[]{:S(2)}, u32[]{:S(2)}) collective-permute-start(bf16[128,1024]{1,0:T(8,128)(2,1)S(1)} %shard_map.91), channel_id=1, source_target_pairs={{0,2},{1,3},{2,0},{3,1},{4,6},{5,7},{6,4},{7,5},{8,10},{9,11},{10,... | collective-permute-start | bytes 786440 | tf_op jit(solution)/shard_map/ppermute | solution.py:413
  53.2 1.6 %collective-permute-start.22 = (bf16[128,1024]{1,0:T(8,128)(2,1)S(1)}, bf16[128,1024]{1,0:T(8,128)(2,1)S(1)}, u32[]{:S(2)}, u32[]{:S(2)}) collective-permute-start(bf16[128,1024]{1,0:T(8,128)(2,1)S(1)} %shard_map.89), channel_id=1, source_target_pairs={{0,2},{1,3},{2,0},{3,1},{4,6},{5,7},{6,4},{7,5},{8,10},{9,11},{10,... | collective-permute-start | bytes 786440 | tf_op jit(solution)/shard_map/ppermute | solution.py:413
  55.4 0.7 collective-permute-done.18.refs_7_.refs_1_
  57.6 1.6 %collective-permute-start.20 = (bf16[64,1024]{1,0:T(8,128)(2,1)S(1)}, bf16[64,1024]{1,0:T(8,128)(2,1)S(1)}, u32[]{:S(2)}, u32[]{:S(2)}) collective-permute-start(bf16[64,1024]{1,0:T(8,128)(2,1)S(1)} %shard_map.86.refs_12_), channel_id=1, source_target_pairs={{0,2},{1,3},{2,0},{3,1},{4,6},{5,7},{6,4},{7,5},{8,10},{9,11},{10,... | collective-permute-start | bytes 393224 | tf_op jit(solution)/shard_map/ppermute | solution.py:413
  59.3 1.7 %shard_map.87.h_ref = f32[512,1024]{1,0:T(8,128)S(1)} custom-call(bf16[128,512]{1,0:T(8,128)(2,1)S(1)} %shard_map.84.refs_3_.refs_0_, bf16[128,512]{1,0:T(8,128)(2,1)S(1)} %collective-permute-done.15.refs_1_, bf16[128,512]{1,0:T(8,128)(2,1)S(1)} %get-tuple-element.79.refs_2_.refs_0_, bf16[128,512]{1,0:T(8,128)(2,1)S(1)} %collective-permute-done.16.refs_3_.refs_1_, ...), custom_call_target="tpu_custom_call" | custom-call | tf_op jit(solution)/shard_map/pallas_call | solution.py:41
  61.7 3.2 %collective-permute-done.23.a_ref = bf16[128,1024]{1,0:T(8,128)(2,1)S(1)} collective-permute-done((bf16[128,1024]{1,0:T(8,128)(2,1)S(1)}, bf16[128,1024]{1,0:T(8,128)(2,1)S(1)}, u32[]{:S(2)}, u32[]{:S(2)}) %collective-permute-start.23) | collective-permute-done | bytes 262176 | tf_op jit(solution)/shard_map/ppermute | solution.py:413
  65.7 4.9 %collective-permute-done.22.a_ref = bf16[128,1024]{1,0:T(8,128)(2,1)S(1)} collective-permute-done((bf16[128,1024]{1,0:T(8,128)(2,1)S(1)}, bf16[128,1024]{1,0:T(8,128)(2,1)S(1)}, u32[]{:S(2)}, u32[]{:S(2)}) %collective-permute-start.22) | collective-permute-done | bytes 262176 | tf_op jit(solution)/shard_map/ppermute | solution.py:413
  71.3 2.1 %collective-permute-done.21.a_ref = bf16[64,1024]{1,0:T(8,128)(2,1)S(1)} collective-permute-done((bf16[64,1024]{1,0:T(8,128)(2,1)S(1)}, bf16[64,1024]{1,0:T(8,128)(2,1)S(1)}, u32[]{:S(2)}, u32[]{:S(2)}) %collective-permute-start.21) | collective-permute-done | bytes 131104 | tf_op jit(solution)/shard_map/ppermute | solution.py:413
  74.0 1.5 %collective-permute-done.20.a_ref = bf16[64,1024]{1,0:T(8,128)(2,1)S(1)} collective-permute-done((bf16[64,1024]{1,0:T(8,128)(2,1)S(1)}, bf16[64,1024]{1,0:T(8,128)(2,1)S(1)}, u32[]{:S(2)}, u32[]{:S(2)}) %collective-permute-start.20) | collective-permute-done | bytes 131104 | tf_op jit(solution)/shard_map/ppermute | solution.py:413
  (52 shorter events, 15.3 us)
Async XLA Ops:
  0.0 3.0 %collective-permute-start.1 = (bf16[512,1024]{1,0:T(8,128)(2,1)}, bf16[512,1024]{1,0:T(8,128)(2,1)S(1)}, u32[]{:S(2)}, u32[]{:S(2)}) collective-permute-start(bf16[512,1024]{1,0:T(8,128)(2,1)} %refs_2_.1), channel_id=1, source_target_pairs={{0,1},{1,0},{2,3},{3,2},{4,5},{5,4},{6,7},{7,6},{8,9},{9,8},{10,11... | collective-permute-start | bytes 3145736 | tf_op jit(solution)/shard_map/ppermute | solution.py:413
  0.5 26.6 %collective-permute-start = (bf16[512,1024]{1,0:T(8,128)(2,1)}, bf16[512,1024]{1,0:T(8,128)(2,1)S(1)}, u32[]{:S(2)}, u32[]{:S(2)}) collective-permute-start(bf16[512,1024]{1,0:T(8,128)(2,1)} %refs_2_.1), channel_id=1, source_target_pairs={{0,2},{1,3},{2,0},{3,1},{4,6},{5,7},{6,4},{7,5},{8,10},{9,11},{10,... | collective-permute-start | bytes 3145736 | tf_op jit(solution)/shard_map/ppermute | solution.py:413
  9.0 18.0 %collective-permute-start.5 = (bf16[512,1024]{1,0:T(8,128)(2,1)S(1)}, bf16[512,1024]{1,0:T(8,128)(2,1)S(1)}, u32[]{:S(2)}, u32[]{:S(2)}) collective-permute-start(bf16[512,1024]{1,0:T(8,128)(2,1)S(1)} %get-tuple-element.56), channel_id=1, source_target_pairs={{0,1},{1,0},{2,3},{3,2},{4,5},{5,4},{6,7},{7,6},{8,9},{9,8},{10,11... | collective-permute-start | bytes 3145736 | tf_op jit(solution)/shard_map/ppermute | solution.py:413
  9.5 17.6 %collective-permute-start.6 = (bf16[512,1024]{1,0:T(8,128)(2,1)S(1)}, bf16[512,1024]{1,0:T(8,128)(2,1)S(1)}, u32[]{:S(2)}, u32[]{:S(2)}) collective-permute-start(bf16[512,1024]{1,0:T(8,128)(2,1)S(1)} %get-tuple-element.57), channel_id=1, source_target_pairs={{0,1},{1,0},{2,3},{3,2},{4,5},{5,4},{6,7},{7,6},{8,9},{9,8},{10,11... | collective-permute-start | bytes 3145736 | tf_op jit(solution)/shard_map/ppermute | solution.py:413
  9.6 17.4 %collective-permute-start.2 = (bf16[1024,256]{1,0:T(8,128)(2,1)S(1)}, bf16[1024,256]{1,0:T(8,128)(2,1)S(1)}, u32[]{:S(2)}, u32[]{:S(2)}) collective-permute-start(bf16[1024,256]{1,0:T(8,128)(2,1)S(1)} %get-tuple-element.51), channel_id=1, source_target_pairs={{0,1},{1,0},{2,3},{3,2},{4,5},{5,4},{6,7},{7,6},{8,9},{9,8},{10,11... | collective-permute-start | bytes 1572872 | tf_op jit(solution)/shard_map/ppermute | solution.py:413
  10.0 4.3 %collective-permute-start.3 = (f32[8,512]{1,0:T(8,128)S(1)}, f32[8,512]{1,0:T(8,128)S(1)}, u32[]{:S(2)}, u32[]{:S(2)}) collective-permute-start(f32[8,512]{1,0:T(8,128)S(1)} %get-tuple-element.52.refs_1_), channel_id=1, source_target_pairs={{0,4},{4,0},{8,12},{12,8},{16,20},{20,16},{24,28},{28,24},{1,5},{5... | collective-permute-start | bytes 49160 | tf_op jit(solution)/shard_map/ppermute | solution.py:416
  14.3 3.9 %collective-permute-start.4 = (f32[8,512]{1,0:T(8,128)S(1)}, f32[8,512]{1,0:T(8,128)S(1)}, u32[]{:S(2)}, u32[]{:S(2)}) collective-permute-start(f32[8,512]{1,0:T(8,128)S(1)} %get-tuple-element.53.refs_1_), channel_id=1, source_target_pairs={{0,8},{4,12},{8,0},{12,4},{16,24},{20,28},{24,16},{28,20},{1,9},{5... | collective-permute-start | bytes 49160 | tf_op jit(solution)/shard_map/ppermute | solution.py:416
  27.5 1.6 %collective-permute-start.7 = (bf16[512,256]{1,0:T(8,128)(2,1)S(1)}, bf16[512,256]{1,0:T(8,128)(2,1)S(1)}, u32[]{:S(2)}, u32[]{:S(2)}) collective-permute-start(bf16[512,256]{1,0:T(8,128)(2,1)S(1)} %shard_map.76.refs_3_), channel_id=1, source_target_pairs={{0,1},{1,0},{2,3},{3,2},{4,5},{5,4},{6,7},{7,6},{8,9},{9,8},{10,11... | collective-permute-start | bytes 786440 | tf_op jit(solution)/shard_map/ppermute | solution.py:413
  29.7 5.6 %collective-permute-start.12 = (bf16[128,512]{1,0:T(8,128)(2,1)S(1)}, bf16[128,512]{1,0:T(8,128)(2,1)S(1)}, u32[]{:S(2)}, u32[]{:S(2)}) collective-permute-start(bf16[128,512]{1,0:T(8,128)(2,1)S(1)} %get-tuple-element.72.refs_0_), channel_id=1, source_target_pairs={{0,4},{4,0},{8,12},{12,8},{16,20},{20,16},{24,28},{28,24},{1,5},{5... | collective-permute-start | bytes 393224 | tf_op jit(solution)/shard_map/ppermute | solution.py:416
  32.6 10.7 %collective-permute-start.8 = (bf16[512,256]{1,0:T(8,128)(2,1)S(1)}, bf16[512,256]{1,0:T(8,128)(2,1)S(1)}, u32[]{:S(2)}, u32[]{:S(2)}) collective-permute-start(bf16[512,256]{1,0:T(8,128)(2,1)S(1)} %get-tuple-element.61), channel_id=1, source_target_pairs={{0,1},{1,0},{2,3},{3,2},{4,5},{5,4},{6,7},{7,6},{8,9},{9,8},{10,11... | collective-permute-start | bytes 786440 | tf_op jit(solution)/shard_map/ppermute | solution.py:413
  32.7 10.6 %collective-permute-start.9 = (bf16[512,256]{1,0:T(8,128)(2,1)S(1)}, bf16[512,256]{1,0:T(8,128)(2,1)S(1)}, u32[]{:S(2)}, u32[]{:S(2)}) collective-permute-start(bf16[512,256]{1,0:T(8,128)(2,1)S(1)} %get-tuple-element.62), channel_id=1, source_target_pairs={{0,1},{1,0},{2,3},{3,2},{4,5},{5,4},{6,7},{7,6},{8,9},{9,8},{10,11... | collective-permute-start | bytes 786440 | tf_op jit(solution)/shard_map/ppermute | solution.py:413
  33.2 10.1 %collective-permute-start.10 = (bf16[512,256]{1,0:T(8,128)(2,1)S(1)}, bf16[512,256]{1,0:T(8,128)(2,1)S(1)}, u32[]{:S(2)}, u32[]{:S(2)}) collective-permute-start(bf16[512,256]{1,0:T(8,128)(2,1)S(1)} %get-tuple-element.63), channel_id=1, source_target_pairs={{0,1},{1,0},{2,3},{3,2},{4,5},{5,4},{6,7},{7,6},{8,9},{9,8},{10,11... | collective-permute-start | bytes 786440 | tf_op jit(solution)/shard_map/ppermute | solution.py:413
  33.2 10.0 %collective-permute-start.11 = (bf16[512,256]{1,0:T(8,128)(2,1)S(1)}, bf16[512,256]{1,0:T(8,128)(2,1)S(1)}, u32[]{:S(2)}, u32[]{:S(2)}) collective-permute-start(bf16[512,256]{1,0:T(8,128)(2,1)S(1)} %get-tuple-element.64), channel_id=1, source_target_pairs={{0,1},{1,0},{2,3},{3,2},{4,5},{5,4},{6,7},{7,6},{8,9},{9,8},{10,11... | collective-permute-start | bytes 786440 | tf_op jit(solution)/shard_map/ppermute | solution.py:413
  35.3 5.0 %collective-permute-start.13 = (bf16[128,512]{1,0:T(8,128)(2,1)S(1)}, bf16[128,512]{1,0:T(8,128)(2,1)S(1)}, u32[]{:S(2)}, u32[]{:S(2)}) collective-permute-start(bf16[128,512]{1,0:T(8,128)(2,1)S(1)} %shard_map.81.refs_0_), channel_id=1, source_target_pairs={{0,8},{4,12},{8,0},{12,4},{16,24},{20,28},{24,16},{28,20},{1,9},{5... | collective-permute-start | bytes 393224 | tf_op jit(solution)/shard_map/ppermute | solution.py:416
  40.4 7.5 %collective-permute-start.14 = (bf16[128,512]{1,0:T(8,128)(2,1)S(1)}, bf16[128,512]{1,0:T(8,128)(2,1)S(1)}, u32[]{:S(2)}, u32[]{:S(2)}) collective-permute-start(bf16[128,512]{1,0:T(8,128)(2,1)S(1)} %shard_map.83), channel_id=1, source_target_pairs={{0,16},{4,20},{8,24},{12,28},{16,0},{20,4},{24,8},{28,12},{1,17},{... | collective-permute-start | bytes 393224 | tf_op jit(solution)/shard_map/ppermute | solution.py:416
  48.2 1.4 %collective-permute-start.15 = (bf16[128,512]{1,0:T(8,128)(2,1)S(1)}, bf16[128,512]{1,0:T(8,128)(2,1)S(1)}, u32[]{:S(2)}, u32[]{:S(2)}) collective-permute-start(bf16[128,512]{1,0:T(8,128)(2,1)S(1)} %shard_map.84.refs_3_.refs_0_), channel_id=1, source_target_pairs={{0,1},{1,0},{2,3},{3,2},{4,5},{5,4},{6,7},{7,6},{8,9},{9,8},{10,11... | collective-permute-start | bytes 393224 | tf_op jit(solution)/shard_map/ppermute | solution.py:413
  48.9 2.9 %collective-permute-start.16 = (bf16[128,512]{1,0:T(8,128)(2,1)S(1)}, bf16[128,512]{1,0:T(8,128)(2,1)S(1)}, u32[]{:S(2)}, u32[]{:S(2)}) collective-permute-start(bf16[128,512]{1,0:T(8,128)(2,1)S(1)} %get-tuple-element.79.refs_2_.refs_0_), channel_id=1, source_target_pairs={{0,1},{1,0},{2,3},{3,2},{4,5},{5,4},{6,7},{7,6},{8,9},{9,8},{10,11... | collective-permute-start | bytes 393224 | tf_op jit(solution)/shard_map/ppermute | solution.py:413
  49.4 3.3 %collective-permute-start.17 = (bf16[128,512]{1,0:T(8,128)(2,1)S(1)}, bf16[128,512]{1,0:T(8,128)(2,1)S(1)}, u32[]{:S(2)}, u32[]{:S(2)}) collective-permute-start(bf16[128,512]{1,0:T(8,128)(2,1)S(1)} %get-tuple-element.80.refs_4_.refs_0_), channel_id=1, source_target_pairs={{0,1},{1,0},{2,3},{3,2},{4,5},{5,4},{6,7},{7,6},{8,9},{9,8},{10,11... | collective-permute-start | bytes 393224 | tf_op jit(solution)/shard_map/ppermute | solution.py:413
  50.1 10.8 %collective-permute-start.24 = (bf16[128,1024]{1,0:T(8,128)(2,1)S(1)}, bf16[128,1024]{1,0:T(8,128)(2,1)S(1)}, u32[]{:S(2)}, u32[]{:S(2)}) collective-permute-start(bf16[128,1024]{1,0:T(8,128)(2,1)S(1)} %shard_map.91), channel_id=1, source_target_pairs={{0,2},{1,3},{2,0},{3,1},{4,6},{5,7},{6,4},{7,5},{8,10},{9,11},{10,... | collective-permute-start | bytes 786440 | tf_op jit(solution)/shard_map/ppermute | solution.py:413
  52.2 12.7 %collective-permute-start.23 = (bf16[128,1024]{1,0:T(8,128)(2,1)S(1)}, bf16[128,1024]{1,0:T(8,128)(2,1)S(1)}, u32[]{:S(2)}, u32[]{:S(2)}) collective-permute-start(bf16[128,1024]{1,0:T(8,128)(2,1)S(1)} %shard_map.90), channel_id=1, source_target_pairs={{0,2},{1,3},{2,0},{3,1},{4,6},{5,7},{6,4},{7,5},{8,10},{9,11},{10,... | collective-permute-start | bytes 786440 | tf_op jit(solution)/shard_map/ppermute | solution.py:413
  53.2 17.3 %collective-permute-start.22 = (bf16[128,1024]{1,0:T(8,128)(2,1)S(1)}, bf16[128,1024]{1,0:T(8,128)(2,1)S(1)}, u32[]{:S(2)}, u32[]{:S(2)}) collective-permute-start(bf16[128,1024]{1,0:T(8,128)(2,1)S(1)} %shard_map.89), channel_id=1, source_target_pairs={{0,2},{1,3},{2,0},{3,1},{4,6},{5,7},{6,4},{7,5},{8,10},{9,11},{10,... | collective-permute-start | bytes 786440 | tf_op jit(solution)/shard_map/ppermute | solution.py:413
  54.9 2.3 %collective-permute-start.19 = (bf16[64,512]{1,0:T(8,128)(2,1)S(1)}, bf16[64,512]{1,0:T(8,128)(2,1)S(1)}, u32[]{:S(2)}, u32[]{:S(2)}) collective-permute-start(bf16[64,512]{1,0:T(8,128)(2,1)S(1)} %get-tuple-element.82.refs_0_.refs_8_), channel_id=1, source_target_pairs={{0,1},{1,0},{2,3},{3,2},{4,5},{5,4},{6,7},{7,6},{8,9},{9,8},{10,11... | collective-permute-start | bytes 196616 | tf_op jit(solution)/shard_map/ppermute | solution.py:413
  56.6 16.7 %collective-permute-start.21 = (bf16[64,1024]{1,0:T(8,128)(2,1)S(1)}, bf16[64,1024]{1,0:T(8,128)(2,1)S(1)}, u32[]{:S(2)}, u32[]{:S(2)}) collective-permute-start(bf16[64,1024]{1,0:T(8,128)(2,1)S(1)} %shard_map.88), channel_id=1, source_target_pairs={{0,2},{1,3},{2,0},{3,1},{4,6},{5,7},{6,4},{7,5},{8,10},{9,11},{10,... | collective-permute-start | bytes 393224 | tf_op jit(solution)/shard_map/ppermute | solution.py:413
  57.6 17.9 %collective-permute-start.20 = (bf16[64,1024]{1,0:T(8,128)(2,1)S(1)}, bf16[64,1024]{1,0:T(8,128)(2,1)S(1)}, u32[]{:S(2)}, u32[]{:S(2)}) collective-permute-start(bf16[64,1024]{1,0:T(8,128)(2,1)S(1)} %shard_map.86.refs_12_), channel_id=1, source_target_pairs={{0,2},{1,3},{2,0},{3,1},{4,6},{5,7},{6,4},{7,5},{8,10},{9,11},{10,... | collective-permute-start | bytes 393224 | tf_op jit(solution)/shard_map/ppermute | solution.py:413
  (2 other events, 2.0 us)

commit v16 on v12

--- a/solution.py
+++ b/solution.py
@@ -416,8 +416,8 @@
     def swap_tp(x, bit):
         return lax.ppermute(x, "tp", [(i, i ^ bit) for i in range(4)])
 
-    def swap_seq(x, bit):
-        return lax.ppermute(x, "seq", [(i, i ^ bit) for i in range(seq_size)])
+    def swap_seq(x, bit, both=True):
+        return lax.ppermute(x, "seq", [(i, i ^ bit) for i in range(seq_size) if both or not i & bit])
 
     far = swap_tp(tokens, 2)
     near = swap_tp(tokens, 1)
@@ -448,7 +448,7 @@
     locals_ = [attend(q, level, k, v, dcol, drow, i, head_size, level_count) for i in range(2)]
     earlier = []
     for b in range(seq_bits):
-        others = [swap_seq(state, 1 << b) for state in states]
+        others = [swap_seq(state, 1 << b, b < seq_bits - 1 or i == 0) for i, state in enumerate(states)]
         earlier.append(others)
         if b < seq_bits - 1:
             afters = (locals_[b : b + 1], ())

time: 77.1 us -> 77.3 us (level)
  starting transfers between devices: 27.1 us -> 29.2 us
  waiting for transfers between devices: 27 us -> 25.1 us
    ppermute x8, starting transfers between devices: 15.2 us -> 17.2 us  [swap_seq(): lax.ppermute(x, 'seq', [(i, i ^ bit) for i in range(seq_size) if both or...]
    ppermute x8, waiting for transfers between devices: 5.57 us -> 3.69 us  [swap_seq(): lax.ppermute(x, 'seq', [(i, i ^ bit) for i in range(seq_size) if both or...]
  transfers between devices with their start and end apart: 27 -> 27, of which waited for: 14 -> 12; matrix products, arithmetic and copies ran while one was open for 0% -> 0% of each run, Pallas kernels for 27% -> 27%
where the time goes in v16:
time: 77.3 us; the launch traced here: 77.1 us
  starting transfers between devices  29.2 us (38%)
  waiting for transfers between devices  25.1 us (32%)
  Pallas kernels  21.9 us (28%)
    ppermute x19, waiting for transfers between devices, swap_tp(): return lax.ppermute(x, 'tp', [(i, i ^ bit) for i in range(4)])  21.4 us
    pallas_call x22, Pallas kernels, call(): pl.pallas_call(run, in_specs=[SMEM] * smem + [HBM] * hbm + [VMEM] * (coun...  18.4 us
    ppermute x8, starting transfers between devices, swap_seq(): lax.ppermute(x, 'seq', [(i, i ^ bit) for i in range(seq_size) if both or...  17.2 us
    ppermute x19, starting transfers between devices, swap_tp(): return lax.ppermute(x, 'tp', [(i, i ^ bit) for i in range(4)])  12 us
    ppermute x8, waiting for transfers between devices, swap_seq(): lax.ppermute(x, 'seq', [(i, i ^ bit) for i in range(seq_size) if both or...  3.69 us
    pallas_call x5, Pallas kernels, add_rows(): pl.pallas_call(kernel, grid=(rows // unit,), in_specs=specs, out_specs=pl...  3.54 us
  transfers between devices with their start and end apart: 27, of which 12 were waited for; matrix products, arithmetic and copies ran while one was open for 0% of the time, Pallas kernels for 27%

profile of v16, /device:TPU:0, one launch (start us, length us, event | category | flops | bytes accessed | tf_op | source)
XLA Modules:
  0.0 77.1 jit_solution(10010276790557333574)
XLA Ops:
  0.5 2.5 %collective-permute-start = (bf16[512,1024]{1,0:T(8,128)(2,1)}, bf16[512,1024]{1,0:T(8,128)(2,1)S(1)}, u32[]{:S(2)}, u32[]{:S(2)}) collective-permute-start(bf16[512,1024]{1,0:T(8,128)(2,1)} %refs_2_.1), channel_id=1, source_target_pairs={{0,2},{1,3},{2,0},{3,1},{4,6},{5,7},{6,4},{7,5},{8,10},{9,11},{10,... | collective-permute-start | bytes 3145736 | tf_op jit(solution)/shard_map/ppermute | solution.py:417
  3.7 5.4 %shard_map.73 = (f32[512,512]{1,0:T(8,128)S(1)}, f32[512,256]{1,0:T(8,128)S(1)}, f32[512,24]{1,0:T(8,128)S(1)}, bf16[2,1024,512]{2,1,0:T(8,128)(2,1)S(1)}, bf16[...) custom-call(s32[1]{0:T(128)} %bitcast.refs_0_, ...), custom_call_target="tpu_custom_call" | custom-call | tf_op jit(solution)/shard_map/pallas_call | solution.py:41
  10.0 2.6 %collective-permute-start.3 = (f32[8,512]{1,0:T(8,128)S(1)}, f32[8,512]{1,0:T(8,128)S(1)}, u32[]{:S(2)}, u32[]{:S(2)}) collective-permute-start(f32[8,512]{1,0:T(8,128)S(1)} %get-tuple-element.57.refs_1_), channel_id=1, source_target_pairs={{0,4},{4,0},{8,12},{12,8},{16,20},{20,16},{24,28},{28,24},{1,5},{5... | collective-permute-start | bytes 49160 | tf_op jit(solution)/shard_map/ppermute | solution.py:420
  12.6 1.7 %collective-permute-done.3.refs_2_ = f32[8,512]{1,0:T(8,128)S(1)} collective-permute-done((f32[8,512]{1,0:T(8,128)S(1)}, f32[8,512]{1,0:T(8,128)S(1)}, u32[]{:S(2)}, u32[]{:S(2)}) %collective-permute-start.3) | collective-permute-done | bytes 16416 | tf_op jit(solution)/shard_map/ppermute | solution.py:420
  14.3 2.2 %collective-permute-start.4 = (f32[8,512]{1,0:T(8,128)S(1)}, f32[8,512]{1,0:T(8,128)S(1)}, u32[]{:S(2)}, u32[]{:S(2)}) collective-permute-start(f32[8,512]{1,0:T(8,128)S(1)} %get-tuple-element.58.refs_1_), channel_id=1, source_target_pairs={{0,8},{4,12},{8,0},{12,4},{16,24},{20,28},{24,16},{28,20},{1,9},{5... | collective-permute-start | bytes 49160 | tf_op jit(solution)/shard_map/ppermute | solution.py:420
  16.5 1.7 %collective-permute-done.4.refs_2_ = f32[8,512]{1,0:T(8,128)S(1)} collective-permute-done((f32[8,512]{1,0:T(8,128)S(1)}, f32[8,512]{1,0:T(8,128)S(1)}, u32[]{:S(2)}, u32[]{:S(2)}) %collective-permute-start.4) | collective-permute-done | bytes 16416 | tf_op jit(solution)/shard_map/ppermute | solution.py:420
  18.8 8.2 %collective-permute-done.refs_0_.refs_1_ = bf16[512,1024]{1,0:T(8,128)(2,1)S(1)} collective-permute-done((bf16[512,1024]{1,0:T(8,128)(2,1)}, bf16[512,1024]{1,0:T(8,128)(2,1)S(1)}, u32[]{:S(2)}, u32[]{:S(2)}) %collective-permute-start) | collective-permute-done | bytes 1048608 | tf_op jit(solution)/shard_map/ppermute | solution.py:417
  27.6 1.3 %shard_map.77 = (f32[512,512]{1,0:T(8,128)S(1)}, f32[512,256]{1,0:T(8,128)S(1)}, f32[512,24]{1,0:T(8,128)S(1)}) custom-call(s32[1]{0:T(128)} %bitcast.refs_0_, bf16[512,1024]{1,0:T(8,128)(2,1)S(1)} %collective-permute-done.refs_0_.refs_1_, ...), custom_call_target="tpu_custom_call", output_to_operand_aliasing={{0}: (5, {}), {1}: (6, {}), {2}: (7, {})} | custom-call | tf_op jit(solution)/shard_map/pallas_call | solution.py:41
  30.1 1.8 %collective-permute-start.9 = (bf16[128,256]{1,0:T(8,128)(2,1)S(1)}, bf16[128,256]{1,0:T(8,128)(2,1)S(1)}, u32[]{:S(2)}, u32[]{:S(2)}) collective-permute-start(bf16[128,256]{1,0:T(8,128)(2,1)S(1)} %get-tuple-element.76.refs_0_), channel_id=1, source_target_pairs={{0,4},{4,0},{8,12},{12,8},{16,20},{20,16},{24,28},{28,24},{1,5},{5... | collective-permute-start | bytes 196616 | tf_op jit(solution)/shard_map/ppermute | solution.py:420
  33.2 1.3 %shard_map.81.refs_4_.refs_0_ = f32[512,256]{1,0:T(8,128)S(1)} custom-call(bf16[512,512]{1,0:T(8,128)(2,1)S(1)} %get-tuple-element.65.refs_0_.refs_2_, f32[512,24]{1,0:T(8,128)S(1)} %get-tuple-element.66.refs_1_.refs_3_, bf16[512,128]{1,0:T(8,128)(2,1)S(1)} %get-tuple-element.69.refs_2_, bf16[512,128]{1,0:T(8,128)(2,1)S(1)} %get-tuple-element.70.refs_3_, ...), custom_call_target="tpu_custom_call" | custom-call | tf_op jit(solution)/shard_map/pallas_call | solution.py:41
  34.6 2.1 %collective-permute-start.11 = (bf16[128,256]{1,0:T(8,128)(2,1)S(1)}, bf16[128,256]{1,0:T(8,128)(2,1)S(1)}, u32[]{:S(2)}, u32[]{:S(2)}) collective-permute-start(bf16[128,256]{1,0:T(8,128)(2,1)S(1)} %shard_map.83.refs_0_), channel_id=1, source_target_pairs={{0,8},{4,12},{8,0},{12,4},{16,24},{20,28},{24,16},{28,20},{1,9},{5... | collective-permute-start | bytes 196616 | tf_op jit(solution)/shard_map/ppermute | solution.py:420
  36.8 1.0 %collective-permute-start.12 = (bf16[128,256]{1,0:T(8,128)(2,1)S(1)}, bf16[128,256]{1,0:T(8,128)(2,1)S(1)}, u32[]{:S(2)}, u32[]{:S(2)}) collective-permute-start(bf16[128,256]{1,0:T(8,128)(2,1)S(1)} %shard_map.84.refs_0_), channel_id=1, source_target_pairs={{0,8},{4,12},{8,0},{12,4},{16,24},{20,28},{24,16},{28,20},{1,9},{5... | collective-permute-start | bytes 196616 | tf_op jit(solution)/shard_map/ppermute | solution.py:420
  37.8 1.3 %shard_map.82.refs_1_.refs_4_ = f32[512,256]{1,0:T(8,128)S(1)} custom-call(bf16[512,512]{1,0:T(8,128)(2,1)S(1)} %get-tuple-element.65.refs_0_.refs_2_, f32[512,24]{1,0:T(8,128)S(1)} %get-tuple-element.66.refs_1_.refs_3_, bf16[512,128]{1,0:T(8,128)(2,1)S(1)} %get-tuple-element.69.refs_2_, bf16[512,128]{1,0:T(8,128)(2,1)S(1)} %get-tuple-element.70.refs_3_, ...), custom_call_target="tpu_custom_call" | custom-call | tf_op jit(solution)/shard_map/pallas_call | solution.py:41
  39.3 3.5 %collective-permute-start.13 = (bf16[128,256]{1,0:T(8,128)(2,1)S(1)}, bf16[128,256]{1,0:T(8,128)(2,1)S(1)}, u32[]{:S(2)}, u32[]{:S(2)}) collective-permute-start(bf16[128,256]{1,0:T(8,128)(2,1)S(1)} %shard_map.86), channel_id=1, source_target_pairs={{0,16},{4,20},{8,24},{12,28},{16,0},{20,4},{24,8},{28,12},{1,17},{... | collective-permute-start | bytes 196616 | tf_op jit(solution)/shard_map/ppermute | solution.py:420
  42.8 3.6 %collective-permute-start.16 = (bf16[128,256]{1,0:T(8,128)(2,1)S(1)}, bf16[128,256]{1,0:T(8,128)(2,1)S(1)}, u32[]{:S(2)}, u32[]{:S(2)}) collective-permute-start(bf16[128,256]{1,0:T(8,128)(2,1)S(1)} %shard_map.88), channel_id=1, source_target_pairs={{0,16},{4,20},{8,24},{12,28},{1,17},{5,21},{9,25},{13,29},{2,18},{... | collective-permute-start | bytes 196616 | tf_op jit(solution)/shard_map/ppermute | solution.py:420
  46.4 1.5 %shard_map.85 = (f32[512,256]{1,0:T(8,128)S(1)}, f32[512,256]{1,0:T(8,128)S(1)}, bf16[512,256]{1,0:T(8,128)(2,1)S(1)}, bf16[512,256]{1,0:T(8,128)(2,1)S(1)}) custom-call(f32[512,256]{1,0:T(8,128)S(1)} %shard_map.81.refs_4_.refs_0_, f32[512,256]{1,0:T(8,128)S(1)} %shard_map.82.refs_1_.refs_4_, bf16[512,512]{1,0:T(8,128)(2,1)S(1)} %get-tuple-element.65.refs_0_.refs_2_, ...), custom_call_target="tpu_custom_call" | custom-call | tf_op jit(solution)/shard_map/pallas_call | solution.py:41
  51.1 1.6 %collective-permute-start.25 = (bf16[128,1024]{1,0:T(8,128)(2,1)S(1)}, bf16[128,1024]{1,0:T(8,128)(2,1)S(1)}, u32[]{:S(2)}, u32[]{:S(2)}) collective-permute-start(bf16[128,1024]{1,0:T(8,128)(2,1)S(1)} %shard_map.94), channel_id=1, source_target_pairs={{0,2},{1,3},{2,0},{3,1},{4,6},{5,7},{6,4},{7,5},{8,10},{9,11},{10,... | collective-permute-start | bytes 786440 | tf_op jit(solution)/shard_map/ppermute | solution.py:417
  54.2 1.6 %collective-permute-start.24 = (bf16[128,1024]{1,0:T(8,128)(2,1)S(1)}, bf16[128,1024]{1,0:T(8,128)(2,1)S(1)}, u32[]{:S(2)}, u32[]{:S(2)}) collective-permute-start(bf16[128,1024]{1,0:T(8,128)(2,1)S(1)} %shard_map.93), channel_id=1, source_target_pairs={{0,2},{1,3},{2,0},{3,1},{4,6},{5,7},{6,4},{7,5},{8,10},{9,11},{10,... | collective-permute-start | bytes 786440 | tf_op jit(solution)/shard_map/ppermute | solution.py:417
  58.6 1.6 %collective-permute-start.22 = (bf16[64,1024]{1,0:T(8,128)(2,1)S(1)}, bf16[64,1024]{1,0:T(8,128)(2,1)S(1)}, u32[]{:S(2)}, u32[]{:S(2)}) collective-permute-start(bf16[64,1024]{1,0:T(8,128)(2,1)S(1)} %shard_map.90.refs_16_), channel_id=1, source_target_pairs={{0,2},{1,3},{2,0},{3,1},{4,6},{5,7},{6,4},{7,5},{8,10},{9,11},{10,... | collective-permute-start | bytes 393224 | tf_op jit(solution)/shard_map/ppermute | solution.py:417
  60.2 1.7 %shard_map.91.h_ref = f32[512,1024]{1,0:T(8,128)S(1)} custom-call(bf16[256,256]{1,0:T(8,128)(2,1)S(1)} %get-tuple-element.84.refs_3_.refs_0_, bf16[256,256]{1,0:T(8,128)(2,1)S(1)} %collective-permute-done.14.refs_1_, bf16[256,256]{1,0:T(8,128)(2,1)S(1)} %get-tuple-element.85.refs_4_.refs_0_.refs_2_, ...), custom_call_target="tpu_custom_call" | custom-call | tf_op jit(solution)/shard_map/pallas_call | solution.py:41
  61.9 4.1 %collective-permute-done.26.a_ref = bf16[128,1024]{1,0:T(8,128)(2,1)S(1)} collective-permute-done((bf16[128,1024]{1,0:T(8,128)(2,1)S(1)}, bf16[128,1024]{1,0:T(8,128)(2,1)S(1)}, u32[]{:S(2)}, u32[]{:S(2)}) %collective-permute-start.26) | collective-permute-done | bytes 262176 | tf_op jit(solution)/shard_map/ppermute | solution.py:417
  67.4 4.2 %collective-permute-done.24.a_ref = bf16[128,1024]{1,0:T(8,128)(2,1)S(1)} collective-permute-done((bf16[128,1024]{1,0:T(8,128)(2,1)S(1)}, bf16[128,1024]{1,0:T(8,128)(2,1)S(1)}, u32[]{:S(2)}, u32[]{:S(2)}) %collective-permute-start.24) | collective-permute-done | bytes 262176 | tf_op jit(solution)/shard_map/ppermute | solution.py:417
  72.3 2.1 %collective-permute-done.23.a_ref = bf16[64,1024]{1,0:T(8,128)(2,1)S(1)} collective-permute-done((bf16[64,1024]{1,0:T(8,128)(2,1)S(1)}, bf16[64,1024]{1,0:T(8,128)(2,1)S(1)}, u32[]{:S(2)}, u32[]{:S(2)}) %collective-permute-start.23) | collective-permute-done | bytes 131104 | tf_op jit(solution)/shard_map/ppermute | solution.py:417
  75.1 1.3 %collective-permute-done.22.a_ref = bf16[64,1024]{1,0:T(8,128)(2,1)S(1)} collective-permute-done((bf16[64,1024]{1,0:T(8,128)(2,1)S(1)}, bf16[64,1024]{1,0:T(8,128)(2,1)S(1)}, u32[]{:S(2)}, u32[]{:S(2)}) %collective-permute-start.22) | collective-permute-done | bytes 131104 | tf_op jit(solution)/shard_map/ppermute | solution.py:417
  (60 shorter events, 17.1 us)
Async XLA Ops:
  0.0 3.0 %collective-permute-start.1 = (bf16[512,1024]{1,0:T(8,128)(2,1)}, bf16[512,1024]{1,0:T(8,128)(2,1)S(1)}, u32[]{:S(2)}, u32[]{:S(2)}) collective-permute-start(bf16[512,1024]{1,0:T(8,128)(2,1)} %refs_2_.1), channel_id=1, source_target_pairs={{0,1},{1,0},{2,3},{3,2},{4,5},{5,4},{6,7},{7,6},{8,9},{9,8},{10,11... | collective-permute-start | bytes 3145736 | tf_op jit(solution)/shard_map/ppermute | solution.py:417
  0.5 26.6 %collective-permute-start = (bf16[512,1024]{1,0:T(8,128)(2,1)}, bf16[512,1024]{1,0:T(8,128)(2,1)S(1)}, u32[]{:S(2)}, u32[]{:S(2)}) collective-permute-start(bf16[512,1024]{1,0:T(8,128)(2,1)} %refs_2_.1), channel_id=1, source_target_pairs={{0,2},{1,3},{2,0},{3,1},{4,6},{5,7},{6,4},{7,5},{8,10},{9,11},{10,... | collective-permute-start | bytes 3145736 | tf_op jit(solution)/shard_map/ppermute | solution.py:417
  9.0 18.0 %collective-permute-start.5 = (bf16[512,1024]{1,0:T(8,128)(2,1)S(1)}, bf16[512,1024]{1,0:T(8,128)(2,1)S(1)}, u32[]{:S(2)}, u32[]{:S(2)}) collective-permute-start(bf16[512,1024]{1,0:T(8,128)(2,1)S(1)} %get-tuple-element.61), channel_id=1, source_target_pairs={{0,1},{1,0},{2,3},{3,2},{4,5},{5,4},{6,7},{7,6},{8,9},{9,8},{10,11... | collective-permute-start | bytes 3145736 | tf_op jit(solution)/shard_map/ppermute | solution.py:417
  9.5 17.6 %collective-permute-start.6 = (bf16[512,1024]{1,0:T(8,128)(2,1)S(1)}, bf16[512,1024]{1,0:T(8,128)(2,1)S(1)}, u32[]{:S(2)}, u32[]{:S(2)}) collective-permute-start(bf16[512,1024]{1,0:T(8,128)(2,1)S(1)} %get-tuple-element.62), channel_id=1, source_target_pairs={{0,1},{1,0},{2,3},{3,2},{4,5},{5,4},{6,7},{7,6},{8,9},{9,8},{10,11... | collective-permute-start | bytes 3145736 | tf_op jit(solution)/shard_map/ppermute | solution.py:417
  9.6 17.4 %collective-permute-start.2 = (bf16[1024,256]{1,0:T(8,128)(2,1)S(1)}, bf16[1024,256]{1,0:T(8,128)(2,1)S(1)}, u32[]{:S(2)}, u32[]{:S(2)}) collective-permute-start(bf16[1024,256]{1,0:T(8,128)(2,1)S(1)} %get-tuple-element.56), channel_id=1, source_target_pairs={{0,1},{1,0},{2,3},{3,2},{4,5},{5,4},{6,7},{7,6},{8,9},{9,8},{10,11... | collective-permute-start | bytes 1572872 | tf_op jit(solution)/shard_map/ppermute | solution.py:417
  10.0 4.3 %collective-permute-start.3 = (f32[8,512]{1,0:T(8,128)S(1)}, f32[8,512]{1,0:T(8,128)S(1)}, u32[]{:S(2)}, u32[]{:S(2)}) collective-permute-start(f32[8,512]{1,0:T(8,128)S(1)} %get-tuple-element.57.refs_1_), channel_id=1, source_target_pairs={{0,4},{4,0},{8,12},{12,8},{16,20},{20,16},{24,28},{28,24},{1,5},{5... | collective-permute-start | bytes 49160 | tf_op jit(solution)/shard_map/ppermute | solution.py:420
  14.3 3.9 %collective-permute-start.4 = (f32[8,512]{1,0:T(8,128)S(1)}, f32[8,512]{1,0:T(8,128)S(1)}, u32[]{:S(2)}, u32[]{:S(2)}) collective-permute-start(f32[8,512]{1,0:T(8,128)S(1)} %get-tuple-element.58.refs_1_), channel_id=1, source_target_pairs={{0,8},{4,12},{8,0},{12,4},{16,24},{20,28},{24,16},{28,20},{1,9},{5... | collective-permute-start | bytes 49160 | tf_op jit(solution)/shard_map/ppermute | solution.py:420
  29.1 3.1 %collective-permute-start.8 = (bf16[512,1024]{1,0:T(8,128)(2,1)S(1)}, bf16[512,1024]{1,0:T(8,128)(2,1)S(1)}, u32[]{:S(2)}, u32[]{:S(2)}) collective-permute-start(bf16[512,1024]{1,0:T(8,128)(2,1)S(1)} %shard_map.78), channel_id=1, source_target_pairs={{0,1},{1,0},{2,3},{3,2},{4,5},{5,4},{6,7},{7,6},{8,9},{9,8},{10,11... | collective-permute-start | bytes 3145736 | tf_op jit(solution)/shard_map/ppermute | solution.py:417
  30.1 4.5 %collective-permute-start.9 = (bf16[128,256]{1,0:T(8,128)(2,1)S(1)}, bf16[128,256]{1,0:T(8,128)(2,1)S(1)}, u32[]{:S(2)}, u32[]{:S(2)}) collective-permute-start(bf16[128,256]{1,0:T(8,128)(2,1)S(1)} %get-tuple-element.76.refs_0_), channel_id=1, source_target_pairs={{0,4},{4,0},{8,12},{12,8},{16,20},{20,16},{24,28},{28,24},{1,5},{5... | collective-permute-start | bytes 196616 | tf_op jit(solution)/shard_map/ppermute | solution.py:420
  31.8 4.9 %collective-permute-start.10 = (bf16[128,256]{1,0:T(8,128)(2,1)S(1)}, bf16[128,256]{1,0:T(8,128)(2,1)S(1)}, u32[]{:S(2)}, u32[]{:S(2)}) collective-permute-start(bf16[128,256]{1,0:T(8,128)(2,1)S(1)} %get-tuple-element.77.refs_0_), channel_id=1, source_target_pairs={{0,4},{4,0},{8,12},{12,8},{16,20},{20,16},{24,28},{28,24},{1,5},{5... | collective-permute-start | bytes 196616 | tf_op jit(solution)/shard_map/ppermute | solution.py:420
  34.6 4.6 %collective-permute-start.11 = (bf16[128,256]{1,0:T(8,128)(2,1)S(1)}, bf16[128,256]{1,0:T(8,128)(2,1)S(1)}, u32[]{:S(2)}, u32[]{:S(2)}) collective-permute-start(bf16[128,256]{1,0:T(8,128)(2,1)S(1)} %shard_map.83.refs_0_), channel_id=1, source_target_pairs={{0,8},{4,12},{8,0},{12,4},{16,24},{20,28},{24,16},{28,20},{1,9},{5... | collective-permute-start | bytes 196616 | tf_op jit(solution)/shard_map/ppermute | solution.py:420
  36.8 6.0 %collective-permute-start.12 = (bf16[128,256]{1,0:T(8,128)(2,1)S(1)}, bf16[128,256]{1,0:T(8,128)(2,1)S(1)}, u32[]{:S(2)}, u32[]{:S(2)}) collective-permute-start(bf16[128,256]{1,0:T(8,128)(2,1)S(1)} %shard_map.84.refs_0_), channel_id=1, source_target_pairs={{0,8},{4,12},{8,0},{12,4},{16,24},{20,28},{24,16},{28,20},{1,9},{5... | collective-permute-start | bytes 196616 | tf_op jit(solution)/shard_map/ppermute | solution.py:420
  39.3 8.6 %collective-permute-start.13 = (bf16[128,256]{1,0:T(8,128)(2,1)S(1)}, bf16[128,256]{1,0:T(8,128)(2,1)S(1)}, u32[]{:S(2)}, u32[]{:S(2)}) collective-permute-start(bf16[128,256]{1,0:T(8,128)(2,1)S(1)} %shard_map.86), channel_id=1, source_target_pairs={{0,16},{4,20},{8,24},{12,28},{16,0},{20,4},{24,8},{28,12},{1,17},{... | collective-permute-start | bytes 196616 | tf_op jit(solution)/shard_map/ppermute | solution.py:420
  42.8 6.1 %collective-permute-start.16 = (bf16[128,256]{1,0:T(8,128)(2,1)S(1)}, bf16[128,256]{1,0:T(8,128)(2,1)S(1)}, u32[]{:S(2)}, u32[]{:S(2)}) collective-permute-start(bf16[128,256]{1,0:T(8,128)(2,1)S(1)} %shard_map.88), channel_id=1, source_target_pairs={{0,16},{4,20},{8,24},{12,28},{1,17},{5,21},{9,25},{13,29},{2,18},{... | collective-permute-start | bytes 196616 | tf_op jit(solution)/shard_map/ppermute | solution.py:420
  48.3 2.3 %collective-permute-start.14 = (bf16[256,256]{1,0:T(8,128)(2,1)S(1)}, bf16[256,256]{1,0:T(8,128)(2,1)S(1)}, u32[]{:S(2)}, u32[]{:S(2)}) collective-permute-start(bf16[256,256]{1,0:T(8,128)(2,1)S(1)} %get-tuple-element.84.refs_3_.refs_0_), channel_id=1, source_target_pairs={{0,1},{1,0},{2,3},{3,2},{4,5},{5,4},{6,7},{7,6},{8,9},{9,8},{10,11... | collective-permute-start | bytes 393224 | tf_op jit(solution)/shard_map/ppermute | solution.py:417
  48.4 5.4 %collective-permute-start.15 = (bf16[256,256]{1,0:T(8,128)(2,1)S(1)}, bf16[256,256]{1,0:T(8,128)(2,1)S(1)}, u32[]{:S(2)}, u32[]{:S(2)}) collective-permute-start(bf16[256,256]{1,0:T(8,128)(2,1)S(1)} %get-tuple-element.85.refs_4_.refs_0_.refs_2_), channel_id=1, source_target_pairs={{0,1},{1,0},{2,3},{3,2},{4,5},{5,4},{6,7},{7,6},{8,9},{9,8},{10,11... | collective-permute-start | bytes 393224 | tf_op jit(solution)/shard_map/ppermute | solution.py:417
  49.5 3.2 %collective-permute-start.17 = (bf16[128,256]{1,0:T(8,128)(2,1)S(1)}, bf16[128,256]{1,0:T(8,128)(2,1)S(1)}, u32[]{:S(2)}, u32[]{:S(2)}) collective-permute-start(bf16[128,256]{1,0:T(8,128)(2,1)S(1)} %get-tuple-element.88.refs_4_.refs_2_), channel_id=1, source_target_pairs={{0,1},{1,0},{2,3},{3,2},{4,5},{5,4},{6,7},{7,6},{8,9},{9,8},{10,11... | collective-permute-start | bytes 196616 | tf_op jit(solution)/shard_map/ppermute | solution.py:417
  49.9 3.8 %collective-permute-start.19 = (bf16[128,256]{1,0:T(8,128)(2,1)S(1)}, bf16[128,256]{1,0:T(8,128)(2,1)S(1)}, u32[]{:S(2)}, u32[]{:S(2)}) collective-permute-start(bf16[128,256]{1,0:T(8,128)(2,1)S(1)} %get-tuple-element.90.refs_8_.refs_2_), channel_id=1, source_target_pairs={{0,1},{1,0},{2,3},{3,2},{4,5},{5,4},{6,7},{7,6},{8,9},{9,8},{10,11... | collective-permute-start | bytes 196616 | tf_op jit(solution)/shard_map/ppermute | solution.py:417
  51.1 15.6 %collective-permute-start.25 = (bf16[128,1024]{1,0:T(8,128)(2,1)S(1)}, bf16[128,1024]{1,0:T(8,128)(2,1)S(1)}, u32[]{:S(2)}, u32[]{:S(2)}) collective-permute-start(bf16[128,1024]{1,0:T(8,128)(2,1)S(1)} %shard_map.94), channel_id=1, source_target_pairs={{0,2},{1,3},{2,0},{3,1},{4,6},{5,7},{6,4},{7,5},{8,10},{9,11},{10,... | collective-permute-start | bytes 786440 | tf_op jit(solution)/shard_map/ppermute | solution.py:417
  53.2 12.8 %collective-permute-start.26 = (bf16[128,1024]{1,0:T(8,128)(2,1)S(1)}, bf16[128,1024]{1,0:T(8,128)(2,1)S(1)}, u32[]{:S(2)}, u32[]{:S(2)}) collective-permute-start(bf16[128,1024]{1,0:T(8,128)(2,1)S(1)} %shard_map.95), channel_id=1, source_target_pairs={{0,2},{1,3},{2,0},{3,1},{4,6},{5,7},{6,4},{7,5},{8,10},{9,11},{10,... | collective-permute-start | bytes 786440 | tf_op jit(solution)/shard_map/ppermute | solution.py:417
  54.2 17.3 %collective-permute-start.24 = (bf16[128,1024]{1,0:T(8,128)(2,1)S(1)}, bf16[128,1024]{1,0:T(8,128)(2,1)S(1)}, u32[]{:S(2)}, u32[]{:S(2)}) collective-permute-start(bf16[128,1024]{1,0:T(8,128)(2,1)S(1)} %shard_map.93), channel_id=1, source_target_pairs={{0,2},{1,3},{2,0},{3,1},{4,6},{5,7},{6,4},{7,5},{8,10},{9,11},{10,... | collective-permute-start | bytes 786440 | tf_op jit(solution)/shard_map/ppermute | solution.py:417
  55.8 2.3 %collective-permute-start.21 = (bf16[64,256]{1,0:T(8,128)(2,1)S(1)}, bf16[64,256]{1,0:T(8,128)(2,1)S(1)}, u32[]{:S(2)}, u32[]{:S(2)}) collective-permute-start(bf16[64,256]{1,0:T(8,128)(2,1)S(1)} %get-tuple-element.92.refs_2_.refs_12_), channel_id=1, source_target_pairs={{0,1},{1,0},{2,3},{3,2},{4,5},{5,4},{6,7},{7,6},{8,9},{9,8},{10,11... | collective-permute-start | bytes 98312 | tf_op jit(solution)/shard_map/ppermute | solution.py:417
  57.5 16.9 %collective-permute-start.23 = (bf16[64,1024]{1,0:T(8,128)(2,1)S(1)}, bf16[64,1024]{1,0:T(8,128)(2,1)S(1)}, u32[]{:S(2)}, u32[]{:S(2)}) collective-permute-start(bf16[64,1024]{1,0:T(8,128)(2,1)S(1)} %shard_map.92), channel_id=1, source_target_pairs={{0,2},{1,3},{2,0},{3,1},{4,6},{5,7},{6,4},{7,5},{8,10},{9,11},{10,... | collective-permute-start | bytes 393224 | tf_op jit(solution)/shard_map/ppermute | solution.py:417
  58.6 17.8 %collective-permute-start.22 = (bf16[64,1024]{1,0:T(8,128)(2,1)S(1)}, bf16[64,1024]{1,0:T(8,128)(2,1)S(1)}, u32[]{:S(2)}, u32[]{:S(2)}) collective-permute-start(bf16[64,1024]{1,0:T(8,128)(2,1)S(1)} %shard_map.90.refs_16_), channel_id=1, source_target_pairs={{0,2},{1,3},{2,0},{3,1},{4,6},{5,7},{6,4},{7,5},{8,10},{9,11},{10,... | collective-permute-start | bytes 393224 | tf_op jit(solution)/shard_map/ppermute | solution.py:417
  (4 other events, 4.8 us)

commit v17 on v10

--- a/solution.py
+++ b/solution.py
@@ -449,13 +449,16 @@
     unit = rows // 8
     ends = (0, 2, 4, 6, 7, 8)
     cuts = [slice(start * unit, stop * unit) for start, stop in zip(ends, ends[1:])]
-    pairs = [(x, swap_tp(x, 1)) for x in finish(local, scaled, earlier[-1], cuts, head_size)]
+    pieces = finish(local, scaled, earlier[-1], cuts[:1], head_size)
+    pieces += finish(local, scaled, earlier[-1], cuts[1:], head_size, pieces)
+    pairs = [(x, swap_tp(x, 1)) for x in pieces]
     crossing = [out_block([pair], w_far_own, w_far, BF16) for pair in pairs]
     own_block = out_block(pairs, w_here_own, w_here, F32, (crossing[-1],))
     out = None
-    for cut, x in zip(cuts, crossing):
+    for cut, x in zip(cuts[:-1], crossing):
         out = add_rows(own_block, swap_tp(x, 2), out, cut.start, unit)
-    return out
+    last = own_block[cuts[-1]] + swap_tp(crossing[-1], 2).astype(F32)
+    return lax.dynamic_update_slice_in_dim(out, last.astype(BF16), cuts[-1].start, 0)
 
 
 def solution(mesh):

time: 76.6 us -> 76.4 us (level)
    pallas_call x5 -> x4, Pallas kernels: 3.57 us -> 2.88 us  [add_rows(): pl.pallas_call(kernel, grid=(rows // unit,), in_specs=specs, out_specs=pl...]
    pallas_call x18 -> x19, Pallas kernels: 17.4 us -> 17.6 us  [call(): pl.pallas_call(run, in_specs=[SMEM] * smem + [HBM] * hbm + [VMEM] * (coun...]
  transfers between devices with their start and end apart: 25 -> 25, of which waited for: 13 -> 13; matrix products, arithmetic and copies ran while one was open for 0% -> 0% of each run, Pallas kernels for 24% -> 25%
where the time goes in v17:
time: 76.4 us; the launch traced here: 76.2 us
  waiting for transfers between devices  30.6 us (40%)
  starting transfers between devices  23.6 us (31%)
  Pallas kernels  20.5 us (27%)
    ppermute x20, waiting for transfers between devices, swap_tp(): return lax.ppermute(x, 'tp', [(i, i ^ bit) for i in range(4)])  21.8 us
    pallas_call x19, Pallas kernels, call(): pl.pallas_call(run, in_specs=[SMEM] * smem + [HBM] * hbm + [VMEM] * (coun...  17.6 us
    ppermute x20, starting transfers between devices, swap_tp(): return lax.ppermute(x, 'tp', [(i, i ^ bit) for i in range(4)])  12.2 us
    ppermute x5, starting transfers between devices, swap_seq(): return lax.ppermute(x, 'seq', [(i, i ^ bit) for i in range(seq_size)])  11.3 us
    ppermute x5, waiting for transfers between devices, swap_seq(): return lax.ppermute(x, 'seq', [(i, i ^ bit) for i in range(seq_size)])  8.77 us
    pallas_call x4, Pallas kernels, add_rows(): pl.pallas_call(kernel, grid=(rows // unit,), in_specs=specs, out_specs=pl...  2.88 us
  transfers between devices with their start and end apart: 25, of which 13 were waited for; matrix products, arithmetic and copies ran while one was open for 0% of the time, Pallas kernels for 25%

profile of v17, /device:TPU:0, one launch (start us, length us, event | category | flops | bytes accessed | tf_op | source)
XLA Modules:
  0.0 76.2 jit_solution(7276444145395683628)
XLA Ops:
  0.5 2.5 %collective-permute-start = (bf16[512,1024]{1,0:T(8,128)(2,1)}, bf16[512,1024]{1,0:T(8,128)(2,1)S(1)}, u32[]{:S(2)}, u32[]{:S(2)}) collective-permute-start(bf16[512,1024]{1,0:T(8,128)(2,1)} %refs_2_.1), channel_id=1, source_target_pairs={{0,2},{1,3},{2,0},{3,1},{4,6},{5,7},{6,4},{7,5},{8,10},{9,11},{10,... | collective-permute-start | bytes 3145736 | tf_op jit(solution)/shard_map/ppermute | solution.py:405
  3.7 5.4 %shard_map.73 = (f32[512,512]{1,0:T(8,128)S(1)}, f32[512,256]{1,0:T(8,128)S(1)}, f32[512,24]{1,0:T(8,128)S(1)}, bf16[2,1024,512]{2,1,0:T(8,128)(2,1)S(1)}, bf16[...) custom-call(s32[1]{0:T(128)} %bitcast.refs_0_, ...), custom_call_target="tpu_custom_call" | custom-call | tf_op jit(solution)/shard_map/pallas_call | solution.py:41
  10.0 2.6 %collective-permute-start.3 = (f32[8,512]{1,0:T(8,128)S(1)}, f32[8,512]{1,0:T(8,128)S(1)}, u32[]{:S(2)}, u32[]{:S(2)}) collective-permute-start(f32[8,512]{1,0:T(8,128)S(1)} %get-tuple-element.52.refs_1_), channel_id=1, source_target_pairs={{0,4},{4,0},{8,12},{12,8},{16,20},{20,16},{24,28},{28,24},{1,5},{5... | collective-permute-start | bytes 49160 | tf_op jit(solution)/shard_map/ppermute | solution.py:408
  12.6 1.7 %collective-permute-done.3.refs_2_ = f32[8,512]{1,0:T(8,128)S(1)} collective-permute-done((f32[8,512]{1,0:T(8,128)S(1)}, f32[8,512]{1,0:T(8,128)S(1)}, u32[]{:S(2)}, u32[]{:S(2)}) %collective-permute-start.3) | collective-permute-done | bytes 16416 | tf_op jit(solution)/shard_map/ppermute | solution.py:408
  14.3 2.2 %collective-permute-start.4 = (f32[8,512]{1,0:T(8,128)S(1)}, f32[8,512]{1,0:T(8,128)S(1)}, u32[]{:S(2)}, u32[]{:S(2)}) collective-permute-start(f32[8,512]{1,0:T(8,128)S(1)} %get-tuple-element.53.refs_1_), channel_id=1, source_target_pairs={{0,8},{4,12},{8,0},{12,4},{16,24},{20,28},{24,16},{28,20},{1,9},{5... | collective-permute-start | bytes 49160 | tf_op jit(solution)/shard_map/ppermute | solution.py:408
  16.5 1.7 %collective-permute-done.4.refs_2_ = f32[8,512]{1,0:T(8,128)S(1)} collective-permute-done((f32[8,512]{1,0:T(8,128)S(1)}, f32[8,512]{1,0:T(8,128)S(1)}, u32[]{:S(2)}, u32[]{:S(2)}) %collective-permute-start.4) | collective-permute-done | bytes 16416 | tf_op jit(solution)/shard_map/ppermute | solution.py:408
  18.8 8.2 %collective-permute-done.refs_0_.refs_1_ = bf16[512,1024]{1,0:T(8,128)(2,1)S(1)} collective-permute-done((bf16[512,1024]{1,0:T(8,128)(2,1)}, bf16[512,1024]{1,0:T(8,128)(2,1)S(1)}, u32[]{:S(2)}, u32[]{:S(2)}) %collective-permute-start) | collective-permute-done | bytes 1048608 | tf_op jit(solution)/shard_map/ppermute | solution.py:405
  28.0 1.1 %collective-permute-done.7.refs_1_ = bf16[512,256]{1,0:T(8,128)(2,1)S(1)} collective-permute-done((bf16[512,256]{1,0:T(8,128)(2,1)S(1)}, bf16[512,256]{1,0:T(8,128)(2,1)S(1)}, u32[]{:S(2)}, u32[]{:S(2)}) %collective-permute-start.7) | collective-permute-done | bytes 262176 | tf_op jit(solution)/shard_map/ppermute | solution.py:405
  29.7 1.8 %collective-permute-start.12 = (bf16[128,512]{1,0:T(8,128)(2,1)S(1)}, bf16[128,512]{1,0:T(8,128)(2,1)S(1)}, u32[]{:S(2)}, u32[]{:S(2)}) collective-permute-start(bf16[128,512]{1,0:T(8,128)(2,1)S(1)} %get-tuple-element.72.refs_0_), channel_id=1, source_target_pairs={{0,4},{4,0},{8,12},{12,8},{16,20},{20,16},{24,28},{28,24},{1,5},{5... | collective-permute-start | bytes 393224 | tf_op jit(solution)/shard_map/ppermute | solution.py:408
  31.4 1.1 %shard_map.79 = (f32[512,512]{1,0:T(8,128)S(1)}, f32[512,24]{1,0:T(8,128)S(1)}) custom-call(s32[1]{0:T(128)} %bitcast.refs_0_, bf16[512,1024]{1,0:T(8,128)(2,1)S(1)} %collective-permute-done.refs_0_.refs_1_, bf16[2,1024,512]{2,1,0:T(8,128)(2,1)S(1)} %get-tuple-element.45.refs_2_.refs_5_, ...), custom_call_target="tpu_custom_call", output_to_operand_aliasing={{0}: (4, {}), {1}: (5, {})} | custom-call | flops 562036736 | bytes 5537796 | tf_op jit(solution)/shard_map/pallas_call | solution.py:41
  33.7 1.6 %collective-permute-done.12.refs_1_.refs_16_ = bf16[128,512]{1,0:T(8,128)(2,1)S(1)} collective-permute-done((bf16[128,512]{1,0:T(8,128)(2,1)S(1)}, bf16[128,512]{1,0:T(8,128)(2,1)S(1)}, u32[]{:S(2)}, u32[]{:S(2)}) %collective-permute-start.12) | collective-permute-done | bytes 131104 | tf_op jit(solution)/shard_map/ppermute | solution.py:408
  35.3 1.9 %collective-permute-start.13 = (bf16[128,512]{1,0:T(8,128)(2,1)S(1)}, bf16[128,512]{1,0:T(8,128)(2,1)S(1)}, u32[]{:S(2)}, u32[]{:S(2)}) collective-permute-start(bf16[128,512]{1,0:T(8,128)(2,1)S(1)} %shard_map.81.refs_0_), channel_id=1, source_target_pairs={{0,8},{4,12},{8,0},{12,4},{16,24},{20,28},{24,16},{28,20},{1,9},{5... | collective-permute-start | bytes 393224 | tf_op jit(solution)/shard_map/ppermute | solution.py:408
  37.2 3.2 %collective-permute-done.13.refs_17_.refs_1_ = bf16[128,512]{1,0:T(8,128)(2,1)S(1)} collective-permute-done((bf16[128,512]{1,0:T(8,128)(2,1)S(1)}, bf16[128,512]{1,0:T(8,128)(2,1)S(1)}, u32[]{:S(2)}, u32[]{:S(2)}) %collective-permute-start.13) | collective-permute-done | bytes 131104 | tf_op jit(solution)/shard_map/ppermute | solution.py:408
  40.4 2.9 %collective-permute-start.14 = (bf16[128,512]{1,0:T(8,128)(2,1)S(1)}, bf16[128,512]{1,0:T(8,128)(2,1)S(1)}, u32[]{:S(2)}, u32[]{:S(2)}) collective-permute-start(bf16[128,512]{1,0:T(8,128)(2,1)S(1)} %shard_map.83), channel_id=1, source_target_pairs={{0,16},{4,20},{8,24},{12,28},{16,0},{20,4},{24,8},{28,12},{1,17},{... | collective-permute-start | bytes 393224 | tf_op jit(solution)/shard_map/ppermute | solution.py:408
  43.3 4.0 %shard_map.82 = (f32[512,512]{1,0:T(8,128)S(1)}, bf16[512,512]{1,0:T(8,128)(2,1)S(1)}, bf16[512,512]{1,0:T(8,128)(2,1)}, f32[512,24]{1,0:T(8,128)}) custom-call(s32[1]{0:T(128)} %bitcast.refs_0_, bf16[512,256]{1,0:T(8,128)(2,1)S(1)} %collective-permute-done.8.refs_1_, bf16[512,256]{1,0:T(8,128)(2,1)S(1)} %collective-permute-done.9.refs_2_, ...), custom_call_target="tpu_custom_call" | custom-call | flops 1073741824 | bytes 7176196 | tf_op jit(solution)/shard_map/pallas_call | solution.py:41
  50.1 1.7 %collective-permute-start.23 = (bf16[128,1024]{1,0:T(8,128)(2,1)S(1)}, bf16[128,1024]{1,0:T(8,128)(2,1)S(1)}, u32[]{:S(2)}, u32[]{:S(2)}) collective-permute-start(bf16[128,1024]{1,0:T(8,128)(2,1)S(1)} %shard_map.91), channel_id=1, source_target_pairs={{0,2},{1,3},{2,0},{3,1},{4,6},{5,7},{6,4},{7,5},{8,10},{9,11},{10,... | collective-permute-start | bytes 786440 | tf_op jit(solution)/shard_map/ppermute | solution.py:405
  53.2 1.6 %collective-permute-start.21 = (bf16[128,1024]{1,0:T(8,128)(2,1)S(1)}, bf16[128,1024]{1,0:T(8,128)(2,1)S(1)}, u32[]{:S(2)}, u32[]{:S(2)}) collective-permute-start(bf16[128,1024]{1,0:T(8,128)(2,1)S(1)} %shard_map.89), channel_id=1, source_target_pairs={{0,2},{1,3},{2,0},{3,1},{4,6},{5,7},{6,4},{7,5},{8,10},{9,11},{10,... | collective-permute-start | bytes 786440 | tf_op jit(solution)/shard_map/ppermute | solution.py:405
  57.6 1.6 %collective-permute-start.24 = (bf16[64,1024]{1,0:T(8,128)(2,1)S(1)}, bf16[64,1024]{1,0:T(8,128)(2,1)S(1)}, u32[]{:S(2)}, u32[]{:S(2)}) collective-permute-start(bf16[64,1024]{1,0:T(8,128)(2,1)S(1)} %shard_map.86.refs_12_), channel_id=1, source_target_pairs={{0,2},{1,3},{2,0},{3,1},{4,6},{5,7},{6,4},{7,5},{8,10},{9,11},{10,... | collective-permute-start | bytes 393224 | tf_op jit(solution)/shard_map/ppermute | solution.py:405
  59.3 1.7 %shard_map.87.h_ref = f32[512,1024]{1,0:T(8,128)S(1)} custom-call(bf16[128,512]{1,0:T(8,128)(2,1)S(1)} %shard_map.84.refs_3_.refs_0_, bf16[128,512]{1,0:T(8,128)(2,1)S(1)} %collective-permute-done.15.refs_1_, bf16[128,512]{1,0:T(8,128)(2,1)S(1)} %get-tuple-element.79.refs_2_.refs_0_, bf16[128,512]{1,0:T(8,128)(2,1)S(1)} %collective-permute-done.16.refs_3_.refs_1_, ...), custom_call_target="tpu_custom_call" | custom-call | tf_op jit(solution)/shard_map/pallas_call | solution.py:41
  61.0 0.8 shard_map.92.refs_0_
  61.7 3.2 %collective-permute-done.22.a_ref = bf16[128,1024]{1,0:T(8,128)(2,1)S(1)} collective-permute-done((bf16[128,1024]{1,0:T(8,128)(2,1)S(1)}, bf16[128,1024]{1,0:T(8,128)(2,1)S(1)}, u32[]{:S(2)}, u32[]{:S(2)}) %collective-permute-start.22) | collective-permute-done | bytes 262176 | tf_op jit(solution)/shard_map/ppermute | solution.py:405
  65.7 4.9 %collective-permute-done.21.a_ref = bf16[128,1024]{1,0:T(8,128)(2,1)S(1)} collective-permute-done((bf16[128,1024]{1,0:T(8,128)(2,1)S(1)}, bf16[128,1024]{1,0:T(8,128)(2,1)S(1)}, u32[]{:S(2)}, u32[]{:S(2)}) %collective-permute-start.21) | collective-permute-done | bytes 262176 | tf_op jit(solution)/shard_map/ppermute | solution.py:405
  71.3 2.1 %collective-permute-done.20.a_ref = bf16[64,1024]{1,0:T(8,128)(2,1)S(1)} collective-permute-done((bf16[64,1024]{1,0:T(8,128)(2,1)S(1)}, bf16[64,1024]{1,0:T(8,128)(2,1)S(1)}, u32[]{:S(2)}, u32[]{:S(2)}) %collective-permute-start.20) | collective-permute-done | bytes 131104 | tf_op jit(solution)/shard_map/ppermute | solution.py:405
  74.0 1.5 %collective-permute-done.24 = bf16[64,1024]{1,0:T(8,128)(2,1)S(1)} collective-permute-done((bf16[64,1024]{1,0:T(8,128)(2,1)S(1)}, bf16[64,1024]{1,0:T(8,128)(2,1)S(1)}, u32[]{:S(2)}, u32[]{:S(2)}) %collective-permute-start.24) | collective-permute-done | bytes 131104 | tf_op jit(solution)/shard_map/ppermute | solution.py:405
  (52 shorter events, 15.3 us)
Async XLA Ops:
  0.0 3.0 %collective-permute-start.1 = (bf16[512,1024]{1,0:T(8,128)(2,1)}, bf16[512,1024]{1,0:T(8,128)(2,1)S(1)}, u32[]{:S(2)}, u32[]{:S(2)}) collective-permute-start(bf16[512,1024]{1,0:T(8,128)(2,1)} %refs_2_.1), channel_id=1, source_target_pairs={{0,1},{1,0},{2,3},{3,2},{4,5},{5,4},{6,7},{7,6},{8,9},{9,8},{10,11... | collective-permute-start | bytes 3145736 | tf_op jit(solution)/shard_map/ppermute | solution.py:405
  0.5 26.6 %collective-permute-start = (bf16[512,1024]{1,0:T(8,128)(2,1)}, bf16[512,1024]{1,0:T(8,128)(2,1)S(1)}, u32[]{:S(2)}, u32[]{:S(2)}) collective-permute-start(bf16[512,1024]{1,0:T(8,128)(2,1)} %refs_2_.1), channel_id=1, source_target_pairs={{0,2},{1,3},{2,0},{3,1},{4,6},{5,7},{6,4},{7,5},{8,10},{9,11},{10,... | collective-permute-start | bytes 3145736 | tf_op jit(solution)/shard_map/ppermute | solution.py:405
  9.0 18.0 %collective-permute-start.5 = (bf16[512,1024]{1,0:T(8,128)(2,1)S(1)}, bf16[512,1024]{1,0:T(8,128)(2,1)S(1)}, u32[]{:S(2)}, u32[]{:S(2)}) collective-permute-start(bf16[512,1024]{1,0:T(8,128)(2,1)S(1)} %get-tuple-element.56), channel_id=1, source_target_pairs={{0,1},{1,0},{2,3},{3,2},{4,5},{5,4},{6,7},{7,6},{8,9},{9,8},{10,11... | collective-permute-start | bytes 3145736 | tf_op jit(solution)/shard_map/ppermute | solution.py:405
  9.5 17.6 %collective-permute-start.6 = (bf16[512,1024]{1,0:T(8,128)(2,1)S(1)}, bf16[512,1024]{1,0:T(8,128)(2,1)S(1)}, u32[]{:S(2)}, u32[]{:S(2)}) collective-permute-start(bf16[512,1024]{1,0:T(8,128)(2,1)S(1)} %get-tuple-element.57), channel_id=1, source_target_pairs={{0,1},{1,0},{2,3},{3,2},{4,5},{5,4},{6,7},{7,6},{8,9},{9,8},{10,11... | collective-permute-start | bytes 3145736 | tf_op jit(solution)/shard_map/ppermute | solution.py:405
  9.6 17.4 %collective-permute-start.2 = (bf16[1024,256]{1,0:T(8,128)(2,1)S(1)}, bf16[1024,256]{1,0:T(8,128)(2,1)S(1)}, u32[]{:S(2)}, u32[]{:S(2)}) collective-permute-start(bf16[1024,256]{1,0:T(8,128)(2,1)S(1)} %get-tuple-element.51), channel_id=1, source_target_pairs={{0,1},{1,0},{2,3},{3,2},{4,5},{5,4},{6,7},{7,6},{8,9},{9,8},{10,11... | collective-permute-start | bytes 1572872 | tf_op jit(solution)/shard_map/ppermute | solution.py:405
  10.0 4.3 %collective-permute-start.3 = (f32[8,512]{1,0:T(8,128)S(1)}, f32[8,512]{1,0:T(8,128)S(1)}, u32[]{:S(2)}, u32[]{:S(2)}) collective-permute-start(f32[8,512]{1,0:T(8,128)S(1)} %get-tuple-element.52.refs_1_), channel_id=1, source_target_pairs={{0,4},{4,0},{8,12},{12,8},{16,20},{20,16},{24,28},{28,24},{1,5},{5... | collective-permute-start | bytes 49160 | tf_op jit(solution)/shard_map/ppermute | solution.py:408
  14.3 3.9 %collective-permute-start.4 = (f32[8,512]{1,0:T(8,128)S(1)}, f32[8,512]{1,0:T(8,128)S(1)}, u32[]{:S(2)}, u32[]{:S(2)}) collective-permute-start(f32[8,512]{1,0:T(8,128)S(1)} %get-tuple-element.53.refs_1_), channel_id=1, source_target_pairs={{0,8},{4,12},{8,0},{12,4},{16,24},{20,28},{24,16},{28,20},{1,9},{5... | collective-permute-start | bytes 49160 | tf_op jit(solution)/shard_map/ppermute | solution.py:408
  27.5 1.6 %collective-permute-start.7 = (bf16[512,256]{1,0:T(8,128)(2,1)S(1)}, bf16[512,256]{1,0:T(8,128)(2,1)S(1)}, u32[]{:S(2)}, u32[]{:S(2)}) collective-permute-start(bf16[512,256]{1,0:T(8,128)(2,1)S(1)} %shard_map.76.refs_3_), channel_id=1, source_target_pairs={{0,1},{1,0},{2,3},{3,2},{4,5},{5,4},{6,7},{7,6},{8,9},{9,8},{10,11... | collective-permute-start | bytes 786440 | tf_op jit(solution)/shard_map/ppermute | solution.py:405
  29.7 5.6 %collective-permute-start.12 = (bf16[128,512]{1,0:T(8,128)(2,1)S(1)}, bf16[128,512]{1,0:T(8,128)(2,1)S(1)}, u32[]{:S(2)}, u32[]{:S(2)}) collective-permute-start(bf16[128,512]{1,0:T(8,128)(2,1)S(1)} %get-tuple-element.72.refs_0_), channel_id=1, source_target_pairs={{0,4},{4,0},{8,12},{12,8},{16,20},{20,16},{24,28},{28,24},{1,5},{5... | collective-permute-start | bytes 393224 | tf_op jit(solution)/shard_map/ppermute | solution.py:408
  32.6 10.7 %collective-permute-start.8 = (bf16[512,256]{1,0:T(8,128)(2,1)S(1)}, bf16[512,256]{1,0:T(8,128)(2,1)S(1)}, u32[]{:S(2)}, u32[]{:S(2)}) collective-permute-start(bf16[512,256]{1,0:T(8,128)(2,1)S(1)} %get-tuple-element.61), channel_id=1, source_target_pairs={{0,1},{1,0},{2,3},{3,2},{4,5},{5,4},{6,7},{7,6},{8,9},{9,8},{10,11... | collective-permute-start | bytes 786440 | tf_op jit(solution)/shard_map/ppermute | solution.py:405
  32.7 10.6 %collective-permute-start.9 = (bf16[512,256]{1,0:T(8,128)(2,1)S(1)}, bf16[512,256]{1,0:T(8,128)(2,1)S(1)}, u32[]{:S(2)}, u32[]{:S(2)}) collective-permute-start(bf16[512,256]{1,0:T(8,128)(2,1)S(1)} %get-tuple-element.62), channel_id=1, source_target_pairs={{0,1},{1,0},{2,3},{3,2},{4,5},{5,4},{6,7},{7,6},{8,9},{9,8},{10,11... | collective-permute-start | bytes 786440 | tf_op jit(solution)/shard_map/ppermute | solution.py:405
  33.2 10.1 %collective-permute-start.10 = (bf16[512,256]{1,0:T(8,128)(2,1)S(1)}, bf16[512,256]{1,0:T(8,128)(2,1)S(1)}, u32[]{:S(2)}, u32[]{:S(2)}) collective-permute-start(bf16[512,256]{1,0:T(8,128)(2,1)S(1)} %get-tuple-element.63), channel_id=1, source_target_pairs={{0,1},{1,0},{2,3},{3,2},{4,5},{5,4},{6,7},{7,6},{8,9},{9,8},{10,11... | collective-permute-start | bytes 786440 | tf_op jit(solution)/shard_map/ppermute | solution.py:405
  33.2 10.0 %collective-permute-start.11 = (bf16[512,256]{1,0:T(8,128)(2,1)S(1)}, bf16[512,256]{1,0:T(8,128)(2,1)S(1)}, u32[]{:S(2)}, u32[]{:S(2)}) collective-permute-start(bf16[512,256]{1,0:T(8,128)(2,1)S(1)} %get-tuple-element.64), channel_id=1, source_target_pairs={{0,1},{1,0},{2,3},{3,2},{4,5},{5,4},{6,7},{7,6},{8,9},{9,8},{10,11... | collective-permute-start | bytes 786440 | tf_op jit(solution)/shard_map/ppermute | solution.py:405
  35.3 5.0 %collective-permute-start.13 = (bf16[128,512]{1,0:T(8,128)(2,1)S(1)}, bf16[128,512]{1,0:T(8,128)(2,1)S(1)}, u32[]{:S(2)}, u32[]{:S(2)}) collective-permute-start(bf16[128,512]{1,0:T(8,128)(2,1)S(1)} %shard_map.81.refs_0_), channel_id=1, source_target_pairs={{0,8},{4,12},{8,0},{12,4},{16,24},{20,28},{24,16},{28,20},{1,9},{5... | collective-permute-start | bytes 393224 | tf_op jit(solution)/shard_map/ppermute | solution.py:408
  40.4 7.5 %collective-permute-start.14 = (bf16[128,512]{1,0:T(8,128)(2,1)S(1)}, bf16[128,512]{1,0:T(8,128)(2,1)S(1)}, u32[]{:S(2)}, u32[]{:S(2)}) collective-permute-start(bf16[128,512]{1,0:T(8,128)(2,1)S(1)} %shard_map.83), channel_id=1, source_target_pairs={{0,16},{4,20},{8,24},{12,28},{16,0},{20,4},{24,8},{28,12},{1,17},{... | collective-permute-start | bytes 393224 | tf_op jit(solution)/shard_map/ppermute | solution.py:408
  48.2 1.4 %collective-permute-start.15 = (bf16[128,512]{1,0:T(8,128)(2,1)S(1)}, bf16[128,512]{1,0:T(8,128)(2,1)S(1)}, u32[]{:S(2)}, u32[]{:S(2)}) collective-permute-start(bf16[128,512]{1,0:T(8,128)(2,1)S(1)} %shard_map.84.refs_3_.refs_0_), channel_id=1, source_target_pairs={{0,1},{1,0},{2,3},{3,2},{4,5},{5,4},{6,7},{7,6},{8,9},{9,8},{10,11... | collective-permute-start | bytes 393224 | tf_op jit(solution)/shard_map/ppermute | solution.py:405
  48.9 2.9 %collective-permute-start.16 = (bf16[128,512]{1,0:T(8,128)(2,1)S(1)}, bf16[128,512]{1,0:T(8,128)(2,1)S(1)}, u32[]{:S(2)}, u32[]{:S(2)}) collective-permute-start(bf16[128,512]{1,0:T(8,128)(2,1)S(1)} %get-tuple-element.79.refs_2_.refs_0_), channel_id=1, source_target_pairs={{0,1},{1,0},{2,3},{3,2},{4,5},{5,4},{6,7},{7,6},{8,9},{9,8},{10,11... | collective-permute-start | bytes 393224 | tf_op jit(solution)/shard_map/ppermute | solution.py:405
  49.4 3.3 %collective-permute-start.17 = (bf16[128,512]{1,0:T(8,128)(2,1)S(1)}, bf16[128,512]{1,0:T(8,128)(2,1)S(1)}, u32[]{:S(2)}, u32[]{:S(2)}) collective-permute-start(bf16[128,512]{1,0:T(8,128)(2,1)S(1)} %get-tuple-element.80.refs_4_.refs_0_), channel_id=1, source_target_pairs={{0,1},{1,0},{2,3},{3,2},{4,5},{5,4},{6,7},{7,6},{8,9},{9,8},{10,11... | collective-permute-start | bytes 393224 | tf_op jit(solution)/shard_map/ppermute | solution.py:405
  50.1 10.8 %collective-permute-start.23 = (bf16[128,1024]{1,0:T(8,128)(2,1)S(1)}, bf16[128,1024]{1,0:T(8,128)(2,1)S(1)}, u32[]{:S(2)}, u32[]{:S(2)}) collective-permute-start(bf16[128,1024]{1,0:T(8,128)(2,1)S(1)} %shard_map.91), channel_id=1, source_target_pairs={{0,2},{1,3},{2,0},{3,1},{4,6},{5,7},{6,4},{7,5},{8,10},{9,11},{10,... | collective-permute-start | bytes 786440 | tf_op jit(solution)/shard_map/ppermute | solution.py:405
  52.2 12.7 %collective-permute-start.22 = (bf16[128,1024]{1,0:T(8,128)(2,1)S(1)}, bf16[128,1024]{1,0:T(8,128)(2,1)S(1)}, u32[]{:S(2)}, u32[]{:S(2)}) collective-permute-start(bf16[128,1024]{1,0:T(8,128)(2,1)S(1)} %shard_map.90), channel_id=1, source_target_pairs={{0,2},{1,3},{2,0},{3,1},{4,6},{5,7},{6,4},{7,5},{8,10},{9,11},{10,... | collective-permute-start | bytes 786440 | tf_op jit(solution)/shard_map/ppermute | solution.py:405
  53.2 17.3 %collective-permute-start.21 = (bf16[128,1024]{1,0:T(8,128)(2,1)S(1)}, bf16[128,1024]{1,0:T(8,128)(2,1)S(1)}, u32[]{:S(2)}, u32[]{:S(2)}) collective-permute-start(bf16[128,1024]{1,0:T(8,128)(2,1)S(1)} %shard_map.89), channel_id=1, source_target_pairs={{0,2},{1,3},{2,0},{3,1},{4,6},{5,7},{6,4},{7,5},{8,10},{9,11},{10,... | collective-permute-start | bytes 786440 | tf_op jit(solution)/shard_map/ppermute | solution.py:405
  54.9 2.3 %collective-permute-start.19 = (bf16[64,512]{1,0:T(8,128)(2,1)S(1)}, bf16[64,512]{1,0:T(8,128)(2,1)S(1)}, u32[]{:S(2)}, u32[]{:S(2)}) collective-permute-start(bf16[64,512]{1,0:T(8,128)(2,1)S(1)} %get-tuple-element.82.refs_0_.refs_8_), channel_id=1, source_target_pairs={{0,1},{1,0},{2,3},{3,2},{4,5},{5,4},{6,7},{7,6},{8,9},{9,8},{10,11... | collective-permute-start | bytes 196616 | tf_op jit(solution)/shard_map/ppermute | solution.py:405
  56.6 16.7 %collective-permute-start.20 = (bf16[64,1024]{1,0:T(8,128)(2,1)S(1)}, bf16[64,1024]{1,0:T(8,128)(2,1)S(1)}, u32[]{:S(2)}, u32[]{:S(2)}) collective-permute-start(bf16[64,1024]{1,0:T(8,128)(2,1)S(1)} %shard_map.88), channel_id=1, source_target_pairs={{0,2},{1,3},{2,0},{3,1},{4,6},{5,7},{6,4},{7,5},{8,10},{9,11},{10,... | collective-permute-start | bytes 393224 | tf_op jit(solution)/shard_map/ppermute | solution.py:405
  57.6 17.9 %collective-permute-start.24 = (bf16[64,1024]{1,0:T(8,128)(2,1)S(1)}, bf16[64,1024]{1,0:T(8,128)(2,1)S(1)}, u32[]{:S(2)}, u32[]{:S(2)}) collective-permute-start(bf16[64,1024]{1,0:T(8,128)(2,1)S(1)} %shard_map.86.refs_12_), channel_id=1, source_target_pairs={{0,2},{1,3},{2,0},{3,1},{4,6},{5,7},{6,4},{7,5},{8,10},{9,11},{10,... | collective-permute-start | bytes 393224 | tf_op jit(solution)/shard_map/ppermute | solution.py:405
  (2 other events, 2.0 us)

commit v18 on v17

--- a/solution.py
+++ b/solution.py
@@ -48,21 +48,6 @@
         compiler_params=pltpu.CompilerParams(vmem_limit_bytes=megabytes * 1024 * 1024),
         cost_estimate=pl.CostEstimate(flops=flops, bytes_accessed=nbytes, transcendentals=0),
     )(*ins, *after)
-
-
-def gate(x, *after):
-    def run(*refs):
-        pass
-
-    return pl.pallas_call(
-        run,
-        in_specs=[ANY] * (1 + len(after)),
-        out_specs=ANY,
-        out_shape=shape(x.shape, x.dtype),
-        input_output_aliases={0: 0},
-        compiler_params=pltpu.CompilerParams(vmem_limit_bytes=1024 * 1024),
-        cost_estimate=pl.CostEstimate(flops=0, bytes_accessed=0, transcendentals=0),
-    )(x, *after)
 
 
 def copies(pairs, sems):
@@ -132,7 +117,7 @@
     heads = log_decay_rows.shape[0]
     block = w_out.shape[1] // 4
 
-    def kernel(me_ref, slab_ref, t_ref, wq_ref, wk_ref, wv_ref, wl_ref, wo_ref, near_ref, decay_ref, *refs):
+    def kernel(me_ref, slab_ref, t_ref, wq_ref, wk_ref, wv_ref, wo_ref, wl_ref, near_ref, decay_ref, *refs):
         total_q, total_kv, total_l, far_q, far_kv, send_kv, all_l = refs[:7]
         decay_outs, blocks, (own_x, own_q, own_kv, sems) = refs[7:12], refs[12:16], refs[16:]
 
@@ -147,26 +132,27 @@
         def columns(i):
             return wo_ref.at[:, pl.ds(pl.multiple_of((me_ref[0] ^ i) * block, 128), block)]
 
-        moves = pairs(0, own_q.at[0], own_kv.at[0]) + [(wl_ref, all_l), (t_ref, own_x)]
+        moves = pairs(0, own_q.at[0], own_kv.at[0]) + [(t_ref, own_x)]
         moves += pairs(1, own_q.at[1], own_kv.at[1])
         moves += pairs(2, far_q.at[0], far_kv) + pairs(3, far_q.at[1], send_kv)
         moves += [(columns(i), blocks[i]) for i in range(4)]
         started = copies(moves, sems)
         decays(slab_ref, decay_ref, *decay_outs)
-        for copy in started[:5]:
+        all_l[...] = wl_ref[...]
+        for copy in started[:4]:
             copy.wait()
         lanes = pl.ds(pl.multiple_of(me_ref[0] * shard, 128), shard)
         own = own_x[...]
         total_kv[...] = dot(own, own_kv[0])
         total_q[...] = dot(own, own_q[0])
         total_l[...] = dot_dims(own, all_l[:, lanes], 1, 1)
-        for copy in started[5:8]:
+        for copy in started[4:7]:
             copy.wait()
         lanes = pl.ds(pl.multiple_of((me_ref[0] ^ 1) * shard, 128), shard)
         total_kv[...] += dot(near_ref[...], own_kv[1])
         total_q[...] += dot(near_ref[...], own_q[1])
         total_l[...] += dot_dims(near_ref[...], all_l[:, lanes], 1, 1)
-        for copy in started[8:]:
+        for copy in started[7:]:
             copy.wait()
 
     wide = shape((8, heads * head_size), F32)
@@ -188,10 +174,10 @@
         pltpu.VMEM((rows, shard), BF16),
         pltpu.VMEM((2, shard, q_width), BF16),
         pltpu.VMEM((2, shard, 2 * kv_width), BF16),
-        pltpu.SemaphoreType.DMA((18,)),
+        pltpu.SemaphoreType.DMA((17,)),
     ]
-    ins = [me, slab, tokens, wq, wk, wv, wl, w_out, near, log_decay_rows]
-    outs = call(kernel, ins, outs, 0, smem=2, hbm=6, scratch=scratch, megabytes=14)
+    ins = [me, slab, tokens, wq, wk, wv, w_out, wl, near, log_decay_rows]
+    outs = call(kernel, ins, outs, 0, smem=2, hbm=5, scratch=scratch, megabytes=14)
     return outs[:3], outs[3:7], outs[7:12], outs[12:]
 
 

time: 76.4 us -> 76.4 us (level)
  local copies, waits for them, and re-layouts: 0.7 us -> 1.62 us
  waiting for transfers between devices: 30.6 us -> 29.8 us
    unnamed x2 -> x4, local copies, waits for them, and re-layouts: 0.7 us -> 1.62 us
    ppermute x20, waiting for transfers between devices: 21.8 us -> 21 us  [swap_tp(): return lax.ppermute(x, 'tp', [(i, i ^ bit) for i in range(4)])]
where the time goes in v18:
time: 76.4 us; the launch traced here: 76.2 us
  waiting for transfers between devices  29.8 us (39%)
  starting transfers between devices  23.6 us (31%)
  Pallas kernels  20.4 us (27%)
  local copies, waits for them, and re-layouts  1.62 us (2%)
    ppermute x20, waiting for transfers between devices, swap_tp(): return lax.ppermute(x, 'tp', [(i, i ^ bit) for i in range(4)])  21 us
    pallas_call x19, Pallas kernels, call(): pl.pallas_call(run, in_specs=[SMEM] * smem + [HBM] * hbm + [VMEM] * (coun...  17.5 us
    ppermute x20, starting transfers between devices, swap_tp(): return lax.ppermute(x, 'tp', [(i, i ^ bit) for i in range(4)])  12.2 us
    ppermute x5, starting transfers between devices, swap_seq(): return lax.ppermute(x, 'seq', [(i, i ^ bit) for i in range(seq_size)])  11.3 us
    ppermute x5, waiting for transfers between devices, swap_seq(): return lax.ppermute(x, 'seq', [(i, i ^ bit) for i in range(seq_size)])  8.77 us
    pallas_call x4, Pallas kernels, add_rows(): pl.pallas_call(kernel, grid=(rows // unit,), in_specs=specs, out_specs=pl...  2.88 us
    unnamed x4, local copies, waits for them, and re-layouts  1.62 us
  transfers between devices with their start and end apart: 25, of which 13 were waited for; matrix products, arithmetic and copies ran while one was open for 0% of the time, Pallas kernels for 25%

profile of v18, /device:TPU:0, one launch (start us, length us, event | category | flops | bytes accessed | tf_op | source)
XLA Modules:
  0.0 76.2 jit_solution(1114031010514996725)
XLA Ops:
  0.5 2.5 %collective-permute-start = (bf16[512,1024]{1,0:T(8,128)(2,1)}, bf16[512,1024]{1,0:T(8,128)(2,1)S(1)}, u32[]{:S(2)}, u32[]{:S(2)}) collective-permute-start(bf16[512,1024]{1,0:T(8,128)(2,1)} %refs_2_.1), channel_id=1, source_target_pairs={{0,2},{1,3},{2,0},{3,1},{4,6},{5,7},{6,4},{7,5},{8,10},{9,11},{10,... | collective-permute-start | bytes 3145736 | tf_op jit(solution)/shard_map/ppermute | solution.py:391
  3.0 0.9 %copy-done = bf16[4096,24]{0,1:T(8,128)(2,1)S(1)} copy-done((bf16[4096,24]{0,1:T(8,128)(2,1)S(1)}, bf16[4096,24]{0,1:T(8,128)(2,1)}, u32[]{:S(2)}) %copy-start) | copy-done | bytes 196632
  4.6 5.3 %shard_map.73 = (f32[512,512]{1,0:T(8,128)S(1)}, f32[512,256]{1,0:T(8,128)S(1)}, f32[512,24]{1,0:T(8,128)S(1)}, bf16[2,1024,512]{2,1,0:T(8,128)(2,1)S(1)}, bf16[...) custom-call(s32[1]{0:T(128)} %bitcast.refs_0_, ...), custom_call_target="tpu_custom_call" | custom-call | tf_op jit(solution)/shard_map/pallas_call | solution.py:41
  10.8 2.6 %collective-permute-start.3 = (f32[8,512]{1,0:T(8,128)S(1)}, f32[8,512]{1,0:T(8,128)S(1)}, u32[]{:S(2)}, u32[]{:S(2)}) collective-permute-start(f32[8,512]{1,0:T(8,128)S(1)} %get-tuple-element.52.refs_1_), channel_id=1, source_target_pairs={{0,4},{4,0},{8,12},{12,8},{16,20},{20,16},{24,28},{28,24},{1,5},{5... | collective-permute-start | bytes 49160 | tf_op jit(solution)/shard_map/ppermute | solution.py:394
  13.4 1.7 %collective-permute-done.3.refs_2_ = f32[8,512]{1,0:T(8,128)S(1)} collective-permute-done((f32[8,512]{1,0:T(8,128)S(1)}, f32[8,512]{1,0:T(8,128)S(1)}, u32[]{:S(2)}, u32[]{:S(2)}) %collective-permute-start.3) | collective-permute-done | bytes 16416 | tf_op jit(solution)/shard_map/ppermute | solution.py:394
  15.2 2.2 %collective-permute-start.4 = (f32[8,512]{1,0:T(8,128)S(1)}, f32[8,512]{1,0:T(8,128)S(1)}, u32[]{:S(2)}, u32[]{:S(2)}) collective-permute-start(f32[8,512]{1,0:T(8,128)S(1)} %get-tuple-element.53.refs_1_), channel_id=1, source_target_pairs={{0,8},{4,12},{8,0},{12,4},{16,24},{20,28},{24,16},{28,20},{1,9},{5... | collective-permute-start | bytes 49160 | tf_op jit(solution)/shard_map/ppermute | solution.py:394
  17.3 1.7 %collective-permute-done.4.refs_2_ = f32[8,512]{1,0:T(8,128)S(1)} collective-permute-done((f32[8,512]{1,0:T(8,128)S(1)}, f32[8,512]{1,0:T(8,128)S(1)}, u32[]{:S(2)}, u32[]{:S(2)}) %collective-permute-start.4) | collective-permute-done | bytes 16416 | tf_op jit(solution)/shard_map/ppermute | solution.py:394
  19.7 7.3 %collective-permute-done.refs_0_.refs_1_ = bf16[512,1024]{1,0:T(8,128)(2,1)S(1)} collective-permute-done((bf16[512,1024]{1,0:T(8,128)(2,1)}, bf16[512,1024]{1,0:T(8,128)(2,1)S(1)}, u32[]{:S(2)}, u32[]{:S(2)}) %collective-permute-start) | collective-permute-done | bytes 1048608 | tf_op jit(solution)/shard_map/ppermute | solution.py:391
  28.0 1.1 %collective-permute-done.7.refs_1_ = bf16[512,256]{1,0:T(8,128)(2,1)S(1)} collective-permute-done((bf16[512,256]{1,0:T(8,128)(2,1)S(1)}, bf16[512,256]{1,0:T(8,128)(2,1)S(1)}, u32[]{:S(2)}, u32[]{:S(2)}) %collective-permute-start.7) | collective-permute-done | bytes 262176 | tf_op jit(solution)/shard_map/ppermute | solution.py:391
  29.7 1.8 %collective-permute-start.12 = (bf16[128,512]{1,0:T(8,128)(2,1)S(1)}, bf16[128,512]{1,0:T(8,128)(2,1)S(1)}, u32[]{:S(2)}, u32[]{:S(2)}) collective-permute-start(bf16[128,512]{1,0:T(8,128)(2,1)S(1)} %get-tuple-element.72.refs_0_), channel_id=1, source_target_pairs={{0,4},{4,0},{8,12},{12,8},{16,20},{20,16},{24,28},{28,24},{1,5},{5... | collective-permute-start | bytes 393224 | tf_op jit(solution)/shard_map/ppermute | solution.py:394
  31.4 1.1 %shard_map.79 = (f32[512,512]{1,0:T(8,128)S(1)}, f32[512,24]{1,0:T(8,128)S(1)}) custom-call(s32[1]{0:T(128)} %bitcast.refs_0_, bf16[512,1024]{1,0:T(8,128)(2,1)S(1)} %collective-permute-done.refs_0_.refs_1_, bf16[2,1024,512]{2,1,0:T(8,128)(2,1)S(1)} %get-tuple-element.45.refs_2_.refs_5_, ...), custom_call_target="tpu_custom_call", output_to_operand_aliasing={{0}: (4, {}), {1}: (5, {})} | custom-call | flops 562036736 | bytes 5537796 | tf_op jit(solution)/shard_map/pallas_call | solution.py:41
  33.7 1.6 %collective-permute-done.12.refs_1_.refs_16_ = bf16[128,512]{1,0:T(8,128)(2,1)S(1)} collective-permute-done((bf16[128,512]{1,0:T(8,128)(2,1)S(1)}, bf16[128,512]{1,0:T(8,128)(2,1)S(1)}, u32[]{:S(2)}, u32[]{:S(2)}) %collective-permute-start.12) | collective-permute-done | bytes 131104 | tf_op jit(solution)/shard_map/ppermute | solution.py:394
  35.3 1.9 %collective-permute-start.13 = (bf16[128,512]{1,0:T(8,128)(2,1)S(1)}, bf16[128,512]{1,0:T(8,128)(2,1)S(1)}, u32[]{:S(2)}, u32[]{:S(2)}) collective-permute-start(bf16[128,512]{1,0:T(8,128)(2,1)S(1)} %shard_map.81.refs_0_), channel_id=1, source_target_pairs={{0,8},{4,12},{8,0},{12,4},{16,24},{20,28},{24,16},{28,20},{1,9},{5... | collective-permute-start | bytes 393224 | tf_op jit(solution)/shard_map/ppermute | solution.py:394
  37.2 3.2 %collective-permute-done.13.refs_17_.refs_1_ = bf16[128,512]{1,0:T(8,128)(2,1)S(1)} collective-permute-done((bf16[128,512]{1,0:T(8,128)(2,1)S(1)}, bf16[128,512]{1,0:T(8,128)(2,1)S(1)}, u32[]{:S(2)}, u32[]{:S(2)}) %collective-permute-start.13) | collective-permute-done | bytes 131104 | tf_op jit(solution)/shard_map/ppermute | solution.py:394
  40.4 2.9 %collective-permute-start.14 = (bf16[128,512]{1,0:T(8,128)(2,1)S(1)}, bf16[128,512]{1,0:T(8,128)(2,1)S(1)}, u32[]{:S(2)}, u32[]{:S(2)}) collective-permute-start(bf16[128,512]{1,0:T(8,128)(2,1)S(1)} %shard_map.83), channel_id=1, source_target_pairs={{0,16},{4,20},{8,24},{12,28},{16,0},{20,4},{24,8},{28,12},{1,17},{... | collective-permute-start | bytes 393224 | tf_op jit(solution)/shard_map/ppermute | solution.py:394
  43.3 4.0 %shard_map.82 = (f32[512,512]{1,0:T(8,128)S(1)}, bf16[512,512]{1,0:T(8,128)(2,1)S(1)}, bf16[512,512]{1,0:T(8,128)(2,1)}, f32[512,24]{1,0:T(8,128)}) custom-call(s32[1]{0:T(128)} %bitcast.refs_0_, bf16[512,256]{1,0:T(8,128)(2,1)S(1)} %collective-permute-done.8.refs_1_, bf16[512,256]{1,0:T(8,128)(2,1)S(1)} %collective-permute-done.9.refs_2_, ...), custom_call_target="tpu_custom_call" | custom-call | flops 1073741824 | bytes 7176196 | tf_op jit(solution)/shard_map/pallas_call | solution.py:41
  50.1 1.7 %collective-permute-start.23 = (bf16[128,1024]{1,0:T(8,128)(2,1)S(1)}, bf16[128,1024]{1,0:T(8,128)(2,1)S(1)}, u32[]{:S(2)}, u32[]{:S(2)}) collective-permute-start(bf16[128,1024]{1,0:T(8,128)(2,1)S(1)} %shard_map.91), channel_id=1, source_target_pairs={{0,2},{1,3},{2,0},{3,1},{4,6},{5,7},{6,4},{7,5},{8,10},{9,11},{10,... | collective-permute-start | bytes 786440 | tf_op jit(solution)/shard_map/ppermute | solution.py:391
  53.2 1.6 %collective-permute-start.21 = (bf16[128,1024]{1,0:T(8,128)(2,1)S(1)}, bf16[128,1024]{1,0:T(8,128)(2,1)S(1)}, u32[]{:S(2)}, u32[]{:S(2)}) collective-permute-start(bf16[128,1024]{1,0:T(8,128)(2,1)S(1)} %shard_map.89), channel_id=1, source_target_pairs={{0,2},{1,3},{2,0},{3,1},{4,6},{5,7},{6,4},{7,5},{8,10},{9,11},{10,... | collective-permute-start | bytes 786440 | tf_op jit(solution)/shard_map/ppermute | solution.py:391
  57.6 1.6 %collective-permute-start.24 = (bf16[64,1024]{1,0:T(8,128)(2,1)S(1)}, bf16[64,1024]{1,0:T(8,128)(2,1)S(1)}, u32[]{:S(2)}, u32[]{:S(2)}) collective-permute-start(bf16[64,1024]{1,0:T(8,128)(2,1)S(1)} %shard_map.86.refs_12_), channel_id=1, source_target_pairs={{0,2},{1,3},{2,0},{3,1},{4,6},{5,7},{6,4},{7,5},{8,10},{9,11},{10,... | collective-permute-start | bytes 393224 | tf_op jit(solution)/shard_map/ppermute | solution.py:391
  59.3 1.7 %shard_map.87.h_ref = f32[512,1024]{1,0:T(8,128)S(1)} custom-call(bf16[128,512]{1,0:T(8,128)(2,1)S(1)} %shard_map.84.refs_3_.refs_0_, bf16[128,512]{1,0:T(8,128)(2,1)S(1)} %collective-permute-done.15.refs_1_, bf16[128,512]{1,0:T(8,128)(2,1)S(1)} %get-tuple-element.79.refs_2_.refs_0_, bf16[128,512]{1,0:T(8,128)(2,1)S(1)} %collective-permute-done.16.refs_3_.refs_1_, ...), custom_call_target="tpu_custom_call" | custom-call | tf_op jit(solution)/shard_map/pallas_call | solution.py:41
  61.7 3.2 %collective-permute-done.22.a_ref = bf16[128,1024]{1,0:T(8,128)(2,1)S(1)} collective-permute-done((bf16[128,1024]{1,0:T(8,128)(2,1)S(1)}, bf16[128,1024]{1,0:T(8,128)(2,1)S(1)}, u32[]{:S(2)}, u32[]{:S(2)}) %collective-permute-start.22) | collective-permute-done | bytes 262176 | tf_op jit(solution)/shard_map/ppermute | solution.py:391
  65.7 4.9 %collective-permute-done.21.a_ref = bf16[128,1024]{1,0:T(8,128)(2,1)S(1)} collective-permute-done((bf16[128,1024]{1,0:T(8,128)(2,1)S(1)}, bf16[128,1024]{1,0:T(8,128)(2,1)S(1)}, u32[]{:S(2)}, u32[]{:S(2)}) %collective-permute-start.21) | collective-permute-done | bytes 262176 | tf_op jit(solution)/shard_map/ppermute | solution.py:391
  71.3 2.1 %collective-permute-done.20.a_ref = bf16[64,1024]{1,0:T(8,128)(2,1)S(1)} collective-permute-done((bf16[64,1024]{1,0:T(8,128)(2,1)S(1)}, bf16[64,1024]{1,0:T(8,128)(2,1)S(1)}, u32[]{:S(2)}, u32[]{:S(2)}) %collective-permute-start.20) | collective-permute-done | bytes 131104 | tf_op jit(solution)/shard_map/ppermute | solution.py:391
  74.0 1.5 %collective-permute-done.24 = bf16[64,1024]{1,0:T(8,128)(2,1)S(1)} collective-permute-done((bf16[64,1024]{1,0:T(8,128)(2,1)S(1)}, bf16[64,1024]{1,0:T(8,128)(2,1)S(1)}, u32[]{:S(2)}, u32[]{:S(2)}) %collective-permute-start.24) | collective-permute-done | bytes 131104 | tf_op jit(solution)/shard_map/ppermute | solution.py:391
  (54 shorter events, 16.0 us)
Async XLA Ops:
  0.0 3.0 %collective-permute-start.1 = (bf16[512,1024]{1,0:T(8,128)(2,1)}, bf16[512,1024]{1,0:T(8,128)(2,1)S(1)}, u32[]{:S(2)}, u32[]{:S(2)}) collective-permute-start(bf16[512,1024]{1,0:T(8,128)(2,1)} %refs_2_.1), channel_id=1, source_target_pairs={{0,1},{1,0},{2,3},{3,2},{4,5},{5,4},{6,7},{7,6},{8,9},{9,8},{10,11... | collective-permute-start | bytes 3145736 | tf_op jit(solution)/shard_map/ppermute | solution.py:391
  0.5 26.6 %collective-permute-start = (bf16[512,1024]{1,0:T(8,128)(2,1)}, bf16[512,1024]{1,0:T(8,128)(2,1)S(1)}, u32[]{:S(2)}, u32[]{:S(2)}) collective-permute-start(bf16[512,1024]{1,0:T(8,128)(2,1)} %refs_2_.1), channel_id=1, source_target_pairs={{0,2},{1,3},{2,0},{3,1},{4,6},{5,7},{6,4},{7,5},{8,10},{9,11},{10,... | collective-permute-start | bytes 3145736 | tf_op jit(solution)/shard_map/ppermute | solution.py:391
  9.9 17.1 %collective-permute-start.5 = (bf16[512,1024]{1,0:T(8,128)(2,1)S(1)}, bf16[512,1024]{1,0:T(8,128)(2,1)S(1)}, u32[]{:S(2)}, u32[]{:S(2)}) collective-permute-start(bf16[512,1024]{1,0:T(8,128)(2,1)S(1)} %get-tuple-element.56), channel_id=1, source_target_pairs={{0,1},{1,0},{2,3},{3,2},{4,5},{5,4},{6,7},{7,6},{8,9},{9,8},{10,11... | collective-permute-start | bytes 3145736 | tf_op jit(solution)/shard_map/ppermute | solution.py:391
  10.3 16.7 %collective-permute-start.6 = (bf16[512,1024]{1,0:T(8,128)(2,1)S(1)}, bf16[512,1024]{1,0:T(8,128)(2,1)S(1)}, u32[]{:S(2)}, u32[]{:S(2)}) collective-permute-start(bf16[512,1024]{1,0:T(8,128)(2,1)S(1)} %get-tuple-element.57), channel_id=1, source_target_pairs={{0,1},{1,0},{2,3},{3,2},{4,5},{5,4},{6,7},{7,6},{8,9},{9,8},{10,11... | collective-permute-start | bytes 3145736 | tf_op jit(solution)/shard_map/ppermute | solution.py:391
  10.5 16.6 %collective-permute-start.2 = (bf16[1024,256]{1,0:T(8,128)(2,1)S(1)}, bf16[1024,256]{1,0:T(8,128)(2,1)S(1)}, u32[]{:S(2)}, u32[]{:S(2)}) collective-permute-start(bf16[1024,256]{1,0:T(8,128)(2,1)S(1)} %get-tuple-element.51), channel_id=1, source_target_pairs={{0,1},{1,0},{2,3},{3,2},{4,5},{5,4},{6,7},{7,6},{8,9},{9,8},{10,11... | collective-permute-start | bytes 1572872 | tf_op jit(solution)/shard_map/ppermute | solution.py:391
  10.8 4.3 %collective-permute-start.3 = (f32[8,512]{1,0:T(8,128)S(1)}, f32[8,512]{1,0:T(8,128)S(1)}, u32[]{:S(2)}, u32[]{:S(2)}) collective-permute-start(f32[8,512]{1,0:T(8,128)S(1)} %get-tuple-element.52.refs_1_), channel_id=1, source_target_pairs={{0,4},{4,0},{8,12},{12,8},{16,20},{20,16},{24,28},{28,24},{1,5},{5... | collective-permute-start | bytes 49160 | tf_op jit(solution)/shard_map/ppermute | solution.py:394
  15.2 3.9 %collective-permute-start.4 = (f32[8,512]{1,0:T(8,128)S(1)}, f32[8,512]{1,0:T(8,128)S(1)}, u32[]{:S(2)}, u32[]{:S(2)}) collective-permute-start(f32[8,512]{1,0:T(8,128)S(1)} %get-tuple-element.53.refs_1_), channel_id=1, source_target_pairs={{0,8},{4,12},{8,0},{12,4},{16,24},{20,28},{24,16},{28,20},{1,9},{5... | collective-permute-start | bytes 49160 | tf_op jit(solution)/shard_map/ppermute | solution.py:394
  27.5 1.6 %collective-permute-start.7 = (bf16[512,256]{1,0:T(8,128)(2,1)S(1)}, bf16[512,256]{1,0:T(8,128)(2,1)S(1)}, u32[]{:S(2)}, u32[]{:S(2)}) collective-permute-start(bf16[512,256]{1,0:T(8,128)(2,1)S(1)} %shard_map.76.refs_3_), channel_id=1, source_target_pairs={{0,1},{1,0},{2,3},{3,2},{4,5},{5,4},{6,7},{7,6},{8,9},{9,8},{10,11... | collective-permute-start | bytes 786440 | tf_op jit(solution)/shard_map/ppermute | solution.py:391
  29.7 5.6 %collective-permute-start.12 = (bf16[128,512]{1,0:T(8,128)(2,1)S(1)}, bf16[128,512]{1,0:T(8,128)(2,1)S(1)}, u32[]{:S(2)}, u32[]{:S(2)}) collective-permute-start(bf16[128,512]{1,0:T(8,128)(2,1)S(1)} %get-tuple-element.72.refs_0_), channel_id=1, source_target_pairs={{0,4},{4,0},{8,12},{12,8},{16,20},{20,16},{24,28},{28,24},{1,5},{5... | collective-permute-start | bytes 393224 | tf_op jit(solution)/shard_map/ppermute | solution.py:394
  32.6 10.7 %collective-permute-start.8 = (bf16[512,256]{1,0:T(8,128)(2,1)S(1)}, bf16[512,256]{1,0:T(8,128)(2,1)S(1)}, u32[]{:S(2)}, u32[]{:S(2)}) collective-permute-start(bf16[512,256]{1,0:T(8,128)(2,1)S(1)} %get-tuple-element.61), channel_id=1, source_target_pairs={{0,1},{1,0},{2,3},{3,2},{4,5},{5,4},{6,7},{7,6},{8,9},{9,8},{10,11... | collective-permute-start | bytes 786440 | tf_op jit(solution)/shard_map/ppermute | solution.py:391
  32.7 10.6 %collective-permute-start.9 = (bf16[512,256]{1,0:T(8,128)(2,1)S(1)}, bf16[512,256]{1,0:T(8,128)(2,1)S(1)}, u32[]{:S(2)}, u32[]{:S(2)}) collective-permute-start(bf16[512,256]{1,0:T(8,128)(2,1)S(1)} %get-tuple-element.62), channel_id=1, source_target_pairs={{0,1},{1,0},{2,3},{3,2},{4,5},{5,4},{6,7},{7,6},{8,9},{9,8},{10,11... | collective-permute-start | bytes 786440 | tf_op jit(solution)/shard_map/ppermute | solution.py:391
  33.2 10.1 %collective-permute-start.10 = (bf16[512,256]{1,0:T(8,128)(2,1)S(1)}, bf16[512,256]{1,0:T(8,128)(2,1)S(1)}, u32[]{:S(2)}, u32[]{:S(2)}) collective-permute-start(bf16[512,256]{1,0:T(8,128)(2,1)S(1)} %get-tuple-element.63), channel_id=1, source_target_pairs={{0,1},{1,0},{2,3},{3,2},{4,5},{5,4},{6,7},{7,6},{8,9},{9,8},{10,11... | collective-permute-start | bytes 786440 | tf_op jit(solution)/shard_map/ppermute | solution.py:391
  33.2 10.0 %collective-permute-start.11 = (bf16[512,256]{1,0:T(8,128)(2,1)S(1)}, bf16[512,256]{1,0:T(8,128)(2,1)S(1)}, u32[]{:S(2)}, u32[]{:S(2)}) collective-permute-start(bf16[512,256]{1,0:T(8,128)(2,1)S(1)} %get-tuple-element.64), channel_id=1, source_target_pairs={{0,1},{1,0},{2,3},{3,2},{4,5},{5,4},{6,7},{7,6},{8,9},{9,8},{10,11... | collective-permute-start | bytes 786440 | tf_op jit(solution)/shard_map/ppermute | solution.py:391
  35.3 5.0 %collective-permute-start.13 = (bf16[128,512]{1,0:T(8,128)(2,1)S(1)}, bf16[128,512]{1,0:T(8,128)(2,1)S(1)}, u32[]{:S(2)}, u32[]{:S(2)}) collective-permute-start(bf16[128,512]{1,0:T(8,128)(2,1)S(1)} %shard_map.81.refs_0_), channel_id=1, source_target_pairs={{0,8},{4,12},{8,0},{12,4},{16,24},{20,28},{24,16},{28,20},{1,9},{5... | collective-permute-start | bytes 393224 | tf_op jit(solution)/shard_map/ppermute | solution.py:394
  40.4 7.5 %collective-permute-start.14 = (bf16[128,512]{1,0:T(8,128)(2,1)S(1)}, bf16[128,512]{1,0:T(8,128)(2,1)S(1)}, u32[]{:S(2)}, u32[]{:S(2)}) collective-permute-start(bf16[128,512]{1,0:T(8,128)(2,1)S(1)} %shard_map.83), channel_id=1, source_target_pairs={{0,16},{4,20},{8,24},{12,28},{16,0},{20,4},{24,8},{28,12},{1,17},{... | collective-permute-start | bytes 393224 | tf_op jit(solution)/shard_map/ppermute | solution.py:394
  48.2 1.4 %collective-permute-start.15 = (bf16[128,512]{1,0:T(8,128)(2,1)S(1)}, bf16[128,512]{1,0:T(8,128)(2,1)S(1)}, u32[]{:S(2)}, u32[]{:S(2)}) collective-permute-start(bf16[128,512]{1,0:T(8,128)(2,1)S(1)} %shard_map.84.refs_3_.refs_0_), channel_id=1, source_target_pairs={{0,1},{1,0},{2,3},{3,2},{4,5},{5,4},{6,7},{7,6},{8,9},{9,8},{10,11... | collective-permute-start | bytes 393224 | tf_op jit(solution)/shard_map/ppermute | solution.py:391
  48.9 2.9 %collective-permute-start.16 = (bf16[128,512]{1,0:T(8,128)(2,1)S(1)}, bf16[128,512]{1,0:T(8,128)(2,1)S(1)}, u32[]{:S(2)}, u32[]{:S(2)}) collective-permute-start(bf16[128,512]{1,0:T(8,128)(2,1)S(1)} %get-tuple-element.79.refs_2_.refs_0_), channel_id=1, source_target_pairs={{0,1},{1,0},{2,3},{3,2},{4,5},{5,4},{6,7},{7,6},{8,9},{9,8},{10,11... | collective-permute-start | bytes 393224 | tf_op jit(solution)/shard_map/ppermute | solution.py:391
  49.4 3.3 %collective-permute-start.17 = (bf16[128,512]{1,0:T(8,128)(2,1)S(1)}, bf16[128,512]{1,0:T(8,128)(2,1)S(1)}, u32[]{:S(2)}, u32[]{:S(2)}) collective-permute-start(bf16[128,512]{1,0:T(8,128)(2,1)S(1)} %get-tuple-element.80.refs_4_.refs_0_), channel_id=1, source_target_pairs={{0,1},{1,0},{2,3},{3,2},{4,5},{5,4},{6,7},{7,6},{8,9},{9,8},{10,11... | collective-permute-start | bytes 393224 | tf_op jit(solution)/shard_map/ppermute | solution.py:391
  50.1 10.8 %collective-permute-start.23 = (bf16[128,1024]{1,0:T(8,128)(2,1)S(1)}, bf16[128,1024]{1,0:T(8,128)(2,1)S(1)}, u32[]{:S(2)}, u32[]{:S(2)}) collective-permute-start(bf16[128,1024]{1,0:T(8,128)(2,1)S(1)} %shard_map.91), channel_id=1, source_target_pairs={{0,2},{1,3},{2,0},{3,1},{4,6},{5,7},{6,4},{7,5},{8,10},{9,11},{10,... | collective-permute-start | bytes 786440 | tf_op jit(solution)/shard_map/ppermute | solution.py:391
  52.2 12.7 %collective-permute-start.22 = (bf16[128,1024]{1,0:T(8,128)(2,1)S(1)}, bf16[128,1024]{1,0:T(8,128)(2,1)S(1)}, u32[]{:S(2)}, u32[]{:S(2)}) collective-permute-start(bf16[128,1024]{1,0:T(8,128)(2,1)S(1)} %shard_map.90), channel_id=1, source_target_pairs={{0,2},{1,3},{2,0},{3,1},{4,6},{5,7},{6,4},{7,5},{8,10},{9,11},{10,... | collective-permute-start | bytes 786440 | tf_op jit(solution)/shard_map/ppermute | solution.py:391
  53.2 17.3 %collective-permute-start.21 = (bf16[128,1024]{1,0:T(8,128)(2,1)S(1)}, bf16[128,1024]{1,0:T(8,128)(2,1)S(1)}, u32[]{:S(2)}, u32[]{:S(2)}) collective-permute-start(bf16[128,1024]{1,0:T(8,128)(2,1)S(1)} %shard_map.89), channel_id=1, source_target_pairs={{0,2},{1,3},{2,0},{3,1},{4,6},{5,7},{6,4},{7,5},{8,10},{9,11},{10,... | collective-permute-start | bytes 786440 | tf_op jit(solution)/shard_map/ppermute | solution.py:391
  54.9 2.3 %collective-permute-start.19 = (bf16[64,512]{1,0:T(8,128)(2,1)S(1)}, bf16[64,512]{1,0:T(8,128)(2,1)S(1)}, u32[]{:S(2)}, u32[]{:S(2)}) collective-permute-start(bf16[64,512]{1,0:T(8,128)(2,1)S(1)} %get-tuple-element.82.refs_0_.refs_8_), channel_id=1, source_target_pairs={{0,1},{1,0},{2,3},{3,2},{4,5},{5,4},{6,7},{7,6},{8,9},{9,8},{10,11... | collective-permute-start | bytes 196616 | tf_op jit(solution)/shard_map/ppermute | solution.py:391
  56.6 16.7 %collective-permute-start.20 = (bf16[64,1024]{1,0:T(8,128)(2,1)S(1)}, bf16[64,1024]{1,0:T(8,128)(2,1)S(1)}, u32[]{:S(2)}, u32[]{:S(2)}) collective-permute-start(bf16[64,1024]{1,0:T(8,128)(2,1)S(1)} %shard_map.88), channel_id=1, source_target_pairs={{0,2},{1,3},{2,0},{3,1},{4,6},{5,7},{6,4},{7,5},{8,10},{9,11},{10,... | collective-permute-start | bytes 393224 | tf_op jit(solution)/shard_map/ppermute | solution.py:391
  57.6 17.9 %collective-permute-start.24 = (bf16[64,1024]{1,0:T(8,128)(2,1)S(1)}, bf16[64,1024]{1,0:T(8,128)(2,1)S(1)}, u32[]{:S(2)}, u32[]{:S(2)}) collective-permute-start(bf16[64,1024]{1,0:T(8,128)(2,1)S(1)} %shard_map.86.refs_12_), channel_id=1, source_target_pairs={{0,2},{1,3},{2,0},{3,1},{4,6},{5,7},{6,4},{7,5},{8,10},{9,11},{10,... | collective-permute-start | bytes 393224 | tf_op jit(solution)/shard_map/ppermute | solution.py:391
  (3 other events, 2.9 us)

commit v19 on v18

--- a/solution.py
+++ b/solution.py
@@ -48,6 +48,21 @@
         compiler_params=pltpu.CompilerParams(vmem_limit_bytes=megabytes * 1024 * 1024),
         cost_estimate=pl.CostEstimate(flops=flops, bytes_accessed=nbytes, transcendentals=0),
     )(*ins, *after)
+
+
+def gate(x, *after):
+    def run(*refs):
+        pass
+
+    return pl.pallas_call(
+        run,
+        in_specs=[ANY] * (1 + len(after)),
+        out_specs=ANY,
+        out_shape=shape(x.shape, x.dtype),
+        input_output_aliases={0: 0},
+        compiler_params=pltpu.CompilerParams(vmem_limit_bytes=1024 * 1024),
+        cost_estimate=pl.CostEstimate(flops=0, bytes_accessed=0, transcendentals=0),
+    )(x, *after)
 
 
 def copies(pairs, sems):
@@ -101,13 +116,13 @@
     return call(kernel, ins, [shape(total.shape, F32)] * 5, 0, smem=1)
 
 
-def combine(state, other, own_factor, other_factor, after):
+def combine(state, other, own_factor, other_factor):
     def kernel(s_ref, o_ref, a_ref, b_ref, out_ref):
         out_ref[...] = (
             a_ref[0:1, :] * s_ref[...].astype(F32) + b_ref[0:1, :] * o_ref[...].astype(F32)
         ).astype(BF16)
 
-    return call(kernel, [state, other, own_factor, other_factor], [shape(state.shape, BF16)], 0, after)[0]
+    return call(kernel, [state, other, own_factor, other_factor], [shape(state.shape, BF16)], 0)[0]
 
 
 def begin(me, slab, tokens, near, log_decay_rows, ws, w_out, head_size):
@@ -187,25 +202,15 @@
     return dot_dims(x, wl_ref[:, pl.ds(start, shard)], 1, 1)
 
 
-def project(me, place, x, wq, wl, total_q, total_l, after):
-    def kernel(me_ref, x_ref, wq_ref, wl_ref, q_ref, l_ref, q_out, l_out):
-        q_out[...] = q_ref[...] + dot(x_ref[...], wq_ref[place - 2])
-        l_out[...] = l_ref[...] + add_levels(me_ref, place, x_ref[...], wl_ref)
-
-    outs = [shape(t.shape, F32) for t in (total_q, total_l)]
-    flops = 2 * x.size * (total_q.shape[1] + total_l.shape[1])
-    return call(kernel, [me, x, wq, wl, total_q, total_l], outs, flops, after, smem=1, aliases={4: 0, 5: 1})
-
-
-def split(x, ways, after):
-    rows, columns = x.shape
-    part = columns // ways
-
-    def kernel(x_ref, *outs):
-        for i, o_ref in enumerate(outs):
-            o_ref[...] = x_ref[:, i * part : (i + 1) * part]
-
-    return call(kernel, [x], [shape((rows, part), x.dtype)] * ways, 0, after)
+def project(me, place, x, wq, wkv, wl, totals, after=()):
+    def kernel(me_ref, x_ref, q_ref, kv_ref, l_ref, *refs):
+        ins, outs = refs[:3], refs[3:]
+        outs[1][...] = ins[1][...] + dot(x_ref[...], kv_ref[...])
+        outs[0][...] = ins[0][...] + dot(x_ref[...], q_ref[place - 2])
+        outs[2][...] = ins[2][...] + add_levels(me_ref, place, x_ref[...], l_ref)
+
+    outs = [shape(t.shape, F32) for t in totals]
+    return call(kernel, [me, x, wq, wkv, wl, *totals], outs, 0, after, smem=1, aliases={5: 0, 6: 1, 7: 2})
 
 
 def partial(x, w, after):
@@ -213,13 +218,6 @@
         o_ref[...] = dot(x_ref[...], w_ref[...]).astype(BF16)
 
     return call(kernel, [x, w], [shape((x.shape[0], w.shape[1]), BF16)], 0, after)[0]
-
-
-def add_product(x, w, total, after):
-    def kernel(x_ref, w_ref, t_ref, o_ref):
-        o_ref[...] = t_ref[...] + dot(x_ref[...], w_ref[...])
-
-    return call(kernel, [x, w, total], [shape(total.shape, F32)], 0, after, aliases={2: 0})[0]
 
 
 def project_state(total_kv, from_near, keep, head_size):
@@ -411,25 +409,21 @@
 
     wq, wkv, wkv_send, wl = ws
     wkv_near = swap_tp(wkv_send, 1)
-    arrived = far
-    for_near = partial(arrived, wkv_near, (total, w_far, w_here))
+    for_near = partial(far, wkv_near, (total, w_far, w_here))
     from_near = swap_tp(for_near, 1)
-    total_q, total_kv, total_l = totals
-    total_kv = add_product(arrived, wkv, total_kv, (for_near,))
+    total_q, total_kv, total_l = project(me, 2, far, wq, wkv, wl, totals, (for_near,))
+    far_near = swap_tp(gate(far, total_q, from_near), 1)
     k, v, state = project_state(total_kv, from_near, keep, head_size)
-    total_q, total_l = project(me, 2, arrived, wq, wl, total_q, total_l, (k,))
-    arrived_near = [swap_tp(x, 1) for x in split(arrived, 4, (total_l,))]
 
     earlier = []
     for b in range(seq_bits):
         other = swap_seq(state, 1 << b)
         earlier.append(other)
         if b < seq_bits - 1:
-            after = () if b else (total_l,)
-            state = combine(state, other, *factors[b], after)
+            state = combine(state, other, *factors[b])
 
     local, scaled = attend(
-        me, 3, arrived_near, wq, wl, total_q, total_l, k, v, dcol, drow, spans, earlier[:-1], head_size, level_count
+        me, 3, [far_near], wq, wl, total_q, total_l, k, v, dcol, drow, spans, earlier[:-1], head_size, level_count
     )
 
     unit = rows // 8

time: 76.4 us -> 76.8 us (level)
  waiting for transfers between devices: 29.8 us -> 31.1 us
    ppermute x5, waiting for transfers between devices: 8.77 us -> 11 us  [swap_seq(): return lax.ppermute(x, 'seq', [(i, i ^ bit) for i in range(seq_size)])]
    ppermute x20 -> x17, waiting for transfers between devices: 21 us -> 20.1 us  [swap_tp(): return lax.ppermute(x, 'tp', [(i, i ^ bit) for i in range(4)])]
    ppermute x20 -> x17, starting transfers between devices: 12.2 us -> 11.5 us  [swap_tp(): return lax.ppermute(x, 'tp', [(i, i ^ bit) for i in range(4)])]
    pallas_call x19 -> x17, Pallas kernels: 17.5 us -> 17.3 us  [call(): pl.pallas_call(run, in_specs=[SMEM] * smem + [HBM] * hbm + [VMEM] * (coun...]
  transfers between devices with their start and end apart: 25 -> 22, of which waited for: 13 -> 13; matrix products, arithmetic and copies ran while one was open for 0% -> 0% of each run, Pallas kernels for 25% -> 25%
where the time goes in v19:
time: 76.8 us; the launch traced here: 76.6 us
  waiting for transfers between devices  31.1 us (40%)
  starting transfers between devices  22.9 us (30%)
  Pallas kernels  20.2 us (26%)
  local copies, waits for them, and re-layouts  1.62 us (2%)
    ppermute x17, waiting for transfers between devices, swap_tp(): return lax.ppermute(x, 'tp', [(i, i ^ bit) for i in range(4)])  20.1 us
    pallas_call x17, Pallas kernels, call(): pl.pallas_call(run, in_specs=[SMEM] * smem + [HBM] * hbm + [VMEM] * (coun...  17.3 us
    ppermute x17, starting transfers between devices, swap_tp(): return lax.ppermute(x, 'tp', [(i, i ^ bit) for i in range(4)])  11.5 us
    ppermute x5, starting transfers between devices, swap_seq(): return lax.ppermute(x, 'seq', [(i, i ^ bit) for i in range(seq_size)])  11.3 us
    ppermute x5, waiting for transfers between devices, swap_seq(): return lax.ppermute(x, 'seq', [(i, i ^ bit) for i in range(seq_size)])  11 us
    pallas_call x4, Pallas kernels, add_rows(): pl.pallas_call(kernel, grid=(rows // unit,), in_specs=specs, out_specs=pl...  2.88 us
    unnamed x4, local copies, waits for them, and re-layouts  1.62 us
  transfers between devices with their start and end apart: 22, of which 13 were waited for; matrix products, arithmetic and copies ran while one was open for 0% of the time, Pallas kernels for 25%

profile of v19, /device:TPU:0, one launch (start us, length us, event | category | flops | bytes accessed | tf_op | source)
XLA Modules:
  0.0 76.6 jit_solution(9752828860814670415)
XLA Ops:
  0.5 2.5 %collective-permute-start = (bf16[512,1024]{1,0:T(8,128)(2,1)}, bf16[512,1024]{1,0:T(8,128)(2,1)S(1)}, u32[]{:S(2)}, u32[]{:S(2)}) collective-permute-start(bf16[512,1024]{1,0:T(8,128)(2,1)} %refs_2_.1), channel_id=1, source_target_pairs={{0,2},{1,3},{2,0},{3,1},{4,6},{5,7},{6,4},{7,5},{8,10},{9,11},{10,... | collective-permute-start | bytes 3145736 | tf_op jit(solution)/shard_map/ppermute | solution.py:389
  3.0 0.9 %copy-done = bf16[4096,24]{0,1:T(8,128)(2,1)S(1)} copy-done((bf16[4096,24]{0,1:T(8,128)(2,1)S(1)}, bf16[4096,24]{0,1:T(8,128)(2,1)}, u32[]{:S(2)}) %copy-start) | copy-done | bytes 196632
  4.6 5.3 %shard_map.73 = (f32[512,512]{1,0:T(8,128)S(1)}, f32[512,256]{1,0:T(8,128)S(1)}, f32[512,24]{1,0:T(8,128)S(1)}, bf16[2,1024,512]{2,1,0:T(8,128)(2,1)S(1)}, bf16[...) custom-call(s32[1]{0:T(128)} %bitcast.refs_0_, ...), custom_call_target="tpu_custom_call" | custom-call | tf_op jit(solution)/shard_map/pallas_call | solution.py:41
  10.8 2.6 %collective-permute-start.3 = (f32[8,512]{1,0:T(8,128)S(1)}, f32[8,512]{1,0:T(8,128)S(1)}, u32[]{:S(2)}, u32[]{:S(2)}) collective-permute-start(f32[8,512]{1,0:T(8,128)S(1)} %get-tuple-element.49.refs_1_), channel_id=1, source_target_pairs={{0,4},{4,0},{8,12},{12,8},{16,20},{20,16},{24,28},{28,24},{1,5},{5... | collective-permute-start | bytes 49160 | tf_op jit(solution)/shard_map/ppermute | solution.py:392
  13.4 1.7 %collective-permute-done.3.refs_2_ = f32[8,512]{1,0:T(8,128)S(1)} collective-permute-done((f32[8,512]{1,0:T(8,128)S(1)}, f32[8,512]{1,0:T(8,128)S(1)}, u32[]{:S(2)}, u32[]{:S(2)}) %collective-permute-start.3) | collective-permute-done | bytes 16416 | tf_op jit(solution)/shard_map/ppermute | solution.py:392
  15.2 2.2 %collective-permute-start.4 = (f32[8,512]{1,0:T(8,128)S(1)}, f32[8,512]{1,0:T(8,128)S(1)}, u32[]{:S(2)}, u32[]{:S(2)}) collective-permute-start(f32[8,512]{1,0:T(8,128)S(1)} %get-tuple-element.50.refs_1_), channel_id=1, source_target_pairs={{0,8},{4,12},{8,0},{12,4},{16,24},{20,28},{24,16},{28,20},{1,9},{5... | collective-permute-start | bytes 49160 | tf_op jit(solution)/shard_map/ppermute | solution.py:392
  17.3 1.7 %collective-permute-done.4.refs_2_ = f32[8,512]{1,0:T(8,128)S(1)} collective-permute-done((f32[8,512]{1,0:T(8,128)S(1)}, f32[8,512]{1,0:T(8,128)S(1)}, u32[]{:S(2)}, u32[]{:S(2)}) %collective-permute-start.4) | collective-permute-done | bytes 16416 | tf_op jit(solution)/shard_map/ppermute | solution.py:392
  19.7 7.3 %collective-permute-done.refs_0_.refs_1_ = bf16[512,1024]{1,0:T(8,128)(2,1)S(1)} collective-permute-done((bf16[512,1024]{1,0:T(8,128)(2,1)}, bf16[512,1024]{1,0:T(8,128)(2,1)S(1)}, u32[]{:S(2)}, u32[]{:S(2)}) %collective-permute-start) | collective-permute-done | bytes 1048608 | tf_op jit(solution)/shard_map/ppermute | solution.py:389
  27.5 1.3 %shard_map.77 = (f32[512,512]{1,0:T(8,128)S(1)}, f32[512,256]{1,0:T(8,128)S(1)}, f32[512,24]{1,0:T(8,128)S(1)}) custom-call(s32[1]{0:T(128)} %bitcast.refs_0_, bf16[512,1024]{1,0:T(8,128)(2,1)S(1)} %collective-permute-done.refs_0_.refs_1_, ...), custom_call_target="tpu_custom_call", output_to_operand_aliasing={{0}: (5, {}), {1}: (6, {}), {2}: (7, {})} | custom-call | tf_op jit(solution)/shard_map/pallas_call | solution.py:41
  30.0 1.8 %collective-permute-start.9 = (bf16[128,512]{1,0:T(8,128)(2,1)S(1)}, bf16[128,512]{1,0:T(8,128)(2,1)S(1)}, u32[]{:S(2)}, u32[]{:S(2)}) collective-permute-start(bf16[128,512]{1,0:T(8,128)(2,1)S(1)} %get-tuple-element.66.refs_0_), channel_id=1, source_target_pairs={{0,4},{4,0},{8,12},{12,8},{16,20},{20,16},{24,28},{28,24},{1,5},{5... | collective-permute-start | bytes 393224 | tf_op jit(solution)/shard_map/ppermute | solution.py:392
  31.8 3.8 %collective-permute-done.9.refs_1_.refs_13_ = bf16[128,512]{1,0:T(8,128)(2,1)S(1)} collective-permute-done((bf16[128,512]{1,0:T(8,128)(2,1)S(1)}, bf16[128,512]{1,0:T(8,128)(2,1)S(1)}, u32[]{:S(2)}, u32[]{:S(2)}) %collective-permute-start.9) | collective-permute-done | bytes 131104 | tf_op jit(solution)/shard_map/ppermute | solution.py:392
  35.7 1.9 %collective-permute-start.10 = (bf16[128,512]{1,0:T(8,128)(2,1)S(1)}, bf16[128,512]{1,0:T(8,128)(2,1)S(1)}, u32[]{:S(2)}, u32[]{:S(2)}) collective-permute-start(bf16[128,512]{1,0:T(8,128)(2,1)S(1)} %shard_map.80.refs_0_), channel_id=1, source_target_pairs={{0,8},{4,12},{8,0},{12,4},{16,24},{20,28},{24,16},{28,20},{1,9},{5... | collective-permute-start | bytes 393224 | tf_op jit(solution)/shard_map/ppermute | solution.py:392
  37.6 3.2 %collective-permute-done.10.refs_14_.refs_1_ = bf16[128,512]{1,0:T(8,128)(2,1)S(1)} collective-permute-done((bf16[128,512]{1,0:T(8,128)(2,1)S(1)}, bf16[128,512]{1,0:T(8,128)(2,1)S(1)}, u32[]{:S(2)}, u32[]{:S(2)}) %collective-permute-start.10) | collective-permute-done | bytes 131104 | tf_op jit(solution)/shard_map/ppermute | solution.py:392
  40.8 2.9 %collective-permute-start.11 = (bf16[128,512]{1,0:T(8,128)(2,1)S(1)}, bf16[128,512]{1,0:T(8,128)(2,1)S(1)}, u32[]{:S(2)}, u32[]{:S(2)}) collective-permute-start(bf16[128,512]{1,0:T(8,128)(2,1)S(1)} %shard_map.82), channel_id=1, source_target_pairs={{0,16},{4,20},{8,24},{12,28},{16,0},{20,4},{24,8},{28,12},{1,17},{... | collective-permute-start | bytes 393224 | tf_op jit(solution)/shard_map/ppermute | solution.py:392
  43.7 4.0 %shard_map.81 = (f32[512,512]{1,0:T(8,128)S(1)}, bf16[512,512]{1,0:T(8,128)(2,1)S(1)}, bf16[512,512]{1,0:T(8,128)(2,1)}, f32[512,24]{1,0:T(8,128)}) custom-call(s32[1]{0:T(128)} %bitcast.refs_0_, bf16[512,1024]{1,0:T(8,128)(2,1)S(1)} %collective-permute-done.8.refs_1_, bf16[2,1024,512]{2,1,0:T(8,128)(2,1)S(1)} %get-tuple-element.42.refs_2_, ...), custom_call_target="tpu_custom_call" | custom-call | flops 1073741824 | bytes 7176196 | tf_op jit(solution)/shard_map/pallas_call | solution.py:41
  50.5 1.7 %collective-permute-start.20 = (bf16[128,1024]{1,0:T(8,128)(2,1)S(1)}, bf16[128,1024]{1,0:T(8,128)(2,1)S(1)}, u32[]{:S(2)}, u32[]{:S(2)}) collective-permute-start(bf16[128,1024]{1,0:T(8,128)(2,1)S(1)} %shard_map.90), channel_id=1, source_target_pairs={{0,2},{1,3},{2,0},{3,1},{4,6},{5,7},{6,4},{7,5},{8,10},{9,11},{10,... | collective-permute-start | bytes 786440 | tf_op jit(solution)/shard_map/ppermute | solution.py:389
  53.6 1.7 %collective-permute-start.18 = (bf16[128,1024]{1,0:T(8,128)(2,1)S(1)}, bf16[128,1024]{1,0:T(8,128)(2,1)S(1)}, u32[]{:S(2)}, u32[]{:S(2)}) collective-permute-start(bf16[128,1024]{1,0:T(8,128)(2,1)S(1)} %shard_map.88), channel_id=1, source_target_pairs={{0,2},{1,3},{2,0},{3,1},{4,6},{5,7},{6,4},{7,5},{8,10},{9,11},{10,... | collective-permute-start | bytes 786440 | tf_op jit(solution)/shard_map/ppermute | solution.py:389
  58.0 1.7 %collective-permute-start.21 = (bf16[64,1024]{1,0:T(8,128)(2,1)S(1)}, bf16[64,1024]{1,0:T(8,128)(2,1)S(1)}, u32[]{:S(2)}, u32[]{:S(2)}) collective-permute-start(bf16[64,1024]{1,0:T(8,128)(2,1)S(1)} %shard_map.85.refs_12_), channel_id=1, source_target_pairs={{0,2},{1,3},{2,0},{3,1},{4,6},{5,7},{6,4},{7,5},{8,10},{9,11},{10,... | collective-permute-start | bytes 393224 | tf_op jit(solution)/shard_map/ppermute | solution.py:389
  59.7 1.7 %shard_map.86.h_ref = f32[512,1024]{1,0:T(8,128)S(1)} custom-call(bf16[128,512]{1,0:T(8,128)(2,1)S(1)} %shard_map.83.refs_3_.refs_0_, bf16[128,512]{1,0:T(8,128)(2,1)S(1)} %collective-permute-done.12.refs_1_, bf16[128,512]{1,0:T(8,128)(2,1)S(1)} %get-tuple-element.73.refs_2_.refs_0_, bf16[128,512]{1,0:T(8,128)(2,1)S(1)} %collective-permute-done.13.refs_3_.refs_1_, ...), custom_call_target="tpu_custom_call" | custom-call | tf_op jit(solution)/shard_map/pallas_call | solution.py:41
  61.4 0.8 shard_map.91.refs_0_
  62.1 3.2 %collective-permute-done.19.a_ref = bf16[128,1024]{1,0:T(8,128)(2,1)S(1)} collective-permute-done((bf16[128,1024]{1,0:T(8,128)(2,1)S(1)}, bf16[128,1024]{1,0:T(8,128)(2,1)S(1)}, u32[]{:S(2)}, u32[]{:S(2)}) %collective-permute-start.19) | collective-permute-done | bytes 262176 | tf_op jit(solution)/shard_map/ppermute | solution.py:389
  66.0 4.9 %collective-permute-done.18.a_ref = bf16[128,1024]{1,0:T(8,128)(2,1)S(1)} collective-permute-done((bf16[128,1024]{1,0:T(8,128)(2,1)S(1)}, bf16[128,1024]{1,0:T(8,128)(2,1)S(1)}, u32[]{:S(2)}, u32[]{:S(2)}) %collective-permute-start.18) | collective-permute-done | bytes 262176 | tf_op jit(solution)/shard_map/ppermute | solution.py:389
  71.6 2.1 %collective-permute-done.17.a_ref = bf16[64,1024]{1,0:T(8,128)(2,1)S(1)} collective-permute-done((bf16[64,1024]{1,0:T(8,128)(2,1)S(1)}, bf16[64,1024]{1,0:T(8,128)(2,1)S(1)}, u32[]{:S(2)}, u32[]{:S(2)}) %collective-permute-start.17) | collective-permute-done | bytes 131104 | tf_op jit(solution)/shard_map/ppermute | solution.py:389
  74.4 1.5 %collective-permute-done.21 = bf16[64,1024]{1,0:T(8,128)(2,1)S(1)} collective-permute-done((bf16[64,1024]{1,0:T(8,128)(2,1)S(1)}, bf16[64,1024]{1,0:T(8,128)(2,1)S(1)}, u32[]{:S(2)}, u32[]{:S(2)}) %collective-permute-start.21) | collective-permute-done | bytes 131104 | tf_op jit(solution)/shard_map/ppermute | solution.py:389
  (47 shorter events, 14.3 us)
Async XLA Ops:
  0.0 3.0 %collective-permute-start.1 = (bf16[512,1024]{1,0:T(8,128)(2,1)}, bf16[512,1024]{1,0:T(8,128)(2,1)S(1)}, u32[]{:S(2)}, u32[]{:S(2)}) collective-permute-start(bf16[512,1024]{1,0:T(8,128)(2,1)} %refs_2_.1), channel_id=1, source_target_pairs={{0,1},{1,0},{2,3},{3,2},{4,5},{5,4},{6,7},{7,6},{8,9},{9,8},{10,11... | collective-permute-start | bytes 3145736 | tf_op jit(solution)/shard_map/ppermute | solution.py:389
  0.5 26.6 %collective-permute-start = (bf16[512,1024]{1,0:T(8,128)(2,1)}, bf16[512,1024]{1,0:T(8,128)(2,1)S(1)}, u32[]{:S(2)}, u32[]{:S(2)}) collective-permute-start(bf16[512,1024]{1,0:T(8,128)(2,1)} %refs_2_.1), channel_id=1, source_target_pairs={{0,2},{1,3},{2,0},{3,1},{4,6},{5,7},{6,4},{7,5},{8,10},{9,11},{10,... | collective-permute-start | bytes 3145736 | tf_op jit(solution)/shard_map/ppermute | solution.py:389
  3.0 0.9 %copy-start = (bf16[4096,24]{0,1:T(8,128)(2,1)S(1)}, bf16[4096,24]{0,1:T(8,128)(2,1)}, u32[]{:S(2)}) copy-start(bf16[4096,24]{0,1:T(8,128)(2,1)} %param.12) | copy-start | bytes 589828
  3.9 0.7 copy-start.1
  9.9 17.1 %collective-permute-start.5 = (bf16[512,1024]{1,0:T(8,128)(2,1)S(1)}, bf16[512,1024]{1,0:T(8,128)(2,1)S(1)}, u32[]{:S(2)}, u32[]{:S(2)}) collective-permute-start(bf16[512,1024]{1,0:T(8,128)(2,1)S(1)} %get-tuple-element.53), channel_id=1, source_target_pairs={{0,1},{1,0},{2,3},{3,2},{4,5},{5,4},{6,7},{7,6},{8,9},{9,8},{10,11... | collective-permute-start | bytes 3145736 | tf_op jit(solution)/shard_map/ppermute | solution.py:389
  10.3 16.7 %collective-permute-start.6 = (bf16[512,1024]{1,0:T(8,128)(2,1)S(1)}, bf16[512,1024]{1,0:T(8,128)(2,1)S(1)}, u32[]{:S(2)}, u32[]{:S(2)}) collective-permute-start(bf16[512,1024]{1,0:T(8,128)(2,1)S(1)} %get-tuple-element.54), channel_id=1, source_target_pairs={{0,1},{1,0},{2,3},{3,2},{4,5},{5,4},{6,7},{7,6},{8,9},{9,8},{10,11... | collective-permute-start | bytes 3145736 | tf_op jit(solution)/shard_map/ppermute | solution.py:389
  10.5 16.6 %collective-permute-start.2 = (bf16[1024,256]{1,0:T(8,128)(2,1)S(1)}, bf16[1024,256]{1,0:T(8,128)(2,1)S(1)}, u32[]{:S(2)}, u32[]{:S(2)}) collective-permute-start(bf16[1024,256]{1,0:T(8,128)(2,1)S(1)} %get-tuple-element.48), channel_id=1, source_target_pairs={{0,1},{1,0},{2,3},{3,2},{4,5},{5,4},{6,7},{7,6},{8,9},{9,8},{10,11... | collective-permute-start | bytes 1572872 | tf_op jit(solution)/shard_map/ppermute | solution.py:389
  10.8 4.3 %collective-permute-start.3 = (f32[8,512]{1,0:T(8,128)S(1)}, f32[8,512]{1,0:T(8,128)S(1)}, u32[]{:S(2)}, u32[]{:S(2)}) collective-permute-start(f32[8,512]{1,0:T(8,128)S(1)} %get-tuple-element.49.refs_1_), channel_id=1, source_target_pairs={{0,4},{4,0},{8,12},{12,8},{16,20},{20,16},{24,28},{28,24},{1,5},{5... | collective-permute-start | bytes 49160 | tf_op jit(solution)/shard_map/ppermute | solution.py:392
  15.2 3.9 %collective-permute-start.4 = (f32[8,512]{1,0:T(8,128)S(1)}, f32[8,512]{1,0:T(8,128)S(1)}, u32[]{:S(2)}, u32[]{:S(2)}) collective-permute-start(f32[8,512]{1,0:T(8,128)S(1)} %get-tuple-element.50.refs_1_), channel_id=1, source_target_pairs={{0,8},{4,12},{8,0},{12,4},{16,24},{20,28},{24,16},{28,20},{1,9},{5... | collective-permute-start | bytes 49160 | tf_op jit(solution)/shard_map/ppermute | solution.py:392
  27.5 1.6 %collective-permute-start.7 = (bf16[512,256]{1,0:T(8,128)(2,1)S(1)}, bf16[512,256]{1,0:T(8,128)(2,1)S(1)}, u32[]{:S(2)}, u32[]{:S(2)}) collective-permute-start(bf16[512,256]{1,0:T(8,128)(2,1)S(1)} %shard_map.76.refs_8_), channel_id=1, source_target_pairs={{0,1},{1,0},{2,3},{3,2},{4,5},{5,4},{6,7},{7,6},{8,9},{9,8},{10,11... | collective-permute-start | bytes 786440 | tf_op jit(solution)/shard_map/ppermute | solution.py:389
  29.1 14.6 %collective-permute-start.8 = (bf16[512,1024]{1,0:T(8,128)(2,1)S(1)}, bf16[512,1024]{1,0:T(8,128)(2,1)S(1)}, u32[]{:S(2)}, u32[]{:S(2)}) collective-permute-start(bf16[512,1024]{1,0:T(8,128)(2,1)S(1)} %shard_map.78), channel_id=1, source_target_pairs={{0,1},{1,0},{2,3},{3,2},{4,5},{5,4},{6,7},{7,6},{8,9},{9,8},{10,11... | collective-permute-start | bytes 3145736 | tf_op jit(solution)/shard_map/ppermute | solution.py:389
  30.0 5.6 %collective-permute-start.9 = (bf16[128,512]{1,0:T(8,128)(2,1)S(1)}, bf16[128,512]{1,0:T(8,128)(2,1)S(1)}, u32[]{:S(2)}, u32[]{:S(2)}) collective-permute-start(bf16[128,512]{1,0:T(8,128)(2,1)S(1)} %get-tuple-element.66.refs_0_), channel_id=1, source_target_pairs={{0,4},{4,0},{8,12},{12,8},{16,20},{20,16},{24,28},{28,24},{1,5},{5... | collective-permute-start | bytes 393224 | tf_op jit(solution)/shard_map/ppermute | solution.py:392
  35.7 5.0 %collective-permute-start.10 = (bf16[128,512]{1,0:T(8,128)(2,1)S(1)}, bf16[128,512]{1,0:T(8,128)(2,1)S(1)}, u32[]{:S(2)}, u32[]{:S(2)}) collective-permute-start(bf16[128,512]{1,0:T(8,128)(2,1)S(1)} %shard_map.80.refs_0_), channel_id=1, source_target_pairs={{0,8},{4,12},{8,0},{12,4},{16,24},{20,28},{24,16},{28,20},{1,9},{5... | collective-permute-start | bytes 393224 | tf_op jit(solution)/shard_map/ppermute | solution.py:392
  40.8 7.5 %collective-permute-start.11 = (bf16[128,512]{1,0:T(8,128)(2,1)S(1)}, bf16[128,512]{1,0:T(8,128)(2,1)S(1)}, u32[]{:S(2)}, u32[]{:S(2)}) collective-permute-start(bf16[128,512]{1,0:T(8,128)(2,1)S(1)} %shard_map.82), channel_id=1, source_target_pairs={{0,16},{4,20},{8,24},{12,28},{16,0},{20,4},{24,8},{28,12},{1,17},{... | collective-permute-start | bytes 393224 | tf_op jit(solution)/shard_map/ppermute | solution.py:392
  48.6 1.4 %collective-permute-start.12 = (bf16[128,512]{1,0:T(8,128)(2,1)S(1)}, bf16[128,512]{1,0:T(8,128)(2,1)S(1)}, u32[]{:S(2)}, u32[]{:S(2)}) collective-permute-start(bf16[128,512]{1,0:T(8,128)(2,1)S(1)} %shard_map.83.refs_3_.refs_0_), channel_id=1, source_target_pairs={{0,1},{1,0},{2,3},{3,2},{4,5},{5,4},{6,7},{7,6},{8,9},{9,8},{10,11... | collective-permute-start | bytes 393224 | tf_op jit(solution)/shard_map/ppermute | solution.py:389
  49.2 2.9 %collective-permute-start.13 = (bf16[128,512]{1,0:T(8,128)(2,1)S(1)}, bf16[128,512]{1,0:T(8,128)(2,1)S(1)}, u32[]{:S(2)}, u32[]{:S(2)}) collective-permute-start(bf16[128,512]{1,0:T(8,128)(2,1)S(1)} %get-tuple-element.73.refs_2_.refs_0_), channel_id=1, source_target_pairs={{0,1},{1,0},{2,3},{3,2},{4,5},{5,4},{6,7},{7,6},{8,9},{9,8},{10,11... | collective-permute-start | bytes 393224 | tf_op jit(solution)/shard_map/ppermute | solution.py:389
  49.8 3.3 %collective-permute-start.14 = (bf16[128,512]{1,0:T(8,128)(2,1)S(1)}, bf16[128,512]{1,0:T(8,128)(2,1)S(1)}, u32[]{:S(2)}, u32[]{:S(2)}) collective-permute-start(bf16[128,512]{1,0:T(8,128)(2,1)S(1)} %get-tuple-element.74.refs_4_.refs_0_), channel_id=1, source_target_pairs={{0,1},{1,0},{2,3},{3,2},{4,5},{5,4},{6,7},{7,6},{8,9},{9,8},{10,11... | collective-permute-start | bytes 393224 | tf_op jit(solution)/shard_map/ppermute | solution.py:389
  50.5 10.9 %collective-permute-start.20 = (bf16[128,1024]{1,0:T(8,128)(2,1)S(1)}, bf16[128,1024]{1,0:T(8,128)(2,1)S(1)}, u32[]{:S(2)}, u32[]{:S(2)}) collective-permute-start(bf16[128,1024]{1,0:T(8,128)(2,1)S(1)} %shard_map.90), channel_id=1, source_target_pairs={{0,2},{1,3},{2,0},{3,1},{4,6},{5,7},{6,4},{7,5},{8,10},{9,11},{10,... | collective-permute-start | bytes 786440 | tf_op jit(solution)/shard_map/ppermute | solution.py:389
  52.6 12.7 %collective-permute-start.19 = (bf16[128,1024]{1,0:T(8,128)(2,1)S(1)}, bf16[128,1024]{1,0:T(8,128)(2,1)S(1)}, u32[]{:S(2)}, u32[]{:S(2)}) collective-permute-start(bf16[128,1024]{1,0:T(8,128)(2,1)S(1)} %shard_map.89), channel_id=1, source_target_pairs={{0,2},{1,3},{2,0},{3,1},{4,6},{5,7},{6,4},{7,5},{8,10},{9,11},{10,... | collective-permute-start | bytes 786440 | tf_op jit(solution)/shard_map/ppermute | solution.py:389
  53.6 17.3 %collective-permute-start.18 = (bf16[128,1024]{1,0:T(8,128)(2,1)S(1)}, bf16[128,1024]{1,0:T(8,128)(2,1)S(1)}, u32[]{:S(2)}, u32[]{:S(2)}) collective-permute-start(bf16[128,1024]{1,0:T(8,128)(2,1)S(1)} %shard_map.88), channel_id=1, source_target_pairs={{0,2},{1,3},{2,0},{3,1},{4,6},{5,7},{6,4},{7,5},{8,10},{9,11},{10,... | collective-permute-start | bytes 786440 | tf_op jit(solution)/shard_map/ppermute | solution.py:389
  55.3 1.3 %collective-permute-start.15 = (bf16[64,512]{1,0:T(8,128)(2,1)S(1)}, bf16[64,512]{1,0:T(8,128)(2,1)S(1)}, u32[]{:S(2)}, u32[]{:S(2)}) collective-permute-start(bf16[64,512]{1,0:T(8,128)(2,1)S(1)} %get-tuple-element.75.refs_6_.refs_0_), channel_id=1, source_target_pairs={{0,1},{1,0},{2,3},{3,2},{4,5},{5,4},{6,7},{7,6},{8,9},{9,8},{10,11... | collective-permute-start | bytes 196616 | tf_op jit(solution)/shard_map/ppermute | solution.py:389
  55.3 2.2 %collective-permute-start.16 = (bf16[64,512]{1,0:T(8,128)(2,1)S(1)}, bf16[64,512]{1,0:T(8,128)(2,1)S(1)}, u32[]{:S(2)}, u32[]{:S(2)}) collective-permute-start(bf16[64,512]{1,0:T(8,128)(2,1)S(1)} %get-tuple-element.76.refs_0_.refs_8_), channel_id=1, source_target_pairs={{0,1},{1,0},{2,3},{3,2},{4,5},{5,4},{6,7},{7,6},{8,9},{9,8},{10,11... | collective-permute-start | bytes 196616 | tf_op jit(solution)/shard_map/ppermute | solution.py:389
  57.0 16.7 %collective-permute-start.17 = (bf16[64,1024]{1,0:T(8,128)(2,1)S(1)}, bf16[64,1024]{1,0:T(8,128)(2,1)S(1)}, u32[]{:S(2)}, u32[]{:S(2)}) collective-permute-start(bf16[64,1024]{1,0:T(8,128)(2,1)S(1)} %shard_map.87), channel_id=1, source_target_pairs={{0,2},{1,3},{2,0},{3,1},{4,6},{5,7},{6,4},{7,5},{8,10},{9,11},{10,... | collective-permute-start | bytes 393224 | tf_op jit(solution)/shard_map/ppermute | solution.py:389
  58.0 17.9 %collective-permute-start.21 = (bf16[64,1024]{1,0:T(8,128)(2,1)S(1)}, bf16[64,1024]{1,0:T(8,128)(2,1)S(1)}, u32[]{:S(2)}, u32[]{:S(2)}) collective-permute-start(bf16[64,1024]{1,0:T(8,128)(2,1)S(1)} %shard_map.85.refs_12_), channel_id=1, source_target_pairs={{0,2},{1,3},{2,0},{3,1},{4,6},{5,7},{6,4},{7,5},{8,10},{9,11},{10,... | collective-permute-start | bytes 393224 | tf_op jit(solution)/shard_map/ppermute | solution.py:389

commit v20 on v18

--- a/solution.py
+++ b/solution.py
@@ -433,7 +433,7 @@
     )
 
     unit = rows // 8
-    ends = (0, 2, 4, 6, 7, 8)
+    ends = (0, 3, 5, 7, 8)
     cuts = [slice(start * unit, stop * unit) for start, stop in zip(ends, ends[1:])]
     pieces = finish(local, scaled, earlier[-1], cuts[:1], head_size)
     pieces += finish(local, scaled, earlier[-1], cuts[1:], head_size, pieces)

time: 76.4 us -> 76.5 us (level)
  waiting for transfers between devices: 29.8 us -> 32.8 us
  starting transfers between devices: 23.6 us -> 21.3 us
    ppermute x20 -> x18, waiting for transfers between devices: 21 us -> 24 us  [swap_tp(): return lax.ppermute(x, 'tp', [(i, i ^ bit) for i in range(4)])]
    ppermute x20 -> x18, starting transfers between devices: 12.2 us -> 10 us  [swap_tp(): return lax.ppermute(x, 'tp', [(i, i ^ bit) for i in range(4)])]
    pallas_call x19 -> x18, Pallas kernels: 17.5 us -> 16.9 us  [call(): pl.pallas_call(run, in_specs=[SMEM] * smem + [HBM] * hbm + [VMEM] * (coun...]
    pallas_call x4 -> x3, Pallas kernels: 2.88 us -> 2.82 us  [add_rows(): pl.pallas_call(kernel, grid=(rows // unit,), in_specs=specs, out_specs=pl...]
  transfers between devices with their start and end apart: 25 -> 23, of which waited for: 13 -> 14; matrix products, arithmetic and copies ran while one was open for 0% -> 0% of each run, Pallas kernels for 25% -> 24%
where the time goes in v20:
time: 76.5 us; the launch traced here: 76.3 us
  waiting for transfers between devices  32.8 us (43%)
  starting transfers between devices  21.3 us (28%)
  Pallas kernels  19.7 us (26%)
  local copies, waits for them, and re-layouts  1.62 us (2%)
    ppermute x18, waiting for transfers between devices, swap_tp(): return lax.ppermute(x, 'tp', [(i, i ^ bit) for i in range(4)])  24 us
    pallas_call x18, Pallas kernels, call(): pl.pallas_call(run, in_specs=[SMEM] * smem + [HBM] * hbm + [VMEM] * (coun...  16.9 us
    ppermute x5, starting transfers between devices, swap_seq(): return lax.ppermute(x, 'seq', [(i, i ^ bit) for i in range(seq_size)])  11.3 us
    ppermute x18, starting transfers between devices, swap_tp(): return lax.ppermute(x, 'tp', [(i, i ^ bit) for i in range(4)])  10 us
    ppermute x5, waiting for transfers between devices, swap_seq(): return lax.ppermute(x, 'seq', [(i, i ^ bit) for i in range(seq_size)])  8.76 us
    pallas_call x3, Pallas kernels, add_rows(): pl.pallas_call(kernel, grid=(rows // unit,), in_specs=specs, out_specs=pl...  2.82 us
    unnamed x4, local copies, waits for them, and re-layouts  1.62 us
  transfers between devices with their start and end apart: 23, of which 14 were waited for; matrix products, arithmetic and copies ran while one was open for 0% of the time, Pallas kernels for 24%

profile of v20, /device:TPU:0, one launch (start us, length us, event | category | flops | bytes accessed | tf_op | source)
XLA Modules:
  0.0 76.3 jit_solution(8233897472809784400)
XLA Ops:
  0.5 2.5 %collective-permute-start = (bf16[512,1024]{1,0:T(8,128)(2,1)}, bf16[512,1024]{1,0:T(8,128)(2,1)S(1)}, u32[]{:S(2)}, u32[]{:S(2)}) collective-permute-start(bf16[512,1024]{1,0:T(8,128)(2,1)} %refs_2_.1), channel_id=1, source_target_pairs={{0,2},{1,3},{2,0},{3,1},{4,6},{5,7},{6,4},{7,5},{8,10},{9,11},{10,... | collective-permute-start | bytes 3145736 | tf_op jit(solution)/shard_map/ppermute | solution.py:391
  4.6 5.3 %shard_map.73 = (f32[512,512]{1,0:T(8,128)S(1)}, f32[512,256]{1,0:T(8,128)S(1)}, f32[512,24]{1,0:T(8,128)S(1)}, bf16[2,1024,512]{2,1,0:T(8,128)(2,1)S(1)}, bf16[...) custom-call(s32[1]{0:T(128)} %bitcast.refs_0_, ...), custom_call_target="tpu_custom_call" | custom-call | tf_op jit(solution)/shard_map/pallas_call | solution.py:41
  10.8 2.6 %collective-permute-start.3 = (f32[8,512]{1,0:T(8,128)S(1)}, f32[8,512]{1,0:T(8,128)S(1)}, u32[]{:S(2)}, u32[]{:S(2)}) collective-permute-start(f32[8,512]{1,0:T(8,128)S(1)} %get-tuple-element.51.refs_1_), channel_id=1, source_target_pairs={{0,4},{4,0},{8,12},{12,8},{16,20},{20,16},{24,28},{28,24},{1,5},{5... | collective-permute-start | bytes 49160 | tf_op jit(solution)/shard_map/ppermute | solution.py:394
  13.4 1.7 %collective-permute-done.3.refs_2_ = f32[8,512]{1,0:T(8,128)S(1)} collective-permute-done((f32[8,512]{1,0:T(8,128)S(1)}, f32[8,512]{1,0:T(8,128)S(1)}, u32[]{:S(2)}, u32[]{:S(2)}) %collective-permute-start.3) | collective-permute-done | bytes 16416 | tf_op jit(solution)/shard_map/ppermute | solution.py:394
  15.2 2.2 %collective-permute-start.4 = (f32[8,512]{1,0:T(8,128)S(1)}, f32[8,512]{1,0:T(8,128)S(1)}, u32[]{:S(2)}, u32[]{:S(2)}) collective-permute-start(f32[8,512]{1,0:T(8,128)S(1)} %get-tuple-element.52.refs_1_), channel_id=1, source_target_pairs={{0,8},{4,12},{8,0},{12,4},{16,24},{20,28},{24,16},{28,20},{1,9},{5... | collective-permute-start | bytes 49160 | tf_op jit(solution)/shard_map/ppermute | solution.py:394
  17.3 1.7 %collective-permute-done.4.refs_2_ = f32[8,512]{1,0:T(8,128)S(1)} collective-permute-done((f32[8,512]{1,0:T(8,128)S(1)}, f32[8,512]{1,0:T(8,128)S(1)}, u32[]{:S(2)}, u32[]{:S(2)}) %collective-permute-start.4) | collective-permute-done | bytes 16416 | tf_op jit(solution)/shard_map/ppermute | solution.py:394
  19.7 7.3 %collective-permute-done.refs_0_.refs_1_ = bf16[512,1024]{1,0:T(8,128)(2,1)S(1)} collective-permute-done((bf16[512,1024]{1,0:T(8,128)(2,1)}, bf16[512,1024]{1,0:T(8,128)(2,1)S(1)}, u32[]{:S(2)}, u32[]{:S(2)}) %collective-permute-start) | collective-permute-done | bytes 1048608 | tf_op jit(solution)/shard_map/ppermute | solution.py:391
  28.0 1.1 %collective-permute-done.7.refs_1_ = bf16[512,256]{1,0:T(8,128)(2,1)S(1)} collective-permute-done((bf16[512,256]{1,0:T(8,128)(2,1)S(1)}, bf16[512,256]{1,0:T(8,128)(2,1)S(1)}, u32[]{:S(2)}, u32[]{:S(2)}) %collective-permute-start.7) | collective-permute-done | bytes 262176 | tf_op jit(solution)/shard_map/ppermute | solution.py:391
  29.7 1.8 %collective-permute-start.12 = (bf16[128,512]{1,0:T(8,128)(2,1)S(1)}, bf16[128,512]{1,0:T(8,128)(2,1)S(1)}, u32[]{:S(2)}, u32[]{:S(2)}) collective-permute-start(bf16[128,512]{1,0:T(8,128)(2,1)S(1)} %get-tuple-element.71.refs_0_), channel_id=1, source_target_pairs={{0,4},{4,0},{8,12},{12,8},{16,20},{20,16},{24,28},{28,24},{1,5},{5... | collective-permute-start | bytes 393224 | tf_op jit(solution)/shard_map/ppermute | solution.py:394
  31.4 1.1 %shard_map.79 = (f32[512,512]{1,0:T(8,128)S(1)}, f32[512,24]{1,0:T(8,128)S(1)}) custom-call(s32[1]{0:T(128)} %bitcast.refs_0_, bf16[512,1024]{1,0:T(8,128)(2,1)S(1)} %collective-permute-done.refs_0_.refs_1_, bf16[2,1024,512]{2,1,0:T(8,128)(2,1)S(1)} %get-tuple-element.44.refs_2_.refs_5_, ...), custom_call_target="tpu_custom_call", output_to_operand_aliasing={{0}: (4, {}), {1}: (5, {})} | custom-call | flops 562036736 | bytes 5537796 | tf_op jit(solution)/shard_map/pallas_call | solution.py:41
  33.7 1.6 %collective-permute-done.12.refs_1_.refs_16_ = bf16[128,512]{1,0:T(8,128)(2,1)S(1)} collective-permute-done((bf16[128,512]{1,0:T(8,128)(2,1)S(1)}, bf16[128,512]{1,0:T(8,128)(2,1)S(1)}, u32[]{:S(2)}, u32[]{:S(2)}) %collective-permute-start.12) | collective-permute-done | bytes 131104 | tf_op jit(solution)/shard_map/ppermute | solution.py:394
  35.3 1.9 %collective-permute-start.13 = (bf16[128,512]{1,0:T(8,128)(2,1)S(1)}, bf16[128,512]{1,0:T(8,128)(2,1)S(1)}, u32[]{:S(2)}, u32[]{:S(2)}) collective-permute-start(bf16[128,512]{1,0:T(8,128)(2,1)S(1)} %shard_map.81.refs_0_), channel_id=1, source_target_pairs={{0,8},{4,12},{8,0},{12,4},{16,24},{20,28},{24,16},{28,20},{1,9},{5... | collective-permute-start | bytes 393224 | tf_op jit(solution)/shard_map/ppermute | solution.py:394
  37.2 3.2 %collective-permute-done.13.refs_17_.refs_1_ = bf16[128,512]{1,0:T(8,128)(2,1)S(1)} collective-permute-done((bf16[128,512]{1,0:T(8,128)(2,1)S(1)}, bf16[128,512]{1,0:T(8,128)(2,1)S(1)}, u32[]{:S(2)}, u32[]{:S(2)}) %collective-permute-start.13) | collective-permute-done | bytes 131104 | tf_op jit(solution)/shard_map/ppermute | solution.py:394
  40.4 2.9 %collective-permute-start.14 = (bf16[128,512]{1,0:T(8,128)(2,1)S(1)}, bf16[128,512]{1,0:T(8,128)(2,1)S(1)}, u32[]{:S(2)}, u32[]{:S(2)}) collective-permute-start(bf16[128,512]{1,0:T(8,128)(2,1)S(1)} %shard_map.83), channel_id=1, source_target_pairs={{0,16},{4,20},{8,24},{12,28},{16,0},{20,4},{24,8},{28,12},{1,17},{... | collective-permute-start | bytes 393224 | tf_op jit(solution)/shard_map/ppermute | solution.py:394
  43.3 4.0 %shard_map.82 = (f32[512,512]{1,0:T(8,128)S(1)}, bf16[512,512]{1,0:T(8,128)(2,1)S(1)}, bf16[512,512]{1,0:T(8,128)(2,1)}, f32[512,24]{1,0:T(8,128)}) custom-call(s32[1]{0:T(128)} %bitcast.refs_0_, bf16[512,256]{1,0:T(8,128)(2,1)S(1)} %collective-permute-done.8.refs_1_, bf16[512,256]{1,0:T(8,128)(2,1)S(1)} %collective-permute-done.9.refs_2_, ...), custom_call_target="tpu_custom_call" | custom-call | flops 1073741824 | bytes 7176196 | tf_op jit(solution)/shard_map/pallas_call | solution.py:41
  50.4 1.6 %collective-permute-start.21 = (bf16[192,1024]{1,0:T(8,128)(2,1)S(1)}, bf16[192,1024]{1,0:T(8,128)(2,1)S(1)}, u32[]{:S(2)}, u32[]{:S(2)}) collective-permute-start(bf16[192,1024]{1,0:T(8,128)(2,1)S(1)} %shard_map.90), channel_id=1, source_target_pairs={{0,2},{1,3},{2,0},{3,1},{4,6},{5,7},{6,4},{7,5},{8,10},{9,11},{10,... | collective-permute-start | bytes 1179656 | tf_op jit(solution)/shard_map/ppermute | solution.py:391
  53.8 1.3 %collective-permute-start.19 = (bf16[128,1024]{1,0:T(8,128)(2,1)S(1)}, bf16[128,1024]{1,0:T(8,128)(2,1)S(1)}, u32[]{:S(2)}, u32[]{:S(2)}) collective-permute-start(bf16[128,1024]{1,0:T(8,128)(2,1)S(1)} %shard_map.88), channel_id=1, source_target_pairs={{0,2},{1,3},{2,0},{3,1},{4,6},{5,7},{6,4},{7,5},{8,10},{9,11},{10,... | collective-permute-start | bytes 786440 | tf_op jit(solution)/shard_map/ppermute | solution.py:391
  55.1 1.3 %collective-permute-done.18.refs_1_.refs_7_ = bf16[64,512]{1,0:T(8,128)(2,1)S(1)} collective-permute-done((bf16[64,512]{1,0:T(8,128)(2,1)S(1)}, bf16[64,512]{1,0:T(8,128)(2,1)S(1)}, u32[]{:S(2)}, u32[]{:S(2)}) %collective-permute-start.18) | collective-permute-done | bytes 65568 | tf_op jit(solution)/shard_map/ppermute | solution.py:391
  57.7 1.5 %shard_map.87.h_ref = f32[512,1024]{1,0:T(8,128)S(1)} custom-call(bf16[192,512]{1,0:T(8,128)(2,1)S(1)} %shard_map.84.refs_3_.refs_0_, bf16[192,512]{1,0:T(8,128)(2,1)S(1)} %collective-permute-done.15.refs_1_, bf16[128,512]{1,0:T(8,128)(2,1)S(1)} %get-tuple-element.78.refs_2_.refs_0_, bf16[128,512]{1,0:T(8,128)(2,1)S(1)} %collective-permute-done.16.refs_3_.refs_1_, ...), custom_call_target="tpu_custom_call" | custom-call | tf_op jit(solution)/shard_map/pallas_call | solution.py:41
  59.2 3.2 %collective-permute-done.21.a_ref = bf16[192,1024]{1,0:T(8,128)(2,1)S(1)} collective-permute-done((bf16[192,1024]{1,0:T(8,128)(2,1)S(1)}, bf16[192,1024]{1,0:T(8,128)(2,1)S(1)}, u32[]{:S(2)}, u32[]{:S(2)}) %collective-permute-start.21) | collective-permute-done | bytes 393248 | tf_op jit(solution)/shard_map/ppermute | solution.py:391
  62.4 1.4 %shard_map.91.refs_0_ = bf16[512,1024]{1,0:T(8,128)(2,1)} custom-call(f32[512,1024]{1,0:T(8,128)S(1)} %shard_map.87.h_ref, bf16[192,1024]{1,0:T(8,128)(2,1)S(1)} %collective-permute-done.21.a_ref), custom_call_target="tpu_custom_call" | custom-call | bytes 1572864 | tf_op jit(solution)/shard_map/pallas_call | solution.py:368
  63.8 4.2 %collective-permute-done.20.a_ref = bf16[128,1024]{1,0:T(8,128)(2,1)S(1)} collective-permute-done((bf16[128,1024]{1,0:T(8,128)(2,1)S(1)}, bf16[128,1024]{1,0:T(8,128)(2,1)S(1)}, u32[]{:S(2)}, u32[]{:S(2)}) %collective-permute-start.20) | collective-permute-done | bytes 262176 | tf_op jit(solution)/shard_map/ppermute | solution.py:391
  68.7 4.9 %collective-permute-done.19.a_ref = bf16[128,1024]{1,0:T(8,128)(2,1)S(1)} collective-permute-done((bf16[128,1024]{1,0:T(8,128)(2,1)S(1)}, bf16[128,1024]{1,0:T(8,128)(2,1)S(1)}, u32[]{:S(2)}, u32[]{:S(2)}) %collective-permute-start.19) | collective-permute-done | bytes 262176 | tf_op jit(solution)/shard_map/ppermute | solution.py:391
  74.4 1.3 %collective-permute-done.22 = bf16[64,1024]{1,0:T(8,128)(2,1)S(1)} collective-permute-done((bf16[64,1024]{1,0:T(8,128)(2,1)S(1)}, bf16[64,1024]{1,0:T(8,128)(2,1)S(1)}, u32[]{:S(2)}, u32[]{:S(2)}) %collective-permute-start.22) | collective-permute-done | bytes 131104 | tf_op jit(solution)/shard_map/ppermute | solution.py:391
  (48 shorter events, 14.7 us)
Async XLA Ops:
  0.0 3.0 %collective-permute-start.1 = (bf16[512,1024]{1,0:T(8,128)(2,1)}, bf16[512,1024]{1,0:T(8,128)(2,1)S(1)}, u32[]{:S(2)}, u32[]{:S(2)}) collective-permute-start(bf16[512,1024]{1,0:T(8,128)(2,1)} %refs_2_.1), channel_id=1, source_target_pairs={{0,1},{1,0},{2,3},{3,2},{4,5},{5,4},{6,7},{7,6},{8,9},{9,8},{10,11... | collective-permute-start | bytes 3145736 | tf_op jit(solution)/shard_map/ppermute | solution.py:391
  0.5 26.6 %collective-permute-start = (bf16[512,1024]{1,0:T(8,128)(2,1)}, bf16[512,1024]{1,0:T(8,128)(2,1)S(1)}, u32[]{:S(2)}, u32[]{:S(2)}) collective-permute-start(bf16[512,1024]{1,0:T(8,128)(2,1)} %refs_2_.1), channel_id=1, source_target_pairs={{0,2},{1,3},{2,0},{3,1},{4,6},{5,7},{6,4},{7,5},{8,10},{9,11},{10,... | collective-permute-start | bytes 3145736 | tf_op jit(solution)/shard_map/ppermute | solution.py:391
  3.0 0.9 %copy-start = (bf16[4096,24]{0,1:T(8,128)(2,1)S(1)}, bf16[4096,24]{0,1:T(8,128)(2,1)}, u32[]{:S(2)}) copy-start(bf16[4096,24]{0,1:T(8,128)(2,1)} %param.12) | copy-start | bytes 589828
  9.9 17.1 %collective-permute-start.5 = (bf16[512,1024]{1,0:T(8,128)(2,1)S(1)}, bf16[512,1024]{1,0:T(8,128)(2,1)S(1)}, u32[]{:S(2)}, u32[]{:S(2)}) collective-permute-start(bf16[512,1024]{1,0:T(8,128)(2,1)S(1)} %get-tuple-element.55), channel_id=1, source_target_pairs={{0,1},{1,0},{2,3},{3,2},{4,5},{5,4},{6,7},{7,6},{8,9},{9,8},{10,11... | collective-permute-start | bytes 3145736 | tf_op jit(solution)/shard_map/ppermute | solution.py:391
  10.3 16.7 %collective-permute-start.6 = (bf16[512,1024]{1,0:T(8,128)(2,1)S(1)}, bf16[512,1024]{1,0:T(8,128)(2,1)S(1)}, u32[]{:S(2)}, u32[]{:S(2)}) collective-permute-start(bf16[512,1024]{1,0:T(8,128)(2,1)S(1)} %get-tuple-element.56), channel_id=1, source_target_pairs={{0,1},{1,0},{2,3},{3,2},{4,5},{5,4},{6,7},{7,6},{8,9},{9,8},{10,11... | collective-permute-start | bytes 3145736 | tf_op jit(solution)/shard_map/ppermute | solution.py:391
  10.5 16.6 %collective-permute-start.2 = (bf16[1024,256]{1,0:T(8,128)(2,1)S(1)}, bf16[1024,256]{1,0:T(8,128)(2,1)S(1)}, u32[]{:S(2)}, u32[]{:S(2)}) collective-permute-start(bf16[1024,256]{1,0:T(8,128)(2,1)S(1)} %get-tuple-element.50), channel_id=1, source_target_pairs={{0,1},{1,0},{2,3},{3,2},{4,5},{5,4},{6,7},{7,6},{8,9},{9,8},{10,11... | collective-permute-start | bytes 1572872 | tf_op jit(solution)/shard_map/ppermute | solution.py:391
  10.8 4.3 %collective-permute-start.3 = (f32[8,512]{1,0:T(8,128)S(1)}, f32[8,512]{1,0:T(8,128)S(1)}, u32[]{:S(2)}, u32[]{:S(2)}) collective-permute-start(f32[8,512]{1,0:T(8,128)S(1)} %get-tuple-element.51.refs_1_), channel_id=1, source_target_pairs={{0,4},{4,0},{8,12},{12,8},{16,20},{20,16},{24,28},{28,24},{1,5},{5... | collective-permute-start | bytes 49160 | tf_op jit(solution)/shard_map/ppermute | solution.py:394
  15.2 3.9 %collective-permute-start.4 = (f32[8,512]{1,0:T(8,128)S(1)}, f32[8,512]{1,0:T(8,128)S(1)}, u32[]{:S(2)}, u32[]{:S(2)}) collective-permute-start(f32[8,512]{1,0:T(8,128)S(1)} %get-tuple-element.52.refs_1_), channel_id=1, source_target_pairs={{0,8},{4,12},{8,0},{12,4},{16,24},{20,28},{24,16},{28,20},{1,9},{5... | collective-permute-start | bytes 49160 | tf_op jit(solution)/shard_map/ppermute | solution.py:394
  27.5 1.6 %collective-permute-start.7 = (bf16[512,256]{1,0:T(8,128)(2,1)S(1)}, bf16[512,256]{1,0:T(8,128)(2,1)S(1)}, u32[]{:S(2)}, u32[]{:S(2)}) collective-permute-start(bf16[512,256]{1,0:T(8,128)(2,1)S(1)} %shard_map.76.refs_3_), channel_id=1, source_target_pairs={{0,1},{1,0},{2,3},{3,2},{4,5},{5,4},{6,7},{7,6},{8,9},{9,8},{10,11... | collective-permute-start | bytes 786440 | tf_op jit(solution)/shard_map/ppermute | solution.py:391
  29.7 5.6 %collective-permute-start.12 = (bf16[128,512]{1,0:T(8,128)(2,1)S(1)}, bf16[128,512]{1,0:T(8,128)(2,1)S(1)}, u32[]{:S(2)}, u32[]{:S(2)}) collective-permute-start(bf16[128,512]{1,0:T(8,128)(2,1)S(1)} %get-tuple-element.71.refs_0_), channel_id=1, source_target_pairs={{0,4},{4,0},{8,12},{12,8},{16,20},{20,16},{24,28},{28,24},{1,5},{5... | collective-permute-start | bytes 393224 | tf_op jit(solution)/shard_map/ppermute | solution.py:394
  32.6 10.7 %collective-permute-start.8 = (bf16[512,256]{1,0:T(8,128)(2,1)S(1)}, bf16[512,256]{1,0:T(8,128)(2,1)S(1)}, u32[]{:S(2)}, u32[]{:S(2)}) collective-permute-start(bf16[512,256]{1,0:T(8,128)(2,1)S(1)} %get-tuple-element.60), channel_id=1, source_target_pairs={{0,1},{1,0},{2,3},{3,2},{4,5},{5,4},{6,7},{7,6},{8,9},{9,8},{10,11... | collective-permute-start | bytes 786440 | tf_op jit(solution)/shard_map/ppermute | solution.py:391
  32.7 10.6 %collective-permute-start.9 = (bf16[512,256]{1,0:T(8,128)(2,1)S(1)}, bf16[512,256]{1,0:T(8,128)(2,1)S(1)}, u32[]{:S(2)}, u32[]{:S(2)}) collective-permute-start(bf16[512,256]{1,0:T(8,128)(2,1)S(1)} %get-tuple-element.61), channel_id=1, source_target_pairs={{0,1},{1,0},{2,3},{3,2},{4,5},{5,4},{6,7},{7,6},{8,9},{9,8},{10,11... | collective-permute-start | bytes 786440 | tf_op jit(solution)/shard_map/ppermute | solution.py:391
  33.2 10.1 %collective-permute-start.10 = (bf16[512,256]{1,0:T(8,128)(2,1)S(1)}, bf16[512,256]{1,0:T(8,128)(2,1)S(1)}, u32[]{:S(2)}, u32[]{:S(2)}) collective-permute-start(bf16[512,256]{1,0:T(8,128)(2,1)S(1)} %get-tuple-element.62), channel_id=1, source_target_pairs={{0,1},{1,0},{2,3},{3,2},{4,5},{5,4},{6,7},{7,6},{8,9},{9,8},{10,11... | collective-permute-start | bytes 786440 | tf_op jit(solution)/shard_map/ppermute | solution.py:391
  33.2 10.0 %collective-permute-start.11 = (bf16[512,256]{1,0:T(8,128)(2,1)S(1)}, bf16[512,256]{1,0:T(8,128)(2,1)S(1)}, u32[]{:S(2)}, u32[]{:S(2)}) collective-permute-start(bf16[512,256]{1,0:T(8,128)(2,1)S(1)} %get-tuple-element.63), channel_id=1, source_target_pairs={{0,1},{1,0},{2,3},{3,2},{4,5},{5,4},{6,7},{7,6},{8,9},{9,8},{10,11... | collective-permute-start | bytes 786440 | tf_op jit(solution)/shard_map/ppermute | solution.py:391
  35.3 5.0 %collective-permute-start.13 = (bf16[128,512]{1,0:T(8,128)(2,1)S(1)}, bf16[128,512]{1,0:T(8,128)(2,1)S(1)}, u32[]{:S(2)}, u32[]{:S(2)}) collective-permute-start(bf16[128,512]{1,0:T(8,128)(2,1)S(1)} %shard_map.81.refs_0_), channel_id=1, source_target_pairs={{0,8},{4,12},{8,0},{12,4},{16,24},{20,28},{24,16},{28,20},{1,9},{5... | collective-permute-start | bytes 393224 | tf_op jit(solution)/shard_map/ppermute | solution.py:394
  40.4 7.5 %collective-permute-start.14 = (bf16[128,512]{1,0:T(8,128)(2,1)S(1)}, bf16[128,512]{1,0:T(8,128)(2,1)S(1)}, u32[]{:S(2)}, u32[]{:S(2)}) collective-permute-start(bf16[128,512]{1,0:T(8,128)(2,1)S(1)} %shard_map.83), channel_id=1, source_target_pairs={{0,16},{4,20},{8,24},{12,28},{16,0},{20,4},{24,8},{28,12},{1,17},{... | collective-permute-start | bytes 393224 | tf_op jit(solution)/shard_map/ppermute | solution.py:394
  48.3 1.5 %collective-permute-start.15 = (bf16[192,512]{1,0:T(8,128)(2,1)S(1)}, bf16[192,512]{1,0:T(8,128)(2,1)S(1)}, u32[]{:S(2)}, u32[]{:S(2)}) collective-permute-start(bf16[192,512]{1,0:T(8,128)(2,1)S(1)} %shard_map.84.refs_3_.refs_0_), channel_id=1, source_target_pairs={{0,1},{1,0},{2,3},{3,2},{4,5},{5,4},{6,7},{7,6},{8,9},{9,8},{10,11... | collective-permute-start | bytes 589832 | tf_op jit(solution)/shard_map/ppermute | solution.py:391
  48.8 3.2 %collective-permute-start.16 = (bf16[128,512]{1,0:T(8,128)(2,1)S(1)}, bf16[128,512]{1,0:T(8,128)(2,1)S(1)}, u32[]{:S(2)}, u32[]{:S(2)}) collective-permute-start(bf16[128,512]{1,0:T(8,128)(2,1)S(1)} %get-tuple-element.78.refs_2_.refs_0_), channel_id=1, source_target_pairs={{0,1},{1,0},{2,3},{3,2},{4,5},{5,4},{6,7},{7,6},{8,9},{9,8},{10,11... | collective-permute-start | bytes 393224 | tf_op jit(solution)/shard_map/ppermute | solution.py:391
  50.4 12.0 %collective-permute-start.21 = (bf16[192,1024]{1,0:T(8,128)(2,1)S(1)}, bf16[192,1024]{1,0:T(8,128)(2,1)S(1)}, u32[]{:S(2)}, u32[]{:S(2)}) collective-permute-start(bf16[192,1024]{1,0:T(8,128)(2,1)S(1)} %shard_map.90), channel_id=1, source_target_pairs={{0,2},{1,3},{2,0},{3,1},{4,6},{5,7},{6,4},{7,5},{8,10},{9,11},{10,... | collective-permute-start | bytes 1179656 | tf_op jit(solution)/shard_map/ppermute | solution.py:391
  52.0 1.3 %collective-permute-start.17 = (bf16[128,512]{1,0:T(8,128)(2,1)S(1)}, bf16[128,512]{1,0:T(8,128)(2,1)S(1)}, u32[]{:S(2)}, u32[]{:S(2)}) collective-permute-start(bf16[128,512]{1,0:T(8,128)(2,1)S(1)} %get-tuple-element.79.refs_4_.refs_0_), channel_id=1, source_target_pairs={{0,1},{1,0},{2,3},{3,2},{4,5},{5,4},{6,7},{7,6},{8,9},{9,8},{10,11... | collective-permute-start | bytes 393224 | tf_op jit(solution)/shard_map/ppermute | solution.py:391
  52.5 15.5 %collective-permute-start.20 = (bf16[128,1024]{1,0:T(8,128)(2,1)S(1)}, bf16[128,1024]{1,0:T(8,128)(2,1)S(1)}, u32[]{:S(2)}, u32[]{:S(2)}) collective-permute-start(bf16[128,1024]{1,0:T(8,128)(2,1)S(1)} %shard_map.89), channel_id=1, source_target_pairs={{0,2},{1,3},{2,0},{3,1},{4,6},{5,7},{6,4},{7,5},{8,10},{9,11},{10,... | collective-permute-start | bytes 786440 | tf_op jit(solution)/shard_map/ppermute | solution.py:391
  53.8 19.8 %collective-permute-start.19 = (bf16[128,1024]{1,0:T(8,128)(2,1)S(1)}, bf16[128,1024]{1,0:T(8,128)(2,1)S(1)}, u32[]{:S(2)}, u32[]{:S(2)}) collective-permute-start(bf16[128,1024]{1,0:T(8,128)(2,1)S(1)} %shard_map.88), channel_id=1, source_target_pairs={{0,2},{1,3},{2,0},{3,1},{4,6},{5,7},{6,4},{7,5},{8,10},{9,11},{10,... | collective-permute-start | bytes 786440 | tf_op jit(solution)/shard_map/ppermute | solution.py:391
  55.1 1.3 %collective-permute-start.18 = (bf16[64,512]{1,0:T(8,128)(2,1)S(1)}, bf16[64,512]{1,0:T(8,128)(2,1)S(1)}, u32[]{:S(2)}, u32[]{:S(2)}) collective-permute-start(bf16[64,512]{1,0:T(8,128)(2,1)S(1)} %get-tuple-element.80.refs_0_.refs_6_), channel_id=1, source_target_pairs={{0,1},{1,0},{2,3},{3,2},{4,5},{5,4},{6,7},{7,6},{8,9},{9,8},{10,11... | collective-permute-start | bytes 196616 | tf_op jit(solution)/shard_map/ppermute | solution.py:391
  56.9 18.8 %collective-permute-start.22 = (bf16[64,1024]{1,0:T(8,128)(2,1)S(1)}, bf16[64,1024]{1,0:T(8,128)(2,1)S(1)}, u32[]{:S(2)}, u32[]{:S(2)}) collective-permute-start(bf16[64,1024]{1,0:T(8,128)(2,1)S(1)} %shard_map.86.refs_10_), channel_id=1, source_target_pairs={{0,2},{1,3},{2,0},{3,1},{4,6},{5,7},{6,4},{7,5},{8,10},{9,11},{10,... | collective-permute-start | bytes 393224 | tf_op jit(solution)/shard_map/ppermute | solution.py:391
  (1 other events, 0.7 us)

commit v21 on v12

--- a/solution.py
+++ b/solution.py
@@ -127,6 +127,19 @@
     return call(kernel, [state, other, own_factor, other_factor], [shape(state.shape, BF16)], 0, after)[0]
 
 
+def combine_both(states, others, own_factor, other_factor, after):
+    rows, half = states[0].shape
+
+    def kernel(s0_ref, s1_ref, o0_ref, o1_ref, a_ref, b_ref, out_ref):
+        for i, (s_ref, o_ref) in enumerate(((s0_ref, o0_ref), (s1_ref, o1_ref))):
+            cols = slice(i * half, (i + 1) * half)
+            out_ref[:, cols] = (
+                a_ref[0:1, cols] * s_ref[...].astype(F32) + b_ref[0:1, cols] * o_ref[...].astype(F32)
+            ).astype(BF16)
+
+    return call(kernel, [*states, *others, own_factor, other_factor], [shape((rows, 2 * half), BF16)], 0, after)[0]
+
+
 def begin(me, slab, tokens, near, log_decay_rows, ws, w_out, head_size):
     wq, wk, wv, wl = ws
     rows, shard = near.shape
@@ -134,7 +147,7 @@
     heads = log_decay_rows.shape[0]
     block = w_out.shape[1] // 4
 
-    def kernel(me_ref, slab_ref, t_ref, wq_ref, wk_ref, wv_ref, wl_ref, wo_ref, near_ref, decay_ref, *refs):
+    def kernel(me_ref, slab_ref, t_ref, wq_ref, wk_ref, wv_ref, wo_ref, wl_ref, near_ref, decay_ref, *refs):
         total_q, total_kv, total_l, far_q, far_kv, send_kv, all_l = refs[:7]
         decay_outs, blocks, (own_x, own_q, own_kv, sems) = refs[7:12], refs[12:16], refs[16:]
 
@@ -149,26 +162,27 @@
         def columns(i):
             return wo_ref.at[:, pl.ds(pl.multiple_of((me_ref[0] ^ i) * block, 128), block)]
 
-        moves = pairs(0, own_q.at[0], own_kv.at[0]) + [(wl_ref, all_l), (t_ref, own_x)]
+        moves = pairs(0, own_q.at[0], own_kv.at[0]) + [(t_ref, own_x)]
         moves += pairs(1, own_q.at[1], own_kv.at[1])
         moves += pairs(2, far_q.at[0], far_kv) + pairs(3, far_q.at[1], send_kv)
         moves += [(columns(i), blocks[i]) for i in range(4)]
         started = copies(moves, sems)
         decays(slab_ref, decay_ref, *decay_outs)
-        for copy in started[:5]:
+        all_l[...] = wl_ref[...]
+        for copy in started[:4]:
             copy.wait()
         lanes = pl.ds(pl.multiple_of(me_ref[0] * shard, 128), shard)
         own = own_x[...]
         total_kv[...] = dot(own, own_kv[0])
         total_q[...] = dot(own, own_q[0])
         total_l[...] = dot_dims(own, all_l[:, lanes], 1, 1)
-        for copy in started[5:8]:
+        for copy in started[4:7]:
             copy.wait()
         lanes = pl.ds(pl.multiple_of((me_ref[0] ^ 1) * shard, 128), shard)
         total_kv[...] += dot(near_ref[...], own_kv[1])
         total_q[...] += dot(near_ref[...], own_q[1])
         total_l[...] += dot_dims(near_ref[...], all_l[:, lanes], 1, 1)
-        for copy in started[8:]:
+        for copy in started[7:]:
             copy.wait()
 
     wide = shape((8, heads * head_size), F32)
@@ -190,10 +204,10 @@
         pltpu.VMEM((rows, shard), BF16),
         pltpu.VMEM((2, shard, q_width), BF16),
         pltpu.VMEM((2, shard, 2 * kv_width), BF16),
-        pltpu.SemaphoreType.DMA((18,)),
+        pltpu.SemaphoreType.DMA((17,)),
     ]
-    ins = [me, slab, tokens, wq, wk, wv, wl, w_out, near, log_decay_rows]
-    outs = call(kernel, ins, outs, 0, smem=2, hbm=6, scratch=scratch, megabytes=14)
+    ins = [me, slab, tokens, wq, wk, wv, w_out, wl, near, log_decay_rows]
+    outs = call(kernel, ins, outs, 0, smem=2, hbm=5, scratch=scratch, megabytes=14)
     return outs[:3], outs[3:7], outs[7:12], outs[12:]
 
 
@@ -343,40 +357,43 @@
     return list(zip(outs[:2], outs[2:]))
 
 
-def finish(local, scaled, state, cuts, head_size, flops, after=()):
-    width = state.shape[1]
-
-    def kernel(o_ref, q_ref, s_ref, *outs):
+def finish(halves, state, cuts, head_size, after=()):
+    half = halves[0][0].shape[1]
+
+    def kernel(o0_ref, q0_ref, o1_ref, q1_ref, s_ref, *outs):
         for rows, n_ref in zip(cuts, outs):
-            for c in range(0, width, head_size):
+            for c in range(0, 2 * half, head_size):
                 cols = slice(c, c + head_size)
-                total = o_ref[rows, cols] + dot_dims(q_ref[rows, cols], s_ref[:, cols], 1, 1)
+                here = slice(c % half, c % half + head_size)
+                o_ref, q_ref = (o0_ref, q0_ref) if c < half else (o1_ref, q1_ref)
+                total = o_ref[rows, here] + dot_dims(q_ref[rows, here], s_ref[:, cols], 1, 1)
                 mean = jnp.mean(total * total, axis=-1, keepdims=True)
                 n_ref[:, cols] = (total * lax.rsqrt(mean + 1e-05)).astype(BF16)
 
-    outs = [shape((cut.stop - cut.start, width), BF16) for cut in cuts]
-    return call(kernel, [local, scaled, state], outs, flops, after)
-
-
-def out_block(first, second, places, w0, w1, dtype, after=()):
+    outs = [shape((cut.stop - cut.start, 2 * half), BF16) for cut in cuts]
+    return call(kernel, [*halves[0], *halves[1], state], outs, 0, after)
+
+
+def out_block(pairs, w0, w1, dtype, after=()):
     columns = w1.shape[1]
-    rows = sum(cut.stop - cut.start for _, cut in places)
+    count = len(pairs)
+    rows = sum(own.shape[0] for own, _ in pairs)
     tile = min(columns, 512)
 
     def kernel(*refs):
-        f_refs, s_refs = refs[: 2 * len(first)], refs[2 * len(first) : -3]
-        w0_ref, w1_ref, o_ref = refs[-3:]
+        w0_ref, w1_ref, o_ref = refs[2 * count :]
         start = 0
-        for i, (which, cut) in enumerate(places):
-            here = slice(start, start + cut.stop - cut.start)
+        for i in range(count):
+            a_ref, b_ref = refs[2 * i], refs[2 * i + 1]
+            here = slice(start, start + a_ref.shape[0])
             start = here.stop
-            own = jnp.concatenate([f_refs[2 * which][cut, :], s_refs[2 * i][...]], axis=1)
-            near = jnp.concatenate([f_refs[2 * which + 1][cut, :], s_refs[2 * i + 1][...]], axis=1)
             for c in range(0, columns, tile):
                 cols = slice(c, c + tile)
-                o_ref[here, cols] = (dot(own, w0_ref[:, cols]) + dot(near, w1_ref[:, cols])).astype(dtype)
-
-    ins = [x for pair in (*first, *second) for x in pair] + [w0, w1]
+                o_ref[here, cols] = (
+                    dot(a_ref[...], w0_ref[:, cols]) + dot(b_ref[...], w1_ref[:, cols])
+                ).astype(dtype)
+
+    ins = [x for pair in pairs for x in pair] + [w0, w1]
     return call(kernel, ins, [shape((rows, columns), dtype)], 0, after)[0]
 
 
@@ -447,37 +464,31 @@
     q, level = queries(me, 3, far_near, wq, wl, total_q, total_l)
     locals_ = [attend(q, level, k, v, dcol, drow, i, head_size, level_count) for i in range(2)]
     earlier = []
-    for b in range(seq_bits):
+    for b in range(seq_bits - 1):
         others = [swap_seq(state, 1 << b) for state in states]
         earlier.append(others)
-        if b < seq_bits - 1:
-            afters = (locals_[b : b + 1], ())
+        if b < seq_bits - 2:
             states = [
-                combine(state, other, *factors[b], i, after)
-                for i, (state, other, after) in enumerate(zip(states, others, afters))
+                combine(state, other, *factors[b], i, ())
+                for i, (state, other) in enumerate(zip(states, others))
             ]
-    before_last = [state for others in earlier[:-1] for state in others]
+    last = swap_seq(combine_both(states, others, *factors[seq_bits - 2], (level,)), 1 << (seq_bits - 1))
+    before_last = [state for others in earlier for state in others]
     halves = attend_earlier(locals_, q, level, dcol, spans, before_last, head_size, level_count)
 
     unit = rows // 8
     ends = (0, 2, 4, 6, 7, 8)
     cuts = [slice(start * unit, stop * unit) for start, stop in zip(ends, ends[1:])]
-    middle = rows // 2
-    tops = finish(*halves[0], earlier[-1][0], [slice(0, middle), slice(middle, rows)], head_size, 10**8)
-    first = [(x, swap_tp(x, 1)) for x in tops]
-    second = finish(*halves[1], earlier[-1][1], cuts, head_size, 0, tops)
-    second = [(x, swap_tp(x, 1)) for x in second]
-    crossing = []
-    for pair, cut in zip(second, cuts):
-        i = cut.start // middle
-        here = slice(cut.start - i * middle, cut.stop - i * middle)
-        crossing.append(out_block([first[i]], [pair], [(0, here)], w_far_own, w_far, BF16))
-    places = [(c.start // middle, slice(c.start % middle, c.start % middle + c.stop - c.start)) for c in cuts]
-    own_block = out_block(first, second, places, w_here_own, w_here, F32, (crossing[-1],))
+    pieces = finish(halves, last, cuts[:1], head_size)
+    pieces += finish(halves, last, cuts[1:], head_size, pieces)
+    pairs = [(x, swap_tp(x, 1)) for x in pieces]
+    crossing = [out_block([pair], w_far_own, w_far, BF16) for pair in pairs]
+    own_block = out_block(pairs, w_here_own, w_here, F32, (crossing[-1],))
     out = None
-    for cut, x in zip(cuts, crossing):
+    for cut, x in zip(cuts[:-1], crossing):
         out = add_rows(own_block, swap_tp(x, 2), out, cut.start, unit)
-    return out
+    last = own_block[cuts[-1]] + swap_tp(crossing[-1], 2).astype(F32)
+    return lax.dynamic_update_slice_in_dim(out, last.astype(BF16), cuts[-1].start, 0)
 
 
 def solution(mesh):

time: 77.1 us -> 77 us (level)
  starting transfers between devices: 27.1 us -> 24.4 us
  waiting for transfers between devices: 27 us -> 28.7 us
  local copies, waits for them, and re-layouts: 0.7 us -> 1.62 us
    ppermute x8 -> x7, waiting for transfers between devices: 5.57 us -> 8.55 us  [swap_seq(): return lax.ppermute(x, 'seq', [(i, i ^ bit) for i in range(seq_size)])]
    ppermute x8 -> x7, starting transfers between devices: 15.2 us -> 12.9 us  [swap_seq(): return lax.ppermute(x, 'seq', [(i, i ^ bit) for i in range(seq_size)])]
    ppermute x19 -> x17, waiting for transfers between devices: 21.4 us -> 20.2 us  [swap_tp(): return lax.ppermute(x, 'tp', [(i, i ^ bit) for i in range(4)])]
    unnamed x2 -> x4, local copies, waits for them, and re-layouts: 0.7 us -> 1.62 us
    pallas_call x5 -> x4, Pallas kernels: 3.54 us -> 2.89 us  [add_rows(): pl.pallas_call(kernel, grid=(rows // unit,), in_specs=specs, out_specs=pl...]
    ppermute x19 -> x17, starting transfers between devices: 12 us -> 11.5 us  [swap_tp(): return lax.ppermute(x, 'tp', [(i, i ^ bit) for i in range(4)])]
    pallas_call x22 -> x21, Pallas kernels: 18.4 us -> 18.3 us  [call(): pl.pallas_call(run, in_specs=[SMEM] * smem + [HBM] * hbm + [VMEM] * (coun...]
  transfers between devices with their start and end apart: 27 -> 24, of which waited for: 14 -> 14; matrix products, arithmetic and copies ran while one was open for 0% -> 0% of each run, Pallas kernels for 27% -> 27%
where the time goes in v21:
time: 77 us; the launch traced here: 76.8 us
  waiting for transfers between devices  28.7 us (37%)
  starting transfers between devices  24.4 us (32%)
  Pallas kernels  21.2 us (28%)
  local copies, waits for them, and re-layouts  1.62 us (2%)
    ppermute x17, waiting for transfers between devices, swap_tp(): return lax.ppermute(x, 'tp', [(i, i ^ bit) for i in range(4)])  20.2 us
    pallas_call x21, Pallas kernels, call(): pl.pallas_call(run, in_specs=[SMEM] * smem + [HBM] * hbm + [VMEM] * (coun...  18.3 us
    ppermute x7, starting transfers between devices, swap_seq(): return lax.ppermute(x, 'seq', [(i, i ^ bit) for i in range(seq_size)])  12.9 us
    ppermute x17, starting transfers between devices, swap_tp(): return lax.ppermute(x, 'tp', [(i, i ^ bit) for i in range(4)])  11.5 us
    ppermute x7, waiting for transfers between devices, swap_seq(): return lax.ppermute(x, 'seq', [(i, i ^ bit) for i in range(seq_size)])  8.55 us
    pallas_call x4, Pallas kernels, add_rows(): pl.pallas_call(kernel, grid=(rows // unit,), in_specs=specs, out_specs=pl...  2.89 us
    unnamed x4, local copies, waits for them, and re-layouts  1.62 us
  transfers between devices with their start and end apart: 24, of which 14 were waited for; matrix products, arithmetic and copies ran while one was open for 0% of the time, Pallas kernels for 27%

profile of v21, /device:TPU:0, one launch (start us, length us, event | category | flops | bytes accessed | tf_op | source)
XLA Modules:
  0.0 76.8 jit_solution(15216253460610357148)
XLA Ops:
  0.5 2.5 %collective-permute-start = (bf16[512,1024]{1,0:T(8,128)(2,1)}, bf16[512,1024]{1,0:T(8,128)(2,1)S(1)}, u32[]{:S(2)}, u32[]{:S(2)}) collective-permute-start(bf16[512,1024]{1,0:T(8,128)(2,1)} %refs_2_.1), channel_id=1, source_target_pairs={{0,2},{1,3},{2,0},{3,1},{4,6},{5,7},{6,4},{7,5},{8,10},{9,11},{10,... | collective-permute-start | bytes 3145736 | tf_op jit(solution)/shard_map/ppermute | solution.py:434
  4.6 5.3 %shard_map.73 = (f32[512,512]{1,0:T(8,128)S(1)}, f32[512,256]{1,0:T(8,128)S(1)}, f32[512,24]{1,0:T(8,128)S(1)}, bf16[2,1024,512]{2,1,0:T(8,128)(2,1)S(1)}, bf16[...) custom-call(s32[1]{0:T(128)} %bitcast.refs_0_, ...), custom_call_target="tpu_custom_call" | custom-call | tf_op jit(solution)/shard_map/pallas_call | solution.py:41
  10.8 2.6 %collective-permute-start.3 = (f32[8,512]{1,0:T(8,128)S(1)}, f32[8,512]{1,0:T(8,128)S(1)}, u32[]{:S(2)}, u32[]{:S(2)}) collective-permute-start(f32[8,512]{1,0:T(8,128)S(1)} %get-tuple-element.54.refs_1_), channel_id=1, source_target_pairs={{0,4},{4,0},{8,12},{12,8},{16,20},{20,16},{24,28},{28,24},{1,5},{5... | collective-permute-start | bytes 49160 | tf_op jit(solution)/shard_map/ppermute | solution.py:437
  13.4 1.7 %collective-permute-done.3.refs_2_ = f32[8,512]{1,0:T(8,128)S(1)} collective-permute-done((f32[8,512]{1,0:T(8,128)S(1)}, f32[8,512]{1,0:T(8,128)S(1)}, u32[]{:S(2)}, u32[]{:S(2)}) %collective-permute-start.3) | collective-permute-done | bytes 16416 | tf_op jit(solution)/shard_map/ppermute | solution.py:437
  15.2 2.2 %collective-permute-start.4 = (f32[8,512]{1,0:T(8,128)S(1)}, f32[8,512]{1,0:T(8,128)S(1)}, u32[]{:S(2)}, u32[]{:S(2)}) collective-permute-start(f32[8,512]{1,0:T(8,128)S(1)} %get-tuple-element.55.refs_1_), channel_id=1, source_target_pairs={{0,8},{4,12},{8,0},{12,4},{16,24},{20,28},{24,16},{28,20},{1,9},{5... | collective-permute-start | bytes 49160 | tf_op jit(solution)/shard_map/ppermute | solution.py:437
  17.3 1.7 %collective-permute-done.4.refs_2_ = f32[8,512]{1,0:T(8,128)S(1)} collective-permute-done((f32[8,512]{1,0:T(8,128)S(1)}, f32[8,512]{1,0:T(8,128)S(1)}, u32[]{:S(2)}, u32[]{:S(2)}) %collective-permute-start.4) | collective-permute-done | bytes 16416 | tf_op jit(solution)/shard_map/ppermute | solution.py:437
  19.7 7.3 %collective-permute-done.refs_0_.refs_1_ = bf16[512,1024]{1,0:T(8,128)(2,1)S(1)} collective-permute-done((bf16[512,1024]{1,0:T(8,128)(2,1)}, bf16[512,1024]{1,0:T(8,128)(2,1)S(1)}, u32[]{:S(2)}, u32[]{:S(2)}) %collective-permute-start) | collective-permute-done | bytes 1048608 | tf_op jit(solution)/shard_map/ppermute | solution.py:434
  27.6 1.3 %shard_map.77 = (f32[512,512]{1,0:T(8,128)S(1)}, f32[512,256]{1,0:T(8,128)S(1)}, f32[512,24]{1,0:T(8,128)S(1)}) custom-call(s32[1]{0:T(128)} %bitcast.refs_0_, bf16[512,1024]{1,0:T(8,128)(2,1)S(1)} %collective-permute-done.refs_0_.refs_1_, ...), custom_call_target="tpu_custom_call", output_to_operand_aliasing={{0}: (5, {}), {1}: (6, {}), {2}: (7, {})} | custom-call | tf_op jit(solution)/shard_map/pallas_call | solution.py:41
  30.1 1.8 %collective-permute-start.9 = (bf16[128,256]{1,0:T(8,128)(2,1)S(1)}, bf16[128,256]{1,0:T(8,128)(2,1)S(1)}, u32[]{:S(2)}, u32[]{:S(2)}) collective-permute-start(bf16[128,256]{1,0:T(8,128)(2,1)S(1)} %get-tuple-element.73.refs_0_), channel_id=1, source_target_pairs={{0,4},{4,0},{8,12},{12,8},{16,20},{20,16},{24,28},{28,24},{1,5},{5... | collective-permute-start | bytes 196616 | tf_op jit(solution)/shard_map/ppermute | solution.py:437
  32.1 2.4 %collective-permute-done.9.refs_1_.refs_8_ = bf16[128,256]{1,0:T(8,128)(2,1)S(1)} collective-permute-done((bf16[128,256]{1,0:T(8,128)(2,1)S(1)}, bf16[128,256]{1,0:T(8,128)(2,1)S(1)}, u32[]{:S(2)}, u32[]{:S(2)}) %collective-permute-start.9) | collective-permute-done | bytes 65568 | tf_op jit(solution)/shard_map/ppermute | solution.py:437
  34.6 2.1 %collective-permute-start.11 = (bf16[128,256]{1,0:T(8,128)(2,1)S(1)}, bf16[128,256]{1,0:T(8,128)(2,1)S(1)}, u32[]{:S(2)}, u32[]{:S(2)}) collective-permute-start(bf16[128,256]{1,0:T(8,128)(2,1)S(1)} %shard_map.83.refs_0_), channel_id=1, source_target_pairs={{0,8},{4,12},{8,0},{12,4},{16,24},{20,28},{24,16},{28,20},{1,9},{5... | collective-permute-start | bytes 196616 | tf_op jit(solution)/shard_map/ppermute | solution.py:437
  39.1 2.0 %collective-permute-done.12.refs_11_.refs_3_ = bf16[128,256]{1,0:T(8,128)(2,1)S(1)} collective-permute-done((bf16[128,256]{1,0:T(8,128)(2,1)S(1)}, bf16[128,256]{1,0:T(8,128)(2,1)S(1)}, u32[]{:S(2)}, u32[]{:S(2)}) %collective-permute-start.12) | collective-permute-done | bytes 65568 | tf_op jit(solution)/shard_map/ppermute | solution.py:437
  41.1 2.8 %collective-permute-start.13 = (bf16[128,512]{1,0:T(8,128)(2,1)S(1)}, bf16[128,512]{1,0:T(8,128)(2,1)S(1)}, u32[]{:S(2)}, u32[]{:S(2)}) collective-permute-start(bf16[128,512]{1,0:T(8,128)(2,1)S(1)} %shard_map.86), channel_id=1, source_target_pairs={{0,16},{4,20},{8,24},{12,28},{16,0},{20,4},{24,8},{28,12},{1,17},{... | collective-permute-start | bytes 393224 | tf_op jit(solution)/shard_map/ppermute | solution.py:437
  44.0 1.3 %shard_map.82.refs_1_ = f32[512,256]{1,0:T(8,128)S(1)} custom-call(bf16[512,512]{1,0:T(8,128)(2,1)S(1)} %get-tuple-element.62.refs_0_.refs_2_, f32[512,24]{1,0:T(8,128)S(1)} %get-tuple-element.63.refs_1_.refs_3_.refs_6_, bf16[512,128]{1,0:T(8,128)(2,1)S(1)} %get-tuple-element.66.refs_2_, bf16[512,128]{1,0:T(8,128)(2,1)S(1)} %get-tuple-element.67.refs_3_, ...), custom_call_target="tpu_custom_call" | custom-call | tf_op jit(solution)/shard_map/pallas_call | solution.py:41
  45.3 1.3 %shard_map.81.refs_0_ = f32[512,256]{1,0:T(8,128)S(1)} custom-call(bf16[512,512]{1,0:T(8,128)(2,1)S(1)} %get-tuple-element.62.refs_0_.refs_2_, f32[512,24]{1,0:T(8,128)S(1)} %get-tuple-element.63.refs_1_.refs_3_.refs_6_, bf16[512,128]{1,0:T(8,128)(2,1)S(1)} %get-tuple-element.66.refs_2_, bf16[512,128]{1,0:T(8,128)(2,1)S(1)} %get-tuple-element.67.refs_3_, ...), custom_call_target="tpu_custom_call" | custom-call | tf_op jit(solution)/shard_map/pallas_call | solution.py:41
  46.5 1.5 %shard_map.85 = (f32[512,256]{1,0:T(8,128)S(1)}, f32[512,256]{1,0:T(8,128)S(1)}, bf16[512,256]{1,0:T(8,128)(2,1)S(1)}, bf16[512,256]{1,0:T(8,128)(2,1)S(1)}) custom-call(f32[512,256]{1,0:T(8,128)S(1)} %shard_map.81.refs_0_, f32[512,256]{1,0:T(8,128)S(1)} %shard_map.82.refs_1_, bf16[512,512]{1,0:T(8,128)(2,1)S(1)} %get-tuple-element.62.refs_0_.refs_2_, ...), custom_call_target="tpu_custom_call" | custom-call | tf_op jit(solution)/shard_map/pallas_call | solution.py:41
  50.7 1.6 %collective-permute-start.22 = (bf16[128,1024]{1,0:T(8,128)(2,1)S(1)}, bf16[128,1024]{1,0:T(8,128)(2,1)S(1)}, u32[]{:S(2)}, u32[]{:S(2)}) collective-permute-start(bf16[128,1024]{1,0:T(8,128)(2,1)S(1)} %shard_map.94), channel_id=1, source_target_pairs={{0,2},{1,3},{2,0},{3,1},{4,6},{5,7},{6,4},{7,5},{8,10},{9,11},{10,... | collective-permute-start | bytes 786440 | tf_op jit(solution)/shard_map/ppermute | solution.py:434
  53.8 1.6 %collective-permute-start.20 = (bf16[128,1024]{1,0:T(8,128)(2,1)S(1)}, bf16[128,1024]{1,0:T(8,128)(2,1)S(1)}, u32[]{:S(2)}, u32[]{:S(2)}) collective-permute-start(bf16[128,1024]{1,0:T(8,128)(2,1)S(1)} %shard_map.92), channel_id=1, source_target_pairs={{0,2},{1,3},{2,0},{3,1},{4,6},{5,7},{6,4},{7,5},{8,10},{9,11},{10,... | collective-permute-start | bytes 786440 | tf_op jit(solution)/shard_map/ppermute | solution.py:434
  58.2 1.6 %collective-permute-start.23 = (bf16[64,1024]{1,0:T(8,128)(2,1)S(1)}, bf16[64,1024]{1,0:T(8,128)(2,1)S(1)}, u32[]{:S(2)}, u32[]{:S(2)}) collective-permute-start(bf16[64,1024]{1,0:T(8,128)(2,1)S(1)} %shard_map.89.refs_12_), channel_id=1, source_target_pairs={{0,2},{1,3},{2,0},{3,1},{4,6},{5,7},{6,4},{7,5},{8,10},{9,11},{10,... | collective-permute-start | bytes 393224 | tf_op jit(solution)/shard_map/ppermute | solution.py:434
  59.8 1.7 %shard_map.90.h_ref = f32[512,1024]{1,0:T(8,128)S(1)} custom-call(bf16[128,512]{1,0:T(8,128)(2,1)S(1)} %shard_map.87.refs_5_.refs_0_, bf16[128,512]{1,0:T(8,128)(2,1)S(1)} %collective-permute-done.14.refs_1_, bf16[128,512]{1,0:T(8,128)(2,1)S(1)} %get-tuple-element.83.refs_2_.refs_0_, bf16[128,512]{1,0:T(8,128)(2,1)S(1)} %collective-permute-done.15.refs_3_.refs_1_, ...), custom_call_target="tpu_custom_call" | custom-call | tf_op jit(solution)/shard_map/pallas_call | solution.py:41
  62.2 3.3 %collective-permute-done.21.a_ref = bf16[128,1024]{1,0:T(8,128)(2,1)S(1)} collective-permute-done((bf16[128,1024]{1,0:T(8,128)(2,1)S(1)}, bf16[128,1024]{1,0:T(8,128)(2,1)S(1)}, u32[]{:S(2)}, u32[]{:S(2)}) %collective-permute-start.21) | collective-permute-done | bytes 262176 | tf_op jit(solution)/shard_map/ppermute | solution.py:434
  66.2 4.9 %collective-permute-done.20.a_ref = bf16[128,1024]{1,0:T(8,128)(2,1)S(1)} collective-permute-done((bf16[128,1024]{1,0:T(8,128)(2,1)S(1)}, bf16[128,1024]{1,0:T(8,128)(2,1)S(1)}, u32[]{:S(2)}, u32[]{:S(2)}) %collective-permute-start.20) | collective-permute-done | bytes 262176 | tf_op jit(solution)/shard_map/ppermute | solution.py:434
  71.8 2.1 %collective-permute-done.19.a_ref = bf16[64,1024]{1,0:T(8,128)(2,1)S(1)} collective-permute-done((bf16[64,1024]{1,0:T(8,128)(2,1)S(1)}, bf16[64,1024]{1,0:T(8,128)(2,1)S(1)}, u32[]{:S(2)}, u32[]{:S(2)}) %collective-permute-start.19) | collective-permute-done | bytes 131104 | tf_op jit(solution)/shard_map/ppermute | solution.py:434
  74.6 1.5 %collective-permute-done.23 = bf16[64,1024]{1,0:T(8,128)(2,1)S(1)} collective-permute-done((bf16[64,1024]{1,0:T(8,128)(2,1)S(1)}, bf16[64,1024]{1,0:T(8,128)(2,1)S(1)}, u32[]{:S(2)}, u32[]{:S(2)}) %collective-permute-start.23) | collective-permute-done | bytes 131104 | tf_op jit(solution)/shard_map/ppermute | solution.py:434
  (55 shorter events, 18.5 us)
Async XLA Ops:
  0.0 3.0 %collective-permute-start.1 = (bf16[512,1024]{1,0:T(8,128)(2,1)}, bf16[512,1024]{1,0:T(8,128)(2,1)S(1)}, u32[]{:S(2)}, u32[]{:S(2)}) collective-permute-start(bf16[512,1024]{1,0:T(8,128)(2,1)} %refs_2_.1), channel_id=1, source_target_pairs={{0,1},{1,0},{2,3},{3,2},{4,5},{5,4},{6,7},{7,6},{8,9},{9,8},{10,11... | collective-permute-start | bytes 3145736 | tf_op jit(solution)/shard_map/ppermute | solution.py:434
  0.5 26.6 %collective-permute-start = (bf16[512,1024]{1,0:T(8,128)(2,1)}, bf16[512,1024]{1,0:T(8,128)(2,1)S(1)}, u32[]{:S(2)}, u32[]{:S(2)}) collective-permute-start(bf16[512,1024]{1,0:T(8,128)(2,1)} %refs_2_.1), channel_id=1, source_target_pairs={{0,2},{1,3},{2,0},{3,1},{4,6},{5,7},{6,4},{7,5},{8,10},{9,11},{10,... | collective-permute-start | bytes 3145736 | tf_op jit(solution)/shard_map/ppermute | solution.py:434
  9.9 17.1 %collective-permute-start.5 = (bf16[512,1024]{1,0:T(8,128)(2,1)S(1)}, bf16[512,1024]{1,0:T(8,128)(2,1)S(1)}, u32[]{:S(2)}, u32[]{:S(2)}) collective-permute-start(bf16[512,1024]{1,0:T(8,128)(2,1)S(1)} %get-tuple-element.58), channel_id=1, source_target_pairs={{0,1},{1,0},{2,3},{3,2},{4,5},{5,4},{6,7},{7,6},{8,9},{9,8},{10,11... | collective-permute-start | bytes 3145736 | tf_op jit(solution)/shard_map/ppermute | solution.py:434
  10.3 16.7 %collective-permute-start.6 = (bf16[512,1024]{1,0:T(8,128)(2,1)S(1)}, bf16[512,1024]{1,0:T(8,128)(2,1)S(1)}, u32[]{:S(2)}, u32[]{:S(2)}) collective-permute-start(bf16[512,1024]{1,0:T(8,128)(2,1)S(1)} %get-tuple-element.59), channel_id=1, source_target_pairs={{0,1},{1,0},{2,3},{3,2},{4,5},{5,4},{6,7},{7,6},{8,9},{9,8},{10,11... | collective-permute-start | bytes 3145736 | tf_op jit(solution)/shard_map/ppermute | solution.py:434
  10.5 16.6 %collective-permute-start.2 = (bf16[1024,256]{1,0:T(8,128)(2,1)S(1)}, bf16[1024,256]{1,0:T(8,128)(2,1)S(1)}, u32[]{:S(2)}, u32[]{:S(2)}) collective-permute-start(bf16[1024,256]{1,0:T(8,128)(2,1)S(1)} %get-tuple-element.53), channel_id=1, source_target_pairs={{0,1},{1,0},{2,3},{3,2},{4,5},{5,4},{6,7},{7,6},{8,9},{9,8},{10,11... | collective-permute-start | bytes 1572872 | tf_op jit(solution)/shard_map/ppermute | solution.py:434
  10.8 4.3 %collective-permute-start.3 = (f32[8,512]{1,0:T(8,128)S(1)}, f32[8,512]{1,0:T(8,128)S(1)}, u32[]{:S(2)}, u32[]{:S(2)}) collective-permute-start(f32[8,512]{1,0:T(8,128)S(1)} %get-tuple-element.54.refs_1_), channel_id=1, source_target_pairs={{0,4},{4,0},{8,12},{12,8},{16,20},{20,16},{24,28},{28,24},{1,5},{5... | collective-permute-start | bytes 49160 | tf_op jit(solution)/shard_map/ppermute | solution.py:437
  15.2 3.9 %collective-permute-start.4 = (f32[8,512]{1,0:T(8,128)S(1)}, f32[8,512]{1,0:T(8,128)S(1)}, u32[]{:S(2)}, u32[]{:S(2)}) collective-permute-start(f32[8,512]{1,0:T(8,128)S(1)} %get-tuple-element.55.refs_1_), channel_id=1, source_target_pairs={{0,8},{4,12},{8,0},{12,4},{16,24},{20,28},{24,16},{28,20},{1,9},{5... | collective-permute-start | bytes 49160 | tf_op jit(solution)/shard_map/ppermute | solution.py:437
  27.5 1.6 %collective-permute-start.7 = (bf16[512,256]{1,0:T(8,128)(2,1)S(1)}, bf16[512,256]{1,0:T(8,128)(2,1)S(1)}, u32[]{:S(2)}, u32[]{:S(2)}) collective-permute-start(bf16[512,256]{1,0:T(8,128)(2,1)S(1)} %shard_map.76.refs_8_), channel_id=1, source_target_pairs={{0,1},{1,0},{2,3},{3,2},{4,5},{5,4},{6,7},{7,6},{8,9},{9,8},{10,11... | collective-permute-start | bytes 786440 | tf_op jit(solution)/shard_map/ppermute | solution.py:434
  29.1 8.7 %collective-permute-start.8 = (bf16[512,1024]{1,0:T(8,128)(2,1)S(1)}, bf16[512,1024]{1,0:T(8,128)(2,1)S(1)}, u32[]{:S(2)}, u32[]{:S(2)}) collective-permute-start(bf16[512,1024]{1,0:T(8,128)(2,1)S(1)} %shard_map.78), channel_id=1, source_target_pairs={{0,1},{1,0},{2,3},{3,2},{4,5},{5,4},{6,7},{7,6},{8,9},{9,8},{10,11... | collective-permute-start | bytes 3145736 | tf_op jit(solution)/shard_map/ppermute | solution.py:434
  30.1 4.5 %collective-permute-start.9 = (bf16[128,256]{1,0:T(8,128)(2,1)S(1)}, bf16[128,256]{1,0:T(8,128)(2,1)S(1)}, u32[]{:S(2)}, u32[]{:S(2)}) collective-permute-start(bf16[128,256]{1,0:T(8,128)(2,1)S(1)} %get-tuple-element.73.refs_0_), channel_id=1, source_target_pairs={{0,4},{4,0},{8,12},{12,8},{16,20},{20,16},{24,28},{28,24},{1,5},{5... | collective-permute-start | bytes 196616 | tf_op jit(solution)/shard_map/ppermute | solution.py:437
  31.8 4.9 %collective-permute-start.10 = (bf16[128,256]{1,0:T(8,128)(2,1)S(1)}, bf16[128,256]{1,0:T(8,128)(2,1)S(1)}, u32[]{:S(2)}, u32[]{:S(2)}) collective-permute-start(bf16[128,256]{1,0:T(8,128)(2,1)S(1)} %get-tuple-element.74.refs_0_), channel_id=1, source_target_pairs={{0,4},{4,0},{8,12},{12,8},{16,20},{20,16},{24,28},{28,24},{1,5},{5... | collective-permute-start | bytes 196616 | tf_op jit(solution)/shard_map/ppermute | solution.py:437
  34.6 4.5 %collective-permute-start.11 = (bf16[128,256]{1,0:T(8,128)(2,1)S(1)}, bf16[128,256]{1,0:T(8,128)(2,1)S(1)}, u32[]{:S(2)}, u32[]{:S(2)}) collective-permute-start(bf16[128,256]{1,0:T(8,128)(2,1)S(1)} %shard_map.83.refs_0_), channel_id=1, source_target_pairs={{0,8},{4,12},{8,0},{12,4},{16,24},{20,28},{24,16},{28,20},{1,9},{5... | collective-permute-start | bytes 196616 | tf_op jit(solution)/shard_map/ppermute | solution.py:437
  36.8 4.3 %collective-permute-start.12 = (bf16[128,256]{1,0:T(8,128)(2,1)S(1)}, bf16[128,256]{1,0:T(8,128)(2,1)S(1)}, u32[]{:S(2)}, u32[]{:S(2)}) collective-permute-start(bf16[128,256]{1,0:T(8,128)(2,1)S(1)} %shard_map.84.refs_1_), channel_id=1, source_target_pairs={{0,8},{4,12},{8,0},{12,4},{16,24},{20,28},{24,16},{28,20},{1,9},{5... | collective-permute-start | bytes 196616 | tf_op jit(solution)/shard_map/ppermute | solution.py:437
  41.1 7.3 %collective-permute-start.13 = (bf16[128,512]{1,0:T(8,128)(2,1)S(1)}, bf16[128,512]{1,0:T(8,128)(2,1)S(1)}, u32[]{:S(2)}, u32[]{:S(2)}) collective-permute-start(bf16[128,512]{1,0:T(8,128)(2,1)S(1)} %shard_map.86), channel_id=1, source_target_pairs={{0,16},{4,20},{8,24},{12,28},{16,0},{20,4},{24,8},{28,12},{1,17},{... | collective-permute-start | bytes 393224 | tf_op jit(solution)/shard_map/ppermute | solution.py:437
  48.8 1.4 %collective-permute-start.14 = (bf16[128,512]{1,0:T(8,128)(2,1)S(1)}, bf16[128,512]{1,0:T(8,128)(2,1)S(1)}, u32[]{:S(2)}, u32[]{:S(2)}) collective-permute-start(bf16[128,512]{1,0:T(8,128)(2,1)S(1)} %shard_map.87.refs_5_.refs_0_), channel_id=1, source_target_pairs={{0,1},{1,0},{2,3},{3,2},{4,5},{5,4},{6,7},{7,6},{8,9},{9,8},{10,11... | collective-permute-start | bytes 393224 | tf_op jit(solution)/shard_map/ppermute | solution.py:434
  49.4 2.8 %collective-permute-start.15 = (bf16[128,512]{1,0:T(8,128)(2,1)S(1)}, bf16[128,512]{1,0:T(8,128)(2,1)S(1)}, u32[]{:S(2)}, u32[]{:S(2)}) collective-permute-start(bf16[128,512]{1,0:T(8,128)(2,1)S(1)} %get-tuple-element.83.refs_2_.refs_0_), channel_id=1, source_target_pairs={{0,1},{1,0},{2,3},{3,2},{4,5},{5,4},{6,7},{7,6},{8,9},{9,8},{10,11... | collective-permute-start | bytes 393224 | tf_op jit(solution)/shard_map/ppermute | solution.py:434
  50.0 3.3 %collective-permute-start.16 = (bf16[128,512]{1,0:T(8,128)(2,1)S(1)}, bf16[128,512]{1,0:T(8,128)(2,1)S(1)}, u32[]{:S(2)}, u32[]{:S(2)}) collective-permute-start(bf16[128,512]{1,0:T(8,128)(2,1)S(1)} %get-tuple-element.84.refs_4_.refs_0_), channel_id=1, source_target_pairs={{0,1},{1,0},{2,3},{3,2},{4,5},{5,4},{6,7},{7,6},{8,9},{9,8},{10,11... | collective-permute-start | bytes 393224 | tf_op jit(solution)/shard_map/ppermute | solution.py:434
  50.7 10.8 %collective-permute-start.22 = (bf16[128,1024]{1,0:T(8,128)(2,1)S(1)}, bf16[128,1024]{1,0:T(8,128)(2,1)S(1)}, u32[]{:S(2)}, u32[]{:S(2)}) collective-permute-start(bf16[128,1024]{1,0:T(8,128)(2,1)S(1)} %shard_map.94), channel_id=1, source_target_pairs={{0,2},{1,3},{2,0},{3,1},{4,6},{5,7},{6,4},{7,5},{8,10},{9,11},{10,... | collective-permute-start | bytes 786440 | tf_op jit(solution)/shard_map/ppermute | solution.py:434
  52.7 12.8 %collective-permute-start.21 = (bf16[128,1024]{1,0:T(8,128)(2,1)S(1)}, bf16[128,1024]{1,0:T(8,128)(2,1)S(1)}, u32[]{:S(2)}, u32[]{:S(2)}) collective-permute-start(bf16[128,1024]{1,0:T(8,128)(2,1)S(1)} %shard_map.93), channel_id=1, source_target_pairs={{0,2},{1,3},{2,0},{3,1},{4,6},{5,7},{6,4},{7,5},{8,10},{9,11},{10,... | collective-permute-start | bytes 786440 | tf_op jit(solution)/shard_map/ppermute | solution.py:434
  53.8 17.3 %collective-permute-start.20 = (bf16[128,1024]{1,0:T(8,128)(2,1)S(1)}, bf16[128,1024]{1,0:T(8,128)(2,1)S(1)}, u32[]{:S(2)}, u32[]{:S(2)}) collective-permute-start(bf16[128,1024]{1,0:T(8,128)(2,1)S(1)} %shard_map.92), channel_id=1, source_target_pairs={{0,2},{1,3},{2,0},{3,1},{4,6},{5,7},{6,4},{7,5},{8,10},{9,11},{10,... | collective-permute-start | bytes 786440 | tf_op jit(solution)/shard_map/ppermute | solution.py:434
  55.4 1.3 %collective-permute-start.17 = (bf16[64,512]{1,0:T(8,128)(2,1)S(1)}, bf16[64,512]{1,0:T(8,128)(2,1)S(1)}, u32[]{:S(2)}, u32[]{:S(2)}) collective-permute-start(bf16[64,512]{1,0:T(8,128)(2,1)S(1)} %get-tuple-element.85.refs_6_.refs_0_), channel_id=1, source_target_pairs={{0,1},{1,0},{2,3},{3,2},{4,5},{5,4},{6,7},{7,6},{8,9},{9,8},{10,11... | collective-permute-start | bytes 196616 | tf_op jit(solution)/shard_map/ppermute | solution.py:434
  55.4 2.3 %collective-permute-start.18 = (bf16[64,512]{1,0:T(8,128)(2,1)S(1)}, bf16[64,512]{1,0:T(8,128)(2,1)S(1)}, u32[]{:S(2)}, u32[]{:S(2)}) collective-permute-start(bf16[64,512]{1,0:T(8,128)(2,1)S(1)} %get-tuple-element.86.refs_0_.refs_8_), channel_id=1, source_target_pairs={{0,1},{1,0},{2,3},{3,2},{4,5},{5,4},{6,7},{7,6},{8,9},{9,8},{10,11... | collective-permute-start | bytes 196616 | tf_op jit(solution)/shard_map/ppermute | solution.py:434
  57.1 16.8 %collective-permute-start.19 = (bf16[64,1024]{1,0:T(8,128)(2,1)S(1)}, bf16[64,1024]{1,0:T(8,128)(2,1)S(1)}, u32[]{:S(2)}, u32[]{:S(2)}) collective-permute-start(bf16[64,1024]{1,0:T(8,128)(2,1)S(1)} %shard_map.91), channel_id=1, source_target_pairs={{0,2},{1,3},{2,0},{3,1},{4,6},{5,7},{6,4},{7,5},{8,10},{9,11},{10,... | collective-permute-start | bytes 393224 | tf_op jit(solution)/shard_map/ppermute | solution.py:434
  58.2 17.9 %collective-permute-start.23 = (bf16[64,1024]{1,0:T(8,128)(2,1)S(1)}, bf16[64,1024]{1,0:T(8,128)(2,1)S(1)}, u32[]{:S(2)}, u32[]{:S(2)}) collective-permute-start(bf16[64,1024]{1,0:T(8,128)(2,1)S(1)} %shard_map.89.refs_12_), channel_id=1, source_target_pairs={{0,2},{1,3},{2,0},{3,1},{4,6},{5,7},{6,4},{7,5},{8,10},{9,11},{10,... | collective-permute-start | bytes 393224 | tf_op jit(solution)/shard_map/ppermute | solution.py:434
  (2 other events, 1.6 us)

commit v22 on v20

--- a/solution.py
+++ b/solution.py
@@ -433,7 +433,7 @@
     )
 
     unit = rows // 8
-    ends = (0, 3, 5, 7, 8)
+    ends = (0, 2, 4, 6, 8)
     cuts = [slice(start * unit, stop * unit) for start, stop in zip(ends, ends[1:])]
     pieces = finish(local, scaled, earlier[-1], cuts[:1], head_size)
     pieces += finish(local, scaled, earlier[-1], cuts[1:], head_size, pieces)

time: 76.5 us -> 76.6 us (level)
  Pallas kernels: 19.7 us -> 18.8 us
  transfers between devices with their start and end apart: 23 -> 23, of which waited for: 14 -> 11; matrix products, arithmetic and copies ran while one was open for 0% -> 0% of each run, Pallas kernels for 24% -> 23%
where the time goes in v22:
time: 76.6 us; the launch traced here: 76.4 us
  waiting for transfers between devices  33.2 us (43%)
  starting transfers between devices  21.8 us (28%)
  Pallas kernels  18.8 us (25%)
  local copies, waits for them, and re-layouts  1.62 us (2%)
  other arithmetic  0.77 us (1%)
    ppermute x18, waiting for transfers between devices, swap_tp(): return lax.ppermute(x, 'tp', [(i, i ^ bit) for i in range(4)])  24.4 us
    pallas_call x18, Pallas kernels, call(): pl.pallas_call(run, in_specs=[SMEM] * smem + [HBM] * hbm + [VMEM] * (coun...  16.6 us
    ppermute x5, starting transfers between devices, swap_seq(): return lax.ppermute(x, 'seq', [(i, i ^ bit) for i in range(seq_size)])  11.3 us
    ppermute x18, starting transfers between devices, swap_tp(): return lax.ppermute(x, 'tp', [(i, i ^ bit) for i in range(4)])  10.5 us
    ppermute x5, waiting for transfers between devices, swap_seq(): return lax.ppermute(x, 'seq', [(i, i ^ bit) for i in range(seq_size)])  8.77 us
    pallas_call x3, Pallas kernels, add_rows(): pl.pallas_call(kernel, grid=(rows // unit,), in_specs=specs, out_specs=pl...  2.19 us
    unnamed x4, local copies, waits for them, and re-layouts  1.62 us
  transfers between devices with their start and end apart: 23, of which 11 were waited for; matrix products, arithmetic and copies ran while one was open for 0% of the time, Pallas kernels for 23%

profile of v22, /device:TPU:0, one launch (start us, length us, event | category | flops | bytes accessed | tf_op | source)
XLA Modules:
  0.0 76.4 jit_solution(12860497786484396389)
XLA Ops:
  0.5 2.5 %collective-permute-start = (bf16[512,1024]{1,0:T(8,128)(2,1)}, bf16[512,1024]{1,0:T(8,128)(2,1)S(1)}, u32[]{:S(2)}, u32[]{:S(2)}) collective-permute-start(bf16[512,1024]{1,0:T(8,128)(2,1)} %refs_2_.1), channel_id=1, source_target_pairs={{0,2},{1,3},{2,0},{3,1},{4,6},{5,7},{6,4},{7,5},{8,10},{9,11},{10,... | collective-permute-start | bytes 3145736 | tf_op jit(solution)/shard_map/ppermute | solution.py:391
  3.0 0.9 %copy-done = bf16[4096,24]{0,1:T(8,128)(2,1)S(1)} copy-done((bf16[4096,24]{0,1:T(8,128)(2,1)S(1)}, bf16[4096,24]{0,1:T(8,128)(2,1)}, u32[]{:S(2)}) %copy-start) | copy-done | bytes 196632
  4.6 5.3 %shard_map.73 = (f32[512,512]{1,0:T(8,128)S(1)}, f32[512,256]{1,0:T(8,128)S(1)}, f32[512,24]{1,0:T(8,128)S(1)}, bf16[2,1024,512]{2,1,0:T(8,128)(2,1)S(1)}, bf16[...) custom-call(s32[1]{0:T(128)} %bitcast.refs_0_, ...), custom_call_target="tpu_custom_call" | custom-call | tf_op jit(solution)/shard_map/pallas_call | solution.py:41
  10.8 2.6 %collective-permute-start.3 = (f32[8,512]{1,0:T(8,128)S(1)}, f32[8,512]{1,0:T(8,128)S(1)}, u32[]{:S(2)}, u32[]{:S(2)}) collective-permute-start(f32[8,512]{1,0:T(8,128)S(1)} %get-tuple-element.51.refs_1_), channel_id=1, source_target_pairs={{0,4},{4,0},{8,12},{12,8},{16,20},{20,16},{24,28},{28,24},{1,5},{5... | collective-permute-start | bytes 49160 | tf_op jit(solution)/shard_map/ppermute | solution.py:394
  13.4 1.7 %collective-permute-done.3.refs_2_ = f32[8,512]{1,0:T(8,128)S(1)} collective-permute-done((f32[8,512]{1,0:T(8,128)S(1)}, f32[8,512]{1,0:T(8,128)S(1)}, u32[]{:S(2)}, u32[]{:S(2)}) %collective-permute-start.3) | collective-permute-done | bytes 16416 | tf_op jit(solution)/shard_map/ppermute | solution.py:394
  15.2 2.2 %collective-permute-start.4 = (f32[8,512]{1,0:T(8,128)S(1)}, f32[8,512]{1,0:T(8,128)S(1)}, u32[]{:S(2)}, u32[]{:S(2)}) collective-permute-start(f32[8,512]{1,0:T(8,128)S(1)} %get-tuple-element.52.refs_1_), channel_id=1, source_target_pairs={{0,8},{4,12},{8,0},{12,4},{16,24},{20,28},{24,16},{28,20},{1,9},{5... | collective-permute-start | bytes 49160 | tf_op jit(solution)/shard_map/ppermute | solution.py:394
  17.3 1.7 %collective-permute-done.4.refs_2_ = f32[8,512]{1,0:T(8,128)S(1)} collective-permute-done((f32[8,512]{1,0:T(8,128)S(1)}, f32[8,512]{1,0:T(8,128)S(1)}, u32[]{:S(2)}, u32[]{:S(2)}) %collective-permute-start.4) | collective-permute-done | bytes 16416 | tf_op jit(solution)/shard_map/ppermute | solution.py:394
  19.7 7.3 %collective-permute-done.refs_0_.refs_1_ = bf16[512,1024]{1,0:T(8,128)(2,1)S(1)} collective-permute-done((bf16[512,1024]{1,0:T(8,128)(2,1)}, bf16[512,1024]{1,0:T(8,128)(2,1)S(1)}, u32[]{:S(2)}, u32[]{:S(2)}) %collective-permute-start) | collective-permute-done | bytes 1048608 | tf_op jit(solution)/shard_map/ppermute | solution.py:391
  28.0 1.1 %collective-permute-done.7.refs_1_ = bf16[512,256]{1,0:T(8,128)(2,1)S(1)} collective-permute-done((bf16[512,256]{1,0:T(8,128)(2,1)S(1)}, bf16[512,256]{1,0:T(8,128)(2,1)S(1)}, u32[]{:S(2)}, u32[]{:S(2)}) %collective-permute-start.7) | collective-permute-done | bytes 262176 | tf_op jit(solution)/shard_map/ppermute | solution.py:391
  29.7 1.8 %collective-permute-start.12 = (bf16[128,512]{1,0:T(8,128)(2,1)S(1)}, bf16[128,512]{1,0:T(8,128)(2,1)S(1)}, u32[]{:S(2)}, u32[]{:S(2)}) collective-permute-start(bf16[128,512]{1,0:T(8,128)(2,1)S(1)} %get-tuple-element.71.refs_0_), channel_id=1, source_target_pairs={{0,4},{4,0},{8,12},{12,8},{16,20},{20,16},{24,28},{28,24},{1,5},{5... | collective-permute-start | bytes 393224 | tf_op jit(solution)/shard_map/ppermute | solution.py:394
  31.4 1.1 %shard_map.79 = (f32[512,512]{1,0:T(8,128)S(1)}, f32[512,24]{1,0:T(8,128)S(1)}) custom-call(s32[1]{0:T(128)} %bitcast.refs_0_, bf16[512,1024]{1,0:T(8,128)(2,1)S(1)} %collective-permute-done.refs_0_.refs_1_, bf16[2,1024,512]{2,1,0:T(8,128)(2,1)S(1)} %get-tuple-element.44.refs_2_.refs_5_, ...), custom_call_target="tpu_custom_call", output_to_operand_aliasing={{0}: (4, {}), {1}: (5, {})} | custom-call | flops 562036736 | bytes 5537796 | tf_op jit(solution)/shard_map/pallas_call | solution.py:41
  33.7 1.6 %collective-permute-done.12.refs_1_.refs_16_ = bf16[128,512]{1,0:T(8,128)(2,1)S(1)} collective-permute-done((bf16[128,512]{1,0:T(8,128)(2,1)S(1)}, bf16[128,512]{1,0:T(8,128)(2,1)S(1)}, u32[]{:S(2)}, u32[]{:S(2)}) %collective-permute-start.12) | collective-permute-done | bytes 131104 | tf_op jit(solution)/shard_map/ppermute | solution.py:394
  35.3 1.9 %collective-permute-start.13 = (bf16[128,512]{1,0:T(8,128)(2,1)S(1)}, bf16[128,512]{1,0:T(8,128)(2,1)S(1)}, u32[]{:S(2)}, u32[]{:S(2)}) collective-permute-start(bf16[128,512]{1,0:T(8,128)(2,1)S(1)} %shard_map.81.refs_0_), channel_id=1, source_target_pairs={{0,8},{4,12},{8,0},{12,4},{16,24},{20,28},{24,16},{28,20},{1,9},{5... | collective-permute-start | bytes 393224 | tf_op jit(solution)/shard_map/ppermute | solution.py:394
  37.2 3.2 %collective-permute-done.13.refs_17_.refs_1_ = bf16[128,512]{1,0:T(8,128)(2,1)S(1)} collective-permute-done((bf16[128,512]{1,0:T(8,128)(2,1)S(1)}, bf16[128,512]{1,0:T(8,128)(2,1)S(1)}, u32[]{:S(2)}, u32[]{:S(2)}) %collective-permute-start.13) | collective-permute-done | bytes 131104 | tf_op jit(solution)/shard_map/ppermute | solution.py:394
  40.4 2.9 %collective-permute-start.14 = (bf16[128,512]{1,0:T(8,128)(2,1)S(1)}, bf16[128,512]{1,0:T(8,128)(2,1)S(1)}, u32[]{:S(2)}, u32[]{:S(2)}) collective-permute-start(bf16[128,512]{1,0:T(8,128)(2,1)S(1)} %shard_map.83), channel_id=1, source_target_pairs={{0,16},{4,20},{8,24},{12,28},{16,0},{20,4},{24,8},{28,12},{1,17},{... | collective-permute-start | bytes 393224 | tf_op jit(solution)/shard_map/ppermute | solution.py:394
  43.3 4.0 %shard_map.82 = (f32[512,512]{1,0:T(8,128)S(1)}, bf16[512,512]{1,0:T(8,128)(2,1)S(1)}, bf16[512,512]{1,0:T(8,128)(2,1)}, f32[512,24]{1,0:T(8,128)}) custom-call(s32[1]{0:T(128)} %bitcast.refs_0_, bf16[512,256]{1,0:T(8,128)(2,1)S(1)} %collective-permute-done.8.refs_1_, bf16[512,256]{1,0:T(8,128)(2,1)S(1)} %collective-permute-done.9.refs_2_, ...), custom_call_target="tpu_custom_call" | custom-call | flops 1073741824 | bytes 7176196 | tf_op jit(solution)/shard_map/pallas_call | solution.py:41
  50.4 1.7 %collective-permute-start.21 = (bf16[128,1024]{1,0:T(8,128)(2,1)S(1)}, bf16[128,1024]{1,0:T(8,128)(2,1)S(1)}, u32[]{:S(2)}, u32[]{:S(2)}) collective-permute-start(bf16[128,1024]{1,0:T(8,128)(2,1)S(1)} %shard_map.90), channel_id=1, source_target_pairs={{0,2},{1,3},{2,0},{3,1},{4,6},{5,7},{6,4},{7,5},{8,10},{9,11},{10,... | collective-permute-start | bytes 786440 | tf_op jit(solution)/shard_map/ppermute | solution.py:391
  53.5 1.7 %collective-permute-start.19 = (bf16[128,1024]{1,0:T(8,128)(2,1)S(1)}, bf16[128,1024]{1,0:T(8,128)(2,1)S(1)}, u32[]{:S(2)}, u32[]{:S(2)}) collective-permute-start(bf16[128,1024]{1,0:T(8,128)(2,1)S(1)} %shard_map.88), channel_id=1, source_target_pairs={{0,2},{1,3},{2,0},{3,1},{4,6},{5,7},{6,4},{7,5},{8,10},{9,11},{10,... | collective-permute-start | bytes 786440 | tf_op jit(solution)/shard_map/ppermute | solution.py:391
  56.1 1.3 %shard_map.87.h_ref = f32[512,1024]{1,0:T(8,128)S(1)} custom-call(bf16[128,512]{1,0:T(8,128)(2,1)S(1)} %shard_map.84.refs_3_.refs_0_, bf16[128,512]{1,0:T(8,128)(2,1)S(1)} %collective-permute-done.15.refs_1_, bf16[128,512]{1,0:T(8,128)(2,1)S(1)} %get-tuple-element.78.refs_2_.refs_0_, bf16[128,512]{1,0:T(8,128)(2,1)S(1)} %collective-permute-done.16.refs_3_.refs_1_, ...), custom_call_target="tpu_custom_call" | custom-call | tf_op jit(solution)/shard_map/pallas_call | solution.py:41
  57.4 2.2 %collective-permute-done.21.a_ref = bf16[128,1024]{1,0:T(8,128)(2,1)S(1)} collective-permute-done((bf16[128,1024]{1,0:T(8,128)(2,1)S(1)}, bf16[128,1024]{1,0:T(8,128)(2,1)S(1)}, u32[]{:S(2)}, u32[]{:S(2)}) %collective-permute-start.21) | collective-permute-done | bytes 262176 | tf_op jit(solution)/shard_map/ppermute | solution.py:391
  60.3 4.9 %collective-permute-done.20.a_ref = bf16[128,1024]{1,0:T(8,128)(2,1)S(1)} collective-permute-done((bf16[128,1024]{1,0:T(8,128)(2,1)S(1)}, bf16[128,1024]{1,0:T(8,128)(2,1)S(1)}, u32[]{:S(2)}, u32[]{:S(2)}) %collective-permute-start.20) | collective-permute-done | bytes 262176 | tf_op jit(solution)/shard_map/ppermute | solution.py:391
  65.9 4.9 %collective-permute-done.19.a_ref = bf16[128,1024]{1,0:T(8,128)(2,1)S(1)} collective-permute-done((bf16[128,1024]{1,0:T(8,128)(2,1)S(1)}, bf16[128,1024]{1,0:T(8,128)(2,1)S(1)}, u32[]{:S(2)}, u32[]{:S(2)}) %collective-permute-start.19) | collective-permute-done | bytes 262176 | tf_op jit(solution)/shard_map/ppermute | solution.py:391
  71.6 4.0 %collective-permute-done.22 = bf16[128,1024]{1,0:T(8,128)(2,1)S(1)} collective-permute-done((bf16[128,1024]{1,0:T(8,128)(2,1)S(1)}, bf16[128,1024]{1,0:T(8,128)(2,1)S(1)}, u32[]{:S(2)}, u32[]{:S(2)}) %collective-permute-start.22) | collective-permute-done | bytes 262176 | tf_op jit(solution)/shard_map/ppermute | solution.py:391
  75.6 0.8 %fusion.1 = bf16[512,1024]{1,0:T(8,128)(2,1)} fusion(bf16[512,1024]{1,0:T(8,128)(2,1)} %shard_map.93, bf16[128,1024]{1,0:T(8,128)(2,1)S(1)} %collective-permute-done.22, f32[512,1024]{1,0:T(8,128)S(1)} %shard_map.87.h_ref), kind=kLoop, calls=%fused_computation.2 | loop fusion | flops 393216 | bytes 1048576 | tf_op jit(solution)/shard_map/dynamic_update_slice | solution.py:447
  (48 shorter events, 13.2 us)
Async XLA Ops:
  0.0 3.0 %collective-permute-start.1 = (bf16[512,1024]{1,0:T(8,128)(2,1)}, bf16[512,1024]{1,0:T(8,128)(2,1)S(1)}, u32[]{:S(2)}, u32[]{:S(2)}) collective-permute-start(bf16[512,1024]{1,0:T(8,128)(2,1)} %refs_2_.1), channel_id=1, source_target_pairs={{0,1},{1,0},{2,3},{3,2},{4,5},{5,4},{6,7},{7,6},{8,9},{9,8},{10,11... | collective-permute-start | bytes 3145736 | tf_op jit(solution)/shard_map/ppermute | solution.py:391
  0.5 26.6 %collective-permute-start = (bf16[512,1024]{1,0:T(8,128)(2,1)}, bf16[512,1024]{1,0:T(8,128)(2,1)S(1)}, u32[]{:S(2)}, u32[]{:S(2)}) collective-permute-start(bf16[512,1024]{1,0:T(8,128)(2,1)} %refs_2_.1), channel_id=1, source_target_pairs={{0,2},{1,3},{2,0},{3,1},{4,6},{5,7},{6,4},{7,5},{8,10},{9,11},{10,... | collective-permute-start | bytes 3145736 | tf_op jit(solution)/shard_map/ppermute | solution.py:391
  3.0 0.9 %copy-start = (bf16[4096,24]{0,1:T(8,128)(2,1)S(1)}, bf16[4096,24]{0,1:T(8,128)(2,1)}, u32[]{:S(2)}) copy-start(bf16[4096,24]{0,1:T(8,128)(2,1)} %param.12) | copy-start | bytes 589828
  9.9 17.1 %collective-permute-start.5 = (bf16[512,1024]{1,0:T(8,128)(2,1)S(1)}, bf16[512,1024]{1,0:T(8,128)(2,1)S(1)}, u32[]{:S(2)}, u32[]{:S(2)}) collective-permute-start(bf16[512,1024]{1,0:T(8,128)(2,1)S(1)} %get-tuple-element.55), channel_id=1, source_target_pairs={{0,1},{1,0},{2,3},{3,2},{4,5},{5,4},{6,7},{7,6},{8,9},{9,8},{10,11... | collective-permute-start | bytes 3145736 | tf_op jit(solution)/shard_map/ppermute | solution.py:391
  10.3 16.7 %collective-permute-start.6 = (bf16[512,1024]{1,0:T(8,128)(2,1)S(1)}, bf16[512,1024]{1,0:T(8,128)(2,1)S(1)}, u32[]{:S(2)}, u32[]{:S(2)}) collective-permute-start(bf16[512,1024]{1,0:T(8,128)(2,1)S(1)} %get-tuple-element.56), channel_id=1, source_target_pairs={{0,1},{1,0},{2,3},{3,2},{4,5},{5,4},{6,7},{7,6},{8,9},{9,8},{10,11... | collective-permute-start | bytes 3145736 | tf_op jit(solution)/shard_map/ppermute | solution.py:391
  10.5 16.6 %collective-permute-start.2 = (bf16[1024,256]{1,0:T(8,128)(2,1)S(1)}, bf16[1024,256]{1,0:T(8,128)(2,1)S(1)}, u32[]{:S(2)}, u32[]{:S(2)}) collective-permute-start(bf16[1024,256]{1,0:T(8,128)(2,1)S(1)} %get-tuple-element.50), channel_id=1, source_target_pairs={{0,1},{1,0},{2,3},{3,2},{4,5},{5,4},{6,7},{7,6},{8,9},{9,8},{10,11... | collective-permute-start | bytes 1572872 | tf_op jit(solution)/shard_map/ppermute | solution.py:391
  10.8 4.3 %collective-permute-start.3 = (f32[8,512]{1,0:T(8,128)S(1)}, f32[8,512]{1,0:T(8,128)S(1)}, u32[]{:S(2)}, u32[]{:S(2)}) collective-permute-start(f32[8,512]{1,0:T(8,128)S(1)} %get-tuple-element.51.refs_1_), channel_id=1, source_target_pairs={{0,4},{4,0},{8,12},{12,8},{16,20},{20,16},{24,28},{28,24},{1,5},{5... | collective-permute-start | bytes 49160 | tf_op jit(solution)/shard_map/ppermute | solution.py:394
  15.2 3.9 %collective-permute-start.4 = (f32[8,512]{1,0:T(8,128)S(1)}, f32[8,512]{1,0:T(8,128)S(1)}, u32[]{:S(2)}, u32[]{:S(2)}) collective-permute-start(f32[8,512]{1,0:T(8,128)S(1)} %get-tuple-element.52.refs_1_), channel_id=1, source_target_pairs={{0,8},{4,12},{8,0},{12,4},{16,24},{20,28},{24,16},{28,20},{1,9},{5... | collective-permute-start | bytes 49160 | tf_op jit(solution)/shard_map/ppermute | solution.py:394
  27.5 1.6 %collective-permute-start.7 = (bf16[512,256]{1,0:T(8,128)(2,1)S(1)}, bf16[512,256]{1,0:T(8,128)(2,1)S(1)}, u32[]{:S(2)}, u32[]{:S(2)}) collective-permute-start(bf16[512,256]{1,0:T(8,128)(2,1)S(1)} %shard_map.76.refs_3_), channel_id=1, source_target_pairs={{0,1},{1,0},{2,3},{3,2},{4,5},{5,4},{6,7},{7,6},{8,9},{9,8},{10,11... | collective-permute-start | bytes 786440 | tf_op jit(solution)/shard_map/ppermute | solution.py:391
  29.7 5.6 %collective-permute-start.12 = (bf16[128,512]{1,0:T(8,128)(2,1)S(1)}, bf16[128,512]{1,0:T(8,128)(2,1)S(1)}, u32[]{:S(2)}, u32[]{:S(2)}) collective-permute-start(bf16[128,512]{1,0:T(8,128)(2,1)S(1)} %get-tuple-element.71.refs_0_), channel_id=1, source_target_pairs={{0,4},{4,0},{8,12},{12,8},{16,20},{20,16},{24,28},{28,24},{1,5},{5... | collective-permute-start | bytes 393224 | tf_op jit(solution)/shard_map/ppermute | solution.py:394
  32.6 10.7 %collective-permute-start.8 = (bf16[512,256]{1,0:T(8,128)(2,1)S(1)}, bf16[512,256]{1,0:T(8,128)(2,1)S(1)}, u32[]{:S(2)}, u32[]{:S(2)}) collective-permute-start(bf16[512,256]{1,0:T(8,128)(2,1)S(1)} %get-tuple-element.60), channel_id=1, source_target_pairs={{0,1},{1,0},{2,3},{3,2},{4,5},{5,4},{6,7},{7,6},{8,9},{9,8},{10,11... | collective-permute-start | bytes 786440 | tf_op jit(solution)/shard_map/ppermute | solution.py:391
  32.7 10.6 %collective-permute-start.9 = (bf16[512,256]{1,0:T(8,128)(2,1)S(1)}, bf16[512,256]{1,0:T(8,128)(2,1)S(1)}, u32[]{:S(2)}, u32[]{:S(2)}) collective-permute-start(bf16[512,256]{1,0:T(8,128)(2,1)S(1)} %get-tuple-element.61), channel_id=1, source_target_pairs={{0,1},{1,0},{2,3},{3,2},{4,5},{5,4},{6,7},{7,6},{8,9},{9,8},{10,11... | collective-permute-start | bytes 786440 | tf_op jit(solution)/shard_map/ppermute | solution.py:391
  33.2 10.1 %collective-permute-start.10 = (bf16[512,256]{1,0:T(8,128)(2,1)S(1)}, bf16[512,256]{1,0:T(8,128)(2,1)S(1)}, u32[]{:S(2)}, u32[]{:S(2)}) collective-permute-start(bf16[512,256]{1,0:T(8,128)(2,1)S(1)} %get-tuple-element.62), channel_id=1, source_target_pairs={{0,1},{1,0},{2,3},{3,2},{4,5},{5,4},{6,7},{7,6},{8,9},{9,8},{10,11... | collective-permute-start | bytes 786440 | tf_op jit(solution)/shard_map/ppermute | solution.py:391
  33.2 10.0 %collective-permute-start.11 = (bf16[512,256]{1,0:T(8,128)(2,1)S(1)}, bf16[512,256]{1,0:T(8,128)(2,1)S(1)}, u32[]{:S(2)}, u32[]{:S(2)}) collective-permute-start(bf16[512,256]{1,0:T(8,128)(2,1)S(1)} %get-tuple-element.63), channel_id=1, source_target_pairs={{0,1},{1,0},{2,3},{3,2},{4,5},{5,4},{6,7},{7,6},{8,9},{9,8},{10,11... | collective-permute-start | bytes 786440 | tf_op jit(solution)/shard_map/ppermute | solution.py:391
  35.3 5.0 %collective-permute-start.13 = (bf16[128,512]{1,0:T(8,128)(2,1)S(1)}, bf16[128,512]{1,0:T(8,128)(2,1)S(1)}, u32[]{:S(2)}, u32[]{:S(2)}) collective-permute-start(bf16[128,512]{1,0:T(8,128)(2,1)S(1)} %shard_map.81.refs_0_), channel_id=1, source_target_pairs={{0,8},{4,12},{8,0},{12,4},{16,24},{20,28},{24,16},{28,20},{1,9},{5... | collective-permute-start | bytes 393224 | tf_op jit(solution)/shard_map/ppermute | solution.py:394
  40.4 7.5 %collective-permute-start.14 = (bf16[128,512]{1,0:T(8,128)(2,1)S(1)}, bf16[128,512]{1,0:T(8,128)(2,1)S(1)}, u32[]{:S(2)}, u32[]{:S(2)}) collective-permute-start(bf16[128,512]{1,0:T(8,128)(2,1)S(1)} %shard_map.83), channel_id=1, source_target_pairs={{0,16},{4,20},{8,24},{12,28},{16,0},{20,4},{24,8},{28,12},{1,17},{... | collective-permute-start | bytes 393224 | tf_op jit(solution)/shard_map/ppermute | solution.py:394
  48.2 1.7 %collective-permute-start.15 = (bf16[128,512]{1,0:T(8,128)(2,1)S(1)}, bf16[128,512]{1,0:T(8,128)(2,1)S(1)}, u32[]{:S(2)}, u32[]{:S(2)}) collective-permute-start(bf16[128,512]{1,0:T(8,128)(2,1)S(1)} %shard_map.84.refs_3_.refs_0_), channel_id=1, source_target_pairs={{0,1},{1,0},{2,3},{3,2},{4,5},{5,4},{6,7},{7,6},{8,9},{9,8},{10,11... | collective-permute-start | bytes 393224 | tf_op jit(solution)/shard_map/ppermute | solution.py:391
  48.8 3.2 %collective-permute-start.16 = (bf16[128,512]{1,0:T(8,128)(2,1)S(1)}, bf16[128,512]{1,0:T(8,128)(2,1)S(1)}, u32[]{:S(2)}, u32[]{:S(2)}) collective-permute-start(bf16[128,512]{1,0:T(8,128)(2,1)S(1)} %get-tuple-element.78.refs_2_.refs_0_), channel_id=1, source_target_pairs={{0,1},{1,0},{2,3},{3,2},{4,5},{5,4},{6,7},{7,6},{8,9},{9,8},{10,11... | collective-permute-start | bytes 393224 | tf_op jit(solution)/shard_map/ppermute | solution.py:391
  49.4 3.6 %collective-permute-start.17 = (bf16[128,512]{1,0:T(8,128)(2,1)S(1)}, bf16[128,512]{1,0:T(8,128)(2,1)S(1)}, u32[]{:S(2)}, u32[]{:S(2)}) collective-permute-start(bf16[128,512]{1,0:T(8,128)(2,1)S(1)} %get-tuple-element.79.refs_4_.refs_0_), channel_id=1, source_target_pairs={{0,1},{1,0},{2,3},{3,2},{4,5},{5,4},{6,7},{7,6},{8,9},{9,8},{10,11... | collective-permute-start | bytes 393224 | tf_op jit(solution)/shard_map/ppermute | solution.py:391
  49.5 5.7 %collective-permute-start.18 = (bf16[128,512]{1,0:T(8,128)(2,1)S(1)}, bf16[128,512]{1,0:T(8,128)(2,1)S(1)}, u32[]{:S(2)}, u32[]{:S(2)}) collective-permute-start(bf16[128,512]{1,0:T(8,128)(2,1)S(1)} %get-tuple-element.80.refs_0_.refs_6_), channel_id=1, source_target_pairs={{0,1},{1,0},{2,3},{3,2},{4,5},{5,4},{6,7},{7,6},{8,9},{9,8},{10,11... | collective-permute-start | bytes 393224 | tf_op jit(solution)/shard_map/ppermute | solution.py:391
  50.4 9.2 %collective-permute-start.21 = (bf16[128,1024]{1,0:T(8,128)(2,1)S(1)}, bf16[128,1024]{1,0:T(8,128)(2,1)S(1)}, u32[]{:S(2)}, u32[]{:S(2)}) collective-permute-start(bf16[128,1024]{1,0:T(8,128)(2,1)S(1)} %shard_map.90), channel_id=1, source_target_pairs={{0,2},{1,3},{2,0},{3,1},{4,6},{5,7},{6,4},{7,5},{8,10},{9,11},{10,... | collective-permute-start | bytes 786440 | tf_op jit(solution)/shard_map/ppermute | solution.py:391
  52.5 12.7 %collective-permute-start.20 = (bf16[128,1024]{1,0:T(8,128)(2,1)S(1)}, bf16[128,1024]{1,0:T(8,128)(2,1)S(1)}, u32[]{:S(2)}, u32[]{:S(2)}) collective-permute-start(bf16[128,1024]{1,0:T(8,128)(2,1)S(1)} %shard_map.89), channel_id=1, source_target_pairs={{0,2},{1,3},{2,0},{3,1},{4,6},{5,7},{6,4},{7,5},{8,10},{9,11},{10,... | collective-permute-start | bytes 786440 | tf_op jit(solution)/shard_map/ppermute | solution.py:391
  53.5 17.3 %collective-permute-start.19 = (bf16[128,1024]{1,0:T(8,128)(2,1)S(1)}, bf16[128,1024]{1,0:T(8,128)(2,1)S(1)}, u32[]{:S(2)}, u32[]{:S(2)}) collective-permute-start(bf16[128,1024]{1,0:T(8,128)(2,1)S(1)} %shard_map.88), channel_id=1, source_target_pairs={{0,2},{1,3},{2,0},{3,1},{4,6},{5,7},{6,4},{7,5},{8,10},{9,11},{10,... | collective-permute-start | bytes 786440 | tf_op jit(solution)/shard_map/ppermute | solution.py:391
  55.6 19.9 %collective-permute-start.22 = (bf16[128,1024]{1,0:T(8,128)(2,1)S(1)}, bf16[128,1024]{1,0:T(8,128)(2,1)S(1)}, u32[]{:S(2)}, u32[]{:S(2)}) collective-permute-start(bf16[128,1024]{1,0:T(8,128)(2,1)S(1)} %shard_map.86.refs_10_), channel_id=1, source_target_pairs={{0,2},{1,3},{2,0},{3,1},{4,6},{5,7},{6,4},{7,5},{8,10},{9,11},{10,... | collective-permute-start | bytes 786440 | tf_op jit(solution)/shard_map/ppermute | solution.py:391
  (1 other events, 0.7 us)

commit v23 on v22

--- a/solution.py
+++ b/solution.py
@@ -433,7 +433,7 @@
     )
 
     unit = rows // 8
-    ends = (0, 2, 4, 6, 8)
+    ends = (0, 3, 6, 8)
     cuts = [slice(start * unit, stop * unit) for start, stop in zip(ends, ends[1:])]
     pieces = finish(local, scaled, earlier[-1], cuts[:1], head_size)
     pieces += finish(local, scaled, earlier[-1], cuts[1:], head_size, pieces)

time: 76.6 us -> 76.6 us (level)
  starting transfers between devices: 21.8 us -> 20.8 us
    ppermute x18 -> x16, starting transfers between devices: 10.5 us -> 9.5 us  [swap_tp(): return lax.ppermute(x, 'tp', [(i, i ^ bit) for i in range(4)])]
    ppermute x18 -> x16, waiting for transfers between devices: 24.4 us -> 25.2 us  [swap_tp(): return lax.ppermute(x, 'tp', [(i, i ^ bit) for i in range(4)])]
    pallas_call x3 -> x2, Pallas kernels: 2.19 us -> 2.75 us  [add_rows(): pl.pallas_call(kernel, grid=(rows // unit,), in_specs=specs, out_specs=pl...]
    pallas_call x18 -> x17, Pallas kernels: 16.6 us -> 16.3 us  [call(): pl.pallas_call(run, in_specs=[SMEM] * smem + [HBM] * hbm + [VMEM] * (coun...]
  transfers between devices with their start and end apart: 23 -> 21, of which waited for: 11 -> 12; matrix products, arithmetic and copies ran while one was open for 0% -> 0% of each run, Pallas kernels for 23% -> 23%
where the time goes in v23:
time: 76.6 us; the launch traced here: 76.4 us
  waiting for transfers between devices  33.9 us (44%)
  starting transfers between devices  20.8 us (27%)
  Pallas kernels  19.1 us (25%)
  local copies, waits for them, and re-layouts  1.62 us (2%)
  other arithmetic  0.77 us (1%)
    ppermute x16, waiting for transfers between devices, swap_tp(): return lax.ppermute(x, 'tp', [(i, i ^ bit) for i in range(4)])  25.2 us
    pallas_call x17, Pallas kernels, call(): pl.pallas_call(run, in_specs=[SMEM] * smem + [HBM] * hbm + [VMEM] * (coun...  16.3 us
    ppermute x5, starting transfers between devices, swap_seq(): return lax.ppermute(x, 'seq', [(i, i ^ bit) for i in range(seq_size)])  11.3 us
    ppermute x16, starting transfers between devices, swap_tp(): return lax.ppermute(x, 'tp', [(i, i ^ bit) for i in range(4)])  9.5 us
    ppermute x5, waiting for transfers between devices, swap_seq(): return lax.ppermute(x, 'seq', [(i, i ^ bit) for i in range(seq_size)])  8.75 us
    pallas_call x2, Pallas kernels, add_rows(): pl.pallas_call(kernel, grid=(rows // unit,), in_specs=specs, out_specs=pl...  2.75 us
    unnamed x4, local copies, waits for them, and re-layouts  1.62 us
  transfers between devices with their start and end apart: 21, of which 12 were waited for; matrix products, arithmetic and copies ran while one was open for 0% of the time, Pallas kernels for 23%

profile of v23, /device:TPU:0, one launch (start us, length us, event | category | flops | bytes accessed | tf_op | source)
XLA Modules:
  0.0 76.4 jit_solution(4735589971397675949)
XLA Ops:
  0.5 2.5 %collective-permute-start = (bf16[512,1024]{1,0:T(8,128)(2,1)}, bf16[512,1024]{1,0:T(8,128)(2,1)S(1)}, u32[]{:S(2)}, u32[]{:S(2)}) collective-permute-start(bf16[512,1024]{1,0:T(8,128)(2,1)} %refs_2_.1), channel_id=1, source_target_pairs={{0,2},{1,3},{2,0},{3,1},{4,6},{5,7},{6,4},{7,5},{8,10},{9,11},{10,... | collective-permute-start | bytes 3145736 | tf_op jit(solution)/shard_map/ppermute | solution.py:391
  4.6 5.3 %shard_map.73 = (f32[512,512]{1,0:T(8,128)S(1)}, f32[512,256]{1,0:T(8,128)S(1)}, f32[512,24]{1,0:T(8,128)S(1)}, bf16[2,1024,512]{2,1,0:T(8,128)(2,1)S(1)}, bf16[...) custom-call(s32[1]{0:T(128)} %bitcast.refs_0_, ...), custom_call_target="tpu_custom_call" | custom-call | tf_op jit(solution)/shard_map/pallas_call | solution.py:41
  10.8 2.6 %collective-permute-start.3 = (f32[8,512]{1,0:T(8,128)S(1)}, f32[8,512]{1,0:T(8,128)S(1)}, u32[]{:S(2)}, u32[]{:S(2)}) collective-permute-start(f32[8,512]{1,0:T(8,128)S(1)} %get-tuple-element.50.refs_1_), channel_id=1, source_target_pairs={{0,4},{4,0},{8,12},{12,8},{16,20},{20,16},{24,28},{28,24},{1,5},{5... | collective-permute-start | bytes 49160 | tf_op jit(solution)/shard_map/ppermute | solution.py:394
  13.4 1.7 %collective-permute-done.3.refs_2_ = f32[8,512]{1,0:T(8,128)S(1)} collective-permute-done((f32[8,512]{1,0:T(8,128)S(1)}, f32[8,512]{1,0:T(8,128)S(1)}, u32[]{:S(2)}, u32[]{:S(2)}) %collective-permute-start.3) | collective-permute-done | bytes 16416 | tf_op jit(solution)/shard_map/ppermute | solution.py:394
  15.2 2.2 %collective-permute-start.4 = (f32[8,512]{1,0:T(8,128)S(1)}, f32[8,512]{1,0:T(8,128)S(1)}, u32[]{:S(2)}, u32[]{:S(2)}) collective-permute-start(f32[8,512]{1,0:T(8,128)S(1)} %get-tuple-element.51.refs_1_), channel_id=1, source_target_pairs={{0,8},{4,12},{8,0},{12,4},{16,24},{20,28},{24,16},{28,20},{1,9},{5... | collective-permute-start | bytes 49160 | tf_op jit(solution)/shard_map/ppermute | solution.py:394
  17.3 1.7 %collective-permute-done.4.refs_2_ = f32[8,512]{1,0:T(8,128)S(1)} collective-permute-done((f32[8,512]{1,0:T(8,128)S(1)}, f32[8,512]{1,0:T(8,128)S(1)}, u32[]{:S(2)}, u32[]{:S(2)}) %collective-permute-start.4) | collective-permute-done | bytes 16416 | tf_op jit(solution)/shard_map/ppermute | solution.py:394
  19.7 7.3 %collective-permute-done.refs_0_.refs_1_ = bf16[512,1024]{1,0:T(8,128)(2,1)S(1)} collective-permute-done((bf16[512,1024]{1,0:T(8,128)(2,1)}, bf16[512,1024]{1,0:T(8,128)(2,1)S(1)}, u32[]{:S(2)}, u32[]{:S(2)}) %collective-permute-start) | collective-permute-done | bytes 1048608 | tf_op jit(solution)/shard_map/ppermute | solution.py:391
  28.0 1.1 %collective-permute-done.7.refs_1_ = bf16[512,256]{1,0:T(8,128)(2,1)S(1)} collective-permute-done((bf16[512,256]{1,0:T(8,128)(2,1)S(1)}, bf16[512,256]{1,0:T(8,128)(2,1)S(1)}, u32[]{:S(2)}, u32[]{:S(2)}) %collective-permute-start.7) | collective-permute-done | bytes 262176 | tf_op jit(solution)/shard_map/ppermute | solution.py:391
  29.7 1.8 %collective-permute-start.12 = (bf16[128,512]{1,0:T(8,128)(2,1)S(1)}, bf16[128,512]{1,0:T(8,128)(2,1)S(1)}, u32[]{:S(2)}, u32[]{:S(2)}) collective-permute-start(bf16[128,512]{1,0:T(8,128)(2,1)S(1)} %get-tuple-element.70.refs_0_), channel_id=1, source_target_pairs={{0,4},{4,0},{8,12},{12,8},{16,20},{20,16},{24,28},{28,24},{1,5},{5... | collective-permute-start | bytes 393224 | tf_op jit(solution)/shard_map/ppermute | solution.py:394
  31.4 1.1 %shard_map.79 = (f32[512,512]{1,0:T(8,128)S(1)}, f32[512,24]{1,0:T(8,128)S(1)}) custom-call(s32[1]{0:T(128)} %bitcast.refs_0_, bf16[512,1024]{1,0:T(8,128)(2,1)S(1)} %collective-permute-done.refs_0_.refs_1_, bf16[2,1024,512]{2,1,0:T(8,128)(2,1)S(1)} %get-tuple-element.43.refs_2_.refs_5_, ...), custom_call_target="tpu_custom_call", output_to_operand_aliasing={{0}: (4, {}), {1}: (5, {})} | custom-call | flops 562036736 | bytes 5537796 | tf_op jit(solution)/shard_map/pallas_call | solution.py:41
  33.7 1.6 %collective-permute-done.12.refs_1_.refs_16_ = bf16[128,512]{1,0:T(8,128)(2,1)S(1)} collective-permute-done((bf16[128,512]{1,0:T(8,128)(2,1)S(1)}, bf16[128,512]{1,0:T(8,128)(2,1)S(1)}, u32[]{:S(2)}, u32[]{:S(2)}) %collective-permute-start.12) | collective-permute-done | bytes 131104 | tf_op jit(solution)/shard_map/ppermute | solution.py:394
  35.3 1.9 %collective-permute-start.13 = (bf16[128,512]{1,0:T(8,128)(2,1)S(1)}, bf16[128,512]{1,0:T(8,128)(2,1)S(1)}, u32[]{:S(2)}, u32[]{:S(2)}) collective-permute-start(bf16[128,512]{1,0:T(8,128)(2,1)S(1)} %shard_map.81.refs_0_), channel_id=1, source_target_pairs={{0,8},{4,12},{8,0},{12,4},{16,24},{20,28},{24,16},{28,20},{1,9},{5... | collective-permute-start | bytes 393224 | tf_op jit(solution)/shard_map/ppermute | solution.py:394
  37.2 3.2 %collective-permute-done.13.refs_17_.refs_1_ = bf16[128,512]{1,0:T(8,128)(2,1)S(1)} collective-permute-done((bf16[128,512]{1,0:T(8,128)(2,1)S(1)}, bf16[128,512]{1,0:T(8,128)(2,1)S(1)}, u32[]{:S(2)}, u32[]{:S(2)}) %collective-permute-start.13) | collective-permute-done | bytes 131104 | tf_op jit(solution)/shard_map/ppermute | solution.py:394
  40.4 2.9 %collective-permute-start.14 = (bf16[128,512]{1,0:T(8,128)(2,1)S(1)}, bf16[128,512]{1,0:T(8,128)(2,1)S(1)}, u32[]{:S(2)}, u32[]{:S(2)}) collective-permute-start(bf16[128,512]{1,0:T(8,128)(2,1)S(1)} %shard_map.83), channel_id=1, source_target_pairs={{0,16},{4,20},{8,24},{12,28},{16,0},{20,4},{24,8},{28,12},{1,17},{... | collective-permute-start | bytes 393224 | tf_op jit(solution)/shard_map/ppermute | solution.py:394
  43.3 4.0 %shard_map.82 = (f32[512,512]{1,0:T(8,128)S(1)}, bf16[512,512]{1,0:T(8,128)(2,1)S(1)}, bf16[512,512]{1,0:T(8,128)(2,1)}, f32[512,24]{1,0:T(8,128)}) custom-call(s32[1]{0:T(128)} %bitcast.refs_0_, bf16[512,256]{1,0:T(8,128)(2,1)S(1)} %collective-permute-done.8.refs_1_, bf16[512,256]{1,0:T(8,128)(2,1)S(1)} %collective-permute-done.9.refs_2_, ...), custom_call_target="tpu_custom_call" | custom-call | flops 1073741824 | bytes 7176196 | tf_op jit(solution)/shard_map/pallas_call | solution.py:41
  50.4 1.6 %collective-permute-start.19 = (bf16[192,1024]{1,0:T(8,128)(2,1)S(1)}, bf16[192,1024]{1,0:T(8,128)(2,1)S(1)}, u32[]{:S(2)}, u32[]{:S(2)}) collective-permute-start(bf16[192,1024]{1,0:T(8,128)(2,1)S(1)} %shard_map.89), channel_id=1, source_target_pairs={{0,2},{1,3},{2,0},{3,1},{4,6},{5,7},{6,4},{7,5},{8,10},{9,11},{10,... | collective-permute-start | bytes 1179656 | tf_op jit(solution)/shard_map/ppermute | solution.py:391
  53.1 1.3 %collective-permute-done.17.refs_1_.refs_5_ = bf16[128,512]{1,0:T(8,128)(2,1)S(1)} collective-permute-done((bf16[128,512]{1,0:T(8,128)(2,1)S(1)}, bf16[128,512]{1,0:T(8,128)(2,1)S(1)}, u32[]{:S(2)}, u32[]{:S(2)}) %collective-permute-start.17) | collective-permute-done | bytes 131104 | tf_op jit(solution)/shard_map/ppermute | solution.py:391
  55.0 1.7 %collective-permute-start.20 = (bf16[128,1024]{1,0:T(8,128)(2,1)S(1)}, bf16[128,1024]{1,0:T(8,128)(2,1)S(1)}, u32[]{:S(2)}, u32[]{:S(2)}) collective-permute-start(bf16[128,1024]{1,0:T(8,128)(2,1)S(1)} %shard_map.86.refs_8_), channel_id=1, source_target_pairs={{0,2},{1,3},{2,0},{3,1},{4,6},{5,7},{6,4},{7,5},{8,10},{9,11},{10,... | collective-permute-start | bytes 786440 | tf_op jit(solution)/shard_map/ppermute | solution.py:391
  56.6 1.3 %shard_map.87.h_ref = f32[512,1024]{1,0:T(8,128)S(1)} custom-call(bf16[192,512]{1,0:T(8,128)(2,1)S(1)} %shard_map.84.refs_3_.refs_0_, bf16[192,512]{1,0:T(8,128)(2,1)S(1)} %collective-permute-done.15.refs_1_, bf16[192,512]{1,0:T(8,128)(2,1)S(1)} %get-tuple-element.77.refs_2_.refs_0_, bf16[192,512]{1,0:T(8,128)(2,1)S(1)} %collective-permute-done.16.refs_3_.refs_1_, ...), custom_call_target="tpu_custom_call" | custom-call | tf_op jit(solution)/shard_map/pallas_call | solution.py:41
  57.9 4.5 %collective-permute-done.19.a_ref = bf16[192,1024]{1,0:T(8,128)(2,1)S(1)} collective-permute-done((bf16[192,1024]{1,0:T(8,128)(2,1)S(1)}, bf16[192,1024]{1,0:T(8,128)(2,1)S(1)}, u32[]{:S(2)}, u32[]{:S(2)}) %collective-permute-start.19) | collective-permute-done | bytes 393248 | tf_op jit(solution)/shard_map/ppermute | solution.py:391
  62.4 1.4 %shard_map.90.refs_0_ = bf16[512,1024]{1,0:T(8,128)(2,1)} custom-call(f32[512,1024]{1,0:T(8,128)S(1)} %shard_map.87.h_ref, bf16[192,1024]{1,0:T(8,128)(2,1)S(1)} %collective-permute-done.19.a_ref), custom_call_target="tpu_custom_call" | custom-call | bytes 1572864 | tf_op jit(solution)/shard_map/pallas_call | solution.py:368
  63.8 7.0 %collective-permute-done.18.a_ref = bf16[192,1024]{1,0:T(8,128)(2,1)S(1)} collective-permute-done((bf16[192,1024]{1,0:T(8,128)(2,1)S(1)}, bf16[192,1024]{1,0:T(8,128)(2,1)S(1)}, u32[]{:S(2)}, u32[]{:S(2)}) %collective-permute-start.18) | collective-permute-done | bytes 393248 | tf_op jit(solution)/shard_map/ppermute | solution.py:391
  70.8 1.4 %shard_map.91 = bf16[512,1024]{1,0:T(8,128)(2,1)} custom-call(f32[512,1024]{1,0:T(8,128)S(1)} %shard_map.87.h_ref, bf16[192,1024]{1,0:T(8,128)(2,1)S(1)} %collective-permute-done.18.a_ref, bf16[512,1024]{1,0:T(8,128)(2,1)} %shard_map.90.refs_0_), custom_call_target="tpu_custom_call", output_to_operand_aliasing={{}: (2, {})} | custom-call | bytes 1572864 | tf_op jit(solution)/shard_map/pallas_call | solution.py:368
  72.2 3.4 %collective-permute-done.20 = bf16[128,1024]{1,0:T(8,128)(2,1)S(1)} collective-permute-done((bf16[128,1024]{1,0:T(8,128)(2,1)S(1)}, bf16[128,1024]{1,0:T(8,128)(2,1)S(1)}, u32[]{:S(2)}, u32[]{:S(2)}) %collective-permute-start.20) | collective-permute-done | bytes 262176 | tf_op jit(solution)/shard_map/ppermute | solution.py:391
  (42 shorter events, 11.8 us)
Async XLA Ops:
  0.0 3.0 %collective-permute-start.1 = (bf16[512,1024]{1,0:T(8,128)(2,1)}, bf16[512,1024]{1,0:T(8,128)(2,1)S(1)}, u32[]{:S(2)}, u32[]{:S(2)}) collective-permute-start(bf16[512,1024]{1,0:T(8,128)(2,1)} %refs_2_.1), channel_id=1, source_target_pairs={{0,1},{1,0},{2,3},{3,2},{4,5},{5,4},{6,7},{7,6},{8,9},{9,8},{10,11... | collective-permute-start | bytes 3145736 | tf_op jit(solution)/shard_map/ppermute | solution.py:391
  0.5 26.6 %collective-permute-start = (bf16[512,1024]{1,0:T(8,128)(2,1)}, bf16[512,1024]{1,0:T(8,128)(2,1)S(1)}, u32[]{:S(2)}, u32[]{:S(2)}) collective-permute-start(bf16[512,1024]{1,0:T(8,128)(2,1)} %refs_2_.1), channel_id=1, source_target_pairs={{0,2},{1,3},{2,0},{3,1},{4,6},{5,7},{6,4},{7,5},{8,10},{9,11},{10,... | collective-permute-start | bytes 3145736 | tf_op jit(solution)/shard_map/ppermute | solution.py:391
  3.0 0.9 %copy-start = (bf16[4096,24]{0,1:T(8,128)(2,1)S(1)}, bf16[4096,24]{0,1:T(8,128)(2,1)}, u32[]{:S(2)}) copy-start(bf16[4096,24]{0,1:T(8,128)(2,1)} %param.12) | copy-start | bytes 589828
  3.9 0.7 copy-start.1
  9.9 17.1 %collective-permute-start.5 = (bf16[512,1024]{1,0:T(8,128)(2,1)S(1)}, bf16[512,1024]{1,0:T(8,128)(2,1)S(1)}, u32[]{:S(2)}, u32[]{:S(2)}) collective-permute-start(bf16[512,1024]{1,0:T(8,128)(2,1)S(1)} %get-tuple-element.54), channel_id=1, source_target_pairs={{0,1},{1,0},{2,3},{3,2},{4,5},{5,4},{6,7},{7,6},{8,9},{9,8},{10,11... | collective-permute-start | bytes 3145736 | tf_op jit(solution)/shard_map/ppermute | solution.py:391
  10.3 16.7 %collective-permute-start.6 = (bf16[512,1024]{1,0:T(8,128)(2,1)S(1)}, bf16[512,1024]{1,0:T(8,128)(2,1)S(1)}, u32[]{:S(2)}, u32[]{:S(2)}) collective-permute-start(bf16[512,1024]{1,0:T(8,128)(2,1)S(1)} %get-tuple-element.55), channel_id=1, source_target_pairs={{0,1},{1,0},{2,3},{3,2},{4,5},{5,4},{6,7},{7,6},{8,9},{9,8},{10,11... | collective-permute-start | bytes 3145736 | tf_op jit(solution)/shard_map/ppermute | solution.py:391
  10.5 16.6 %collective-permute-start.2 = (bf16[1024,256]{1,0:T(8,128)(2,1)S(1)}, bf16[1024,256]{1,0:T(8,128)(2,1)S(1)}, u32[]{:S(2)}, u32[]{:S(2)}) collective-permute-start(bf16[1024,256]{1,0:T(8,128)(2,1)S(1)} %get-tuple-element.49), channel_id=1, source_target_pairs={{0,1},{1,0},{2,3},{3,2},{4,5},{5,4},{6,7},{7,6},{8,9},{9,8},{10,11... | collective-permute-start | bytes 1572872 | tf_op jit(solution)/shard_map/ppermute | solution.py:391
  10.8 4.3 %collective-permute-start.3 = (f32[8,512]{1,0:T(8,128)S(1)}, f32[8,512]{1,0:T(8,128)S(1)}, u32[]{:S(2)}, u32[]{:S(2)}) collective-permute-start(f32[8,512]{1,0:T(8,128)S(1)} %get-tuple-element.50.refs_1_), channel_id=1, source_target_pairs={{0,4},{4,0},{8,12},{12,8},{16,20},{20,16},{24,28},{28,24},{1,5},{5... | collective-permute-start | bytes 49160 | tf_op jit(solution)/shard_map/ppermute | solution.py:394
  15.2 3.9 %collective-permute-start.4 = (f32[8,512]{1,0:T(8,128)S(1)}, f32[8,512]{1,0:T(8,128)S(1)}, u32[]{:S(2)}, u32[]{:S(2)}) collective-permute-start(f32[8,512]{1,0:T(8,128)S(1)} %get-tuple-element.51.refs_1_), channel_id=1, source_target_pairs={{0,8},{4,12},{8,0},{12,4},{16,24},{20,28},{24,16},{28,20},{1,9},{5... | collective-permute-start | bytes 49160 | tf_op jit(solution)/shard_map/ppermute | solution.py:394
  27.5 1.6 %collective-permute-start.7 = (bf16[512,256]{1,0:T(8,128)(2,1)S(1)}, bf16[512,256]{1,0:T(8,128)(2,1)S(1)}, u32[]{:S(2)}, u32[]{:S(2)}) collective-permute-start(bf16[512,256]{1,0:T(8,128)(2,1)S(1)} %shard_map.76.refs_3_), channel_id=1, source_target_pairs={{0,1},{1,0},{2,3},{3,2},{4,5},{5,4},{6,7},{7,6},{8,9},{9,8},{10,11... | collective-permute-start | bytes 786440 | tf_op jit(solution)/shard_map/ppermute | solution.py:391
  29.7 5.6 %collective-permute-start.12 = (bf16[128,512]{1,0:T(8,128)(2,1)S(1)}, bf16[128,512]{1,0:T(8,128)(2,1)S(1)}, u32[]{:S(2)}, u32[]{:S(2)}) collective-permute-start(bf16[128,512]{1,0:T(8,128)(2,1)S(1)} %get-tuple-element.70.refs_0_), channel_id=1, source_target_pairs={{0,4},{4,0},{8,12},{12,8},{16,20},{20,16},{24,28},{28,24},{1,5},{5... | collective-permute-start | bytes 393224 | tf_op jit(solution)/shard_map/ppermute | solution.py:394
  32.6 10.7 %collective-permute-start.8 = (bf16[512,256]{1,0:T(8,128)(2,1)S(1)}, bf16[512,256]{1,0:T(8,128)(2,1)S(1)}, u32[]{:S(2)}, u32[]{:S(2)}) collective-permute-start(bf16[512,256]{1,0:T(8,128)(2,1)S(1)} %get-tuple-element.59), channel_id=1, source_target_pairs={{0,1},{1,0},{2,3},{3,2},{4,5},{5,4},{6,7},{7,6},{8,9},{9,8},{10,11... | collective-permute-start | bytes 786440 | tf_op jit(solution)/shard_map/ppermute | solution.py:391
  32.7 10.6 %collective-permute-start.9 = (bf16[512,256]{1,0:T(8,128)(2,1)S(1)}, bf16[512,256]{1,0:T(8,128)(2,1)S(1)}, u32[]{:S(2)}, u32[]{:S(2)}) collective-permute-start(bf16[512,256]{1,0:T(8,128)(2,1)S(1)} %get-tuple-element.60), channel_id=1, source_target_pairs={{0,1},{1,0},{2,3},{3,2},{4,5},{5,4},{6,7},{7,6},{8,9},{9,8},{10,11... | collective-permute-start | bytes 786440 | tf_op jit(solution)/shard_map/ppermute | solution.py:391
  33.2 10.1 %collective-permute-start.10 = (bf16[512,256]{1,0:T(8,128)(2,1)S(1)}, bf16[512,256]{1,0:T(8,128)(2,1)S(1)}, u32[]{:S(2)}, u32[]{:S(2)}) collective-permute-start(bf16[512,256]{1,0:T(8,128)(2,1)S(1)} %get-tuple-element.61), channel_id=1, source_target_pairs={{0,1},{1,0},{2,3},{3,2},{4,5},{5,4},{6,7},{7,6},{8,9},{9,8},{10,11... | collective-permute-start | bytes 786440 | tf_op jit(solution)/shard_map/ppermute | solution.py:391
  33.2 10.0 %collective-permute-start.11 = (bf16[512,256]{1,0:T(8,128)(2,1)S(1)}, bf16[512,256]{1,0:T(8,128)(2,1)S(1)}, u32[]{:S(2)}, u32[]{:S(2)}) collective-permute-start(bf16[512,256]{1,0:T(8,128)(2,1)S(1)} %get-tuple-element.62), channel_id=1, source_target_pairs={{0,1},{1,0},{2,3},{3,2},{4,5},{5,4},{6,7},{7,6},{8,9},{9,8},{10,11... | collective-permute-start | bytes 786440 | tf_op jit(solution)/shard_map/ppermute | solution.py:391
  35.3 5.0 %collective-permute-start.13 = (bf16[128,512]{1,0:T(8,128)(2,1)S(1)}, bf16[128,512]{1,0:T(8,128)(2,1)S(1)}, u32[]{:S(2)}, u32[]{:S(2)}) collective-permute-start(bf16[128,512]{1,0:T(8,128)(2,1)S(1)} %shard_map.81.refs_0_), channel_id=1, source_target_pairs={{0,8},{4,12},{8,0},{12,4},{16,24},{20,28},{24,16},{28,20},{1,9},{5... | collective-permute-start | bytes 393224 | tf_op jit(solution)/shard_map/ppermute | solution.py:394
  40.4 7.5 %collective-permute-start.14 = (bf16[128,512]{1,0:T(8,128)(2,1)S(1)}, bf16[128,512]{1,0:T(8,128)(2,1)S(1)}, u32[]{:S(2)}, u32[]{:S(2)}) collective-permute-start(bf16[128,512]{1,0:T(8,128)(2,1)S(1)} %shard_map.83), channel_id=1, source_target_pairs={{0,16},{4,20},{8,24},{12,28},{16,0},{20,4},{24,8},{28,12},{1,17},{... | collective-permute-start | bytes 393224 | tf_op jit(solution)/shard_map/ppermute | solution.py:394
  48.3 1.5 %collective-permute-start.15 = (bf16[192,512]{1,0:T(8,128)(2,1)S(1)}, bf16[192,512]{1,0:T(8,128)(2,1)S(1)}, u32[]{:S(2)}, u32[]{:S(2)}) collective-permute-start(bf16[192,512]{1,0:T(8,128)(2,1)S(1)} %shard_map.84.refs_3_.refs_0_), channel_id=1, source_target_pairs={{0,1},{1,0},{2,3},{3,2},{4,5},{5,4},{6,7},{7,6},{8,9},{9,8},{10,11... | collective-permute-start | bytes 589832 | tf_op jit(solution)/shard_map/ppermute | solution.py:391
  48.8 3.2 %collective-permute-start.16 = (bf16[192,512]{1,0:T(8,128)(2,1)S(1)}, bf16[192,512]{1,0:T(8,128)(2,1)S(1)}, u32[]{:S(2)}, u32[]{:S(2)}) collective-permute-start(bf16[192,512]{1,0:T(8,128)(2,1)S(1)} %get-tuple-element.77.refs_2_.refs_0_), channel_id=1, source_target_pairs={{0,1},{1,0},{2,3},{3,2},{4,5},{5,4},{6,7},{7,6},{8,9},{9,8},{10,11... | collective-permute-start | bytes 589832 | tf_op jit(solution)/shard_map/ppermute | solution.py:391
  50.4 12.0 %collective-permute-start.19 = (bf16[192,1024]{1,0:T(8,128)(2,1)S(1)}, bf16[192,1024]{1,0:T(8,128)(2,1)S(1)}, u32[]{:S(2)}, u32[]{:S(2)}) collective-permute-start(bf16[192,1024]{1,0:T(8,128)(2,1)S(1)} %shard_map.89), channel_id=1, source_target_pairs={{0,2},{1,3},{2,0},{3,1},{4,6},{5,7},{6,4},{7,5},{8,10},{9,11},{10,... | collective-permute-start | bytes 1179656 | tf_op jit(solution)/shard_map/ppermute | solution.py:391
  52.6 18.2 %collective-permute-start.18 = (bf16[192,1024]{1,0:T(8,128)(2,1)S(1)}, bf16[192,1024]{1,0:T(8,128)(2,1)S(1)}, u32[]{:S(2)}, u32[]{:S(2)}) collective-permute-start(bf16[192,1024]{1,0:T(8,128)(2,1)S(1)} %shard_map.88), channel_id=1, source_target_pairs={{0,2},{1,3},{2,0},{3,1},{4,6},{5,7},{6,4},{7,5},{8,10},{9,11},{10,... | collective-permute-start | bytes 1179656 | tf_op jit(solution)/shard_map/ppermute | solution.py:391
  53.1 1.3 %collective-permute-start.17 = (bf16[128,512]{1,0:T(8,128)(2,1)S(1)}, bf16[128,512]{1,0:T(8,128)(2,1)S(1)}, u32[]{:S(2)}, u32[]{:S(2)}) collective-permute-start(bf16[128,512]{1,0:T(8,128)(2,1)S(1)} %get-tuple-element.78.refs_0_.refs_4_), channel_id=1, source_target_pairs={{0,1},{1,0},{2,3},{3,2},{4,5},{5,4},{6,7},{7,6},{8,9},{9,8},{10,11... | collective-permute-start | bytes 393224 | tf_op jit(solution)/shard_map/ppermute | solution.py:391
  55.0 20.7 %collective-permute-start.20 = (bf16[128,1024]{1,0:T(8,128)(2,1)S(1)}, bf16[128,1024]{1,0:T(8,128)(2,1)S(1)}, u32[]{:S(2)}, u32[]{:S(2)}) collective-permute-start(bf16[128,1024]{1,0:T(8,128)(2,1)S(1)} %shard_map.86.refs_8_), channel_id=1, source_target_pairs={{0,2},{1,3},{2,0},{3,1},{4,6},{5,7},{6,4},{7,5},{8,10},{9,11},{10,... | collective-permute-start | bytes 786440 | tf_op jit(solution)/shard_map/ppermute | solution.py:391
